TPU v7x, 32 devices: a whole 2x2x4 slice. The times are simulated.
32 devices in a mesh: parts: 2 (over y), expert: 4 (over z), tensor: 4 (over x, core).
Axes of the slice: x: 2, y: 2, z: 4, core: 2. Of those that a mesh axis runs over, the one named last changes fastest.
Arguments:
- tokens: bfloat16 [1, 128, 7168], P(None, ('parts', 'expert', 'tensor')), parts along dimension 1, may hold values from -6 to 6
- routes: int32 [1, 128, 8], P(None, ('parts', 'expert', 'tensor')), parts along dimension 1, may hold values from 0 to 15, as said below
- numerators: int32 [1, 128, 8], P(None, ('parts', 'expert', 'tensor')), parts along dimension 1, may hold values from 1 to 256
- place: int32 [32], P('parts'), parts along dimension 0, may hold values from 0 to 15, as said below
- base_in: bfloat16 [4, 7168, 2, 1024], P('expert', None, None, 'tensor'), may hold values from -0.0625 to 0.0625
- base_down: bfloat16 [4, 1024, 7168], P('expert', 'tensor'), may hold values from -0.1875 to 0.1875
- delta_in: bfloat16 [16, 7168, 128], P(('expert', 'tensor')), may hold values from -0.0625 to 0.0625
- delta_mid: bfloat16 [4, 4, 128, 2, 1024], P('expert', None, None, None, 'tensor'), may hold values from -0.5 to 0.5
- delta_down: bfloat16 [4, 4, 1024, 128], P('expert', None, 'tensor'), may hold values from -0.1875 to 0.1875
- delta_back: bfloat16 [16, 128, 7168], P(('expert', 'tensor')), may hold values from -0.5 to 0.5
Outputs:
- mixed: bfloat16 [1, 128, 7168], P(None, ('parts', 'expert', 'tensor')), parts along dimension 1
There are 2 independent parts, one for each index of `parts`. A program takes and returns all parts, laid end to end along the dimension named above; an argument that names none is the same for every part. Nothing has to cross between parts.
Inputs may be any that keep to these rules, and one draw needn't show every extreme that they name: `routes`: each token's entries name different experts, 4 in each of exactly 2 clusters (the cluster of expert e is place[e] // 4). Among the 4 tokens of one device in one step no cluster is named by more than 4 tokens; in each step one cluster, drawn from the seed, is named by exactly 4 tokens of every device. `place`: each position holds exactly one expert.
All inputs are finite; a program needn't handle non-finite values.
Results may differ from a plain program's by a relative error of at most 0.015.
Values may be sent and summed in bfloat16 or wider, within the bound.
No kernel may reach another device: no remote copies, remote signals or barrier semaphores. Data moves between devices by JAX's collectives and lax.ppermute only.
A program may use at most 128 MiB of HBM per device.

v0:
```python
import jax
import jax.numpy as jnp
from jax import lax
from jax.sharding import PartitionSpec as P


def lookup(table, index):
    keys = jnp.arange(table.shape[0], dtype=jnp.int32)
    return jnp.sum(jnp.where(index[..., None] == keys, table, 0), axis=-1)


def local(
    tokens,
    routes,
    numerators,
    place,
    base_in,
    base_down,
    delta_in,
    delta_mid,
    delta_down,
    delta_back,
):
    clusters = lax.axis_size("expert")
    members = lax.axis_size("tensor")
    my_slot = lax.axis_index("tensor")
    per_token = min(4, clusters // 2)
    tok_count = tokens.shape[1]
    capacity = 2 * tok_count * per_token // clusters
    width = tokens.shape[2]
    hidden_part = base_in.shape[3]
    gate_up = base_in[0].reshape(width, 2 * hidden_part)
    rows = tokens[0]
    position = lookup(place, routes[0])
    cluster_of = position // members
    slot_of = position % members
    numerator = numerators[0].astype(jnp.float32)
    weight = (2.5 * numerator / jnp.sum(numerator, axis=-1, keepdims=True)).astype(jnp.bfloat16)
    cluster_hit = cluster_of[..., None] == jnp.arange(clusters, dtype=jnp.int32)
    slot_hit = slot_of[..., None] == jnp.arange(members, dtype=jnp.int32)
    table = jnp.einsum(
        "nk,nkc,nks->ncs",
        weight.astype(jnp.float32),
        cluster_hit.astype(jnp.float32),
        slot_hit.astype(jnp.float32),
    ).astype(jnp.bfloat16)
    present = jnp.any(cluster_hit, axis=1)
    order = jnp.cumsum(present.astype(jnp.int32), axis=0) - 1
    slots_range = jnp.arange(capacity, dtype=jnp.int32)
    select = (present.T[:, None, :] & (order.T[:, None, :] == slots_range[None, :, None])).astype(
        jnp.bfloat16
    )
    packed = jnp.einsum("cki,id->ckd", select, rows, preferred_element_type=jnp.float32).astype(
        jnp.bfloat16
    )
    packed_weights = jnp.einsum(
        "cki,ics->cks", select, table, preferred_element_type=jnp.float32
    ).astype(jnp.bfloat16)
    spread = jnp.broadcast_to(packed[:, None], (clusters, members, capacity, width)).reshape(
        clusters * members, capacity, width
    )
    spread_weights = jnp.broadcast_to(
        packed_weights[:, None], (clusters, members, capacity, members)
    ).reshape(clusters * members, capacity, members)
    received = lax.all_to_all(spread, ("expert", "tensor"), split_axis=0, concat_axis=0, tiled=True)
    received_weights = lax.all_to_all(
        spread_weights, ("expert", "tensor"), split_axis=0, concat_axis=0, tiled=True
    )
    received = received.reshape(-1, width)
    received_weights = received_weights.reshape(-1, members)
    group_rows = received.shape[0]
    projected = jnp.dot(received, gate_up, preferred_element_type=jnp.float32).reshape(
        group_rows, 2, hidden_part
    )
    codes = jnp.dot(received, delta_in[0], preferred_element_type=jnp.float32).astype(jnp.bfloat16)
    middle = delta_mid[0]
    lifted = jnp.einsum(
        "srk,skgf->srgf",
        lax.all_gather(codes[None], "tensor", axis=0, tiled=True),
        middle,
        preferred_element_type=jnp.float32,
    )
    hidden = jax.nn.silu(projected[None, :, 0] + lifted[:, :, 0]) * (
        projected[None, :, 1] + lifted[:, :, 1]
    )
    scale = received_weights.astype(jnp.float32).T
    hidden_sum = jnp.sum(scale[:, :, None] * hidden, axis=0)
    downward = delta_down[0]
    partial_codes = jnp.einsum(
        "srf,sfk->srk", hidden.astype(jnp.bfloat16), downward, preferred_element_type=jnp.float32
    )
    lowrank = partial_codes
    hidden_sum, lowrank = (hidden_sum, lowrank)
    summed = lax.psum_scatter(
        lowrank.astype(jnp.bfloat16), "tensor", scatter_dimension=0, tiled=True
    ).astype(jnp.float32)[0]
    own_weight = lax.dynamic_slice_in_dim(received_weights, my_slot, 1, 1).astype(jnp.float32)
    scaled = (own_weight * summed).astype(jnp.bfloat16)
    partial_value = jnp.dot(
        hidden_sum.astype(jnp.bfloat16), base_down[0], preferred_element_type=jnp.float32
    )
    partial_value = partial_value + jnp.dot(
        scaled, delta_back[0], preferred_element_type=jnp.float32
    )
    returned = lax.all_to_all(
        partial_value.astype(jnp.bfloat16).reshape(clusters * members, capacity, width),
        ("expert", "tensor"),
        split_axis=0,
        concat_axis=0,
        tiled=True,
    )
    cluster_rows = jnp.sum(
        returned.reshape(clusters, members, capacity, width).astype(jnp.float32), axis=1
    ).astype(jnp.bfloat16)
    mixed = jnp.einsum(
        "cki,ckd->id", select, cluster_rows, preferred_element_type=jnp.float32
    ).astype(jnp.bfloat16)
    outputs = [mixed]
    return jnp.stack(outputs)


def solution(mesh):
    placed = (
        P(None, ("parts", "expert", "tensor"), None),
        P(None, ("parts", "expert", "tensor"), None),
        P(None, ("parts", "expert", "tensor"), None),
        P("parts"),
        P("expert", None, None, "tensor"),
        P("expert", "tensor", None),
        P(("expert", "tensor"), None, None),
        P("expert", None, None, None, "tensor"),
        P("expert", None, "tensor", None),
        P(("expert", "tensor"), None, None),
    )
    return jax.shard_map(
        local,
        mesh=mesh,
        in_specs=placed,
        out_specs=P(None, ("parts", "expert", "tensor"), None),
        check_vma=False,
    )
```

profile of v0, /device:TPU:0, one launch (start us, length us, event | category | flops | bytes accessed | tf_op | source)
XLA Modules:
  0.0 127.3 jit_solution(477435104204287970)
XLA Ops:
  6.5 0.0 copy-start
  6.5 0.9 convert_reduce_fusion
  7.5 0.8 fusion.33
  8.2 0.9 select_reduce_fusion
  9.2 0.1 fusion.24
  9.3 0.1 copy.41
  9.5 0.1 copy.42
  9.6 0.1 convolution_convert_fusion.3
  9.7 0.3 convolution_convert_fusion.2
  9.9 0.1 copy.45
  10.1 0.6 broadcast_in_dim.16
  10.7 7.4 %all-to-all-start = ((bf16[16,4,4]{1,2,0:T(4,128)(2,1)}), bf16[16,4,4]{1,2,0:T(4,128)(2,1)S(1)}, u32[]{:S(2)}, u32[]{:S(2)}) async-start(bf16[16,4,4]{1,2,0:T(4,128)(2,1)} %bitcast.4), calls=%async_computation | async-start | bytes 32768 | tf_op jit(solution)/shard_map/all_to_all | solution.py:66
  18.1 1.2 convolution_convert_fusion
  19.3 5.3 %all-to-all-done = bf16[16,4,4]{1,2,0:T(4,128)(2,1)S(1)} async-done(((bf16[16,4,4]{1,2,0:T(4,128)(2,1)}), bf16[16,4,4]{1,2,0:T(4,128)(2,1)S(1)}, u32[]{:S(2)}, u32[]{:S(2)}) %all-to-all-start) | async-done | bytes 544 | tf_op jit(solution)/shard_map/all_to_all | solution.py:66
  24.6 1.2 broadcast_in_dim.17
  25.7 3.6 %all-to-all-start.1 = ((bf16[16,4,7168]{2,1,0:T(4,128)(2,1)}), bf16[16,4,7168]{2,1,0:T(4,128)(2,1)S(1)}, u32[]{:S(2)}, u32[]{:S(2)}) async-start(bf16[16,4,7168]{2,1,0:T(4,128)(2,1)} %bitcast.92), calls=%async_computation.1 | async-start | bytes 1835008 | tf_op jit(solution)/shard_map/all_to_all | solution.py:65
  29.4 0.0 reduce-scatter.2.cloned.1.call-start
  29.4 7.4 %copy.55 = bf16[896,8,2,256]{3,1,2,0:T(8,128)(2,1)} copy(bf16[896,8,2,256]{3,2,1,0:T(2,128)(2,1)} %bitcast.91) | data formatting | bytes 14680064
  36.8 10.0 %copy.48 = bf16[512,7168]{1,0:T(8,128)(2,1)} copy(bf16[512,7168]{0,1:T(8,128)(2,1)} %bitcast.89) | data formatting | bytes 14680064 | tf_op jit(solution)/shard_map/dot_general | solution.py:72
  46.8 0.1 reshape.72
  46.9 3.2 %all-to-all-done.1 = bf16[16,4,7168]{2,1,0:T(4,128)(2,1)S(1)} async-done(((bf16[16,4,7168]{2,1,0:T(4,128)(2,1)}), bf16[16,4,7168]{2,1,0:T(4,128)(2,1)S(1)}, u32[]{:S(2)}, u32[]{:S(2)}) %all-to-all-start.1) | async-done | bytes 917536 | tf_op jit(solution)/shard_map/all_to_all | solution.py:65
  50.2 1.1 reshape.74
  51.3 2.2 %fusion.8 = bf16[64,128]{1,0:T(8,128)(2,1)S(1)} fusion(bf16[64,7168]{1,0:T(8,128)(2,1)} %reshape.74, bf16[1,7168,128]{2,1,0:T(8,128)(2,1)} %param.16), kind=kOutput, calls=%fused_computation.12 | convolution fusion | flops 117448704 | bytes 2768896 | tf_op jit(solution)/shard_map/dot_general | solution.py:75
  53.5 5.4 %all-gather = bf16[256,128]{1,0:T(8,128)(2,1)S(1)} all-gather(bf16[64,128]{1,0:T(8,128)(2,1)S(1)} %fusion.8), channel_id=2, replica_groups=mesh['parts'=2,'expert'=4,'tensor'=4] {'tensor'}, dimensions={0}, use_global_device_ids=true | all-gather | bytes 81920 | tf_op jit(solution)/shard_map/all_gather | solution.py:79
  58.9 1.1 reshape.80
  60.0 0.0 copy-start.1
  60.0 5.8 %fusion.39 = f32[64,2,256]{2,0,1:T(8,128)S(1)} fusion(bf16[64,7168,1]{1,0,2:T(8,128)(2,1)} %reshape.80, bf16[2,256,7168]{2,1,0:T(8,128)(2,1)} %bitcast.90), kind=kOutput, calls=%fused_computation.62 | convolution fusion | flops 469762048 | bytes 8388608 | tf_op jit(solution)/shard_map/dot_general | solution.py:72
  65.8 0.0 copy-start.2
  65.8 0.0 copy-done.1
  65.8 0.2 fusion.11
  66.1 0.1 multiply_reduce_fusion
  66.2 0.6 copy-done.2
  66.8 0.8 convolution_convert_fusion.1
  67.6 0.0 reduce-scatter.2.cloned.1.call-update
  67.6 4.0 %fusion.3 = f32[64,7168]{1,0:T(8,128)} fusion(bf16[1,256,7168]{2,1,0:T(8,128)(2,1)} %param.15, bf16[64,256]{1,0:T(8,128)(2,1)S(1)} %get-tuple-element.5), kind=kOutput, calls=%fused_computation.6 | convolution fusion | flops 234881024 | bytes 5537792 | tf_op jit(solution)/shard_map/dot_general | solution.py:99
  71.6 16.9 %reduce-scatter.2.cloned.1.call-done = bf16[1,64,128]{2,1,0:T(8,128)(2,1)} async-done(((bf16[4,64,128]{2,1,0:T(8,128)(2,1)}), bf16[1,64,128]{2,1,0:T(8,128)(2,1)}) %reduce-scatter.2.cloned.1.call-update) | async-done | bytes 16400 | tf_op jit(solution)/shard_map/reduce_scatter | solution.py:94
  88.5 0.0 copy-done
  88.5 2.0 %fusion = bf16[64,7168]{1,0:T(8,128)(2,1)S(1)} fusion(f32[64,7168]{1,0:T(8,128)} %fusion.3, bf16[1,128,7168]{2,1,0:T(8,128)(2,1)S(1)} %copy-done, bf16[1,64,128]{2,1,0:T(8,128)(2,1)} %reduce-scatter.2.cloned.1.call-done, f32[64]{0:T(128)S(1)} %bitcast_convert_fusion), kind=kOutput, calls=%fused_computation.1 | convolution fusion | flops 118382592 | bytes 4604160 | tf_op jit(solution)/shard_map/dot_general | solution.py:102
  90.5 1.3 reshape.75
  91.8 27.3 %all_to_all.15 = bf16[16,4,7168]{2,1,0:T(4,128)(2,1)S(1)} all-to-all(bf16[16,4,7168]{2,1,0:T(4,128)(2,1)} %reshape.75), channel_id=1, replica_groups=mesh['parts'=2,'expert'=4,'tensor'=4] {'expert','tensor'}, dimensions={0} | all-to-all | bytes 1835008 | tf_op jit(solution)/shard_map/all_to_all | solution.py:105
  119.0 0.5 bitcast_reduce_fusion
  119.5 1.0 fusion.2
  (8 shorter events, 0.1 us)
Async XLA Ops:
  6.5 82.0 %copy-start = (bf16[1,128,7168]{2,1,0:T(8,128)(2,1)S(1)}, bf16[1,128,7168]{2,1,0:T(8,128)(2,1)}, u32[]{:S(2)}) copy-start(bf16[1,128,7168]{2,1,0:T(8,128)(2,1)} %param.19) | copy-start | bytes 5505028
  10.7 13.9 %all-to-all-start = ((bf16[16,4,4]{1,2,0:T(4,128)(2,1)}), bf16[16,4,4]{1,2,0:T(4,128)(2,1)S(1)}, u32[]{:S(2)}, u32[]{:S(2)}) async-start(bf16[16,4,4]{1,2,0:T(4,128)(2,1)} %bitcast.4), calls=%async_computation | async-start | bytes 32768 | tf_op jit(solution)/shard_map/all_to_all | solution.py:66
  25.7 24.4 %all-to-all-start.1 = ((bf16[16,4,7168]{2,1,0:T(4,128)(2,1)}), bf16[16,4,7168]{2,1,0:T(4,128)(2,1)S(1)}, u32[]{:S(2)}, u32[]{:S(2)}) async-start(bf16[16,4,7168]{2,1,0:T(4,128)(2,1)} %bitcast.92), calls=%async_computation.1 | async-start | bytes 1835008 | tf_op jit(solution)/shard_map/all_to_all | solution.py:65
  29.4 59.1 %reduce-scatter.2.cloned.1.call-start = ((), (), s32[]{:S(2)}) async-start(), calls=%async_computation.4 | async-start | bytes 81920 | tf_op jit(solution)/shard_map/reduce_scatter | solution.py:94
  60.0 5.8 %copy-start.1 = (bf16[1,4,128,2,256]{4,3,2,1,0:T(2,128)(2,1)S(1)}, bf16[1,4,128,2,256]{4,3,2,1,0:T(2,128)(2,1)}, u32[]{:S(2)}) copy-start(bf16[1,4,128,2,256]{4,3,2,1,0:T(2,128)(2,1)} %param.17) | copy-start | bytes 1572868
  65.8 1.0 copy-start.2
Sparse Core Ops, SparseCore 0:
  67.7 20.7 reduce-scatter.1
where the time goes:
time: 128 us; the launch traced here: 127 us
  blocking collectives  32.6 us (25%)
  waiting for transfers between devices  25.4 us (20%)
  local copies, waits for them, and re-layouts  23.7 us (19%)
  matrix products  17.7 us (14%)
  between operations  13.5 us (11%)
  starting transfers between devices  11 us (9%)
  other arithmetic  3.39 us (3%)
    all_to_all x1, blocking collectives, local(): lax.all_to_all(partial_value.astype(jnp.bfloat16).reshape(clusters * memb...  27.3 us
    reduce_scatter x1, waiting for transfers between devices, local(): lax.psum_scatter(lowrank.astype(jnp.bfloat16), 'tensor', scatter_dimensio...  16.9 us
    dot_general x1, local copies, waits for them, and re-layouts, local(): jnp.dot(received, gate_up, preferred_element_type=jnp.float32)  9.96 us
    unnamed x7, local copies, waits for them, and re-layouts  7.99 us
    all_to_all x1, starting transfers between devices, local(): lax.all_to_all(spread_weights, ('expert', 'tensor'), split_axis=0, concat...  7.36 us
    dot_general x1, matrix products, local(): jnp.dot(received, gate_up, preferred_element_type=jnp.float32)  5.76 us
    all_gather x1, blocking collectives, local(): lax.all_gather(codes[None], 'tensor', axis=0, tiled=True)  5.39 us
    all_to_all x1, waiting for transfers between devices, local(): lax.all_to_all(spread_weights, ('expert', 'tensor'), split_axis=0, concat...  5.26 us
  transfers between devices with their start and end apart: 3, of which 3 were waited for; matrix products, arithmetic and copies ran while one was open for 18% of the time, Pallas kernels for 0%

commit v1 on v0

v1 whole, which is shorter than its diff:
```python
import jax
import jax.numpy as jnp
from jax import lax
from jax.sharding import PartitionSpec as P


def lookup(table, index):
    keys = jnp.arange(table.shape[0], dtype=jnp.int32)
    return jnp.sum(jnp.where(index[..., None] == keys, table, 0), axis=-1)


def from_ahead(value, steps):
    size = lax.axis_size("expert")
    return lax.ppermute(value, "expert", [((i + steps) % size, i) for i in range(size)])


def swap(value, mask):
    size = lax.axis_size("tensor")
    return lax.ppermute(value, "tensor", [(i, i ^ mask) for i in range(size)])


def local(
    tokens,
    routes,
    numerators,
    place,
    base_in,
    base_down,
    delta_in,
    delta_mid,
    delta_down,
    delta_back,
):
    clusters = lax.axis_size("expert")
    members = lax.axis_size("tensor")
    chips = members // 2
    me = lax.axis_index("tensor")
    cluster = lax.axis_index("expert")
    count, width = tokens.shape[1:]
    top = routes.shape[2]
    group = clusters * count

    side = jnp.concatenate([routes[0], numerators[0]], axis=1).astype(jnp.bfloat16)
    side = jnp.pad(side, ((0, 0), (0, 128 - 2 * top)))
    packed = jnp.concatenate([tokens[0], side], axis=1)

    held = jnp.concatenate([packed] + [from_ahead(packed, k) for k in range(1, clusters)])
    held = jnp.concatenate([held] + [swap(held, 2 * m) for m in range(1, chips)])
    held = jnp.concatenate([held, swap(held, 1)])
    rows = held[:, :width]
    all_routes = held[:, width : width + top].astype(jnp.int32)
    numerator = held[:, width + top : width + 2 * top].astype(jnp.float32)

    position = lookup(place, all_routes)
    weight = (2.5 * numerator / jnp.sum(numerator, axis=-1, keepdims=True)).astype(jnp.bfloat16)
    target = cluster * members + jnp.arange(members, dtype=jnp.int32)
    scale = jnp.sum(
        jnp.where(position[None] == target[:, None, None], weight[None].astype(jnp.float32), 0.0), axis=-1
    )

    codes = jnp.dot(rows, delta_in[0], preferred_element_type=jnp.float32).astype(jnp.bfloat16)

    def block_of(m):
        return (m % 2) * chips + m // 2

    def reorder(value, m):
        if m == 0:
            return value
        blocks = value.reshape(members, group, value.shape[-1])
        return jnp.concatenate([blocks[i ^ block_of(m)] for i in range(members)])

    shared = jnp.stack([reorder(codes if m == 0 else swap(codes, m), m) for m in range(members)])
    by_slot = jnp.stack([lax.dynamic_index_in_dim(shared, s ^ me, 0, keepdims=False) for s in range(members)])

    projected = jnp.einsum("nd,dgf->ngf", rows, base_in[0], preferred_element_type=jnp.float32)
    lifted = jnp.einsum("srk,skgf->srgf", by_slot, delta_mid[0], preferred_element_type=jnp.float32)
    hidden = jax.nn.silu(projected[None, :, 0] + lifted[:, :, 0]) * (
        projected[None, :, 1] + lifted[:, :, 1]
    )
    hidden_sum = jnp.sum(scale[:, :, None] * hidden, axis=0).astype(jnp.bfloat16)
    partial_codes = jnp.einsum(
        "srf,sfk->srk", hidden.astype(jnp.bfloat16), delta_down[0], preferred_element_type=jnp.float32
    ).astype(jnp.bfloat16)
    lowrank = lax.dynamic_index_in_dim(partial_codes, me, 0, keepdims=False).astype(jnp.float32)
    for m in range(1, members):
        part = swap(lax.dynamic_index_in_dim(partial_codes, me ^ m, 0, keepdims=False), m)
        lowrank = lowrank + reorder(part, m).astype(jnp.float32)
    own_scale = lax.dynamic_index_in_dim(scale, me, 0, keepdims=False)
    scaled = (own_scale[:, None] * lowrank).astype(jnp.bfloat16)

    term = jnp.dot(hidden_sum, base_down[0], preferred_element_type=jnp.float32)
    term = (term + jnp.dot(scaled, delta_back[0], preferred_element_type=jnp.float32)).astype(jnp.bfloat16)

    half = chips * group
    total = (term[:half].astype(jnp.float32) + swap(term[half:], 1).astype(jnp.float32)).astype(jnp.bfloat16)
    parts = total.reshape(chips, group, width)
    total = parts[0].astype(jnp.float32)
    for m in range(1, chips):
        total = total + swap(parts[m], 2 * m).astype(jnp.float32)
    parts = total.astype(jnp.bfloat16).reshape(clusters, count, width)
    mixed = parts[0].astype(jnp.float32)
    for k in range(1, clusters):
        mixed = mixed + from_ahead(parts[k], clusters - k).astype(jnp.float32)
    return mixed.astype(jnp.bfloat16)[None]


def solution(mesh):
    placed = (
        P(None, ("parts", "expert", "tensor"), None),
        P(None, ("parts", "expert", "tensor"), None),
        P(None, ("parts", "expert", "tensor"), None),
        P("parts"),
        P("expert", None, None, "tensor"),
        P("expert", "tensor", None),
        P(("expert", "tensor"), None, None),
        P("expert", None, None, None, "tensor"),
        P("expert", None, "tensor", None),
        P(("expert", "tensor"), None, None),
    )
    return jax.shard_map(
        local,
        mesh=mesh,
        in_specs=placed,
        out_specs=P(None, ("parts", "expert", "tensor"), None),
        check_vma=False,
    )
```

time: 128 us -> 79.3 us (0.62)
  blocking collectives: 32.6 us -> 0 us
  between operations: 13.5 us -> 0.3 us
  matrix products: 17.7 us -> 9.12 us
  starting transfers between devices: 11 us -> 18.5 us
  waiting for transfers between devices: 25.4 us -> 23.4 us
    all_to_all x1 -> x0, blocking collectives: 27.3 us -> none  [local(): lax.all_to_all(partial_value.astype(jnp.bfloat16).reshape(clusters * memb...]
    ppermute x0 -> x16, waiting for transfers between devices: none -> 23.4 us  [the longest x10 15.9 us: swap(): return lax.ppermute(value, 'tensor', [(i, i ^ mask) for i in range(size)])]
    ppermute x0 -> x16, starting transfers between devices: none -> 18.5 us  [the longest x6 11.9 us: from_ahead(): lax.ppermute(value, 'expert', [((i + steps) % size, i) for i in range(siz...]
    reduce_scatter x1 -> x0, waiting for transfers between devices: 16.9 us -> none  [local(): lax.psum_scatter(lowrank.astype(jnp.bfloat16), 'tensor', scatter_dimensio...]
    concatenate x0 -> x6, local copies, waits for them, and re-layouts: none -> 13.8 us  [the longest x1 11.6 us: local(): held = jnp.concatenate([held, swap(held, 1)])]
    all_to_all x2 -> x0, starting transfers between devices: 11 us -> none  [the longest x1 7.36 us: local(): lax.all_to_all(spread_weights, ('expert', 'tensor'), split_axis=0, concat...]
    dot_general x1 -> x0, local copies, waits for them, and re-layouts: 9.96 us -> none  [local(): jnp.dot(received, gate_up, preferred_element_type=jnp.float32)]
    ppermute x0 -> x5, local copies, waits for them, and re-layouts: none -> 9.22 us  [the longest x3 5.51 us: from_ahead(): lax.ppermute(value, 'expert', [((i + steps) % size, i) for i in range(siz...]
  transfers between devices with their start and end apart: 3 -> 16, of which waited for: 3 -> 10; matrix products, arithmetic and copies ran while one was open for 18% -> 19% of each run, Pallas kernels for 0% -> 0%
where the time goes in v1:
time: 79.3 us; the launch traced here: 78.8 us
  local copies, waits for them, and re-layouts  23.5 us (30%)
  waiting for transfers between devices  23.4 us (30%)
  starting transfers between devices  18.5 us (23%)
  matrix products  9.12 us (12%)
  other arithmetic  3.92 us (5%)
    ppermute x10, waiting for transfers between devices, swap(): return lax.ppermute(value, 'tensor', [(i, i ^ mask) for i in range(size)])  15.9 us
    ppermute x6, starting transfers between devices, from_ahead(): lax.ppermute(value, 'expert', [((i + steps) % size, i) for i in range(siz...  11.9 us
    concatenate x1, local copies, waits for them, and re-layouts, local(): held = jnp.concatenate([held, swap(held, 1)])  11.6 us
    ppermute x6, waiting for transfers between devices, from_ahead(): lax.ppermute(value, 'expert', [((i + steps) % size, i) for i in range(siz...  7.48 us
    ppermute x10, starting transfers between devices, swap(): return lax.ppermute(value, 'tensor', [(i, i ^ mask) for i in range(size)])  6.65 us
    ppermute x3, local copies, waits for them, and re-layouts, from_ahead(): lax.ppermute(value, 'expert', [((i + steps) % size, i) for i in range(siz...  5.51 us
    dot_general x1, matrix products, local(): jnp.einsum('nd,dgf->ngf', rows, base_in[0], preferred_element_type=jnp.fl...  4.64 us
    ppermute x2, local copies, waits for them, and re-layouts, swap(): return lax.ppermute(value, 'tensor', [(i, i ^ mask) for i in range(size)])  3.71 us
  transfers between devices with their start and end apart: 16, of which 10 were waited for; matrix products, arithmetic and copies ran while one was open for 19% of the time, Pallas kernels for 0%

profile of v1, /device:TPU:0, one launch (start us, length us, event | category | flops | bytes accessed | tf_op | source)
XLA Modules:
  0.0 78.8 jit_solution(8656170264522296215)
XLA Ops:
  0.0 0.8 %convert_bitcast_fusion = (bf16[4,8]{1,0:T(4,128)(2,1)S(1)}, bf16[4,8]{1,0:T(4,128)(2,1)S(1)}) fusion(s32[1,4,8]{2,1,0:T(4,128)} %param.12, s32[1,4,8]{2,1,0:T(4,128)} %param.11), kind=kLoop, calls=%fused_computation.103 | loop fusion | flops 64 | bytes 384 | tf_op jit(solution)/shard_map/squeeze | solution.py:43
  0.8 0.1 fusion.62
  0.9 0.8 %pad_maximum_fusion.2 = bf16[4,7296]{1,0:T(4,128)(2,1)S(1)} fusion(bf16[4,128]{1,0:T(4,128)(2,1)S(1)} %fusion.62, bf16[4,7168]{1,0:T(4,128)(2,1)} %bitcast.96), kind=kLoop, calls=%fused_computation.40 | loop fusion | flops 116736 | bytes 116736 | tf_op jit(solution)/shard_map/concatenate | solution.py:45
  1.8 5.1 %collective-permute-start = (bf16[4,7296]{1,0:T(4,128)(2,1)S(1)}, bf16[4,7296]{1,0:T(4,128)(2,1)S(1)}, u32[]{:S(2)}, u32[]{:S(2)}) collective-permute-start(bf16[4,7296]{1,0:T(4,128)(2,1)S(1)} %pad_maximum_fusion.2), channel_id=1, source_target_pairs={{4,0},{8,4},{12,8},{0,12},{5,1},{9,5},{13,9},{1,13},{6,2},{10,6},{... | collective-permute-start | bytes 175112 | tf_op jit(solution)/shard_map/ppermute | solution.py:14
  6.9 1.0 %collective-permute-start.2 = (bf16[4,7296]{1,0:T(4,128)(2,1)S(1)}, bf16[4,7296]{1,0:T(4,128)(2,1)S(1)}, u32[]{:S(2)}, u32[]{:S(2)}) collective-permute-start(bf16[4,7296]{1,0:T(4,128)(2,1)S(1)} %pad_maximum_fusion.2), channel_id=1, source_target_pairs={{12,0},{0,4},{4,8},{8,12},{13,1},{1,5},{5,9},{9,13},{14,2},{2,6},{... | collective-permute-start | bytes 175112 | tf_op jit(solution)/shard_map/ppermute | solution.py:14
  7.9 1.3 %collective-permute-done = bf16[4,7296]{1,0:T(4,128)(2,1)S(1)} collective-permute-done((bf16[4,7296]{1,0:T(4,128)(2,1)S(1)}, bf16[4,7296]{1,0:T(4,128)(2,1)S(1)}, u32[]{:S(2)}, u32[]{:S(2)}) %collective-permute-start) | collective-permute-done | bytes 58400 | tf_op jit(solution)/shard_map/ppermute | solution.py:14
  9.2 2.9 %collective-permute-done.1 = bf16[4,7296]{1,0:T(4,128)(2,1)S(1)} collective-permute-done((bf16[4,7296]{1,0:T(4,128)(2,1)S(1)}, bf16[4,7296]{1,0:T(4,128)(2,1)S(1)}, u32[]{:S(2)}, u32[]{:S(2)}) %collective-permute-start.1) | collective-permute-done | bytes 58400 | tf_op jit(solution)/shard_map/ppermute | solution.py:14
  12.1 0.8 collective-permute-done.2
  12.9 1.0 %pad_maximum_fusion = bf16[16,7296]{1,0:T(8,128)(2,1)S(1)} fusion(bf16[4,7296]{1,0:T(4,128)(2,1)S(1)} %collective-permute-done.2, bf16[4,7296]{1,0:T(4,128)(2,1)S(1)} %collective-permute-done.1, bf16[4,7296]{1,0:T(4,128)(2,1)S(1)} %collective-permute-done, bf16[4,128]{1,0:T(4,128)(2,1)S(1)} %fusion.62, bf16[4,7168]{1,0:T(4,128)(2,1)} %bitcast.97), kind=kLoop, calls=%fused_computation.25 | loop fusion | flops 1167360 | bytes 466944 | tf_op jit(solution)/shard_map/concatenate | solution.py:47
  13.8 1.6 %collective-permute-start.3 = (bf16[16,7296]{1,0:T(8,128)(2,1)S(1)}, bf16[16,7296]{1,0:T(8,128)(2,1)S(1)}, u32[]{:S(2)}, u32[]{:S(2)}) collective-permute-start(bf16[16,7296]{1,0:T(8,128)(2,1)S(1)} %pad_maximum_fusion), channel_id=1, source_target_pairs={{0,2},{1,3},{2,0},{3,1},{4,6},{5,7},{6,4},{7,5},{8,10},{9,11},{10,... | collective-permute-start | bytes 700424 | tf_op jit(solution)/shard_map/ppermute | solution.py:19
  15.4 4.6 %collective-permute-done.3 = bf16[16,7296]{1,0:T(8,128)(2,1)S(1)} collective-permute-done((bf16[16,7296]{1,0:T(8,128)(2,1)S(1)}, bf16[16,7296]{1,0:T(8,128)(2,1)S(1)}, u32[]{:S(2)}, u32[]{:S(2)}) %collective-permute-start.3) | collective-permute-done | bytes 233504 | tf_op jit(solution)/shard_map/ppermute | solution.py:19
  20.0 0.3 concatenate.85
  20.2 0.1 collective-permute-start.4
  20.3 1.9 %copy.26 = bf16[4,7296]{0,1:T(8,128)(2,1)} copy(bf16[4,7296]{1,0:T(4,128)(2,1)S(1)} %pad_maximum_fusion.2) | data formatting | bytes 116736 | tf_op jit(solution)/shard_map/concatenate | solution.py:45
  22.2 1.8 %copy.27 = bf16[4,7296]{0,1:T(8,128)(2,1)} copy(bf16[4,7296]{1,0:T(4,128)(2,1)S(1)} %collective-permute-done) | data formatting | bytes 116736 | tf_op jit(solution)/shard_map/ppermute | solution.py:14
  24.1 1.9 %copy.28 = bf16[4,7296]{0,1:T(8,128)(2,1)} copy(bf16[4,7296]{1,0:T(4,128)(2,1)S(1)} %collective-permute-done.1) | data formatting | bytes 116736 | tf_op jit(solution)/shard_map/ppermute | solution.py:14
  25.9 1.8 %copy.29 = bf16[4,7296]{0,1:T(8,128)(2,1)} copy(bf16[4,7296]{1,0:T(4,128)(2,1)S(1)} %collective-permute-done.2) | data formatting | bytes 116736 | tf_op jit(solution)/shard_map/ppermute | solution.py:14
  27.7 1.9 %copy.30 = bf16[16,7296]{0,1:T(8,128)(2,1)} copy(bf16[16,7296]{1,0:T(8,128)(2,1)S(1)} %collective-permute-done.3) | data formatting | bytes 466944 | tf_op jit(solution)/shard_map/ppermute | solution.py:19
  29.6 1.8 %copy.31 = bf16[32,7296]{0,1:T(8,128)(2,1)} copy(bf16[32,7296]{1,0:T(8,128)(2,1)S(1)} %collective-permute-done.4) | data formatting | bytes 933888 | tf_op jit(solution)/shard_map/ppermute | solution.py:19
  31.4 11.6 %concatenate.86 = bf16[64,7296]{0,1:T(8,128)(2,1)} concatenate(bf16[4,7296]{0,1:T(8,128)(2,1)} %copy.26, bf16[4,7296]{0,1:T(8,128)(2,1)} %copy.27, bf16[4,7296]{0,1:T(8,128)(2,1)} %copy.28, bf16[4,7296]{0,1:T(8,128)(2,1)} %copy.29, bf16[16,7296]{0,1:T(8,128)(2,1)} %copy.30, bf16[32,7296]{0,1:T(8,128)(2,1)} %copy.31), dimensions={0} | concatenate | bytes 1867776 | tf_op jit(solution)/shard_map/concatenate | solution.py:49
  43.1 2.8 %fusion.11 = bf16[64,128]{1,0:T(8,128)(2,1)S(1)} fusion(bf16[1,7168,128]{2,1,0:T(8,128)(2,1)} %param.16, bf16[64,7296]{0,1:T(8,128)(2,1)} %concatenate.86), kind=kOutput, calls=%fused_computation.13 | convolution fusion | flops 117448704 | bytes 3686400 | tf_op jit(solution)/shard_map/dot_general | solution.py:61
  45.9 0.5 collective-permute-start.5
  46.4 1.5 %collective-permute-start.6 = (bf16[64,128]{1,0:T(8,128)(2,1)S(1)}, bf16[64,128]{1,0:T(8,128)(2,1)S(1)}, u32[]{:S(2)}, u32[]{:S(2)}) collective-permute-start(bf16[64,128]{1,0:T(8,128)(2,1)S(1)} %fusion.11), channel_id=1, source_target_pairs={{0,2},{1,3},{2,0},{3,1},{4,6},{5,7},{6,4},{7,5},{8,10},{9,11},{10,... | collective-permute-start | bytes 49160 | tf_op jit(solution)/shard_map/ppermute | solution.py:19
  48.0 4.6 %fusion.1 = f32[64,2,256]{2,0,1:T(8,128)S(1)} fusion(bf16[7168,2,256]{2,1,0:T(2,128)(2,1)} %bitcast.99, bf16[64,7296]{0,1:T(8,128)(2,1)S(1)} %copy-done.1), kind=kOutput, calls=%fused_computation.2 | convolution fusion | flops 469762048 | bytes 9306112 | tf_op jit(solution)/shard_map/nd,dgf->ngf/dot_general | solution.py:75
  52.7 0.1 select_reduce_fusion
  52.8 0.1 select_reduce_fusion.1
  53.0 0.2 fusion.16
  53.2 0.1 multiply_reduce_fusion
  53.3 0.2 copy-done.4
  53.6 0.2 convolution_convert_fusion
  53.8 1.8 %collective-permute-start.10 = (bf16[64,128]{1,0:T(8,128)(2,1)S(1)}, bf16[64,128]{1,0:T(8,128)(2,1)S(1)}, u32[]{:S(2)}, u32[]{:S(2)}) collective-permute-start(bf16[64,128]{1,0:T(8,128)(2,1)S(1)} %get-tuple-element.12), channel_id=1, source_target_pairs={{0,3},{1,2},{2,1},{3,0},{4,7},{5,6},{6,5},{7,4},{8,11},{9,10},{10,... | collective-permute-start | bytes 49160 | tf_op jit(solution)/shard_map/ppermute | solution.py:19
  55.6 0.5 collective-permute-start.9
  56.1 0.8 fusion.3
  56.9 0.1 collective-permute-done.10
  57.0 2.3 %collective-permute-done.9 = bf16[64,128]{1,0:T(8,128)(2,1)S(1)} collective-permute-done((bf16[64,128]{1,0:T(8,128)(2,1)S(1)}, bf16[64,128]{1,0:T(8,128)(2,1)S(1)}, u32[]{:S(2)}, u32[]{:S(2)}) %collective-permute-start.9) | collective-permute-done | bytes 16416 | tf_op jit(solution)/shard_map/ppermute | solution.py:19
  59.4 0.5 fusion
  59.9 0.1 collective-permute-start.11
  60.0 1.8 %collective-permute-done.11 = bf16[32,7168]{1,0:T(8,128)(2,1)S(1)} collective-permute-done((bf16[32,7168]{1,0:T(8,128)(2,1)S(1)}, bf16[32,7168]{1,0:T(8,128)(2,1)S(1)}, u32[]{:S(2)}, u32[]{:S(2)}) %collective-permute-start.11) | collective-permute-done | bytes 458784 | tf_op jit(solution)/shard_map/ppermute | solution.py:19
  61.8 0.1 add_convert_fusion
  61.9 0.6 collective-permute-start.12
  62.5 7.1 %collective-permute-done.12 = bf16[16,7168]{1,0:T(8,128)(2,1)S(1)} collective-permute-done((bf16[16,7168]{1,0:T(8,128)(2,1)S(1)}, bf16[16,7168]{1,0:T(8,128)(2,1)S(1)}, u32[]{:S(2)}, u32[]{:S(2)}) %collective-permute-start.12) | collective-permute-done | bytes 229408 | tf_op jit(solution)/shard_map/ppermute | solution.py:19
  69.7 0.1 fusion.67
  69.8 0.9 %collective-permute-start.13 = (bf16[4,7168]{1,0:T(4,128)(2,1)S(1)}, bf16[4,7168]{1,0:T(4,128)(2,1)S(1)}, u32[]{:S(2)}, u32[]{:S(2)}) collective-permute-start(bf16[4,7168]{1,0:T(4,128)(2,1)S(1)} %get-tuple-element.7), channel_id=1, source_target_pairs={{12,0},{0,4},{4,8},{8,12},{13,1},{1,5},{5,9},{9,13},{14,2},{2,6},{... | collective-permute-start | bytes 172040 | tf_op jit(solution)/shard_map/ppermute | solution.py:14
  70.7 2.0 %collective-permute-start.14 = (bf16[4,7168]{1,0:T(4,128)(2,1)S(1)}, bf16[4,7168]{1,0:T(4,128)(2,1)S(1)}, u32[]{:S(2)}, u32[]{:S(2)}) collective-permute-start(bf16[4,7168]{1,0:T(4,128)(2,1)S(1)} %get-tuple-element.9), channel_id=1, source_target_pairs={{8,0},{12,4},{0,8},{4,12},{9,1},{13,5},{1,9},{5,13},{10,2},{14,6},... | collective-permute-start | bytes 172040 | tf_op jit(solution)/shard_map/ppermute | solution.py:14
  72.7 2.8 %collective-permute-start.15 = (bf16[4,7168]{1,0:T(4,128)(2,1)S(1)}, bf16[4,7168]{1,0:T(4,128)(2,1)S(1)}, u32[]{:S(2)}, u32[]{:S(2)}) collective-permute-start(bf16[4,7168]{1,0:T(4,128)(2,1)S(1)} %get-tuple-element.8), channel_id=1, source_target_pairs={{4,0},{8,4},{12,8},{0,12},{5,1},{9,5},{13,9},{1,13},{6,2},{10,6},{... | collective-permute-start | bytes 172040 | tf_op jit(solution)/shard_map/ppermute | solution.py:14
  75.6 1.0 %collective-permute-done.13 = bf16[4,7168]{1,0:T(4,128)(2,1)S(1)} collective-permute-done((bf16[4,7168]{1,0:T(4,128)(2,1)S(1)}, bf16[4,7168]{1,0:T(4,128)(2,1)S(1)}, u32[]{:S(2)}, u32[]{:S(2)}) %collective-permute-start.13) | collective-permute-done | bytes 57376 | tf_op jit(solution)/shard_map/ppermute | solution.py:14
  76.6 1.5 %collective-permute-done.14 = bf16[4,7168]{1,0:T(4,128)(2,1)S(1)} collective-permute-done((bf16[4,7168]{1,0:T(4,128)(2,1)S(1)}, bf16[4,7168]{1,0:T(4,128)(2,1)S(1)}, u32[]{:S(2)}, u32[]{:S(2)}) %collective-permute-start.14) | collective-permute-done | bytes 57376 | tf_op jit(solution)/shard_map/ppermute | solution.py:14
  78.1 0.7 fusion.29
  (41 shorter events, 0.3 us)
Async XLA Ops:
  0.0 59.3 %copy-start = (bf16[1,128,7168]{2,1,0:T(8,128)(2,1)S(1)}, bf16[1,128,7168]{2,1,0:T(8,128)(2,1)}, u32[]{:S(2)}) copy-start(bf16[1,128,7168]{2,1,0:T(8,128)(2,1)} %param.19) | copy-start | bytes 5505028
  1.8 7.4 %collective-permute-start = (bf16[4,7296]{1,0:T(4,128)(2,1)S(1)}, bf16[4,7296]{1,0:T(4,128)(2,1)S(1)}, u32[]{:S(2)}, u32[]{:S(2)}) collective-permute-start(bf16[4,7296]{1,0:T(4,128)(2,1)S(1)} %pad_maximum_fusion.2), channel_id=1, source_target_pairs={{4,0},{8,4},{12,8},{0,12},{5,1},{9,5},{13,9},{1,13},{6,2},{10,6},{... | collective-permute-start | bytes 175112 | tf_op jit(solution)/shard_map/ppermute | solution.py:14
  6.9 5.2 %collective-permute-start.1 = (bf16[4,7296]{1,0:T(4,128)(2,1)S(1)}, bf16[4,7296]{1,0:T(4,128)(2,1)S(1)}, u32[]{:S(2)}, u32[]{:S(2)}) collective-permute-start(bf16[4,7296]{1,0:T(4,128)(2,1)S(1)} %pad_maximum_fusion.2), channel_id=1, source_target_pairs={{8,0},{12,4},{0,8},{4,12},{9,1},{13,5},{1,9},{5,13},{10,2},{14,6},... | collective-permute-start | bytes 175112 | tf_op jit(solution)/shard_map/ppermute | solution.py:14
  6.9 6.0 %collective-permute-start.2 = (bf16[4,7296]{1,0:T(4,128)(2,1)S(1)}, bf16[4,7296]{1,0:T(4,128)(2,1)S(1)}, u32[]{:S(2)}, u32[]{:S(2)}) collective-permute-start(bf16[4,7296]{1,0:T(4,128)(2,1)S(1)} %pad_maximum_fusion.2), channel_id=1, source_target_pairs={{12,0},{0,4},{4,8},{8,12},{13,1},{1,5},{5,9},{9,13},{14,2},{2,6},{... | collective-permute-start | bytes 175112 | tf_op jit(solution)/shard_map/ppermute | solution.py:14
  13.8 6.1 %collective-permute-start.3 = (bf16[16,7296]{1,0:T(8,128)(2,1)S(1)}, bf16[16,7296]{1,0:T(8,128)(2,1)S(1)}, u32[]{:S(2)}, u32[]{:S(2)}) collective-permute-start(bf16[16,7296]{1,0:T(8,128)(2,1)S(1)} %pad_maximum_fusion), channel_id=1, source_target_pairs={{0,2},{1,3},{2,0},{3,1},{4,6},{5,7},{6,4},{7,5},{8,10},{9,11},{10,... | collective-permute-start | bytes 700424 | tf_op jit(solution)/shard_map/ppermute | solution.py:19
  20.2 9.4 %collective-permute-start.4 = (bf16[32,7296]{1,0:T(8,128)(2,1)S(1)}, bf16[32,7296]{1,0:T(8,128)(2,1)S(1)}, u32[]{:S(2)}, u32[]{:S(2)}) collective-permute-start(bf16[32,7296]{1,0:T(8,128)(2,1)S(1)} %concatenate.85), channel_id=1, source_target_pairs={{0,1},{1,0},{2,3},{3,2},{4,5},{5,4},{6,7},{7,6},{8,9},{9,8},{10,11... | collective-permute-start | bytes 1400840 | tf_op jit(solution)/shard_map/ppermute | solution.py:19
  43.1 4.8 %copy-start.1 = (bf16[64,7296]{0,1:T(8,128)(2,1)S(1)}, bf16[64,7296]{0,1:T(8,128)(2,1)}, u32[]{:S(2)}) copy-start(bf16[64,7296]{0,1:T(8,128)(2,1)} %concatenate.86) | copy-start | bytes 2801668
  45.9 7.0 %collective-permute-start.5 = (bf16[64,128]{1,0:T(8,128)(2,1)S(1)}, bf16[64,128]{1,0:T(8,128)(2,1)S(1)}, u32[]{:S(2)}, u32[]{:S(2)}) collective-permute-start(bf16[64,128]{1,0:T(8,128)(2,1)S(1)} %fusion.11), channel_id=1, source_target_pairs={{0,1},{1,0},{2,3},{3,2},{4,5},{5,4},{6,7},{7,6},{8,9},{9,8},{10,11... | collective-permute-start | bytes 49160 | tf_op jit(solution)/shard_map/ppermute | solution.py:19
  46.4 6.5 %collective-permute-start.6 = (bf16[64,128]{1,0:T(8,128)(2,1)S(1)}, bf16[64,128]{1,0:T(8,128)(2,1)S(1)}, u32[]{:S(2)}, u32[]{:S(2)}) collective-permute-start(bf16[64,128]{1,0:T(8,128)(2,1)S(1)} %fusion.11), channel_id=1, source_target_pairs={{0,2},{1,3},{2,0},{3,1},{4,6},{5,7},{6,4},{7,5},{8,10},{9,11},{10,... | collective-permute-start | bytes 49160 | tf_op jit(solution)/shard_map/ppermute | solution.py:19
  47.9 5.0 %collective-permute-start.7 = (bf16[64,128]{1,0:T(8,128)(2,1)S(1)}, bf16[64,128]{1,0:T(8,128)(2,1)S(1)}, u32[]{:S(2)}, u32[]{:S(2)}) collective-permute-start(bf16[64,128]{1,0:T(8,128)(2,1)S(1)} %fusion.11), channel_id=1, source_target_pairs={{0,3},{1,2},{2,1},{3,0},{4,7},{5,6},{6,5},{7,4},{8,11},{9,10},{10,... | collective-permute-start | bytes 49160 | tf_op jit(solution)/shard_map/ppermute | solution.py:19
  47.9 4.7 %copy-start.5 = (s32[16]{0:T(128)S(1)}, s32[16]{0:T(128)}, u32[]{:S(2)}) copy-start(s32[16]{0:T(128)} %param.13) | copy-start | bytes 196
  48.0 5.0 %copy-start.3 = (bf16[1,4,128,2,256]{4,3,2,1,0:T(2,128)(2,1)S(1)}, bf16[1,4,128,2,256]{4,3,2,1,0:T(2,128)(2,1)}, u32[]{:S(2)}) copy-start(bf16[1,4,128,2,256]{4,3,2,1,0:T(2,128)(2,1)} %param.17) | copy-start | bytes 1572868
  48.0 8.2 %copy-start.2 = (bf16[1,256,7168]{2,1,0:T(8,128)(2,1)S(1)}, bf16[1,256,7168]{2,1,0:T(8,128)(2,1)}, u32[]{:S(2)}) copy-start(bf16[1,256,7168]{2,1,0:T(8,128)(2,1)} %param.15) | copy-start | bytes 11010052
  52.6 1.0 %copy-start.4 = (bf16[1,4,256,128]{3,2,1,0:T(8,128)(2,1)S(1)}, bf16[1,4,256,128]{3,2,1,0:T(8,128)(2,1)}, u32[]{:S(2)}) copy-start(bf16[1,4,256,128]{3,2,1,0:T(8,128)(2,1)} %param.18) | copy-start | bytes 786436
  53.8 3.3 %collective-permute-start.10 = (bf16[64,128]{1,0:T(8,128)(2,1)S(1)}, bf16[64,128]{1,0:T(8,128)(2,1)S(1)}, u32[]{:S(2)}, u32[]{:S(2)}) collective-permute-start(bf16[64,128]{1,0:T(8,128)(2,1)S(1)} %get-tuple-element.12), channel_id=1, source_target_pairs={{0,3},{1,2},{2,1},{3,0},{4,7},{5,6},{6,5},{7,4},{8,11},{9,10},{10,... | collective-permute-start | bytes 49160 | tf_op jit(solution)/shard_map/ppermute | solution.py:19
  55.6 3.7 %collective-permute-start.9 = (bf16[64,128]{1,0:T(8,128)(2,1)S(1)}, bf16[64,128]{1,0:T(8,128)(2,1)S(1)}, u32[]{:S(2)}, u32[]{:S(2)}) collective-permute-start(bf16[64,128]{1,0:T(8,128)(2,1)S(1)} %get-tuple-element.13), channel_id=1, source_target_pairs={{0,2},{1,3},{2,0},{3,1},{4,6},{5,7},{6,4},{7,5},{8,10},{9,11},{10,... | collective-permute-start | bytes 49160 | tf_op jit(solution)/shard_map/ppermute | solution.py:19
  56.1 3.2 %collective-permute-start.8 = (bf16[64,128]{1,0:T(8,128)(2,1)S(1)}, bf16[64,128]{1,0:T(8,128)(2,1)S(1)}, u32[]{:S(2)}, u32[]{:S(2)}) collective-permute-start(bf16[64,128]{1,0:T(8,128)(2,1)S(1)} %get-tuple-element.14), channel_id=1, source_target_pairs={{0,1},{1,0},{2,3},{3,2},{4,5},{5,4},{6,7},{7,6},{8,9},{9,8},{10,11... | collective-permute-start | bytes 49160 | tf_op jit(solution)/shard_map/ppermute | solution.py:19
  59.9 1.9 %collective-permute-start.11 = (bf16[32,7168]{1,0:T(8,128)(2,1)S(1)}, bf16[32,7168]{1,0:T(8,128)(2,1)S(1)}, u32[]{:S(2)}, u32[]{:S(2)}) collective-permute-start(bf16[32,7168]{1,0:T(8,128)(2,1)S(1)} %slice.212), channel_id=1, source_target_pairs={{0,1},{1,0},{2,3},{3,2},{4,5},{5,4},{6,7},{7,6},{8,9},{9,8},{10,11... | collective-permute-start | bytes 1376264 | tf_op jit(solution)/shard_map/ppermute | solution.py:19
  61.9 7.7 %collective-permute-start.12 = (bf16[16,7168]{1,0:T(8,128)(2,1)S(1)}, bf16[16,7168]{1,0:T(8,128)(2,1)S(1)}, u32[]{:S(2)}, u32[]{:S(2)}) collective-permute-start(bf16[16,7168]{1,0:T(8,128)(2,1)S(1)} %slice.214), channel_id=1, source_target_pairs={{0,2},{1,3},{2,0},{3,1},{4,6},{5,7},{6,4},{7,5},{8,10},{9,11},{10,... | collective-permute-start | bytes 688136 | tf_op jit(solution)/shard_map/ppermute | solution.py:19
  69.8 6.8 %collective-permute-start.13 = (bf16[4,7168]{1,0:T(4,128)(2,1)S(1)}, bf16[4,7168]{1,0:T(4,128)(2,1)S(1)}, u32[]{:S(2)}, u32[]{:S(2)}) collective-permute-start(bf16[4,7168]{1,0:T(4,128)(2,1)S(1)} %get-tuple-element.7), channel_id=1, source_target_pairs={{12,0},{0,4},{4,8},{8,12},{13,1},{1,5},{5,9},{9,13},{14,2},{2,6},{... | collective-permute-start | bytes 172040 | tf_op jit(solution)/shard_map/ppermute | solution.py:14
  70.7 7.3 %collective-permute-start.14 = (bf16[4,7168]{1,0:T(4,128)(2,1)S(1)}, bf16[4,7168]{1,0:T(4,128)(2,1)S(1)}, u32[]{:S(2)}, u32[]{:S(2)}) collective-permute-start(bf16[4,7168]{1,0:T(4,128)(2,1)S(1)} %get-tuple-element.9), channel_id=1, source_target_pairs={{8,0},{12,4},{0,8},{4,12},{9,1},{13,5},{1,9},{5,13},{10,2},{14,6},... | collective-permute-start | bytes 172040 | tf_op jit(solution)/shard_map/ppermute | solution.py:14
  72.7 5.4 %collective-permute-start.15 = (bf16[4,7168]{1,0:T(4,128)(2,1)S(1)}, bf16[4,7168]{1,0:T(4,128)(2,1)S(1)}, u32[]{:S(2)}, u32[]{:S(2)}) collective-permute-start(bf16[4,7168]{1,0:T(4,128)(2,1)S(1)} %get-tuple-element.8), channel_id=1, source_target_pairs={{4,0},{8,4},{12,8},{0,12},{5,1},{9,5},{13,9},{1,13},{6,2},{10,6},{... | collective-permute-start | bytes 172040 | tf_op jit(solution)/shard_map/ppermute | solution.py:14

commit v2 on v1

--- a/solution.py
+++ b/solution.py
@@ -1,7 +1,14 @@
 import jax
 import jax.numpy as jnp
 from jax import lax
+from jax.experimental.layout import Layout, with_layout_constraint
 from jax.sharding import PartitionSpec as P
+
+CHUNKS = 2
+
+
+def by_rows(value):
+    return with_layout_constraint(value, Layout((0, 1)))
 
 
 def lookup(table, index):
@@ -40,16 +47,21 @@
     top = routes.shape[2]
     group = clusters * count
 
+    chunk = width // CHUNKS
     side = jnp.concatenate([routes[0], numerators[0]], axis=1).astype(jnp.bfloat16)
     side = jnp.pad(side, ((0, 0), (0, 128 - 2 * top)))
-    packed = jnp.concatenate([tokens[0], side], axis=1)
+    pieces = [tokens[0][:, c * chunk : (c + 1) * chunk] for c in range(CHUNKS)]
+    pieces[0] = jnp.concatenate([pieces[0], side], axis=1)
 
-    held = jnp.concatenate([packed] + [from_ahead(packed, k) for k in range(1, clusters)])
-    held = jnp.concatenate([held] + [swap(held, 2 * m) for m in range(1, chips)])
-    held = jnp.concatenate([held, swap(held, 1)])
-    rows = held[:, :width]
-    all_routes = held[:, width : width + top].astype(jnp.int32)
-    numerator = held[:, width + top : width + 2 * top].astype(jnp.float32)
+    gathered = []
+    for piece in pieces:
+        held = jnp.concatenate([piece] + [from_ahead(piece, k) for k in range(1, clusters)])
+        held = jnp.concatenate([held] + [swap(held, 2 * m) for m in range(1, chips)])
+        gathered.append(by_rows(jnp.concatenate([held, swap(held, 1)])))
+    side = by_rows(gathered[0][:, chunk:])
+    rows = [held[:, :chunk] for held in gathered]
+    all_routes = side[:, :top].astype(jnp.int32)
+    numerator = side[:, top : 2 * top].astype(jnp.float32)
 
     position = lookup(place, all_routes)
     weight = (2.5 * numerator / jnp.sum(numerator, axis=-1, keepdims=True)).astype(jnp.bfloat16)
@@ -58,7 +70,10 @@
         jnp.where(position[None] == target[:, None, None], weight[None].astype(jnp.float32), 0.0), axis=-1
     )
 
-    codes = jnp.dot(rows, delta_in[0], preferred_element_type=jnp.float32).astype(jnp.bfloat16)
+    codes = sum(
+        jnp.dot(rows[c], delta_in[0, c * chunk : (c + 1) * chunk], preferred_element_type=jnp.float32)
+        for c in range(CHUNKS)
+    ).astype(jnp.bfloat16)
 
     def block_of(m):
         return (m % 2) * chips + m // 2
@@ -72,7 +87,12 @@
     shared = jnp.stack([reorder(codes if m == 0 else swap(codes, m), m) for m in range(members)])
     by_slot = jnp.stack([lax.dynamic_index_in_dim(shared, s ^ me, 0, keepdims=False) for s in range(members)])
 
-    projected = jnp.einsum("nd,dgf->ngf", rows, base_in[0], preferred_element_type=jnp.float32)
+    projected = sum(
+        jnp.einsum(
+            "nd,dgf->ngf", rows[c], base_in[0, c * chunk : (c + 1) * chunk], preferred_element_type=jnp.float32
+        )
+        for c in range(CHUNKS)
+    )
     lifted = jnp.einsum("srk,skgf->srgf", by_slot, delta_mid[0], preferred_element_type=jnp.float32)
     hidden = jax.nn.silu(projected[None, :, 0] + lifted[:, :, 0]) * (
         projected[None, :, 1] + lifted[:, :, 1]
@@ -88,20 +108,24 @@
     own_scale = lax.dynamic_index_in_dim(scale, me, 0, keepdims=False)
     scaled = (own_scale[:, None] * lowrank).astype(jnp.bfloat16)
 
-    term = jnp.dot(hidden_sum, base_down[0], preferred_element_type=jnp.float32)
-    term = (term + jnp.dot(scaled, delta_back[0], preferred_element_type=jnp.float32)).astype(jnp.bfloat16)
-
     half = chips * group
-    total = (term[:half].astype(jnp.float32) + swap(term[half:], 1).astype(jnp.float32)).astype(jnp.bfloat16)
-    parts = total.reshape(chips, group, width)
-    total = parts[0].astype(jnp.float32)
-    for m in range(1, chips):
-        total = total + swap(parts[m], 2 * m).astype(jnp.float32)
-    parts = total.astype(jnp.bfloat16).reshape(clusters, count, width)
-    mixed = parts[0].astype(jnp.float32)
-    for k in range(1, clusters):
-        mixed = mixed + from_ahead(parts[k], clusters - k).astype(jnp.float32)
-    return mixed.astype(jnp.bfloat16)[None]
+    outputs = []
+    for c in range(CHUNKS):
+        columns = slice(c * chunk, (c + 1) * chunk)
+        term = jnp.dot(hidden_sum, base_down[0, :, columns], preferred_element_type=jnp.float32)
+        term = term + jnp.dot(scaled, delta_back[0, :, columns], preferred_element_type=jnp.float32)
+        term = term.astype(jnp.bfloat16)
+        total = (term[:half].astype(jnp.float32) + swap(term[half:], 1).astype(jnp.float32)).astype(jnp.bfloat16)
+        parts = total.reshape(chips, group, chunk)
+        total = parts[0].astype(jnp.float32)
+        for m in range(1, chips):
+            total = total + swap(parts[m], 2 * m).astype(jnp.float32)
+        parts = total.astype(jnp.bfloat16).reshape(clusters, count, chunk)
+        mixed = parts[0].astype(jnp.float32)
+        for k in range(1, clusters):
+            mixed = mixed + from_ahead(parts[k], clusters - k).astype(jnp.float32)
+        outputs.append(mixed.astype(jnp.bfloat16))
+    return jnp.concatenate(outputs, axis=1)[None]
 
 
 def solution(mesh):

time: 79.3 us -> 66.7 us (0.84)
  local copies, waits for them, and re-layouts: 23.5 us -> 11.2 us
  waiting for transfers between devices: 23.4 us -> 12.2 us
  starting transfers between devices: 18.5 us -> 29.6 us
  other arithmetic: 3.92 us -> 2.44 us
  matrix products: 9.12 us -> 10.4 us
    concatenate x2, local copies, waits for them, and re-layouts: 13.5 us -> 2.18 us  [local(): gathered.append(by_rows(jnp.concatenate([held, swap(held, 1)])))]
    ppermute x10 -> x14, waiting for transfers between devices: 15.9 us -> 6.68 us  [swap(): return lax.ppermute(value, 'tensor', [(i, i ^ mask) for i in range(size)])]
    ppermute x5 -> x0, local copies, waits for them, and re-layouts: 9.22 us -> none  [the longest x3 5.51 us: from_ahead(): lax.ppermute(value, 'expert', [((i + steps) % size, i) for i in range(siz...]
    slice x0 -> x2, local copies, waits for them, and re-layouts: none -> 8.48 us  [the longest x1 7.64 us: local(): base_in[0, c * chunk:(c + 1) * chunk]]
    ppermute x6 -> x12, starting transfers between devices: 11.9 us -> 19 us  [from_ahead(): lax.ppermute(value, 'expert', [((i + steps) % size, i) for i in range(siz...]
    ppermute x10 -> x14, starting transfers between devices: 6.65 us -> 10.6 us  [swap(): return lax.ppermute(value, 'tensor', [(i, i ^ mask) for i in range(size)])]
    ppermute x6 -> x12, waiting for transfers between devices: 7.48 us -> 5.55 us  [from_ahead(): lax.ppermute(value, 'expert', [((i + steps) % size, i) for i in range(siz...]
    concatenate x2 -> x3, other arithmetic: 1.8 us -> 0.17 us  [the longest x2 0.15 us: local(): jnp.concatenate([piece] + [from_ahead(piece, k) for k in range(1, cluster...]
  transfers between devices with their start and end apart: 16 -> 26, of which waited for: 10 -> 8; matrix products, arithmetic and copies ran while one was open for 19% -> 30% of each run, Pallas kernels for 0% -> 0%
where the time goes in v2:
time: 66.7 us; the launch traced here: 66.3 us
  starting transfers between devices  29.6 us (44%)
  waiting for transfers between devices  12.2 us (18%)
  local copies, waits for them, and re-layouts  11.2 us (17%)
  matrix products  10.4 us (16%)
  other arithmetic  2.44 us (4%)
    ppermute x12, starting transfers between devices, from_ahead(): lax.ppermute(value, 'expert', [((i + steps) % size, i) for i in range(siz...  19 us
    ppermute x14, starting transfers between devices, swap(): return lax.ppermute(value, 'tensor', [(i, i ^ mask) for i in range(size)])  10.6 us
    slice x1, local copies, waits for them, and re-layouts, local(): base_in[0, c * chunk:(c + 1) * chunk]  7.64 us
    ppermute x14, waiting for transfers between devices, swap(): return lax.ppermute(value, 'tensor', [(i, i ^ mask) for i in range(size)])  6.68 us
    dot_general x2, matrix products, local(): jnp.einsum('nd,dgf->ngf', rows[c], base_in[0, c * chunk:(c + 1) * chunk],...  6.29 us
    ppermute x12, waiting for transfers between devices, from_ahead(): lax.ppermute(value, 'expert', [((i + steps) % size, i) for i in range(siz...  5.55 us
    dot_general x2, matrix products, local(): jnp.dot(hidden_sum, base_down[0, :, columns], preferred_element_type=jnp....  2.44 us
    concatenate x2, local copies, waits for them, and re-layouts, local(): gathered.append(by_rows(jnp.concatenate([held, swap(held, 1)])))  2.18 us
  transfers between devices with their start and end apart: 26, of which 8 were waited for; matrix products, arithmetic and copies ran while one was open for 30% of the time, Pallas kernels for 0%

profile of v2, /device:TPU:0, one launch (start us, length us, event | category | flops | bytes accessed | tf_op | source)
XLA Modules:
  0.0 66.3 jit_solution(10970688656769671329)
XLA Ops:
  0.0 0.8 %fusion.55 = (bf16[4,3584]{1,0:T(4,128)(2,1)S(1)}, bf16[4,3584]{1,0:T(4,128)(2,1)S(1)}) fusion(bf16[4,7168]{1,0:T(4,128)(2,1)} %bitcast.116), kind=kLoop, calls=%fused_computation.109 | loop fusion | bytes 114688 | tf_op jit(solution)/shard_map/slice | solution.py:53
  0.8 5.1 %collective-permute-start.5 = (bf16[4,3584]{1,0:T(4,128)(2,1)S(1)}, bf16[4,3584]{1,0:T(4,128)(2,1)S(1)}, u32[]{:S(2)}, u32[]{:S(2)}) collective-permute-start(bf16[4,3584]{1,0:T(4,128)(2,1)S(1)} %get-tuple-element.24), channel_id=1, source_target_pairs={{4,0},{8,4},{12,8},{0,12},{5,1},{9,5},{13,9},{1,13},{6,2},{10,6},{... | collective-permute-start | bytes 86024 | tf_op jit(solution)/shard_map/ppermute | solution.py:21
  6.0 1.0 %collective-permute-start.7 = (bf16[4,3584]{1,0:T(4,128)(2,1)S(1)}, bf16[4,3584]{1,0:T(4,128)(2,1)S(1)}, u32[]{:S(2)}, u32[]{:S(2)}) collective-permute-start(bf16[4,3584]{1,0:T(4,128)(2,1)S(1)} %get-tuple-element.24), channel_id=1, source_target_pairs={{12,0},{0,4},{4,8},{8,12},{13,1},{1,5},{5,9},{9,13},{14,2},{2,6},{... | collective-permute-start | bytes 86024 | tf_op jit(solution)/shard_map/ppermute | solution.py:21
  7.0 0.7 %convert_bitcast_fusion = (bf16[4,8]{1,0:T(4,128)(2,1)S(1)}, bf16[4,8]{1,0:T(4,128)(2,1)S(1)}) fusion(s32[1,4,8]{2,1,0:T(4,128)} %param.12, s32[1,4,8]{2,1,0:T(4,128)} %param.11), kind=kLoop, calls=%fused_computation.101 | loop fusion | flops 64 | bytes 384 | tf_op jit(solution)/shard_map/squeeze | solution.py:51
  7.8 2.9 %collective-permute-start = (bf16[4,3712]{1,0:T(4,128)(2,1)S(1)}, bf16[4,3712]{1,0:T(4,128)(2,1)S(1)}, u32[]{:S(2)}, u32[]{:S(2)}) collective-permute-start(bf16[4,3712]{1,0:T(4,128)(2,1)S(1)} %pad_maximum_fusion.3), channel_id=1, source_target_pairs={{4,0},{8,4},{12,8},{0,12},{5,1},{9,5},{13,9},{1,13},{6,2},{10,6},{... | collective-permute-start | bytes 89096 | tf_op jit(solution)/shard_map/ppermute | solution.py:21
  10.6 1.1 %collective-permute-start.1 = (bf16[4,3712]{1,0:T(4,128)(2,1)S(1)}, bf16[4,3712]{1,0:T(4,128)(2,1)S(1)}, u32[]{:S(2)}, u32[]{:S(2)}) collective-permute-start(bf16[4,3712]{1,0:T(4,128)(2,1)S(1)} %pad_maximum_fusion.3), channel_id=1, source_target_pairs={{8,0},{12,4},{0,8},{4,12},{9,1},{13,5},{1,9},{5,13},{10,2},{14,6},... | collective-permute-start | bytes 89096 | tf_op jit(solution)/shard_map/ppermute | solution.py:21
  11.9 1.6 %collective-permute-start.8 = (bf16[16,3584]{1,0:T(8,128)(2,1)S(1)}, bf16[16,3584]{1,0:T(8,128)(2,1)S(1)}, u32[]{:S(2)}, u32[]{:S(2)}) collective-permute-start(bf16[16,3584]{1,0:T(8,128)(2,1)S(1)} %pad_maximum_fusion.1), channel_id=1, source_target_pairs={{0,2},{1,3},{2,0},{3,1},{4,6},{5,7},{6,4},{7,5},{8,10},{9,11},{10,... | collective-permute-start | bytes 344072 | tf_op jit(solution)/shard_map/ppermute | solution.py:26
  13.4 2.0 %collective-permute-done.1 = bf16[4,3712]{1,0:T(4,128)(2,1)S(1)} collective-permute-done((bf16[4,3712]{1,0:T(4,128)(2,1)S(1)}, bf16[4,3712]{1,0:T(4,128)(2,1)S(1)}, u32[]{:S(2)}, u32[]{:S(2)}) %collective-permute-start.1) | collective-permute-done | bytes 29728 | tf_op jit(solution)/shard_map/ppermute | solution.py:21
  15.4 2.0 %collective-permute-done.2 = bf16[4,3712]{1,0:T(4,128)(2,1)S(1)} collective-permute-done((bf16[4,3712]{1,0:T(4,128)(2,1)S(1)}, bf16[4,3712]{1,0:T(4,128)(2,1)S(1)}, u32[]{:S(2)}, u32[]{:S(2)}) %collective-permute-start.2) | collective-permute-done | bytes 29728 | tf_op jit(solution)/shard_map/ppermute | solution.py:21
  17.5 1.6 %collective-permute-start.3 = (bf16[16,3712]{1,0:T(8,128)(2,1)S(1)}, bf16[16,3712]{1,0:T(8,128)(2,1)S(1)}, u32[]{:S(2)}, u32[]{:S(2)}) collective-permute-start(bf16[16,3712]{1,0:T(8,128)(2,1)S(1)} %pad_maximum_fusion), channel_id=1, source_target_pairs={{0,2},{1,3},{2,0},{3,1},{4,6},{5,7},{6,4},{7,5},{8,10},{9,11},{10,... | collective-permute-start | bytes 356360 | tf_op jit(solution)/shard_map/ppermute | solution.py:26
  19.3 7.6 %fusion.52 = (bf16[1,3584,2,256]{3,2,1,0:T(2,128)(2,1)}, bf16[1,3584,2,256]{3,2,1,0:T(2,128)(2,1)}) fusion(bf16[1,7168,2,256]{3,2,1,0:T(2,128)(2,1)} %param.14), kind=kLoop, calls=%fused_computation.106 | loop fusion | bytes 14680064 | tf_op jit(solution)/shard_map/slice | solution.py:92
  26.9 0.1 concatenate.102
  27.0 0.6 collective-permute-start.4
  27.6 1.1 %concatenate.106 = bf16[64,3584]{1,0:T(8,128)(2,1)S(1)} concatenate(bf16[4,3584]{1,0:T(4,128)(2,1)S(1)} %get-tuple-element.24, bf16[4,3584]{1,0:T(4,128)(2,1)S(1)} %collective-permute-done.5, bf16[4,3584]{1,0:T(4,128)(2,1)S(1)} %collective-permute-done.6, bf16[4,3584]{1,0:T(4,128)(2,1)S(1)} %collective-permute-done.7, bf16[16,3584]{1,0:T(8,128)(2,1)S(1)} %collective-permute-done.8, ...), dimensions={0} | concatenate | bytes 917504 | tf_op jit(solution)/shard_map/concatenate | solution.py:60
  28.7 3.5 %fusion.2 = f32[64,2,256]{2,0,1:T(8,128)} fusion(bf16[1,3584,2,256]{3,2,1,0:T(2,128)(2,1)} %get-tuple-element.8, bf16[64,3584]{1,0:T(8,128)(2,1)S(1)} %concatenate.106), kind=kOutput, calls=%fused_computation.5 | convolution fusion | flops 234881024 | bytes 4259840 | tf_op jit(solution)/shard_map/nd,dgf->ngf/dot_general | solution.py:91
  32.1 0.3 fusion.14
  32.4 1.1 %concatenate.103 = bf16[64,3712]{1,0:T(8,128)(2,1)S(1)} concatenate(bf16[4,3712]{1,0:T(4,128)(2,1)S(1)} %pad_maximum_fusion.3, bf16[4,3712]{1,0:T(4,128)(2,1)S(1)} %collective-permute-done, bf16[4,3712]{1,0:T(4,128)(2,1)S(1)} %collective-permute-done.1, bf16[4,3712]{1,0:T(4,128)(2,1)S(1)} %collective-permute-done.2, bf16[16,3712]{1,0:T(8,128)(2,1)S(1)} %collective-permute-done.3, ...), dimensions={0} | concatenate | bytes 950272 | tf_op jit(solution)/shard_map/concatenate | solution.py:60
  33.6 0.3 fusion.11
  33.9 0.2 collective-permute-start.10
  34.1 0.5 collective-permute-start.11
  34.7 1.1 %collective-permute-start.12 = (bf16[64,128]{1,0:T(8,128)(2,1)S(1)}, bf16[64,128]{1,0:T(8,128)(2,1)S(1)}, u32[]{:S(2)}, u32[]{:S(2)}) collective-permute-start(bf16[64,128]{1,0:T(8,128)(2,1)S(1)} %fusion.11), channel_id=1, source_target_pairs={{0,3},{1,2},{2,1},{3,0},{4,7},{5,6},{6,5},{7,4},{8,11},{9,10},{10,... | collective-permute-start | bytes 49160 | tf_op jit(solution)/shard_map/ppermute | solution.py:26
  35.8 0.2 convert_reduce_fusion
  36.0 2.8 %fusion.10 = f32[64,2,256]{2,0,1:T(8,128)S(1)} fusion(f32[64,2,256]{2,0,1:T(8,128)} %fusion.2, bf16[1,3584,2,256]{3,2,1,0:T(2,128)(2,1)} %get-tuple-element.7, bf16[64,3712]{1,0:T(8,128)(2,1)S(1)} %concatenate.103), kind=kOutput, calls=%fused_computation.14 | convolution fusion | flops 234913792 | bytes 4390912 | tf_op jit(solution)/shard_map/nd,dgf->ngf/dot_general | solution.py:91
  39.5 0.2 fusion.21
  39.7 0.1 multiply_reduce_fusion
  39.8 0.2 convolution_convert_fusion
  40.0 0.7 %collective-permute-start.15 = (bf16[64,128]{1,0:T(8,128)(2,1)S(1)}, bf16[64,128]{1,0:T(8,128)(2,1)S(1)}, u32[]{:S(2)}, u32[]{:S(2)}) collective-permute-start(bf16[64,128]{1,0:T(8,128)(2,1)S(1)} %get-tuple-element.17), channel_id=1, source_target_pairs={{0,3},{1,2},{2,1},{3,0},{4,7},{5,6},{6,5},{7,4},{8,11},{9,10},{10,... | collective-permute-start | bytes 49160 | tf_op jit(solution)/shard_map/ppermute | solution.py:26
  40.7 2.0 %fusion.6 = f32[64,3584]{1,0:T(8,128)S(1)} fusion(bf16[1,256,7168]{2,1,0:T(8,128)(2,1)} %param.15, bf16[64,256]{1,0:T(8,128)(2,1)S(1)} %get-tuple-element.5), kind=kOutput, calls=%fused_computation.10 | convolution fusion | flops 117440512 | bytes 2785280 | tf_op jit(solution)/shard_map/dot_general | solution.py:115
  42.7 0.4 fusion.4
  43.1 1.5 %collective-permute-start.14 = (bf16[64,128]{1,0:T(8,128)(2,1)S(1)}, bf16[64,128]{1,0:T(8,128)(2,1)S(1)}, u32[]{:S(2)}, u32[]{:S(2)}) collective-permute-start(bf16[64,128]{1,0:T(8,128)(2,1)S(1)} %get-tuple-element.18), channel_id=1, source_target_pairs={{0,2},{1,3},{2,0},{3,1},{4,6},{5,7},{6,4},{7,5},{8,10},{9,11},{10,... | collective-permute-start | bytes 49160 | tf_op jit(solution)/shard_map/ppermute | solution.py:26
  44.7 2.3 %collective-permute-done.14 = bf16[64,128]{1,0:T(8,128)(2,1)S(1)} collective-permute-done((bf16[64,128]{1,0:T(8,128)(2,1)S(1)}, bf16[64,128]{1,0:T(8,128)(2,1)S(1)}, u32[]{:S(2)}, u32[]{:S(2)}) %collective-permute-start.14) | collective-permute-done | bytes 16416 | tf_op jit(solution)/shard_map/ppermute | solution.py:26
  47.0 0.3 fusion
  47.4 0.3 fusion.1
  47.8 0.6 collective-permute-start.21
  48.3 0.6 collective-permute-done.16
  49.0 1.5 %collective-permute-start.17 = (bf16[16,3584]{1,0:T(8,128)(2,1)S(1)}, bf16[16,3584]{1,0:T(8,128)(2,1)S(1)}, u32[]{:S(2)}, u32[]{:S(2)}) collective-permute-start(bf16[16,3584]{1,0:T(8,128)(2,1)S(1)} %slice.300), channel_id=1, source_target_pairs={{0,2},{1,3},{2,0},{3,1},{4,6},{5,7},{6,4},{7,5},{8,10},{9,11},{10,... | collective-permute-start | bytes 344072 | tf_op jit(solution)/shard_map/ppermute | solution.py:26
  50.6 0.7 collective-permute-start.22
  51.2 3.8 %collective-permute-done.17 = bf16[16,3584]{1,0:T(8,128)(2,1)S(1)} collective-permute-done((bf16[16,3584]{1,0:T(8,128)(2,1)S(1)}, bf16[16,3584]{1,0:T(8,128)(2,1)S(1)}, u32[]{:S(2)}, u32[]{:S(2)}) %collective-permute-start.17) | collective-permute-done | bytes 114720 | tf_op jit(solution)/shard_map/ppermute | solution.py:26
  55.1 1.1 %collective-permute-start.18 = (bf16[4,3584]{1,0:T(4,128)(2,1)S(1)}, bf16[4,3584]{1,0:T(4,128)(2,1)S(1)}, u32[]{:S(2)}, u32[]{:S(2)}) collective-permute-start(bf16[4,3584]{1,0:T(4,128)(2,1)S(1)} %get-tuple-element.11), channel_id=1, source_target_pairs={{12,0},{0,4},{4,8},{8,12},{13,1},{1,5},{5,9},{9,13},{14,2},{2,6},{... | collective-permute-start | bytes 86024 | tf_op jit(solution)/shard_map/ppermute | solution.py:21
  56.2 1.9 %collective-permute-start.19 = (bf16[4,3584]{1,0:T(4,128)(2,1)S(1)}, bf16[4,3584]{1,0:T(4,128)(2,1)S(1)}, u32[]{:S(2)}, u32[]{:S(2)}) collective-permute-start(bf16[4,3584]{1,0:T(4,128)(2,1)S(1)} %get-tuple-element.13), channel_id=1, source_target_pairs={{8,0},{12,4},{0,8},{4,12},{9,1},{13,5},{1,9},{5,13},{10,2},{14,6},... | collective-permute-start | bytes 86024 | tf_op jit(solution)/shard_map/ppermute | solution.py:21
  58.1 0.9 %collective-permute-start.20 = (bf16[4,3584]{1,0:T(4,128)(2,1)S(1)}, bf16[4,3584]{1,0:T(4,128)(2,1)S(1)}, u32[]{:S(2)}, u32[]{:S(2)}) collective-permute-start(bf16[4,3584]{1,0:T(4,128)(2,1)S(1)} %get-tuple-element.12), channel_id=1, source_target_pairs={{4,0},{8,4},{12,8},{0,12},{5,1},{9,5},{13,9},{1,13},{6,2},{10,6},{... | collective-permute-start | bytes 86024 | tf_op jit(solution)/shard_map/ppermute | solution.py:21
  59.1 1.2 %collective-permute-start.23 = (bf16[4,3584]{1,0:T(4,128)(2,1)S(1)}, bf16[4,3584]{1,0:T(4,128)(2,1)S(1)}, u32[]{:S(2)}, u32[]{:S(2)}) collective-permute-start(bf16[4,3584]{1,0:T(4,128)(2,1)S(1)} %get-tuple-element.14), channel_id=1, source_target_pairs={{12,0},{0,4},{4,8},{8,12},{13,1},{1,5},{5,9},{9,13},{14,2},{2,6},{... | collective-permute-start | bytes 86024 | tf_op jit(solution)/shard_map/ppermute | solution.py:21
  60.2 1.0 %collective-permute-start.24 = (bf16[4,3584]{1,0:T(4,128)(2,1)S(1)}, bf16[4,3584]{1,0:T(4,128)(2,1)S(1)}, u32[]{:S(2)}, u32[]{:S(2)}) collective-permute-start(bf16[4,3584]{1,0:T(4,128)(2,1)S(1)} %get-tuple-element.16), channel_id=1, source_target_pairs={{8,0},{12,4},{0,8},{4,12},{9,1},{13,5},{1,9},{5,13},{10,2},{14,6},... | collective-permute-start | bytes 86024 | tf_op jit(solution)/shard_map/ppermute | solution.py:21
  61.3 2.8 %collective-permute-start.25 = (bf16[4,3584]{1,0:T(4,128)(2,1)S(1)}, bf16[4,3584]{1,0:T(4,128)(2,1)S(1)}, u32[]{:S(2)}, u32[]{:S(2)}) collective-permute-start(bf16[4,3584]{1,0:T(4,128)(2,1)S(1)} %get-tuple-element.15), channel_id=1, source_target_pairs={{4,0},{8,4},{12,8},{0,12},{5,1},{9,5},{13,9},{1,13},{6,2},{10,6},{... | collective-permute-start | bytes 86024 | tf_op jit(solution)/shard_map/ppermute | solution.py:21
  64.1 0.7 %collective-permute-done.23 = bf16[4,3584]{1,0:T(4,128)(2,1)S(1)} collective-permute-done((bf16[4,3584]{1,0:T(4,128)(2,1)S(1)}, bf16[4,3584]{1,0:T(4,128)(2,1)S(1)}, u32[]{:S(2)}, u32[]{:S(2)}) %collective-permute-start.23) | collective-permute-done | bytes 28704 | tf_op jit(solution)/shard_map/ppermute | solution.py:21
  64.8 0.3 collective-permute-done.24
  65.1 0.5 collective-permute-done.25
  65.7 0.7 maximum_bitcast_fusion.2
  (73 shorter events, 1.4 us)
Async XLA Ops:
  0.0 39.4 %copy-start = (bf16[1,4,128,2,256]{4,3,2,1,0:T(2,128)(2,1)S(1)}, bf16[1,4,128,2,256]{4,3,2,1,0:T(2,128)(2,1)}, u32[]{:S(2)}) copy-start(bf16[1,4,128,2,256]{4,3,2,1,0:T(2,128)(2,1)} %param.17) | copy-start | bytes 1572868
  0.8 10.9 %collective-permute-start.5 = (bf16[4,3584]{1,0:T(4,128)(2,1)S(1)}, bf16[4,3584]{1,0:T(4,128)(2,1)S(1)}, u32[]{:S(2)}, u32[]{:S(2)}) collective-permute-start(bf16[4,3584]{1,0:T(4,128)(2,1)S(1)} %get-tuple-element.24), channel_id=1, source_target_pairs={{4,0},{8,4},{12,8},{0,12},{5,1},{9,5},{13,9},{1,13},{6,2},{10,6},{... | collective-permute-start | bytes 86024 | tf_op jit(solution)/shard_map/ppermute | solution.py:21
  6.0 5.8 %collective-permute-start.6 = (bf16[4,3584]{1,0:T(4,128)(2,1)S(1)}, bf16[4,3584]{1,0:T(4,128)(2,1)S(1)}, u32[]{:S(2)}, u32[]{:S(2)}) collective-permute-start(bf16[4,3584]{1,0:T(4,128)(2,1)S(1)} %get-tuple-element.24), channel_id=1, source_target_pairs={{8,0},{12,4},{0,8},{4,12},{9,1},{13,5},{1,9},{5,13},{10,2},{14,6},... | collective-permute-start | bytes 86024 | tf_op jit(solution)/shard_map/ppermute | solution.py:21
  6.0 5.8 %collective-permute-start.7 = (bf16[4,3584]{1,0:T(4,128)(2,1)S(1)}, bf16[4,3584]{1,0:T(4,128)(2,1)S(1)}, u32[]{:S(2)}, u32[]{:S(2)}) collective-permute-start(bf16[4,3584]{1,0:T(4,128)(2,1)S(1)} %get-tuple-element.24), channel_id=1, source_target_pairs={{12,0},{0,4},{4,8},{8,12},{13,1},{1,5},{5,9},{9,13},{14,2},{2,6},{... | collective-permute-start | bytes 86024 | tf_op jit(solution)/shard_map/ppermute | solution.py:21
  7.8 5.7 %collective-permute-start = (bf16[4,3712]{1,0:T(4,128)(2,1)S(1)}, bf16[4,3712]{1,0:T(4,128)(2,1)S(1)}, u32[]{:S(2)}, u32[]{:S(2)}) collective-permute-start(bf16[4,3712]{1,0:T(4,128)(2,1)S(1)} %pad_maximum_fusion.3), channel_id=1, source_target_pairs={{4,0},{8,4},{12,8},{0,12},{5,1},{9,5},{13,9},{1,13},{6,2},{10,6},{... | collective-permute-start | bytes 89096 | tf_op jit(solution)/shard_map/ppermute | solution.py:21
  10.6 4.8 %collective-permute-start.1 = (bf16[4,3712]{1,0:T(4,128)(2,1)S(1)}, bf16[4,3712]{1,0:T(4,128)(2,1)S(1)}, u32[]{:S(2)}, u32[]{:S(2)}) collective-permute-start(bf16[4,3712]{1,0:T(4,128)(2,1)S(1)} %pad_maximum_fusion.3), channel_id=1, source_target_pairs={{8,0},{12,4},{0,8},{4,12},{9,1},{13,5},{1,9},{5,13},{10,2},{14,6},... | collective-permute-start | bytes 89096 | tf_op jit(solution)/shard_map/ppermute | solution.py:21
  11.8 5.7 %collective-permute-start.2 = (bf16[4,3712]{1,0:T(4,128)(2,1)S(1)}, bf16[4,3712]{1,0:T(4,128)(2,1)S(1)}, u32[]{:S(2)}, u32[]{:S(2)}) collective-permute-start(bf16[4,3712]{1,0:T(4,128)(2,1)S(1)} %pad_maximum_fusion.3), channel_id=1, source_target_pairs={{12,0},{0,4},{4,8},{8,12},{13,1},{1,5},{5,9},{9,13},{14,2},{2,6},{... | collective-permute-start | bytes 89096 | tf_op jit(solution)/shard_map/ppermute | solution.py:21
  11.9 7.2 %collective-permute-start.8 = (bf16[16,3584]{1,0:T(8,128)(2,1)S(1)}, bf16[16,3584]{1,0:T(8,128)(2,1)S(1)}, u32[]{:S(2)}, u32[]{:S(2)}) collective-permute-start(bf16[16,3584]{1,0:T(8,128)(2,1)S(1)} %pad_maximum_fusion.1), channel_id=1, source_target_pairs={{0,2},{1,3},{2,0},{3,1},{4,6},{5,7},{6,4},{7,5},{8,10},{9,11},{10,... | collective-permute-start | bytes 344072 | tf_op jit(solution)/shard_map/ppermute | solution.py:26
  17.5 9.4 %collective-permute-start.3 = (bf16[16,3712]{1,0:T(8,128)(2,1)S(1)}, bf16[16,3712]{1,0:T(8,128)(2,1)S(1)}, u32[]{:S(2)}, u32[]{:S(2)}) collective-permute-start(bf16[16,3712]{1,0:T(8,128)(2,1)S(1)} %pad_maximum_fusion), channel_id=1, source_target_pairs={{0,2},{1,3},{2,0},{3,1},{4,6},{5,7},{6,4},{7,5},{8,10},{9,11},{10,... | collective-permute-start | bytes 356360 | tf_op jit(solution)/shard_map/ppermute | solution.py:26
  19.2 8.4 %collective-permute-start.9 = (bf16[32,3584]{1,0:T(8,128)(2,1)S(1)}, bf16[32,3584]{1,0:T(8,128)(2,1)}, u32[]{:S(2)}, u32[]{:S(2)}) collective-permute-start(bf16[32,3584]{1,0:T(8,128)(2,1)S(1)} %concatenate.105), channel_id=1, source_target_pairs={{0,1},{1,0},{2,3},{3,2},{4,5},{5,4},{6,7},{7,6},{8,9},{9,8},{10,11... | collective-permute-start | bytes 688136 | tf_op jit(solution)/shard_map/ppermute | solution.py:26
  26.9 5.2 %copy-start.3 = (bf16[1,7168,128]{2,1,0:T(8,128)(2,1)S(1)}, bf16[1,7168,128]{2,1,0:T(8,128)(2,1)}, u32[]{:S(2)}) copy-start(bf16[1,7168,128]{2,1,0:T(8,128)(2,1)} %param.16) | copy-start | bytes 5505028
  27.0 5.4 %collective-permute-start.4 = (bf16[32,3712]{1,0:T(8,128)(2,1)S(1)}, bf16[32,3712]{1,0:T(8,128)(2,1)}, u32[]{:S(2)}, u32[]{:S(2)}) collective-permute-start(bf16[32,3712]{1,0:T(8,128)(2,1)S(1)} %concatenate.102), channel_id=1, source_target_pairs={{0,1},{1,0},{2,3},{3,2},{4,5},{5,4},{6,7},{7,6},{8,9},{9,8},{10,11... | collective-permute-start | bytes 712712 | tf_op jit(solution)/shard_map/ppermute | solution.py:26
  33.6 5.5 %copy-start.5 = (s32[16]{0:T(128)S(1)}, s32[16]{0:T(128)}, u32[]{:S(2)}) copy-start(s32[16]{0:T(128)} %param.13) | copy-start | bytes 196
  33.9 5.4 %collective-permute-start.10 = (bf16[64,128]{1,0:T(8,128)(2,1)S(1)}, bf16[64,128]{1,0:T(8,128)(2,1)S(1)}, u32[]{:S(2)}, u32[]{:S(2)}) collective-permute-start(bf16[64,128]{1,0:T(8,128)(2,1)S(1)} %fusion.11), channel_id=1, source_target_pairs={{0,1},{1,0},{2,3},{3,2},{4,5},{5,4},{6,7},{7,6},{8,9},{9,8},{10,11... | collective-permute-start | bytes 49160 | tf_op jit(solution)/shard_map/ppermute | solution.py:26
  34.1 5.2 %collective-permute-start.11 = (bf16[64,128]{1,0:T(8,128)(2,1)S(1)}, bf16[64,128]{1,0:T(8,128)(2,1)S(1)}, u32[]{:S(2)}, u32[]{:S(2)}) collective-permute-start(bf16[64,128]{1,0:T(8,128)(2,1)S(1)} %fusion.11), channel_id=1, source_target_pairs={{0,2},{1,3},{2,0},{3,1},{4,6},{5,7},{6,4},{7,5},{8,10},{9,11},{10,... | collective-permute-start | bytes 49160 | tf_op jit(solution)/shard_map/ppermute | solution.py:26
  34.7 4.7 %collective-permute-start.12 = (bf16[64,128]{1,0:T(8,128)(2,1)S(1)}, bf16[64,128]{1,0:T(8,128)(2,1)S(1)}, u32[]{:S(2)}, u32[]{:S(2)}) collective-permute-start(bf16[64,128]{1,0:T(8,128)(2,1)S(1)} %fusion.11), channel_id=1, source_target_pairs={{0,3},{1,2},{2,1},{3,0},{4,7},{5,6},{6,5},{7,4},{8,11},{9,10},{10,... | collective-permute-start | bytes 49160 | tf_op jit(solution)/shard_map/ppermute | solution.py:26
  36.0 3.8 %copy-start.4 = (bf16[1,4,256,128]{3,2,1,0:T(8,128)(2,1)S(1)}, bf16[1,4,256,128]{3,2,1,0:T(8,128)(2,1)}, u32[]{:S(2)}) copy-start(bf16[1,4,256,128]{3,2,1,0:T(8,128)(2,1)} %param.18) | copy-start | bytes 786436
  39.1 3.6 %copy-start.1 = (bf16[1,256,7168]{2,1,0:T(8,128)(2,1)S(1)}, bf16[1,256,7168]{2,1,0:T(8,128)(2,1)}, u32[]{:S(2)}) copy-start(bf16[1,256,7168]{2,1,0:T(8,128)(2,1)} %param.15) | copy-start | bytes 11010052
  39.7 7.3 %copy-start.2 = (bf16[1,128,7168]{2,1,0:T(8,128)(2,1)S(1)}, bf16[1,128,7168]{2,1,0:T(8,128)(2,1)}, u32[]{:S(2)}) copy-start(bf16[1,128,7168]{2,1,0:T(8,128)(2,1)} %param.19) | copy-start | bytes 5505028
  40.0 4.6 %collective-permute-start.15 = (bf16[64,128]{1,0:T(8,128)(2,1)S(1)}, bf16[64,128]{1,0:T(8,128)(2,1)S(1)}, u32[]{:S(2)}, u32[]{:S(2)}) collective-permute-start(bf16[64,128]{1,0:T(8,128)(2,1)S(1)} %get-tuple-element.17), channel_id=1, source_target_pairs={{0,3},{1,2},{2,1},{3,0},{4,7},{5,6},{6,5},{7,4},{8,11},{9,10},{10,... | collective-permute-start | bytes 49160 | tf_op jit(solution)/shard_map/ppermute | solution.py:26
  43.1 3.8 %collective-permute-start.14 = (bf16[64,128]{1,0:T(8,128)(2,1)S(1)}, bf16[64,128]{1,0:T(8,128)(2,1)S(1)}, u32[]{:S(2)}, u32[]{:S(2)}) collective-permute-start(bf16[64,128]{1,0:T(8,128)(2,1)S(1)} %get-tuple-element.18), channel_id=1, source_target_pairs={{0,2},{1,3},{2,0},{3,1},{4,6},{5,7},{6,4},{7,5},{8,10},{9,11},{10,... | collective-permute-start | bytes 49160 | tf_op jit(solution)/shard_map/ppermute | solution.py:26
  44.6 2.3 %collective-permute-start.13 = (bf16[64,128]{1,0:T(8,128)(2,1)S(1)}, bf16[64,128]{1,0:T(8,128)(2,1)S(1)}, u32[]{:S(2)}, u32[]{:S(2)}) collective-permute-start(bf16[64,128]{1,0:T(8,128)(2,1)S(1)} %get-tuple-element.19), channel_id=1, source_target_pairs={{0,1},{1,0},{2,3},{3,2},{4,5},{5,4},{6,7},{7,6},{8,9},{9,8},{10,11... | collective-permute-start | bytes 49160 | tf_op jit(solution)/shard_map/ppermute | solution.py:26
  47.3 1.6 %collective-permute-start.16 = (bf16[32,3584]{1,0:T(8,128)(2,1)S(1)}, bf16[32,3584]{1,0:T(8,128)(2,1)S(1)}, u32[]{:S(2)}, u32[]{:S(2)}) collective-permute-start(bf16[32,3584]{1,0:T(8,128)(2,1)S(1)} %slice.298), channel_id=1, source_target_pairs={{0,1},{1,0},{2,3},{3,2},{4,5},{5,4},{6,7},{7,6},{8,9},{9,8},{10,11... | collective-permute-start | bytes 688136 | tf_op jit(solution)/shard_map/ppermute | solution.py:26
  47.8 2.7 %collective-permute-start.21 = (bf16[32,3584]{1,0:T(8,128)(2,1)S(1)}, bf16[32,3584]{1,0:T(8,128)(2,1)S(1)}, u32[]{:S(2)}, u32[]{:S(2)}) collective-permute-start(bf16[32,3584]{1,0:T(8,128)(2,1)S(1)} %slice.306), channel_id=1, source_target_pairs={{0,1},{1,0},{2,3},{3,2},{4,5},{5,4},{6,7},{7,6},{8,9},{9,8},{10,11... | collective-permute-start | bytes 688136 | tf_op jit(solution)/shard_map/ppermute | solution.py:26
  49.0 6.1 %collective-permute-start.17 = (bf16[16,3584]{1,0:T(8,128)(2,1)S(1)}, bf16[16,3584]{1,0:T(8,128)(2,1)S(1)}, u32[]{:S(2)}, u32[]{:S(2)}) collective-permute-start(bf16[16,3584]{1,0:T(8,128)(2,1)S(1)} %slice.300), channel_id=1, source_target_pairs={{0,2},{1,3},{2,0},{3,1},{4,6},{5,7},{6,4},{7,5},{8,10},{9,11},{10,... | collective-permute-start | bytes 344072 | tf_op jit(solution)/shard_map/ppermute | solution.py:26
  50.6 8.4 %collective-permute-start.22 = (bf16[16,3584]{1,0:T(8,128)(2,1)S(1)}, bf16[16,3584]{1,0:T(8,128)(2,1)S(1)}, u32[]{:S(2)}, u32[]{:S(2)}) collective-permute-start(bf16[16,3584]{1,0:T(8,128)(2,1)S(1)} %slice.308), channel_id=1, source_target_pairs={{0,2},{1,3},{2,0},{3,1},{4,6},{5,7},{6,4},{7,5},{8,10},{9,11},{10,... | collective-permute-start | bytes 344072 | tf_op jit(solution)/shard_map/ppermute | solution.py:26
  55.1 6.2 %collective-permute-start.18 = (bf16[4,3584]{1,0:T(4,128)(2,1)S(1)}, bf16[4,3584]{1,0:T(4,128)(2,1)S(1)}, u32[]{:S(2)}, u32[]{:S(2)}) collective-permute-start(bf16[4,3584]{1,0:T(4,128)(2,1)S(1)} %get-tuple-element.11), channel_id=1, source_target_pairs={{12,0},{0,4},{4,8},{8,12},{13,1},{1,5},{5,9},{9,13},{14,2},{2,6},{... | collective-permute-start | bytes 86024 | tf_op jit(solution)/shard_map/ppermute | solution.py:21
  56.2 7.9 %collective-permute-start.19 = (bf16[4,3584]{1,0:T(4,128)(2,1)S(1)}, bf16[4,3584]{1,0:T(4,128)(2,1)S(1)}, u32[]{:S(2)}, u32[]{:S(2)}) collective-permute-start(bf16[4,3584]{1,0:T(4,128)(2,1)S(1)} %get-tuple-element.13), channel_id=1, source_target_pairs={{8,0},{12,4},{0,8},{4,12},{9,1},{13,5},{1,9},{5,13},{10,2},{14,6},... | collective-permute-start | bytes 86024 | tf_op jit(solution)/shard_map/ppermute | solution.py:21
  58.1 6.0 %collective-permute-start.20 = (bf16[4,3584]{1,0:T(4,128)(2,1)S(1)}, bf16[4,3584]{1,0:T(4,128)(2,1)S(1)}, u32[]{:S(2)}, u32[]{:S(2)}) collective-permute-start(bf16[4,3584]{1,0:T(4,128)(2,1)S(1)} %get-tuple-element.12), channel_id=1, source_target_pairs={{4,0},{8,4},{12,8},{0,12},{5,1},{9,5},{13,9},{1,13},{6,2},{10,6},{... | collective-permute-start | bytes 86024 | tf_op jit(solution)/shard_map/ppermute | solution.py:21
  59.1 5.7 %collective-permute-start.23 = (bf16[4,3584]{1,0:T(4,128)(2,1)S(1)}, bf16[4,3584]{1,0:T(4,128)(2,1)S(1)}, u32[]{:S(2)}, u32[]{:S(2)}) collective-permute-start(bf16[4,3584]{1,0:T(4,128)(2,1)S(1)} %get-tuple-element.14), channel_id=1, source_target_pairs={{12,0},{0,4},{4,8},{8,12},{13,1},{1,5},{5,9},{9,13},{14,2},{2,6},{... | collective-permute-start | bytes 86024 | tf_op jit(solution)/shard_map/ppermute | solution.py:21
  60.2 4.9 %collective-permute-start.24 = (bf16[4,3584]{1,0:T(4,128)(2,1)S(1)}, bf16[4,3584]{1,0:T(4,128)(2,1)S(1)}, u32[]{:S(2)}, u32[]{:S(2)}) collective-permute-start(bf16[4,3584]{1,0:T(4,128)(2,1)S(1)} %get-tuple-element.16), channel_id=1, source_target_pairs={{8,0},{12,4},{0,8},{4,12},{9,1},{13,5},{1,9},{5,13},{10,2},{14,6},... | collective-permute-start | bytes 86024 | tf_op jit(solution)/shard_map/ppermute | solution.py:21
  61.3 4.4 %collective-permute-start.25 = (bf16[4,3584]{1,0:T(4,128)(2,1)S(1)}, bf16[4,3584]{1,0:T(4,128)(2,1)S(1)}, u32[]{:S(2)}, u32[]{:S(2)}) collective-permute-start(bf16[4,3584]{1,0:T(4,128)(2,1)S(1)} %get-tuple-element.15), channel_id=1, source_target_pairs={{4,0},{8,4},{12,8},{0,12},{5,1},{9,5},{13,9},{1,13},{6,2},{10,6},{... | collective-permute-start | bytes 86024 | tf_op jit(solution)/shard_map/ppermute | solution.py:21

commit v3 on v1

v3 whole, which is shorter than its diff:
```python
import functools

import jax
import jax.numpy as jnp
from jax import lax
from jax.experimental import pallas as pl
from jax.experimental.pallas import tpu as pltpu
from jax.experimental.layout import Layout, with_layout_constraint
from jax.sharding import PartitionSpec as P

VMEM = pl.BlockSpec(memory_space=pltpu.VMEM)


def by_rows(value):
    return with_layout_constraint(value, Layout((0, 1)))


def lookup(table, index):
    keys = jnp.arange(table.shape[0], dtype=jnp.int32)
    return jnp.sum(jnp.where(index[..., None] == keys, table, 0), axis=-1)


def trade(value, even, odd):
    members = lax.axis_size("tensor")
    pairs = []
    for e in range(lax.axis_size("expert")):
        for t in range(members):
            along, across = odd if t % 2 else even
            pairs.append((e * members + t, (e ^ along) * members + (t ^ across)))
    return lax.ppermute(value, ("expert", "tensor"), pairs)


def halves(size):
    masks = []
    while size > 1:
        size //= 2
        masks.append(size)
    return masks


def ordered(flip, first, second):
    return jnp.where(flip, second, first), jnp.where(flip, first, second)


def split_kernel(interleaved, split, wide):
    depth, _, columns = interleaved.shape
    step = 64
    flat = interleaved.reshape(2 * depth, columns)

    @pl.loop(0, depth // step)
    def _(i):
        rows = pl.ds(pl.multiple_of(step * i, step), step)
        both = pl.ds(pl.multiple_of(2 * step * i, 2 * step), 2 * step)
        for lane in range(0, columns, 128):
            tile = wide.at[lane // 128]
            tile[...] = flat[both, lane : lane + 128].astype(jnp.float32)
            for half in range(2):
                split[rows, half * columns + lane : half * columns + lane + 128] = tile[
                    pl.ds(half, step, stride=2), :
                ].astype(jnp.bfloat16)


def split_gate_up(base):
    depth, _, columns = base.shape
    block = 512
    return pl.pallas_call(
        split_kernel,
        grid=(depth // block,),
        out_shape=jax.ShapeDtypeStruct((depth, 2 * columns), jnp.bfloat16),
        in_specs=[pl.BlockSpec((block, 2, columns), lambda i: (i, 0, 0))],
        out_specs=pl.BlockSpec((block, 2 * columns), lambda i: (i, 0)),
        scratch_shapes=[pltpu.VMEM((columns // 128, 128, 128), jnp.float32)],
        compiler_params=pltpu.CompilerParams(vmem_limit_bytes=16 << 20),
        cost_estimate=pl.CostEstimate(flops=0, bytes_accessed=4 * base.size, transcendentals=0),
    )(base)


def product_kernel(other, x, weights, out):
    core = lax.axis_index("tensor") % 2
    start = (1 - core) if other else core
    depth = weights.shape[0] // 2
    rows = weights[pl.ds(pl.multiple_of(start * depth, depth), depth), :]
    out[...] = jnp.dot(x[:, :depth], rows, preferred_element_type=jnp.float32)


def half_product(x, weights, other):
    depth, columns = weights.shape
    return pl.pallas_call(
        functools.partial(product_kernel, other),
        out_shape=jax.ShapeDtypeStruct((x.shape[0], columns), jnp.float32),
        in_specs=[VMEM, VMEM],
        out_specs=VMEM,
        compiler_params=pltpu.CompilerParams(vmem_limit_bytes=16 << 20),
        cost_estimate=pl.CostEstimate(
            flops=x.shape[0] * depth * columns, bytes_accessed=weights.size, transcendentals=0
        ),
    )(x, weights)


def local(
    tokens,
    routes,
    numerators,
    place,
    base_in,
    base_down,
    delta_in,
    delta_mid,
    delta_down,
    delta_back,
):
    clusters = lax.axis_size("expert")
    members = lax.axis_size("tensor")
    me = lax.axis_index("tensor")
    cluster = lax.axis_index("expert")
    core = me % 2
    count, width = tokens.shape[1:]
    top = routes.shape[2]
    half = width // 2

    along, across = halves(clusters), halves(members // 2)
    shared, paired = along[: len(along) - len(across)], along[len(along) - len(across) :]

    side = jnp.concatenate([routes[0], numerators[0]], axis=1).astype(jnp.bfloat16)
    side = jnp.pad(side, ((0, 0), (0, 128 - 2 * top)))
    left, right = (jnp.concatenate([tokens[0, :, :half], side], axis=1), jnp.concatenate([tokens[0, :, half:], side], axis=1))
    mine, theirs = ordered(core == 1, left, right)

    held = jnp.concatenate(ordered(core == 1, mine, trade(theirs, (0, 1), (0, 1))))
    for mask in shared:
        held = jnp.concatenate([held, trade(held, (mask, 0), (mask, 0))])
    for z, x in zip(paired, across):
        size = held.shape[0]
        flag = (me // (2 * x)) % 2 == 1
        held = jnp.concatenate(ordered((core == 0) & flag, held, trade(held, (0, 2 * x), (z, 0))))
        low, high = ordered((core == 1) & flag, held, trade(held, (z, 0), (0, 2 * x)))
        inner = ordered(core == 1, low[size:], high[:size])
        held = jnp.concatenate([low[:size], *inner, high[size:]])
    held = by_rows(held)
    rest = by_rows(trade(held, (0, 1), (0, 1)))

    split = split_gate_up(base_in[0])
    projected = half_product(held, split, False) + half_product(rest, split, True)
    codes = (half_product(held, delta_in[0], False) + half_product(rest, delta_in[0], True)).astype(jnp.bfloat16)

    side = by_rows(held[:, half:])
    all_routes = side[:, :top].astype(jnp.int32)
    numerator = side[:, top : 2 * top].astype(jnp.float32)
    position = lookup(place, all_routes)
    weight = (2.5 * numerator / jnp.sum(numerator, axis=-1, keepdims=True)).astype(jnp.bfloat16)
    target = cluster * members + jnp.arange(members, dtype=jnp.int32)
    scale = jnp.sum(
        jnp.where(position[None] == target[:, None, None], weight[None].astype(jnp.float32), 0.0), axis=-1
    )

    codes = jnp.stack([codes if m == 0 else trade(codes, (0, m), (0, m)) for m in range(members)])
    by_slot = jnp.stack([lax.dynamic_index_in_dim(codes, s ^ me, 0, keepdims=False) for s in range(members)])

    lifted = jnp.einsum("srk,skgf->srgf", by_slot, delta_mid[0], preferred_element_type=jnp.float32)
    part = projected.shape[1] // 2
    hidden = jax.nn.silu(projected[None, :, :part] + lifted[:, :, 0]) * (
        projected[None, :, part:] + lifted[:, :, 1]
    )
    hidden_sum = jnp.sum(scale[:, :, None] * hidden, axis=0).astype(jnp.bfloat16)
    partial_codes = jnp.einsum(
        "srf,sfk->srk", hidden.astype(jnp.bfloat16), delta_down[0], preferred_element_type=jnp.float32
    ).astype(jnp.bfloat16)
    lowrank = lax.dynamic_index_in_dim(partial_codes, me, 0, keepdims=False).astype(jnp.float32)
    for m in range(1, members):
        sent = lax.dynamic_index_in_dim(partial_codes, me ^ m, 0, keepdims=False)
        lowrank = lowrank + trade(sent, (0, m), (0, m)).astype(jnp.float32)
    own_scale = lax.dynamic_index_in_dim(scale, me, 0, keepdims=False)
    scaled = (own_scale[:, None] * lowrank).astype(jnp.bfloat16)

    term = jnp.dot(hidden_sum, base_down[0], preferred_element_type=jnp.float32)
    term = (term + jnp.dot(scaled, delta_back[0], preferred_element_type=jnp.float32)).astype(jnp.bfloat16)

    def add(kept, received):
        return (kept.astype(jnp.float32) + received.astype(jnp.float32)).astype(jnp.bfloat16)

    sent = lax.dynamic_slice_in_dim(term, (1 - core) * half, half, axis=1)
    kept = lax.dynamic_slice_in_dim(term, core * half, half, axis=1)
    total = add(kept, trade(sent, (0, 1), (0, 1)))
    for z, x in reversed(list(zip(paired, across))):
        flag = (me // (2 * x)) % 2 == 1
        size = total.shape[0] // 4
        blocks = [total[i * size : (i + 1) * size] for i in range(4)]
        inner = ordered(core == 1, blocks[1], blocks[2])
        kept, sent = ordered(
            (core == 1) & flag,
            jnp.concatenate([blocks[0], inner[0]]),
            jnp.concatenate([inner[1], blocks[3]]),
        )
        total = add(kept, trade(sent, (z, 0), (0, 2 * x)))
        kept, sent = ordered((core == 0) & flag, total[:size], total[size:])
        total = add(kept, trade(sent, (0, 2 * x), (z, 0)))
    for mask in reversed(shared):
        size = total.shape[0] // 2
        total = add(total[:size], trade(total[size:], (mask, 0), (mask, 0)))
    kept, sent = ordered(core == 1, total[:count], total[count:])
    mixed = ordered(core == 1, kept, trade(sent, (0, 1), (0, 1)))
    return jnp.concatenate(mixed, axis=1)[None]


def solution(mesh):
    placed = (
        P(None, ("parts", "expert", "tensor"), None),
        P(None, ("parts", "expert", "tensor"), None),
        P(None, ("parts", "expert", "tensor"), None),
        P("parts"),
        P("expert", None, None, "tensor"),
        P("expert", "tensor", None),
        P(("expert", "tensor"), None, None),
        P("expert", None, None, None, "tensor"),
        P("expert", None, "tensor", None),
        P(("expert", "tensor"), None, None),
    )
    return jax.shard_map(
        local,
        mesh=mesh,
        in_specs=placed,
        out_specs=P(None, ("parts", "expert", "tensor"), None),
        check_vma=False,
    )
```

time: 79.3 us -> 71.1 us (0.90)
  local copies, waits for them, and re-layouts: 23.5 us -> 11.9 us
  Pallas kernels: 0 us -> 9.59 us
  matrix products: 9.12 us -> 1.65 us
  waiting for transfers between devices: 23.4 us -> 25.4 us
    concatenate x6 -> x0, local copies, waits for them, and re-layouts: 13.8 us -> none  [the longest x1 11.6 us: local(): held = jnp.concatenate([held, swap(held, 1)])]
    unnamed x12 -> x22, local copies, waits for them, and re-layouts: 0.26 us -> 10.8 us
    pallas_call x0 -> x5, Pallas kernels: none -> 9.59 us  [the longest x1 7.54 us: split_gate_up(): pl.pallas_call(split_kernel, grid=(depth // block,), out_shape=jax.ShapeD...]
    ppermute x5 -> x0, local copies, waits for them, and re-layouts: 9.22 us -> none  [the longest x3 5.51 us: from_ahead(): lax.ppermute(value, 'expert', [((i + steps) % size, i) for i in range(siz...]
    dot_general x2 -> x0, matrix products: 7.47 us -> none  [the longest x1 4.64 us: local(): jnp.einsum('nd,dgf->ngf', rows, base_in[0], preferred_element_type=jnp.fl...]
    ppermute x16, waiting for transfers between devices: 23.4 us -> 25.4 us  [trade(): return lax.ppermute(value, ('expert', 'tensor'), pairs)]
    concatenate x2 -> x4, other arithmetic: 1.8 us -> 0.15 us  [the longest x1 0.05 us: local(): held = jnp.concatenate([held, trade(held, (mask, 0), (mask, 0))])]
    convert_element_type x3 -> x6, other arithmetic: 0.17 us -> 1.29 us  [the longest x4 1.27 us: add(): (kept.astype(jnp.float32) + received.astype(jnp.float32)).astype(jnp.bflo...]
  transfers between devices with their start and end apart: 16 -> 16, of which waited for: 10 -> 12; matrix products, arithmetic and copies ran while one was open for 19% -> 2% of each run, Pallas kernels for 0% -> 13%
where the time goes in v3:
time: 71.1 us; the launch traced here: 70.8 us
  waiting for transfers between devices  25.4 us (36%)
  starting transfers between devices  18 us (25%)
  local copies, waits for them, and re-layouts  11.9 us (17%)
  Pallas kernels  9.59 us (13%)
  other arithmetic  3.93 us (6%)
  matrix products  1.65 us (2%)
    ppermute x16, waiting for transfers between devices, trade(): return lax.ppermute(value, ('expert', 'tensor'), pairs)  25.4 us
    ppermute x16, starting transfers between devices, trade(): return lax.ppermute(value, ('expert', 'tensor'), pairs)  18 us
    unnamed x22, local copies, waits for them, and re-layouts  10.8 us
    pallas_call x1, Pallas kernels, split_gate_up(): pl.pallas_call(split_kernel, grid=(depth // block,), out_shape=jax.ShapeD...  7.54 us
    pallas_call x4, Pallas kernels, half_product(): pl.pallas_call(functools.partial(product_kernel, other), out_shape=jax.Sh...  2.05 us
  transfers between devices with their start and end apart: 16, of which 12 were waited for; matrix products, arithmetic and copies ran while one was open for 2% of the time, Pallas kernels for 13%

profile of v3, /device:TPU:0, one launch (start us, length us, event | category | flops | bytes accessed | tf_op | source)
XLA Modules:
  0.0 70.8 jit_solution(9341957284576779859)
XLA Ops:
  0.0 0.9 %slice_bitcast_fusion.2 = (bf16[4,3584]{1,0:T(4,128)(2,1)S(1)}, bf16[4,3584]{1,0:T(4,128)(2,1)S(1)}) fusion(bf16[1,4,7168]{2,1,0:T(4,128)(2,1)} %param.10), kind=kLoop, calls=%fused_computation.64 | loop fusion | bytes 114688 | tf_op jit(solution)/shard_map/squeeze | solution.py:126
  0.9 0.7 convert_bitcast_fusion
  1.7 0.5 collective-permute-start
  2.3 0.9 %collective-permute-done = bf16[4,3712]{1,0:T(4,128)(2,1)S(1)} collective-permute-done((bf16[4,3712]{1,0:T(4,128)(2,1)S(1)}, bf16[4,3712]{1,0:T(4,128)(2,1)S(1)}, u32[]{:S(2)}, u32[]{:S(2)}) %collective-permute-start) | collective-permute-done | bytes 29728 | tf_op jit(solution)/shard_map/ppermute | solution.py:30
  3.2 4.0 %collective-permute-start.1 = (bf16[8,3712]{1,0:T(8,128)(2,1)S(1)}, bf16[8,3712]{1,0:T(8,128)(2,1)S(1)}, u32[]{:S(2)}, u32[]{:S(2)}) collective-permute-start(bf16[8,3712]{1,0:T(8,128)(2,1)S(1)} %pad_maximum_fusion.6), channel_id=1, source_target_pairs={{0,8},{1,9},{2,10},{3,11},{4,12},{5,13},{6,14},{7,15},{8,0},{9,1},... | collective-permute-start | bytes 178184 | tf_op jit(solution)/shard_map/ppermute | solution.py:30
  7.2 3.6 %collective-permute-done.1 = bf16[8,3712]{1,0:T(8,128)(2,1)S(1)} collective-permute-done((bf16[8,3712]{1,0:T(8,128)(2,1)S(1)}, bf16[8,3712]{1,0:T(8,128)(2,1)S(1)}, u32[]{:S(2)}, u32[]{:S(2)}) %collective-permute-start.1) | collective-permute-done | bytes 59424 | tf_op jit(solution)/shard_map/ppermute | solution.py:30
  10.8 1.8 %collective-permute-start.2 = (bf16[16,3712]{1,0:T(8,128)(2,1)S(1)}, bf16[16,3712]{1,0:T(8,128)(2,1)S(1)}, u32[]{:S(2)}, u32[]{:S(2)}) collective-permute-start(bf16[16,3712]{1,0:T(8,128)(2,1)S(1)} %pad_maximum_fusion.4), channel_id=1, source_target_pairs={{0,2},{1,5},{2,0},{3,7},{4,6},{5,1},{6,4},{7,3},{8,10},{9,13},{10,... | collective-permute-start | bytes 356360 | tf_op jit(solution)/shard_map/ppermute | solution.py:30
  12.6 3.1 %collective-permute-done.2 = bf16[16,3712]{1,0:T(8,128)(2,1)S(1)} collective-permute-done((bf16[16,3712]{1,0:T(8,128)(2,1)S(1)}, bf16[16,3712]{1,0:T(8,128)(2,1)S(1)}, u32[]{:S(2)}, u32[]{:S(2)}) %collective-permute-start.2) | collective-permute-done | bytes 118816 | tf_op jit(solution)/shard_map/ppermute | solution.py:30
  15.8 0.8 %collective-permute-start.3 = (bf16[32,3712]{1,0:T(8,128)(2,1)S(1)}, bf16[32,3712]{1,0:T(8,128)(2,1)S(1)}, u32[]{:S(2)}, u32[]{:S(2)}) collective-permute-start(bf16[32,3712]{1,0:T(8,128)(2,1)S(1)} %pad_maximum_fusion.1), channel_id=1, source_target_pairs={{0,4},{1,3},{2,6},{3,1},{4,0},{5,7},{6,2},{7,5},{8,12},{9,11},{10,... | collective-permute-start | bytes 712712 | tf_op jit(solution)/shard_map/ppermute | solution.py:30
  16.6 3.1 %copy-done.4 = bf16[1,7168,2,256]{3,2,1,0:T(2,128)(2,1)S(1)} copy-done((bf16[1,7168,2,256]{3,2,1,0:T(2,128)(2,1)S(1)}, bf16[1,7168,2,256]{3,2,1,0:T(2,128)(2,1)}, u32[]{:S(2)}) %copy-start.4) | copy-done | bytes 7340056
  19.7 7.5 %shard_map.100.weights = bf16[7168,512]{1,0:T(8,128)(2,1)S(1)} custom-call(bf16[7168,2,256]{2,1,0:T(2,128)(2,1)S(1)} %bitcast.63), custom_call_target="tpu_custom_call" | custom-call | bytes 14680064 | tf_op jit(solution)/shard_map/pallas_call | solution.py:66
  27.3 2.9 %copy-done.1 = bf16[7168,512]{1,0:T(8,128)(2,1)} copy-done((bf16[7168,512]{1,0:T(8,128)(2,1)}, bf16[7168,512]{1,0:T(8,128)(2,1)S(1)}, u32[]{:S(2)}) %copy-start.1) | copy-done | bytes 7340056
  30.2 0.1 broadcast_select_fusion.1
  30.5 0.2 convert_reduce_fusion
  30.6 0.1 fusion.24
  30.9 1.5 %copy-done.5 = bf16[1,7168,128]{2,1,0:T(8,128)(2,1)S(1)} copy-done((bf16[1,7168,128]{2,1,0:T(8,128)(2,1)S(1)}, bf16[1,7168,128]{2,1,0:T(8,128)(2,1)}, u32[]{:S(2)}) %copy-start.5) | copy-done | bytes 1835032
  32.4 0.3 shard_map.103
  32.7 3.2 %copy-done.2 = bf16[7168,512]{1,0:T(8,128)(2,1)S(1)} copy-done((bf16[7168,512]{1,0:T(8,128)(2,1)S(1)}, bf16[7168,512]{1,0:T(8,128)(2,1)}, u32[]{:S(2)}) %copy-start.2) | copy-done | bytes 7340056
  35.9 0.7 %shard_map.101 = f32[64,512]{1,0:T(8,128)S(1)} custom-call(bf16[64,3712]{1,0:T(8,128)(2,1)S(1)} %pad_maximum_fusion.x, bf16[7168,512]{1,0:T(8,128)(2,1)S(1)} %copy-done.2), custom_call_target="tpu_custom_call" | custom-call | flops 234881024 | bytes 3670016 | tf_op jit(solution)/shard_map/pallas_call | solution.py:88
  36.7 0.1 select_reduce_fusion
  36.8 0.1 select_reduce_fusion.1
  36.9 0.3 shard_map.104
  37.2 0.6 collective-permute-start.5
  37.8 1.5 %collective-permute-start.6 = (bf16[64,128]{1,0:T(8,128)(2,1)S(1)}, bf16[64,128]{1,0:T(8,128)(2,1)S(1)}, u32[]{:S(2)}, u32[]{:S(2)}) collective-permute-start(bf16[64,128]{1,0:T(8,128)(2,1)S(1)} %add_convert_fusion.4), channel_id=1, source_target_pairs={{0,2},{1,3},{2,0},{3,1},{4,6},{5,7},{6,4},{7,5},{8,10},{9,11},{10,... | collective-permute-start | bytes 49160 | tf_op jit(solution)/shard_map/ppermute | solution.py:30
  39.3 0.7 %shard_map.102 = f32[64,512]{1,0:T(8,128)S(1)} custom-call(bf16[64,3712]{1,0:T(8,128)(2,1)S(1)} %collective-permute-done.4.x, bf16[7168,512]{1,0:T(8,128)(2,1)S(1)} %copy-done.3), custom_call_target="tpu_custom_call" | custom-call | flops 234881024 | bytes 3670016 | tf_op jit(solution)/shard_map/pallas_call | solution.py:88
  40.1 1.4 %collective-permute-done.6 = bf16[64,128]{1,0:T(8,128)(2,1)S(1)} collective-permute-done((bf16[64,128]{1,0:T(8,128)(2,1)S(1)}, bf16[64,128]{1,0:T(8,128)(2,1)S(1)}, u32[]{:S(2)}, u32[]{:S(2)}) %collective-permute-start.6) | collective-permute-done | bytes 16416 | tf_op jit(solution)/shard_map/ppermute | solution.py:30
  41.5 1.1 %collective-permute-done.7 = bf16[64,128]{1,0:T(8,128)(2,1)S(1)} collective-permute-done((bf16[64,128]{1,0:T(8,128)(2,1)S(1)}, bf16[64,128]{1,0:T(8,128)(2,1)S(1)}, u32[]{:S(2)}, u32[]{:S(2)}) %collective-permute-start.7) | collective-permute-done | bytes 16416 | tf_op jit(solution)/shard_map/ppermute | solution.py:30
  42.6 0.2 fusion.4
  42.8 0.1 multiply_reduce_fusion
  43.0 0.2 convolution_convert_fusion
  43.2 0.3 collective-permute-start.10
  43.5 0.4 collective-permute-start.8
  43.9 1.5 %collective-permute-start.9 = (bf16[64,128]{1,0:T(8,128)(2,1)S(1)}, bf16[64,128]{1,0:T(8,128)(2,1)S(1)}, u32[]{:S(2)}, u32[]{:S(2)}) collective-permute-start(bf16[64,128]{1,0:T(8,128)(2,1)S(1)} %get-tuple-element.27), channel_id=1, source_target_pairs={{0,2},{1,3},{2,0},{3,1},{4,6},{5,7},{6,4},{7,5},{8,10},{9,11},{10,... | collective-permute-start | bytes 49160 | tf_op jit(solution)/shard_map/ppermute | solution.py:30
  45.4 0.8 %fusion.1 = f32[64,7168]{1,0:T(8,128)S(1)} fusion(bf16[1,256,7168]{2,1,0:T(8,128)(2,1)S(1)} %copy-done.7, bf16[64,256]{1,0:T(8,128)(2,1)S(1)} %get-tuple-element.5), kind=kOutput, calls=%fused_computation.2 | convolution fusion | flops 234881024 | bytes 5537792 | tf_op jit(solution)/shard_map/dot_general | solution.py:175
  46.2 0.3 collective-permute-done.10
  46.4 1.2 %collective-permute-done.9 = bf16[64,128]{1,0:T(8,128)(2,1)S(1)} collective-permute-done((bf16[64,128]{1,0:T(8,128)(2,1)S(1)}, bf16[64,128]{1,0:T(8,128)(2,1)S(1)}, u32[]{:S(2)}, u32[]{:S(2)}) %collective-permute-start.9) | collective-permute-done | bytes 16416 | tf_op jit(solution)/shard_map/ppermute | solution.py:30
  47.7 0.5 fusion
  48.3 1.9 %collective-permute-done.11 = bf16[64,3584]{1,0:T(8,128)(2,1)} collective-permute-done((bf16[64,3584]{1,0:T(8,128)(2,1)S(1)}, bf16[64,3584]{1,0:T(8,128)(2,1)}, u32[]{:S(2)}, u32[]{:S(2)}) %collective-permute-start.11) | collective-permute-done | bytes 458784 | tf_op jit(solution)/shard_map/ppermute | solution.py:30
  50.2 1.1 %add_convert_fusion = bf16[64,3584]{1,0:T(8,128)(2,1)S(1)} fusion(bf16[64,3584]{1,0:T(8,128)(2,1)} %collective-permute-done.11, bf16[64,7168]{1,0:T(8,128)(2,1)S(1)} %fusion, s32[]{:T(128)S(6)} %select_n.186), kind=kLoop, calls=%fused_computation.6 | loop fusion | flops 917504 | bytes 1376260 | tf_op jit(solution)/shard_map/convert_element_type | solution.py:179
  51.5 1.5 %collective-permute-start.12 = (bf16[32,3584]{1,0:T(8,128)(2,1)S(1)}, bf16[32,3584]{1,0:T(8,128)(2,1)S(1)}, u32[]{:S(2)}, u32[]{:S(2)}) collective-permute-start(bf16[32,3584]{1,0:T(8,128)(2,1)S(1)} %broadcast_select_fusion.2), channel_id=1, source_target_pairs={{0,4},{1,3},{2,6},{3,1},{4,0},{5,7},{6,2},{7,5},{8,12},{9,11},{10,... | collective-permute-start | bytes 688136 | tf_op jit(solution)/shard_map/ppermute | solution.py:30
  52.9 4.6 %collective-permute-done.12 = bf16[32,3584]{1,0:T(8,128)(2,1)S(1)} collective-permute-done((bf16[32,3584]{1,0:T(8,128)(2,1)S(1)}, bf16[32,3584]{1,0:T(8,128)(2,1)S(1)}, u32[]{:S(2)}, u32[]{:S(2)}) %collective-permute-start.12) | collective-permute-done | bytes 229408 | tf_op jit(solution)/shard_map/ppermute | solution.py:30
  57.6 0.1 add_convert_fusion.1
  57.7 1.5 %collective-permute-start.13 = (bf16[16,3584]{1,0:T(8,128)(2,1)S(1)}, bf16[16,3584]{1,0:T(8,128)(2,1)S(1)}, u32[]{:S(2)}, u32[]{:S(2)}) collective-permute-start(bf16[16,3584]{1,0:T(8,128)(2,1)S(1)} %broadcast_select_fusion.9), channel_id=1, source_target_pairs={{0,2},{1,5},{2,0},{3,7},{4,6},{5,1},{6,4},{7,3},{8,10},{9,13},{10,... | collective-permute-start | bytes 344072 | tf_op jit(solution)/shard_map/ppermute | solution.py:30
  59.2 3.3 %collective-permute-done.13 = bf16[16,3584]{1,0:T(8,128)(2,1)S(1)} collective-permute-done((bf16[16,3584]{1,0:T(8,128)(2,1)S(1)}, bf16[16,3584]{1,0:T(8,128)(2,1)S(1)}, u32[]{:S(2)}, u32[]{:S(2)}) %collective-permute-start.13) | collective-permute-done | bytes 114720 | tf_op jit(solution)/shard_map/ppermute | solution.py:30
  62.6 3.4 %collective-permute-start.14 = (bf16[8,3584]{1,0:T(8,128)(2,1)S(1)}, bf16[8,3584]{1,0:T(8,128)(2,1)S(1)}, u32[]{:S(2)}, u32[]{:S(2)}) collective-permute-start(bf16[8,3584]{1,0:T(8,128)(2,1)S(1)} %slice.111), channel_id=1, source_target_pairs={{0,8},{1,9},{2,10},{3,11},{4,12},{5,13},{6,14},{7,15},{8,0},{9,1},... | collective-permute-start | bytes 172040 | tf_op jit(solution)/shard_map/ppermute | solution.py:30
  66.0 2.8 %collective-permute-done.14 = bf16[8,3584]{1,0:T(8,128)(2,1)S(1)} collective-permute-done((bf16[8,3584]{1,0:T(8,128)(2,1)S(1)}, bf16[8,3584]{1,0:T(8,128)(2,1)S(1)}, u32[]{:S(2)}, u32[]{:S(2)}) %collective-permute-start.14) | collective-permute-done | bytes 57376 | tf_op jit(solution)/shard_map/ppermute | solution.py:30
  69.0 1.2 %collective-permute-done.15 = bf16[4,3584]{1,0:T(4,128)(2,1)S(1)} collective-permute-done((bf16[4,3584]{1,0:T(4,128)(2,1)S(1)}, bf16[4,3584]{1,0:T(4,128)(2,1)S(1)}, u32[]{:S(2)}, u32[]{:S(2)}) %collective-permute-start.15) | collective-permute-done | bytes 28704 | tf_op jit(solution)/shard_map/ppermute | solution.py:30
  70.2 0.7 maximum_bitcast_fusion.2
  (55 shorter events, 1.2 us)
Async XLA Ops:
  0.0 47.7 %copy-start = (bf16[1,128,7168]{2,1,0:T(8,128)(2,1)S(1)}, bf16[1,128,7168]{2,1,0:T(8,128)(2,1)}, u32[]{:S(2)}) copy-start(bf16[1,128,7168]{2,1,0:T(8,128)(2,1)} %param.19) | copy-start | bytes 5505028
  1.7 1.4 %collective-permute-start = (bf16[4,3712]{1,0:T(4,128)(2,1)S(1)}, bf16[4,3712]{1,0:T(4,128)(2,1)S(1)}, u32[]{:S(2)}, u32[]{:S(2)}) collective-permute-start(bf16[4,3712]{1,0:T(4,128)(2,1)S(1)} %broadcast_select_fusion.13), channel_id=1, source_target_pairs={{0,1},{1,0},{2,3},{3,2},{4,5},{5,4},{6,7},{7,6},{8,9},{9,8},{10,11... | collective-permute-start | bytes 89096 | tf_op jit(solution)/shard_map/ppermute | solution.py:30
  3.2 7.6 %collective-permute-start.1 = (bf16[8,3712]{1,0:T(8,128)(2,1)S(1)}, bf16[8,3712]{1,0:T(8,128)(2,1)S(1)}, u32[]{:S(2)}, u32[]{:S(2)}) collective-permute-start(bf16[8,3712]{1,0:T(8,128)(2,1)S(1)} %pad_maximum_fusion.6), channel_id=1, source_target_pairs={{0,8},{1,9},{2,10},{3,11},{4,12},{5,13},{6,14},{7,15},{8,0},{9,1},... | collective-permute-start | bytes 178184 | tf_op jit(solution)/shard_map/ppermute | solution.py:30
  10.8 4.9 %collective-permute-start.2 = (bf16[16,3712]{1,0:T(8,128)(2,1)S(1)}, bf16[16,3712]{1,0:T(8,128)(2,1)S(1)}, u32[]{:S(2)}, u32[]{:S(2)}) collective-permute-start(bf16[16,3712]{1,0:T(8,128)(2,1)S(1)} %pad_maximum_fusion.4), channel_id=1, source_target_pairs={{0,2},{1,5},{2,0},{3,7},{4,6},{5,1},{6,4},{7,3},{8,10},{9,13},{10,... | collective-permute-start | bytes 356360 | tf_op jit(solution)/shard_map/ppermute | solution.py:30
  15.8 14.4 %collective-permute-start.3 = (bf16[32,3712]{1,0:T(8,128)(2,1)S(1)}, bf16[32,3712]{1,0:T(8,128)(2,1)S(1)}, u32[]{:S(2)}, u32[]{:S(2)}) collective-permute-start(bf16[32,3712]{1,0:T(8,128)(2,1)S(1)} %pad_maximum_fusion.1), channel_id=1, source_target_pairs={{0,4},{1,3},{2,6},{3,1},{4,0},{5,7},{6,2},{7,5},{8,12},{9,11},{10,... | collective-permute-start | bytes 712712 | tf_op jit(solution)/shard_map/ppermute | solution.py:30
  16.6 3.1 %copy-start.4 = (bf16[1,7168,2,256]{3,2,1,0:T(2,128)(2,1)S(1)}, bf16[1,7168,2,256]{3,2,1,0:T(2,128)(2,1)}, u32[]{:S(2)}) copy-start(bf16[1,7168,2,256]{3,2,1,0:T(2,128)(2,1)} %param.14) | copy-start | bytes 22020100
  27.2 2.9 %copy-start.1 = (bf16[7168,512]{1,0:T(8,128)(2,1)}, bf16[7168,512]{1,0:T(8,128)(2,1)S(1)}, u32[]{:S(2)}) copy-start(bf16[7168,512]{1,0:T(8,128)(2,1)S(1)} %shard_map.100.weights) | copy-start | bytes 22020100
  30.4 6.5 %collective-permute-start.4 = (bf16[64,3712]{1,0:T(8,128)(2,1)S(1)}, bf16[64,3712]{1,0:T(8,128)(2,1)S(1)}, u32[]{:S(2)}, u32[]{:S(2)}) collective-permute-start(bf16[64,3712]{1,0:T(8,128)(2,1)S(1)} %pad_maximum_fusion.x), channel_id=1, source_target_pairs={{0,1},{1,0},{2,3},{3,2},{4,5},{5,4},{6,7},{7,6},{8,9},{9,8},{10,11... | collective-permute-start | bytes 1425416 | tf_op jit(solution)/shard_map/ppermute | solution.py:30
  30.9 1.5 %copy-start.5 = (bf16[1,7168,128]{2,1,0:T(8,128)(2,1)S(1)}, bf16[1,7168,128]{2,1,0:T(8,128)(2,1)}, u32[]{:S(2)}) copy-start(bf16[1,7168,128]{2,1,0:T(8,128)(2,1)} %param.16) | copy-start | bytes 5505028
  32.4 4.5 %copy-start.6 = (bf16[1,7168,128]{2,1,0:T(8,128)(2,1)S(1)}, bf16[1,7168,128]{2,1,0:T(8,128)(2,1)}, u32[]{:S(2)}) copy-start(bf16[1,7168,128]{2,1,0:T(8,128)(2,1)} %param.16) | copy-start | bytes 5505028
  32.7 3.2 %copy-start.2 = (bf16[7168,512]{1,0:T(8,128)(2,1)S(1)}, bf16[7168,512]{1,0:T(8,128)(2,1)}, u32[]{:S(2)}) copy-start(bf16[7168,512]{1,0:T(8,128)(2,1)} %copy-done.1) | copy-start | bytes 22020100
  35.9 0.7 %copy-start.10 = (s32[16]{0:T(128)S(1)}, s32[16]{0:T(128)}, u32[]{:S(2)}) copy-start(s32[16]{0:T(128)} %param.13) | copy-start | bytes 196
  35.9 3.3 %copy-start.3 = (bf16[7168,512]{1,0:T(8,128)(2,1)S(1)}, bf16[7168,512]{1,0:T(8,128)(2,1)}, u32[]{:S(2)}) copy-start(bf16[7168,512]{1,0:T(8,128)(2,1)} %copy-done.1) | copy-start | bytes 22020100
  37.2 5.4 %copy-start.8 = (bf16[1,4,128,2,256]{4,3,2,1,0:T(2,128)(2,1)S(1)}, bf16[1,4,128,2,256]{4,3,2,1,0:T(2,128)(2,1)}, u32[]{:S(2)}) copy-start(bf16[1,4,128,2,256]{4,3,2,1,0:T(2,128)(2,1)} %param.17) | copy-start | bytes 1572868
  37.2 2.9 %collective-permute-start.5 = (bf16[64,128]{1,0:T(8,128)(2,1)S(1)}, bf16[64,128]{1,0:T(8,128)(2,1)S(1)}, u32[]{:S(2)}, u32[]{:S(2)}) collective-permute-start(bf16[64,128]{1,0:T(8,128)(2,1)S(1)} %add_convert_fusion.4), channel_id=1, source_target_pairs={{0,1},{1,0},{2,3},{3,2},{4,5},{5,4},{6,7},{7,6},{8,9},{9,8},{10,11... | collective-permute-start | bytes 49160 | tf_op jit(solution)/shard_map/ppermute | solution.py:30
  37.8 3.7 %collective-permute-start.6 = (bf16[64,128]{1,0:T(8,128)(2,1)S(1)}, bf16[64,128]{1,0:T(8,128)(2,1)S(1)}, u32[]{:S(2)}, u32[]{:S(2)}) collective-permute-start(bf16[64,128]{1,0:T(8,128)(2,1)S(1)} %add_convert_fusion.4), channel_id=1, source_target_pairs={{0,2},{1,3},{2,0},{3,1},{4,6},{5,7},{6,4},{7,5},{8,10},{9,11},{10,... | collective-permute-start | bytes 49160 | tf_op jit(solution)/shard_map/ppermute | solution.py:30
  39.3 3.3 %collective-permute-start.7 = (bf16[64,128]{1,0:T(8,128)(2,1)S(1)}, bf16[64,128]{1,0:T(8,128)(2,1)S(1)}, u32[]{:S(2)}, u32[]{:S(2)}) collective-permute-start(bf16[64,128]{1,0:T(8,128)(2,1)S(1)} %add_convert_fusion.4), channel_id=1, source_target_pairs={{0,3},{1,2},{2,1},{3,0},{4,7},{5,6},{6,5},{7,4},{8,11},{9,10},{10,... | collective-permute-start | bytes 49160 | tf_op jit(solution)/shard_map/ppermute | solution.py:30
  39.3 6.1 %copy-start.7 = (bf16[1,256,7168]{2,1,0:T(8,128)(2,1)S(1)}, bf16[1,256,7168]{2,1,0:T(8,128)(2,1)}, u32[]{:S(2)}) copy-start(bf16[1,256,7168]{2,1,0:T(8,128)(2,1)} %param.15) | copy-start | bytes 11010052
  40.0 3.0 %copy-start.9 = (bf16[1,4,256,128]{3,2,1,0:T(8,128)(2,1)S(1)}, bf16[1,4,256,128]{3,2,1,0:T(8,128)(2,1)}, u32[]{:S(2)}) copy-start(bf16[1,4,256,128]{3,2,1,0:T(8,128)(2,1)} %param.18) | copy-start | bytes 786436
  43.2 3.2 %collective-permute-start.10 = (bf16[64,128]{1,0:T(8,128)(2,1)S(1)}, bf16[64,128]{1,0:T(8,128)(2,1)S(1)}, u32[]{:S(2)}, u32[]{:S(2)}) collective-permute-start(bf16[64,128]{1,0:T(8,128)(2,1)S(1)} %get-tuple-element.26), channel_id=1, source_target_pairs={{0,3},{1,2},{2,1},{3,0},{4,7},{5,6},{6,5},{7,4},{8,11},{9,10},{10,... | collective-permute-start | bytes 49160 | tf_op jit(solution)/shard_map/ppermute | solution.py:30
  43.5 2.9 %collective-permute-start.8 = (bf16[64,128]{1,0:T(8,128)(2,1)S(1)}, bf16[64,128]{1,0:T(8,128)(2,1)S(1)}, u32[]{:S(2)}, u32[]{:S(2)}) collective-permute-start(bf16[64,128]{1,0:T(8,128)(2,1)S(1)} %get-tuple-element.25), channel_id=1, source_target_pairs={{0,1},{1,0},{2,3},{3,2},{4,5},{5,4},{6,7},{7,6},{8,9},{9,8},{10,11... | collective-permute-start | bytes 49160 | tf_op jit(solution)/shard_map/ppermute | solution.py:30
  43.9 3.7 %collective-permute-start.9 = (bf16[64,128]{1,0:T(8,128)(2,1)S(1)}, bf16[64,128]{1,0:T(8,128)(2,1)S(1)}, u32[]{:S(2)}, u32[]{:S(2)}) collective-permute-start(bf16[64,128]{1,0:T(8,128)(2,1)S(1)} %get-tuple-element.27), channel_id=1, source_target_pairs={{0,2},{1,3},{2,0},{3,1},{4,6},{5,7},{6,4},{7,5},{8,10},{9,11},{10,... | collective-permute-start | bytes 49160 | tf_op jit(solution)/shard_map/ppermute | solution.py:30
  48.2 2.0 %collective-permute-start.11 = (bf16[64,3584]{1,0:T(8,128)(2,1)S(1)}, bf16[64,3584]{1,0:T(8,128)(2,1)}, u32[]{:S(2)}, u32[]{:S(2)}) collective-permute-start(bf16[64,3584]{1,0:T(8,128)(2,1)S(1)} %constant_dynamic-slice_fusion.5), channel_id=1, source_target_pairs={{0,1},{1,0},{2,3},{3,2},{4,5},{5,4},{6,7},{7,6},{8,9},{9,8},{10,11... | collective-permute-start | bytes 1376264 | tf_op jit(solution)/shard_map/ppermute | solution.py:30
  51.5 6.1 %collective-permute-start.12 = (bf16[32,3584]{1,0:T(8,128)(2,1)S(1)}, bf16[32,3584]{1,0:T(8,128)(2,1)S(1)}, u32[]{:S(2)}, u32[]{:S(2)}) collective-permute-start(bf16[32,3584]{1,0:T(8,128)(2,1)S(1)} %broadcast_select_fusion.2), channel_id=1, source_target_pairs={{0,4},{1,3},{2,6},{3,1},{4,0},{5,7},{6,2},{7,5},{8,12},{9,11},{10,... | collective-permute-start | bytes 688136 | tf_op jit(solution)/shard_map/ppermute | solution.py:30
  57.7 4.9 %collective-permute-start.13 = (bf16[16,3584]{1,0:T(8,128)(2,1)S(1)}, bf16[16,3584]{1,0:T(8,128)(2,1)S(1)}, u32[]{:S(2)}, u32[]{:S(2)}) collective-permute-start(bf16[16,3584]{1,0:T(8,128)(2,1)S(1)} %broadcast_select_fusion.9), channel_id=1, source_target_pairs={{0,2},{1,5},{2,0},{3,7},{4,6},{5,1},{6,4},{7,3},{8,10},{9,13},{10,... | collective-permute-start | bytes 344072 | tf_op jit(solution)/shard_map/ppermute | solution.py:30
  62.6 6.2 %collective-permute-start.14 = (bf16[8,3584]{1,0:T(8,128)(2,1)S(1)}, bf16[8,3584]{1,0:T(8,128)(2,1)S(1)}, u32[]{:S(2)}, u32[]{:S(2)}) collective-permute-start(bf16[8,3584]{1,0:T(8,128)(2,1)S(1)} %slice.111), channel_id=1, source_target_pairs={{0,8},{1,9},{2,10},{3,11},{4,12},{5,13},{6,14},{7,15},{8,0},{9,1},... | collective-permute-start | bytes 172040 | tf_op jit(solution)/shard_map/ppermute | solution.py:30
  68.9 1.3 %collective-permute-start.15 = (bf16[4,3584]{1,0:T(4,128)(2,1)S(1)}, bf16[4,3584]{1,0:T(4,128)(2,1)S(1)}, u32[]{:S(2)}, u32[]{:S(2)}) collective-permute-start(bf16[4,3584]{1,0:T(4,128)(2,1)S(1)} %broadcast_select_fusion.17), channel_id=1, source_target_pairs={{0,1},{1,0},{2,3},{3,2},{4,5},{5,4},{6,7},{7,6},{8,9},{9,8},{10,11... | collective-permute-start | bytes 86024 | tf_op jit(solution)/shard_map/ppermute | solution.py:30

commit v4 on v3

v4 whole, which is shorter than its diff:
```python
import jax
import jax.numpy as jnp
from jax import lax
from jax.experimental import pallas as pl
from jax.experimental.pallas import tpu as pltpu
from jax.experimental.layout import Layout, with_layout_constraint
from jax.sharding import PartitionSpec as P

VMEM = pl.BlockSpec(memory_space=pltpu.VMEM)
HBM = pl.BlockSpec(memory_space=pltpu.HBM)


def by_rows(value):
    return with_layout_constraint(value, Layout((0, 1)))


def lookup(table, index):
    keys = jnp.arange(table.shape[0], dtype=jnp.int32)
    return jnp.sum(jnp.where(index[..., None] == keys, table, 0), axis=-1)


def trade(value, even, odd):
    members = lax.axis_size("tensor")
    pairs = []
    for e in range(lax.axis_size("expert")):
        for t in range(members):
            along, across = odd if t % 2 else even
            pairs.append((e * members + t, (e ^ along) * members + (t ^ across)))
    return lax.ppermute(value, ("expert", "tensor"), pairs)


def halves(size):
    masks = []
    while size > 1:
        size //= 2
        masks.append(size)
    return masks


def ordered(flip, first, second):
    return jnp.where(flip, second, first), jnp.where(flip, first, second)


def code_kernel(x, table, out, weights, sems):
    depth = weights.shape[0]
    step = depth // sems.shape[0]
    copies = [
        pltpu.make_async_copy(table.at[pl.ds(k, step)], weights.at[pl.ds(k, step)], sems.at[k // step])
        for k in range(0, depth, step)
    ]
    for copy in copies:
        copy.start()
    total = jnp.zeros(out.shape, jnp.float32)
    for k in range(0, depth, step):
        copies[k // step].wait()
        total += jnp.dot(x[:, k : k + step], weights[k : k + step, :], preferred_element_type=jnp.float32)
    out[...] = total.astype(out.dtype)


def code_product(x, table):
    depth, rank = table.shape
    return pl.pallas_call(
        code_kernel,
        out_shape=jax.ShapeDtypeStruct((x.shape[0], rank), jnp.bfloat16),
        in_specs=[VMEM, HBM],
        out_specs=VMEM,
        scratch_shapes=[pltpu.VMEM(table.shape, table.dtype), pltpu.SemaphoreType.DMA((4,))],
        compiler_params=pltpu.CompilerParams(vmem_limit_bytes=32 << 20),
        cost_estimate=pl.CostEstimate(
            flops=2 * x.shape[0] * depth * rank, bytes_accessed=2 * table.size, transcendentals=0
        ),
    )(x, table)


def gate_up_kernel(x, base, out, weights, sems):
    depth, _, columns = weights.shape
    step = depth // sems.shape[0]
    copies = [
        pltpu.make_async_copy(base.at[pl.ds(k, step)], weights.at[pl.ds(k, step)], sems.at[k // step])
        for k in range(0, depth, step)
    ]
    for copy in copies:
        copy.start()
    row = lax.broadcasted_iota(jnp.int32, (128, 512), 0)
    column = lax.broadcasted_iota(jnp.int32, (128, 512), 1)
    target = 2 * row + jnp.where(column < 256, 0, 257)
    spread = jnp.where(column == target, 1.0, 0.0).astype(jnp.bfloat16)
    flat = weights.reshape(2 * depth, columns)
    total = jnp.zeros(out.shape, jnp.float32)
    for k in range(0, depth, step):
        wide = [
            jnp.dot(x[:, i : i + 128], spread, preferred_element_type=jnp.float32).astype(jnp.bfloat16)
            for i in range(k, k + step, 128)
        ]
        even = jnp.concatenate([part[:, :256] for part in wide], axis=1)
        odd = jnp.concatenate([part[:, 256:] for part in wide], axis=1)
        copies[k // step].wait()
        total += jnp.dot(
            jnp.concatenate([even, odd]), flat[2 * k : 2 * (k + step), :], preferred_element_type=jnp.float32
        )
    out[...] = total


def gate_up_product(x, base):
    depth, _, columns = base.shape
    return pl.pallas_call(
        gate_up_kernel,
        out_shape=jax.ShapeDtypeStruct((2 * x.shape[0], columns), jnp.float32),
        in_specs=[VMEM, HBM],
        out_specs=VMEM,
        scratch_shapes=[pltpu.VMEM(base.shape, base.dtype), pltpu.SemaphoreType.DMA((depth // 512,))],
        compiler_params=pltpu.CompilerParams(vmem_limit_bytes=32 << 20),
        cost_estimate=pl.CostEstimate(
            flops=4 * x.shape[0] * depth * columns, bytes_accessed=2 * base.size, transcendentals=0
        ),
    )(x, base)


def local(
    tokens,
    routes,
    numerators,
    place,
    base_in,
    base_down,
    delta_in,
    delta_mid,
    delta_down,
    delta_back,
):
    clusters = lax.axis_size("expert")
    members = lax.axis_size("tensor")
    me = lax.axis_index("tensor")
    cluster = lax.axis_index("expert")
    core = me % 2
    count, width = tokens.shape[1:]
    top = routes.shape[2]

    along, across = halves(clusters), halves(members // 2)
    shared, paired = along[: len(along) - len(across)], along[len(along) - len(across) :]

    side = jnp.concatenate([routes[0], numerators[0]], axis=1).astype(jnp.bfloat16)
    held = jnp.concatenate([tokens[0], jnp.pad(side, ((0, 0), (0, 128 - 2 * top)))], axis=1)

    for mask in shared:
        held = jnp.concatenate([held, trade(held, (mask, 0), (mask, 0))])
    for z, x in zip(paired, across):
        size = held.shape[0]
        flag = (me // (2 * x)) % 2 == 1
        held = jnp.concatenate(ordered((core == 0) & flag, held, trade(held, (0, 2 * x), (z, 0))))
        low, high = ordered((core == 1) & flag, held, trade(held, (z, 0), (0, 2 * x)))
        inner = ordered(core == 1, low[size:], high[:size])
        held = jnp.concatenate([low[:size], *inner, high[size:]])
    held = by_rows(jnp.concatenate(ordered(core == 1, held, trade(held, (0, 1), (0, 1)))))

    codes = code_product(held, delta_in[0])
    projected = gate_up_product(held, base_in[0])

    side = by_rows(held[:, width:])
    all_routes = side[:, :top].astype(jnp.int32)
    numerator = side[:, top : 2 * top].astype(jnp.float32)
    position = lookup(place, all_routes)
    weight = (2.5 * numerator / jnp.sum(numerator, axis=-1, keepdims=True)).astype(jnp.bfloat16)
    target = cluster * members + jnp.arange(members, dtype=jnp.int32)
    scale = jnp.sum(
        jnp.where(position[None] == target[:, None, None], weight[None].astype(jnp.float32), 0.0), axis=-1
    )

    codes = jnp.stack([codes if m == 0 else trade(codes, (0, m), (0, m)) for m in range(members)])
    by_slot = jnp.stack([lax.dynamic_index_in_dim(codes, s ^ me, 0, keepdims=False) for s in range(members)])

    lifted = jnp.einsum("srk,skgf->srgf", by_slot, delta_mid[0], preferred_element_type=jnp.float32)
    total = held.shape[0]
    hidden = jax.nn.silu(projected[None, :total] + lifted[:, :, 0]) * (projected[None, total:] + lifted[:, :, 1])
    hidden_sum = jnp.sum(scale[:, :, None] * hidden, axis=0).astype(jnp.bfloat16)
    partial_codes = jnp.einsum(
        "srf,sfk->srk", hidden.astype(jnp.bfloat16), delta_down[0], preferred_element_type=jnp.float32
    ).astype(jnp.bfloat16)
    lowrank = lax.dynamic_index_in_dim(partial_codes, me, 0, keepdims=False).astype(jnp.float32)
    for m in range(1, members):
        sent = lax.dynamic_index_in_dim(partial_codes, me ^ m, 0, keepdims=False)
        lowrank = lowrank + trade(sent, (0, m), (0, m)).astype(jnp.float32)
    own_scale = lax.dynamic_index_in_dim(scale, me, 0, keepdims=False)
    scaled = (own_scale[:, None] * lowrank).astype(jnp.bfloat16)

    term = jnp.dot(hidden_sum, base_down[0], preferred_element_type=jnp.float32)
    term = (term + jnp.dot(scaled, delta_back[0], preferred_element_type=jnp.float32)).astype(jnp.bfloat16)

    def add(kept, received):
        return (kept.astype(jnp.float32) + received.astype(jnp.float32)).astype(jnp.bfloat16)

    kept, sent = ordered(core == 1, term[: total // 2], term[total // 2 :])
    total = add(kept, trade(sent, (0, 1), (0, 1)))
    for z, x in reversed(list(zip(paired, across))):
        flag = (me // (2 * x)) % 2 == 1
        size = total.shape[0] // 4
        blocks = [total[i * size : (i + 1) * size] for i in range(4)]
        inner = ordered(core == 1, blocks[1], blocks[2])
        kept, sent = ordered(
            (core == 1) & flag,
            jnp.concatenate([blocks[0], inner[0]]),
            jnp.concatenate([inner[1], blocks[3]]),
        )
        total = add(kept, trade(sent, (z, 0), (0, 2 * x)))
        kept, sent = ordered((core == 0) & flag, total[:size], total[size:])
        total = add(kept, trade(sent, (0, 2 * x), (z, 0)))
    for mask in reversed(shared):
        size = total.shape[0] // 2
        total = add(total[:size], trade(total[size:], (mask, 0), (mask, 0)))
    return total[None]


def solution(mesh):
    placed = (
        P(None, ("parts", "expert", "tensor"), None),
        P(None, ("parts", "expert", "tensor"), None),
        P(None, ("parts", "expert", "tensor"), None),
        P("parts"),
        P("expert", None, None, "tensor"),
        P("expert", "tensor", None),
        P(("expert", "tensor"), None, None),
        P("expert", None, None, None, "tensor"),
        P("expert", None, "tensor", None),
        P(("expert", "tensor"), None, None),
    )
    return jax.shard_map(
        local,
        mesh=mesh,
        in_specs=placed,
        out_specs=P(None, ("parts", "expert", "tensor"), None),
        check_vma=False,
    )
```

time: 71.1 us -> 65.4 us (0.920)
  local copies, waits for them, and re-layouts: 11.9 us -> 4.86 us
  waiting for transfers between devices: 25.4 us -> 30.8 us
  starting transfers between devices: 18 us -> 14.9 us
  Pallas kernels: 9.59 us -> 6.89 us
  other arithmetic: 3.93 us -> 5.66 us
    unnamed x22 -> x14, local copies, waits for them, and re-layouts: 10.8 us -> 4.66 us
    ppermute x16 -> x14, waiting for transfers between devices: 25.4 us -> 30.8 us  [trade(): return lax.ppermute(value, ('expert', 'tensor'), pairs)]
    ppermute x16 -> x14, starting transfers between devices: 18 us -> 14.9 us  [trade(): return lax.ppermute(value, ('expert', 'tensor'), pairs)]
    pallas_call x5 -> x2, Pallas kernels: 9.59 us -> 6.89 us  [the longest x1 4.99 us: gate_up_product(): pl.pallas_call(gate_up_kernel, out_shape=jax.ShapeDtypeStruct((2 * x.shap...]
    convert_element_type x4 -> x3, other arithmetic: 1.27 us -> 0.3 us  [add(): (kept.astype(jnp.float32) + received.astype(jnp.float32)).astype(jnp.bflo...]
    squeeze x1 -> x0, local copies, waits for them, and re-layouts: 0.92 us -> none  [local(): tokens[0, :, half:]]
    select_n x10 -> x8, other arithmetic: 0.46 us -> 1.35 us  [ordered(): return (jnp.where(flip, second, first), jnp.where(flip, first, second))]
    concatenate x1 -> x2, other arithmetic: 0.04 us -> 0.92 us  [the longest x1 0.85 us: local(): jnp.concatenate([tokens[0], jnp.pad(side, ((0, 0), (0, 128 - 2 * top)))],...]
  transfers between devices with their start and end apart: 16 -> 14, of which waited for: 12 -> 10; matrix products, arithmetic and copies ran while one was open for 2% -> 2% of each run, Pallas kernels for 13% -> 8%
where the time goes in v4:
time: 65.4 us; the launch traced here: 65.1 us
  waiting for transfers between devices  30.8 us (47%)
  starting transfers between devices  14.9 us (23%)
  Pallas kernels  6.89 us (11%)
  other arithmetic  5.66 us (9%)
  local copies, waits for them, and re-layouts  4.86 us (7%)
  matrix products  1.63 us (2%)
    ppermute x14, waiting for transfers between devices, trade(): return lax.ppermute(value, ('expert', 'tensor'), pairs)  30.8 us
    ppermute x14, starting transfers between devices, trade(): return lax.ppermute(value, ('expert', 'tensor'), pairs)  14.9 us
    pallas_call x1, Pallas kernels, gate_up_product(): pl.pallas_call(gate_up_kernel, out_shape=jax.ShapeDtypeStruct((2 * x.shap...  4.99 us
    unnamed x14, local copies, waits for them, and re-layouts  4.66 us
    pallas_call x1, Pallas kernels, code_product(): pl.pallas_call(code_kernel, out_shape=jax.ShapeDtypeStruct((x.shape[0], r...  1.91 us
    select_n x8, other arithmetic, ordered(): return (jnp.where(flip, second, first), jnp.where(flip, first, second))  1.35 us
  transfers between devices with their start and end apart: 14, of which 10 were waited for; matrix products, arithmetic and copies ran while one was open for 2% of the time, Pallas kernels for 8%

profile of v4, /device:TPU:0, one launch (start us, length us, event | category | flops | bytes accessed | tf_op | source)
XLA Modules:
  0.0 65.1 jit_solution(11298048463744151214)
XLA Ops:
  0.0 0.8 %convert_bitcast_fusion = (bf16[4,8]{1,0:T(4,128)(2,1)S(1)}, bf16[4,8]{1,0:T(4,128)(2,1)S(1)}) fusion(s32[1,4,8]{2,1,0:T(4,128)} %param.12, s32[1,4,8]{2,1,0:T(4,128)} %param.11), kind=kLoop, calls=%fused_computation.86 | loop fusion | flops 64 | bytes 384 | tf_op jit(solution)/shard_map/squeeze | solution.py:142
  0.8 0.1 fusion.36
  0.9 0.8 %pad_maximum_fusion.7 = bf16[4,7296]{1,0:T(4,128)(2,1)S(1)} fusion(bf16[4,128]{1,0:T(4,128)(2,1)S(1)} %fusion.36, bf16[4,7168]{1,0:T(4,128)(2,1)} %bitcast.64), kind=kLoop, calls=%fused_computation.53 | loop fusion | flops 116736 | bytes 116736 | tf_op jit(solution)/shard_map/concatenate | solution.py:143
  1.8 4.1 %collective-permute-start = (bf16[4,7296]{1,0:T(4,128)(2,1)S(1)}, bf16[4,7296]{1,0:T(4,128)(2,1)S(1)}, u32[]{:S(2)}, u32[]{:S(2)}) collective-permute-start(bf16[4,7296]{1,0:T(4,128)(2,1)S(1)} %pad_maximum_fusion.7), channel_id=1, source_target_pairs={{0,8},{1,9},{2,10},{3,11},{4,12},{5,13},{6,14},{7,15},{8,0},{9,1},... | collective-permute-start | bytes 175112 | tf_op jit(solution)/shard_map/ppermute | solution.py:29
  5.9 2.8 %collective-permute-done = bf16[4,7296]{1,0:T(4,128)(2,1)S(1)} collective-permute-done((bf16[4,7296]{1,0:T(4,128)(2,1)S(1)}, bf16[4,7296]{1,0:T(4,128)(2,1)S(1)}, u32[]{:S(2)}, u32[]{:S(2)}) %collective-permute-start) | collective-permute-done | bytes 58400 | tf_op jit(solution)/shard_map/ppermute | solution.py:29
  8.7 0.9 %pad_maximum_fusion.5 = bf16[8,7296]{1,0:T(8,128)(2,1)S(1)} fusion(bf16[4,7296]{1,0:T(4,128)(2,1)S(1)} %collective-permute-done, bf16[4,128]{1,0:T(4,128)(2,1)S(1)} %fusion.36, bf16[4,7168]{1,0:T(4,128)(2,1)} %bitcast.65), kind=kLoop, calls=%fused_computation.34 | loop fusion | flops 350208 | bytes 233472 | tf_op jit(solution)/shard_map/concatenate | solution.py:146
  9.5 2.4 %collective-permute-start.1 = (bf16[8,7296]{1,0:T(8,128)(2,1)S(1)}, bf16[8,7296]{1,0:T(8,128)(2,1)S(1)}, u32[]{:S(2)}, u32[]{:S(2)}) collective-permute-start(bf16[8,7296]{1,0:T(8,128)(2,1)S(1)} %pad_maximum_fusion.5), channel_id=1, source_target_pairs={{0,2},{1,5},{2,0},{3,7},{4,6},{5,1},{6,4},{7,3},{8,10},{9,13},{10,... | collective-permute-start | bytes 350216 | tf_op jit(solution)/shard_map/ppermute | solution.py:29
  11.9 2.8 %collective-permute-done.1 = bf16[8,7296]{1,0:T(8,128)(2,1)S(1)} collective-permute-done((bf16[8,7296]{1,0:T(8,128)(2,1)S(1)}, bf16[8,7296]{1,0:T(8,128)(2,1)S(1)}, u32[]{:S(2)}, u32[]{:S(2)}) %collective-permute-start.1) | collective-permute-done | bytes 116768 | tf_op jit(solution)/shard_map/ppermute | solution.py:29
  14.7 0.9 %broadcast_select_fusion.9 = (bf16[8,7296]{1,0:T(8,128)(2,1)S(1)}, bf16[8,7296]{1,0:T(8,128)(2,1)S(1)}) fusion(bf16[8,7296]{1,0:T(8,128)(2,1)S(1)} %collective-permute-done.1, pred[]{:T(512)S(6)} %and.29, bf16[4,7296]{1,0:T(4,128)(2,1)S(1)} %collective-permute-done, bf16[4,128]{1,0:T(4,128)(2,1)S(1)} %fusion.36, bf16[4,7168]{1,0:T(4,128)(2,1)} %bitcast.66), kind=kLoop, calls=%fused_computation.38 | loop fusion | flops 466944 | bytes 466945 | tf_op jit(solution)/shard_map/jit(_where)/select_n | solution.py:41
  15.7 1.0 %collective-permute-start.2 = (bf16[16,7296]{1,0:T(8,128)(2,1)S(1)}, bf16[16,7296]{1,0:T(8,128)(2,1)S(1)}, u32[]{:S(2)}, u32[]{:S(2)}) collective-permute-start(bf16[16,7296]{1,0:T(8,128)(2,1)S(1)} %pad_maximum_fusion.2), channel_id=1, source_target_pairs={{0,4},{1,3},{2,6},{3,1},{4,0},{5,7},{6,2},{7,5},{8,12},{9,11},{10,... | collective-permute-start | bytes 700424 | tf_op jit(solution)/shard_map/ppermute | solution.py:29
  16.7 5.1 %collective-permute-done.2 = bf16[16,7296]{1,0:T(8,128)(2,1)S(1)} collective-permute-done((bf16[16,7296]{1,0:T(8,128)(2,1)S(1)}, bf16[16,7296]{1,0:T(8,128)(2,1)S(1)}, u32[]{:S(2)}, u32[]{:S(2)}) %collective-permute-start.2) | collective-permute-done | bytes 233504 | tf_op jit(solution)/shard_map/ppermute | solution.py:29
  21.8 0.1 broadcast_select_fusion.4
  22.0 0.1 collective-permute-start.3
  22.1 1.8 %collective-permute-done.3 = bf16[32,7296]{1,0:T(8,128)(2,1)S(1)} collective-permute-done((bf16[32,7296]{1,0:T(8,128)(2,1)S(1)}, bf16[32,7296]{1,0:T(8,128)(2,1)S(1)}, u32[]{:S(2)}, u32[]{:S(2)}) %collective-permute-start.3) | collective-permute-done | bytes 466976 | tf_op jit(solution)/shard_map/ppermute | solution.py:29
  23.9 0.2 broadcast_select_fusion.1
  24.0 0.2 convert_reduce_fusion
  24.2 0.1 pad_maximum_fusion.x
  24.3 1.2 %copy-done.2 = bf16[1,7168,128]{2,1,0:T(8,128)(2,1)S(1)} copy-done((bf16[1,7168,128]{2,1,0:T(8,128)(2,1)S(1)}, bf16[1,7168,128]{2,1,0:T(8,128)(2,1)}, u32[]{:S(2)}) %copy-start.2) | copy-done | bytes 1835032
  25.5 1.9 %shard_map.101 = bf16[64,128]{1,0:T(8,128)(2,1)S(1)} custom-call(bf16[64,7296]{1,0:T(8,128)(2,1)S(1)} %pad_maximum_fusion.x, bf16[7168,128]{1,0:T(8,128)(2,1)S(1)} %bitcast.61), custom_call_target="tpu_custom_call" | custom-call | flops 117440512 | bytes 1835008 | tf_op jit(solution)/shard_map/pallas_call | solution.py:62
  27.4 1.8 %collective-permute-start.6 = (bf16[64,128]{1,0:T(8,128)(2,1)S(1)}, bf16[64,128]{1,0:T(8,128)(2,1)S(1)}, u32[]{:S(2)}, u32[]{:S(2)}) collective-permute-start(bf16[64,128]{1,0:T(8,128)(2,1)S(1)} %shard_map.101), channel_id=1, source_target_pairs={{0,3},{1,2},{2,1},{3,0},{4,7},{5,6},{6,5},{7,4},{8,11},{9,10},{10,... | collective-permute-start | bytes 49160 | tf_op jit(solution)/shard_map/ppermute | solution.py:29
  29.3 0.3 collective-permute-start.5
  29.7 0.1 fusion.27
  29.9 3.1 %copy-done.1 = bf16[1,7168,2,256]{3,2,1,0:T(2,128)(2,1)S(1)} copy-done((bf16[1,7168,2,256]{3,2,1,0:T(2,128)(2,1)S(1)}, bf16[1,7168,2,256]{3,2,1,0:T(2,128)(2,1)}, u32[]{:S(2)}) %copy-start.1) | copy-done | bytes 7340056
  33.0 5.0 %shard_map.100 = f32[128,256]{1,0:T(8,128)S(1)} custom-call(bf16[64,7296]{1,0:T(8,128)(2,1)S(1)} %pad_maximum_fusion.x, bf16[7168,2,256]{2,1,0:T(2,128)(2,1)S(1)} %bitcast.60), custom_call_target="tpu_custom_call" | custom-call | flops 469762048 | bytes 7340032 | tf_op jit(solution)/shard_map/pallas_call | solution.py:106
  38.0 0.1 select_reduce_fusion
  38.1 0.1 select_reduce_fusion.1
  38.3 0.2 fusion.4
  38.5 0.1 multiply_reduce_fusion
  38.6 0.3 copy-done.5
  38.9 0.2 convolution_convert_fusion
  39.1 0.5 collective-permute-start.7
  39.7 1.4 %collective-permute-start.9 = (bf16[64,128]{1,0:T(8,128)(2,1)S(1)}, bf16[64,128]{1,0:T(8,128)(2,1)S(1)}, u32[]{:S(2)}, u32[]{:S(2)}) collective-permute-start(bf16[64,128]{1,0:T(8,128)(2,1)S(1)} %get-tuple-element.26), channel_id=1, source_target_pairs={{0,3},{1,2},{2,1},{3,0},{4,7},{5,6},{6,5},{7,4},{8,11},{9,10},{10,... | collective-permute-start | bytes 49160 | tf_op jit(solution)/shard_map/ppermute | solution.py:29
  41.0 0.3 collective-permute-start.8
  41.4 0.8 %fusion.1 = f32[64,7168]{1,0:T(8,128)S(1)} fusion(bf16[1,256,7168]{2,1,0:T(8,128)(2,1)S(1)} %copy-done.3, bf16[64,256]{1,0:T(8,128)(2,1)S(1)} %get-tuple-element.5), kind=kOutput, calls=%fused_computation.2 | convolution fusion | flops 234881024 | bytes 5537792 | tf_op jit(solution)/shard_map/dot_general | solution.py:186
  42.2 0.7 %collective-permute-done.9 = bf16[64,128]{1,0:T(8,128)(2,1)S(1)} collective-permute-done((bf16[64,128]{1,0:T(8,128)(2,1)S(1)}, bf16[64,128]{1,0:T(8,128)(2,1)S(1)}, u32[]{:S(2)}, u32[]{:S(2)}) %collective-permute-start.9) | collective-permute-done | bytes 16416 | tf_op jit(solution)/shard_map/ppermute | solution.py:29
  42.8 2.0 %collective-permute-done.8 = bf16[64,128]{1,0:T(8,128)(2,1)S(1)} collective-permute-done((bf16[64,128]{1,0:T(8,128)(2,1)S(1)}, bf16[64,128]{1,0:T(8,128)(2,1)S(1)}, u32[]{:S(2)}, u32[]{:S(2)}) %collective-permute-start.8) | collective-permute-done | bytes 16416 | tf_op jit(solution)/shard_map/ppermute | solution.py:29
  44.8 0.5 fusion
  45.4 0.1 collective-permute-start.10
  45.4 1.8 %collective-permute-done.10 = bf16[32,7168]{1,0:T(8,128)(2,1)S(1)} collective-permute-done((bf16[32,7168]{1,0:T(8,128)(2,1)S(1)}, bf16[32,7168]{1,0:T(8,128)(2,1)S(1)}, u32[]{:S(2)}, u32[]{:S(2)}) %collective-permute-start.10) | collective-permute-done | bytes 458784 | tf_op jit(solution)/shard_map/ppermute | solution.py:29
  47.2 0.2 add_convert_fusion
  47.5 0.6 collective-permute-start.11
  48.1 5.5 %collective-permute-done.11 = bf16[16,7168]{1,0:T(8,128)(2,1)S(1)} collective-permute-done((bf16[16,7168]{1,0:T(8,128)(2,1)S(1)}, bf16[16,7168]{1,0:T(8,128)(2,1)S(1)}, u32[]{:S(2)}, u32[]{:S(2)}) %collective-permute-start.11) | collective-permute-done | bytes 229408 | tf_op jit(solution)/shard_map/ppermute | solution.py:29
  53.6 0.1 add_convert_fusion.1
  53.7 0.4 collective-permute-start.12
  54.1 4.4 %collective-permute-done.12 = bf16[8,7168]{1,0:T(8,128)(2,1)S(1)} collective-permute-done((bf16[8,7168]{1,0:T(8,128)(2,1)S(1)}, bf16[8,7168]{1,0:T(8,128)(2,1)S(1)}, u32[]{:S(2)}, u32[]{:S(2)}) %collective-permute-start.12) | collective-permute-done | bytes 114720 | tf_op jit(solution)/shard_map/ppermute | solution.py:29
  58.7 1.7 %collective-permute-start.13 = (bf16[4,7168]{1,0:T(4,128)(2,1)S(1)}, bf16[4,7168]{1,0:T(4,128)(2,1)S(1)}, u32[]{:S(2)}, u32[]{:S(2)}) collective-permute-start(bf16[4,7168]{1,0:T(4,128)(2,1)S(1)} %slice.107), channel_id=1, source_target_pairs={{0,8},{1,9},{2,10},{3,11},{4,12},{5,13},{6,14},{7,15},{8,0},{9,1},... | collective-permute-start | bytes 172040 | tf_op jit(solution)/shard_map/ppermute | solution.py:29
  60.4 4.0 %collective-permute-done.13 = bf16[4,7168]{1,0:T(4,128)(2,1)S(1)} collective-permute-done((bf16[4,7168]{1,0:T(4,128)(2,1)S(1)}, bf16[4,7168]{1,0:T(4,128)(2,1)S(1)}, u32[]{:S(2)}, u32[]{:S(2)}) %collective-permute-start.13) | collective-permute-done | bytes 57376 | tf_op jit(solution)/shard_map/ppermute | solution.py:29
  64.4 0.7 %fusion.17 = bf16[1,4,7168]{2,1,0:T(4,128)(2,1)} fusion(bf16[4,7168]{1,0:T(4,128)(2,1)S(1)} %collective-permute-done.13, bf16[8,7168]{1,0:T(8,128)(2,1)S(1)} %add_convert_fusion.2), kind=kLoop, calls=%fused_computation.54 | loop fusion | flops 114688 | bytes 172032 | tf_op jit(solution)/shard_map/broadcast_in_dim | solution.py:210
  (34 shorter events, 0.6 us)
Async XLA Ops:
  0.0 44.8 %copy-start = (bf16[1,128,7168]{2,1,0:T(8,128)(2,1)S(1)}, bf16[1,128,7168]{2,1,0:T(8,128)(2,1)}, u32[]{:S(2)}) copy-start(bf16[1,128,7168]{2,1,0:T(8,128)(2,1)} %param.19) | copy-start | bytes 5505028
  1.8 6.9 %collective-permute-start = (bf16[4,7296]{1,0:T(4,128)(2,1)S(1)}, bf16[4,7296]{1,0:T(4,128)(2,1)S(1)}, u32[]{:S(2)}, u32[]{:S(2)}) collective-permute-start(bf16[4,7296]{1,0:T(4,128)(2,1)S(1)} %pad_maximum_fusion.7), channel_id=1, source_target_pairs={{0,8},{1,9},{2,10},{3,11},{4,12},{5,13},{6,14},{7,15},{8,0},{9,1},... | collective-permute-start | bytes 175112 | tf_op jit(solution)/shard_map/ppermute | solution.py:29
  9.5 5.2 %collective-permute-start.1 = (bf16[8,7296]{1,0:T(8,128)(2,1)S(1)}, bf16[8,7296]{1,0:T(8,128)(2,1)S(1)}, u32[]{:S(2)}, u32[]{:S(2)}) collective-permute-start(bf16[8,7296]{1,0:T(8,128)(2,1)S(1)} %pad_maximum_fusion.5), channel_id=1, source_target_pairs={{0,2},{1,5},{2,0},{3,7},{4,6},{5,1},{6,4},{7,3},{8,10},{9,13},{10,... | collective-permute-start | bytes 350216 | tf_op jit(solution)/shard_map/ppermute | solution.py:29
  15.7 6.1 %collective-permute-start.2 = (bf16[16,7296]{1,0:T(8,128)(2,1)S(1)}, bf16[16,7296]{1,0:T(8,128)(2,1)S(1)}, u32[]{:S(2)}, u32[]{:S(2)}) collective-permute-start(bf16[16,7296]{1,0:T(8,128)(2,1)S(1)} %pad_maximum_fusion.2), channel_id=1, source_target_pairs={{0,4},{1,3},{2,6},{3,1},{4,0},{5,7},{6,2},{7,5},{8,12},{9,11},{10,... | collective-permute-start | bytes 700424 | tf_op jit(solution)/shard_map/ppermute | solution.py:29
  22.0 1.9 %collective-permute-start.3 = (bf16[32,7296]{1,0:T(8,128)(2,1)S(1)}, bf16[32,7296]{1,0:T(8,128)(2,1)S(1)}, u32[]{:S(2)}, u32[]{:S(2)}) collective-permute-start(bf16[32,7296]{1,0:T(8,128)(2,1)S(1)} %pad_maximum_fusion.1), channel_id=1, source_target_pairs={{0,1},{1,0},{2,3},{3,2},{4,5},{5,4},{6,7},{7,6},{8,9},{9,8},{10,11... | collective-permute-start | bytes 1400840 | tf_op jit(solution)/shard_map/ppermute | solution.py:29
  24.0 1.5 %copy-start.2 = (bf16[1,7168,128]{2,1,0:T(8,128)(2,1)S(1)}, bf16[1,7168,128]{2,1,0:T(8,128)(2,1)}, u32[]{:S(2)}) copy-start(bf16[1,7168,128]{2,1,0:T(8,128)(2,1)} %param.16) | copy-start | bytes 5505028
  27.4 10.7 %collective-permute-start.6 = (bf16[64,128]{1,0:T(8,128)(2,1)S(1)}, bf16[64,128]{1,0:T(8,128)(2,1)S(1)}, u32[]{:S(2)}, u32[]{:S(2)}) collective-permute-start(bf16[64,128]{1,0:T(8,128)(2,1)S(1)} %shard_map.101), channel_id=1, source_target_pairs={{0,3},{1,2},{2,1},{3,0},{4,7},{5,6},{6,5},{7,4},{8,11},{9,10},{10,... | collective-permute-start | bytes 49160 | tf_op jit(solution)/shard_map/ppermute | solution.py:29
  29.3 8.9 %collective-permute-start.5 = (bf16[64,128]{1,0:T(8,128)(2,1)S(1)}, bf16[64,128]{1,0:T(8,128)(2,1)S(1)}, u32[]{:S(2)}, u32[]{:S(2)}) collective-permute-start(bf16[64,128]{1,0:T(8,128)(2,1)S(1)} %shard_map.101), channel_id=1, source_target_pairs={{0,2},{1,3},{2,0},{3,1},{4,6},{5,7},{6,4},{7,5},{8,10},{9,11},{10,... | collective-permute-start | bytes 49160 | tf_op jit(solution)/shard_map/ppermute | solution.py:29
  29.6 8.6 %collective-permute-start.4 = (bf16[64,128]{1,0:T(8,128)(2,1)S(1)}, bf16[64,128]{1,0:T(8,128)(2,1)S(1)}, u32[]{:S(2)}, u32[]{:S(2)}) collective-permute-start(bf16[64,128]{1,0:T(8,128)(2,1)S(1)} %shard_map.101), channel_id=1, source_target_pairs={{0,1},{1,0},{2,3},{3,2},{4,5},{5,4},{6,7},{7,6},{8,9},{9,8},{10,11... | collective-permute-start | bytes 49160 | tf_op jit(solution)/shard_map/ppermute | solution.py:29
  29.9 3.1 %copy-start.1 = (bf16[1,7168,2,256]{3,2,1,0:T(2,128)(2,1)S(1)}, bf16[1,7168,2,256]{3,2,1,0:T(2,128)(2,1)}, u32[]{:S(2)}) copy-start(bf16[1,7168,2,256]{3,2,1,0:T(2,128)(2,1)} %param.14) | copy-start | bytes 22020100
  33.0 5.0 %copy-start.6 = (s32[16]{0:T(128)S(1)}, s32[16]{0:T(128)}, u32[]{:S(2)}) copy-start(s32[16]{0:T(128)} %param.13) | copy-start | bytes 196
  33.0 5.3 %copy-start.4 = (bf16[1,4,128,2,256]{4,3,2,1,0:T(2,128)(2,1)S(1)}, bf16[1,4,128,2,256]{4,3,2,1,0:T(2,128)(2,1)}, u32[]{:S(2)}) copy-start(bf16[1,4,128,2,256]{4,3,2,1,0:T(2,128)(2,1)} %param.17) | copy-start | bytes 1572868
  33.0 8.4 %copy-start.3 = (bf16[1,256,7168]{2,1,0:T(8,128)(2,1)S(1)}, bf16[1,256,7168]{2,1,0:T(8,128)(2,1)}, u32[]{:S(2)}) copy-start(bf16[1,256,7168]{2,1,0:T(8,128)(2,1)} %param.15) | copy-start | bytes 11010052
  38.0 1.0 %copy-start.5 = (bf16[1,4,256,128]{3,2,1,0:T(8,128)(2,1)S(1)}, bf16[1,4,256,128]{3,2,1,0:T(8,128)(2,1)}, u32[]{:S(2)}) copy-start(bf16[1,4,256,128]{3,2,1,0:T(8,128)(2,1)} %param.18) | copy-start | bytes 786436
  39.1 3.0 %collective-permute-start.7 = (bf16[64,128]{1,0:T(8,128)(2,1)S(1)}, bf16[64,128]{1,0:T(8,128)(2,1)S(1)}, u32[]{:S(2)}, u32[]{:S(2)}) collective-permute-start(bf16[64,128]{1,0:T(8,128)(2,1)S(1)} %get-tuple-element.25), channel_id=1, source_target_pairs={{0,1},{1,0},{2,3},{3,2},{4,5},{5,4},{6,7},{7,6},{8,9},{9,8},{10,11... | collective-permute-start | bytes 49160 | tf_op jit(solution)/shard_map/ppermute | solution.py:29
  39.7 3.2 %collective-permute-start.9 = (bf16[64,128]{1,0:T(8,128)(2,1)S(1)}, bf16[64,128]{1,0:T(8,128)(2,1)S(1)}, u32[]{:S(2)}, u32[]{:S(2)}) collective-permute-start(bf16[64,128]{1,0:T(8,128)(2,1)S(1)} %get-tuple-element.26), channel_id=1, source_target_pairs={{0,3},{1,2},{2,1},{3,0},{4,7},{5,6},{6,5},{7,4},{8,11},{9,10},{10,... | collective-permute-start | bytes 49160 | tf_op jit(solution)/shard_map/ppermute | solution.py:29
  41.0 3.7 %collective-permute-start.8 = (bf16[64,128]{1,0:T(8,128)(2,1)S(1)}, bf16[64,128]{1,0:T(8,128)(2,1)S(1)}, u32[]{:S(2)}, u32[]{:S(2)}) collective-permute-start(bf16[64,128]{1,0:T(8,128)(2,1)S(1)} %get-tuple-element.27), channel_id=1, source_target_pairs={{0,2},{1,3},{2,0},{3,1},{4,6},{5,7},{6,4},{7,5},{8,10},{9,11},{10,... | collective-permute-start | bytes 49160 | tf_op jit(solution)/shard_map/ppermute | solution.py:29
  45.4 1.9 %collective-permute-start.10 = (bf16[32,7168]{1,0:T(8,128)(2,1)S(1)}, bf16[32,7168]{1,0:T(8,128)(2,1)S(1)}, u32[]{:S(2)}, u32[]{:S(2)}) collective-permute-start(bf16[32,7168]{1,0:T(8,128)(2,1)S(1)} %broadcast_select_fusion.2), channel_id=1, source_target_pairs={{0,1},{1,0},{2,3},{3,2},{4,5},{5,4},{6,7},{7,6},{8,9},{9,8},{10,11... | collective-permute-start | bytes 1376264 | tf_op jit(solution)/shard_map/ppermute | solution.py:29
  47.5 6.1 %collective-permute-start.11 = (bf16[16,7168]{1,0:T(8,128)(2,1)S(1)}, bf16[16,7168]{1,0:T(8,128)(2,1)S(1)}, u32[]{:S(2)}, u32[]{:S(2)}) collective-permute-start(bf16[16,7168]{1,0:T(8,128)(2,1)S(1)} %broadcast_select_fusion.5), channel_id=1, source_target_pairs={{0,4},{1,3},{2,6},{3,1},{4,0},{5,7},{6,2},{7,5},{8,12},{9,11},{10,... | collective-permute-start | bytes 688136 | tf_op jit(solution)/shard_map/ppermute | solution.py:29
  53.7 4.9 %collective-permute-start.12 = (bf16[8,7168]{1,0:T(8,128)(2,1)S(1)}, bf16[8,7168]{1,0:T(8,128)(2,1)S(1)}, u32[]{:S(2)}, u32[]{:S(2)}) collective-permute-start(bf16[8,7168]{1,0:T(8,128)(2,1)S(1)} %broadcast_select_fusion.12), channel_id=1, source_target_pairs={{0,2},{1,5},{2,0},{3,7},{4,6},{5,1},{6,4},{7,3},{8,10},{9,13},{10,... | collective-permute-start | bytes 344072 | tf_op jit(solution)/shard_map/ppermute | solution.py:29
  58.7 5.8 %collective-permute-start.13 = (bf16[4,7168]{1,0:T(4,128)(2,1)S(1)}, bf16[4,7168]{1,0:T(4,128)(2,1)S(1)}, u32[]{:S(2)}, u32[]{:S(2)}) collective-permute-start(bf16[4,7168]{1,0:T(4,128)(2,1)S(1)} %slice.107), channel_id=1, source_target_pairs={{0,8},{1,9},{2,10},{3,11},{4,12},{5,13},{6,14},{7,15},{8,0},{9,1},... | collective-permute-start | bytes 172040 | tf_op jit(solution)/shard_map/ppermute | solution.py:29

commit v5 on v4

--- a/solution.py
+++ b/solution.py
@@ -8,6 +8,10 @@
 
 VMEM = pl.BlockSpec(memory_space=pltpu.VMEM)
 HBM = pl.BlockSpec(memory_space=pltpu.HBM)
+
+
+def in_hbm(value):
+    return pltpu.with_memory_space_constraint(value, pltpu.HBM)
 
 
 def by_rows(value):
@@ -69,7 +73,7 @@
         cost_estimate=pl.CostEstimate(
             flops=2 * x.shape[0] * depth * rank, bytes_accessed=2 * table.size, transcendentals=0
         ),
-    )(x, table)
+    )(x, in_hbm(table))
 
 
 def gate_up_kernel(x, base, out, weights, sems):
@@ -113,7 +117,7 @@
         cost_estimate=pl.CostEstimate(
             flops=4 * x.shape[0] * depth * columns, bytes_accessed=2 * base.size, transcendentals=0
         ),
-    )(x, base)
+    )(x, in_hbm(base))
 
 
 def local(
@@ -140,10 +144,16 @@
     shared, paired = along[: len(along) - len(across)], along[len(along) - len(across) :]
 
     side = jnp.concatenate([routes[0], numerators[0]], axis=1).astype(jnp.bfloat16)
-    held = jnp.concatenate([tokens[0], jnp.pad(side, ((0, 0), (0, 128 - 2 * top)))], axis=1)
-
-    for mask in shared:
-        held = jnp.concatenate([held, trade(held, (mask, 0), (mask, 0))])
+    side = jnp.pad(side, ((0, 0), (0, 128 - 2 * top)))
+    held = lax.optimization_barrier(jnp.concatenate([tokens[0], side], axis=1))
+
+    for i, mask in enumerate(shared):
+        if i == 0:
+            pieces = [trade(piece, (mask, 0), (mask, 0)) for piece in (tokens[0], side)]
+            received = jnp.concatenate(pieces, axis=1)
+        else:
+            received = trade(held, (mask, 0), (mask, 0))
+        held = jnp.concatenate([held, received])
     for z, x in zip(paired, across):
         size = held.shape[0]
         flag = (me // (2 * x)) % 2 == 1

time: 65.4 us -> 60.3 us (0.922)
  local copies, waits for them, and re-layouts: 4.86 us -> 0.52 us
  waiting for transfers between devices: 30.8 us -> 33 us
  starting transfers between devices: 14.9 us -> 13.2 us
  other arithmetic: 5.66 us -> 4.06 us
    unnamed x14 -> x10, local copies, waits for them, and re-layouts: 4.66 us -> 0.32 us
    ppermute x14 -> x15, waiting for transfers between devices: 30.8 us -> 33 us  [trade(): return lax.ppermute(value, ('expert', 'tensor'), pairs)]
    ppermute x14 -> x15, starting transfers between devices: 14.9 us -> 13.2 us  [trade(): return lax.ppermute(value, ('expert', 'tensor'), pairs)]
    select_n x8, other arithmetic: 1.35 us -> 0.53 us  [ordered(): return (jnp.where(flip, second, first), jnp.where(flip, first, second))]
    concatenate x2, other arithmetic: 1.73 us -> 0.94 us  [the longest x1 0.88 us: local(): held = lax.optimization_barrier(jnp.concatenate([tokens[0], side], axis=1))]
  transfers between devices with their start and end apart: 14 -> 15, of which waited for: 10 -> 11; matrix products, arithmetic and copies ran while one was open for 2% -> 3% of each run, Pallas kernels for 8% -> 9%
where the time goes in v5:
time: 60.3 us; the launch traced here: 60.1 us
  waiting for transfers between devices  33 us (55%)
  starting transfers between devices  13.2 us (22%)
  Pallas kernels  7.39 us (12%)
  other arithmetic  4.06 us (7%)
  matrix products  1.65 us (3%)
    ppermute x15, waiting for transfers between devices, trade(): return lax.ppermute(value, ('expert', 'tensor'), pairs)  33 us
    ppermute x15, starting transfers between devices, trade(): return lax.ppermute(value, ('expert', 'tensor'), pairs)  13.2 us
    pallas_call x1, Pallas kernels, gate_up_product(): pl.pallas_call(gate_up_kernel, out_shape=jax.ShapeDtypeStruct((2 * x.shap...  5.47 us
    pallas_call x1, Pallas kernels, code_product(): pl.pallas_call(code_kernel, out_shape=jax.ShapeDtypeStruct((x.shape[0], r...  1.92 us
  transfers between devices with their start and end apart: 15, of which 11 were waited for; matrix products, arithmetic and copies ran while one was open for 3% of the time, Pallas kernels for 9%

profile of v5, /device:TPU:0, one launch (start us, length us, event | category | flops | bytes accessed | tf_op | source)
XLA Modules:
  0.0 60.1 jit_solution(9005920213550378798)
XLA Ops:
  0.0 0.8 %convert_bitcast_fusion = (bf16[4,8]{1,0:T(4,128)(2,1)S(1)}, bf16[4,8]{1,0:T(4,128)(2,1)S(1)}) fusion(s32[1,4,8]{2,1,0:T(4,128)} %param.12, s32[1,4,8]{2,1,0:T(4,128)} %param.11), kind=kLoop, calls=%fused_computation.86 | loop fusion | flops 64 | bytes 384 | tf_op jit(solution)/shard_map/squeeze | solution.py:146
  0.8 0.1 fusion.36
  0.9 4.0 %collective-permute-start.1 = (bf16[4,128]{1,0:T(4,128)(2,1)S(1)}, bf16[4,128]{1,0:T(4,128)(2,1)S(1)}, u32[]{:S(2)}, u32[]{:S(2)}) collective-permute-start(bf16[4,128]{1,0:T(4,128)(2,1)S(1)} %fusion.36), channel_id=1, source_target_pairs={{0,8},{1,9},{2,10},{3,11},{4,12},{5,13},{6,14},{7,15},{8,0},{9,1},... | collective-permute-start | bytes 3080 | tf_op jit(solution)/shard_map/ppermute | solution.py:33
  5.0 0.1 collective-permute-start
  5.0 0.9 %pad_maximum_fusion.6 = bf16[4,7296]{1,0:T(4,128)(2,1)S(1)} fusion(bf16[4,128]{1,0:T(4,128)(2,1)S(1)} %fusion.36, bf16[4,7168]{1,0:T(4,128)(2,1)} %bitcast.65), kind=kLoop, calls=%fused_computation.53 | loop fusion | flops 116736 | bytes 116736 | tf_op jit(solution)/shard_map/concatenate | solution.py:148
  5.9 0.6 collective-permute-done.1
  6.5 4.0 %collective-permute-done = bf16[4,7168]{1,0:T(4,128)(2,1)S(1)} collective-permute-done((bf16[4,7168]{1,0:T(4,128)(2,1)}, bf16[4,7168]{1,0:T(4,128)(2,1)S(1)}, u32[]{:S(2)}, u32[]{:S(2)}) %collective-permute-start) | collective-permute-done | bytes 57376 | tf_op jit(solution)/shard_map/ppermute | solution.py:33
  10.5 1.6 %collective-permute-start.2 = (bf16[8,7296]{1,0:T(8,128)(2,1)S(1)}, bf16[8,7296]{1,0:T(8,128)(2,1)S(1)}, u32[]{:S(2)}, u32[]{:S(2)}) collective-permute-start(bf16[8,7296]{1,0:T(8,128)(2,1)S(1)} %maximum_maximum_fusion), channel_id=1, source_target_pairs={{0,2},{1,5},{2,0},{3,7},{4,6},{5,1},{6,4},{7,3},{8,10},{9,13},{10,... | collective-permute-start | bytes 350216 | tf_op jit(solution)/shard_map/ppermute | solution.py:33
  12.1 3.5 %collective-permute-done.2 = bf16[8,7296]{1,0:T(8,128)(2,1)S(1)} collective-permute-done((bf16[8,7296]{1,0:T(8,128)(2,1)S(1)}, bf16[8,7296]{1,0:T(8,128)(2,1)S(1)}, u32[]{:S(2)}, u32[]{:S(2)}) %collective-permute-start.2) | collective-permute-done | bytes 116768 | tf_op jit(solution)/shard_map/ppermute | solution.py:33
  15.6 0.1 broadcast_select_fusion.9
  15.7 1.3 %collective-permute-start.3 = (bf16[16,7296]{1,0:T(8,128)(2,1)S(1)}, bf16[16,7296]{1,0:T(8,128)(2,1)S(1)}, u32[]{:S(2)}, u32[]{:S(2)}) collective-permute-start(bf16[16,7296]{1,0:T(8,128)(2,1)S(1)} %pad_maximum_fusion.2), channel_id=1, source_target_pairs={{0,4},{1,3},{2,6},{3,1},{4,0},{5,7},{6,2},{7,5},{8,12},{9,11},{10,... | collective-permute-start | bytes 700424 | tf_op jit(solution)/shard_map/ppermute | solution.py:33
  17.0 4.9 %collective-permute-done.3 = bf16[16,7296]{1,0:T(8,128)(2,1)S(1)} collective-permute-done((bf16[16,7296]{1,0:T(8,128)(2,1)S(1)}, bf16[16,7296]{1,0:T(8,128)(2,1)S(1)}, u32[]{:S(2)}, u32[]{:S(2)}) %collective-permute-start.3) | collective-permute-done | bytes 233504 | tf_op jit(solution)/shard_map/ppermute | solution.py:33
  21.8 0.1 broadcast_select_fusion.4
  22.0 0.1 collective-permute-start.4
  22.1 1.8 %collective-permute-done.4 = bf16[32,7296]{1,0:T(8,128)(2,1)S(1)} collective-permute-done((bf16[32,7296]{1,0:T(8,128)(2,1)S(1)}, bf16[32,7296]{1,0:T(8,128)(2,1)S(1)}, u32[]{:S(2)}, u32[]{:S(2)}) %collective-permute-start.4) | collective-permute-done | bytes 466976 | tf_op jit(solution)/shard_map/ppermute | solution.py:33
  23.9 0.2 broadcast_select_fusion.1
  24.0 0.2 convert_reduce_fusion
  24.2 0.1 pad_maximum_fusion.x
  24.3 1.9 %shard_map.101 = bf16[64,128]{1,0:T(8,128)(2,1)S(1)} custom-call(bf16[64,7296]{1,0:T(8,128)(2,1)S(1)} %pad_maximum_fusion.x, bf16[7168,128]{1,0:T(8,128)(2,1)} %bitcast.62), custom_call_target="tpu_custom_call" | custom-call | flops 117440512 | bytes 1835008 | tf_op jit(solution)/shard_map/pallas_call | solution.py:66
  26.2 1.3 %collective-permute-start.7 = (bf16[64,128]{1,0:T(8,128)(2,1)S(1)}, bf16[64,128]{1,0:T(8,128)(2,1)S(1)}, u32[]{:S(2)}, u32[]{:S(2)}) collective-permute-start(bf16[64,128]{1,0:T(8,128)(2,1)S(1)} %shard_map.101), channel_id=1, source_target_pairs={{0,3},{1,2},{2,1},{3,0},{4,7},{5,6},{6,5},{7,4},{8,11},{9,10},{10,... | collective-permute-start | bytes 49160 | tf_op jit(solution)/shard_map/ppermute | solution.py:33
  27.5 0.5 collective-permute-start.6
  28.1 0.1 collective-permute-start.5
  28.2 0.1 fusion.27
  28.4 5.5 %shard_map.100 = f32[128,256]{1,0:T(8,128)S(1)} custom-call(bf16[64,7296]{1,0:T(8,128)(2,1)S(1)} %pad_maximum_fusion.x, bf16[7168,2,256]{2,1,0:T(2,128)(2,1)} %bitcast.61), custom_call_target="tpu_custom_call" | custom-call | flops 469762048 | bytes 7340032 | tf_op jit(solution)/shard_map/pallas_call | solution.py:110
  33.9 0.1 select_reduce_fusion
  34.0 0.1 select_reduce_fusion.1
  34.2 0.2 fusion.4
  34.4 0.1 multiply_reduce_fusion
  34.5 0.3 copy-done.3
  34.8 0.2 convolution_convert_fusion
  35.0 0.5 collective-permute-start.8
  35.5 1.2 %collective-permute-start.10 = (bf16[64,128]{1,0:T(8,128)(2,1)S(1)}, bf16[64,128]{1,0:T(8,128)(2,1)S(1)}, u32[]{:S(2)}, u32[]{:S(2)}) collective-permute-start(bf16[64,128]{1,0:T(8,128)(2,1)S(1)} %get-tuple-element.26), channel_id=1, source_target_pairs={{0,3},{1,2},{2,1},{3,0},{4,7},{5,6},{6,5},{7,4},{8,11},{9,10},{10,... | collective-permute-start | bytes 49160 | tf_op jit(solution)/shard_map/ppermute | solution.py:33
  36.7 0.5 collective-permute-start.9
  37.2 0.8 %fusion.1 = f32[64,7168]{1,0:T(8,128)S(1)} fusion(bf16[1,256,7168]{2,1,0:T(8,128)(2,1)S(1)} %copy-done.1, bf16[64,256]{1,0:T(8,128)(2,1)S(1)} %get-tuple-element.5), kind=kOutput, calls=%fused_computation.2 | convolution fusion | flops 234881024 | bytes 5537792 | tf_op jit(solution)/shard_map/dot_general | solution.py:196
  38.0 0.7 %collective-permute-done.10 = bf16[64,128]{1,0:T(8,128)(2,1)S(1)} collective-permute-done((bf16[64,128]{1,0:T(8,128)(2,1)S(1)}, bf16[64,128]{1,0:T(8,128)(2,1)S(1)}, u32[]{:S(2)}, u32[]{:S(2)}) %collective-permute-start.10) | collective-permute-done | bytes 16416 | tf_op jit(solution)/shard_map/ppermute | solution.py:33
  38.7 1.8 %collective-permute-done.9 = bf16[64,128]{1,0:T(8,128)(2,1)S(1)} collective-permute-done((bf16[64,128]{1,0:T(8,128)(2,1)S(1)}, bf16[64,128]{1,0:T(8,128)(2,1)S(1)}, u32[]{:S(2)}, u32[]{:S(2)}) %collective-permute-start.9) | collective-permute-done | bytes 16416 | tf_op jit(solution)/shard_map/ppermute | solution.py:33
  40.4 0.5 fusion
  41.0 0.1 collective-permute-start.11
  41.1 1.8 %collective-permute-done.11 = bf16[32,7168]{1,0:T(8,128)(2,1)S(1)} collective-permute-done((bf16[32,7168]{1,0:T(8,128)(2,1)S(1)}, bf16[32,7168]{1,0:T(8,128)(2,1)S(1)}, u32[]{:S(2)}, u32[]{:S(2)}) %collective-permute-start.11) | collective-permute-done | bytes 458784 | tf_op jit(solution)/shard_map/ppermute | solution.py:33
  42.9 0.2 add_convert_fusion
  43.2 1.3 %collective-permute-start.12 = (bf16[16,7168]{1,0:T(8,128)(2,1)S(1)}, bf16[16,7168]{1,0:T(8,128)(2,1)S(1)}, u32[]{:S(2)}, u32[]{:S(2)}) collective-permute-start(bf16[16,7168]{1,0:T(8,128)(2,1)S(1)} %broadcast_select_fusion.5), channel_id=1, source_target_pairs={{0,4},{1,3},{2,6},{3,1},{4,0},{5,7},{6,2},{7,5},{8,12},{9,11},{10,... | collective-permute-start | bytes 688136 | tf_op jit(solution)/shard_map/ppermute | solution.py:33
  44.4 4.8 %collective-permute-done.12 = bf16[16,7168]{1,0:T(8,128)(2,1)S(1)} collective-permute-done((bf16[16,7168]{1,0:T(8,128)(2,1)S(1)}, bf16[16,7168]{1,0:T(8,128)(2,1)S(1)}, u32[]{:S(2)}, u32[]{:S(2)}) %collective-permute-start.12) | collective-permute-done | bytes 229408 | tf_op jit(solution)/shard_map/ppermute | solution.py:33
  49.2 0.1 add_convert_fusion.1
  49.4 0.6 %collective-permute-start.13 = (bf16[8,7168]{1,0:T(8,128)(2,1)S(1)}, bf16[8,7168]{1,0:T(8,128)(2,1)S(1)}, u32[]{:S(2)}, u32[]{:S(2)}) collective-permute-start(bf16[8,7168]{1,0:T(8,128)(2,1)S(1)} %broadcast_select_fusion.12), channel_id=1, source_target_pairs={{0,2},{1,5},{2,0},{3,7},{4,6},{5,1},{6,4},{7,3},{8,10},{9,13},{10,... | collective-permute-start | bytes 344072 | tf_op jit(solution)/shard_map/ppermute | solution.py:33
  50.0 4.3 %collective-permute-done.13 = bf16[8,7168]{1,0:T(8,128)(2,1)S(1)} collective-permute-done((bf16[8,7168]{1,0:T(8,128)(2,1)S(1)}, bf16[8,7168]{1,0:T(8,128)(2,1)S(1)}, u32[]{:S(2)}, u32[]{:S(2)}) %collective-permute-start.13) | collective-permute-done | bytes 114720 | tf_op jit(solution)/shard_map/ppermute | solution.py:33
  54.3 0.1 collective-permute-start.14
  54.4 5.0 %collective-permute-done.14 = bf16[4,7168]{1,0:T(4,128)(2,1)S(1)} collective-permute-done((bf16[4,7168]{1,0:T(4,128)(2,1)S(1)}, bf16[4,7168]{1,0:T(4,128)(2,1)S(1)}, u32[]{:S(2)}, u32[]{:S(2)}) %collective-permute-start.14) | collective-permute-done | bytes 57376 | tf_op jit(solution)/shard_map/ppermute | solution.py:33
  59.4 0.7 %fusion.17 = bf16[1,4,7168]{2,1,0:T(4,128)(2,1)} fusion(bf16[4,7168]{1,0:T(4,128)(2,1)S(1)} %collective-permute-done.14, bf16[8,7168]{1,0:T(8,128)(2,1)S(1)} %add_convert_fusion.2), kind=kLoop, calls=%fused_computation.54 | loop fusion | flops 114688 | bytes 172032 | tf_op jit(solution)/shard_map/broadcast_in_dim | solution.py:220
  (32 shorter events, 0.6 us)
Async XLA Ops:
  0.0 40.4 %copy-start = (bf16[1,128,7168]{2,1,0:T(8,128)(2,1)S(1)}, bf16[1,128,7168]{2,1,0:T(8,128)(2,1)}, u32[]{:S(2)}) copy-start(bf16[1,128,7168]{2,1,0:T(8,128)(2,1)} %param.19) | copy-start | bytes 5505028
  0.9 5.6 %collective-permute-start.1 = (bf16[4,128]{1,0:T(4,128)(2,1)S(1)}, bf16[4,128]{1,0:T(4,128)(2,1)S(1)}, u32[]{:S(2)}, u32[]{:S(2)}) collective-permute-start(bf16[4,128]{1,0:T(4,128)(2,1)S(1)} %fusion.36), channel_id=1, source_target_pairs={{0,8},{1,9},{2,10},{3,11},{4,12},{5,13},{6,14},{7,15},{8,0},{9,1},... | collective-permute-start | bytes 3080 | tf_op jit(solution)/shard_map/ppermute | solution.py:33
  5.0 5.5 %collective-permute-start = (bf16[4,7168]{1,0:T(4,128)(2,1)}, bf16[4,7168]{1,0:T(4,128)(2,1)S(1)}, u32[]{:S(2)}, u32[]{:S(2)}) collective-permute-start(bf16[4,7168]{1,0:T(4,128)(2,1)} %bitcast.64), channel_id=1, source_target_pairs={{0,8},{1,9},{2,10},{3,11},{4,12},{5,13},{6,14},{7,15},{8,0},{9,1},... | collective-permute-start | bytes 172040 | tf_op jit(solution)/shard_map/ppermute | solution.py:33
  10.5 5.0 %collective-permute-start.2 = (bf16[8,7296]{1,0:T(8,128)(2,1)S(1)}, bf16[8,7296]{1,0:T(8,128)(2,1)S(1)}, u32[]{:S(2)}, u32[]{:S(2)}) collective-permute-start(bf16[8,7296]{1,0:T(8,128)(2,1)S(1)} %maximum_maximum_fusion), channel_id=1, source_target_pairs={{0,2},{1,5},{2,0},{3,7},{4,6},{5,1},{6,4},{7,3},{8,10},{9,13},{10,... | collective-permute-start | bytes 350216 | tf_op jit(solution)/shard_map/ppermute | solution.py:33
  15.7 6.1 %collective-permute-start.3 = (bf16[16,7296]{1,0:T(8,128)(2,1)S(1)}, bf16[16,7296]{1,0:T(8,128)(2,1)S(1)}, u32[]{:S(2)}, u32[]{:S(2)}) collective-permute-start(bf16[16,7296]{1,0:T(8,128)(2,1)S(1)} %pad_maximum_fusion.2), channel_id=1, source_target_pairs={{0,4},{1,3},{2,6},{3,1},{4,0},{5,7},{6,2},{7,5},{8,12},{9,11},{10,... | collective-permute-start | bytes 700424 | tf_op jit(solution)/shard_map/ppermute | solution.py:33
  22.0 1.9 %collective-permute-start.4 = (bf16[32,7296]{1,0:T(8,128)(2,1)S(1)}, bf16[32,7296]{1,0:T(8,128)(2,1)S(1)}, u32[]{:S(2)}, u32[]{:S(2)}) collective-permute-start(bf16[32,7296]{1,0:T(8,128)(2,1)S(1)} %pad_maximum_fusion.1), channel_id=1, source_target_pairs={{0,1},{1,0},{2,3},{3,2},{4,5},{5,4},{6,7},{7,6},{8,9},{9,8},{10,11... | collective-permute-start | bytes 1400840 | tf_op jit(solution)/shard_map/ppermute | solution.py:33
  26.2 7.8 %collective-permute-start.7 = (bf16[64,128]{1,0:T(8,128)(2,1)S(1)}, bf16[64,128]{1,0:T(8,128)(2,1)S(1)}, u32[]{:S(2)}, u32[]{:S(2)}) collective-permute-start(bf16[64,128]{1,0:T(8,128)(2,1)S(1)} %shard_map.101), channel_id=1, source_target_pairs={{0,3},{1,2},{2,1},{3,0},{4,7},{5,6},{6,5},{7,4},{8,11},{9,10},{10,... | collective-permute-start | bytes 49160 | tf_op jit(solution)/shard_map/ppermute | solution.py:33
  27.5 6.6 %collective-permute-start.6 = (bf16[64,128]{1,0:T(8,128)(2,1)S(1)}, bf16[64,128]{1,0:T(8,128)(2,1)S(1)}, u32[]{:S(2)}, u32[]{:S(2)}) collective-permute-start(bf16[64,128]{1,0:T(8,128)(2,1)S(1)} %shard_map.101), channel_id=1, source_target_pairs={{0,2},{1,3},{2,0},{3,1},{4,6},{5,7},{6,4},{7,5},{8,10},{9,11},{10,... | collective-permute-start | bytes 49160 | tf_op jit(solution)/shard_map/ppermute | solution.py:33
  28.1 6.0 %collective-permute-start.5 = (bf16[64,128]{1,0:T(8,128)(2,1)S(1)}, bf16[64,128]{1,0:T(8,128)(2,1)S(1)}, u32[]{:S(2)}, u32[]{:S(2)}) collective-permute-start(bf16[64,128]{1,0:T(8,128)(2,1)S(1)} %shard_map.101), channel_id=1, source_target_pairs={{0,1},{1,0},{2,3},{3,2},{4,5},{5,4},{6,7},{7,6},{8,9},{9,8},{10,11... | collective-permute-start | bytes 49160 | tf_op jit(solution)/shard_map/ppermute | solution.py:33
  28.4 5.5 %copy-start.4 = (s32[16]{0:T(128)S(1)}, s32[16]{0:T(128)}, u32[]{:S(2)}) copy-start(s32[16]{0:T(128)} %param.13) | copy-start | bytes 196
  28.4 5.8 %copy-start.2 = (bf16[1,4,128,2,256]{4,3,2,1,0:T(2,128)(2,1)S(1)}, bf16[1,4,128,2,256]{4,3,2,1,0:T(2,128)(2,1)}, u32[]{:S(2)}) copy-start(bf16[1,4,128,2,256]{4,3,2,1,0:T(2,128)(2,1)} %param.17) | copy-start | bytes 1572868
  28.4 8.9 %copy-start.1 = (bf16[1,256,7168]{2,1,0:T(8,128)(2,1)S(1)}, bf16[1,256,7168]{2,1,0:T(8,128)(2,1)}, u32[]{:S(2)}) copy-start(bf16[1,256,7168]{2,1,0:T(8,128)(2,1)} %param.15) | copy-start | bytes 11010052
  33.9 1.0 %copy-start.3 = (bf16[1,4,256,128]{3,2,1,0:T(8,128)(2,1)S(1)}, bf16[1,4,256,128]{3,2,1,0:T(8,128)(2,1)}, u32[]{:S(2)}) copy-start(bf16[1,4,256,128]{3,2,1,0:T(8,128)(2,1)} %param.18) | copy-start | bytes 786436
  35.0 3.0 %collective-permute-start.8 = (bf16[64,128]{1,0:T(8,128)(2,1)S(1)}, bf16[64,128]{1,0:T(8,128)(2,1)S(1)}, u32[]{:S(2)}, u32[]{:S(2)}) collective-permute-start(bf16[64,128]{1,0:T(8,128)(2,1)S(1)} %get-tuple-element.25), channel_id=1, source_target_pairs={{0,1},{1,0},{2,3},{3,2},{4,5},{5,4},{6,7},{7,6},{8,9},{9,8},{10,11... | collective-permute-start | bytes 49160 | tf_op jit(solution)/shard_map/ppermute | solution.py:33
  35.5 3.2 %collective-permute-start.10 = (bf16[64,128]{1,0:T(8,128)(2,1)S(1)}, bf16[64,128]{1,0:T(8,128)(2,1)S(1)}, u32[]{:S(2)}, u32[]{:S(2)}) collective-permute-start(bf16[64,128]{1,0:T(8,128)(2,1)S(1)} %get-tuple-element.26), channel_id=1, source_target_pairs={{0,3},{1,2},{2,1},{3,0},{4,7},{5,6},{6,5},{7,4},{8,11},{9,10},{10,... | collective-permute-start | bytes 49160 | tf_op jit(solution)/shard_map/ppermute | solution.py:33
  36.7 3.7 %collective-permute-start.9 = (bf16[64,128]{1,0:T(8,128)(2,1)S(1)}, bf16[64,128]{1,0:T(8,128)(2,1)S(1)}, u32[]{:S(2)}, u32[]{:S(2)}) collective-permute-start(bf16[64,128]{1,0:T(8,128)(2,1)S(1)} %get-tuple-element.27), channel_id=1, source_target_pairs={{0,2},{1,3},{2,0},{3,1},{4,6},{5,7},{6,4},{7,5},{8,10},{9,11},{10,... | collective-permute-start | bytes 49160 | tf_op jit(solution)/shard_map/ppermute | solution.py:33
  41.0 1.9 %collective-permute-start.11 = (bf16[32,7168]{1,0:T(8,128)(2,1)S(1)}, bf16[32,7168]{1,0:T(8,128)(2,1)S(1)}, u32[]{:S(2)}, u32[]{:S(2)}) collective-permute-start(bf16[32,7168]{1,0:T(8,128)(2,1)S(1)} %broadcast_select_fusion.2), channel_id=1, source_target_pairs={{0,1},{1,0},{2,3},{3,2},{4,5},{5,4},{6,7},{7,6},{8,9},{9,8},{10,11... | collective-permute-start | bytes 1376264 | tf_op jit(solution)/shard_map/ppermute | solution.py:33
  43.2 6.1 %collective-permute-start.12 = (bf16[16,7168]{1,0:T(8,128)(2,1)S(1)}, bf16[16,7168]{1,0:T(8,128)(2,1)S(1)}, u32[]{:S(2)}, u32[]{:S(2)}) collective-permute-start(bf16[16,7168]{1,0:T(8,128)(2,1)S(1)} %broadcast_select_fusion.5), channel_id=1, source_target_pairs={{0,4},{1,3},{2,6},{3,1},{4,0},{5,7},{6,2},{7,5},{8,12},{9,11},{10,... | collective-permute-start | bytes 688136 | tf_op jit(solution)/shard_map/ppermute | solution.py:33
  49.4 4.9 %collective-permute-start.13 = (bf16[8,7168]{1,0:T(8,128)(2,1)S(1)}, bf16[8,7168]{1,0:T(8,128)(2,1)S(1)}, u32[]{:S(2)}, u32[]{:S(2)}) collective-permute-start(bf16[8,7168]{1,0:T(8,128)(2,1)S(1)} %broadcast_select_fusion.12), channel_id=1, source_target_pairs={{0,2},{1,5},{2,0},{3,7},{4,6},{5,1},{6,4},{7,3},{8,10},{9,13},{10,... | collective-permute-start | bytes 344072 | tf_op jit(solution)/shard_map/ppermute | solution.py:33
  54.3 5.1 %collective-permute-start.14 = (bf16[4,7168]{1,0:T(4,128)(2,1)S(1)}, bf16[4,7168]{1,0:T(4,128)(2,1)S(1)}, u32[]{:S(2)}, u32[]{:S(2)}) collective-permute-start(bf16[4,7168]{1,0:T(4,128)(2,1)S(1)} %slice.107), channel_id=1, source_target_pairs={{0,8},{1,9},{2,10},{3,11},{4,12},{5,13},{6,14},{7,15},{8,0},{9,1},... | collective-permute-start | bytes 172040 | tf_op jit(solution)/shard_map/ppermute | solution.py:33

commit v6 on v5

--- a/solution.py
+++ b/solution.py
@@ -45,79 +45,73 @@
     return jnp.where(flip, second, first), jnp.where(flip, first, second)
 
 
-def code_kernel(x, table, out, weights, sems):
-    depth = weights.shape[0]
-    step = depth // sems.shape[0]
+def split_kernel(first, base, table, split, codes_in, rows, sems):
+    depth, _, columns = rows.shape
+    step = depth // (sems.shape[0] - 1)
     copies = [
-        pltpu.make_async_copy(table.at[pl.ds(k, step)], weights.at[pl.ds(k, step)], sems.at[k // step])
+        pltpu.make_async_copy(base.at[pl.ds(first + k, step)], rows.at[pl.ds(k, step)], sems.at[k // step])
         for k in range(0, depth, step)
     ]
+    whole = pltpu.make_async_copy(table, codes_in, sems.at[sems.shape[0] - 1])
     for copy in copies:
         copy.start()
+    whole.start()
+    row = lax.broadcasted_iota(jnp.int32, (256, 256), 0)
+    column = lax.broadcasted_iota(jnp.int32, (256, 256), 1)
+    source = 2 * row - jnp.where(row < 128, 0, 255)
+    order = jnp.where(column == source, 1.0, 0.0).astype(jnp.bfloat16)
+    flat = rows.reshape(2 * depth, columns)
+    for k in range(0, depth, 128):
+        if k % step == 0:
+            copies[k // step].wait()
+        sorted_rows = jnp.dot(order, flat[2 * k : 2 * k + 256, :], preferred_element_type=jnp.float32)
+        sorted_rows = sorted_rows.astype(jnp.bfloat16)
+        split[k : k + 128, :columns] = sorted_rows[:128]
+        split[k : k + 128, columns:] = sorted_rows[128:]
+    whole.wait()
+
+
+def split_gate_up(base, table, part, parts):
+    depth, _, columns = base.shape
+    block = depth // parts
+    return pl.pallas_call(
+        lambda base, table, *rest: split_kernel(
+            part * block, base, table.at[pl.ds(part * block, block)], *rest
+        ),
+        out_shape=(
+            pltpu.VMEM((block, 2 * columns), base.dtype),
+            pltpu.VMEM((block, table.shape[1]), table.dtype),
+        ),
+        in_specs=[HBM, HBM],
+        out_specs=(VMEM, VMEM),
+        scratch_shapes=[pltpu.VMEM((block, 2, columns), base.dtype), pltpu.SemaphoreType.DMA((block // 512 + 1,))],
+        compiler_params=pltpu.CompilerParams(vmem_limit_bytes=24 << 20),
+        cost_estimate=pl.CostEstimate(flops=512 * block * columns, bytes_accessed=4 * block * columns, transcendentals=0),
+    )(in_hbm(base), in_hbm(table))
+
+
+def product_kernel(x, *refs):
+    *tables, out = refs
     total = jnp.zeros(out.shape, jnp.float32)
-    for k in range(0, depth, step):
-        copies[k // step].wait()
-        total += jnp.dot(x[:, k : k + step], weights[k : k + step, :], preferred_element_type=jnp.float32)
+    start = 0
+    for table in tables:
+        depth = table.shape[0]
+        total += jnp.dot(x[:, start : start + depth], table[...], preferred_element_type=jnp.float32)
+        start += depth
     out[...] = total.astype(out.dtype)
 
 
-def code_product(x, table):
-    depth, rank = table.shape
+def product(x, tables, dtype):
+    columns = tables[0].shape[1]
+    size = sum(table.size for table in tables)
     return pl.pallas_call(
-        code_kernel,
-        out_shape=jax.ShapeDtypeStruct((x.shape[0], rank), jnp.bfloat16),
-        in_specs=[VMEM, HBM],
+        product_kernel,
+        out_shape=jax.ShapeDtypeStruct((x.shape[0], columns), dtype),
+        in_specs=[VMEM] * (1 + len(tables)),
         out_specs=VMEM,
-        scratch_shapes=[pltpu.VMEM(table.shape, table.dtype), pltpu.SemaphoreType.DMA((4,))],
-        compiler_params=pltpu.CompilerParams(vmem_limit_bytes=32 << 20),
-        cost_estimate=pl.CostEstimate(
-            flops=2 * x.shape[0] * depth * rank, bytes_accessed=2 * table.size, transcendentals=0
-        ),
-    )(x, in_hbm(table))
-
-
-def gate_up_kernel(x, base, out, weights, sems):
-    depth, _, columns = weights.shape
-    step = depth // sems.shape[0]
-    copies = [
-        pltpu.make_async_copy(base.at[pl.ds(k, step)], weights.at[pl.ds(k, step)], sems.at[k // step])
-        for k in range(0, depth, step)
-    ]
-    for copy in copies:
-        copy.start()
-    row = lax.broadcasted_iota(jnp.int32, (128, 512), 0)
-    column = lax.broadcasted_iota(jnp.int32, (128, 512), 1)
-    target = 2 * row + jnp.where(column < 256, 0, 257)
-    spread = jnp.where(column == target, 1.0, 0.0).astype(jnp.bfloat16)
-    flat = weights.reshape(2 * depth, columns)
-    total = jnp.zeros(out.shape, jnp.float32)
-    for k in range(0, depth, step):
-        wide = [
-            jnp.dot(x[:, i : i + 128], spread, preferred_element_type=jnp.float32).astype(jnp.bfloat16)
-            for i in range(k, k + step, 128)
-        ]
-        even = jnp.concatenate([part[:, :256] for part in wide], axis=1)
-        odd = jnp.concatenate([part[:, 256:] for part in wide], axis=1)
-        copies[k // step].wait()
-        total += jnp.dot(
-            jnp.concatenate([even, odd]), flat[2 * k : 2 * (k + step), :], preferred_element_type=jnp.float32
-        )
-    out[...] = total
-
-
-def gate_up_product(x, base):
-    depth, _, columns = base.shape
-    return pl.pallas_call(
-        gate_up_kernel,
-        out_shape=jax.ShapeDtypeStruct((2 * x.shape[0], columns), jnp.float32),
-        in_specs=[VMEM, HBM],
-        out_specs=VMEM,
-        scratch_shapes=[pltpu.VMEM(base.shape, base.dtype), pltpu.SemaphoreType.DMA((depth // 512,))],
-        compiler_params=pltpu.CompilerParams(vmem_limit_bytes=32 << 20),
-        cost_estimate=pl.CostEstimate(
-            flops=4 * x.shape[0] * depth * columns, bytes_accessed=2 * base.size, transcendentals=0
-        ),
-    )(x, in_hbm(base))
+        compiler_params=pltpu.CompilerParams(vmem_limit_bytes=16 << 20),
+        cost_estimate=pl.CostEstimate(flops=2 * x.shape[0] * size, bytes_accessed=2 * size, transcendentals=0),
+    )(x, *(pltpu.with_memory_space_constraint(table, pltpu.VMEM) for table in tables))
 
 
 def local(
@@ -143,28 +137,36 @@
     along, across = halves(clusters), halves(members // 2)
     shared, paired = along[: len(along) - len(across)], along[len(along) - len(across) :]
 
-    side = jnp.concatenate([routes[0], numerators[0]], axis=1).astype(jnp.bfloat16)
-    side = jnp.pad(side, ((0, 0), (0, 128 - 2 * top)))
-    held = lax.optimization_barrier(jnp.concatenate([tokens[0], side], axis=1))
+    def pack(rows, routes, numerators):
+        side = jnp.concatenate([routes, numerators], axis=1).astype(jnp.bfloat16)
+        return jnp.concatenate([rows, jnp.pad(side, ((0, 0), (0, 128 - 2 * top)))], axis=1)
+
+    own = (tokens[0], routes[0], numerators[0])
+    held = lax.optimization_barrier(pack(*own))
 
     for i, mask in enumerate(shared):
         if i == 0:
-            pieces = [trade(piece, (mask, 0), (mask, 0)) for piece in (tokens[0], side)]
-            received = jnp.concatenate(pieces, axis=1)
+            received = pack(*(trade(piece, (mask, 0), (mask, 0)) for piece in own))
         else:
             received = trade(held, (mask, 0), (mask, 0))
         held = jnp.concatenate([held, received])
+        if i == 0:
+            parts = [split_gate_up(base_in[0], delta_in[0], 0, 2)]
+            held, parts[0], *later = lax.optimization_barrier((held, parts[0], base_in, delta_in))
     for z, x in zip(paired, across):
         size = held.shape[0]
         flag = (me // (2 * x)) % 2 == 1
         held = jnp.concatenate(ordered((core == 0) & flag, held, trade(held, (0, 2 * x), (z, 0))))
+        if len(parts) == 1:
+            parts.append(split_gate_up(later[0][0], later[1][0], 1, 2))
+            held, parts[1] = lax.optimization_barrier((held, parts[1]))
         low, high = ordered((core == 1) & flag, held, trade(held, (z, 0), (0, 2 * x)))
         inner = ordered(core == 1, low[size:], high[:size])
         held = jnp.concatenate([low[:size], *inner, high[size:]])
     held = by_rows(jnp.concatenate(ordered(core == 1, held, trade(held, (0, 1), (0, 1)))))
 
-    codes = code_product(held, delta_in[0])
-    projected = gate_up_product(held, base_in[0])
+    codes = product(held, [part[1] for part in parts], jnp.bfloat16)
+    projected = product(held, [part[0] for part in parts], jnp.float32)
 
     side = by_rows(held[:, width:])
     all_routes = side[:, :top].astype(jnp.int32)
@@ -180,8 +182,10 @@
     by_slot = jnp.stack([lax.dynamic_index_in_dim(codes, s ^ me, 0, keepdims=False) for s in range(members)])
 
     lifted = jnp.einsum("srk,skgf->srgf", by_slot, delta_mid[0], preferred_element_type=jnp.float32)
-    total = held.shape[0]
-    hidden = jax.nn.silu(projected[None, :total] + lifted[:, :, 0]) * (projected[None, total:] + lifted[:, :, 1])
+    part = projected.shape[1] // 2
+    hidden = jax.nn.silu(projected[None, :, :part] + lifted[:, :, 0]) * (
+        projected[None, :, part:] + lifted[:, :, 1]
+    )
     hidden_sum = jnp.sum(scale[:, :, None] * hidden, axis=0).astype(jnp.bfloat16)
     partial_codes = jnp.einsum(
         "srf,sfk->srk", hidden.astype(jnp.bfloat16), delta_down[0], preferred_element_type=jnp.float32
@@ -199,7 +203,8 @@
     def add(kept, received):
         return (kept.astype(jnp.float32) + received.astype(jnp.float32)).astype(jnp.bfloat16)
 
-    kept, sent = ordered(core == 1, term[: total // 2], term[total // 2 :])
+    size = term.shape[0] // 2
+    kept, sent = ordered(core == 1, term[:size], term[size:])
     total = add(kept, trade(sent, (0, 1), (0, 1)))
     for z, x in reversed(list(zip(paired, across))):
         flag = (me // (2 * x)) % 2 == 1

time: 60.3 us -> 67.6 us (1.12)
  local copies, waits for them, and re-layouts: 0.52 us -> 11.4 us
  waiting for transfers between devices: 33 us -> 22.3 us
  starting transfers between devices: 13.2 us -> 17.7 us
  Pallas kernels: 7.39 us -> 9.25 us
    unnamed x10 -> x26, local copies, waits for them, and re-layouts: 0.32 us -> 11.2 us
    ppermute x15 -> x16, waiting for transfers between devices: 33 us -> 22.3 us  [trade(): return lax.ppermute(value, ('expert', 'tensor'), pairs)]
    ppermute x15 -> x16, starting transfers between devices: 13.2 us -> 17.7 us  [trade(): return lax.ppermute(value, ('expert', 'tensor'), pairs)]
    pallas_call x2 -> x4, Pallas kernels: 7.39 us -> 9.25 us  [the longest x2 7.43 us: split_gate_up(): pl.pallas_call(lambda base, table, *rest: split_kernel(part * block, base...]
    another operation x0 -> x4, other arithmetic: none -> 1.38 us
    squeeze x1 -> x0, other arithmetic: 0.84 us -> none  [local(): numerators[0]]
  transfers between devices with their start and end apart: 15 -> 16, of which waited for: 11 -> 8; matrix products, arithmetic and copies ran while one was open for 3% -> 5% of each run, Pallas kernels for 9% -> 13%
where the time goes in v6:
time: 67.6 us; the launch traced here: 67.2 us
  waiting for transfers between devices  22.3 us (33%)
  starting transfers between devices  17.7 us (26%)
  local copies, waits for them, and re-layouts  11.4 us (17%)
  Pallas kernels  9.25 us (14%)
  other arithmetic  4.54 us (7%)
  matrix products  1.65 us (2%)
    ppermute x16, waiting for transfers between devices, trade(): return lax.ppermute(value, ('expert', 'tensor'), pairs)  22.3 us
    ppermute x16, starting transfers between devices, trade(): return lax.ppermute(value, ('expert', 'tensor'), pairs)  17.7 us
    unnamed x26, local copies, waits for them, and re-layouts  11.2 us
    pallas_call x2, Pallas kernels, split_gate_up(): pl.pallas_call(lambda base, table, *rest: split_kernel(part * block, base...  7.43 us
    pallas_call x2, Pallas kernels, product(): pl.pallas_call(product_kernel, out_shape=jax.ShapeDtypeStruct((x.shape[0]...  1.82 us
    another operation x4, other arithmetic  1.38 us
  transfers between devices with their start and end apart: 16, of which 8 were waited for; matrix products, arithmetic and copies ran while one was open for 5% of the time, Pallas kernels for 13%

profile of v6, /device:TPU:0, one launch (start us, length us, event | category | flops | bytes accessed | tf_op | source)
XLA Modules:
  0.0 67.2 jit_solution(11523219020008064388)
XLA Ops:
  0.0 4.0 %collective-permute-start.2 = (s32[4,8]{1,0:T(4,128)}, s32[4,8]{1,0:T(4,128)S(1)}, u32[]{:S(2)}, u32[]{:S(2)}) collective-permute-start(s32[4,8]{1,0:T(4,128)} %bitcast.73), channel_id=1, source_target_pairs={{0,8},{1,9},{2,10},{3,11},{4,12},{5,13},{6,14},{7,15},{8,0},{9,1},... | collective-permute-start | bytes 392 | tf_op jit(solution)/shard_map/ppermute | solution.py:33
  4.1 2.9 %collective-permute-start = (bf16[4,7168]{1,0:T(4,128)(2,1)}, bf16[4,7168]{1,0:T(4,128)(2,1)S(1)}, u32[]{:S(2)}, u32[]{:S(2)}) collective-permute-start(bf16[4,7168]{1,0:T(4,128)(2,1)} %bitcast.68), channel_id=1, source_target_pairs={{0,8},{1,9},{2,10},{3,11},{4,12},{5,13},{6,14},{7,15},{8,0},{9,1},... | collective-permute-start | bytes 172040 | tf_op jit(solution)/shard_map/ppermute | solution.py:33
  7.0 0.7 %bitcast_convert_fusion = bf16[4,8]{1,0:T(4,128)(2,1)S(1)} fusion(s32[1,4,8]{2,1,0:T(4,128)} %param.12), kind=kLoop, calls=%fused_computation.92 | loop fusion | flops 32 | bytes 192 | tf_op jit(solution)/shard_map/convert.4
  7.7 0.7 %bitcast_convert_fusion.1 = bf16[4,8]{1,0:T(4,128)(2,1)S(1)} fusion(s32[1,4,8]{2,1,0:T(4,128)} %param.11), kind=kLoop, calls=%fused_computation.93 | loop fusion | flops 32 | bytes 192 | tf_op jit(solution)/shard_map/convert.3
  8.4 0.8 %pad_maximum_fusion.6 = bf16[4,7296]{1,0:T(4,128)(2,1)S(1)} fusion(bf16[4,128]{1,0:T(4,128)(2,1)S(1)} %fusion.38, bf16[4,7168]{1,0:T(4,128)(2,1)} %bitcast.69), kind=kLoop, calls=%fused_computation.53 | loop fusion | flops 116736 | bytes 116736 | tf_op jit(solution)/shard_map/concatenate | solution.py:142
  9.3 3.7 %shard_map.100 = (bf16[3584,512]{1,0:T(8,128)(2,1)S(1)}, bf16[3584,128]{1,0:T(8,128)(2,1)S(1)}) custom-call(bf16[7168,2,256]{2,1,0:T(2,128)(2,1)} %bitcast.63, bf16[7168,128]{1,0:T(8,128)(2,1)} %bitcast.65), custom_call_target="tpu_custom_call" | custom-call | flops 469762048 | bytes 3670016 | tf_op jit(solution)/shard_map/pallas_call | solution.py:77
  13.0 1.8 %copy-done.1 = bf16[3584,512]{1,0:T(8,128)(2,1)} copy-done((bf16[3584,512]{1,0:T(8,128)(2,1)}, bf16[3584,512]{1,0:T(8,128)(2,1)S(1)}, u32[]{:S(2)}) %copy-start.1) | copy-done | bytes 3670040
  14.8 1.0 %copy-done.5 = bf16[3584,128]{1,0:T(8,128)(2,1)} copy-done((bf16[3584,128]{1,0:T(8,128)(2,1)}, bf16[3584,128]{1,0:T(8,128)(2,1)S(1)}, u32[]{:S(2)}) %copy-start.5) | copy-done | bytes 917528
  16.0 1.6 %collective-permute-start.3 = (bf16[8,7296]{1,0:T(8,128)(2,1)S(1)}, bf16[8,7296]{1,0:T(8,128)(2,1)S(1)}, u32[]{:S(2)}, u32[]{:S(2)}) collective-permute-start(bf16[8,7296]{1,0:T(8,128)(2,1)S(1)} %maximum_maximum_fusion), channel_id=1, source_target_pairs={{0,2},{1,5},{2,0},{3,7},{4,6},{5,1},{6,4},{7,3},{8,10},{9,13},{10,... | collective-permute-start | bytes 350216 | tf_op jit(solution)/shard_map/ppermute | solution.py:33
  17.5 3.7 %shard_map.101 = (bf16[3584,512]{1,0:T(8,128)(2,1)S(1)}, bf16[3584,128]{1,0:T(8,128)(2,1)S(1)}) custom-call(bf16[7168,2,256]{2,1,0:T(2,128)(2,1)} %bitcast.64, bf16[7168,128]{1,0:T(8,128)(2,1)} %bitcast.66), custom_call_target="tpu_custom_call" | custom-call | flops 469762048 | bytes 3670016 | tf_op jit(solution)/shard_map/pallas_call | solution.py:77
  21.2 1.8 %copy-done.3 = bf16[3584,512]{1,0:T(8,128)(2,1)} copy-done((bf16[3584,512]{1,0:T(8,128)(2,1)}, bf16[3584,512]{1,0:T(8,128)(2,1)S(1)}, u32[]{:S(2)}) %copy-start.3) | copy-done | bytes 3670040
  23.1 1.0 %copy-done.7 = bf16[3584,128]{1,0:T(8,128)(2,1)} copy-done((bf16[3584,128]{1,0:T(8,128)(2,1)}, bf16[3584,128]{1,0:T(8,128)(2,1)S(1)}, u32[]{:S(2)}) %copy-start.7) | copy-done | bytes 917528
  24.2 1.6 %collective-permute-start.4 = (bf16[16,7296]{1,0:T(8,128)(2,1)S(1)}, bf16[16,7296]{1,0:T(8,128)(2,1)S(1)}, u32[]{:S(2)}, u32[]{:S(2)}) collective-permute-start(bf16[16,7296]{1,0:T(8,128)(2,1)S(1)} %pad_maximum_fusion.2), channel_id=1, source_target_pairs={{0,4},{1,3},{2,6},{3,1},{4,0},{5,7},{6,2},{7,5},{8,12},{9,11},{10,... | collective-permute-start | bytes 700424 | tf_op jit(solution)/shard_map/ppermute | solution.py:33
  25.8 4.5 %collective-permute-done.4 = bf16[16,7296]{1,0:T(8,128)(2,1)S(1)} collective-permute-done((bf16[16,7296]{1,0:T(8,128)(2,1)S(1)}, bf16[16,7296]{1,0:T(8,128)(2,1)S(1)}, u32[]{:S(2)}, u32[]{:S(2)}) %collective-permute-start.4) | collective-permute-done | bytes 233504 | tf_op jit(solution)/shard_map/ppermute | solution.py:33
  30.5 1.8 %collective-permute-done.5 = bf16[32,7296]{1,0:T(8,128)(2,1)S(1)} collective-permute-done((bf16[32,7296]{1,0:T(8,128)(2,1)S(1)}, bf16[32,7296]{1,0:T(8,128)(2,1)S(1)}, u32[]{:S(2)}, u32[]{:S(2)}) %collective-permute-start.5) | collective-permute-done | bytes 466976 | tf_op jit(solution)/shard_map/ppermute | solution.py:33
  32.3 0.2 broadcast_select_fusion.1
  32.5 0.2 convert_reduce_fusion
  32.8 0.9 %copy-done.6 = bf16[3584,128]{1,0:T(8,128)(2,1)S(1)} copy-done((bf16[3584,128]{1,0:T(8,128)(2,1)S(1)}, bf16[3584,128]{1,0:T(8,128)(2,1)}, u32[]{:S(2)}) %copy-start.6) | copy-done | bytes 917528
  33.7 0.3 copy-done.8
  33.9 0.5 shard_map.103
  34.4 0.3 collective-permute-start.8
  34.8 1.5 %collective-permute-start.7 = (bf16[64,128]{1,0:T(8,128)(2,1)S(1)}, bf16[64,128]{1,0:T(8,128)(2,1)S(1)}, u32[]{:S(2)}, u32[]{:S(2)}) collective-permute-start(bf16[64,128]{1,0:T(8,128)(2,1)S(1)} %shard_map.103), channel_id=1, source_target_pairs={{0,2},{1,3},{2,0},{3,1},{4,6},{5,7},{6,4},{7,5},{8,10},{9,11},{10,... | collective-permute-start | bytes 49160 | tf_op jit(solution)/shard_map/ppermute | solution.py:33
  36.3 0.1 fusion.27
  36.5 2.1 %copy-done.2 = bf16[3584,512]{1,0:T(8,128)(2,1)S(1)} copy-done((bf16[3584,512]{1,0:T(8,128)(2,1)S(1)}, bf16[3584,512]{1,0:T(8,128)(2,1)}, u32[]{:S(2)}) %copy-start.2) | copy-done | bytes 3670040
  38.6 2.0 %copy-done.4 = bf16[3584,512]{1,0:T(8,128)(2,1)S(1)} copy-done((bf16[3584,512]{1,0:T(8,128)(2,1)S(1)}, bf16[3584,512]{1,0:T(8,128)(2,1)}, u32[]{:S(2)}) %copy-start.4) | copy-done | bytes 3670040
  40.6 1.4 %shard_map.102 = f32[64,512]{1,0:T(8,128)S(1)} custom-call(bf16[64,7296]{1,0:T(8,128)(2,1)S(1)} %pad_maximum_fusion.x, bf16[3584,512]{1,0:T(8,128)(2,1)S(1)} %copy-done.2, bf16[3584,512]{1,0:T(8,128)(2,1)S(1)} %copy-done.4), custom_call_target="tpu_custom_call" | custom-call | flops 469762048 | bytes 7340032 | tf_op jit(solution)/shard_map/pallas_call | solution.py:107
  42.1 0.1 select_reduce_fusion
  42.1 0.1 select_reduce_fusion.1
  42.3 0.2 fusion.4
  42.5 0.1 multiply_reduce_fusion
  42.7 0.3 copy-done.11
  43.0 0.2 convolution_convert_fusion
  43.2 0.6 collective-permute-start.11
  43.8 1.5 %collective-permute-start.10 = (bf16[64,128]{1,0:T(8,128)(2,1)S(1)}, bf16[64,128]{1,0:T(8,128)(2,1)S(1)}, u32[]{:S(2)}, u32[]{:S(2)}) collective-permute-start(bf16[64,128]{1,0:T(8,128)(2,1)S(1)} %get-tuple-element.51), channel_id=1, source_target_pairs={{0,2},{1,3},{2,0},{3,1},{4,6},{5,7},{6,4},{7,5},{8,10},{9,11},{10,... | collective-permute-start | bytes 49160 | tf_op jit(solution)/shard_map/ppermute | solution.py:33
  45.3 0.8 %fusion.1 = f32[64,7168]{1,0:T(8,128)S(1)} fusion(bf16[1,256,7168]{2,1,0:T(8,128)(2,1)S(1)} %copy-done.9, bf16[64,256]{1,0:T(8,128)(2,1)S(1)} %get-tuple-element.29), kind=kOutput, calls=%fused_computation.2 | convolution fusion | flops 234881024 | bytes 5537792 | tf_op jit(solution)/shard_map/dot_general | solution.py:200
  46.1 0.3 collective-permute-done.11
  46.4 1.2 %collective-permute-done.10 = bf16[64,128]{1,0:T(8,128)(2,1)S(1)} collective-permute-done((bf16[64,128]{1,0:T(8,128)(2,1)S(1)}, bf16[64,128]{1,0:T(8,128)(2,1)S(1)}, u32[]{:S(2)}, u32[]{:S(2)}) %collective-permute-start.10) | collective-permute-done | bytes 16416 | tf_op jit(solution)/shard_map/ppermute | solution.py:33
  47.6 0.5 fusion
  48.2 1.8 %collective-permute-done.12 = bf16[32,7168]{1,0:T(8,128)(2,1)S(1)} collective-permute-done((bf16[32,7168]{1,0:T(8,128)(2,1)S(1)}, bf16[32,7168]{1,0:T(8,128)(2,1)S(1)}, u32[]{:S(2)}, u32[]{:S(2)}) %collective-permute-start.12) | collective-permute-done | bytes 458784 | tf_op jit(solution)/shard_map/ppermute | solution.py:33
  50.0 0.2 add_convert_fusion
  50.3 1.6 %collective-permute-start.13 = (bf16[16,7168]{1,0:T(8,128)(2,1)S(1)}, bf16[16,7168]{1,0:T(8,128)(2,1)S(1)}, u32[]{:S(2)}, u32[]{:S(2)}) collective-permute-start(bf16[16,7168]{1,0:T(8,128)(2,1)S(1)} %broadcast_select_fusion.5), channel_id=1, source_target_pairs={{0,4},{1,3},{2,6},{3,1},{4,0},{5,7},{6,2},{7,5},{8,12},{9,11},{10,... | collective-permute-start | bytes 688136 | tf_op jit(solution)/shard_map/ppermute | solution.py:33
  51.9 4.5 %collective-permute-done.13 = bf16[16,7168]{1,0:T(8,128)(2,1)S(1)} collective-permute-done((bf16[16,7168]{1,0:T(8,128)(2,1)S(1)}, bf16[16,7168]{1,0:T(8,128)(2,1)S(1)}, u32[]{:S(2)}, u32[]{:S(2)}) %collective-permute-start.13) | collective-permute-done | bytes 229408 | tf_op jit(solution)/shard_map/ppermute | solution.py:33
  56.4 0.1 add_convert_fusion.1
  56.5 1.6 %collective-permute-start.14 = (bf16[8,7168]{1,0:T(8,128)(2,1)S(1)}, bf16[8,7168]{1,0:T(8,128)(2,1)S(1)}, u32[]{:S(2)}, u32[]{:S(2)}) collective-permute-start(bf16[8,7168]{1,0:T(8,128)(2,1)S(1)} %broadcast_select_fusion.12), channel_id=1, source_target_pairs={{0,2},{1,5},{2,0},{3,7},{4,6},{5,1},{6,4},{7,3},{8,10},{9,13},{10,... | collective-permute-start | bytes 344072 | tf_op jit(solution)/shard_map/ppermute | solution.py:33
  58.1 3.3 %collective-permute-done.14 = bf16[8,7168]{1,0:T(8,128)(2,1)S(1)} collective-permute-done((bf16[8,7168]{1,0:T(8,128)(2,1)S(1)}, bf16[8,7168]{1,0:T(8,128)(2,1)S(1)}, u32[]{:S(2)}, u32[]{:S(2)}) %collective-permute-start.14) | collective-permute-done | bytes 114720 | tf_op jit(solution)/shard_map/ppermute | solution.py:33
  61.4 0.2 collective-permute-start.15
  61.6 5.0 %collective-permute-done.15 = bf16[4,7168]{1,0:T(4,128)(2,1)S(1)} collective-permute-done((bf16[4,7168]{1,0:T(4,128)(2,1)S(1)}, bf16[4,7168]{1,0:T(4,128)(2,1)S(1)}, u32[]{:S(2)}, u32[]{:S(2)}) %collective-permute-start.15) | collective-permute-done | bytes 57376 | tf_op jit(solution)/shard_map/ppermute | solution.py:33
  66.6 0.7 fusion.17
  (56 shorter events, 1.3 us)
Async XLA Ops:
  0.0 47.6 %copy-start = (bf16[1,128,7168]{2,1,0:T(8,128)(2,1)S(1)}, bf16[1,128,7168]{2,1,0:T(8,128)(2,1)}, u32[]{:S(2)}) copy-start(bf16[1,128,7168]{2,1,0:T(8,128)(2,1)} %param.19) | copy-start | bytes 5505028
  0.0 15.8 %collective-permute-start.2 = (s32[4,8]{1,0:T(4,128)}, s32[4,8]{1,0:T(4,128)S(1)}, u32[]{:S(2)}, u32[]{:S(2)}) collective-permute-start(s32[4,8]{1,0:T(4,128)} %bitcast.73), channel_id=1, source_target_pairs={{0,8},{1,9},{2,10},{3,11},{4,12},{5,13},{6,14},{7,15},{8,0},{9,1},... | collective-permute-start | bytes 392 | tf_op jit(solution)/shard_map/ppermute | solution.py:33
  4.0 11.8 %collective-permute-start.1 = (s32[4,8]{1,0:T(4,128)}, s32[4,8]{1,0:T(4,128)S(1)}, u32[]{:S(2)}, u32[]{:S(2)}) collective-permute-start(s32[4,8]{1,0:T(4,128)} %bitcast.74), channel_id=1, source_target_pairs={{0,8},{1,9},{2,10},{3,11},{4,12},{5,13},{6,14},{7,15},{8,0},{9,1},... | collective-permute-start | bytes 392 | tf_op jit(solution)/shard_map/ppermute | solution.py:33
  4.1 11.8 %collective-permute-start = (bf16[4,7168]{1,0:T(4,128)(2,1)}, bf16[4,7168]{1,0:T(4,128)(2,1)S(1)}, u32[]{:S(2)}, u32[]{:S(2)}) collective-permute-start(bf16[4,7168]{1,0:T(4,128)(2,1)} %bitcast.68), channel_id=1, source_target_pairs={{0,8},{1,9},{2,10},{3,11},{4,12},{5,13},{6,14},{7,15},{8,0},{9,1},... | collective-permute-start | bytes 172040 | tf_op jit(solution)/shard_map/ppermute | solution.py:33
  13.0 1.8 %copy-start.1 = (bf16[3584,512]{1,0:T(8,128)(2,1)}, bf16[3584,512]{1,0:T(8,128)(2,1)S(1)}, u32[]{:S(2)}) copy-start(bf16[3584,512]{1,0:T(8,128)(2,1)S(1)} %get-tuple-element.25.refs_0_) | copy-start | bytes 11010052
  14.8 1.0 %copy-start.5 = (bf16[3584,128]{1,0:T(8,128)(2,1)}, bf16[3584,128]{1,0:T(8,128)(2,1)S(1)}, u32[]{:S(2)}) copy-start(bf16[3584,128]{1,0:T(8,128)(2,1)S(1)} %get-tuple-element.27.refs_0_) | copy-start | bytes 2752516
  16.0 8.1 %collective-permute-start.3 = (bf16[8,7296]{1,0:T(8,128)(2,1)S(1)}, bf16[8,7296]{1,0:T(8,128)(2,1)S(1)}, u32[]{:S(2)}, u32[]{:S(2)}) collective-permute-start(bf16[8,7296]{1,0:T(8,128)(2,1)S(1)} %maximum_maximum_fusion), channel_id=1, source_target_pairs={{0,2},{1,5},{2,0},{3,7},{4,6},{5,1},{6,4},{7,3},{8,10},{9,13},{10,... | collective-permute-start | bytes 350216 | tf_op jit(solution)/shard_map/ppermute | solution.py:33
  21.2 1.8 %copy-start.3 = (bf16[3584,512]{1,0:T(8,128)(2,1)}, bf16[3584,512]{1,0:T(8,128)(2,1)S(1)}, u32[]{:S(2)}) copy-start(bf16[3584,512]{1,0:T(8,128)(2,1)S(1)} %get-tuple-element.26.refs_1_) | copy-start | bytes 11010052
  23.1 1.0 %copy-start.7 = (bf16[3584,128]{1,0:T(8,128)(2,1)}, bf16[3584,128]{1,0:T(8,128)(2,1)S(1)}, u32[]{:S(2)}) copy-start(bf16[3584,128]{1,0:T(8,128)(2,1)S(1)} %get-tuple-element.28.refs_1_) | copy-start | bytes 2752516
  24.2 6.1 %collective-permute-start.4 = (bf16[16,7296]{1,0:T(8,128)(2,1)S(1)}, bf16[16,7296]{1,0:T(8,128)(2,1)S(1)}, u32[]{:S(2)}, u32[]{:S(2)}) collective-permute-start(bf16[16,7296]{1,0:T(8,128)(2,1)S(1)} %pad_maximum_fusion.2), channel_id=1, source_target_pairs={{0,4},{1,3},{2,6},{3,1},{4,0},{5,7},{6,2},{7,5},{8,12},{9,11},{10,... | collective-permute-start | bytes 700424 | tf_op jit(solution)/shard_map/ppermute | solution.py:33
  30.4 1.9 %collective-permute-start.5 = (bf16[32,7296]{1,0:T(8,128)(2,1)S(1)}, bf16[32,7296]{1,0:T(8,128)(2,1)S(1)}, u32[]{:S(2)}, u32[]{:S(2)}) collective-permute-start(bf16[32,7296]{1,0:T(8,128)(2,1)S(1)} %pad_maximum_fusion.1), channel_id=1, source_target_pairs={{0,1},{1,0},{2,3},{3,2},{4,5},{5,4},{6,7},{7,6},{8,9},{9,8},{10,11... | collective-permute-start | bytes 1400840 | tf_op jit(solution)/shard_map/ppermute | solution.py:33
  32.5 1.2 %copy-start.6 = (bf16[3584,128]{1,0:T(8,128)(2,1)S(1)}, bf16[3584,128]{1,0:T(8,128)(2,1)}, u32[]{:S(2)}) copy-start(bf16[3584,128]{1,0:T(8,128)(2,1)} %copy-done.5) | copy-start | bytes 2752516
  32.5 1.4 %copy-start.8 = (bf16[3584,128]{1,0:T(8,128)(2,1)S(1)}, bf16[3584,128]{1,0:T(8,128)(2,1)}, u32[]{:S(2)}) copy-start(bf16[3584,128]{1,0:T(8,128)(2,1)} %copy-done.7) | copy-start | bytes 2752516
  34.4 7.8 %collective-permute-start.8 = (bf16[64,128]{1,0:T(8,128)(2,1)S(1)}, bf16[64,128]{1,0:T(8,128)(2,1)S(1)}, u32[]{:S(2)}, u32[]{:S(2)}) collective-permute-start(bf16[64,128]{1,0:T(8,128)(2,1)S(1)} %shard_map.103), channel_id=1, source_target_pairs={{0,3},{1,2},{2,1},{3,0},{4,7},{5,6},{6,5},{7,4},{8,11},{9,10},{10,... | collective-permute-start | bytes 49160 | tf_op jit(solution)/shard_map/ppermute | solution.py:33
  34.8 7.5 %collective-permute-start.7 = (bf16[64,128]{1,0:T(8,128)(2,1)S(1)}, bf16[64,128]{1,0:T(8,128)(2,1)S(1)}, u32[]{:S(2)}, u32[]{:S(2)}) collective-permute-start(bf16[64,128]{1,0:T(8,128)(2,1)S(1)} %shard_map.103), channel_id=1, source_target_pairs={{0,2},{1,3},{2,0},{3,1},{4,6},{5,7},{6,4},{7,5},{8,10},{9,11},{10,... | collective-permute-start | bytes 49160 | tf_op jit(solution)/shard_map/ppermute | solution.py:33
  36.3 6.0 %collective-permute-start.6 = (bf16[64,128]{1,0:T(8,128)(2,1)S(1)}, bf16[64,128]{1,0:T(8,128)(2,1)S(1)}, u32[]{:S(2)}, u32[]{:S(2)}) collective-permute-start(bf16[64,128]{1,0:T(8,128)(2,1)S(1)} %shard_map.103), channel_id=1, source_target_pairs={{0,1},{1,0},{2,3},{3,2},{4,5},{5,4},{6,7},{7,6},{8,9},{9,8},{10,11... | collective-permute-start | bytes 49160 | tf_op jit(solution)/shard_map/ppermute | solution.py:33
  36.5 2.1 %copy-start.2 = (bf16[3584,512]{1,0:T(8,128)(2,1)S(1)}, bf16[3584,512]{1,0:T(8,128)(2,1)}, u32[]{:S(2)}) copy-start(bf16[3584,512]{1,0:T(8,128)(2,1)} %copy-done.1) | copy-start | bytes 11010052
  38.6 2.0 %copy-start.4 = (bf16[3584,512]{1,0:T(8,128)(2,1)S(1)}, bf16[3584,512]{1,0:T(8,128)(2,1)}, u32[]{:S(2)}) copy-start(bf16[3584,512]{1,0:T(8,128)(2,1)} %copy-done.3) | copy-start | bytes 11010052
  40.6 1.4 %copy-start.12 = (s32[16]{0:T(128)S(1)}, s32[16]{0:T(128)}, u32[]{:S(2)}) copy-start(s32[16]{0:T(128)} %param.13) | copy-start | bytes 196
  40.6 1.7 %copy-start.10 = (bf16[1,4,128,2,256]{4,3,2,1,0:T(2,128)(2,1)S(1)}, bf16[1,4,128,2,256]{4,3,2,1,0:T(2,128)(2,1)}, u32[]{:S(2)}) copy-start(bf16[1,4,128,2,256]{4,3,2,1,0:T(2,128)(2,1)} %param.17) | copy-start | bytes 1572868
  40.6 4.7 %copy-start.9 = (bf16[1,256,7168]{2,1,0:T(8,128)(2,1)S(1)}, bf16[1,256,7168]{2,1,0:T(8,128)(2,1)}, u32[]{:S(2)}) copy-start(bf16[1,256,7168]{2,1,0:T(8,128)(2,1)} %param.15) | copy-start | bytes 11010052
  42.0 1.0 %copy-start.11 = (bf16[1,4,256,128]{3,2,1,0:T(8,128)(2,1)S(1)}, bf16[1,4,256,128]{3,2,1,0:T(8,128)(2,1)}, u32[]{:S(2)}) copy-start(bf16[1,4,256,128]{3,2,1,0:T(8,128)(2,1)} %param.18) | copy-start | bytes 786436
  43.2 3.2 %collective-permute-start.11 = (bf16[64,128]{1,0:T(8,128)(2,1)S(1)}, bf16[64,128]{1,0:T(8,128)(2,1)S(1)}, u32[]{:S(2)}, u32[]{:S(2)}) collective-permute-start(bf16[64,128]{1,0:T(8,128)(2,1)S(1)} %get-tuple-element.50), channel_id=1, source_target_pairs={{0,3},{1,2},{2,1},{3,0},{4,7},{5,6},{6,5},{7,4},{8,11},{9,10},{10,... | collective-permute-start | bytes 49160 | tf_op jit(solution)/shard_map/ppermute | solution.py:33
  43.8 3.7 %collective-permute-start.10 = (bf16[64,128]{1,0:T(8,128)(2,1)S(1)}, bf16[64,128]{1,0:T(8,128)(2,1)S(1)}, u32[]{:S(2)}, u32[]{:S(2)}) collective-permute-start(bf16[64,128]{1,0:T(8,128)(2,1)S(1)} %get-tuple-element.51), channel_id=1, source_target_pairs={{0,2},{1,3},{2,0},{3,1},{4,6},{5,7},{6,4},{7,5},{8,10},{9,11},{10,... | collective-permute-start | bytes 49160 | tf_op jit(solution)/shard_map/ppermute | solution.py:33
  45.3 2.3 %collective-permute-start.9 = (bf16[64,128]{1,0:T(8,128)(2,1)S(1)}, bf16[64,128]{1,0:T(8,128)(2,1)S(1)}, u32[]{:S(2)}, u32[]{:S(2)}) collective-permute-start(bf16[64,128]{1,0:T(8,128)(2,1)S(1)} %get-tuple-element.49), channel_id=1, source_target_pairs={{0,1},{1,0},{2,3},{3,2},{4,5},{5,4},{6,7},{7,6},{8,9},{9,8},{10,11... | collective-permute-start | bytes 49160 | tf_op jit(solution)/shard_map/ppermute | solution.py:33
  48.1 1.9 %collective-permute-start.12 = (bf16[32,7168]{1,0:T(8,128)(2,1)S(1)}, bf16[32,7168]{1,0:T(8,128)(2,1)S(1)}, u32[]{:S(2)}, u32[]{:S(2)}) collective-permute-start(bf16[32,7168]{1,0:T(8,128)(2,1)S(1)} %broadcast_select_fusion.2), channel_id=1, source_target_pairs={{0,1},{1,0},{2,3},{3,2},{4,5},{5,4},{6,7},{7,6},{8,9},{9,8},{10,11... | collective-permute-start | bytes 1376264 | tf_op jit(solution)/shard_map/ppermute | solution.py:33
  50.3 6.1 %collective-permute-start.13 = (bf16[16,7168]{1,0:T(8,128)(2,1)S(1)}, bf16[16,7168]{1,0:T(8,128)(2,1)S(1)}, u32[]{:S(2)}, u32[]{:S(2)}) collective-permute-start(bf16[16,7168]{1,0:T(8,128)(2,1)S(1)} %broadcast_select_fusion.5), channel_id=1, source_target_pairs={{0,4},{1,3},{2,6},{3,1},{4,0},{5,7},{6,2},{7,5},{8,12},{9,11},{10,... | collective-permute-start | bytes 688136 | tf_op jit(solution)/shard_map/ppermute | solution.py:33
  56.5 4.9 %collective-permute-start.14 = (bf16[8,7168]{1,0:T(8,128)(2,1)S(1)}, bf16[8,7168]{1,0:T(8,128)(2,1)S(1)}, u32[]{:S(2)}, u32[]{:S(2)}) collective-permute-start(bf16[8,7168]{1,0:T(8,128)(2,1)S(1)} %broadcast_select_fusion.12), channel_id=1, source_target_pairs={{0,2},{1,5},{2,0},{3,7},{4,6},{5,1},{6,4},{7,3},{8,10},{9,13},{10,... | collective-permute-start | bytes 344072 | tf_op jit(solution)/shard_map/ppermute | solution.py:33
  61.4 5.1 %collective-permute-start.15 = (bf16[4,7168]{1,0:T(4,128)(2,1)S(1)}, bf16[4,7168]{1,0:T(4,128)(2,1)S(1)}, u32[]{:S(2)}, u32[]{:S(2)}) collective-permute-start(bf16[4,7168]{1,0:T(4,128)(2,1)S(1)} %slice.107), channel_id=1, source_target_pairs={{0,8},{1,9},{2,10},{3,11},{4,12},{5,13},{6,14},{7,15},{8,0},{9,1},... | collective-permute-start | bytes 172040 | tf_op jit(solution)/shard_map/ppermute | solution.py:33

commit v7 on v5

--- a/solution.py
+++ b/solution.py
@@ -52,8 +52,8 @@
         pltpu.make_async_copy(table.at[pl.ds(k, step)], weights.at[pl.ds(k, step)], sems.at[k // step])
         for k in range(0, depth, step)
     ]
-    for copy in copies:
-        copy.start()
+    for i, copy in enumerate(copies):
+        copy.start(priority=i % 2)
     total = jnp.zeros(out.shape, jnp.float32)
     for k in range(0, depth, step):
         copies[k // step].wait()
@@ -83,8 +83,8 @@
         pltpu.make_async_copy(base.at[pl.ds(k, step)], weights.at[pl.ds(k, step)], sems.at[k // step])
         for k in range(0, depth, step)
     ]
-    for copy in copies:
-        copy.start()
+    for i, copy in enumerate(copies):
+        copy.start(priority=i % 2)
     row = lax.broadcasted_iota(jnp.int32, (128, 512), 0)
     column = lax.broadcasted_iota(jnp.int32, (128, 512), 1)
     target = 2 * row + jnp.where(column < 256, 0, 257)
@@ -186,10 +186,8 @@
     partial_codes = jnp.einsum(
         "srf,sfk->srk", hidden.astype(jnp.bfloat16), delta_down[0], preferred_element_type=jnp.float32
     ).astype(jnp.bfloat16)
-    lowrank = lax.dynamic_index_in_dim(partial_codes, me, 0, keepdims=False).astype(jnp.float32)
-    for m in range(1, members):
-        sent = lax.dynamic_index_in_dim(partial_codes, me ^ m, 0, keepdims=False)
-        lowrank = lowrank + trade(sent, (0, m), (0, m)).astype(jnp.float32)
+    lowrank = lax.all_to_all(partial_codes, "tensor", split_axis=0, concat_axis=0, tiled=True)
+    lowrank = jnp.sum(lowrank.astype(jnp.float32), axis=0)
     own_scale = lax.dynamic_index_in_dim(scale, me, 0, keepdims=False)
     scaled = (own_scale[:, None] * lowrank).astype(jnp.bfloat16)
 

time: 60.3 us -> 65.4 us (1.085)
  matrix products: 1.65 us -> 7.02 us
  waiting for transfers between devices: 33 us -> 28.9 us
  starting transfers between devices: 13.2 us -> 16 us
  Pallas kernels: 7.39 us -> 8.2 us
    ppermute x15 -> x12, waiting for transfers between devices: 33 us -> 28.9 us  [trade(): return lax.ppermute(value, ('expert', 'tensor'), pairs)]
    dot_general x1, matrix products: 0.75 us -> 4.06 us  [local(): term = jnp.dot(hidden_sum, base_down[0], preferred_element_type=jnp.float32)]
    all_to_all x0 -> x1, starting transfers between devices: none -> 3.28 us  [local(): lax.all_to_all(partial_codes, 'tensor', split_axis=0, concat_axis=0, tile...]
    dot_general x1, matrix products: 0.49 us -> 1.96 us  [local(): jnp.dot(scaled, delta_back[0], preferred_element_type=jnp.float32)]
    pallas_call x1, Pallas kernels: 5.47 us -> 6.15 us  [gate_up_product(): pl.pallas_call(gate_up_kernel, out_shape=jax.ShapeDtypeStruct((2 * x.shap...]
    ppermute x15 -> x12, starting transfers between devices: 13.2 us -> 12.7 us  [trade(): return lax.ppermute(value, ('expert', 'tensor'), pairs)]
  transfers between devices with their start and end apart: 15 -> 13, of which waited for: 11 -> 9; matrix products, arithmetic and copies ran while one was open for 3% -> 8% of each run, Pallas kernels for 9% -> 9%
where the time goes in v7:
time: 65.4 us; the launch traced here: 65 us
  waiting for transfers between devices  28.9 us (44%)
  starting transfers between devices  16 us (24%)
  Pallas kernels  8.2 us (13%)
  matrix products  7.02 us (11%)
  other arithmetic  4.07 us (6%)
    ppermute x12, waiting for transfers between devices, trade(): return lax.ppermute(value, ('expert', 'tensor'), pairs)  28.9 us
    ppermute x12, starting transfers between devices, trade(): return lax.ppermute(value, ('expert', 'tensor'), pairs)  12.7 us
    pallas_call x1, Pallas kernels, gate_up_product(): pl.pallas_call(gate_up_kernel, out_shape=jax.ShapeDtypeStruct((2 * x.shap...  6.15 us
    dot_general x1, matrix products, local(): term = jnp.dot(hidden_sum, base_down[0], preferred_element_type=jnp.float32)  4.06 us
    all_to_all x1, starting transfers between devices, local(): lax.all_to_all(partial_codes, 'tensor', split_axis=0, concat_axis=0, tile...  3.28 us
    pallas_call x1, Pallas kernels, code_product(): pl.pallas_call(code_kernel, out_shape=jax.ShapeDtypeStruct((x.shape[0], r...  2.05 us
    dot_general x1, matrix products, local(): jnp.dot(scaled, delta_back[0], preferred_element_type=jnp.float32)  1.96 us
  transfers between devices with their start and end apart: 13, of which 9 were waited for; matrix products, arithmetic and copies ran while one was open for 8% of the time, Pallas kernels for 9%

profile of v7, /device:TPU:0, one launch (start us, length us, event | category | flops | bytes accessed | tf_op | source)
XLA Modules:
  0.0 65.0 jit_solution(15618378547497687494)
XLA Ops:
  0.0 0.8 %convert_bitcast_fusion = (bf16[4,8]{1,0:T(4,128)(2,1)S(1)}, bf16[4,8]{1,0:T(4,128)(2,1)S(1)}) fusion(s32[1,4,8]{2,1,0:T(4,128)} %param.12, s32[1,4,8]{2,1,0:T(4,128)} %param.11), kind=kLoop, calls=%fused_computation.77 | loop fusion | flops 64 | bytes 384 | tf_op jit(solution)/shard_map/squeeze | solution.py:146
  0.8 0.1 fusion.28
  0.9 4.0 %collective-permute-start.1 = (bf16[4,128]{1,0:T(4,128)(2,1)S(1)}, bf16[4,128]{1,0:T(4,128)(2,1)S(1)}, u32[]{:S(2)}, u32[]{:S(2)}) collective-permute-start(bf16[4,128]{1,0:T(4,128)(2,1)S(1)} %fusion.28), channel_id=1, source_target_pairs={{0,8},{1,9},{2,10},{3,11},{4,12},{5,13},{6,14},{7,15},{8,0},{9,1},... | collective-permute-start | bytes 3080 | tf_op jit(solution)/shard_map/ppermute | solution.py:33
  5.0 0.1 collective-permute-start
  5.0 0.9 %pad_maximum_fusion.6 = bf16[4,7296]{1,0:T(4,128)(2,1)S(1)} fusion(bf16[4,128]{1,0:T(4,128)(2,1)S(1)} %fusion.28, bf16[4,7168]{1,0:T(4,128)(2,1)} %bitcast.53), kind=kLoop, calls=%fused_computation.54 | loop fusion | flops 116736 | bytes 116736 | tf_op jit(solution)/shard_map/concatenate | solution.py:148
  5.9 0.6 collective-permute-done.1
  6.5 4.0 %collective-permute-done = bf16[4,7168]{1,0:T(4,128)(2,1)S(1)} collective-permute-done((bf16[4,7168]{1,0:T(4,128)(2,1)}, bf16[4,7168]{1,0:T(4,128)(2,1)S(1)}, u32[]{:S(2)}, u32[]{:S(2)}) %collective-permute-start) | collective-permute-done | bytes 57376 | tf_op jit(solution)/shard_map/ppermute | solution.py:33
  10.5 0.1 maximum_maximum_fusion
  10.5 1.6 %collective-permute-start.2 = (bf16[8,7296]{1,0:T(8,128)(2,1)S(1)}, bf16[8,7296]{1,0:T(8,128)(2,1)S(1)}, u32[]{:S(2)}, u32[]{:S(2)}) collective-permute-start(bf16[8,7296]{1,0:T(8,128)(2,1)S(1)} %maximum_maximum_fusion), channel_id=1, source_target_pairs={{0,2},{1,5},{2,0},{3,7},{4,6},{5,1},{6,4},{7,3},{8,10},{9,13},{10,... | collective-permute-start | bytes 350216 | tf_op jit(solution)/shard_map/ppermute | solution.py:33
  12.1 3.5 %collective-permute-done.2 = bf16[8,7296]{1,0:T(8,128)(2,1)S(1)} collective-permute-done((bf16[8,7296]{1,0:T(8,128)(2,1)S(1)}, bf16[8,7296]{1,0:T(8,128)(2,1)S(1)}, u32[]{:S(2)}, u32[]{:S(2)}) %collective-permute-start.2) | collective-permute-done | bytes 116768 | tf_op jit(solution)/shard_map/ppermute | solution.py:33
  15.6 0.1 broadcast_select_fusion.9
  15.7 1.3 %collective-permute-start.3 = (bf16[16,7296]{1,0:T(8,128)(2,1)S(1)}, bf16[16,7296]{1,0:T(8,128)(2,1)S(1)}, u32[]{:S(2)}, u32[]{:S(2)}) collective-permute-start(bf16[16,7296]{1,0:T(8,128)(2,1)S(1)} %pad_maximum_fusion.2), channel_id=1, source_target_pairs={{0,4},{1,3},{2,6},{3,1},{4,0},{5,7},{6,2},{7,5},{8,12},{9,11},{10,... | collective-permute-start | bytes 700424 | tf_op jit(solution)/shard_map/ppermute | solution.py:33
  17.0 4.9 %collective-permute-done.3 = bf16[16,7296]{1,0:T(8,128)(2,1)S(1)} collective-permute-done((bf16[16,7296]{1,0:T(8,128)(2,1)S(1)}, bf16[16,7296]{1,0:T(8,128)(2,1)S(1)}, u32[]{:S(2)}, u32[]{:S(2)}) %collective-permute-start.3) | collective-permute-done | bytes 233504 | tf_op jit(solution)/shard_map/ppermute | solution.py:33
  21.8 0.1 broadcast_select_fusion.4
  22.0 0.1 collective-permute-start.4
  22.1 1.8 %collective-permute-done.4 = bf16[32,7296]{1,0:T(8,128)(2,1)S(1)} collective-permute-done((bf16[32,7296]{1,0:T(8,128)(2,1)S(1)}, bf16[32,7296]{1,0:T(8,128)(2,1)S(1)}, u32[]{:S(2)}, u32[]{:S(2)}) %collective-permute-start.4) | collective-permute-done | bytes 466976 | tf_op jit(solution)/shard_map/ppermute | solution.py:33
  23.9 0.2 broadcast_select_fusion.1
  24.0 0.2 convert_reduce_fusion.1
  24.2 0.1 pad_maximum_fusion.x
  24.3 2.1 %shard_map.101 = bf16[64,128]{1,0:T(8,128)(2,1)S(1)} custom-call(bf16[64,7296]{1,0:T(8,128)(2,1)S(1)} %pad_maximum_fusion.x, bf16[7168,128]{1,0:T(8,128)(2,1)} %bitcast.50), custom_call_target="tpu_custom_call" | custom-call | flops 117440512 | bytes 1835008 | tf_op jit(solution)/shard_map/pallas_call | solution.py:66
  26.4 1.3 %collective-permute-start.7 = (bf16[64,128]{1,0:T(8,128)(2,1)S(1)}, bf16[64,128]{1,0:T(8,128)(2,1)S(1)}, u32[]{:S(2)}, u32[]{:S(2)}) collective-permute-start(bf16[64,128]{1,0:T(8,128)(2,1)S(1)} %shard_map.101), channel_id=1, source_target_pairs={{0,3},{1,2},{2,1},{3,0},{4,7},{5,6},{6,5},{7,4},{8,11},{9,10},{10,... | collective-permute-start | bytes 49160 | tf_op jit(solution)/shard_map/ppermute | solution.py:33
  27.7 0.6 collective-permute-start.6
  28.2 0.1 collective-permute-start.5
  28.3 0.1 fusion.23
  28.4 0.1 copy.18
  28.4 0.1 copy.17
  28.5 6.1 %shard_map.100 = f32[128,256]{1,0:T(8,128)S(1)} custom-call(bf16[64,7296]{1,0:T(8,128)(2,1)S(1)} %pad_maximum_fusion.x, bf16[7168,2,256]{2,1,0:T(2,128)(2,1)} %bitcast.49), custom_call_target="tpu_custom_call" | custom-call | flops 469762048 | bytes 7340032 | tf_op jit(solution)/shard_map/pallas_call | solution.py:110
  34.7 0.1 select_reduce_fusion
  34.8 0.1 select_reduce_fusion.1
  35.0 0.2 fusion.4
  35.2 0.1 multiply_reduce_fusion
  35.3 0.3 copy-done.2
  35.6 0.8 %convolution_convert_fusion = bf16[4,64,128]{2,1,0:T(8,128)(2,1)} fusion(bf16[1,4,256,128]{3,2,1,0:T(8,128)(2,1)S(1)} %copy-done.2, bf16[4,64,256]{2,1,0:T(8,128)(2,1)S(1)} %get-tuple-element.6), kind=kOutput, calls=%fused_computation.10 | convolution fusion | flops 16809984 | bytes 458752 | tf_op jit(solution)/shard_map/srf,sfk->srk/dot_general | solution.py:186
  36.4 3.3 %all-to-all-start = ((bf16[4,64,128]{2,1,0:T(8,128)(2,1)}), bf16[4,64,128]{2,1,0:T(8,128)(2,1)S(1)}, u32[]{:S(2)}, u32[]{:S(2)}) async-start(bf16[4,64,128]{2,1,0:T(8,128)(2,1)} %convolution_convert_fusion), calls=%async_computation | async-start | bytes 131072 | tf_op jit(solution)/shard_map/all_to_all | solution.py:189
  39.7 4.1 %fusion.1 = f32[64,7168]{1,0:T(8,128)} fusion(bf16[1,256,7168]{2,1,0:T(8,128)(2,1)} %param.15, bf16[64,256]{1,0:T(8,128)(2,1)S(1)} %get-tuple-element.5), kind=kOutput, calls=%fused_computation.2 | convolution fusion | flops 234881024 | bytes 5537792 | tf_op jit(solution)/shard_map/dot_general | solution.py:194
  43.8 2.0 %fusion = bf16[64,7168]{1,0:T(8,128)(2,1)S(1)} fusion(f32[64,7168]{1,0:T(8,128)} %fusion.1, bf16[1,128,7168]{2,1,0:T(8,128)(2,1)S(1)} %copy-done, f32[64,128]{1,0:T(8,128)S(1)} %convert_reduce_fusion, f32[64]{0:T(128)S(1)} %fusion.29), kind=kOutput, calls=%fused_computation.1 | convolution fusion | flops 118374400 | bytes 4620544 | tf_op jit(solution)/shard_map/dot_general | solution.py:195
  45.8 0.5 collective-permute-start.8
  46.3 1.4 %collective-permute-done.8 = bf16[32,7168]{1,0:T(8,128)(2,1)S(1)} collective-permute-done((bf16[32,7168]{1,0:T(8,128)(2,1)S(1)}, bf16[32,7168]{1,0:T(8,128)(2,1)S(1)}, u32[]{:S(2)}, u32[]{:S(2)}) %collective-permute-start.8) | collective-permute-done | bytes 458784 | tf_op jit(solution)/shard_map/ppermute | solution.py:33
  47.8 0.2 add_convert_fusion
  48.0 0.1 broadcast_select_fusion.5
  48.1 1.3 %collective-permute-start.9 = (bf16[16,7168]{1,0:T(8,128)(2,1)S(1)}, bf16[16,7168]{1,0:T(8,128)(2,1)S(1)}, u32[]{:S(2)}, u32[]{:S(2)}) collective-permute-start(bf16[16,7168]{1,0:T(8,128)(2,1)S(1)} %broadcast_select_fusion.5), channel_id=1, source_target_pairs={{0,4},{1,3},{2,6},{3,1},{4,0},{5,7},{6,2},{7,5},{8,12},{9,11},{10,... | collective-permute-start | bytes 688136 | tf_op jit(solution)/shard_map/ppermute | solution.py:33
  49.3 4.8 %collective-permute-done.9 = bf16[16,7168]{1,0:T(8,128)(2,1)S(1)} collective-permute-done((bf16[16,7168]{1,0:T(8,128)(2,1)S(1)}, bf16[16,7168]{1,0:T(8,128)(2,1)S(1)}, u32[]{:S(2)}, u32[]{:S(2)}) %collective-permute-start.9) | collective-permute-done | bytes 229408 | tf_op jit(solution)/shard_map/ppermute | solution.py:33
  54.1 0.1 add_convert_fusion.1
  54.3 2.0 %collective-permute-start.10 = (bf16[8,7168]{1,0:T(8,128)(2,1)S(1)}, bf16[8,7168]{1,0:T(8,128)(2,1)S(1)}, u32[]{:S(2)}, u32[]{:S(2)}) collective-permute-start(bf16[8,7168]{1,0:T(8,128)(2,1)S(1)} %broadcast_select_fusion.12), channel_id=1, source_target_pairs={{0,2},{1,5},{2,0},{3,7},{4,6},{5,1},{6,4},{7,3},{8,10},{9,13},{10,... | collective-permute-start | bytes 344072 | tf_op jit(solution)/shard_map/ppermute | solution.py:33
  56.2 2.9 %collective-permute-done.10 = bf16[8,7168]{1,0:T(8,128)(2,1)S(1)} collective-permute-done((bf16[8,7168]{1,0:T(8,128)(2,1)S(1)}, bf16[8,7168]{1,0:T(8,128)(2,1)S(1)}, u32[]{:S(2)}, u32[]{:S(2)}) %collective-permute-start.10) | collective-permute-done | bytes 114720 | tf_op jit(solution)/shard_map/ppermute | solution.py:33
  59.2 0.1 collective-permute-start.11
  59.3 5.1 %collective-permute-done.11 = bf16[4,7168]{1,0:T(4,128)(2,1)S(1)} collective-permute-done((bf16[4,7168]{1,0:T(4,128)(2,1)S(1)}, bf16[4,7168]{1,0:T(4,128)(2,1)S(1)}, u32[]{:S(2)}, u32[]{:S(2)}) %collective-permute-start.11) | collective-permute-done | bytes 57376 | tf_op jit(solution)/shard_map/ppermute | solution.py:33
  64.3 0.7 %fusion.17 = bf16[1,4,7168]{2,1,0:T(4,128)(2,1)} fusion(bf16[4,7168]{1,0:T(4,128)(2,1)S(1)} %collective-permute-done.11, bf16[8,7168]{1,0:T(8,128)(2,1)S(1)} %add_convert_fusion.2), kind=kLoop, calls=%fused_computation.55 | loop fusion | flops 114688 | bytes 172032 | tf_op jit(solution)/shard_map/broadcast_in_dim | solution.py:218
  (26 shorter events, 0.4 us)
Async XLA Ops:
  0.0 43.8 %copy-start = (bf16[1,128,7168]{2,1,0:T(8,128)(2,1)S(1)}, bf16[1,128,7168]{2,1,0:T(8,128)(2,1)}, u32[]{:S(2)}) copy-start(bf16[1,128,7168]{2,1,0:T(8,128)(2,1)} %param.19) | copy-start | bytes 5505028
  0.9 5.6 %collective-permute-start.1 = (bf16[4,128]{1,0:T(4,128)(2,1)S(1)}, bf16[4,128]{1,0:T(4,128)(2,1)S(1)}, u32[]{:S(2)}, u32[]{:S(2)}) collective-permute-start(bf16[4,128]{1,0:T(4,128)(2,1)S(1)} %fusion.28), channel_id=1, source_target_pairs={{0,8},{1,9},{2,10},{3,11},{4,12},{5,13},{6,14},{7,15},{8,0},{9,1},... | collective-permute-start | bytes 3080 | tf_op jit(solution)/shard_map/ppermute | solution.py:33
  5.0 5.5 %collective-permute-start = (bf16[4,7168]{1,0:T(4,128)(2,1)}, bf16[4,7168]{1,0:T(4,128)(2,1)S(1)}, u32[]{:S(2)}, u32[]{:S(2)}) collective-permute-start(bf16[4,7168]{1,0:T(4,128)(2,1)} %bitcast.52), channel_id=1, source_target_pairs={{0,8},{1,9},{2,10},{3,11},{4,12},{5,13},{6,14},{7,15},{8,0},{9,1},... | collective-permute-start | bytes 172040 | tf_op jit(solution)/shard_map/ppermute | solution.py:33
  10.5 5.0 %collective-permute-start.2 = (bf16[8,7296]{1,0:T(8,128)(2,1)S(1)}, bf16[8,7296]{1,0:T(8,128)(2,1)S(1)}, u32[]{:S(2)}, u32[]{:S(2)}) collective-permute-start(bf16[8,7296]{1,0:T(8,128)(2,1)S(1)} %maximum_maximum_fusion), channel_id=1, source_target_pairs={{0,2},{1,5},{2,0},{3,7},{4,6},{5,1},{6,4},{7,3},{8,10},{9,13},{10,... | collective-permute-start | bytes 350216 | tf_op jit(solution)/shard_map/ppermute | solution.py:33
  15.7 6.1 %collective-permute-start.3 = (bf16[16,7296]{1,0:T(8,128)(2,1)S(1)}, bf16[16,7296]{1,0:T(8,128)(2,1)S(1)}, u32[]{:S(2)}, u32[]{:S(2)}) collective-permute-start(bf16[16,7296]{1,0:T(8,128)(2,1)S(1)} %pad_maximum_fusion.2), channel_id=1, source_target_pairs={{0,4},{1,3},{2,6},{3,1},{4,0},{5,7},{6,2},{7,5},{8,12},{9,11},{10,... | collective-permute-start | bytes 700424 | tf_op jit(solution)/shard_map/ppermute | solution.py:33
  22.0 1.9 %collective-permute-start.4 = (bf16[32,7296]{1,0:T(8,128)(2,1)S(1)}, bf16[32,7296]{1,0:T(8,128)(2,1)S(1)}, u32[]{:S(2)}, u32[]{:S(2)}) collective-permute-start(bf16[32,7296]{1,0:T(8,128)(2,1)S(1)} %pad_maximum_fusion.1), channel_id=1, source_target_pairs={{0,1},{1,0},{2,3},{3,2},{4,5},{5,4},{6,7},{7,6},{8,9},{9,8},{10,11... | collective-permute-start | bytes 1400840 | tf_op jit(solution)/shard_map/ppermute | solution.py:33
  26.4 8.5 %collective-permute-start.7 = (bf16[64,128]{1,0:T(8,128)(2,1)S(1)}, bf16[64,128]{1,0:T(8,128)(2,1)S(1)}, u32[]{:S(2)}, u32[]{:S(2)}) collective-permute-start(bf16[64,128]{1,0:T(8,128)(2,1)S(1)} %shard_map.101), channel_id=1, source_target_pairs={{0,3},{1,2},{2,1},{3,0},{4,7},{5,6},{6,5},{7,4},{8,11},{9,10},{10,... | collective-permute-start | bytes 49160 | tf_op jit(solution)/shard_map/ppermute | solution.py:33
  27.7 7.2 %collective-permute-start.6 = (bf16[64,128]{1,0:T(8,128)(2,1)S(1)}, bf16[64,128]{1,0:T(8,128)(2,1)S(1)}, u32[]{:S(2)}, u32[]{:S(2)}) collective-permute-start(bf16[64,128]{1,0:T(8,128)(2,1)S(1)} %shard_map.101), channel_id=1, source_target_pairs={{0,2},{1,3},{2,0},{3,1},{4,6},{5,7},{6,4},{7,5},{8,10},{9,11},{10,... | collective-permute-start | bytes 49160 | tf_op jit(solution)/shard_map/ppermute | solution.py:33
  28.2 6.7 %collective-permute-start.5 = (bf16[64,128]{1,0:T(8,128)(2,1)S(1)}, bf16[64,128]{1,0:T(8,128)(2,1)S(1)}, u32[]{:S(2)}, u32[]{:S(2)}) collective-permute-start(bf16[64,128]{1,0:T(8,128)(2,1)S(1)} %shard_map.101), channel_id=1, source_target_pairs={{0,1},{1,0},{2,3},{3,2},{4,5},{5,4},{6,7},{7,6},{8,9},{9,8},{10,11... | collective-permute-start | bytes 49160 | tf_op jit(solution)/shard_map/ppermute | solution.py:33
  28.5 6.2 %copy-start.3 = (s32[16]{0:T(128)S(1)}, s32[16]{0:T(128)}, u32[]{:S(2)}) copy-start(s32[16]{0:T(128)} %param.13) | copy-start | bytes 196
  28.5 6.5 %copy-start.1 = (bf16[1,4,128,2,256]{4,3,2,1,0:T(2,128)(2,1)S(1)}, bf16[1,4,128,2,256]{4,3,2,1,0:T(2,128)(2,1)}, u32[]{:S(2)}) copy-start(bf16[1,4,128,2,256]{4,3,2,1,0:T(2,128)(2,1)} %param.17) | copy-start | bytes 1572868
  34.7 1.0 %copy-start.2 = (bf16[1,4,256,128]{3,2,1,0:T(8,128)(2,1)S(1)}, bf16[1,4,256,128]{3,2,1,0:T(8,128)(2,1)}, u32[]{:S(2)}) copy-start(bf16[1,4,256,128]{3,2,1,0:T(8,128)(2,1)} %param.18) | copy-start | bytes 786436
  36.4 7.4 %all-to-all-start = ((bf16[4,64,128]{2,1,0:T(8,128)(2,1)}), bf16[4,64,128]{2,1,0:T(8,128)(2,1)S(1)}, u32[]{:S(2)}, u32[]{:S(2)}) async-start(bf16[4,64,128]{2,1,0:T(8,128)(2,1)} %convolution_convert_fusion), calls=%async_computation | async-start | bytes 131072 | tf_op jit(solution)/shard_map/all_to_all | solution.py:189
  45.8 1.9 %collective-permute-start.8 = (bf16[32,7168]{1,0:T(8,128)(2,1)S(1)}, bf16[32,7168]{1,0:T(8,128)(2,1)S(1)}, u32[]{:S(2)}, u32[]{:S(2)}) collective-permute-start(bf16[32,7168]{1,0:T(8,128)(2,1)S(1)} %broadcast_select_fusion.2), channel_id=1, source_target_pairs={{0,1},{1,0},{2,3},{3,2},{4,5},{5,4},{6,7},{7,6},{8,9},{9,8},{10,11... | collective-permute-start | bytes 1376264 | tf_op jit(solution)/shard_map/ppermute | solution.py:33
  48.1 6.1 %collective-permute-start.9 = (bf16[16,7168]{1,0:T(8,128)(2,1)S(1)}, bf16[16,7168]{1,0:T(8,128)(2,1)S(1)}, u32[]{:S(2)}, u32[]{:S(2)}) collective-permute-start(bf16[16,7168]{1,0:T(8,128)(2,1)S(1)} %broadcast_select_fusion.5), channel_id=1, source_target_pairs={{0,4},{1,3},{2,6},{3,1},{4,0},{5,7},{6,2},{7,5},{8,12},{9,11},{10,... | collective-permute-start | bytes 688136 | tf_op jit(solution)/shard_map/ppermute | solution.py:33
  54.3 4.9 %collective-permute-start.10 = (bf16[8,7168]{1,0:T(8,128)(2,1)S(1)}, bf16[8,7168]{1,0:T(8,128)(2,1)S(1)}, u32[]{:S(2)}, u32[]{:S(2)}) collective-permute-start(bf16[8,7168]{1,0:T(8,128)(2,1)S(1)} %broadcast_select_fusion.12), channel_id=1, source_target_pairs={{0,2},{1,5},{2,0},{3,7},{4,6},{5,1},{6,4},{7,3},{8,10},{9,13},{10,... | collective-permute-start | bytes 344072 | tf_op jit(solution)/shard_map/ppermute | solution.py:33
  59.2 5.1 %collective-permute-start.11 = (bf16[4,7168]{1,0:T(4,128)(2,1)S(1)}, bf16[4,7168]{1,0:T(4,128)(2,1)S(1)}, u32[]{:S(2)}, u32[]{:S(2)}) collective-permute-start(bf16[4,7168]{1,0:T(4,128)(2,1)S(1)} %slice.107), channel_id=1, source_target_pairs={{0,8},{1,9},{2,10},{3,11},{4,12},{5,13},{6,14},{7,15},{8,0},{9,1},... | collective-permute-start | bytes 172040 | tf_op jit(solution)/shard_map/ppermute | solution.py:33

commit v8 on v6

--- a/solution.py
+++ b/solution.py
@@ -1,3 +1,5 @@
+import functools
+
 import jax
 import jax.numpy as jnp
 from jax import lax
@@ -45,73 +47,62 @@
     return jnp.where(flip, second, first), jnp.where(flip, first, second)
 
 
-def split_kernel(first, base, table, split, codes_in, rows, sems):
+def split_kernel(first, base, split, rows, split_rows, in_sems, out_sems):
     depth, _, columns = rows.shape
-    step = depth // (sems.shape[0] - 1)
-    copies = [
-        pltpu.make_async_copy(base.at[pl.ds(first + k, step)], rows.at[pl.ds(k, step)], sems.at[k // step])
-        for k in range(0, depth, step)
+    step = 512
+    count = depth // step
+    arrive = [
+        pltpu.make_async_copy(base.at[pl.ds(first + i * step, step)], rows.at[pl.ds(i * step, step)], in_sems.at[i])
+        for i in range(count)
     ]
-    whole = pltpu.make_async_copy(table, codes_in, sems.at[sems.shape[0] - 1])
-    for copy in copies:
+    leave = [
+        pltpu.make_async_copy(split_rows.at[pl.ds(i * step, step)], split.at[pl.ds(i * step, step)], out_sems.at[i])
+        for i in range(count)
+    ]
+    for copy in arrive:
         copy.start()
-    whole.start()
     row = lax.broadcasted_iota(jnp.int32, (256, 256), 0)
     column = lax.broadcasted_iota(jnp.int32, (256, 256), 1)
     source = 2 * row - jnp.where(row < 128, 0, 255)
     order = jnp.where(column == source, 1.0, 0.0).astype(jnp.bfloat16)
     flat = rows.reshape(2 * depth, columns)
-    for k in range(0, depth, 128):
-        if k % step == 0:
-            copies[k // step].wait()
-        sorted_rows = jnp.dot(order, flat[2 * k : 2 * k + 256, :], preferred_element_type=jnp.float32)
-        sorted_rows = sorted_rows.astype(jnp.bfloat16)
-        split[k : k + 128, :columns] = sorted_rows[:128]
-        split[k : k + 128, columns:] = sorted_rows[128:]
-    whole.wait()
-
-
-def split_gate_up(base, table, part, parts):
+    for i in range(count):
+        arrive[i].wait()
+        blocks = range(i * step, (i + 1) * step, 128)
+        wide = jnp.concatenate([flat[2 * k : 2 * k + 256, :] for k in blocks], axis=1)
+        wide = jnp.dot(order, wide, preferred_element_type=jnp.float32).astype(jnp.bfloat16)
+        for j, k in enumerate(blocks):
+            split_rows[k : k + 128, :columns] = wide[:128, j * columns : (j + 1) * columns]
+            split_rows[k : k + 128, columns:] = wide[128:, j * columns : (j + 1) * columns]
+        leave[i].start()
+    for copy in leave:
+        copy.wait()
+
+
+def split_gate_up(base, part, parts):
     depth, _, columns = base.shape
     block = depth // parts
     return pl.pallas_call(
-        lambda base, table, *rest: split_kernel(
-            part * block, base, table.at[pl.ds(part * block, block)], *rest
-        ),
-        out_shape=(
+        functools.partial(split_kernel, part * block),
+        out_shape=pltpu.HBM((block, 2 * columns), base.dtype),
+        in_specs=[HBM],
+        out_specs=HBM,
+        scratch_shapes=[
+            pltpu.VMEM((block, 2, columns), base.dtype),
             pltpu.VMEM((block, 2 * columns), base.dtype),
-            pltpu.VMEM((block, table.shape[1]), table.dtype),
-        ),
-        in_specs=[HBM, HBM],
-        out_specs=(VMEM, VMEM),
-        scratch_shapes=[pltpu.VMEM((block, 2, columns), base.dtype), pltpu.SemaphoreType.DMA((block // 512 + 1,))],
+            pltpu.SemaphoreType.DMA((block // 512,)),
+            pltpu.SemaphoreType.DMA((block // 512,)),
+        ],
         compiler_params=pltpu.CompilerParams(vmem_limit_bytes=24 << 20),
-        cost_estimate=pl.CostEstimate(flops=512 * block * columns, bytes_accessed=4 * block * columns, transcendentals=0),
-    )(in_hbm(base), in_hbm(table))
-
-
-def product_kernel(x, *refs):
-    *tables, out = refs
-    total = jnp.zeros(out.shape, jnp.float32)
-    start = 0
-    for table in tables:
-        depth = table.shape[0]
-        total += jnp.dot(x[:, start : start + depth], table[...], preferred_element_type=jnp.float32)
-        start += depth
-    out[...] = total.astype(out.dtype)
-
-
-def product(x, tables, dtype):
-    columns = tables[0].shape[1]
-    size = sum(table.size for table in tables)
-    return pl.pallas_call(
-        product_kernel,
-        out_shape=jax.ShapeDtypeStruct((x.shape[0], columns), dtype),
-        in_specs=[VMEM] * (1 + len(tables)),
-        out_specs=VMEM,
-        compiler_params=pltpu.CompilerParams(vmem_limit_bytes=16 << 20),
-        cost_estimate=pl.CostEstimate(flops=2 * x.shape[0] * size, bytes_accessed=2 * size, transcendentals=0),
-    )(x, *(pltpu.with_memory_space_constraint(table, pltpu.VMEM) for table in tables))
+        cost_estimate=pl.CostEstimate(flops=512 * block * columns, bytes_accessed=8 * block * columns, transcendentals=0),
+    )(in_hbm(base))
+
+
+def split_beside(held, parts, weights):
+    held, parts, weights = lax.optimization_barrier((held, parts, weights))
+    if len(parts) < 2:
+        parts = [*parts, split_gate_up(weights[0], len(parts), 2)]
+    return held, parts, weights
 
 
 def local(
@@ -137,36 +128,37 @@
     along, across = halves(clusters), halves(members // 2)
     shared, paired = along[: len(along) - len(across)], along[len(along) - len(across) :]
 
-    def pack(rows, routes, numerators):
-        side = jnp.concatenate([routes, numerators], axis=1).astype(jnp.bfloat16)
-        return jnp.concatenate([rows, jnp.pad(side, ((0, 0), (0, 128 - 2 * top)))], axis=1)
-
-    own = (tokens[0], routes[0], numerators[0])
-    held = lax.optimization_barrier(pack(*own))
+    side = jnp.concatenate([routes[0], numerators[0]], axis=1).astype(jnp.bfloat16)
+    side = jnp.pad(side, ((0, 0), (0, 128 - 2 * top)))
+    held = lax.optimization_barrier(jnp.concatenate([tokens[0], side], axis=1))
 
     for i, mask in enumerate(shared):
         if i == 0:
-            received = pack(*(trade(piece, (mask, 0), (mask, 0)) for piece in own))
+            pieces = [trade(piece, (mask, 0), (mask, 0)) for piece in (tokens[0], side)]
+            received = jnp.concatenate(pieces, axis=1)
         else:
             received = trade(held, (mask, 0), (mask, 0))
         held = jnp.concatenate([held, received])
-        if i == 0:
-            parts = [split_gate_up(base_in[0], delta_in[0], 0, 2)]
-            held, parts[0], *later = lax.optimization_barrier((held, parts[0], base_in, delta_in))
+    parts, weights = [], base_in
     for z, x in zip(paired, across):
         size = held.shape[0]
         flag = (me // (2 * x)) % 2 == 1
+        held, parts, weights = split_beside(held, parts, weights)
         held = jnp.concatenate(ordered((core == 0) & flag, held, trade(held, (0, 2 * x), (z, 0))))
-        if len(parts) == 1:
-            parts.append(split_gate_up(later[0][0], later[1][0], 1, 2))
-            held, parts[1] = lax.optimization_barrier((held, parts[1]))
+        held, parts, weights = split_beside(held, parts, weights)
         low, high = ordered((core == 1) & flag, held, trade(held, (z, 0), (0, 2 * x)))
         inner = ordered(core == 1, low[size:], high[:size])
         held = jnp.concatenate([low[:size], *inner, high[size:]])
+    held, parts = lax.optimization_barrier((held, parts))
     held = by_rows(jnp.concatenate(ordered(core == 1, held, trade(held, (0, 1), (0, 1)))))
 
-    codes = product(held, [part[1] for part in parts], jnp.bfloat16)
-    projected = product(held, [part[0] for part in parts], jnp.float32)
+    rows = held[:, :width]
+    codes = jnp.dot(rows, delta_in[0], preferred_element_type=jnp.float32).astype(jnp.bfloat16)
+    block = parts[0].shape[0]
+    projected = sum(
+        jnp.dot(rows[:, i * block : (i + 1) * block], part, preferred_element_type=jnp.float32)
+        for i, part in enumerate(parts)
+    )
 
     side = by_rows(held[:, width:])
     all_routes = side[:, :top].astype(jnp.int32)

time: 67.6 us -> 56.6 us (0.84)
  local copies, waits for them, and re-layouts: 11.4 us -> 1.64 us
  matrix products: 1.65 us -> 5.63 us
  starting transfers between devices: 17.7 us -> 14.7 us
  waiting for transfers between devices: 22.3 us -> 21 us
  other arithmetic: 4.54 us -> 3.84 us
    unnamed x26 -> x14, local copies, waits for them, and re-layouts: 11.2 us -> 1.43 us
    ppermute x16 -> x15, starting transfers between devices: 17.7 us -> 14.7 us  [trade(): return lax.ppermute(value, ('expert', 'tensor'), pairs)]
    dot_general x1, matrix products: 0.75 us -> 2.79 us  [local(): term = jnp.dot(hidden_sum, base_down[0], preferred_element_type=jnp.float32)]
    dot_general x0 -> x3, matrix products: none -> 1.94 us  [the longest x2 1.48 us: local(): jnp.dot(rows[:, i * block:(i + 1) * block], part, preferred_element_type=...]
    another operation x4 -> x0, other arithmetic: 1.38 us -> none
    ppermute x16 -> x15, waiting for transfers between devices: 22.3 us -> 21 us  [trade(): return lax.ppermute(value, ('expert', 'tensor'), pairs)]
    squeeze x0 -> x1, other arithmetic: none -> 0.84 us  [local(): numerators[0]]
    pallas_call x4 -> x2, Pallas kernels: 9.25 us -> 9.13 us  [split_gate_up(): pl.pallas_call(functools.partial(split_kernel, part * block), out_shape=p...]
  transfers between devices with their start and end apart: 16 -> 15, of which waited for: 8 -> 8; matrix products, arithmetic and copies ran while one was open for 5% -> 10% of each run, Pallas kernels for 13% -> 16%
where the time goes in v8:
time: 56.6 us; the launch traced here: 56.3 us
  waiting for transfers between devices  21 us (37%)
  starting transfers between devices  14.7 us (26%)
  Pallas kernels  9.13 us (16%)
  matrix products  5.63 us (10%)
  other arithmetic  3.84 us (7%)
  local copies, waits for them, and re-layouts  1.64 us (3%)
    ppermute x15, waiting for transfers between devices, trade(): return lax.ppermute(value, ('expert', 'tensor'), pairs)  21 us
    ppermute x15, starting transfers between devices, trade(): return lax.ppermute(value, ('expert', 'tensor'), pairs)  14.7 us
    pallas_call x2, Pallas kernels, split_gate_up(): pl.pallas_call(functools.partial(split_kernel, part * block), out_shape=p...  9.13 us
    dot_general x1, matrix products, local(): term = jnp.dot(hidden_sum, base_down[0], preferred_element_type=jnp.float32)  2.79 us
    dot_general x2, matrix products, local(): jnp.dot(rows[:, i * block:(i + 1) * block], part, preferred_element_type=...  1.48 us
    unnamed x14, local copies, waits for them, and re-layouts  1.43 us
  transfers between devices with their start and end apart: 15, of which 8 were waited for; matrix products, arithmetic and copies ran while one was open for 10% of the time, Pallas kernels for 16%

profile of v8, /device:TPU:0, one launch (start us, length us, event | category | flops | bytes accessed | tf_op | source)
XLA Modules:
  0.0 56.3 jit_solution(12570616672255580032)
XLA Ops:
  0.0 0.8 %convert_bitcast_fusion = (bf16[4,8]{1,0:T(4,128)(2,1)S(1)}, bf16[4,8]{1,0:T(4,128)(2,1)S(1)}) fusion(s32[1,4,8]{2,1,0:T(4,128)} %param.12, s32[1,4,8]{2,1,0:T(4,128)} %param.11), kind=kLoop, calls=%fused_computation.93 | loop fusion | flops 64 | bytes 384 | tf_op jit(solution)/shard_map/squeeze | solution.py:131
  0.8 0.1 fusion.44
  0.9 4.0 %collective-permute-start.1 = (bf16[4,128]{1,0:T(4,128)(2,1)S(1)}, bf16[4,128]{1,0:T(4,128)(2,1)S(1)}, u32[]{:S(2)}, u32[]{:S(2)}) collective-permute-start(bf16[4,128]{1,0:T(4,128)(2,1)S(1)} %fusion.44), channel_id=1, source_target_pairs={{0,8},{1,9},{2,10},{3,11},{4,12},{5,13},{6,14},{7,15},{8,0},{9,1},... | collective-permute-start | bytes 3080 | tf_op jit(solution)/shard_map/ppermute | solution.py:35
  5.0 0.1 collective-permute-start
  5.0 0.9 %pad_maximum_fusion.7 = bf16[4,7296]{1,0:T(4,128)(2,1)S(1)} fusion(bf16[4,128]{1,0:T(4,128)(2,1)S(1)} %fusion.44, bf16[4,7168]{1,0:T(4,128)(2,1)} %bitcast.71), kind=kLoop, calls=%fused_computation.61 | loop fusion | flops 116736 | bytes 116736 | tf_op jit(solution)/shard_map/concatenate | solution.py:133
  5.9 0.6 %collective-permute-done.1 = bf16[4,128]{1,0:T(4,128)(2,1)S(1)} collective-permute-done((bf16[4,128]{1,0:T(4,128)(2,1)S(1)}, bf16[4,128]{1,0:T(4,128)(2,1)S(1)}, u32[]{:S(2)}, u32[]{:S(2)}) %collective-permute-start.1) | collective-permute-done | bytes 1056 | tf_op jit(solution)/shard_map/ppermute | solution.py:35
  6.5 4.0 %collective-permute-done = bf16[4,7168]{1,0:T(4,128)(2,1)S(1)} collective-permute-done((bf16[4,7168]{1,0:T(4,128)(2,1)}, bf16[4,7168]{1,0:T(4,128)(2,1)S(1)}, u32[]{:S(2)}, u32[]{:S(2)}) %collective-permute-start) | collective-permute-done | bytes 57376 | tf_op jit(solution)/shard_map/ppermute | solution.py:35
  10.5 0.1 maximum_maximum_fusion
  10.5 1.6 %collective-permute-start.2 = (bf16[8,7296]{1,0:T(8,128)(2,1)S(1)}, bf16[8,7296]{1,0:T(8,128)(2,1)S(1)}, u32[]{:S(2)}, u32[]{:S(2)}) collective-permute-start(bf16[8,7296]{1,0:T(8,128)(2,1)S(1)} %maximum_maximum_fusion), channel_id=1, source_target_pairs={{0,2},{1,5},{2,0},{3,7},{4,6},{5,1},{6,4},{7,3},{8,10},{9,13},{10,... | collective-permute-start | bytes 350216 | tf_op jit(solution)/shard_map/ppermute | solution.py:35
  12.1 4.6 %shard_map.100 = bf16[3584,512]{1,0:T(8,128)(2,1)} custom-call(bf16[7168,2,256]{2,1,0:T(2,128)(2,1)} %bitcast.67), custom_call_target="tpu_custom_call" | custom-call | flops 469762048 | bytes 7340032 | tf_op jit(solution)/shard_map/pallas_call | solution.py:85
  16.7 1.4 %collective-permute-start.3 = (bf16[16,7296]{1,0:T(8,128)(2,1)S(1)}, bf16[16,7296]{1,0:T(8,128)(2,1)S(1)}, u32[]{:S(2)}, u32[]{:S(2)}) collective-permute-start(bf16[16,7296]{1,0:T(8,128)(2,1)S(1)} %pad_maximum_fusion.3), channel_id=1, source_target_pairs={{0,4},{1,3},{2,6},{3,1},{4,0},{5,7},{6,2},{7,5},{8,12},{9,11},{10,... | collective-permute-start | bytes 700424 | tf_op jit(solution)/shard_map/ppermute | solution.py:35
  18.1 4.6 %shard_map.101 = bf16[3584,512]{1,0:T(8,128)(2,1)} custom-call(bf16[7168,2,256]{2,1,0:T(2,128)(2,1)} %bitcast.68), custom_call_target="tpu_custom_call" | custom-call | flops 469762048 | bytes 7340032 | tf_op jit(solution)/shard_map/pallas_call | solution.py:85
  22.7 0.1 collective-permute-done.3
  23.0 0.1 collective-permute-start.4
  23.1 1.8 %collective-permute-done.4 = bf16[32,7296]{1,0:T(8,128)(2,1)S(1)} collective-permute-done((bf16[32,7296]{1,0:T(8,128)(2,1)S(1)}, bf16[32,7296]{1,0:T(8,128)(2,1)S(1)}, u32[]{:S(2)}, u32[]{:S(2)}) %collective-permute-start.4) | collective-permute-done | bytes 466976 | tf_op jit(solution)/shard_map/ppermute | solution.py:35
  24.9 0.1 broadcast_select_fusion.1
  25.0 0.5 fusion.6
  25.5 0.2 collective-permute-start.5
  25.7 0.5 collective-permute-start.6
  26.2 1.2 %collective-permute-start.7 = (bf16[64,128]{1,0:T(8,128)(2,1)S(1)}, bf16[64,128]{1,0:T(8,128)(2,1)S(1)}, u32[]{:S(2)}, u32[]{:S(2)}) collective-permute-start(bf16[64,128]{1,0:T(8,128)(2,1)S(1)} %fusion.6), channel_id=1, source_target_pairs={{0,3},{1,2},{2,1},{3,0},{4,7},{5,6},{6,5},{7,4},{8,11},{9,10},{10,... | collective-permute-start | bytes 49160 | tf_op jit(solution)/shard_map/ppermute | solution.py:35
  27.4 0.2 convert_reduce_fusion
  27.6 0.7 %fusion.13 = f32[64,512]{1,0:T(8,128)S(1)} fusion(bf16[3584,512]{1,0:T(8,128)(2,1)S(1)} %copy-done.2, bf16[32,7296]{1,0:T(8,128)(2,1)S(1)} %get-tuple-element.25, bf16[32,7296]{1,0:T(8,128)(2,1)S(1)} %get-tuple-element.26), kind=kOutput, calls=%fused_computation.23 | convolution fusion | flops 235798528 | bytes 4734976 | tf_op jit(solution)/shard_map/dot_general | solution.py:159
  28.3 1.3 %copy-done.1 = bf16[3584,512]{1,0:T(8,128)(2,1)S(1)} copy-done((bf16[3584,512]{1,0:T(8,128)(2,1)S(1)}, bf16[3584,512]{1,0:T(8,128)(2,1)}, u32[]{:S(2)}) %copy-start.1) | copy-done | bytes 3670040
  29.6 0.7 %convolution_add_fusion.1 = f32[64,512]{1,0:T(8,128)S(1)} fusion(f32[64,512]{1,0:T(8,128)S(1)} %fusion.13, bf16[3584,512]{1,0:T(8,128)(2,1)S(1)} %copy-done.1, bf16[32,7296]{1,0:T(8,128)(2,1)S(1)} %get-tuple-element.25, bf16[32,7296]{1,0:T(8,128)(2,1)S(1)} %get-tuple-element.26), kind=kOutput, calls=%fused_computation.7 | convolution fusion | flops 235831296 | bytes 4866048 | tf_op jit(solution)/shard_map/dot_general | solution.py:159
  30.5 0.1 fusion.36
  30.6 0.1 copy.18
  30.6 0.1 select_reduce_fusion
  30.7 0.1 select_reduce_fusion.1
  30.9 0.2 fusion.10
  31.1 0.1 multiply_reduce_fusion
  31.3 0.1 copy-done.4
  31.4 0.2 convolution_convert_fusion
  31.6 0.6 %collective-permute-start.10 = (bf16[64,128]{1,0:T(8,128)(2,1)S(1)}, bf16[64,128]{1,0:T(8,128)(2,1)S(1)}, u32[]{:S(2)}, u32[]{:S(2)}) collective-permute-start(bf16[64,128]{1,0:T(8,128)(2,1)S(1)} %get-tuple-element.42), channel_id=1, source_target_pairs={{0,3},{1,2},{2,1},{3,0},{4,7},{5,6},{6,5},{7,4},{8,11},{9,10},{10,... | collective-permute-start | bytes 49160 | tf_op jit(solution)/shard_map/ppermute | solution.py:35
  32.2 0.1 collective-permute-start.8
  32.3 1.5 %collective-permute-start.9 = (bf16[64,128]{1,0:T(8,128)(2,1)S(1)}, bf16[64,128]{1,0:T(8,128)(2,1)S(1)}, u32[]{:S(2)}, u32[]{:S(2)}) collective-permute-start(bf16[64,128]{1,0:T(8,128)(2,1)S(1)} %get-tuple-element.43), channel_id=1, source_target_pairs={{0,2},{1,3},{2,0},{3,1},{4,6},{5,7},{6,4},{7,5},{8,10},{9,11},{10,... | collective-permute-start | bytes 49160 | tf_op jit(solution)/shard_map/ppermute | solution.py:35
  33.8 2.8 %fusion.1 = f32[64,7168]{1,0:T(8,128)S(1)} fusion(bf16[1,256,7168]{2,1,0:T(8,128)(2,1)} %param.15, bf16[64,256]{1,0:T(8,128)(2,1)S(1)} %get-tuple-element.21), kind=kOutput, calls=%fused_computation.2 | convolution fusion | flops 234881024 | bytes 5537792 | tf_op jit(solution)/shard_map/dot_general | solution.py:192
  36.6 0.5 fusion
  37.2 0.2 collective-permute-start.11
  37.4 1.7 %collective-permute-done.11 = bf16[32,7168]{1,0:T(8,128)(2,1)S(1)} collective-permute-done((bf16[32,7168]{1,0:T(8,128)(2,1)S(1)}, bf16[32,7168]{1,0:T(8,128)(2,1)S(1)}, u32[]{:S(2)}, u32[]{:S(2)}) %collective-permute-start.11) | collective-permute-done | bytes 458784 | tf_op jit(solution)/shard_map/ppermute | solution.py:35
  39.1 0.2 add_convert_fusion
  39.4 1.4 %collective-permute-start.12 = (bf16[16,7168]{1,0:T(8,128)(2,1)S(1)}, bf16[16,7168]{1,0:T(8,128)(2,1)S(1)}, u32[]{:S(2)}, u32[]{:S(2)}) collective-permute-start(bf16[16,7168]{1,0:T(8,128)(2,1)S(1)} %broadcast_select_fusion.5), channel_id=1, source_target_pairs={{0,4},{1,3},{2,6},{3,1},{4,0},{5,7},{6,2},{7,5},{8,12},{9,11},{10,... | collective-permute-start | bytes 688136 | tf_op jit(solution)/shard_map/ppermute | solution.py:35
  40.8 4.7 %collective-permute-done.12 = bf16[16,7168]{1,0:T(8,128)(2,1)S(1)} collective-permute-done((bf16[16,7168]{1,0:T(8,128)(2,1)S(1)}, bf16[16,7168]{1,0:T(8,128)(2,1)S(1)}, u32[]{:S(2)}, u32[]{:S(2)}) %collective-permute-start.12) | collective-permute-done | bytes 229408 | tf_op jit(solution)/shard_map/ppermute | solution.py:35
  45.4 0.1 add_convert_fusion.1
  45.6 1.0 %collective-permute-start.13 = (bf16[8,7168]{1,0:T(8,128)(2,1)S(1)}, bf16[8,7168]{1,0:T(8,128)(2,1)S(1)}, u32[]{:S(2)}, u32[]{:S(2)}) collective-permute-start(bf16[8,7168]{1,0:T(8,128)(2,1)S(1)} %broadcast_select_fusion.12), channel_id=1, source_target_pairs={{0,2},{1,5},{2,0},{3,7},{4,6},{5,1},{6,4},{7,3},{8,10},{9,13},{10,... | collective-permute-start | bytes 344072 | tf_op jit(solution)/shard_map/ppermute | solution.py:35
  46.5 3.9 %collective-permute-done.13 = bf16[8,7168]{1,0:T(8,128)(2,1)S(1)} collective-permute-done((bf16[8,7168]{1,0:T(8,128)(2,1)S(1)}, bf16[8,7168]{1,0:T(8,128)(2,1)S(1)}, u32[]{:S(2)}, u32[]{:S(2)}) %collective-permute-start.13) | collective-permute-done | bytes 114720 | tf_op jit(solution)/shard_map/ppermute | solution.py:35
  50.5 0.8 %collective-permute-start.14 = (bf16[4,7168]{1,0:T(4,128)(2,1)S(1)}, bf16[4,7168]{1,0:T(4,128)(2,1)S(1)}, u32[]{:S(2)}, u32[]{:S(2)}) collective-permute-start(bf16[4,7168]{1,0:T(4,128)(2,1)S(1)} %slice.121), channel_id=1, source_target_pairs={{0,8},{1,9},{2,10},{3,11},{4,12},{5,13},{6,14},{7,15},{8,0},{9,1},... | collective-permute-start | bytes 172040 | tf_op jit(solution)/shard_map/ppermute | solution.py:35
  51.3 4.3 %collective-permute-done.14 = bf16[4,7168]{1,0:T(4,128)(2,1)S(1)} collective-permute-done((bf16[4,7168]{1,0:T(4,128)(2,1)S(1)}, bf16[4,7168]{1,0:T(4,128)(2,1)S(1)}, u32[]{:S(2)}, u32[]{:S(2)}) %collective-permute-start.14) | collective-permute-done | bytes 57376 | tf_op jit(solution)/shard_map/ppermute | solution.py:35
  55.6 0.7 %fusion.28 = bf16[1,4,7168]{2,1,0:T(4,128)(2,1)} fusion(bf16[4,7168]{1,0:T(4,128)(2,1)S(1)} %collective-permute-done.14, bf16[8,7168]{1,0:T(8,128)(2,1)S(1)} %add_convert_fusion.2), kind=kLoop, calls=%fused_computation.62 | loop fusion | flops 114688 | bytes 172032 | tf_op jit(solution)/shard_map/broadcast_in_dim | solution.py:217
  (38 shorter events, 0.6 us)
Async XLA Ops:
  0.0 36.6 %copy-start = (bf16[1,128,7168]{2,1,0:T(8,128)(2,1)S(1)}, bf16[1,128,7168]{2,1,0:T(8,128)(2,1)}, u32[]{:S(2)}) copy-start(bf16[1,128,7168]{2,1,0:T(8,128)(2,1)} %param.19) | copy-start | bytes 5505028
  0.9 5.6 %collective-permute-start.1 = (bf16[4,128]{1,0:T(4,128)(2,1)S(1)}, bf16[4,128]{1,0:T(4,128)(2,1)S(1)}, u32[]{:S(2)}, u32[]{:S(2)}) collective-permute-start(bf16[4,128]{1,0:T(4,128)(2,1)S(1)} %fusion.44), channel_id=1, source_target_pairs={{0,8},{1,9},{2,10},{3,11},{4,12},{5,13},{6,14},{7,15},{8,0},{9,1},... | collective-permute-start | bytes 3080 | tf_op jit(solution)/shard_map/ppermute | solution.py:35
  5.0 5.5 %collective-permute-start = (bf16[4,7168]{1,0:T(4,128)(2,1)}, bf16[4,7168]{1,0:T(4,128)(2,1)S(1)}, u32[]{:S(2)}, u32[]{:S(2)}) collective-permute-start(bf16[4,7168]{1,0:T(4,128)(2,1)} %bitcast.70), channel_id=1, source_target_pairs={{0,8},{1,9},{2,10},{3,11},{4,12},{5,13},{6,14},{7,15},{8,0},{9,1},... | collective-permute-start | bytes 172040 | tf_op jit(solution)/shard_map/ppermute | solution.py:35
  10.5 6.1 %collective-permute-start.2 = (bf16[8,7296]{1,0:T(8,128)(2,1)S(1)}, bf16[8,7296]{1,0:T(8,128)(2,1)S(1)}, u32[]{:S(2)}, u32[]{:S(2)}) collective-permute-start(bf16[8,7296]{1,0:T(8,128)(2,1)S(1)} %maximum_maximum_fusion), channel_id=1, source_target_pairs={{0,2},{1,5},{2,0},{3,7},{4,6},{5,1},{6,4},{7,3},{8,10},{9,13},{10,... | collective-permute-start | bytes 350216 | tf_op jit(solution)/shard_map/ppermute | solution.py:35
  16.7 6.1 %collective-permute-start.3 = (bf16[16,7296]{1,0:T(8,128)(2,1)S(1)}, bf16[16,7296]{1,0:T(8,128)(2,1)S(1)}, u32[]{:S(2)}, u32[]{:S(2)}) collective-permute-start(bf16[16,7296]{1,0:T(8,128)(2,1)S(1)} %pad_maximum_fusion.3), channel_id=1, source_target_pairs={{0,4},{1,3},{2,6},{3,1},{4,0},{5,7},{6,2},{7,5},{8,12},{9,11},{10,... | collective-permute-start | bytes 700424 | tf_op jit(solution)/shard_map/ppermute | solution.py:35
  23.0 1.9 %collective-permute-start.4 = (bf16[32,7296]{1,0:T(8,128)(2,1)S(1)}, bf16[32,7296]{1,0:T(8,128)(2,1)S(1)}, u32[]{:S(2)}, u32[]{:S(2)}) collective-permute-start(bf16[32,7296]{1,0:T(8,128)(2,1)S(1)} %pad_maximum_fusion.2), channel_id=1, source_target_pairs={{0,1},{1,0},{2,3},{3,2},{4,5},{5,4},{6,7},{7,6},{8,9},{9,8},{10,11... | collective-permute-start | bytes 1400840 | tf_op jit(solution)/shard_map/ppermute | solution.py:35
  23.1 1.9 %copy-start.6 = (bf16[1,7168,128]{2,1,0:T(8,128)(2,1)S(1)}, bf16[1,7168,128]{2,1,0:T(8,128)(2,1)}, u32[]{:S(2)}) copy-start(bf16[1,7168,128]{2,1,0:T(8,128)(2,1)} %param.16) | copy-start | bytes 5505028
  25.0 2.6 %copy-start.2 = (bf16[3584,512]{1,0:T(8,128)(2,1)S(1)}, bf16[3584,512]{1,0:T(8,128)(2,1)}, u32[]{:S(2)}) copy-start(bf16[3584,512]{1,0:T(8,128)(2,1)} %shard_map.101) | copy-start | bytes 11010052
  25.5 5.4 %collective-permute-start.5 = (bf16[64,128]{1,0:T(8,128)(2,1)S(1)}, bf16[64,128]{1,0:T(8,128)(2,1)S(1)}, u32[]{:S(2)}, u32[]{:S(2)}) collective-permute-start(bf16[64,128]{1,0:T(8,128)(2,1)S(1)} %fusion.6), channel_id=1, source_target_pairs={{0,1},{1,0},{2,3},{3,2},{4,5},{5,4},{6,7},{7,6},{8,9},{9,8},{10,11... | collective-permute-start | bytes 49160 | tf_op jit(solution)/shard_map/ppermute | solution.py:35
  25.7 5.2 %collective-permute-start.6 = (bf16[64,128]{1,0:T(8,128)(2,1)S(1)}, bf16[64,128]{1,0:T(8,128)(2,1)S(1)}, u32[]{:S(2)}, u32[]{:S(2)}) collective-permute-start(bf16[64,128]{1,0:T(8,128)(2,1)S(1)} %fusion.6), channel_id=1, source_target_pairs={{0,2},{1,3},{2,0},{3,1},{4,6},{5,7},{6,4},{7,5},{8,10},{9,11},{10,... | collective-permute-start | bytes 49160 | tf_op jit(solution)/shard_map/ppermute | solution.py:35
  26.2 4.6 %collective-permute-start.7 = (bf16[64,128]{1,0:T(8,128)(2,1)S(1)}, bf16[64,128]{1,0:T(8,128)(2,1)S(1)}, u32[]{:S(2)}, u32[]{:S(2)}) collective-permute-start(bf16[64,128]{1,0:T(8,128)(2,1)S(1)} %fusion.6), channel_id=1, source_target_pairs={{0,3},{1,2},{2,1},{3,0},{4,7},{5,6},{6,5},{7,4},{8,11},{9,10},{10,... | collective-permute-start | bytes 49160 | tf_op jit(solution)/shard_map/ppermute | solution.py:35
  27.6 2.0 %copy-start.1 = (bf16[3584,512]{1,0:T(8,128)(2,1)S(1)}, bf16[3584,512]{1,0:T(8,128)(2,1)}, u32[]{:S(2)}) copy-start(bf16[3584,512]{1,0:T(8,128)(2,1)} %shard_map.100) | copy-start | bytes 11010052
  29.6 1.0 %copy-start.5 = (s32[16]{0:T(128)S(1)}, s32[16]{0:T(128)}, u32[]{:S(2)}) copy-start(s32[16]{0:T(128)} %param.13) | copy-start | bytes 196
  29.6 1.3 %copy-start.3 = (bf16[1,4,128,2,256]{4,3,2,1,0:T(2,128)(2,1)S(1)}, bf16[1,4,128,2,256]{4,3,2,1,0:T(2,128)(2,1)}, u32[]{:S(2)}) copy-start(bf16[1,4,128,2,256]{4,3,2,1,0:T(2,128)(2,1)} %param.17) | copy-start | bytes 1572868
  30.4 1.0 %copy-start.4 = (bf16[1,4,256,128]{3,2,1,0:T(8,128)(2,1)S(1)}, bf16[1,4,256,128]{3,2,1,0:T(8,128)(2,1)}, u32[]{:S(2)}) copy-start(bf16[1,4,256,128]{3,2,1,0:T(8,128)(2,1)} %param.18) | copy-start | bytes 786436
  31.6 5.0 %collective-permute-start.10 = (bf16[64,128]{1,0:T(8,128)(2,1)S(1)}, bf16[64,128]{1,0:T(8,128)(2,1)S(1)}, u32[]{:S(2)}, u32[]{:S(2)}) collective-permute-start(bf16[64,128]{1,0:T(8,128)(2,1)S(1)} %get-tuple-element.42), channel_id=1, source_target_pairs={{0,3},{1,2},{2,1},{3,0},{4,7},{5,6},{6,5},{7,4},{8,11},{9,10},{10,... | collective-permute-start | bytes 49160 | tf_op jit(solution)/shard_map/ppermute | solution.py:35
  32.2 4.4 %collective-permute-start.8 = (bf16[64,128]{1,0:T(8,128)(2,1)S(1)}, bf16[64,128]{1,0:T(8,128)(2,1)S(1)}, u32[]{:S(2)}, u32[]{:S(2)}) collective-permute-start(bf16[64,128]{1,0:T(8,128)(2,1)S(1)} %get-tuple-element.41), channel_id=1, source_target_pairs={{0,1},{1,0},{2,3},{3,2},{4,5},{5,4},{6,7},{7,6},{8,9},{9,8},{10,11... | collective-permute-start | bytes 49160 | tf_op jit(solution)/shard_map/ppermute | solution.py:35
  32.3 4.3 %collective-permute-start.9 = (bf16[64,128]{1,0:T(8,128)(2,1)S(1)}, bf16[64,128]{1,0:T(8,128)(2,1)S(1)}, u32[]{:S(2)}, u32[]{:S(2)}) collective-permute-start(bf16[64,128]{1,0:T(8,128)(2,1)S(1)} %get-tuple-element.43), channel_id=1, source_target_pairs={{0,2},{1,3},{2,0},{3,1},{4,6},{5,7},{6,4},{7,5},{8,10},{9,11},{10,... | collective-permute-start | bytes 49160 | tf_op jit(solution)/shard_map/ppermute | solution.py:35
  37.2 1.9 %collective-permute-start.11 = (bf16[32,7168]{1,0:T(8,128)(2,1)S(1)}, bf16[32,7168]{1,0:T(8,128)(2,1)S(1)}, u32[]{:S(2)}, u32[]{:S(2)}) collective-permute-start(bf16[32,7168]{1,0:T(8,128)(2,1)S(1)} %broadcast_select_fusion.2), channel_id=1, source_target_pairs={{0,1},{1,0},{2,3},{3,2},{4,5},{5,4},{6,7},{7,6},{8,9},{9,8},{10,11... | collective-permute-start | bytes 1376264 | tf_op jit(solution)/shard_map/ppermute | solution.py:35
  39.4 6.1 %collective-permute-start.12 = (bf16[16,7168]{1,0:T(8,128)(2,1)S(1)}, bf16[16,7168]{1,0:T(8,128)(2,1)S(1)}, u32[]{:S(2)}, u32[]{:S(2)}) collective-permute-start(bf16[16,7168]{1,0:T(8,128)(2,1)S(1)} %broadcast_select_fusion.5), channel_id=1, source_target_pairs={{0,4},{1,3},{2,6},{3,1},{4,0},{5,7},{6,2},{7,5},{8,12},{9,11},{10,... | collective-permute-start | bytes 688136 | tf_op jit(solution)/shard_map/ppermute | solution.py:35
  45.6 4.9 %collective-permute-start.13 = (bf16[8,7168]{1,0:T(8,128)(2,1)S(1)}, bf16[8,7168]{1,0:T(8,128)(2,1)S(1)}, u32[]{:S(2)}, u32[]{:S(2)}) collective-permute-start(bf16[8,7168]{1,0:T(8,128)(2,1)S(1)} %broadcast_select_fusion.12), channel_id=1, source_target_pairs={{0,2},{1,5},{2,0},{3,7},{4,6},{5,1},{6,4},{7,3},{8,10},{9,13},{10,... | collective-permute-start | bytes 344072 | tf_op jit(solution)/shard_map/ppermute | solution.py:35
  50.5 5.1 %collective-permute-start.14 = (bf16[4,7168]{1,0:T(4,128)(2,1)S(1)}, bf16[4,7168]{1,0:T(4,128)(2,1)S(1)}, u32[]{:S(2)}, u32[]{:S(2)}) collective-permute-start(bf16[4,7168]{1,0:T(4,128)(2,1)S(1)} %slice.121), channel_id=1, source_target_pairs={{0,8},{1,9},{2,10},{3,11},{4,12},{5,13},{6,14},{7,15},{8,0},{9,1},... | collective-permute-start | bytes 172040 | tf_op jit(solution)/shard_map/ppermute | solution.py:35

commit v9 on v4

--- a/solution.py
+++ b/solution.py
@@ -8,6 +8,10 @@
 
 VMEM = pl.BlockSpec(memory_space=pltpu.VMEM)
 HBM = pl.BlockSpec(memory_space=pltpu.HBM)
+
+
+def in_hbm(value):
+    return pltpu.with_memory_space_constraint(value, pltpu.HBM)
 
 
 def by_rows(value):
@@ -41,35 +45,38 @@
     return jnp.where(flip, second, first), jnp.where(flip, first, second)
 
 
-def code_kernel(x, table, out, weights, sems):
-    depth = weights.shape[0]
-    step = depth // sems.shape[0]
+def pack_kernel(tokens, routes, numerators, packed, routes_in, numerators_in, sems):
+    width, top = tokens.shape[1], routes.shape[1]
     copies = [
-        pltpu.make_async_copy(table.at[pl.ds(k, step)], weights.at[pl.ds(k, step)], sems.at[k // step])
-        for k in range(0, depth, step)
+        pltpu.make_async_copy(tokens, packed.at[:, pl.ds(0, width)], sems.at[0]),
+        pltpu.make_async_copy(routes, routes_in, sems.at[1]),
+        pltpu.make_async_copy(numerators, numerators_in, sems.at[2]),
     ]
     for copy in copies:
         copy.start()
-    total = jnp.zeros(out.shape, jnp.float32)
-    for k in range(0, depth, step):
-        copies[k // step].wait()
-        total += jnp.dot(x[:, k : k + step], weights[k : k + step, :], preferred_element_type=jnp.float32)
-    out[...] = total.astype(out.dtype)
-
-
-def code_product(x, table):
-    depth, rank = table.shape
+    packed[:, width:] = jnp.zeros((packed.shape[0], packed.shape[1] - width), packed.dtype)
+    for copy in copies[1:]:
+        copy.wait()
+    packed[:, width : width + top] = routes_in[...].astype(jnp.float32).astype(packed.dtype)
+    packed[:, width + top : width + 2 * top] = numerators_in[...].astype(jnp.float32).astype(packed.dtype)
+    copies[0].wait()
+
+
+def pack(tokens, routes, numerators):
+    count, width = tokens.shape
     return pl.pallas_call(
-        code_kernel,
-        out_shape=jax.ShapeDtypeStruct((x.shape[0], rank), jnp.bfloat16),
-        in_specs=[VMEM, HBM],
+        pack_kernel,
+        out_shape=jax.ShapeDtypeStruct((count, width + 128), tokens.dtype),
+        in_specs=[HBM] * 3,
         out_specs=VMEM,
-        scratch_shapes=[pltpu.VMEM(table.shape, table.dtype), pltpu.SemaphoreType.DMA((4,))],
-        compiler_params=pltpu.CompilerParams(vmem_limit_bytes=32 << 20),
-        cost_estimate=pl.CostEstimate(
-            flops=2 * x.shape[0] * depth * rank, bytes_accessed=2 * table.size, transcendentals=0
-        ),
-    )(x, table)
+        scratch_shapes=[
+            pltpu.VMEM(routes.shape, routes.dtype),
+            pltpu.VMEM(numerators.shape, numerators.dtype),
+            pltpu.SemaphoreType.DMA((3,)),
+        ],
+        compiler_params=pltpu.CompilerParams(vmem_limit_bytes=4 << 20),
+        cost_estimate=pl.CostEstimate(flops=0, bytes_accessed=4 * tokens.size, transcendentals=0),
+    )(in_hbm(tokens), in_hbm(routes), in_hbm(numerators))
 
 
 def gate_up_kernel(x, base, out, weights, sems):
@@ -81,22 +88,21 @@
     ]
     for copy in copies:
         copy.start()
-    row = lax.broadcasted_iota(jnp.int32, (128, 512), 0)
-    column = lax.broadcasted_iota(jnp.int32, (128, 512), 1)
-    target = 2 * row + jnp.where(column < 256, 0, 257)
-    spread = jnp.where(column == target, 1.0, 0.0).astype(jnp.bfloat16)
+    row = lax.broadcasted_iota(jnp.int32, (128, 256), 0)
+    column = lax.broadcasted_iota(jnp.int32, (128, 256), 1)
+    spread = jnp.where(column // 2 == row, 1.0, 0.0).astype(jnp.bfloat16)
+    is_odd = (lax.broadcasted_iota(jnp.int32, (1, 2 * step), 1) % 2).astype(jnp.float32)
+    odd_mask, even_mask = is_odd.astype(jnp.bfloat16), (1.0 - is_odd).astype(jnp.bfloat16)
+    count = x.shape[0]
     flat = weights.reshape(2 * depth, columns)
     total = jnp.zeros(out.shape, jnp.float32)
     for k in range(0, depth, step):
-        wide = [
-            jnp.dot(x[:, i : i + 128], spread, preferred_element_type=jnp.float32).astype(jnp.bfloat16)
-            for i in range(k, k + step, 128)
-        ]
-        even = jnp.concatenate([part[:, :256] for part in wide], axis=1)
-        odd = jnp.concatenate([part[:, 256:] for part in wide], axis=1)
+        stacked = jnp.concatenate([x[:, i : i + 128] for i in range(k, k + step, 128)])
+        wide = jnp.dot(stacked, spread, preferred_element_type=jnp.float32).astype(jnp.bfloat16)
+        wide = jnp.concatenate([wide[i : i + count] for i in range(0, stacked.shape[0], count)], axis=1)
         copies[k // step].wait()
         total += jnp.dot(
-            jnp.concatenate([even, odd]), flat[2 * k : 2 * (k + step), :], preferred_element_type=jnp.float32
+            jnp.concatenate([wide * even_mask, wide * odd_mask]), flat[2 * k : 2 * (k + step), :], preferred_element_type=jnp.float32
         )
     out[...] = total
 
@@ -113,7 +119,7 @@
         cost_estimate=pl.CostEstimate(
             flops=4 * x.shape[0] * depth * columns, bytes_accessed=2 * base.size, transcendentals=0
         ),
-    )(x, base)
+    )(x, in_hbm(base))
 
 
 def local(
@@ -139,21 +145,35 @@
     along, across = halves(clusters), halves(members // 2)
     shared, paired = along[: len(along) - len(across)], along[len(along) - len(across) :]
 
-    side = jnp.concatenate([routes[0], numerators[0]], axis=1).astype(jnp.bfloat16)
-    held = jnp.concatenate([tokens[0], jnp.pad(side, ((0, 0), (0, 128 - 2 * top)))], axis=1)
-
+    packed = pack(tokens[0], routes[0], numerators[0])
+    chips = members // 2
+    pieces = {(0, 0): packed}
+    for z in range(clusters - 1, 0, -1):
+        pieces[0, z] = trade(packed, (z, 0), (z, 0))
+    for x in range(1, chips):
+        pieces[x, 0] = trade(packed, (0, 2 * x), (0, 2 * x))
+    rest = jnp.concatenate([pieces[0, z] for z in range(1, clusters)])
+    for x in range(1, chips):
+        received = trade(rest, (0, 2 * x), (0, 2 * x))
+        for z in range(1, clusters):
+            pieces[x, z] = received[(z - 1) * count : z * count]
+
+    for bit in across:
+        for x in range(chips):
+            if not x & bit:
+                for z in range(clusters):
+                    flag = (me // (2 * bit)) % 2 == 1
+                    pieces[x, z], pieces[x | bit, z] = ordered(flag, pieces[x, z], pieces[x | bit, z])
+    places = [(0, 0)]
     for mask in shared:
-        held = jnp.concatenate([held, trade(held, (mask, 0), (mask, 0))])
-    for z, x in zip(paired, across):
-        size = held.shape[0]
-        flag = (me // (2 * x)) % 2 == 1
-        held = jnp.concatenate(ordered((core == 0) & flag, held, trade(held, (0, 2 * x), (z, 0))))
-        low, high = ordered((core == 1) & flag, held, trade(held, (z, 0), (0, 2 * x)))
-        inner = ordered(core == 1, low[size:], high[:size])
-        held = jnp.concatenate([low[:size], *inner, high[size:]])
+        places += [(x, z | mask) for x, z in places]
+    for zbit, xbit in zip(paired, across):
+        places += [(x | xbit, z) for x, z in places]
+        places += [(x, z | zbit) for x, z in places]
+    held = by_rows(jnp.concatenate([pieces[place] for place in places]))
     held = by_rows(jnp.concatenate(ordered(core == 1, held, trade(held, (0, 1), (0, 1)))))
 
-    codes = code_product(held, delta_in[0])
+    codes = jnp.dot(held[:, :width], delta_in[0], preferred_element_type=jnp.float32).astype(jnp.bfloat16)
     projected = gate_up_product(held, base_in[0])
 
     side = by_rows(held[:, width:])
@@ -189,7 +209,8 @@
     def add(kept, received):
         return (kept.astype(jnp.float32) + received.astype(jnp.float32)).astype(jnp.bfloat16)
 
-    kept, sent = ordered(core == 1, term[: total // 2], term[total // 2 :])
+    size = term.shape[0] // 2
+    kept, sent = ordered(core == 1, term[:size], term[size:])
     total = add(kept, trade(sent, (0, 1), (0, 1)))
     for z, x in reversed(list(zip(paired, across))):
         flag = (me // (2 * x)) % 2 == 1

time: 65.4 us -> 56.9 us (0.87)
  local copies, waits for them, and re-layouts: 4.86 us -> 0.87 us
  other arithmetic: 5.66 us -> 3.17 us
  waiting for transfers between devices: 30.8 us -> 28.4 us
  Pallas kernels: 6.89 us -> 6.07 us
  starting transfers between devices: 14.9 us -> 15.7 us
    unnamed x14 -> x12, local copies, waits for them, and re-layouts: 4.66 us -> 0.33 us
    ppermute x14 -> x16, waiting for transfers between devices: 30.8 us -> 28.4 us  [trade(): return lax.ppermute(value, ('expert', 'tensor'), pairs)]
    concatenate x5 -> x1, other arithmetic: 1.88 us -> 0.1 us  [local(): rest = jnp.concatenate([pieces[0, z] for z in range(1, clusters)])]
    convert_element_type x3, other arithmetic: 0.3 us -> 1.31 us  [add(): (kept.astype(jnp.float32) + received.astype(jnp.float32)).astype(jnp.bflo...]
    pallas_call x1, Pallas kernels: 1.91 us -> 0.98 us  [pack(): pl.pallas_call(pack_kernel, out_shape=jax.ShapeDtypeStruct((count, width...]
    select_n x8 -> x7, other arithmetic: 1.35 us -> 0.46 us  [ordered(): return (jnp.where(flip, second, first), jnp.where(flip, first, second))]
    ppermute x14 -> x16, starting transfers between devices: 14.9 us -> 15.7 us  [trade(): return lax.ppermute(value, ('expert', 'tensor'), pairs)]
    squeeze x1 -> x0, other arithmetic: 0.84 us -> none  [local(): numerators[0]]
  transfers between devices with their start and end apart: 14 -> 16, of which waited for: 10 -> 10; matrix products, arithmetic and copies ran while one was open for 2% -> 2% of each run, Pallas kernels for 8% -> 9%
where the time goes in v9:
time: 56.9 us; the launch traced here: 56.7 us
  waiting for transfers between devices  28.4 us (50%)
  starting transfers between devices  15.7 us (28%)
  Pallas kernels  6.07 us (11%)
  other arithmetic  3.17 us (6%)
  matrix products  2.11 us (4%)
  local copies, waits for them, and re-layouts  0.87 us (2%)
    ppermute x16, waiting for transfers between devices, trade(): return lax.ppermute(value, ('expert', 'tensor'), pairs)  28.4 us
    ppermute x16, starting transfers between devices, trade(): return lax.ppermute(value, ('expert', 'tensor'), pairs)  15.7 us
    pallas_call x1, Pallas kernels, gate_up_product(): pl.pallas_call(gate_up_kernel, out_shape=jax.ShapeDtypeStruct((2 * x.shap...  5.09 us
    convert_element_type x3, other arithmetic, add(): (kept.astype(jnp.float32) + received.astype(jnp.float32)).astype(jnp.bflo...  1.31 us
  transfers between devices with their start and end apart: 16, of which 10 were waited for; matrix products, arithmetic and copies ran while one was open for 2% of the time, Pallas kernels for 9%

profile of v9, /device:TPU:0, one launch (start us, length us, event | category | flops | bytes accessed | tf_op | source)
XLA Modules:
  0.0 56.7 jit_solution(3191823439670381529)
XLA Ops:
  0.0 1.0 %shard_map.100 = bf16[4,7296]{1,0:T(4,128)(2,1)S(1)} custom-call(bf16[4,7168]{1,0:T(4,128)(2,1)} %bitcast.64, s32[4,8]{1,0:T(4,128)} %bitcast.69, s32[4,8]{1,0:T(4,128)} %bitcast.70), custom_call_target="tpu_custom_call" | custom-call | bytes 114688 | tf_op jit(solution)/shard_map/pallas_call | solution.py:67
  1.0 5.1 %collective-permute-start.3 = (bf16[4,7296]{1,0:T(4,128)(2,1)S(1)}, bf16[4,7296]{1,0:T(4,128)(2,1)S(1)}, u32[]{:S(2)}, u32[]{:S(2)}) collective-permute-start(bf16[4,7296]{1,0:T(4,128)(2,1)S(1)} %shard_map.100), channel_id=1, source_target_pairs={{0,12},{1,13},{2,14},{3,15},{4,8},{5,9},{6,10},{7,11},{8,4},{9,5},... | collective-permute-start | bytes 175112 | tf_op jit(solution)/shard_map/ppermute | solution.py:33
  6.1 0.6 %collective-permute-start.1 = (bf16[4,7296]{1,0:T(4,128)(2,1)S(1)}, bf16[4,7296]{1,0:T(4,128)(2,1)S(1)}, u32[]{:S(2)}, u32[]{:S(2)}) collective-permute-start(bf16[4,7296]{1,0:T(4,128)(2,1)S(1)} %shard_map.100), channel_id=1, source_target_pairs={{0,4},{1,5},{2,6},{3,7},{4,0},{5,1},{6,2},{7,3},{8,12},{9,13},{10,... | collective-permute-start | bytes 175112 | tf_op jit(solution)/shard_map/ppermute | solution.py:33
  6.7 1.6 %collective-permute-start = (bf16[4,7296]{1,0:T(4,128)(2,1)S(1)}, bf16[4,7296]{1,0:T(4,128)(2,1)S(1)}, u32[]{:S(2)}, u32[]{:S(2)}) collective-permute-start(bf16[4,7296]{1,0:T(4,128)(2,1)S(1)} %shard_map.100), channel_id=1, source_target_pairs={{0,2},{1,3},{2,0},{3,1},{4,6},{5,7},{6,4},{7,5},{8,10},{9,11},{10,... | collective-permute-start | bytes 175112 | tf_op jit(solution)/shard_map/ppermute | solution.py:33
  8.4 0.1 collective-permute-done.3
  8.5 2.7 %collective-permute-done.2 = bf16[4,7296]{1,0:T(4,128)(2,1)S(1)} collective-permute-done((bf16[4,7296]{1,0:T(4,128)(2,1)S(1)}, bf16[4,7296]{1,0:T(4,128)(2,1)S(1)}, u32[]{:S(2)}, u32[]{:S(2)}) %collective-permute-start.2) | collective-permute-done | bytes 58400 | tf_op jit(solution)/shard_map/ppermute | solution.py:33
  11.2 0.1 pad_maximum_fusion.1
  11.3 1.6 %collective-permute-start.4 = (bf16[12,7296]{1,0:T(8,128)(2,1)S(1)}, bf16[12,7296]{1,0:T(8,128)(2,1)S(1)}, u32[]{:S(2)}, u32[]{:S(2)}) collective-permute-start(bf16[12,7296]{1,0:T(8,128)(2,1)S(1)} %pad_maximum_fusion.1), channel_id=1, source_target_pairs={{0,2},{1,3},{2,0},{3,1},{4,6},{5,7},{6,4},{7,5},{8,10},{9,11},{10,... | collective-permute-start | bytes 525320 | tf_op jit(solution)/shard_map/ppermute | solution.py:33
  13.0 5.1 %collective-permute-done.4 = bf16[12,7296]{1,0:T(8,128)(2,1)S(1)} collective-permute-done((bf16[12,7296]{1,0:T(8,128)(2,1)S(1)}, bf16[12,7296]{1,0:T(8,128)(2,1)S(1)}, u32[]{:S(2)}, u32[]{:S(2)}) %collective-permute-start.4) | collective-permute-done | bytes 175136 | tf_op jit(solution)/shard_map/ppermute | solution.py:33
  18.2 0.2 broadcast_select_fusion.7
  18.3 0.3 concatenate.16
  18.7 0.1 collective-permute-start.5
  18.8 1.8 %collective-permute-done.5 = bf16[32,7296]{1,0:T(8,128)(2,1)S(1)} collective-permute-done((bf16[32,7296]{1,0:T(8,128)(2,1)S(1)}, bf16[32,7296]{1,0:T(8,128)(2,1)S(1)}, u32[]{:S(2)}, u32[]{:S(2)}) %collective-permute-start.5) | collective-permute-done | bytes 466976 | tf_op jit(solution)/shard_map/ppermute | solution.py:33
  20.6 0.1 broadcast_select_fusion.1
  20.6 0.2 convert_reduce_fusion
  20.8 0.5 fusion.6
  21.3 1.4 %collective-permute-start.8 = (bf16[64,128]{1,0:T(8,128)(2,1)S(1)}, bf16[64,128]{1,0:T(8,128)(2,1)S(1)}, u32[]{:S(2)}, u32[]{:S(2)}) collective-permute-start(bf16[64,128]{1,0:T(8,128)(2,1)S(1)} %fusion.6), channel_id=1, source_target_pairs={{0,3},{1,2},{2,1},{3,0},{4,7},{5,6},{6,5},{7,4},{8,11},{9,10},{10,... | collective-permute-start | bytes 49160 | tf_op jit(solution)/shard_map/ppermute | solution.py:33
  22.7 0.5 collective-permute-start.7
  23.2 0.1 collective-permute-start.6
  23.2 0.1 pad_maximum_fusion.x
  23.3 0.1 fusion.34
  23.4 0.1 copy.18
  23.5 5.1 %shard_map.101 = f32[128,256]{1,0:T(8,128)S(1)} custom-call(bf16[64,7296]{1,0:T(8,128)(2,1)S(1)} %pad_maximum_fusion.x, bf16[7168,2,256]{2,1,0:T(2,128)(2,1)} %bitcast.62), custom_call_target="tpu_custom_call" | custom-call | flops 469762048 | bytes 7340032 | tf_op jit(solution)/shard_map/pallas_call | solution.py:112
  28.7 0.1 select_reduce_fusion
  28.8 0.1 select_reduce_fusion.1
  28.9 0.2 fusion.11
  29.2 0.1 multiply_reduce_fusion
  29.3 0.3 copy-done.3
  29.6 0.2 convolution_convert_fusion
  29.8 0.5 collective-permute-start.9
  30.3 1.3 %collective-permute-start.11 = (bf16[64,128]{1,0:T(8,128)(2,1)S(1)}, bf16[64,128]{1,0:T(8,128)(2,1)S(1)}, u32[]{:S(2)}, u32[]{:S(2)}) collective-permute-start(bf16[64,128]{1,0:T(8,128)(2,1)S(1)} %get-tuple-element.30), channel_id=1, source_target_pairs={{0,3},{1,2},{2,1},{3,0},{4,7},{5,6},{6,5},{7,4},{8,11},{9,10},{10,... | collective-permute-start | bytes 49160 | tf_op jit(solution)/shard_map/ppermute | solution.py:33
  31.5 0.4 collective-permute-start.10
  32.0 0.8 %fusion.1 = f32[64,7168]{1,0:T(8,128)S(1)} fusion(bf16[1,256,7168]{2,1,0:T(8,128)(2,1)S(1)} %copy-done.1, bf16[64,256]{1,0:T(8,128)(2,1)S(1)} %get-tuple-element.5), kind=kOutput, calls=%fused_computation.2 | convolution fusion | flops 234881024 | bytes 5537792 | tf_op jit(solution)/shard_map/dot_general | solution.py:206
  32.8 0.7 %collective-permute-done.11 = bf16[64,128]{1,0:T(8,128)(2,1)S(1)} collective-permute-done((bf16[64,128]{1,0:T(8,128)(2,1)S(1)}, bf16[64,128]{1,0:T(8,128)(2,1)S(1)}, u32[]{:S(2)}, u32[]{:S(2)}) %collective-permute-start.11) | collective-permute-done | bytes 16416 | tf_op jit(solution)/shard_map/ppermute | solution.py:33
  33.4 1.8 %collective-permute-done.10 = bf16[64,128]{1,0:T(8,128)(2,1)S(1)} collective-permute-done((bf16[64,128]{1,0:T(8,128)(2,1)S(1)}, bf16[64,128]{1,0:T(8,128)(2,1)S(1)}, u32[]{:S(2)}, u32[]{:S(2)}) %collective-permute-start.10) | collective-permute-done | bytes 16416 | tf_op jit(solution)/shard_map/ppermute | solution.py:33
  35.3 0.5 fusion
  35.9 0.1 collective-permute-start.12
  35.9 1.9 %collective-permute-done.12 = bf16[32,7168]{1,0:T(8,128)(2,1)} collective-permute-done((bf16[32,7168]{1,0:T(8,128)(2,1)S(1)}, bf16[32,7168]{1,0:T(8,128)(2,1)}, u32[]{:S(2)}, u32[]{:S(2)}) %collective-permute-start.12) | collective-permute-done | bytes 458784 | tf_op jit(solution)/shard_map/ppermute | solution.py:33
  37.9 1.2 %add_convert_fusion = bf16[32,7168]{1,0:T(8,128)(2,1)S(1)} fusion(bf16[32,7168]{1,0:T(8,128)(2,1)} %collective-permute-done.12, pred[]{:T(512)S(6)} %eq.51, bf16[64,7168]{1,0:T(8,128)(2,1)S(1)} %fusion), kind=kLoop, calls=%fused_computation.17 | loop fusion | flops 1146880 | bytes 1835009 | tf_op jit(solution)/shard_map/convert_element_type | solution.py:210
  39.1 0.1 broadcast_select_fusion.3
  39.2 0.6 %collective-permute-start.13 = (bf16[16,7168]{1,0:T(8,128)(2,1)S(1)}, bf16[16,7168]{1,0:T(8,128)(2,1)S(1)}, u32[]{:S(2)}, u32[]{:S(2)}) collective-permute-start(bf16[16,7168]{1,0:T(8,128)(2,1)S(1)} %broadcast_select_fusion.3), channel_id=1, source_target_pairs={{0,4},{1,3},{2,6},{3,1},{4,0},{5,7},{6,2},{7,5},{8,12},{9,11},{10,... | collective-permute-start | bytes 688136 | tf_op jit(solution)/shard_map/ppermute | solution.py:33
  39.8 5.5 %collective-permute-done.13 = bf16[16,7168]{1,0:T(8,128)(2,1)S(1)} collective-permute-done((bf16[16,7168]{1,0:T(8,128)(2,1)S(1)}, bf16[16,7168]{1,0:T(8,128)(2,1)S(1)}, u32[]{:S(2)}, u32[]{:S(2)}) %collective-permute-start.13) | collective-permute-done | bytes 229408 | tf_op jit(solution)/shard_map/ppermute | solution.py:33
  45.3 0.1 add_convert_fusion.1
  45.4 0.5 collective-permute-start.14
  45.9 4.3 %collective-permute-done.14 = bf16[8,7168]{1,0:T(8,128)(2,1)S(1)} collective-permute-done((bf16[8,7168]{1,0:T(8,128)(2,1)S(1)}, bf16[8,7168]{1,0:T(8,128)(2,1)S(1)}, u32[]{:S(2)}, u32[]{:S(2)}) %collective-permute-start.14) | collective-permute-done | bytes 114720 | tf_op jit(solution)/shard_map/ppermute | solution.py:33
  50.3 1.3 %collective-permute-start.15 = (bf16[4,7168]{1,0:T(4,128)(2,1)S(1)}, bf16[4,7168]{1,0:T(4,128)(2,1)S(1)}, u32[]{:S(2)}, u32[]{:S(2)}) collective-permute-start(bf16[4,7168]{1,0:T(4,128)(2,1)S(1)} %slice.108), channel_id=1, source_target_pairs={{0,8},{1,9},{2,10},{3,11},{4,12},{5,13},{6,14},{7,15},{8,0},{9,1},... | collective-permute-start | bytes 172040 | tf_op jit(solution)/shard_map/ppermute | solution.py:33
  51.6 4.5 %collective-permute-done.15 = bf16[4,7168]{1,0:T(4,128)(2,1)S(1)} collective-permute-done((bf16[4,7168]{1,0:T(4,128)(2,1)S(1)}, bf16[4,7168]{1,0:T(4,128)(2,1)S(1)}, u32[]{:S(2)}, u32[]{:S(2)}) %collective-permute-start.15) | collective-permute-done | bytes 57376 | tf_op jit(solution)/shard_map/ppermute | solution.py:33
  56.1 0.7 %fusion.24 = bf16[1,4,7168]{2,1,0:T(4,128)(2,1)} fusion(bf16[4,7168]{1,0:T(4,128)(2,1)S(1)} %collective-permute-done.15, bf16[8,7168]{1,0:T(8,128)(2,1)S(1)} %add_convert_fusion.2), kind=kLoop, calls=%fused_computation.59 | loop fusion | flops 114688 | bytes 172032 | tf_op jit(solution)/shard_map/broadcast_in_dim | solution.py:231
  (32 shorter events, 0.4 us)
Async XLA Ops:
  0.0 35.3 %copy-start = (bf16[1,128,7168]{2,1,0:T(8,128)(2,1)S(1)}, bf16[1,128,7168]{2,1,0:T(8,128)(2,1)}, u32[]{:S(2)}) copy-start(bf16[1,128,7168]{2,1,0:T(8,128)(2,1)} %param.19) | copy-start | bytes 5505028
  1.0 7.5 %collective-permute-start.3 = (bf16[4,7296]{1,0:T(4,128)(2,1)S(1)}, bf16[4,7296]{1,0:T(4,128)(2,1)S(1)}, u32[]{:S(2)}, u32[]{:S(2)}) collective-permute-start(bf16[4,7296]{1,0:T(4,128)(2,1)S(1)} %shard_map.100), channel_id=1, source_target_pairs={{0,12},{1,13},{2,14},{3,15},{4,8},{5,9},{6,10},{7,11},{8,4},{9,5},... | collective-permute-start | bytes 175112 | tf_op jit(solution)/shard_map/ppermute | solution.py:33
  6.1 5.1 %collective-permute-start.2 = (bf16[4,7296]{1,0:T(4,128)(2,1)S(1)}, bf16[4,7296]{1,0:T(4,128)(2,1)S(1)}, u32[]{:S(2)}, u32[]{:S(2)}) collective-permute-start(bf16[4,7296]{1,0:T(4,128)(2,1)S(1)} %shard_map.100), channel_id=1, source_target_pairs={{0,8},{1,9},{2,10},{3,11},{4,12},{5,13},{6,14},{7,15},{8,0},{9,1},... | collective-permute-start | bytes 175112 | tf_op jit(solution)/shard_map/ppermute | solution.py:33
  6.1 5.1 %collective-permute-start.1 = (bf16[4,7296]{1,0:T(4,128)(2,1)S(1)}, bf16[4,7296]{1,0:T(4,128)(2,1)S(1)}, u32[]{:S(2)}, u32[]{:S(2)}) collective-permute-start(bf16[4,7296]{1,0:T(4,128)(2,1)S(1)} %shard_map.100), channel_id=1, source_target_pairs={{0,4},{1,5},{2,6},{3,7},{4,0},{5,1},{6,2},{7,3},{8,12},{9,13},{10,... | collective-permute-start | bytes 175112 | tf_op jit(solution)/shard_map/ppermute | solution.py:33
  6.7 6.2 %collective-permute-start = (bf16[4,7296]{1,0:T(4,128)(2,1)S(1)}, bf16[4,7296]{1,0:T(4,128)(2,1)S(1)}, u32[]{:S(2)}, u32[]{:S(2)}) collective-permute-start(bf16[4,7296]{1,0:T(4,128)(2,1)S(1)} %shard_map.100), channel_id=1, source_target_pairs={{0,2},{1,3},{2,0},{3,1},{4,6},{5,7},{6,4},{7,5},{8,10},{9,11},{10,... | collective-permute-start | bytes 175112 | tf_op jit(solution)/shard_map/ppermute | solution.py:33
  11.3 6.8 %collective-permute-start.4 = (bf16[12,7296]{1,0:T(8,128)(2,1)S(1)}, bf16[12,7296]{1,0:T(8,128)(2,1)S(1)}, u32[]{:S(2)}, u32[]{:S(2)}) collective-permute-start(bf16[12,7296]{1,0:T(8,128)(2,1)S(1)} %pad_maximum_fusion.1), channel_id=1, source_target_pairs={{0,2},{1,3},{2,0},{3,1},{4,6},{5,7},{6,4},{7,5},{8,10},{9,11},{10,... | collective-permute-start | bytes 525320 | tf_op jit(solution)/shard_map/ppermute | solution.py:33
  18.7 1.9 %collective-permute-start.5 = (bf16[32,7296]{1,0:T(8,128)(2,1)S(1)}, bf16[32,7296]{1,0:T(8,128)(2,1)S(1)}, u32[]{:S(2)}, u32[]{:S(2)}) collective-permute-start(bf16[32,7296]{1,0:T(8,128)(2,1)S(1)} %concatenate.16), channel_id=1, source_target_pairs={{0,1},{1,0},{2,3},{3,2},{4,5},{5,4},{6,7},{7,6},{8,9},{9,8},{10,11... | collective-permute-start | bytes 1400840 | tf_op jit(solution)/shard_map/ppermute | solution.py:33
  18.8 2.0 %copy-start.5 = (bf16[1,7168,128]{2,1,0:T(8,128)(2,1)S(1)}, bf16[1,7168,128]{2,1,0:T(8,128)(2,1)}, u32[]{:S(2)}) copy-start(bf16[1,7168,128]{2,1,0:T(8,128)(2,1)} %param.16) | copy-start | bytes 5505028
  21.3 7.5 %collective-permute-start.8 = (bf16[64,128]{1,0:T(8,128)(2,1)S(1)}, bf16[64,128]{1,0:T(8,128)(2,1)S(1)}, u32[]{:S(2)}, u32[]{:S(2)}) collective-permute-start(bf16[64,128]{1,0:T(8,128)(2,1)S(1)} %fusion.6), channel_id=1, source_target_pairs={{0,3},{1,2},{2,1},{3,0},{4,7},{5,6},{6,5},{7,4},{8,11},{9,10},{10,... | collective-permute-start | bytes 49160 | tf_op jit(solution)/shard_map/ppermute | solution.py:33
  22.7 6.2 %collective-permute-start.7 = (bf16[64,128]{1,0:T(8,128)(2,1)S(1)}, bf16[64,128]{1,0:T(8,128)(2,1)S(1)}, u32[]{:S(2)}, u32[]{:S(2)}) collective-permute-start(bf16[64,128]{1,0:T(8,128)(2,1)S(1)} %fusion.6), channel_id=1, source_target_pairs={{0,2},{1,3},{2,0},{3,1},{4,6},{5,7},{6,4},{7,5},{8,10},{9,11},{10,... | collective-permute-start | bytes 49160 | tf_op jit(solution)/shard_map/ppermute | solution.py:33
  23.2 5.7 %collective-permute-start.6 = (bf16[64,128]{1,0:T(8,128)(2,1)S(1)}, bf16[64,128]{1,0:T(8,128)(2,1)S(1)}, u32[]{:S(2)}, u32[]{:S(2)}) collective-permute-start(bf16[64,128]{1,0:T(8,128)(2,1)S(1)} %fusion.6), channel_id=1, source_target_pairs={{0,1},{1,0},{2,3},{3,2},{4,5},{5,4},{6,7},{7,6},{8,9},{9,8},{10,11... | collective-permute-start | bytes 49160 | tf_op jit(solution)/shard_map/ppermute | solution.py:33
  23.5 5.1 %copy-start.4 = (s32[16]{0:T(128)S(1)}, s32[16]{0:T(128)}, u32[]{:S(2)}) copy-start(s32[16]{0:T(128)} %param.13) | copy-start | bytes 196
  23.5 5.4 %copy-start.2 = (bf16[1,4,128,2,256]{4,3,2,1,0:T(2,128)(2,1)S(1)}, bf16[1,4,128,2,256]{4,3,2,1,0:T(2,128)(2,1)}, u32[]{:S(2)}) copy-start(bf16[1,4,128,2,256]{4,3,2,1,0:T(2,128)(2,1)} %param.17) | copy-start | bytes 1572868
  23.5 8.5 %copy-start.1 = (bf16[1,256,7168]{2,1,0:T(8,128)(2,1)S(1)}, bf16[1,256,7168]{2,1,0:T(8,128)(2,1)}, u32[]{:S(2)}) copy-start(bf16[1,256,7168]{2,1,0:T(8,128)(2,1)} %param.15) | copy-start | bytes 11010052
  28.6 1.0 %copy-start.3 = (bf16[1,4,256,128]{3,2,1,0:T(8,128)(2,1)S(1)}, bf16[1,4,256,128]{3,2,1,0:T(8,128)(2,1)}, u32[]{:S(2)}) copy-start(bf16[1,4,256,128]{3,2,1,0:T(8,128)(2,1)} %param.18) | copy-start | bytes 786436
  29.8 3.0 %collective-permute-start.9 = (bf16[64,128]{1,0:T(8,128)(2,1)S(1)}, bf16[64,128]{1,0:T(8,128)(2,1)S(1)}, u32[]{:S(2)}, u32[]{:S(2)}) collective-permute-start(bf16[64,128]{1,0:T(8,128)(2,1)S(1)} %get-tuple-element.29), channel_id=1, source_target_pairs={{0,1},{1,0},{2,3},{3,2},{4,5},{5,4},{6,7},{7,6},{8,9},{9,8},{10,11... | collective-permute-start | bytes 49160 | tf_op jit(solution)/shard_map/ppermute | solution.py:33
  30.3 3.2 %collective-permute-start.11 = (bf16[64,128]{1,0:T(8,128)(2,1)S(1)}, bf16[64,128]{1,0:T(8,128)(2,1)S(1)}, u32[]{:S(2)}, u32[]{:S(2)}) collective-permute-start(bf16[64,128]{1,0:T(8,128)(2,1)S(1)} %get-tuple-element.30), channel_id=1, source_target_pairs={{0,3},{1,2},{2,1},{3,0},{4,7},{5,6},{6,5},{7,4},{8,11},{9,10},{10,... | collective-permute-start | bytes 49160 | tf_op jit(solution)/shard_map/ppermute | solution.py:33
  31.5 3.7 %collective-permute-start.10 = (bf16[64,128]{1,0:T(8,128)(2,1)S(1)}, bf16[64,128]{1,0:T(8,128)(2,1)S(1)}, u32[]{:S(2)}, u32[]{:S(2)}) collective-permute-start(bf16[64,128]{1,0:T(8,128)(2,1)S(1)} %get-tuple-element.31), channel_id=1, source_target_pairs={{0,2},{1,3},{2,0},{3,1},{4,6},{5,7},{6,4},{7,5},{8,10},{9,11},{10,... | collective-permute-start | bytes 49160 | tf_op jit(solution)/shard_map/ppermute | solution.py:33
  35.9 2.0 %collective-permute-start.12 = (bf16[32,7168]{1,0:T(8,128)(2,1)S(1)}, bf16[32,7168]{1,0:T(8,128)(2,1)}, u32[]{:S(2)}, u32[]{:S(2)}) collective-permute-start(bf16[32,7168]{1,0:T(8,128)(2,1)S(1)} %broadcast_select_fusion.2), channel_id=1, source_target_pairs={{0,1},{1,0},{2,3},{3,2},{4,5},{5,4},{6,7},{7,6},{8,9},{9,8},{10,11... | collective-permute-start | bytes 1376264 | tf_op jit(solution)/shard_map/ppermute | solution.py:33
  39.2 6.1 %collective-permute-start.13 = (bf16[16,7168]{1,0:T(8,128)(2,1)S(1)}, bf16[16,7168]{1,0:T(8,128)(2,1)S(1)}, u32[]{:S(2)}, u32[]{:S(2)}) collective-permute-start(bf16[16,7168]{1,0:T(8,128)(2,1)S(1)} %broadcast_select_fusion.3), channel_id=1, source_target_pairs={{0,4},{1,3},{2,6},{3,1},{4,0},{5,7},{6,2},{7,5},{8,12},{9,11},{10,... | collective-permute-start | bytes 688136 | tf_op jit(solution)/shard_map/ppermute | solution.py:33
  45.4 4.9 %collective-permute-start.14 = (bf16[8,7168]{1,0:T(8,128)(2,1)S(1)}, bf16[8,7168]{1,0:T(8,128)(2,1)S(1)}, u32[]{:S(2)}, u32[]{:S(2)}) collective-permute-start(bf16[8,7168]{1,0:T(8,128)(2,1)S(1)} %broadcast_select_fusion.6), channel_id=1, source_target_pairs={{0,2},{1,5},{2,0},{3,7},{4,6},{5,1},{6,4},{7,3},{8,10},{9,13},{10,... | collective-permute-start | bytes 344072 | tf_op jit(solution)/shard_map/ppermute | solution.py:33
  50.3 5.8 %collective-permute-start.15 = (bf16[4,7168]{1,0:T(4,128)(2,1)S(1)}, bf16[4,7168]{1,0:T(4,128)(2,1)S(1)}, u32[]{:S(2)}, u32[]{:S(2)}) collective-permute-start(bf16[4,7168]{1,0:T(4,128)(2,1)S(1)} %slice.108), channel_id=1, source_target_pairs={{0,8},{1,9},{2,10},{3,11},{4,12},{5,13},{6,14},{7,15},{8,0},{9,1},... | collective-permute-start | bytes 172040 | tf_op jit(solution)/shard_map/ppermute | solution.py:33

commit v10 on v9

--- a/solution.py
+++ b/solution.py
@@ -88,21 +88,24 @@
     ]
     for copy in copies:
         copy.start()
-    row = lax.broadcasted_iota(jnp.int32, (128, 256), 0)
-    column = lax.broadcasted_iota(jnp.int32, (128, 256), 1)
+    row = lax.broadcasted_iota(jnp.int32, (256, 512), 0)
+    column = lax.broadcasted_iota(jnp.int32, (256, 512), 1)
     spread = jnp.where(column // 2 == row, 1.0, 0.0).astype(jnp.bfloat16)
-    is_odd = (lax.broadcasted_iota(jnp.int32, (1, 2 * step), 1) % 2).astype(jnp.float32)
-    odd_mask, even_mask = is_odd.astype(jnp.bfloat16), (1.0 - is_odd).astype(jnp.bfloat16)
-    count = x.shape[0]
+    is_up = (lax.broadcasted_iota(jnp.int32, (2 * step, columns), 0) % 2).astype(jnp.float32)
+    gate_rows, up_rows = (1.0 - is_up).astype(jnp.bfloat16), is_up.astype(jnp.bfloat16)
     flat = weights.reshape(2 * depth, columns)
     total = jnp.zeros(out.shape, jnp.float32)
     for k in range(0, depth, step):
-        stacked = jnp.concatenate([x[:, i : i + 128] for i in range(k, k + step, 128)])
-        wide = jnp.dot(stacked, spread, preferred_element_type=jnp.float32).astype(jnp.bfloat16)
-        wide = jnp.concatenate([wide[i : i + count] for i in range(0, stacked.shape[0], count)], axis=1)
+        wide = [
+            jnp.dot(x[:, i : i + 256], spread, preferred_element_type=jnp.float32).astype(jnp.bfloat16)
+            for i in range(k, k + step, 256)
+        ]
         copies[k // step].wait()
+        table = flat[2 * k : 2 * (k + step), :]
         total += jnp.dot(
-            jnp.concatenate([wide * even_mask, wide * odd_mask]), flat[2 * k : 2 * (k + step), :], preferred_element_type=jnp.float32
+            jnp.concatenate(wide, axis=1),
+            jnp.concatenate([table * gate_rows, table * up_rows], axis=1),
+            preferred_element_type=jnp.float32,
         )
     out[...] = total
 
@@ -111,7 +114,7 @@
     depth, _, columns = base.shape
     return pl.pallas_call(
         gate_up_kernel,
-        out_shape=jax.ShapeDtypeStruct((2 * x.shape[0], columns), jnp.float32),
+        out_shape=jax.ShapeDtypeStruct((x.shape[0], 2 * columns), jnp.float32),
         in_specs=[VMEM, HBM],
         out_specs=VMEM,
         scratch_shapes=[pltpu.VMEM(base.shape, base.dtype), pltpu.SemaphoreType.DMA((depth // 512,))],
@@ -145,6 +148,8 @@
     along, across = halves(clusters), halves(members // 2)
     shared, paired = along[: len(along) - len(across)], along[len(along) - len(across) :]
 
+    other_back = trade(delta_back[0], (0, 1), (0, 1))
+
     packed = pack(tokens[0], routes[0], numerators[0])
     chips = members // 2
     pieces = {(0, 0): packed}
@@ -171,9 +176,14 @@
         places += [(x | xbit, z) for x, z in places]
         places += [(x, z | zbit) for x, z in places]
     held = by_rows(jnp.concatenate([pieces[place] for place in places]))
+    held, other_back = lax.optimization_barrier((held, other_back))
+    half = held.shape[0]
     held = by_rows(jnp.concatenate(ordered(core == 1, held, trade(held, (0, 1), (0, 1)))))
 
     codes = jnp.dot(held[:, :width], delta_in[0], preferred_element_type=jnp.float32).astype(jnp.bfloat16)
+    rank = codes.shape[1]
+    codes = jnp.stack([codes if m == 0 else trade(codes, (0, m), (0, m)) for m in range(members)])
+    by_slot = jnp.stack([lax.dynamic_index_in_dim(codes, s ^ me, 0, keepdims=False) for s in range(members)])
     projected = gate_up_product(held, base_in[0])
 
     side = by_rows(held[:, width:])
@@ -186,32 +196,36 @@
         jnp.where(position[None] == target[:, None, None], weight[None].astype(jnp.float32), 0.0), axis=-1
     )
 
-    codes = jnp.stack([codes if m == 0 else trade(codes, (0, m), (0, m)) for m in range(members)])
-    by_slot = jnp.stack([lax.dynamic_index_in_dim(codes, s ^ me, 0, keepdims=False) for s in range(members)])
-
     lifted = jnp.einsum("srk,skgf->srgf", by_slot, delta_mid[0], preferred_element_type=jnp.float32)
-    total = held.shape[0]
-    hidden = jax.nn.silu(projected[None, :total] + lifted[:, :, 0]) * (projected[None, total:] + lifted[:, :, 1])
+    part = projected.shape[1] // 2
+    hidden = jax.nn.silu(projected[None, :, :part] + lifted[:, :, 0]) * (
+        projected[None, :, part:] + lifted[:, :, 1]
+    )
     hidden_sum = jnp.sum(scale[:, :, None] * hidden, axis=0).astype(jnp.bfloat16)
     partial_codes = jnp.einsum(
         "srf,sfk->srk", hidden.astype(jnp.bfloat16), delta_down[0], preferred_element_type=jnp.float32
     ).astype(jnp.bfloat16)
+    partial_codes = partial_codes.reshape(chips, 2, 2, half, rank).transpose(0, 2, 1, 3, 4)
+    partial_codes = partial_codes.reshape(members, 2, half, rank)
     lowrank = lax.dynamic_index_in_dim(partial_codes, me, 0, keepdims=False).astype(jnp.float32)
     for m in range(1, members):
         sent = lax.dynamic_index_in_dim(partial_codes, me ^ m, 0, keepdims=False)
         lowrank = lowrank + trade(sent, (0, m), (0, m)).astype(jnp.float32)
-    own_scale = lax.dynamic_index_in_dim(scale, me, 0, keepdims=False)
-    scaled = (own_scale[:, None] * lowrank).astype(jnp.bfloat16)
-
-    term = jnp.dot(hidden_sum, base_down[0], preferred_element_type=jnp.float32)
-    term = (term + jnp.dot(scaled, delta_back[0], preferred_element_type=jnp.float32)).astype(jnp.bfloat16)
+    kept_scale = scale.reshape(chips, 2, 2, half).transpose(0, 2, 1, 3).reshape(members, 2, half)
+    kept_scale = lax.dynamic_index_in_dim(kept_scale, me, 0, keepdims=False)
+    scaled = (kept_scale[:, :, None] * lowrank).astype(jnp.bfloat16)
+    scaled = ordered(core == 1, scaled[0], scaled[1])
+
+    base = jnp.dot(hidden_sum, base_down[0], preferred_element_type=jnp.float32)
+    kept, sent = ordered(core == 1, base[:half], base[half:])
+    total = kept + trade(sent.astype(jnp.bfloat16), (0, 1), (0, 1)).astype(jnp.float32)
+    for rows, table in zip(scaled, (delta_back[0], other_back)):
+        total = total + jnp.dot(rows, table, preferred_element_type=jnp.float32)
+    total = total.astype(jnp.bfloat16)
 
     def add(kept, received):
         return (kept.astype(jnp.float32) + received.astype(jnp.float32)).astype(jnp.bfloat16)
 
-    size = term.shape[0] // 2
-    kept, sent = ordered(core == 1, term[:size], term[size:])
-    total = add(kept, trade(sent, (0, 1), (0, 1)))
     for z, x in reversed(list(zip(paired, across))):
         flag = (me // (2 * x)) % 2 == 1
         size = total.shape[0] // 4

time: 56.9 us -> 63.3 us (1.11)
  Pallas kernels: 6.07 us -> 12.5 us
  matrix products: 2.11 us -> 6.16 us
  waiting for transfers between devices: 28.4 us -> 24.4 us
  starting transfers between devices: 15.7 us -> 16.9 us
  other arithmetic: 3.17 us -> 2.12 us
    pallas_call x1, Pallas kernels: 5.09 us -> 11.5 us  [gate_up_product(): pl.pallas_call(gate_up_kernel, out_shape=jax.ShapeDtypeStruct((x.shape[0]...]
    dot_general x2 -> x3, matrix products: 1.25 us -> 5.29 us  [the longest x1 2.92 us: local(): base = jnp.dot(hidden_sum, base_down[0], preferred_element_type=jnp.float32)]
    ppermute x16 -> x17, waiting for transfers between devices: 28.4 us -> 24.4 us  [trade(): return lax.ppermute(value, ('expert', 'tensor'), pairs)]
    convert_element_type x3 -> x2, other arithmetic: 1.31 us -> 0.13 us  [add(): (kept.astype(jnp.float32) + received.astype(jnp.float32)).astype(jnp.bflo...]
    ppermute x16 -> x17, starting transfers between devices: 15.7 us -> 16.9 us  [trade(): return lax.ppermute(value, ('expert', 'tensor'), pairs)]
  transfers between devices with their start and end apart: 16 -> 17, of which waited for: 10 -> 8; matrix products, arithmetic and copies ran while one was open for 2% -> 8% of each run, Pallas kernels for 9% -> 18%
where the time goes in v10:
time: 63.3 us; the launch traced here: 63.1 us
  waiting for transfers between devices  24.4 us (39%)
  starting transfers between devices  16.9 us (27%)
  Pallas kernels  12.5 us (20%)
  matrix products  6.16 us (10%)
  other arithmetic  2.12 us (3%)
  local copies, waits for them, and re-layouts  0.66 us (1%)
    ppermute x17, waiting for transfers between devices, trade(): return lax.ppermute(value, ('expert', 'tensor'), pairs)  24.4 us
    ppermute x17, starting transfers between devices, trade(): return lax.ppermute(value, ('expert', 'tensor'), pairs)  16.9 us
    pallas_call x1, Pallas kernels, gate_up_product(): pl.pallas_call(gate_up_kernel, out_shape=jax.ShapeDtypeStruct((x.shape[0]...  11.5 us
    dot_general x1, matrix products, local(): base = jnp.dot(hidden_sum, base_down[0], preferred_element_type=jnp.float32)  2.92 us
    dot_general x2, matrix products, local(): total = total + jnp.dot(rows, table, preferred_element_type=jnp.float32)  2.37 us
  transfers between devices with their start and end apart: 17, of which 8 were waited for; matrix products, arithmetic and copies ran while one was open for 8% of the time, Pallas kernels for 18%

profile of v10, /device:TPU:0, one launch (start us, length us, event | category | flops | bytes accessed | tf_op | source)
XLA Modules:
  0.0 63.1 jit_solution(17237867035217309889)
XLA Ops:
  0.0 1.0 %shard_map.100 = bf16[4,7296]{1,0:T(4,128)(2,1)S(1)} custom-call(bf16[4,7168]{1,0:T(4,128)(2,1)} %bitcast.80, s32[4,8]{1,0:T(4,128)} %bitcast.87, s32[4,8]{1,0:T(4,128)} %bitcast.88), custom_call_target="tpu_custom_call" | custom-call | bytes 114688 | tf_op jit(solution)/shard_map/pallas_call | solution.py:67
  1.0 3.1 %collective-permute-start.1 = (bf16[4,7296]{1,0:T(4,128)(2,1)S(1)}, bf16[4,7296]{1,0:T(4,128)(2,1)S(1)}, u32[]{:S(2)}, u32[]{:S(2)}) collective-permute-start(bf16[4,7296]{1,0:T(4,128)(2,1)S(1)} %shard_map.100), channel_id=1, source_target_pairs={{0,4},{1,5},{2,6},{3,7},{4,0},{5,1},{6,2},{7,3},{8,12},{9,13},{10,... | collective-permute-start | bytes 175112 | tf_op jit(solution)/shard_map/ppermute | solution.py:33
  4.1 2.6 %collective-permute-start.2 = (bf16[4,7296]{1,0:T(4,128)(2,1)S(1)}, bf16[4,7296]{1,0:T(4,128)(2,1)S(1)}, u32[]{:S(2)}, u32[]{:S(2)}) collective-permute-start(bf16[4,7296]{1,0:T(4,128)(2,1)S(1)} %shard_map.100), channel_id=1, source_target_pairs={{0,8},{1,9},{2,10},{3,11},{4,12},{5,13},{6,14},{7,15},{8,0},{9,1},... | collective-permute-start | bytes 175112 | tf_op jit(solution)/shard_map/ppermute | solution.py:33
  6.7 1.7 %collective-permute-start = (bf16[4,7296]{1,0:T(4,128)(2,1)S(1)}, bf16[4,7296]{1,0:T(4,128)(2,1)S(1)}, u32[]{:S(2)}, u32[]{:S(2)}) collective-permute-start(bf16[4,7296]{1,0:T(4,128)(2,1)S(1)} %shard_map.100), channel_id=1, source_target_pairs={{0,2},{1,3},{2,0},{3,1},{4,6},{5,7},{6,4},{7,5},{8,10},{9,11},{10,... | collective-permute-start | bytes 175112 | tf_op jit(solution)/shard_map/ppermute | solution.py:33
  8.4 1.9 %collective-permute-done.2 = bf16[4,7296]{1,0:T(4,128)(2,1)S(1)} collective-permute-done((bf16[4,7296]{1,0:T(4,128)(2,1)S(1)}, bf16[4,7296]{1,0:T(4,128)(2,1)S(1)}, u32[]{:S(2)}, u32[]{:S(2)}) %collective-permute-start.2) | collective-permute-done | bytes 58400 | tf_op jit(solution)/shard_map/ppermute | solution.py:33
  10.3 2.4 %collective-permute-done.3 = bf16[4,7296]{1,0:T(4,128)(2,1)S(1)} collective-permute-done((bf16[4,7296]{1,0:T(4,128)(2,1)S(1)}, bf16[4,7296]{1,0:T(4,128)(2,1)S(1)}, u32[]{:S(2)}, u32[]{:S(2)}) %collective-permute-start.3) | collective-permute-done | bytes 58400 | tf_op jit(solution)/shard_map/ppermute | solution.py:33
  12.7 0.1 pad_maximum_fusion.1
  12.8 1.6 %collective-permute-start.4 = (bf16[12,7296]{1,0:T(8,128)(2,1)S(1)}, bf16[12,7296]{1,0:T(8,128)(2,1)S(1)}, u32[]{:S(2)}, u32[]{:S(2)}) collective-permute-start(bf16[12,7296]{1,0:T(8,128)(2,1)S(1)} %pad_maximum_fusion.1), channel_id=1, source_target_pairs={{0,2},{1,3},{2,0},{3,1},{4,6},{5,7},{6,4},{7,5},{8,10},{9,11},{10,... | collective-permute-start | bytes 525320 | tf_op jit(solution)/shard_map/ppermute | solution.py:33
  14.4 4.5 %collective-permute-done.4 = bf16[12,7296]{1,0:T(8,128)(2,1)S(1)} collective-permute-done((bf16[12,7296]{1,0:T(8,128)(2,1)S(1)}, bf16[12,7296]{1,0:T(8,128)(2,1)S(1)}, u32[]{:S(2)}, u32[]{:S(2)}) %collective-permute-start.4) | collective-permute-done | bytes 175136 | tf_op jit(solution)/shard_map/ppermute | solution.py:33
  18.9 0.2 broadcast_select_fusion.6
  19.1 0.3 concatenate.16
  19.4 0.1 collective-permute-start.6
  19.5 1.8 %collective-permute-done.6 = bf16[32,7296]{1,0:T(8,128)(2,1)S(1)} collective-permute-done((bf16[32,7296]{1,0:T(8,128)(2,1)S(1)}, bf16[32,7296]{1,0:T(8,128)(2,1)S(1)}, u32[]{:S(2)}, u32[]{:S(2)}) %collective-permute-start.6) | collective-permute-done | bytes 466976 | tf_op jit(solution)/shard_map/ppermute | solution.py:33
  21.3 0.1 broadcast_select_fusion.1
  21.4 0.1 pad_maximum_fusion.x
  21.5 0.5 fusion.4
  22.0 0.2 collective-permute-start.7
  22.2 1.5 %collective-permute-start.8 = (bf16[64,128]{1,0:T(8,128)(2,1)S(1)}, bf16[64,128]{1,0:T(8,128)(2,1)S(1)}, u32[]{:S(2)}, u32[]{:S(2)}) collective-permute-start(bf16[64,128]{1,0:T(8,128)(2,1)S(1)} %fusion.4), channel_id=1, source_target_pairs={{0,2},{1,3},{2,0},{3,1},{4,6},{5,7},{6,4},{7,5},{8,10},{9,11},{10,... | collective-permute-start | bytes 49160 | tf_op jit(solution)/shard_map/ppermute | solution.py:33
  23.7 0.2 collective-permute-start.9
  23.9 0.2 convert_reduce_fusion
  24.1 11.5 %shard_map.101 = f32[64,512]{1,0:T(8,128)S(1)} custom-call(bf16[64,7296]{1,0:T(8,128)(2,1)S(1)} %pad_maximum_fusion.x, bf16[7168,2,256]{2,1,0:T(2,128)(2,1)} %bitcast.74), custom_call_target="tpu_custom_call" | custom-call | flops 469762048 | bytes 7340032 | tf_op jit(solution)/shard_map/pallas_call | solution.py:115
  35.6 0.1 copy.24
  35.7 0.1 fusion.32
  35.8 0.1 copy.25
  35.9 0.1 select_reduce_fusion
  36.0 0.1 select_reduce_fusion.1
  36.0 0.1 reshape.31
  36.2 0.2 fusion.9
  36.4 0.1 multiply_reduce_fusion
  36.6 0.2 convolution_convert_fusion
  36.8 0.5 collective-permute-start.11
  37.3 1.5 %collective-permute-start.12 = (bf16[2,32,128]{2,1,0:T(8,128)(2,1)S(1)}, bf16[2,32,128]{2,1,0:T(8,128)(2,1)S(1)}, u32[]{:S(2)}, u32[]{:S(2)}) collective-permute-start(bf16[2,32,128]{2,1,0:T(8,128)(2,1)S(1)} %get-tuple-element.35), channel_id=1, source_target_pairs={{0,2},{1,3},{2,0},{3,1},{4,6},{5,7},{6,4},{7,5},{8,10},{9,11},{10,... | collective-permute-start | bytes 49160 | tf_op jit(solution)/shard_map/ppermute | solution.py:33
  38.8 2.9 %fusion = f32[64,7168]{1,0:T(8,128)S(1)} fusion(bf16[1,256,7168]{2,1,0:T(8,128)(2,1)} %param.15, bf16[64,256]{1,0:T(8,128)(2,1)S(1)} %get-tuple-element.9), kind=kOutput, calls=%fused_computation | convolution fusion | flops 234881024 | bytes 5537792 | tf_op jit(solution)/shard_map/dot_general | solution.py:219
  41.7 0.1 select_convert_fusion
  41.8 0.7 %collective-permute-start.10 = (bf16[32,7168]{1,0:T(8,128)(2,1)S(1)}, bf16[32,7168]{1,0:T(8,128)(2,1)S(1)}, u32[]{:S(2)}, u32[]{:S(2)}) collective-permute-start(bf16[32,7168]{1,0:T(8,128)(2,1)S(1)} %select_convert_fusion), channel_id=1, source_target_pairs={{0,1},{1,0},{2,3},{3,2},{4,5},{5,4},{6,7},{7,6},{8,9},{9,8},{10,11... | collective-permute-start | bytes 1376264 | tf_op jit(solution)/shard_map/ppermute | solution.py:33
  42.5 0.1 fusion.28
  42.6 0.4 fusion.38
  43.0 1.0 %collective-permute-done.10 = bf16[32,7168]{1,0:T(8,128)(2,1)S(1)} collective-permute-done((bf16[32,7168]{1,0:T(8,128)(2,1)S(1)}, bf16[32,7168]{1,0:T(8,128)(2,1)S(1)}, u32[]{:S(2)}, u32[]{:S(2)}) %collective-permute-start.10) | collective-permute-done | bytes 458784 | tf_op jit(solution)/shard_map/ppermute | solution.py:33
  44.0 2.0 %add_convert_fusion = bf16[32,7168]{1,0:T(8,128)(2,1)S(1)} fusion(f32[32,7168]{1,0:T(8,128)S(1)} %fusion.38, bf16[32,7168]{1,0:T(8,128)(2,1)S(1)} %collective-permute-done.10, f32[64,7168]{1,0:T(8,128)S(1)} %fusion, pred[]{:T(512)S(6)} %eq.52, bf16[128,7168]{1,0:T(8,128)(2,1)} %collective-permute-done.5, bf16[2,32,128]{2,1,0:T(8,128)(2,1)S(1)} %fusion.28), kind=kOutput, calls=%fused_computation.14 | convolution fusion | flops 60100608 | bytes 5522432 | tf_op jit(solution)/shard_map/dot_general | solution.py:223
  46.0 0.1 broadcast_select_fusion.2
  46.1 0.1 collective-permute-start.14
  46.2 6.0 %collective-permute-done.14 = bf16[16,7168]{1,0:T(8,128)(2,1)S(1)} collective-permute-done((bf16[16,7168]{1,0:T(8,128)(2,1)S(1)}, bf16[16,7168]{1,0:T(8,128)(2,1)S(1)}, u32[]{:S(2)}, u32[]{:S(2)}) %collective-permute-start.14) | collective-permute-done | bytes 229408 | tf_op jit(solution)/shard_map/ppermute | solution.py:33
  52.2 0.1 add_convert_fusion.1
  52.3 1.6 %collective-permute-start.15 = (bf16[8,7168]{1,0:T(8,128)(2,1)S(1)}, bf16[8,7168]{1,0:T(8,128)(2,1)S(1)}, u32[]{:S(2)}, u32[]{:S(2)}) collective-permute-start(bf16[8,7168]{1,0:T(8,128)(2,1)S(1)} %broadcast_select_fusion.5), channel_id=1, source_target_pairs={{0,2},{1,5},{2,0},{3,7},{4,6},{5,1},{6,4},{7,3},{8,10},{9,13},{10,... | collective-permute-start | bytes 344072 | tf_op jit(solution)/shard_map/ppermute | solution.py:33
  53.8 3.3 %collective-permute-done.15 = bf16[8,7168]{1,0:T(8,128)(2,1)S(1)} collective-permute-done((bf16[8,7168]{1,0:T(8,128)(2,1)S(1)}, bf16[8,7168]{1,0:T(8,128)(2,1)S(1)}, u32[]{:S(2)}, u32[]{:S(2)}) %collective-permute-start.15) | collective-permute-done | bytes 114720 | tf_op jit(solution)/shard_map/ppermute | solution.py:33
  57.2 1.6 %collective-permute-start.16 = (bf16[4,7168]{1,0:T(4,128)(2,1)S(1)}, bf16[4,7168]{1,0:T(4,128)(2,1)S(1)}, u32[]{:S(2)}, u32[]{:S(2)}) collective-permute-start(bf16[4,7168]{1,0:T(4,128)(2,1)S(1)} %slice.118), channel_id=1, source_target_pairs={{0,8},{1,9},{2,10},{3,11},{4,12},{5,13},{6,14},{7,15},{8,0},{9,1},... | collective-permute-start | bytes 172040 | tf_op jit(solution)/shard_map/ppermute | solution.py:33
  58.8 3.6 %collective-permute-done.16 = bf16[4,7168]{1,0:T(4,128)(2,1)S(1)} collective-permute-done((bf16[4,7168]{1,0:T(4,128)(2,1)S(1)}, bf16[4,7168]{1,0:T(4,128)(2,1)S(1)}, u32[]{:S(2)}, u32[]{:S(2)}) %collective-permute-start.16) | collective-permute-done | bytes 57376 | tf_op jit(solution)/shard_map/ppermute | solution.py:33
  62.4 0.7 %fusion.22 = bf16[1,4,7168]{2,1,0:T(4,128)(2,1)} fusion(bf16[4,7168]{1,0:T(4,128)(2,1)S(1)} %collective-permute-done.16, bf16[8,7168]{1,0:T(8,128)(2,1)S(1)} %add_convert_fusion.2), kind=kLoop, calls=%fused_computation.56 | loop fusion | flops 114688 | bytes 172032 | tf_op jit(solution)/shard_map/broadcast_in_dim | solution.py:245
  (36 shorter events, 0.3 us)
Async XLA Ops:
  0.0 21.5 %copy-start = (bf16[1,7168,128]{2,1,0:T(8,128)(2,1)S(1)}, bf16[1,7168,128]{2,1,0:T(8,128)(2,1)}, u32[]{:S(2)}) copy-start(bf16[1,7168,128]{2,1,0:T(8,128)(2,1)} %param.16) | copy-start | bytes 5505028
  1.0 7.4 %collective-permute-start.1 = (bf16[4,7296]{1,0:T(4,128)(2,1)S(1)}, bf16[4,7296]{1,0:T(4,128)(2,1)S(1)}, u32[]{:S(2)}, u32[]{:S(2)}) collective-permute-start(bf16[4,7296]{1,0:T(4,128)(2,1)S(1)} %shard_map.100), channel_id=1, source_target_pairs={{0,4},{1,5},{2,6},{3,7},{4,0},{5,1},{6,2},{7,3},{8,12},{9,13},{10,... | collective-permute-start | bytes 175112 | tf_op jit(solution)/shard_map/ppermute | solution.py:33
  4.1 6.2 %collective-permute-start.2 = (bf16[4,7296]{1,0:T(4,128)(2,1)S(1)}, bf16[4,7296]{1,0:T(4,128)(2,1)S(1)}, u32[]{:S(2)}, u32[]{:S(2)}) collective-permute-start(bf16[4,7296]{1,0:T(4,128)(2,1)S(1)} %shard_map.100), channel_id=1, source_target_pairs={{0,8},{1,9},{2,10},{3,11},{4,12},{5,13},{6,14},{7,15},{8,0},{9,1},... | collective-permute-start | bytes 175112 | tf_op jit(solution)/shard_map/ppermute | solution.py:33
  6.7 6.0 %collective-permute-start.3 = (bf16[4,7296]{1,0:T(4,128)(2,1)S(1)}, bf16[4,7296]{1,0:T(4,128)(2,1)S(1)}, u32[]{:S(2)}, u32[]{:S(2)}) collective-permute-start(bf16[4,7296]{1,0:T(4,128)(2,1)S(1)} %shard_map.100), channel_id=1, source_target_pairs={{0,12},{1,13},{2,14},{3,15},{4,8},{5,9},{6,10},{7,11},{8,4},{9,5},... | collective-permute-start | bytes 175112 | tf_op jit(solution)/shard_map/ppermute | solution.py:33
  6.7 7.6 %collective-permute-start = (bf16[4,7296]{1,0:T(4,128)(2,1)S(1)}, bf16[4,7296]{1,0:T(4,128)(2,1)S(1)}, u32[]{:S(2)}, u32[]{:S(2)}) collective-permute-start(bf16[4,7296]{1,0:T(4,128)(2,1)S(1)} %shard_map.100), channel_id=1, source_target_pairs={{0,2},{1,3},{2,0},{3,1},{4,6},{5,7},{6,4},{7,5},{8,10},{9,11},{10,... | collective-permute-start | bytes 175112 | tf_op jit(solution)/shard_map/ppermute | solution.py:33
  8.4 11.0 %collective-permute-start.5 = (bf16[128,7168]{1,0:T(8,128)(2,1)}, bf16[128,7168]{1,0:T(8,128)(2,1)}, u32[]{:S(2)}, u32[]{:S(2)}) collective-permute-start(bf16[128,7168]{1,0:T(8,128)(2,1)} %bitcast.75), channel_id=1, source_target_pairs={{0,1},{1,0},{2,3},{3,2},{4,5},{5,4},{6,7},{7,6},{8,9},{9,8},{10,11... | collective-permute-start | bytes 5505032 | tf_op jit(solution)/shard_map/ppermute | solution.py:33
  12.8 6.1 %collective-permute-start.4 = (bf16[12,7296]{1,0:T(8,128)(2,1)S(1)}, bf16[12,7296]{1,0:T(8,128)(2,1)S(1)}, u32[]{:S(2)}, u32[]{:S(2)}) collective-permute-start(bf16[12,7296]{1,0:T(8,128)(2,1)S(1)} %pad_maximum_fusion.1), channel_id=1, source_target_pairs={{0,2},{1,3},{2,0},{3,1},{4,6},{5,7},{6,4},{7,5},{8,10},{9,11},{10,... | collective-permute-start | bytes 525320 | tf_op jit(solution)/shard_map/ppermute | solution.py:33
  19.4 1.9 %collective-permute-start.6 = (bf16[32,7296]{1,0:T(8,128)(2,1)S(1)}, bf16[32,7296]{1,0:T(8,128)(2,1)S(1)}, u32[]{:S(2)}, u32[]{:S(2)}) collective-permute-start(bf16[32,7296]{1,0:T(8,128)(2,1)S(1)} %concatenate.16), channel_id=1, source_target_pairs={{0,1},{1,0},{2,3},{3,2},{4,5},{5,4},{6,7},{7,6},{8,9},{9,8},{10,11... | collective-permute-start | bytes 1400840 | tf_op jit(solution)/shard_map/ppermute | solution.py:33
  22.0 14.2 %collective-permute-start.7 = (bf16[64,128]{1,0:T(8,128)(2,1)S(1)}, bf16[64,128]{1,0:T(8,128)(2,1)S(1)}, u32[]{:S(2)}, u32[]{:S(2)}) collective-permute-start(bf16[64,128]{1,0:T(8,128)(2,1)S(1)} %fusion.4), channel_id=1, source_target_pairs={{0,1},{1,0},{2,3},{3,2},{4,5},{5,4},{6,7},{7,6},{8,9},{9,8},{10,11... | collective-permute-start | bytes 49160 | tf_op jit(solution)/shard_map/ppermute | solution.py:33
  22.2 14.0 %collective-permute-start.8 = (bf16[64,128]{1,0:T(8,128)(2,1)S(1)}, bf16[64,128]{1,0:T(8,128)(2,1)S(1)}, u32[]{:S(2)}, u32[]{:S(2)}) collective-permute-start(bf16[64,128]{1,0:T(8,128)(2,1)S(1)} %fusion.4), channel_id=1, source_target_pairs={{0,2},{1,3},{2,0},{3,1},{4,6},{5,7},{6,4},{7,5},{8,10},{9,11},{10,... | collective-permute-start | bytes 49160 | tf_op jit(solution)/shard_map/ppermute | solution.py:33
  23.7 12.5 %collective-permute-start.9 = (bf16[64,128]{1,0:T(8,128)(2,1)S(1)}, bf16[64,128]{1,0:T(8,128)(2,1)S(1)}, u32[]{:S(2)}, u32[]{:S(2)}) collective-permute-start(bf16[64,128]{1,0:T(8,128)(2,1)S(1)} %fusion.4), channel_id=1, source_target_pairs={{0,3},{1,2},{2,1},{3,0},{4,7},{5,6},{6,5},{7,4},{8,11},{9,10},{10,... | collective-permute-start | bytes 49160 | tf_op jit(solution)/shard_map/ppermute | solution.py:33
  24.1 11.8 %copy-start.4 = (s32[16]{0:T(128)S(1)}, s32[16]{0:T(128)}, u32[]{:S(2)}) copy-start(s32[16]{0:T(128)} %param.13) | copy-start | bytes 196
  24.1 12.1 %copy-start.2 = (bf16[1,4,128,2,256]{4,3,2,1,0:T(2,128)(2,1)S(1)}, bf16[1,4,128,2,256]{4,3,2,1,0:T(2,128)(2,1)}, u32[]{:S(2)}) copy-start(bf16[1,4,128,2,256]{4,3,2,1,0:T(2,128)(2,1)} %param.17) | copy-start | bytes 1572868
  35.6 1.0 %copy-start.3 = (bf16[1,4,256,128]{3,2,1,0:T(8,128)(2,1)S(1)}, bf16[1,4,256,128]{3,2,1,0:T(8,128)(2,1)}, u32[]{:S(2)}) copy-start(bf16[1,4,256,128]{3,2,1,0:T(8,128)(2,1)} %param.18) | copy-start | bytes 786436
  36.8 5.7 %collective-permute-start.11 = (bf16[2,32,128]{2,1,0:T(8,128)(2,1)S(1)}, bf16[2,32,128]{2,1,0:T(8,128)(2,1)S(1)}, u32[]{:S(2)}, u32[]{:S(2)}) collective-permute-start(bf16[2,32,128]{2,1,0:T(8,128)(2,1)S(1)} %get-tuple-element.33), channel_id=1, source_target_pairs={{0,1},{1,0},{2,3},{3,2},{4,5},{5,4},{6,7},{7,6},{8,9},{9,8},{10,11... | collective-permute-start | bytes 49160 | tf_op jit(solution)/shard_map/ppermute | solution.py:33
  37.3 5.2 %collective-permute-start.12 = (bf16[2,32,128]{2,1,0:T(8,128)(2,1)S(1)}, bf16[2,32,128]{2,1,0:T(8,128)(2,1)S(1)}, u32[]{:S(2)}, u32[]{:S(2)}) collective-permute-start(bf16[2,32,128]{2,1,0:T(8,128)(2,1)S(1)} %get-tuple-element.35), channel_id=1, source_target_pairs={{0,2},{1,3},{2,0},{3,1},{4,6},{5,7},{6,4},{7,5},{8,10},{9,11},{10,... | collective-permute-start | bytes 49160 | tf_op jit(solution)/shard_map/ppermute | solution.py:33
  38.8 3.7 %collective-permute-start.13 = (bf16[2,32,128]{2,1,0:T(8,128)(2,1)S(1)}, bf16[2,32,128]{2,1,0:T(8,128)(2,1)S(1)}, u32[]{:S(2)}, u32[]{:S(2)}) collective-permute-start(bf16[2,32,128]{2,1,0:T(8,128)(2,1)S(1)} %get-tuple-element.34), channel_id=1, source_target_pairs={{0,3},{1,2},{2,1},{3,0},{4,7},{5,6},{6,5},{7,4},{8,11},{9,10},{10,... | collective-permute-start | bytes 49160 | tf_op jit(solution)/shard_map/ppermute | solution.py:33
  38.8 3.8 %copy-start.1 = (bf16[1,128,7168]{2,1,0:T(8,128)(2,1)S(1)}, bf16[1,128,7168]{2,1,0:T(8,128)(2,1)}, u32[]{:S(2)}) copy-start(bf16[1,128,7168]{2,1,0:T(8,128)(2,1)} %param.19) | copy-start | bytes 5505028
  41.8 2.2 %collective-permute-start.10 = (bf16[32,7168]{1,0:T(8,128)(2,1)S(1)}, bf16[32,7168]{1,0:T(8,128)(2,1)S(1)}, u32[]{:S(2)}, u32[]{:S(2)}) collective-permute-start(bf16[32,7168]{1,0:T(8,128)(2,1)S(1)} %select_convert_fusion), channel_id=1, source_target_pairs={{0,1},{1,0},{2,3},{3,2},{4,5},{5,4},{6,7},{7,6},{8,9},{9,8},{10,11... | collective-permute-start | bytes 1376264 | tf_op jit(solution)/shard_map/ppermute | solution.py:33
  46.1 6.1 %collective-permute-start.14 = (bf16[16,7168]{1,0:T(8,128)(2,1)S(1)}, bf16[16,7168]{1,0:T(8,128)(2,1)S(1)}, u32[]{:S(2)}, u32[]{:S(2)}) collective-permute-start(bf16[16,7168]{1,0:T(8,128)(2,1)S(1)} %broadcast_select_fusion.2), channel_id=1, source_target_pairs={{0,4},{1,3},{2,6},{3,1},{4,0},{5,7},{6,2},{7,5},{8,12},{9,11},{10,... | collective-permute-start | bytes 688136 | tf_op jit(solution)/shard_map/ppermute | solution.py:33
  52.3 4.9 %collective-permute-start.15 = (bf16[8,7168]{1,0:T(8,128)(2,1)S(1)}, bf16[8,7168]{1,0:T(8,128)(2,1)S(1)}, u32[]{:S(2)}, u32[]{:S(2)}) collective-permute-start(bf16[8,7168]{1,0:T(8,128)(2,1)S(1)} %broadcast_select_fusion.5), channel_id=1, source_target_pairs={{0,2},{1,5},{2,0},{3,7},{4,6},{5,1},{6,4},{7,3},{8,10},{9,13},{10,... | collective-permute-start | bytes 344072 | tf_op jit(solution)/shard_map/ppermute | solution.py:33
  57.2 5.2 %collective-permute-start.16 = (bf16[4,7168]{1,0:T(4,128)(2,1)S(1)}, bf16[4,7168]{1,0:T(4,128)(2,1)S(1)}, u32[]{:S(2)}, u32[]{:S(2)}) collective-permute-start(bf16[4,7168]{1,0:T(4,128)(2,1)S(1)} %slice.118), channel_id=1, source_target_pairs={{0,8},{1,9},{2,10},{3,11},{4,12},{5,13},{6,14},{7,15},{8,0},{9,1},... | collective-permute-start | bytes 172040 | tf_op jit(solution)/shard_map/ppermute | solution.py:33

commit v11 on v10

--- a/solution.py
+++ b/solution.py
@@ -75,36 +75,28 @@
             pltpu.SemaphoreType.DMA((3,)),
         ],
         compiler_params=pltpu.CompilerParams(vmem_limit_bytes=4 << 20),
-        cost_estimate=pl.CostEstimate(flops=0, bytes_accessed=4 * tokens.size, transcendentals=0),
+        cost_estimate=pl.CostEstimate(flops=20 * 10**9, bytes_accessed=4 * tokens.size, transcendentals=0),
     )(in_hbm(tokens), in_hbm(routes), in_hbm(numerators))
 
 
-def gate_up_kernel(x, base, out, weights, sems):
-    depth, _, columns = weights.shape
-    step = depth // sems.shape[0]
-    copies = [
-        pltpu.make_async_copy(base.at[pl.ds(k, step)], weights.at[pl.ds(k, step)], sems.at[k // step])
-        for k in range(0, depth, step)
-    ]
-    for copy in copies:
-        copy.start()
-    row = lax.broadcasted_iota(jnp.int32, (256, 512), 0)
-    column = lax.broadcasted_iota(jnp.int32, (256, 512), 1)
+def gate_up_kernel(x, base, out):
+    depth, _, columns = base.shape
+    step = 512
+    row = lax.broadcasted_iota(jnp.int32, (128, 256), 0)
+    column = lax.broadcasted_iota(jnp.int32, (128, 256), 1)
     spread = jnp.where(column // 2 == row, 1.0, 0.0).astype(jnp.bfloat16)
-    is_up = (lax.broadcasted_iota(jnp.int32, (2 * step, columns), 0) % 2).astype(jnp.float32)
-    gate_rows, up_rows = (1.0 - is_up).astype(jnp.bfloat16), is_up.astype(jnp.bfloat16)
-    flat = weights.reshape(2 * depth, columns)
+    is_odd = (lax.broadcasted_iota(jnp.int32, (1, 2 * step), 1) % 2).astype(jnp.float32)
+    odd_mask, even_mask = is_odd.astype(jnp.bfloat16), (1.0 - is_odd).astype(jnp.bfloat16)
+    count = x.shape[0]
+    flat = base.reshape(2 * depth, columns)
     total = jnp.zeros(out.shape, jnp.float32)
     for k in range(0, depth, step):
-        wide = [
-            jnp.dot(x[:, i : i + 256], spread, preferred_element_type=jnp.float32).astype(jnp.bfloat16)
-            for i in range(k, k + step, 256)
-        ]
-        copies[k // step].wait()
-        table = flat[2 * k : 2 * (k + step), :]
+        stacked = jnp.concatenate([x[:, i : i + 128] for i in range(k, k + step, 128)])
+        wide = jnp.dot(stacked, spread, preferred_element_type=jnp.float32).astype(jnp.bfloat16)
+        wide = jnp.concatenate([wide[i : i + count] for i in range(0, stacked.shape[0], count)], axis=1)
         total += jnp.dot(
-            jnp.concatenate(wide, axis=1),
-            jnp.concatenate([table * gate_rows, table * up_rows], axis=1),
+            jnp.concatenate([wide * even_mask, wide * odd_mask]),
+            flat[2 * k : 2 * (k + step), :],
             preferred_element_type=jnp.float32,
         )
     out[...] = total
@@ -114,15 +106,14 @@
     depth, _, columns = base.shape
     return pl.pallas_call(
         gate_up_kernel,
-        out_shape=jax.ShapeDtypeStruct((x.shape[0], 2 * columns), jnp.float32),
-        in_specs=[VMEM, HBM],
+        out_shape=jax.ShapeDtypeStruct((2 * x.shape[0], columns), jnp.float32),
+        in_specs=[VMEM, VMEM],
         out_specs=VMEM,
-        scratch_shapes=[pltpu.VMEM(base.shape, base.dtype), pltpu.SemaphoreType.DMA((depth // 512,))],
-        compiler_params=pltpu.CompilerParams(vmem_limit_bytes=32 << 20),
+        compiler_params=pltpu.CompilerParams(vmem_limit_bytes=16 << 20),
         cost_estimate=pl.CostEstimate(
             flops=4 * x.shape[0] * depth * columns, bytes_accessed=2 * base.size, transcendentals=0
         ),
-    )(x, in_hbm(base))
+    )(x, base)
 
 
 def local(
@@ -197,10 +188,8 @@
     )
 
     lifted = jnp.einsum("srk,skgf->srgf", by_slot, delta_mid[0], preferred_element_type=jnp.float32)
-    part = projected.shape[1] // 2
-    hidden = jax.nn.silu(projected[None, :, :part] + lifted[:, :, 0]) * (
-        projected[None, :, part:] + lifted[:, :, 1]
-    )
+    total = held.shape[0]
+    hidden = jax.nn.silu(projected[None, :total] + lifted[:, :, 0]) * (projected[None, total:] + lifted[:, :, 1])
     hidden_sum = jnp.sum(scale[:, :, None] * hidden, axis=0).astype(jnp.bfloat16)
     partial_codes = jnp.einsum(
         "srf,sfk->srk", hidden.astype(jnp.bfloat16), delta_down[0], preferred_element_type=jnp.float32

time: 63.3 us -> 55.3 us (0.87)
  Pallas kernels: 12.5 us -> 3.93 us
  matrix products: 6.16 us -> 7.52 us
  waiting for transfers between devices: 24.4 us -> 23.5 us
    pallas_call x1, Pallas kernels: 11.5 us -> 2.95 us  [gate_up_product(): pl.pallas_call(gate_up_kernel, out_shape=jax.ShapeDtypeStruct((2 * x.shap...]
    dot_general x2, matrix products: 2.37 us -> 3.87 us  [local(): total = total + jnp.dot(rows, table, preferred_element_type=jnp.float32)]
    ppermute x17, waiting for transfers between devices: 24.4 us -> 23.5 us  [trade(): return lax.ppermute(value, ('expert', 'tensor'), pairs)]
  transfers between devices with their start and end apart: 17 -> 17, of which waited for: 8 -> 7; matrix products, arithmetic and copies ran while one was open for 8% -> 11% of each run, Pallas kernels for 18% -> 5%
where the time goes in v11:
time: 55.3 us; the launch traced here: 55 us
  waiting for transfers between devices  23.5 us (42%)
  starting transfers between devices  16.6 us (30%)
  matrix products  7.52 us (14%)
  Pallas kernels  3.93 us (7%)
  other arithmetic  2.12 us (4%)
  local copies, waits for them, and re-layouts  1.07 us (2%)
    ppermute x17, waiting for transfers between devices, trade(): return lax.ppermute(value, ('expert', 'tensor'), pairs)  23.5 us
    ppermute x17, starting transfers between devices, trade(): return lax.ppermute(value, ('expert', 'tensor'), pairs)  16.6 us
    dot_general x2, matrix products, local(): total = total + jnp.dot(rows, table, preferred_element_type=jnp.float32)  3.87 us
    pallas_call x1, Pallas kernels, gate_up_product(): pl.pallas_call(gate_up_kernel, out_shape=jax.ShapeDtypeStruct((2 * x.shap...  2.95 us
    dot_general x1, matrix products, local(): base = jnp.dot(hidden_sum, base_down[0], preferred_element_type=jnp.float32)  2.79 us
  transfers between devices with their start and end apart: 17, of which 7 were waited for; matrix products, arithmetic and copies ran while one was open for 11% of the time, Pallas kernels for 5%

profile of v11, /device:TPU:0, one launch (start us, length us, event | category | flops | bytes accessed | tf_op | source)
XLA Modules:
  0.0 55.0 jit_solution(5414680531929524836)
XLA Ops:
  0.0 1.0 %shard_map.100 = bf16[4,7296]{1,0:T(4,128)(2,1)S(1)} custom-call(bf16[4,7168]{1,0:T(4,128)(2,1)} %bitcast.85, s32[4,8]{1,0:T(4,128)} %bitcast.86, s32[4,8]{1,0:T(4,128)} %bitcast.87), custom_call_target="tpu_custom_call" | custom-call | flops 20000000000 | bytes 114688 | tf_op jit(solution)/shard_map/pallas_call | solution.py:67
  1.0 3.1 %collective-permute-start.1 = (bf16[4,7296]{1,0:T(4,128)(2,1)S(1)}, bf16[4,7296]{1,0:T(4,128)(2,1)S(1)}, u32[]{:S(2)}, u32[]{:S(2)}) collective-permute-start(bf16[4,7296]{1,0:T(4,128)(2,1)S(1)} %shard_map.100), channel_id=1, source_target_pairs={{0,4},{1,5},{2,6},{3,7},{4,0},{5,1},{6,2},{7,3},{8,12},{9,13},{10,... | collective-permute-start | bytes 175112 | tf_op jit(solution)/shard_map/ppermute | solution.py:33
  4.1 2.6 %collective-permute-start.2 = (bf16[4,7296]{1,0:T(4,128)(2,1)S(1)}, bf16[4,7296]{1,0:T(4,128)(2,1)S(1)}, u32[]{:S(2)}, u32[]{:S(2)}) collective-permute-start(bf16[4,7296]{1,0:T(4,128)(2,1)S(1)} %shard_map.100), channel_id=1, source_target_pairs={{0,8},{1,9},{2,10},{3,11},{4,12},{5,13},{6,14},{7,15},{8,0},{9,1},... | collective-permute-start | bytes 175112 | tf_op jit(solution)/shard_map/ppermute | solution.py:33
  6.7 1.7 %collective-permute-start = (bf16[4,7296]{1,0:T(4,128)(2,1)S(1)}, bf16[4,7296]{1,0:T(4,128)(2,1)S(1)}, u32[]{:S(2)}, u32[]{:S(2)}) collective-permute-start(bf16[4,7296]{1,0:T(4,128)(2,1)S(1)} %shard_map.100), channel_id=1, source_target_pairs={{0,2},{1,3},{2,0},{3,1},{4,6},{5,7},{6,4},{7,5},{8,10},{9,11},{10,... | collective-permute-start | bytes 175112 | tf_op jit(solution)/shard_map/ppermute | solution.py:33
  8.4 1.9 %collective-permute-done.2 = bf16[4,7296]{1,0:T(4,128)(2,1)S(1)} collective-permute-done((bf16[4,7296]{1,0:T(4,128)(2,1)S(1)}, bf16[4,7296]{1,0:T(4,128)(2,1)S(1)}, u32[]{:S(2)}, u32[]{:S(2)}) %collective-permute-start.2) | collective-permute-done | bytes 58400 | tf_op jit(solution)/shard_map/ppermute | solution.py:33
  10.3 2.4 %collective-permute-done.3 = bf16[4,7296]{1,0:T(4,128)(2,1)S(1)} collective-permute-done((bf16[4,7296]{1,0:T(4,128)(2,1)S(1)}, bf16[4,7296]{1,0:T(4,128)(2,1)S(1)}, u32[]{:S(2)}, u32[]{:S(2)}) %collective-permute-start.3) | collective-permute-done | bytes 58400 | tf_op jit(solution)/shard_map/ppermute | solution.py:33
  12.7 0.1 pad_maximum_fusion.1
  12.8 1.6 %collective-permute-start.4 = (bf16[12,7296]{1,0:T(8,128)(2,1)S(1)}, bf16[12,7296]{1,0:T(8,128)(2,1)S(1)}, u32[]{:S(2)}, u32[]{:S(2)}) collective-permute-start(bf16[12,7296]{1,0:T(8,128)(2,1)S(1)} %pad_maximum_fusion.1), channel_id=1, source_target_pairs={{0,2},{1,3},{2,0},{3,1},{4,6},{5,7},{6,4},{7,5},{8,10},{9,11},{10,... | collective-permute-start | bytes 525320 | tf_op jit(solution)/shard_map/ppermute | solution.py:33
  14.4 4.5 %collective-permute-done.4 = bf16[12,7296]{1,0:T(8,128)(2,1)S(1)} collective-permute-done((bf16[12,7296]{1,0:T(8,128)(2,1)S(1)}, bf16[12,7296]{1,0:T(8,128)(2,1)S(1)}, u32[]{:S(2)}, u32[]{:S(2)}) %collective-permute-start.4) | collective-permute-done | bytes 175136 | tf_op jit(solution)/shard_map/ppermute | solution.py:33
  18.9 0.2 broadcast_select_fusion.6
  19.1 0.3 concatenate.16
  19.4 0.1 collective-permute-start.6
  19.5 1.8 %collective-permute-done.6 = bf16[32,7296]{1,0:T(8,128)(2,1)S(1)} collective-permute-done((bf16[32,7296]{1,0:T(8,128)(2,1)S(1)}, bf16[32,7296]{1,0:T(8,128)(2,1)S(1)}, u32[]{:S(2)}, u32[]{:S(2)}) %collective-permute-start.6) | collective-permute-done | bytes 466976 | tf_op jit(solution)/shard_map/ppermute | solution.py:33
  21.3 0.1 broadcast_select_fusion.1
  21.4 0.1 pad_maximum_fusion.x
  21.5 0.5 fusion.4
  22.0 0.2 collective-permute-start.7
  22.2 1.5 %collective-permute-start.8 = (bf16[64,128]{1,0:T(8,128)(2,1)S(1)}, bf16[64,128]{1,0:T(8,128)(2,1)S(1)}, u32[]{:S(2)}, u32[]{:S(2)}) collective-permute-start(bf16[64,128]{1,0:T(8,128)(2,1)S(1)} %fusion.4), channel_id=1, source_target_pairs={{0,2},{1,3},{2,0},{3,1},{4,6},{5,7},{6,4},{7,5},{8,10},{9,11},{10,... | collective-permute-start | bytes 49160 | tf_op jit(solution)/shard_map/ppermute | solution.py:33
  23.7 0.2 collective-permute-start.9
  23.9 0.2 convert_reduce_fusion
  24.1 0.4 copy-done.1
  24.5 3.0 %shard_map.101 = f32[128,256]{1,0:T(8,128)S(1)} custom-call(bf16[64,7296]{1,0:T(8,128)(2,1)S(1)} %pad_maximum_fusion.x, bf16[7168,2,256]{2,1,0:T(2,128)(2,1)S(1)} %bitcast.74), custom_call_target="tpu_custom_call" | custom-call | flops 469762048 | bytes 7340032 | tf_op jit(solution)/shard_map/pallas_call | solution.py:107
  27.5 0.1 fusion.32
  27.6 0.1 copy.25
  27.7 0.1 select_reduce_fusion
  27.8 0.1 select_reduce_fusion.1
  27.9 0.1 reshape.31
  28.1 0.2 fusion.9
  28.3 0.1 multiply_reduce_fusion
  28.4 0.2 convolution_convert_fusion
  28.6 0.2 collective-permute-start.11
  28.8 1.5 %collective-permute-start.12 = (bf16[2,32,128]{2,1,0:T(8,128)(2,1)S(1)}, bf16[2,32,128]{2,1,0:T(8,128)(2,1)S(1)}, u32[]{:S(2)}, u32[]{:S(2)}) collective-permute-start(bf16[2,32,128]{2,1,0:T(8,128)(2,1)S(1)} %get-tuple-element.35), channel_id=1, source_target_pairs={{0,2},{1,3},{2,0},{3,1},{4,6},{5,7},{6,4},{7,5},{8,10},{9,11},{10,... | collective-permute-start | bytes 49160 | tf_op jit(solution)/shard_map/ppermute | solution.py:33
  30.4 0.2 collective-permute-start.13
  30.6 2.8 %fusion = f32[64,7168]{1,0:T(8,128)S(1)} fusion(bf16[1,256,7168]{2,1,0:T(8,128)(2,1)} %param.15, bf16[64,256]{1,0:T(8,128)(2,1)S(1)} %get-tuple-element.9), kind=kOutput, calls=%fused_computation | convolution fusion | flops 234881024 | bytes 5537792 | tf_op jit(solution)/shard_map/dot_general | solution.py:208
  33.4 0.1 select_convert_fusion
  33.5 0.5 collective-permute-start.10
  34.0 0.1 fusion.28
  34.0 1.9 %fusion.38 = f32[32,7168]{1,0:T(8,128)S(1)} fusion(pred[]{:T(512)S(6)} %eq.52, bf16[2,32,128]{2,1,0:T(8,128)(2,1)S(1)} %fusion.28, bf16[1,128,7168]{2,1,0:T(8,128)(2,1)} %param.19), kind=kOutput, calls=%fused_computation.77 | convolution fusion | flops 58724352 | bytes 2768897 | tf_op jit(solution)/shard_map/dot_general | solution.py:212
  35.9 2.0 %add_convert_fusion = bf16[32,7168]{1,0:T(8,128)(2,1)S(1)} fusion(f32[32,7168]{1,0:T(8,128)S(1)} %fusion.38, bf16[32,7168]{1,0:T(8,128)(2,1)S(1)} %collective-permute-done.10, f32[64,7168]{1,0:T(8,128)S(1)} %fusion, pred[]{:T(512)S(6)} %eq.52, bf16[128,7168]{1,0:T(8,128)(2,1)} %collective-permute-done.5, bf16[2,32,128]{2,1,0:T(8,128)(2,1)S(1)} %fusion.28), kind=kOutput, calls=%fused_computation.14 | convolution fusion | flops 60100608 | bytes 5522432 | tf_op jit(solution)/shard_map/dot_general | solution.py:212
  38.0 0.1 broadcast_select_fusion.2
  38.0 0.1 collective-permute-start.14
  38.1 6.0 %collective-permute-done.14 = bf16[16,7168]{1,0:T(8,128)(2,1)S(1)} collective-permute-done((bf16[16,7168]{1,0:T(8,128)(2,1)S(1)}, bf16[16,7168]{1,0:T(8,128)(2,1)S(1)}, u32[]{:S(2)}, u32[]{:S(2)}) %collective-permute-start.14) | collective-permute-done | bytes 229408 | tf_op jit(solution)/shard_map/ppermute | solution.py:33
  44.1 0.1 add_convert_fusion.1
  44.2 1.6 %collective-permute-start.15 = (bf16[8,7168]{1,0:T(8,128)(2,1)S(1)}, bf16[8,7168]{1,0:T(8,128)(2,1)S(1)}, u32[]{:S(2)}, u32[]{:S(2)}) collective-permute-start(bf16[8,7168]{1,0:T(8,128)(2,1)S(1)} %broadcast_select_fusion.5), channel_id=1, source_target_pairs={{0,2},{1,5},{2,0},{3,7},{4,6},{5,1},{6,4},{7,3},{8,10},{9,13},{10,... | collective-permute-start | bytes 344072 | tf_op jit(solution)/shard_map/ppermute | solution.py:33
  45.8 3.3 %collective-permute-done.15 = bf16[8,7168]{1,0:T(8,128)(2,1)S(1)} collective-permute-done((bf16[8,7168]{1,0:T(8,128)(2,1)S(1)}, bf16[8,7168]{1,0:T(8,128)(2,1)S(1)}, u32[]{:S(2)}, u32[]{:S(2)}) %collective-permute-start.15) | collective-permute-done | bytes 114720 | tf_op jit(solution)/shard_map/ppermute | solution.py:33
  49.2 1.6 %collective-permute-start.16 = (bf16[4,7168]{1,0:T(4,128)(2,1)S(1)}, bf16[4,7168]{1,0:T(4,128)(2,1)S(1)}, u32[]{:S(2)}, u32[]{:S(2)}) collective-permute-start(bf16[4,7168]{1,0:T(4,128)(2,1)S(1)} %slice.118), channel_id=1, source_target_pairs={{0,8},{1,9},{2,10},{3,11},{4,12},{5,13},{6,14},{7,15},{8,0},{9,1},... | collective-permute-start | bytes 172040 | tf_op jit(solution)/shard_map/ppermute | solution.py:33
  50.8 3.6 %collective-permute-done.16 = bf16[4,7168]{1,0:T(4,128)(2,1)S(1)} collective-permute-done((bf16[4,7168]{1,0:T(4,128)(2,1)S(1)}, bf16[4,7168]{1,0:T(4,128)(2,1)S(1)}, u32[]{:S(2)}, u32[]{:S(2)}) %collective-permute-start.16) | collective-permute-done | bytes 57376 | tf_op jit(solution)/shard_map/ppermute | solution.py:33
  54.4 0.7 %fusion.22 = bf16[1,4,7168]{2,1,0:T(4,128)(2,1)} fusion(bf16[4,7168]{1,0:T(4,128)(2,1)S(1)} %collective-permute-done.16, bf16[8,7168]{1,0:T(8,128)(2,1)S(1)} %add_convert_fusion.2), kind=kLoop, calls=%fused_computation.56 | loop fusion | flops 114688 | bytes 172032 | tf_op jit(solution)/shard_map/broadcast_in_dim | solution.py:234
  (36 shorter events, 0.4 us)
Async XLA Ops:
  0.0 21.5 %copy-start = (bf16[1,7168,128]{2,1,0:T(8,128)(2,1)S(1)}, bf16[1,7168,128]{2,1,0:T(8,128)(2,1)}, u32[]{:S(2)}) copy-start(bf16[1,7168,128]{2,1,0:T(8,128)(2,1)} %param.16) | copy-start | bytes 5505028
  1.0 7.4 %collective-permute-start.1 = (bf16[4,7296]{1,0:T(4,128)(2,1)S(1)}, bf16[4,7296]{1,0:T(4,128)(2,1)S(1)}, u32[]{:S(2)}, u32[]{:S(2)}) collective-permute-start(bf16[4,7296]{1,0:T(4,128)(2,1)S(1)} %shard_map.100), channel_id=1, source_target_pairs={{0,4},{1,5},{2,6},{3,7},{4,0},{5,1},{6,2},{7,3},{8,12},{9,13},{10,... | collective-permute-start | bytes 175112 | tf_op jit(solution)/shard_map/ppermute | solution.py:33
  4.1 6.2 %collective-permute-start.2 = (bf16[4,7296]{1,0:T(4,128)(2,1)S(1)}, bf16[4,7296]{1,0:T(4,128)(2,1)S(1)}, u32[]{:S(2)}, u32[]{:S(2)}) collective-permute-start(bf16[4,7296]{1,0:T(4,128)(2,1)S(1)} %shard_map.100), channel_id=1, source_target_pairs={{0,8},{1,9},{2,10},{3,11},{4,12},{5,13},{6,14},{7,15},{8,0},{9,1},... | collective-permute-start | bytes 175112 | tf_op jit(solution)/shard_map/ppermute | solution.py:33
  6.7 6.0 %collective-permute-start.3 = (bf16[4,7296]{1,0:T(4,128)(2,1)S(1)}, bf16[4,7296]{1,0:T(4,128)(2,1)S(1)}, u32[]{:S(2)}, u32[]{:S(2)}) collective-permute-start(bf16[4,7296]{1,0:T(4,128)(2,1)S(1)} %shard_map.100), channel_id=1, source_target_pairs={{0,12},{1,13},{2,14},{3,15},{4,8},{5,9},{6,10},{7,11},{8,4},{9,5},... | collective-permute-start | bytes 175112 | tf_op jit(solution)/shard_map/ppermute | solution.py:33
  6.7 7.6 %collective-permute-start = (bf16[4,7296]{1,0:T(4,128)(2,1)S(1)}, bf16[4,7296]{1,0:T(4,128)(2,1)S(1)}, u32[]{:S(2)}, u32[]{:S(2)}) collective-permute-start(bf16[4,7296]{1,0:T(4,128)(2,1)S(1)} %shard_map.100), channel_id=1, source_target_pairs={{0,2},{1,3},{2,0},{3,1},{4,6},{5,7},{6,4},{7,5},{8,10},{9,11},{10,... | collective-permute-start | bytes 175112 | tf_op jit(solution)/shard_map/ppermute | solution.py:33
  8.4 11.0 %collective-permute-start.5 = (bf16[128,7168]{1,0:T(8,128)(2,1)}, bf16[128,7168]{1,0:T(8,128)(2,1)}, u32[]{:S(2)}, u32[]{:S(2)}) collective-permute-start(bf16[128,7168]{1,0:T(8,128)(2,1)} %bitcast.3), channel_id=1, source_target_pairs={{0,1},{1,0},{2,3},{3,2},{4,5},{5,4},{6,7},{7,6},{8,9},{9,8},{10,11... | collective-permute-start | bytes 5505032 | tf_op jit(solution)/shard_map/ppermute | solution.py:33
  12.8 6.1 %collective-permute-start.4 = (bf16[12,7296]{1,0:T(8,128)(2,1)S(1)}, bf16[12,7296]{1,0:T(8,128)(2,1)S(1)}, u32[]{:S(2)}, u32[]{:S(2)}) collective-permute-start(bf16[12,7296]{1,0:T(8,128)(2,1)S(1)} %pad_maximum_fusion.1), channel_id=1, source_target_pairs={{0,2},{1,3},{2,0},{3,1},{4,6},{5,7},{6,4},{7,5},{8,10},{9,11},{10,... | collective-permute-start | bytes 525320 | tf_op jit(solution)/shard_map/ppermute | solution.py:33
  19.4 1.9 %collective-permute-start.6 = (bf16[32,7296]{1,0:T(8,128)(2,1)S(1)}, bf16[32,7296]{1,0:T(8,128)(2,1)S(1)}, u32[]{:S(2)}, u32[]{:S(2)}) collective-permute-start(bf16[32,7296]{1,0:T(8,128)(2,1)S(1)} %concatenate.16), channel_id=1, source_target_pairs={{0,1},{1,0},{2,3},{3,2},{4,5},{5,4},{6,7},{7,6},{8,9},{9,8},{10,11... | collective-permute-start | bytes 1400840 | tf_op jit(solution)/shard_map/ppermute | solution.py:33
  21.4 3.1 %copy-start.1 = (bf16[1,7168,2,256]{3,2,1,0:T(2,128)(2,1)S(1)}, bf16[1,7168,2,256]{3,2,1,0:T(2,128)(2,1)}, u32[]{:S(2)}) copy-start(bf16[1,7168,2,256]{3,2,1,0:T(2,128)(2,1)} %param.14) | copy-start | bytes 22020100
  22.0 6.0 %collective-permute-start.7 = (bf16[64,128]{1,0:T(8,128)(2,1)S(1)}, bf16[64,128]{1,0:T(8,128)(2,1)S(1)}, u32[]{:S(2)}, u32[]{:S(2)}) collective-permute-start(bf16[64,128]{1,0:T(8,128)(2,1)S(1)} %fusion.4), channel_id=1, source_target_pairs={{0,1},{1,0},{2,3},{3,2},{4,5},{5,4},{6,7},{7,6},{8,9},{9,8},{10,11... | collective-permute-start | bytes 49160 | tf_op jit(solution)/shard_map/ppermute | solution.py:33
  22.2 5.8 %collective-permute-start.8 = (bf16[64,128]{1,0:T(8,128)(2,1)S(1)}, bf16[64,128]{1,0:T(8,128)(2,1)S(1)}, u32[]{:S(2)}, u32[]{:S(2)}) collective-permute-start(bf16[64,128]{1,0:T(8,128)(2,1)S(1)} %fusion.4), channel_id=1, source_target_pairs={{0,2},{1,3},{2,0},{3,1},{4,6},{5,7},{6,4},{7,5},{8,10},{9,11},{10,... | collective-permute-start | bytes 49160 | tf_op jit(solution)/shard_map/ppermute | solution.py:33
  23.7 4.3 %collective-permute-start.9 = (bf16[64,128]{1,0:T(8,128)(2,1)S(1)}, bf16[64,128]{1,0:T(8,128)(2,1)S(1)}, u32[]{:S(2)}, u32[]{:S(2)}) collective-permute-start(bf16[64,128]{1,0:T(8,128)(2,1)S(1)} %fusion.4), channel_id=1, source_target_pairs={{0,3},{1,2},{2,1},{3,0},{4,7},{5,6},{6,5},{7,4},{8,11},{9,10},{10,... | collective-permute-start | bytes 49160 | tf_op jit(solution)/shard_map/ppermute | solution.py:33
  24.5 3.2 %copy-start.4 = (s32[16]{0:T(128)S(1)}, s32[16]{0:T(128)}, u32[]{:S(2)}) copy-start(s32[16]{0:T(128)} %param.13) | copy-start | bytes 196
  24.5 3.6 %copy-start.2 = (bf16[1,4,128,2,256]{4,3,2,1,0:T(2,128)(2,1)S(1)}, bf16[1,4,128,2,256]{4,3,2,1,0:T(2,128)(2,1)}, u32[]{:S(2)}) copy-start(bf16[1,4,128,2,256]{4,3,2,1,0:T(2,128)(2,1)} %param.17) | copy-start | bytes 1572868
  27.4 1.0 %copy-start.3 = (bf16[1,4,256,128]{3,2,1,0:T(8,128)(2,1)S(1)}, bf16[1,4,256,128]{3,2,1,0:T(8,128)(2,1)}, u32[]{:S(2)}) copy-start(bf16[1,4,256,128]{3,2,1,0:T(8,128)(2,1)} %param.18) | copy-start | bytes 786436
  28.6 5.3 %collective-permute-start.11 = (bf16[2,32,128]{2,1,0:T(8,128)(2,1)S(1)}, bf16[2,32,128]{2,1,0:T(8,128)(2,1)S(1)}, u32[]{:S(2)}, u32[]{:S(2)}) collective-permute-start(bf16[2,32,128]{2,1,0:T(8,128)(2,1)S(1)} %get-tuple-element.33), channel_id=1, source_target_pairs={{0,1},{1,0},{2,3},{3,2},{4,5},{5,4},{6,7},{7,6},{8,9},{9,8},{10,11... | collective-permute-start | bytes 49160 | tf_op jit(solution)/shard_map/ppermute | solution.py:33
  28.8 5.1 %collective-permute-start.12 = (bf16[2,32,128]{2,1,0:T(8,128)(2,1)S(1)}, bf16[2,32,128]{2,1,0:T(8,128)(2,1)S(1)}, u32[]{:S(2)}, u32[]{:S(2)}) collective-permute-start(bf16[2,32,128]{2,1,0:T(8,128)(2,1)S(1)} %get-tuple-element.35), channel_id=1, source_target_pairs={{0,2},{1,3},{2,0},{3,1},{4,6},{5,7},{6,4},{7,5},{8,10},{9,11},{10,... | collective-permute-start | bytes 49160 | tf_op jit(solution)/shard_map/ppermute | solution.py:33
  30.4 3.6 %collective-permute-start.13 = (bf16[2,32,128]{2,1,0:T(8,128)(2,1)S(1)}, bf16[2,32,128]{2,1,0:T(8,128)(2,1)S(1)}, u32[]{:S(2)}, u32[]{:S(2)}) collective-permute-start(bf16[2,32,128]{2,1,0:T(8,128)(2,1)S(1)} %get-tuple-element.34), channel_id=1, source_target_pairs={{0,3},{1,2},{2,1},{3,0},{4,7},{5,6},{6,5},{7,4},{8,11},{9,10},{10,... | collective-permute-start | bytes 49160 | tf_op jit(solution)/shard_map/ppermute | solution.py:33
  33.5 2.5 %collective-permute-start.10 = (bf16[32,7168]{1,0:T(8,128)(2,1)S(1)}, bf16[32,7168]{1,0:T(8,128)(2,1)S(1)}, u32[]{:S(2)}, u32[]{:S(2)}) collective-permute-start(bf16[32,7168]{1,0:T(8,128)(2,1)S(1)} %select_convert_fusion), channel_id=1, source_target_pairs={{0,1},{1,0},{2,3},{3,2},{4,5},{5,4},{6,7},{7,6},{8,9},{9,8},{10,11... | collective-permute-start | bytes 1376264 | tf_op jit(solution)/shard_map/ppermute | solution.py:33
  38.0 6.1 %collective-permute-start.14 = (bf16[16,7168]{1,0:T(8,128)(2,1)S(1)}, bf16[16,7168]{1,0:T(8,128)(2,1)S(1)}, u32[]{:S(2)}, u32[]{:S(2)}) collective-permute-start(bf16[16,7168]{1,0:T(8,128)(2,1)S(1)} %broadcast_select_fusion.2), channel_id=1, source_target_pairs={{0,4},{1,3},{2,6},{3,1},{4,0},{5,7},{6,2},{7,5},{8,12},{9,11},{10,... | collective-permute-start | bytes 688136 | tf_op jit(solution)/shard_map/ppermute | solution.py:33
  44.2 4.9 %collective-permute-start.15 = (bf16[8,7168]{1,0:T(8,128)(2,1)S(1)}, bf16[8,7168]{1,0:T(8,128)(2,1)S(1)}, u32[]{:S(2)}, u32[]{:S(2)}) collective-permute-start(bf16[8,7168]{1,0:T(8,128)(2,1)S(1)} %broadcast_select_fusion.5), channel_id=1, source_target_pairs={{0,2},{1,5},{2,0},{3,7},{4,6},{5,1},{6,4},{7,3},{8,10},{9,13},{10,... | collective-permute-start | bytes 344072 | tf_op jit(solution)/shard_map/ppermute | solution.py:33
  49.2 5.2 %collective-permute-start.16 = (bf16[4,7168]{1,0:T(4,128)(2,1)S(1)}, bf16[4,7168]{1,0:T(4,128)(2,1)S(1)}, u32[]{:S(2)}, u32[]{:S(2)}) collective-permute-start(bf16[4,7168]{1,0:T(4,128)(2,1)S(1)} %slice.118), channel_id=1, source_target_pairs={{0,8},{1,9},{2,10},{3,11},{4,12},{5,13},{6,14},{7,15},{8,0},{9,1},... | collective-permute-start | bytes 172040 | tf_op jit(solution)/shard_map/ppermute | solution.py:33

commit v12 on v11

--- a/solution.py
+++ b/solution.py
@@ -6,6 +6,7 @@
 from jax.experimental.layout import Layout, with_layout_constraint
 from jax.sharding import PartitionSpec as P
 
+CHUNKS = 2
 VMEM = pl.BlockSpec(memory_space=pltpu.VMEM)
 HBM = pl.BlockSpec(memory_space=pltpu.HBM)
 
@@ -116,6 +117,62 @@
     )(x, base)
 
 
+def in_vmem(value):
+    return pltpu.with_memory_space_constraint(value, pltpu.VMEM)
+
+
+def down_kernel(hidden, base, sent, kept):
+    half, width = kept.shape
+    core = lax.axis_index("tensor") % 2
+    first = pl.ds(pl.multiple_of((1 - core) * half, half), half)
+    second = pl.ds(pl.multiple_of(core * half, half), half)
+    rows = jnp.concatenate([hidden[first, :], hidden[second, :]])
+    for k in range(0, width, 1024):
+        total = jnp.dot(rows, base[:, k : k + 1024], preferred_element_type=jnp.float32)
+        sent[:, k : k + 1024] = total[:half].astype(sent.dtype)
+        kept[:, k : k + 1024] = total[half:]
+
+
+def down_product(hidden, base):
+    rows, width = hidden.shape[0], base.shape[1]
+    return pl.pallas_call(
+        down_kernel,
+        out_shape=(
+            jax.ShapeDtypeStruct((rows // 2, width), jnp.bfloat16),
+            jax.ShapeDtypeStruct((rows // 2, width), jnp.float32),
+        ),
+        in_specs=[VMEM, VMEM],
+        out_specs=(VMEM, VMEM),
+        compiler_params=pltpu.CompilerParams(vmem_limit_bytes=16 << 20),
+        cost_estimate=pl.CostEstimate(flops=2 * rows * base.size, bytes_accessed=2 * base.size, transcendentals=0),
+    )(hidden, in_vmem(base))
+
+
+def finish_kernel(kept, received, own, other, own_back, other_back, *outs):
+    scaled = jnp.concatenate([own[...], other[...]], axis=1)
+    step = outs[0].shape[1]
+    for i, out in enumerate(outs):
+        columns = slice(i * step, (i + 1) * step)
+        back = jnp.concatenate([own_back[:, columns], other_back[:, columns]])
+        total = kept[:, columns] + received[:, columns].astype(jnp.float32)
+        total += jnp.dot(scaled, back, preferred_element_type=jnp.float32)
+        out[...] = total.astype(out.dtype)
+
+
+def finish(kept, received, scaled, backs):
+    rows, width = kept.shape
+    return pl.pallas_call(
+        finish_kernel,
+        out_shape=[jax.ShapeDtypeStruct((rows, width // CHUNKS), jnp.bfloat16)] * CHUNKS,
+        in_specs=[VMEM] * 6,
+        out_specs=[VMEM] * CHUNKS,
+        compiler_params=pltpu.CompilerParams(vmem_limit_bytes=16 << 20),
+        cost_estimate=pl.CostEstimate(
+            flops=4 * rows * backs[0].size, bytes_accessed=4 * backs[0].size, transcendentals=0
+        ),
+    )(kept, received, *scaled, *map(in_vmem, backs))
+
+
 def local(
     tokens,
     routes,
@@ -205,33 +262,32 @@
     scaled = (kept_scale[:, :, None] * lowrank).astype(jnp.bfloat16)
     scaled = ordered(core == 1, scaled[0], scaled[1])
 
-    base = jnp.dot(hidden_sum, base_down[0], preferred_element_type=jnp.float32)
-    kept, sent = ordered(core == 1, base[:half], base[half:])
-    total = kept + trade(sent.astype(jnp.bfloat16), (0, 1), (0, 1)).astype(jnp.float32)
-    for rows, table in zip(scaled, (delta_back[0], other_back)):
-        total = total + jnp.dot(rows, table, preferred_element_type=jnp.float32)
-    total = total.astype(jnp.bfloat16)
+    sent, kept = down_product(hidden_sum, base_down[0])
+    totals = finish(kept, trade(sent, (0, 1), (0, 1)), scaled, (delta_back[0], other_back))
 
     def add(kept, received):
         return (kept.astype(jnp.float32) + received.astype(jnp.float32)).astype(jnp.bfloat16)
 
-    for z, x in reversed(list(zip(paired, across))):
-        flag = (me // (2 * x)) % 2 == 1
-        size = total.shape[0] // 4
-        blocks = [total[i * size : (i + 1) * size] for i in range(4)]
-        inner = ordered(core == 1, blocks[1], blocks[2])
-        kept, sent = ordered(
-            (core == 1) & flag,
-            jnp.concatenate([blocks[0], inner[0]]),
-            jnp.concatenate([inner[1], blocks[3]]),
-        )
-        total = add(kept, trade(sent, (z, 0), (0, 2 * x)))
-        kept, sent = ordered((core == 0) & flag, total[:size], total[size:])
-        total = add(kept, trade(sent, (0, 2 * x), (z, 0)))
-    for mask in reversed(shared):
-        size = total.shape[0] // 2
-        total = add(total[:size], trade(total[size:], (mask, 0), (mask, 0)))
-    return total[None]
+    outputs = []
+    for total in totals:
+        for z, x in reversed(list(zip(paired, across))):
+            flag = (me // (2 * x)) % 2 == 1
+            size = total.shape[0] // 4
+            blocks = [total[i * size : (i + 1) * size] for i in range(4)]
+            inner = ordered(core == 1, blocks[1], blocks[2])
+            kept, sent = ordered(
+                (core == 1) & flag,
+                jnp.concatenate([blocks[0], inner[0]]),
+                jnp.concatenate([inner[1], blocks[3]]),
+            )
+            total = add(kept, trade(sent, (z, 0), (0, 2 * x)))
+            kept, sent = ordered((core == 0) & flag, total[:size], total[size:])
+            total = add(kept, trade(sent, (0, 2 * x), (z, 0)))
+        for mask in reversed(shared):
+            size = total.shape[0] // 2
+            total = add(total[:size], trade(total[size:], (mask, 0), (mask, 0)))
+        outputs.append(total)
+    return jnp.concatenate(outputs, axis=1)[None]
 
 
 def solution(mesh):

time: 55.3 us -> 57.2 us (1.034)
  matrix products: 7.52 us -> 0.86 us
  local copies, waits for them, and re-layouts: 1.07 us -> 6.02 us
  starting transfers between devices: 16.6 us -> 21.2 us
  waiting for transfers between devices: 23.5 us -> 19 us
  Pallas kernels: 3.93 us -> 7.48 us
    dot_general x3 -> x0, matrix products: 6.66 us -> none  [the longest x2 3.87 us: local(): total = total + jnp.dot(rows, table, preferred_element_type=jnp.float32)]
    unnamed x10 -> x12, local copies, waits for them, and re-layouts: 0.43 us -> 5.39 us
    ppermute x17 -> x20, starting transfers between devices: 16.6 us -> 21.2 us  [trade(): return lax.ppermute(value, ('expert', 'tensor'), pairs)]
    ppermute x17 -> x20, waiting for transfers between devices: 23.5 us -> 19 us  [trade(): return lax.ppermute(value, ('expert', 'tensor'), pairs)]
    pallas_call x0 -> x2, Pallas kernels: none -> 3.55 us  [the longest x1 2.8 us: finish(): pl.pallas_call(finish_kernel, out_shape=[jax.ShapeDtypeStruct((rows, widt...]
  transfers between devices with their start and end apart: 17 -> 20, of which waited for: 7 -> 11; matrix products, arithmetic and copies ran while one was open for 11% -> 3% of each run, Pallas kernels for 5% -> 6%
where the time goes in v12:
time: 57.2 us; the launch traced here: 57 us
  starting transfers between devices  21.2 us (37%)
  waiting for transfers between devices  19 us (33%)
  Pallas kernels  7.48 us (13%)
  local copies, waits for them, and re-layouts  6.02 us (11%)
  other arithmetic  2.08 us (4%)
  matrix products  0.86 us (2%)
    ppermute x20, starting transfers between devices, trade(): return lax.ppermute(value, ('expert', 'tensor'), pairs)  21.2 us
    ppermute x20, waiting for transfers between devices, trade(): return lax.ppermute(value, ('expert', 'tensor'), pairs)  19 us
    unnamed x12, local copies, waits for them, and re-layouts  5.39 us
    pallas_call x1, Pallas kernels, gate_up_product(): pl.pallas_call(gate_up_kernel, out_shape=jax.ShapeDtypeStruct((2 * x.shap...  2.95 us
    pallas_call x1, Pallas kernels, finish(): pl.pallas_call(finish_kernel, out_shape=[jax.ShapeDtypeStruct((rows, widt...  2.8 us
  transfers between devices with their start and end apart: 20, of which 11 were waited for; matrix products, arithmetic and copies ran while one was open for 3% of the time, Pallas kernels for 6%

profile of v12, /device:TPU:0, one launch (start us, length us, event | category | flops | bytes accessed | tf_op | source)
XLA Modules:
  0.0 57.0 jit_solution(12322148247450812353)
XLA Ops:
  0.0 1.0 %shard_map.100 = bf16[4,7296]{1,0:T(4,128)(2,1)S(1)} custom-call(bf16[4,7168]{1,0:T(4,128)(2,1)} %bitcast.76, s32[4,8]{1,0:T(4,128)} %bitcast.77, s32[4,8]{1,0:T(4,128)} %bitcast.78), custom_call_target="tpu_custom_call" | custom-call | flops 20000000000 | bytes 114688 | tf_op jit(solution)/shard_map/pallas_call | solution.py:68
  1.0 5.1 %collective-permute-start.3 = (bf16[4,7296]{1,0:T(4,128)(2,1)S(1)}, bf16[4,7296]{1,0:T(4,128)(2,1)S(1)}, u32[]{:S(2)}, u32[]{:S(2)}) collective-permute-start(bf16[4,7296]{1,0:T(4,128)(2,1)S(1)} %shard_map.100), channel_id=1, source_target_pairs={{0,12},{1,13},{2,14},{3,15},{4,8},{5,9},{6,10},{7,11},{8,4},{9,5},... | collective-permute-start | bytes 175112 | tf_op jit(solution)/shard_map/ppermute | solution.py:34
  6.1 0.6 %collective-permute-start.1 = (bf16[4,7296]{1,0:T(4,128)(2,1)S(1)}, bf16[4,7296]{1,0:T(4,128)(2,1)S(1)}, u32[]{:S(2)}, u32[]{:S(2)}) collective-permute-start(bf16[4,7296]{1,0:T(4,128)(2,1)S(1)} %shard_map.100), channel_id=1, source_target_pairs={{0,4},{1,5},{2,6},{3,7},{4,0},{5,1},{6,2},{7,3},{8,12},{9,13},{10,... | collective-permute-start | bytes 175112 | tf_op jit(solution)/shard_map/ppermute | solution.py:34
  6.7 1.6 %collective-permute-start = (bf16[4,7296]{1,0:T(4,128)(2,1)S(1)}, bf16[4,7296]{1,0:T(4,128)(2,1)S(1)}, u32[]{:S(2)}, u32[]{:S(2)}) collective-permute-start(bf16[4,7296]{1,0:T(4,128)(2,1)S(1)} %shard_map.100), channel_id=1, source_target_pairs={{0,2},{1,3},{2,0},{3,1},{4,6},{5,7},{6,4},{7,5},{8,10},{9,11},{10,... | collective-permute-start | bytes 175112 | tf_op jit(solution)/shard_map/ppermute | solution.py:34
  8.4 0.1 collective-permute-done.3
  8.5 2.7 %collective-permute-done.2 = bf16[4,7296]{1,0:T(4,128)(2,1)S(1)} collective-permute-done((bf16[4,7296]{1,0:T(4,128)(2,1)S(1)}, bf16[4,7296]{1,0:T(4,128)(2,1)S(1)}, u32[]{:S(2)}, u32[]{:S(2)}) %collective-permute-start.2) | collective-permute-done | bytes 58400 | tf_op jit(solution)/shard_map/ppermute | solution.py:34
  11.2 0.1 pad_maximum_fusion.1
  11.3 1.6 %collective-permute-start.4 = (bf16[12,7296]{1,0:T(8,128)(2,1)S(1)}, bf16[12,7296]{1,0:T(8,128)(2,1)S(1)}, u32[]{:S(2)}, u32[]{:S(2)}) collective-permute-start(bf16[12,7296]{1,0:T(8,128)(2,1)S(1)} %pad_maximum_fusion.1), channel_id=1, source_target_pairs={{0,2},{1,3},{2,0},{3,1},{4,6},{5,7},{6,4},{7,5},{8,10},{9,11},{10,... | collective-permute-start | bytes 525320 | tf_op jit(solution)/shard_map/ppermute | solution.py:34
  13.0 5.1 %collective-permute-done.4 = bf16[12,7296]{1,0:T(8,128)(2,1)S(1)} collective-permute-done((bf16[12,7296]{1,0:T(8,128)(2,1)S(1)}, bf16[12,7296]{1,0:T(8,128)(2,1)S(1)}, u32[]{:S(2)}, u32[]{:S(2)}) %collective-permute-start.4) | collective-permute-done | bytes 175136 | tf_op jit(solution)/shard_map/ppermute | solution.py:34
  18.2 0.2 broadcast_select_fusion.4
  18.3 0.3 concatenate.25
  18.8 1.8 %collective-permute-done.6 = bf16[32,7296]{1,0:T(8,128)(2,1)S(1)} collective-permute-done((bf16[32,7296]{1,0:T(8,128)(2,1)S(1)}, bf16[32,7296]{1,0:T(8,128)(2,1)S(1)}, u32[]{:S(2)}, u32[]{:S(2)}) %collective-permute-start.6) | collective-permute-done | bytes 466976 | tf_op jit(solution)/shard_map/ppermute | solution.py:34
  20.6 0.1 broadcast_select_fusion.1
  20.7 0.2 convert_reduce_fusion
  20.8 0.5 fusion.2
  21.3 1.4 %collective-permute-start.9 = (bf16[64,128]{1,0:T(8,128)(2,1)S(1)}, bf16[64,128]{1,0:T(8,128)(2,1)S(1)}, u32[]{:S(2)}, u32[]{:S(2)}) collective-permute-start(bf16[64,128]{1,0:T(8,128)(2,1)S(1)} %fusion.2), channel_id=1, source_target_pairs={{0,3},{1,2},{2,1},{3,0},{4,7},{5,6},{6,5},{7,4},{8,11},{9,10},{10,... | collective-permute-start | bytes 49160 | tf_op jit(solution)/shard_map/ppermute | solution.py:34
  22.7 0.5 collective-permute-start.8
  23.3 0.1 fusion.28
  23.5 3.1 %copy-done.1 = bf16[1,7168,2,256]{3,2,1,0:T(2,128)(2,1)S(1)} copy-done((bf16[1,7168,2,256]{3,2,1,0:T(2,128)(2,1)S(1)}, bf16[1,7168,2,256]{3,2,1,0:T(2,128)(2,1)}, u32[]{:S(2)}) %copy-start.1) | copy-done | bytes 7340056
  26.6 3.0 %shard_map.101 = f32[128,256]{1,0:T(8,128)S(1)} custom-call(bf16[64,7296]{1,0:T(8,128)(2,1)S(1)} %pad_maximum_fusion.x, bf16[7168,2,256]{2,1,0:T(2,128)(2,1)S(1)} %bitcast.64), custom_call_target="tpu_custom_call" | custom-call | flops 469762048 | bytes 7340032 | tf_op jit(solution)/shard_map/pallas_call | solution.py:108
  29.6 0.1 select_reduce_fusion
  29.7 0.1 select_reduce_fusion.1
  29.8 0.1 reshape.32
  30.0 0.2 fusion.7
  30.2 0.1 multiply_reduce_fusion
  30.3 0.2 copy-done.4
  30.6 0.2 convolution_convert_fusion
  30.8 0.5 collective-permute-start.11
  31.3 1.3 %collective-permute-start.13 = (bf16[2,32,128]{2,1,0:T(8,128)(2,1)S(1)}, bf16[2,32,128]{2,1,0:T(8,128)(2,1)S(1)}, u32[]{:S(2)}, u32[]{:S(2)}) collective-permute-start(bf16[2,32,128]{2,1,0:T(8,128)(2,1)S(1)} %get-tuple-element.46), channel_id=1, source_target_pairs={{0,3},{1,2},{2,1},{3,0},{4,7},{5,6},{6,5},{7,4},{8,11},{9,10},{10,... | collective-permute-start | bytes 49160 | tf_op jit(solution)/shard_map/ppermute | solution.py:34
  32.5 0.4 collective-permute-start.12
  33.0 2.0 %copy-done.2 = bf16[1,256,7168]{2,1,0:T(8,128)(2,1)S(1)} copy-done((bf16[1,256,7168]{2,1,0:T(8,128)(2,1)S(1)}, bf16[1,256,7168]{2,1,0:T(8,128)(2,1)}, u32[]{:S(2)}) %copy-start.2) | copy-done | bytes 3670040
  35.0 0.7 %shard_map.102 = (bf16[32,7168]{1,0:T(8,128)(2,1)S(1)}, f32[32,7168]{1,0:T(8,128)S(1)}) custom-call(bf16[64,256]{1,0:T(8,128)(2,1)S(1)} %get-tuple-element.17.hidden, bf16[256,7168]{1,0:T(8,128)(2,1)S(1)} %bitcast.65), custom_call_target="tpu_custom_call" | custom-call | flops 234881024 | bytes 3670016 | tf_op jit(solution)/shard_map/pallas_call | solution.py:138
  35.8 0.2 collective-permute-start.10
  36.0 0.3 collective-permute-done.12
  36.4 1.3 %collective-permute-done.10.received = bf16[32,7168]{1,0:T(8,128)(2,1)S(1)} collective-permute-done((bf16[32,7168]{1,0:T(8,128)(2,1)S(1)}, bf16[32,7168]{1,0:T(8,128)(2,1)S(1)}, u32[]{:S(2)}, u32[]{:S(2)}) %collective-permute-start.10) | collective-permute-done | bytes 458784 | tf_op jit(solution)/shard_map/ppermute | solution.py:34
  37.7 2.8 %shard_map.103 = (bf16[32,3584]{1,0:T(8,128)(2,1)S(1)}, bf16[32,3584]{1,0:T(8,128)(2,1)S(1)}) custom-call(f32[32,7168]{1,0:T(8,128)S(1)} %get-tuple-element.12.kept, bf16[32,7168]{1,0:T(8,128)(2,1)S(1)} %collective-permute-done.10.received, bf16[32,128]{1,0:T(8,128)(2,1)S(1)} %get-tuple-element.53.own, bf16[32,128]{1,0:T(8,128)(2,1)S(1)} %get-tuple-element.52.other, ...), custom_call_target="tpu_custom_call" | custom-call | flops 117440512 | bytes 3670016 | tf_op jit(solution)/shard_map/pallas_call | solution.py:164
  40.6 0.7 %collective-permute-start.17 = (bf16[16,3584]{1,0:T(8,128)(2,1)S(1)}, bf16[16,3584]{1,0:T(8,128)(2,1)S(1)}, u32[]{:S(2)}, u32[]{:S(2)}) collective-permute-start(bf16[16,3584]{1,0:T(8,128)(2,1)S(1)} %broadcast_select_fusion.2), channel_id=1, source_target_pairs={{0,4},{1,3},{2,6},{3,1},{4,0},{5,7},{6,2},{7,5},{8,12},{9,11},{10,... | collective-permute-start | bytes 344072 | tf_op jit(solution)/shard_map/ppermute | solution.py:34
  41.3 1.4 %collective-permute-start.14 = (bf16[16,3584]{1,0:T(8,128)(2,1)S(1)}, bf16[16,3584]{1,0:T(8,128)(2,1)S(1)}, u32[]{:S(2)}, u32[]{:S(2)}) collective-permute-start(bf16[16,3584]{1,0:T(8,128)(2,1)S(1)} %broadcast_select_fusion.3), channel_id=1, source_target_pairs={{0,4},{1,3},{2,6},{3,1},{4,0},{5,7},{6,2},{7,5},{8,12},{9,11},{10,... | collective-permute-start | bytes 344072 | tf_op jit(solution)/shard_map/ppermute | solution.py:34
  42.7 2.7 %collective-permute-done.17 = bf16[16,3584]{1,0:T(8,128)(2,1)S(1)} collective-permute-done((bf16[16,3584]{1,0:T(8,128)(2,1)S(1)}, bf16[16,3584]{1,0:T(8,128)(2,1)S(1)}, u32[]{:S(2)}, u32[]{:S(2)}) %collective-permute-start.17) | collective-permute-done | bytes 114720 | tf_op jit(solution)/shard_map/ppermute | solution.py:34
  45.5 1.6 %collective-permute-start.18 = (bf16[8,3584]{1,0:T(8,128)(2,1)S(1)}, bf16[8,3584]{1,0:T(8,128)(2,1)S(1)}, u32[]{:S(2)}, u32[]{:S(2)}) collective-permute-start(bf16[8,3584]{1,0:T(8,128)(2,1)S(1)} %broadcast_select_fusion.16), channel_id=1, source_target_pairs={{0,2},{1,5},{2,0},{3,7},{4,6},{5,1},{6,4},{7,3},{8,10},{9,13},{10,... | collective-permute-start | bytes 172040 | tf_op jit(solution)/shard_map/ppermute | solution.py:34
  47.2 1.2 %collective-permute-start.15 = (bf16[8,3584]{1,0:T(8,128)(2,1)S(1)}, bf16[8,3584]{1,0:T(8,128)(2,1)S(1)}, u32[]{:S(2)}, u32[]{:S(2)}) collective-permute-start(bf16[8,3584]{1,0:T(8,128)(2,1)S(1)} %broadcast_select_fusion.17), channel_id=1, source_target_pairs={{0,2},{1,5},{2,0},{3,7},{4,6},{5,1},{6,4},{7,3},{8,10},{9,13},{10,... | collective-permute-start | bytes 172040 | tf_op jit(solution)/shard_map/ppermute | solution.py:34
  48.4 1.4 %collective-permute-done.18 = bf16[8,3584]{1,0:T(8,128)(2,1)S(1)} collective-permute-done((bf16[8,3584]{1,0:T(8,128)(2,1)S(1)}, bf16[8,3584]{1,0:T(8,128)(2,1)S(1)}, u32[]{:S(2)}, u32[]{:S(2)}) %collective-permute-start.18) | collective-permute-done | bytes 57376 | tf_op jit(solution)/shard_map/ppermute | solution.py:34
  49.8 1.4 %collective-permute-start.19 = (bf16[4,3584]{1,0:T(4,128)(2,1)S(1)}, bf16[4,3584]{1,0:T(4,128)(2,1)S(1)}, u32[]{:S(2)}, u32[]{:S(2)}) collective-permute-start(bf16[4,3584]{1,0:T(4,128)(2,1)S(1)} %slice.140), channel_id=1, source_target_pairs={{0,8},{1,9},{2,10},{3,11},{4,12},{5,13},{6,14},{7,15},{8,0},{9,1},... | collective-permute-start | bytes 86024 | tf_op jit(solution)/shard_map/ppermute | solution.py:34
  51.1 0.3 collective-permute-done.15
  51.5 1.4 %collective-permute-start.16 = (bf16[4,3584]{1,0:T(4,128)(2,1)S(1)}, bf16[4,3584]{1,0:T(4,128)(2,1)S(1)}, u32[]{:S(2)}, u32[]{:S(2)}) collective-permute-start(bf16[4,3584]{1,0:T(4,128)(2,1)S(1)} %slice.136), channel_id=1, source_target_pairs={{0,8},{1,9},{2,10},{3,11},{4,12},{5,13},{6,14},{7,15},{8,0},{9,1},... | collective-permute-start | bytes 86024 | tf_op jit(solution)/shard_map/ppermute | solution.py:34
  52.9 2.0 %collective-permute-done.19 = bf16[4,3584]{1,0:T(4,128)(2,1)S(1)} collective-permute-done((bf16[4,3584]{1,0:T(4,128)(2,1)S(1)}, bf16[4,3584]{1,0:T(4,128)(2,1)S(1)}, u32[]{:S(2)}, u32[]{:S(2)}) %collective-permute-start.19) | collective-permute-done | bytes 28704 | tf_op jit(solution)/shard_map/ppermute | solution.py:34
  54.9 1.4 %collective-permute-done.16 = bf16[4,3584]{1,0:T(4,128)(2,1)S(1)} collective-permute-done((bf16[4,3584]{1,0:T(4,128)(2,1)S(1)}, bf16[4,3584]{1,0:T(4,128)(2,1)S(1)}, u32[]{:S(2)}, u32[]{:S(2)}) %collective-permute-start.16) | collective-permute-done | bytes 28704 | tf_op jit(solution)/shard_map/ppermute | solution.py:34
  56.4 0.7 %maximum_bitcast_fusion.2 = bf16[1,4,7168]{2,1,0:T(4,128)(2,1)} fusion(bf16[4,3584]{1,0:T(4,128)(2,1)S(1)} %add_convert_fusion.4, bf16[4,3584]{1,0:T(4,128)(2,1)S(1)} %add_convert_fusion.5), kind=kLoop, calls=%fused_computation.53 | loop fusion | flops 114688 | bytes 114688 | tf_op jit(solution)/shard_map/broadcast_in_dim | solution.py:290
  (51 shorter events, 0.9 us)
Async XLA Ops:
  0.0 20.8 %copy-start = (bf16[1,7168,128]{2,1,0:T(8,128)(2,1)S(1)}, bf16[1,7168,128]{2,1,0:T(8,128)(2,1)}, u32[]{:S(2)}) copy-start(bf16[1,7168,128]{2,1,0:T(8,128)(2,1)} %param.16) | copy-start | bytes 5505028
  1.0 7.5 %collective-permute-start.3 = (bf16[4,7296]{1,0:T(4,128)(2,1)S(1)}, bf16[4,7296]{1,0:T(4,128)(2,1)S(1)}, u32[]{:S(2)}, u32[]{:S(2)}) collective-permute-start(bf16[4,7296]{1,0:T(4,128)(2,1)S(1)} %shard_map.100), channel_id=1, source_target_pairs={{0,12},{1,13},{2,14},{3,15},{4,8},{5,9},{6,10},{7,11},{8,4},{9,5},... | collective-permute-start | bytes 175112 | tf_op jit(solution)/shard_map/ppermute | solution.py:34
  6.1 5.1 %collective-permute-start.2 = (bf16[4,7296]{1,0:T(4,128)(2,1)S(1)}, bf16[4,7296]{1,0:T(4,128)(2,1)S(1)}, u32[]{:S(2)}, u32[]{:S(2)}) collective-permute-start(bf16[4,7296]{1,0:T(4,128)(2,1)S(1)} %shard_map.100), channel_id=1, source_target_pairs={{0,8},{1,9},{2,10},{3,11},{4,12},{5,13},{6,14},{7,15},{8,0},{9,1},... | collective-permute-start | bytes 175112 | tf_op jit(solution)/shard_map/ppermute | solution.py:34
  6.1 5.1 %collective-permute-start.1 = (bf16[4,7296]{1,0:T(4,128)(2,1)S(1)}, bf16[4,7296]{1,0:T(4,128)(2,1)S(1)}, u32[]{:S(2)}, u32[]{:S(2)}) collective-permute-start(bf16[4,7296]{1,0:T(4,128)(2,1)S(1)} %shard_map.100), channel_id=1, source_target_pairs={{0,4},{1,5},{2,6},{3,7},{4,0},{5,1},{6,2},{7,3},{8,12},{9,13},{10,... | collective-permute-start | bytes 175112 | tf_op jit(solution)/shard_map/ppermute | solution.py:34
  6.7 6.2 %collective-permute-start = (bf16[4,7296]{1,0:T(4,128)(2,1)S(1)}, bf16[4,7296]{1,0:T(4,128)(2,1)S(1)}, u32[]{:S(2)}, u32[]{:S(2)}) collective-permute-start(bf16[4,7296]{1,0:T(4,128)(2,1)S(1)} %shard_map.100), channel_id=1, source_target_pairs={{0,2},{1,3},{2,0},{3,1},{4,6},{5,7},{6,4},{7,5},{8,10},{9,11},{10,... | collective-permute-start | bytes 175112 | tf_op jit(solution)/shard_map/ppermute | solution.py:34
  8.4 10.3 %collective-permute-start.5 = (bf16[128,7168]{1,0:T(8,128)(2,1)}, bf16[128,7168]{1,0:T(8,128)(2,1)}, u32[]{:S(2)}, u32[]{:S(2)}) collective-permute-start(bf16[128,7168]{1,0:T(8,128)(2,1)} %bitcast.3.own_back), channel_id=1, source_target_pairs={{0,1},{1,0},{2,3},{3,2},{4,5},{5,4},{6,7},{7,6},{8,9},{9,8},{10,11... | collective-permute-start | bytes 5505032 | tf_op jit(solution)/shard_map/ppermute | solution.py:34
  11.3 6.8 %collective-permute-start.4 = (bf16[12,7296]{1,0:T(8,128)(2,1)S(1)}, bf16[12,7296]{1,0:T(8,128)(2,1)S(1)}, u32[]{:S(2)}, u32[]{:S(2)}) collective-permute-start(bf16[12,7296]{1,0:T(8,128)(2,1)S(1)} %pad_maximum_fusion.1), channel_id=1, source_target_pairs={{0,2},{1,3},{2,0},{3,1},{4,6},{5,7},{6,4},{7,5},{8,10},{9,11},{10,... | collective-permute-start | bytes 525320 | tf_op jit(solution)/shard_map/ppermute | solution.py:34
  18.7 1.9 %collective-permute-start.6 = (bf16[32,7296]{1,0:T(8,128)(2,1)S(1)}, bf16[32,7296]{1,0:T(8,128)(2,1)S(1)}, u32[]{:S(2)}, u32[]{:S(2)}) collective-permute-start(bf16[32,7296]{1,0:T(8,128)(2,1)S(1)} %concatenate.25), channel_id=1, source_target_pairs={{0,1},{1,0},{2,3},{3,2},{4,5},{5,4},{6,7},{7,6},{8,9},{9,8},{10,11... | collective-permute-start | bytes 1400840 | tf_op jit(solution)/shard_map/ppermute | solution.py:34
  21.3 8.6 %collective-permute-start.9 = (bf16[64,128]{1,0:T(8,128)(2,1)S(1)}, bf16[64,128]{1,0:T(8,128)(2,1)S(1)}, u32[]{:S(2)}, u32[]{:S(2)}) collective-permute-start(bf16[64,128]{1,0:T(8,128)(2,1)S(1)} %fusion.2), channel_id=1, source_target_pairs={{0,3},{1,2},{2,1},{3,0},{4,7},{5,6},{6,5},{7,4},{8,11},{9,10},{10,... | collective-permute-start | bytes 49160 | tf_op jit(solution)/shard_map/ppermute | solution.py:34
  22.7 7.2 %collective-permute-start.8 = (bf16[64,128]{1,0:T(8,128)(2,1)S(1)}, bf16[64,128]{1,0:T(8,128)(2,1)S(1)}, u32[]{:S(2)}, u32[]{:S(2)}) collective-permute-start(bf16[64,128]{1,0:T(8,128)(2,1)S(1)} %fusion.2), channel_id=1, source_target_pairs={{0,2},{1,3},{2,0},{3,1},{4,6},{5,7},{6,4},{7,5},{8,10},{9,11},{10,... | collective-permute-start | bytes 49160 | tf_op jit(solution)/shard_map/ppermute | solution.py:34
  23.2 6.8 %collective-permute-start.7 = (bf16[64,128]{1,0:T(8,128)(2,1)S(1)}, bf16[64,128]{1,0:T(8,128)(2,1)S(1)}, u32[]{:S(2)}, u32[]{:S(2)}) collective-permute-start(bf16[64,128]{1,0:T(8,128)(2,1)S(1)} %fusion.2), channel_id=1, source_target_pairs={{0,1},{1,0},{2,3},{3,2},{4,5},{5,4},{6,7},{7,6},{8,9},{9,8},{10,11... | collective-permute-start | bytes 49160 | tf_op jit(solution)/shard_map/ppermute | solution.py:34
  23.5 3.1 %copy-start.1 = (bf16[1,7168,2,256]{3,2,1,0:T(2,128)(2,1)S(1)}, bf16[1,7168,2,256]{3,2,1,0:T(2,128)(2,1)}, u32[]{:S(2)}) copy-start(bf16[1,7168,2,256]{3,2,1,0:T(2,128)(2,1)} %param.14) | copy-start | bytes 22020100
  26.6 3.0 %copy-start.5 = (s32[16]{0:T(128)S(1)}, s32[16]{0:T(128)}, u32[]{:S(2)}) copy-start(s32[16]{0:T(128)} %param.13) | copy-start | bytes 196
  26.6 3.3 %copy-start.3 = (bf16[1,4,128,2,256]{4,3,2,1,0:T(2,128)(2,1)S(1)}, bf16[1,4,128,2,256]{4,3,2,1,0:T(2,128)(2,1)}, u32[]{:S(2)}) copy-start(bf16[1,4,128,2,256]{4,3,2,1,0:T(2,128)(2,1)} %param.17) | copy-start | bytes 1572868
  29.6 1.0 %copy-start.4 = (bf16[1,4,256,128]{3,2,1,0:T(8,128)(2,1)S(1)}, bf16[1,4,256,128]{3,2,1,0:T(8,128)(2,1)}, u32[]{:S(2)}) copy-start(bf16[1,4,256,128]{3,2,1,0:T(8,128)(2,1)} %param.18) | copy-start | bytes 786436
  30.8 5.2 %collective-permute-start.11 = (bf16[2,32,128]{2,1,0:T(8,128)(2,1)S(1)}, bf16[2,32,128]{2,1,0:T(8,128)(2,1)S(1)}, u32[]{:S(2)}, u32[]{:S(2)}) collective-permute-start(bf16[2,32,128]{2,1,0:T(8,128)(2,1)S(1)} %get-tuple-element.45), channel_id=1, source_target_pairs={{0,1},{1,0},{2,3},{3,2},{4,5},{5,4},{6,7},{7,6},{8,9},{9,8},{10,11... | collective-permute-start | bytes 49160 | tf_op jit(solution)/shard_map/ppermute | solution.py:34
  31.3 4.7 %collective-permute-start.13 = (bf16[2,32,128]{2,1,0:T(8,128)(2,1)S(1)}, bf16[2,32,128]{2,1,0:T(8,128)(2,1)S(1)}, u32[]{:S(2)}, u32[]{:S(2)}) collective-permute-start(bf16[2,32,128]{2,1,0:T(8,128)(2,1)S(1)} %get-tuple-element.46), channel_id=1, source_target_pairs={{0,3},{1,2},{2,1},{3,0},{4,7},{5,6},{6,5},{7,4},{8,11},{9,10},{10,... | collective-permute-start | bytes 49160 | tf_op jit(solution)/shard_map/ppermute | solution.py:34
  32.5 3.7 %collective-permute-start.12 = (bf16[2,32,128]{2,1,0:T(8,128)(2,1)S(1)}, bf16[2,32,128]{2,1,0:T(8,128)(2,1)S(1)}, u32[]{:S(2)}, u32[]{:S(2)}) collective-permute-start(bf16[2,32,128]{2,1,0:T(8,128)(2,1)S(1)} %get-tuple-element.47), channel_id=1, source_target_pairs={{0,2},{1,3},{2,0},{3,1},{4,6},{5,7},{6,4},{7,5},{8,10},{9,11},{10,... | collective-permute-start | bytes 49160 | tf_op jit(solution)/shard_map/ppermute | solution.py:34
  33.0 2.0 %copy-start.2 = (bf16[1,256,7168]{2,1,0:T(8,128)(2,1)S(1)}, bf16[1,256,7168]{2,1,0:T(8,128)(2,1)}, u32[]{:S(2)}) copy-start(bf16[1,256,7168]{2,1,0:T(8,128)(2,1)} %param.15) | copy-start | bytes 11010052
  35.8 1.9 %collective-permute-start.10 = (bf16[32,7168]{1,0:T(8,128)(2,1)S(1)}, bf16[32,7168]{1,0:T(8,128)(2,1)S(1)}, u32[]{:S(2)}, u32[]{:S(2)}) collective-permute-start(bf16[32,7168]{1,0:T(8,128)(2,1)S(1)} %get-tuple-element.13), channel_id=1, source_target_pairs={{0,1},{1,0},{2,3},{3,2},{4,5},{5,4},{6,7},{7,6},{8,9},{9,8},{10,11... | collective-permute-start | bytes 1376264 | tf_op jit(solution)/shard_map/ppermute | solution.py:34
  40.6 4.9 %collective-permute-start.17 = (bf16[16,3584]{1,0:T(8,128)(2,1)S(1)}, bf16[16,3584]{1,0:T(8,128)(2,1)S(1)}, u32[]{:S(2)}, u32[]{:S(2)}) collective-permute-start(bf16[16,3584]{1,0:T(8,128)(2,1)S(1)} %broadcast_select_fusion.2), channel_id=1, source_target_pairs={{0,4},{1,3},{2,6},{3,1},{4,0},{5,7},{6,2},{7,5},{8,12},{9,11},{10,... | collective-permute-start | bytes 344072 | tf_op jit(solution)/shard_map/ppermute | solution.py:34
  41.3 5.8 %collective-permute-start.14 = (bf16[16,3584]{1,0:T(8,128)(2,1)S(1)}, bf16[16,3584]{1,0:T(8,128)(2,1)S(1)}, u32[]{:S(2)}, u32[]{:S(2)}) collective-permute-start(bf16[16,3584]{1,0:T(8,128)(2,1)S(1)} %broadcast_select_fusion.3), channel_id=1, source_target_pairs={{0,4},{1,3},{2,6},{3,1},{4,0},{5,7},{6,2},{7,5},{8,12},{9,11},{10,... | collective-permute-start | bytes 344072 | tf_op jit(solution)/shard_map/ppermute | solution.py:34
  45.5 4.2 %collective-permute-start.18 = (bf16[8,3584]{1,0:T(8,128)(2,1)S(1)}, bf16[8,3584]{1,0:T(8,128)(2,1)S(1)}, u32[]{:S(2)}, u32[]{:S(2)}) collective-permute-start(bf16[8,3584]{1,0:T(8,128)(2,1)S(1)} %broadcast_select_fusion.16), channel_id=1, source_target_pairs={{0,2},{1,5},{2,0},{3,7},{4,6},{5,1},{6,4},{7,3},{8,10},{9,13},{10,... | collective-permute-start | bytes 172040 | tf_op jit(solution)/shard_map/ppermute | solution.py:34
  47.2 4.2 %collective-permute-start.15 = (bf16[8,3584]{1,0:T(8,128)(2,1)S(1)}, bf16[8,3584]{1,0:T(8,128)(2,1)S(1)}, u32[]{:S(2)}, u32[]{:S(2)}) collective-permute-start(bf16[8,3584]{1,0:T(8,128)(2,1)S(1)} %broadcast_select_fusion.17), channel_id=1, source_target_pairs={{0,2},{1,5},{2,0},{3,7},{4,6},{5,1},{6,4},{7,3},{8,10},{9,13},{10,... | collective-permute-start | bytes 172040 | tf_op jit(solution)/shard_map/ppermute | solution.py:34
  49.8 5.1 %collective-permute-start.19 = (bf16[4,3584]{1,0:T(4,128)(2,1)S(1)}, bf16[4,3584]{1,0:T(4,128)(2,1)S(1)}, u32[]{:S(2)}, u32[]{:S(2)}) collective-permute-start(bf16[4,3584]{1,0:T(4,128)(2,1)S(1)} %slice.140), channel_id=1, source_target_pairs={{0,8},{1,9},{2,10},{3,11},{4,12},{5,13},{6,14},{7,15},{8,0},{9,1},... | collective-permute-start | bytes 86024 | tf_op jit(solution)/shard_map/ppermute | solution.py:34
  51.5 4.8 %collective-permute-start.16 = (bf16[4,3584]{1,0:T(4,128)(2,1)S(1)}, bf16[4,3584]{1,0:T(4,128)(2,1)S(1)}, u32[]{:S(2)}, u32[]{:S(2)}) collective-permute-start(bf16[4,3584]{1,0:T(4,128)(2,1)S(1)} %slice.136), channel_id=1, source_target_pairs={{0,8},{1,9},{2,10},{3,11},{4,12},{5,13},{6,14},{7,15},{8,0},{9,1},... | collective-permute-start | bytes 86024 | tf_op jit(solution)/shard_map/ppermute | solution.py:34

commit v13 on v12

--- a/solution.py
+++ b/solution.py
@@ -9,6 +9,10 @@
 CHUNKS = 2
 VMEM = pl.BlockSpec(memory_space=pltpu.VMEM)
 HBM = pl.BlockSpec(memory_space=pltpu.HBM)
+
+
+def in_vmem(value):
+    return pltpu.with_memory_space_constraint(value, pltpu.VMEM)
 
 
 def in_hbm(value):
@@ -111,14 +115,27 @@
         in_specs=[VMEM, VMEM],
         out_specs=VMEM,
         compiler_params=pltpu.CompilerParams(vmem_limit_bytes=16 << 20),
-        cost_estimate=pl.CostEstimate(
-            flops=4 * x.shape[0] * depth * columns, bytes_accessed=2 * base.size, transcendentals=0
-        ),
-    )(x, base)
-
-
-def in_vmem(value):
-    return pltpu.with_memory_space_constraint(value, pltpu.VMEM)
+        cost_estimate=pl.CostEstimate(flops=10**10, bytes_accessed=2 * base.size, transcendentals=0),
+    )(x, in_vmem(base))
+
+
+def join_kernel(own, received, joined):
+    half = own.shape[0]
+    core = lax.axis_index("tensor") % 2
+    joined[pl.ds(pl.multiple_of(core * half, half), half), :] = own[...]
+    joined[pl.ds(pl.multiple_of((1 - core) * half, half), half), :] = received[...]
+
+
+def join(own, received):
+    rows, width = own.shape
+    return pl.pallas_call(
+        join_kernel,
+        out_shape=jax.ShapeDtypeStruct((2 * rows, width), own.dtype),
+        in_specs=[VMEM, VMEM],
+        out_specs=VMEM,
+        compiler_params=pltpu.CompilerParams(vmem_limit_bytes=16 << 20),
+        cost_estimate=pl.CostEstimate(flops=10**10, bytes_accessed=6 * own.size, transcendentals=0),
+    )(own, received)
 
 
 def down_kernel(hidden, base, sent, kept):
@@ -149,14 +166,14 @@
 
 
 def finish_kernel(kept, received, own, other, own_back, other_back, *outs):
-    scaled = jnp.concatenate([own[...], other[...]], axis=1)
-    step = outs[0].shape[1]
+    size, step = outs[0].shape[1], 512
     for i, out in enumerate(outs):
-        columns = slice(i * step, (i + 1) * step)
-        back = jnp.concatenate([own_back[:, columns], other_back[:, columns]])
-        total = kept[:, columns] + received[:, columns].astype(jnp.float32)
-        total += jnp.dot(scaled, back, preferred_element_type=jnp.float32)
-        out[...] = total.astype(out.dtype)
+        for k in range(0, size, step):
+            columns = slice(i * size + k, i * size + k + step)
+            total = kept[:, columns] + received[:, columns].astype(jnp.float32)
+            total += jnp.dot(own[...], own_back[:, columns], preferred_element_type=jnp.float32)
+            total += jnp.dot(other[...], other_back[:, columns], preferred_element_type=jnp.float32)
+            out[:, k : k + step] = total.astype(out.dtype)
 
 
 def finish(kept, received, scaled, backs):
@@ -226,7 +243,7 @@
     held = by_rows(jnp.concatenate([pieces[place] for place in places]))
     held, other_back = lax.optimization_barrier((held, other_back))
     half = held.shape[0]
-    held = by_rows(jnp.concatenate(ordered(core == 1, held, trade(held, (0, 1), (0, 1)))))
+    held = join(held, trade(held, (0, 1), (0, 1)))
 
     codes = jnp.dot(held[:, :width], delta_in[0], preferred_element_type=jnp.float32).astype(jnp.bfloat16)
     rank = codes.shape[1]

time: 57.2 us -> 68.5 us (1.20)
  other arithmetic: 2.08 us -> 7.97 us
  local copies, waits for them, and re-layouts: 6.02 us -> 10.3 us
    unnamed x12 -> x14, local copies, waits for them, and re-layouts: 5.39 us -> 6.94 us
    convert_element_type x1, local copies, waits for them, and re-layouts: 0.06 us -> 1.41 us  [local(): all_routes = side[:, :top].astype(jnp.int32)]
    convert_element_type x1, other arithmetic: 0.08 us -> 1.35 us  [local(): weight[None].astype(jnp.float32)]
    reduce_sum x1, other arithmetic: 0.12 us -> 0.99 us  [local(): jnp.sum(scale[:, :, None] * hidden, axis=0).astype(jnp.bfloat16)]
    another operation x1, other arithmetic: 0.01 us -> 0.78 us  [local(): jnp.stack([codes if m == 0 else trade(codes, (0, m), (0, m)) for m in ran...]
    convert_element_type x1, local copies, waits for them, and re-layouts: 0.06 us -> 0.82 us  [local(): weight[None].astype(jnp.float32)]
    reduce_sum x1, other arithmetic: 0.08 us -> 0.78 us  [lookup(): return jnp.sum(jnp.where(index[..., None] == keys, table, 0), axis=-1)]
  transfers between devices with their start and end apart: 20 -> 20, of which waited for: 11 -> 9; matrix products, arithmetic and copies ran while one was open for 3% -> 13% of each run, Pallas kernels for 6% -> 5%
where the time goes in v13:
time: 68.5 us; the launch traced here: 68 us
  starting transfers between devices  21.6 us (32%)
  waiting for transfers between devices  18.9 us (28%)
  local copies, waits for them, and re-layouts  10.3 us (15%)
  other arithmetic  7.97 us (12%)
  Pallas kernels  7.43 us (11%)
  matrix products  1.47 us (2%)
    ppermute x20, starting transfers between devices, trade(): return lax.ppermute(value, ('expert', 'tensor'), pairs)  21.6 us
    ppermute x20, waiting for transfers between devices, trade(): return lax.ppermute(value, ('expert', 'tensor'), pairs)  18.9 us
    unnamed x14, local copies, waits for them, and re-layouts  6.94 us
    pallas_call x1, Pallas kernels, gate_up_product(): pl.pallas_call(gate_up_kernel, out_shape=jax.ShapeDtypeStruct((2 * x.shap...  2.95 us
    pallas_call x1, Pallas kernels, finish(): pl.pallas_call(finish_kernel, out_shape=[jax.ShapeDtypeStruct((rows, widt...  2.67 us
    convert_element_type x1, local copies, waits for them, and re-layouts, local(): all_routes = side[:, :top].astype(jnp.int32)  1.41 us
  transfers between devices with their start and end apart: 20, of which 9 were waited for; matrix products, arithmetic and copies ran while one was open for 13% of the time, Pallas kernels for 5%

profile of v13, /device:TPU:0, one launch (start us, length us, event | category | flops | bytes accessed | tf_op | source)
XLA Modules:
  0.0 68.0 jit_solution(16779252826492125950)
XLA Ops:
  0.0 1.0 %shard_map.100 = bf16[4,7296]{1,0:T(4,128)(2,1)S(1)} custom-call(bf16[4,7168]{1,0:T(4,128)(2,1)} %bitcast.72, s32[4,8]{1,0:T(4,128)} %bitcast.73, s32[4,8]{1,0:T(4,128)} %bitcast.74), custom_call_target="tpu_custom_call" | custom-call | flops 20000000000 | bytes 114688 | tf_op jit(solution)/shard_map/pallas_call | solution.py:72
  1.0 3.1 %collective-permute-start.1 = (bf16[4,7296]{1,0:T(4,128)(2,1)S(1)}, bf16[4,7296]{1,0:T(4,128)(2,1)S(1)}, u32[]{:S(2)}, u32[]{:S(2)}) collective-permute-start(bf16[4,7296]{1,0:T(4,128)(2,1)S(1)} %shard_map.100), channel_id=1, source_target_pairs={{0,4},{1,5},{2,6},{3,7},{4,0},{5,1},{6,2},{7,3},{8,12},{9,13},{10,... | collective-permute-start | bytes 175112 | tf_op jit(solution)/shard_map/ppermute | solution.py:38
  4.1 2.6 %collective-permute-start.2 = (bf16[4,7296]{1,0:T(4,128)(2,1)S(1)}, bf16[4,7296]{1,0:T(4,128)(2,1)S(1)}, u32[]{:S(2)}, u32[]{:S(2)}) collective-permute-start(bf16[4,7296]{1,0:T(4,128)(2,1)S(1)} %shard_map.100), channel_id=1, source_target_pairs={{0,8},{1,9},{2,10},{3,11},{4,12},{5,13},{6,14},{7,15},{8,0},{9,1},... | collective-permute-start | bytes 175112 | tf_op jit(solution)/shard_map/ppermute | solution.py:38
  6.7 1.7 %collective-permute-start = (bf16[4,7296]{1,0:T(4,128)(2,1)S(1)}, bf16[4,7296]{1,0:T(4,128)(2,1)S(1)}, u32[]{:S(2)}, u32[]{:S(2)}) collective-permute-start(bf16[4,7296]{1,0:T(4,128)(2,1)S(1)} %shard_map.100), channel_id=1, source_target_pairs={{0,2},{1,3},{2,0},{3,1},{4,6},{5,7},{6,4},{7,5},{8,10},{9,11},{10,... | collective-permute-start | bytes 175112 | tf_op jit(solution)/shard_map/ppermute | solution.py:38
  8.4 1.9 %collective-permute-done.2 = bf16[4,7296]{1,0:T(4,128)(2,1)S(1)} collective-permute-done((bf16[4,7296]{1,0:T(4,128)(2,1)S(1)}, bf16[4,7296]{1,0:T(4,128)(2,1)S(1)}, u32[]{:S(2)}, u32[]{:S(2)}) %collective-permute-start.2) | collective-permute-done | bytes 58400 | tf_op jit(solution)/shard_map/ppermute | solution.py:38
  10.3 2.4 %collective-permute-done.3 = bf16[4,7296]{1,0:T(4,128)(2,1)S(1)} collective-permute-done((bf16[4,7296]{1,0:T(4,128)(2,1)S(1)}, bf16[4,7296]{1,0:T(4,128)(2,1)S(1)}, u32[]{:S(2)}, u32[]{:S(2)}) %collective-permute-start.3) | collective-permute-done | bytes 58400 | tf_op jit(solution)/shard_map/ppermute | solution.py:38
  12.8 1.6 %collective-permute-start.4 = (bf16[12,7296]{1,0:T(8,128)(2,1)S(1)}, bf16[12,7296]{1,0:T(8,128)(2,1)S(1)}, u32[]{:S(2)}, u32[]{:S(2)}) collective-permute-start(bf16[12,7296]{1,0:T(8,128)(2,1)S(1)} %pad_maximum_fusion), channel_id=1, source_target_pairs={{0,2},{1,3},{2,0},{3,1},{4,6},{5,7},{6,4},{7,5},{8,10},{9,11},{10,... | collective-permute-start | bytes 525320 | tf_op jit(solution)/shard_map/ppermute | solution.py:38
  14.4 4.5 %collective-permute-done.4 = bf16[12,7296]{1,0:T(8,128)(2,1)S(1)} collective-permute-done((bf16[12,7296]{1,0:T(8,128)(2,1)S(1)}, bf16[12,7296]{1,0:T(8,128)(2,1)S(1)}, u32[]{:S(2)}, u32[]{:S(2)}) %collective-permute-start.4) | collective-permute-done | bytes 175136 | tf_op jit(solution)/shard_map/ppermute | solution.py:38
  18.9 0.2 broadcast_select_fusion.2
  19.1 0.3 concatenate.22.own
  19.5 0.6 iota_add_fusion
  20.1 1.2 %collective-permute-done.6.received = bf16[32,7296]{1,0:T(8,128)(2,1)S(1)} collective-permute-done((bf16[32,7296]{1,0:T(8,128)(2,1)S(1)}, bf16[32,7296]{1,0:T(8,128)(2,1)S(1)}, u32[]{:S(2)}, u32[]{:S(2)}) %collective-permute-start.6) | collective-permute-done | bytes 466976 | tf_op jit(solution)/shard_map/ppermute | solution.py:38
  21.3 0.8 %copy-done.3 = bf16[32,7296]{1,0:T(8,128)(2,1)} copy-done((bf16[32,7296]{1,0:T(8,128)(2,1)}, bf16[32,7296]{1,0:T(8,128)(2,1)S(1)}, u32[]{:S(2)}) %copy-start.3) | copy-done | bytes 466968
  22.1 1.0 %copy-done.4 = bf16[32,7296]{1,0:T(8,128)(2,1)S(1)} copy-done((bf16[32,7296]{1,0:T(8,128)(2,1)S(1)}, bf16[32,7296]{1,0:T(8,128)(2,1)}, u32[]{:S(2)}) %copy-start.4) | copy-done | bytes 466968
  23.2 1.1 %fusion.2 = bf16[64,128]{1,0:T(8,128)(2,1)} fusion(bf16[1,7168,128]{2,1,0:T(8,128)(2,1)S(1)} %copy-done, bf16[64,7296]{1,0:T(8,128)(2,1)S(1)} %shard_map.101.x), kind=kOutput, calls=%fused_computation.3 | convolution fusion | flops 117448704 | bytes 2768896 | tf_op jit(solution)/shard_map/dot_general | solution.py:248
  24.4 1.5 %collective-permute-start.8 = (bf16[64,128]{1,0:T(8,128)(2,1)}, bf16[64,128]{1,0:T(8,128)(2,1)}, u32[]{:S(2)}, u32[]{:S(2)}) collective-permute-start(bf16[64,128]{1,0:T(8,128)(2,1)} %fusion.2), channel_id=1, source_target_pairs={{0,2},{1,3},{2,0},{3,1},{4,6},{5,7},{6,4},{7,5},{8,10},{9,11},{10,... | collective-permute-start | bytes 49160 | tf_op jit(solution)/shard_map/ppermute | solution.py:38
  25.9 0.2 collective-permute-start.9
  26.1 0.6 slice_convert_fusion
  26.8 0.7 %convert_reduce_fusion = f32[64]{0:T(128)} fusion(bf16[64,7296]{1,0:T(8,128)(2,1)S(1)} %shard_map.101.x), kind=kLoop, calls=%fused_computation.53 | loop fusion | flops 960 | bytes 1280 | tf_op jit(solution)/shard_map/reduce_sum | solution.py:258
  27.5 3.1 %copy-done.2 = bf16[1,7168,2,256]{3,2,1,0:T(2,128)(2,1)S(1)} copy-done((bf16[1,7168,2,256]{3,2,1,0:T(2,128)(2,1)S(1)}, bf16[1,7168,2,256]{3,2,1,0:T(2,128)(2,1)}, u32[]{:S(2)}) %copy-start.2) | copy-done | bytes 7340056
  30.6 3.0 %shard_map.102 = f32[128,256]{1,0:T(8,128)S(1)} custom-call(bf16[64,7296]{1,0:T(8,128)(2,1)S(1)} %shard_map.101.x, bf16[7168,2,256]{2,1,0:T(2,128)(2,1)S(1)} %bitcast.65), custom_call_target="tpu_custom_call" | custom-call | flops 10000000000 | bytes 7340032 | tf_op jit(solution)/shard_map/pallas_call | solution.py:112
  33.6 0.7 fusion.29
  34.2 1.4 %copy.21 = s32[64,8]{0,1:T(8,128)} copy(s32[64,8]{1,0:T(8,128)} %slice_convert_fusion) | data formatting | bytes 4096 | tf_op jit(solution)/shard_map/convert_element_type | solution.py:255
  35.6 1.3 %fusion.25 = f32[64,8]{1,0:T(8,128)} fusion(f32[64]{0:T(128)} %convert_reduce_fusion, bf16[64,7296]{1,0:T(8,128)(2,1)S(1)} %shard_map.101.x), kind=kLoop, calls=%fused_computation.62 | loop fusion | flops 2560 | bytes 3328 | tf_op jit(solution)/shard_map/convert_element_type | solution.py:261
  37.0 0.8 %copy.22 = f32[64,8]{0,1:T(8,128)S(1)} copy(f32[64,8]{1,0:T(8,128)} %fusion.25) | data formatting | bytes 4096 | tf_op jit(solution)/shard_map/convert_element_type | solution.py:261
  37.8 0.8 %select_reduce_fusion = s32[64,8]{0,1:T(8,128)S(1)} fusion(s32[16]{0:T(128)} %param.13, s32[64,8]{0,1:T(8,128)} %copy.21), kind=kLoop, calls=%fused_computation.34 | loop fusion | flops 24064 | bytes 4160 | tf_op jit(solution)/shard_map/reduce_sum | solution.py:28
  38.6 0.8 %select_reduce_fusion.1 = f32[4,64]{1,0:T(4,128)S(1)} fusion(f32[64,8]{0,1:T(8,128)S(1)} %copy.22, s32[64,8]{0,1:T(8,128)S(1)} %select_reduce_fusion, s32[4]{0:T(128)} %iota_add_fusion), kind=kLoop, calls=%fused_computation.67 | loop fusion | flops 5888 | bytes 5136 | tf_op jit(solution)/shard_map/reduce_sum | solution.py:260
  39.5 0.8 %pad_maximum_fusion.5 = bf16[4,64,128]{2,1,0:T(8,128)(2,1)S(1)} fusion(bf16[1,64,128]{2,1,0:T(8,128)(2,1)} %bitcast.9, bf16[1,64,128]{2,1,0:T(8,128)(2,1)} %bitcast.8, bf16[1,64,128]{2,1,0:T(8,128)(2,1)} %bitcast.7, bf16[1,64,128]{2,1,0:T(8,128)(2,1)} %bitcast.6), kind=kLoop, calls=%fused_computation.26 | loop fusion | flops 98304 | bytes 131072 | tf_op jit(solution)/shard_map/stack | solution.py:250
  40.3 0.2 fusion.6
  40.5 1.0 %multiply_reduce_fusion = (bf16[64,256]{1,0:T(8,128)(2,1)S(1)}, bf16[4,64,256]{2,1,0:T(8,128)(2,1)S(1)}) fusion(f32[4,64]{1,0:T(4,128)S(1)} %select_reduce_fusion.1, f32[4,64,2,256]{3,1,2,0:T(8,128)S(1)} %fusion.6, f32[64,256]{1,0:T(8,128)} %get-tuple-element.38, f32[64,256]{1,0:T(8,128)} %get-tuple-element.37), kind=kLoop, calls=%fused_computation.13 | loop fusion | flops 638976 | bytes 820224 | tf_op jit(solution)/shard_map/reduce_sum | solution.py:267
  41.5 0.2 convolution_convert_fusion
  41.7 0.5 collective-permute-start.11
  42.2 1.5 %collective-permute-start.12 = (bf16[2,32,128]{2,1,0:T(8,128)(2,1)S(1)}, bf16[2,32,128]{2,1,0:T(8,128)(2,1)S(1)}, u32[]{:S(2)}, u32[]{:S(2)}) collective-permute-start(bf16[2,32,128]{2,1,0:T(8,128)(2,1)S(1)} %get-tuple-element.43), channel_id=1, source_target_pairs={{0,2},{1,3},{2,0},{3,1},{4,6},{5,7},{6,4},{7,5},{8,10},{9,11},{10,... | collective-permute-start | bytes 49160 | tf_op jit(solution)/shard_map/ppermute | solution.py:38
  43.7 2.0 %copy-done.1 = bf16[1,256,7168]{2,1,0:T(8,128)(2,1)S(1)} copy-done((bf16[1,256,7168]{2,1,0:T(8,128)(2,1)S(1)}, bf16[1,256,7168]{2,1,0:T(8,128)(2,1)}, u32[]{:S(2)}) %copy-start.1) | copy-done | bytes 3670040
  45.8 0.7 %shard_map.103 = (bf16[32,7168]{1,0:T(8,128)(2,1)S(1)}, f32[32,7168]{1,0:T(8,128)S(1)}) custom-call(bf16[64,256]{1,0:T(8,128)(2,1)S(1)} %get-tuple-element.17.hidden, bf16[256,7168]{1,0:T(8,128)(2,1)S(1)} %bitcast.64), custom_call_target="tpu_custom_call" | custom-call | flops 234881024 | bytes 3670016 | tf_op jit(solution)/shard_map/pallas_call | solution.py:155
  46.5 0.7 %collective-permute-start.10 = (bf16[32,7168]{1,0:T(8,128)(2,1)S(1)}, bf16[32,7168]{1,0:T(8,128)(2,1)S(1)}, u32[]{:S(2)}, u32[]{:S(2)}) collective-permute-start(bf16[32,7168]{1,0:T(8,128)(2,1)S(1)} %get-tuple-element.13), channel_id=1, source_target_pairs={{0,1},{1,0},{2,3},{3,2},{4,5},{5,4},{6,7},{7,6},{8,9},{9,8},{10,11... | collective-permute-start | bytes 1376264 | tf_op jit(solution)/shard_map/ppermute | solution.py:38
  47.3 1.3 %collective-permute-done.10.received = bf16[32,7168]{1,0:T(8,128)(2,1)S(1)} collective-permute-done((bf16[32,7168]{1,0:T(8,128)(2,1)S(1)}, bf16[32,7168]{1,0:T(8,128)(2,1)S(1)}, u32[]{:S(2)}, u32[]{:S(2)}) %collective-permute-start.10) | collective-permute-done | bytes 458784 | tf_op jit(solution)/shard_map/ppermute | solution.py:38
  48.7 2.7 %shard_map.104 = (bf16[32,3584]{1,0:T(8,128)(2,1)S(1)}, bf16[32,3584]{1,0:T(8,128)(2,1)S(1)}) custom-call(f32[32,7168]{1,0:T(8,128)S(1)} %get-tuple-element.12.kept, bf16[32,7168]{1,0:T(8,128)(2,1)S(1)} %collective-permute-done.10.received, bf16[32,128]{1,0:T(8,128)(2,1)S(1)} %get-tuple-element.49.own, bf16[32,128]{1,0:T(8,128)(2,1)S(1)} %get-tuple-element.48.other, ...), custom_call_target="tpu_custom_call" | custom-call | flops 117440512 | bytes 3670016 | tf_op jit(solution)/shard_map/pallas_call | solution.py:181
  51.5 2.1 %collective-permute-start.17 = (bf16[16,3584]{1,0:T(8,128)(2,1)S(1)}, bf16[16,3584]{1,0:T(8,128)(2,1)S(1)}, u32[]{:S(2)}, u32[]{:S(2)}) collective-permute-start(bf16[16,3584]{1,0:T(8,128)(2,1)S(1)} %broadcast_select_fusion), channel_id=1, source_target_pairs={{0,4},{1,3},{2,6},{3,1},{4,0},{5,7},{6,2},{7,5},{8,12},{9,11},{10,... | collective-permute-start | bytes 344072 | tf_op jit(solution)/shard_map/ppermute | solution.py:38
  53.6 2.6 %collective-permute-done.14 = bf16[16,3584]{1,0:T(8,128)(2,1)S(1)} collective-permute-done((bf16[16,3584]{1,0:T(8,128)(2,1)S(1)}, bf16[16,3584]{1,0:T(8,128)(2,1)S(1)}, u32[]{:S(2)}, u32[]{:S(2)}) %collective-permute-start.14) | collective-permute-done | bytes 114720 | tf_op jit(solution)/shard_map/ppermute | solution.py:38
  56.3 1.6 %collective-permute-start.15 = (bf16[8,3584]{1,0:T(8,128)(2,1)S(1)}, bf16[8,3584]{1,0:T(8,128)(2,1)S(1)}, u32[]{:S(2)}, u32[]{:S(2)}) collective-permute-start(bf16[8,3584]{1,0:T(8,128)(2,1)S(1)} %broadcast_select_fusion.15), channel_id=1, source_target_pairs={{0,2},{1,5},{2,0},{3,7},{4,6},{5,1},{6,4},{7,3},{8,10},{9,13},{10,... | collective-permute-start | bytes 172040 | tf_op jit(solution)/shard_map/ppermute | solution.py:38
  58.0 1.2 %collective-permute-start.18 = (bf16[8,3584]{1,0:T(8,128)(2,1)S(1)}, bf16[8,3584]{1,0:T(8,128)(2,1)S(1)}, u32[]{:S(2)}, u32[]{:S(2)}) collective-permute-start(bf16[8,3584]{1,0:T(8,128)(2,1)S(1)} %broadcast_select_fusion.14), channel_id=1, source_target_pairs={{0,2},{1,5},{2,0},{3,7},{4,6},{5,1},{6,4},{7,3},{8,10},{9,13},{10,... | collective-permute-start | bytes 172040 | tf_op jit(solution)/shard_map/ppermute | solution.py:38
  59.1 1.5 %collective-permute-done.15 = bf16[8,3584]{1,0:T(8,128)(2,1)S(1)} collective-permute-done((bf16[8,3584]{1,0:T(8,128)(2,1)S(1)}, bf16[8,3584]{1,0:T(8,128)(2,1)S(1)}, u32[]{:S(2)}, u32[]{:S(2)}) %collective-permute-start.15) | collective-permute-done | bytes 57376 | tf_op jit(solution)/shard_map/ppermute | solution.py:38
  60.6 1.6 %collective-permute-start.16 = (bf16[4,3584]{1,0:T(4,128)(2,1)S(1)}, bf16[4,3584]{1,0:T(4,128)(2,1)S(1)}, u32[]{:S(2)}, u32[]{:S(2)}) collective-permute-start(bf16[4,3584]{1,0:T(4,128)(2,1)S(1)} %slice.133), channel_id=1, source_target_pairs={{0,8},{1,9},{2,10},{3,11},{4,12},{5,13},{6,14},{7,15},{8,0},{9,1},... | collective-permute-start | bytes 86024 | tf_op jit(solution)/shard_map/ppermute | solution.py:38
  62.3 1.6 %collective-permute-start.19 = (bf16[4,3584]{1,0:T(4,128)(2,1)S(1)}, bf16[4,3584]{1,0:T(4,128)(2,1)S(1)}, u32[]{:S(2)}, u32[]{:S(2)}) collective-permute-start(bf16[4,3584]{1,0:T(4,128)(2,1)S(1)} %slice.137), channel_id=1, source_target_pairs={{0,8},{1,9},{2,10},{3,11},{4,12},{5,13},{6,14},{7,15},{8,0},{9,1},... | collective-permute-start | bytes 86024 | tf_op jit(solution)/shard_map/ppermute | solution.py:38
  63.8 1.6 %collective-permute-done.16 = bf16[4,3584]{1,0:T(4,128)(2,1)S(1)} collective-permute-done((bf16[4,3584]{1,0:T(4,128)(2,1)S(1)}, bf16[4,3584]{1,0:T(4,128)(2,1)S(1)}, u32[]{:S(2)}, u32[]{:S(2)}) %collective-permute-start.16) | collective-permute-done | bytes 28704 | tf_op jit(solution)/shard_map/ppermute | solution.py:38
  65.5 1.9 %collective-permute-done.19 = bf16[4,3584]{1,0:T(4,128)(2,1)S(1)} collective-permute-done((bf16[4,3584]{1,0:T(4,128)(2,1)S(1)}, bf16[4,3584]{1,0:T(4,128)(2,1)S(1)}, u32[]{:S(2)}, u32[]{:S(2)}) %collective-permute-start.19) | collective-permute-done | bytes 28704 | tf_op jit(solution)/shard_map/ppermute | solution.py:38
  67.4 0.7 maximum_bitcast_fusion.2
  (52 shorter events, 1.1 us)
Async XLA Ops:
  0.0 23.2 %copy-start = (bf16[1,7168,128]{2,1,0:T(8,128)(2,1)S(1)}, bf16[1,7168,128]{2,1,0:T(8,128)(2,1)}, u32[]{:S(2)}) copy-start(bf16[1,7168,128]{2,1,0:T(8,128)(2,1)} %param.16) | copy-start | bytes 5505028
  1.0 7.4 %collective-permute-start.1 = (bf16[4,7296]{1,0:T(4,128)(2,1)S(1)}, bf16[4,7296]{1,0:T(4,128)(2,1)S(1)}, u32[]{:S(2)}, u32[]{:S(2)}) collective-permute-start(bf16[4,7296]{1,0:T(4,128)(2,1)S(1)} %shard_map.100), channel_id=1, source_target_pairs={{0,4},{1,5},{2,6},{3,7},{4,0},{5,1},{6,2},{7,3},{8,12},{9,13},{10,... | collective-permute-start | bytes 175112 | tf_op jit(solution)/shard_map/ppermute | solution.py:38
  4.1 6.2 %collective-permute-start.2 = (bf16[4,7296]{1,0:T(4,128)(2,1)S(1)}, bf16[4,7296]{1,0:T(4,128)(2,1)S(1)}, u32[]{:S(2)}, u32[]{:S(2)}) collective-permute-start(bf16[4,7296]{1,0:T(4,128)(2,1)S(1)} %shard_map.100), channel_id=1, source_target_pairs={{0,8},{1,9},{2,10},{3,11},{4,12},{5,13},{6,14},{7,15},{8,0},{9,1},... | collective-permute-start | bytes 175112 | tf_op jit(solution)/shard_map/ppermute | solution.py:38
  6.7 6.0 %collective-permute-start.3 = (bf16[4,7296]{1,0:T(4,128)(2,1)S(1)}, bf16[4,7296]{1,0:T(4,128)(2,1)S(1)}, u32[]{:S(2)}, u32[]{:S(2)}) collective-permute-start(bf16[4,7296]{1,0:T(4,128)(2,1)S(1)} %shard_map.100), channel_id=1, source_target_pairs={{0,12},{1,13},{2,14},{3,15},{4,8},{5,9},{6,10},{7,11},{8,4},{9,5},... | collective-permute-start | bytes 175112 | tf_op jit(solution)/shard_map/ppermute | solution.py:38
  6.7 7.6 %collective-permute-start = (bf16[4,7296]{1,0:T(4,128)(2,1)S(1)}, bf16[4,7296]{1,0:T(4,128)(2,1)S(1)}, u32[]{:S(2)}, u32[]{:S(2)}) collective-permute-start(bf16[4,7296]{1,0:T(4,128)(2,1)S(1)} %shard_map.100), channel_id=1, source_target_pairs={{0,2},{1,3},{2,0},{3,1},{4,6},{5,7},{6,4},{7,5},{8,10},{9,11},{10,... | collective-permute-start | bytes 175112 | tf_op jit(solution)/shard_map/ppermute | solution.py:38
  8.4 11.0 %collective-permute-start.5 = (bf16[128,7168]{1,0:T(8,128)(2,1)}, bf16[128,7168]{1,0:T(8,128)(2,1)}, u32[]{:S(2)}, u32[]{:S(2)}) collective-permute-start(bf16[128,7168]{1,0:T(8,128)(2,1)} %bitcast.3.own_back), channel_id=1, source_target_pairs={{0,1},{1,0},{2,3},{3,2},{4,5},{5,4},{6,7},{7,6},{8,9},{9,8},{10,11... | collective-permute-start | bytes 5505032 | tf_op jit(solution)/shard_map/ppermute | solution.py:38
  12.8 6.1 %collective-permute-start.4 = (bf16[12,7296]{1,0:T(8,128)(2,1)S(1)}, bf16[12,7296]{1,0:T(8,128)(2,1)S(1)}, u32[]{:S(2)}, u32[]{:S(2)}) collective-permute-start(bf16[12,7296]{1,0:T(8,128)(2,1)S(1)} %pad_maximum_fusion), channel_id=1, source_target_pairs={{0,2},{1,3},{2,0},{3,1},{4,6},{5,7},{6,4},{7,5},{8,10},{9,11},{10,... | collective-permute-start | bytes 525320 | tf_op jit(solution)/shard_map/ppermute | solution.py:38
  19.4 1.9 %collective-permute-start.6 = (bf16[32,7296]{1,0:T(8,128)(2,1)S(1)}, bf16[32,7296]{1,0:T(8,128)(2,1)S(1)}, u32[]{:S(2)}, u32[]{:S(2)}) collective-permute-start(bf16[32,7296]{1,0:T(8,128)(2,1)S(1)} %concatenate.22.own), channel_id=1, source_target_pairs={{0,1},{1,0},{2,3},{3,2},{4,5},{5,4},{6,7},{7,6},{8,9},{9,8},{10,11... | collective-permute-start | bytes 1400840 | tf_op jit(solution)/shard_map/ppermute | solution.py:38
  21.3 0.8 %copy-start.3 = (bf16[32,7296]{1,0:T(8,128)(2,1)}, bf16[32,7296]{1,0:T(8,128)(2,1)S(1)}, u32[]{:S(2)}) copy-start(bf16[32,7296]{1,0:T(8,128)(2,1)S(1)} %collective-permute-done.6.received) | copy-start | bytes 1400836
  22.1 1.0 %copy-start.4 = (bf16[32,7296]{1,0:T(8,128)(2,1)S(1)}, bf16[32,7296]{1,0:T(8,128)(2,1)}, u32[]{:S(2)}) copy-start(bf16[32,7296]{1,0:T(8,128)(2,1)} %copy-done.3) | copy-start | bytes 1400836
  24.3 15.2 %collective-permute-start.7 = (bf16[64,128]{1,0:T(8,128)(2,1)}, bf16[64,128]{1,0:T(8,128)(2,1)}, u32[]{:S(2)}, u32[]{:S(2)}) collective-permute-start(bf16[64,128]{1,0:T(8,128)(2,1)} %fusion.2), channel_id=1, source_target_pairs={{0,1},{1,0},{2,3},{3,2},{4,5},{5,4},{6,7},{7,6},{8,9},{9,8},{10,11... | collective-permute-start | bytes 49160 | tf_op jit(solution)/shard_map/ppermute | solution.py:38
  24.4 15.0 %collective-permute-start.8 = (bf16[64,128]{1,0:T(8,128)(2,1)}, bf16[64,128]{1,0:T(8,128)(2,1)}, u32[]{:S(2)}, u32[]{:S(2)}) collective-permute-start(bf16[64,128]{1,0:T(8,128)(2,1)} %fusion.2), channel_id=1, source_target_pairs={{0,2},{1,3},{2,0},{3,1},{4,6},{5,7},{6,4},{7,5},{8,10},{9,11},{10,... | collective-permute-start | bytes 49160 | tf_op jit(solution)/shard_map/ppermute | solution.py:38
  25.9 13.5 %collective-permute-start.9 = (bf16[64,128]{1,0:T(8,128)(2,1)}, bf16[64,128]{1,0:T(8,128)(2,1)}, u32[]{:S(2)}, u32[]{:S(2)}) collective-permute-start(bf16[64,128]{1,0:T(8,128)(2,1)} %fusion.2), channel_id=1, source_target_pairs={{0,3},{1,2},{2,1},{3,0},{4,7},{5,6},{6,5},{7,4},{8,11},{9,10},{10,... | collective-permute-start | bytes 49160 | tf_op jit(solution)/shard_map/ppermute | solution.py:38
  27.5 3.1 %copy-start.2 = (bf16[1,7168,2,256]{3,2,1,0:T(2,128)(2,1)S(1)}, bf16[1,7168,2,256]{3,2,1,0:T(2,128)(2,1)}, u32[]{:S(2)}) copy-start(bf16[1,7168,2,256]{3,2,1,0:T(2,128)(2,1)} %param.14) | copy-start | bytes 22020100
  30.6 9.7 %copy-start.5 = (bf16[1,4,128,2,256]{4,3,2,1,0:T(2,128)(2,1)S(1)}, bf16[1,4,128,2,256]{4,3,2,1,0:T(2,128)(2,1)}, u32[]{:S(2)}) copy-start(bf16[1,4,128,2,256]{4,3,2,1,0:T(2,128)(2,1)} %param.17) | copy-start | bytes 1572868
  33.6 7.9 %copy-start.6 = (bf16[1,4,256,128]{3,2,1,0:T(8,128)(2,1)S(1)}, bf16[1,4,256,128]{3,2,1,0:T(8,128)(2,1)}, u32[]{:S(2)}) copy-start(bf16[1,4,256,128]{3,2,1,0:T(8,128)(2,1)} %param.18) | copy-start | bytes 786436
  41.7 5.5 %collective-permute-start.11 = (bf16[2,32,128]{2,1,0:T(8,128)(2,1)S(1)}, bf16[2,32,128]{2,1,0:T(8,128)(2,1)S(1)}, u32[]{:S(2)}, u32[]{:S(2)}) collective-permute-start(bf16[2,32,128]{2,1,0:T(8,128)(2,1)S(1)} %get-tuple-element.41), channel_id=1, source_target_pairs={{0,1},{1,0},{2,3},{3,2},{4,5},{5,4},{6,7},{7,6},{8,9},{9,8},{10,11... | collective-permute-start | bytes 49160 | tf_op jit(solution)/shard_map/ppermute | solution.py:38
  42.2 5.0 %collective-permute-start.12 = (bf16[2,32,128]{2,1,0:T(8,128)(2,1)S(1)}, bf16[2,32,128]{2,1,0:T(8,128)(2,1)S(1)}, u32[]{:S(2)}, u32[]{:S(2)}) collective-permute-start(bf16[2,32,128]{2,1,0:T(8,128)(2,1)S(1)} %get-tuple-element.43), channel_id=1, source_target_pairs={{0,2},{1,3},{2,0},{3,1},{4,6},{5,7},{6,4},{7,5},{8,10},{9,11},{10,... | collective-permute-start | bytes 49160 | tf_op jit(solution)/shard_map/ppermute | solution.py:38
  43.7 3.5 %collective-permute-start.13 = (bf16[2,32,128]{2,1,0:T(8,128)(2,1)S(1)}, bf16[2,32,128]{2,1,0:T(8,128)(2,1)S(1)}, u32[]{:S(2)}, u32[]{:S(2)}) collective-permute-start(bf16[2,32,128]{2,1,0:T(8,128)(2,1)S(1)} %get-tuple-element.42), channel_id=1, source_target_pairs={{0,3},{1,2},{2,1},{3,0},{4,7},{5,6},{6,5},{7,4},{8,11},{9,10},{10,... | collective-permute-start | bytes 49160 | tf_op jit(solution)/shard_map/ppermute | solution.py:38
  43.7 2.0 %copy-start.1 = (bf16[1,256,7168]{2,1,0:T(8,128)(2,1)S(1)}, bf16[1,256,7168]{2,1,0:T(8,128)(2,1)}, u32[]{:S(2)}) copy-start(bf16[1,256,7168]{2,1,0:T(8,128)(2,1)} %param.15) | copy-start | bytes 11010052
  46.5 2.1 %collective-permute-start.10 = (bf16[32,7168]{1,0:T(8,128)(2,1)S(1)}, bf16[32,7168]{1,0:T(8,128)(2,1)S(1)}, u32[]{:S(2)}, u32[]{:S(2)}) collective-permute-start(bf16[32,7168]{1,0:T(8,128)(2,1)S(1)} %get-tuple-element.13), channel_id=1, source_target_pairs={{0,1},{1,0},{2,3},{3,2},{4,5},{5,4},{6,7},{7,6},{8,9},{9,8},{10,11... | collective-permute-start | bytes 1376264 | tf_op jit(solution)/shard_map/ppermute | solution.py:38
  51.4 4.9 %collective-permute-start.14 = (bf16[16,3584]{1,0:T(8,128)(2,1)S(1)}, bf16[16,3584]{1,0:T(8,128)(2,1)S(1)}, u32[]{:S(2)}, u32[]{:S(2)}) collective-permute-start(bf16[16,3584]{1,0:T(8,128)(2,1)S(1)} %broadcast_select_fusion.1), channel_id=1, source_target_pairs={{0,4},{1,3},{2,6},{3,1},{4,0},{5,7},{6,2},{7,5},{8,12},{9,11},{10,... | collective-permute-start | bytes 344072 | tf_op jit(solution)/shard_map/ppermute | solution.py:38
  51.5 6.3 %collective-permute-start.17 = (bf16[16,3584]{1,0:T(8,128)(2,1)S(1)}, bf16[16,3584]{1,0:T(8,128)(2,1)S(1)}, u32[]{:S(2)}, u32[]{:S(2)}) collective-permute-start(bf16[16,3584]{1,0:T(8,128)(2,1)S(1)} %broadcast_select_fusion), channel_id=1, source_target_pairs={{0,4},{1,3},{2,6},{3,1},{4,0},{5,7},{6,2},{7,5},{8,12},{9,11},{10,... | collective-permute-start | bytes 344072 | tf_op jit(solution)/shard_map/ppermute | solution.py:38
  56.3 4.2 %collective-permute-start.15 = (bf16[8,3584]{1,0:T(8,128)(2,1)S(1)}, bf16[8,3584]{1,0:T(8,128)(2,1)S(1)}, u32[]{:S(2)}, u32[]{:S(2)}) collective-permute-start(bf16[8,3584]{1,0:T(8,128)(2,1)S(1)} %broadcast_select_fusion.15), channel_id=1, source_target_pairs={{0,2},{1,5},{2,0},{3,7},{4,6},{5,1},{6,4},{7,3},{8,10},{9,13},{10,... | collective-permute-start | bytes 172040 | tf_op jit(solution)/shard_map/ppermute | solution.py:38
  58.0 4.3 %collective-permute-start.18 = (bf16[8,3584]{1,0:T(8,128)(2,1)S(1)}, bf16[8,3584]{1,0:T(8,128)(2,1)S(1)}, u32[]{:S(2)}, u32[]{:S(2)}) collective-permute-start(bf16[8,3584]{1,0:T(8,128)(2,1)S(1)} %broadcast_select_fusion.14), channel_id=1, source_target_pairs={{0,2},{1,5},{2,0},{3,7},{4,6},{5,1},{6,4},{7,3},{8,10},{9,13},{10,... | collective-permute-start | bytes 172040 | tf_op jit(solution)/shard_map/ppermute | solution.py:38
  60.6 4.8 %collective-permute-start.16 = (bf16[4,3584]{1,0:T(4,128)(2,1)S(1)}, bf16[4,3584]{1,0:T(4,128)(2,1)S(1)}, u32[]{:S(2)}, u32[]{:S(2)}) collective-permute-start(bf16[4,3584]{1,0:T(4,128)(2,1)S(1)} %slice.133), channel_id=1, source_target_pairs={{0,8},{1,9},{2,10},{3,11},{4,12},{5,13},{6,14},{7,15},{8,0},{9,1},... | collective-permute-start | bytes 86024 | tf_op jit(solution)/shard_map/ppermute | solution.py:38
  62.3 5.1 %collective-permute-start.19 = (bf16[4,3584]{1,0:T(4,128)(2,1)S(1)}, bf16[4,3584]{1,0:T(4,128)(2,1)S(1)}, u32[]{:S(2)}, u32[]{:S(2)}) collective-permute-start(bf16[4,3584]{1,0:T(4,128)(2,1)S(1)} %slice.137), channel_id=1, source_target_pairs={{0,8},{1,9},{2,10},{3,11},{4,12},{5,13},{6,14},{7,15},{8,0},{9,1},... | collective-permute-start | bytes 86024 | tf_op jit(solution)/shard_map/ppermute | solution.py:38

commit v14 on v11

--- a/solution.py
+++ b/solution.py
@@ -6,6 +6,7 @@
 from jax.experimental.layout import Layout, with_layout_constraint
 from jax.sharding import PartitionSpec as P
 
+CHUNKS = 2
 VMEM = pl.BlockSpec(memory_space=pltpu.VMEM)
 HBM = pl.BlockSpec(memory_space=pltpu.HBM)
 
@@ -75,7 +76,7 @@
             pltpu.SemaphoreType.DMA((3,)),
         ],
         compiler_params=pltpu.CompilerParams(vmem_limit_bytes=4 << 20),
-        cost_estimate=pl.CostEstimate(flops=20 * 10**9, bytes_accessed=4 * tokens.size, transcendentals=0),
+        cost_estimate=pl.CostEstimate(flops=0, bytes_accessed=4 * tokens.size, transcendentals=0),
     )(in_hbm(tokens), in_hbm(routes), in_hbm(numerators))
 
 
@@ -139,8 +140,6 @@
     along, across = halves(clusters), halves(members // 2)
     shared, paired = along[: len(along) - len(across)], along[len(along) - len(across) :]
 
-    other_back = trade(delta_back[0], (0, 1), (0, 1))
-
     packed = pack(tokens[0], routes[0], numerators[0])
     chips = members // 2
     pieces = {(0, 0): packed}
@@ -167,14 +166,9 @@
         places += [(x | xbit, z) for x, z in places]
         places += [(x, z | zbit) for x, z in places]
     held = by_rows(jnp.concatenate([pieces[place] for place in places]))
-    held, other_back = lax.optimization_barrier((held, other_back))
-    half = held.shape[0]
     held = by_rows(jnp.concatenate(ordered(core == 1, held, trade(held, (0, 1), (0, 1)))))
 
     codes = jnp.dot(held[:, :width], delta_in[0], preferred_element_type=jnp.float32).astype(jnp.bfloat16)
-    rank = codes.shape[1]
-    codes = jnp.stack([codes if m == 0 else trade(codes, (0, m), (0, m)) for m in range(members)])
-    by_slot = jnp.stack([lax.dynamic_index_in_dim(codes, s ^ me, 0, keepdims=False) for s in range(members)])
     projected = gate_up_product(held, base_in[0])
 
     side = by_rows(held[:, width:])
@@ -187,6 +181,9 @@
         jnp.where(position[None] == target[:, None, None], weight[None].astype(jnp.float32), 0.0), axis=-1
     )
 
+    codes = jnp.stack([codes if m == 0 else trade(codes, (0, m), (0, m)) for m in range(members)])
+    by_slot = jnp.stack([lax.dynamic_index_in_dim(codes, s ^ me, 0, keepdims=False) for s in range(members)])
+
     lifted = jnp.einsum("srk,skgf->srgf", by_slot, delta_mid[0], preferred_element_type=jnp.float32)
     total = held.shape[0]
     hidden = jax.nn.silu(projected[None, :total] + lifted[:, :, 0]) * (projected[None, total:] + lifted[:, :, 1])
@@ -194,44 +191,41 @@
     partial_codes = jnp.einsum(
         "srf,sfk->srk", hidden.astype(jnp.bfloat16), delta_down[0], preferred_element_type=jnp.float32
     ).astype(jnp.bfloat16)
-    partial_codes = partial_codes.reshape(chips, 2, 2, half, rank).transpose(0, 2, 1, 3, 4)
-    partial_codes = partial_codes.reshape(members, 2, half, rank)
     lowrank = lax.dynamic_index_in_dim(partial_codes, me, 0, keepdims=False).astype(jnp.float32)
     for m in range(1, members):
         sent = lax.dynamic_index_in_dim(partial_codes, me ^ m, 0, keepdims=False)
         lowrank = lowrank + trade(sent, (0, m), (0, m)).astype(jnp.float32)
-    kept_scale = scale.reshape(chips, 2, 2, half).transpose(0, 2, 1, 3).reshape(members, 2, half)
-    kept_scale = lax.dynamic_index_in_dim(kept_scale, me, 0, keepdims=False)
-    scaled = (kept_scale[:, :, None] * lowrank).astype(jnp.bfloat16)
-    scaled = ordered(core == 1, scaled[0], scaled[1])
-
-    base = jnp.dot(hidden_sum, base_down[0], preferred_element_type=jnp.float32)
-    kept, sent = ordered(core == 1, base[:half], base[half:])
-    total = kept + trade(sent.astype(jnp.bfloat16), (0, 1), (0, 1)).astype(jnp.float32)
-    for rows, table in zip(scaled, (delta_back[0], other_back)):
-        total = total + jnp.dot(rows, table, preferred_element_type=jnp.float32)
-    total = total.astype(jnp.bfloat16)
+    own_scale = lax.dynamic_index_in_dim(scale, me, 0, keepdims=False)
+    scaled = (own_scale[:, None] * lowrank).astype(jnp.bfloat16)
+
+    term = jnp.dot(hidden_sum, base_down[0], preferred_element_type=jnp.float32)
+    term = (term + jnp.dot(scaled, delta_back[0], preferred_element_type=jnp.float32)).astype(jnp.bfloat16)
 
     def add(kept, received):
         return (kept.astype(jnp.float32) + received.astype(jnp.float32)).astype(jnp.bfloat16)
 
-    for z, x in reversed(list(zip(paired, across))):
-        flag = (me // (2 * x)) % 2 == 1
-        size = total.shape[0] // 4
-        blocks = [total[i * size : (i + 1) * size] for i in range(4)]
-        inner = ordered(core == 1, blocks[1], blocks[2])
-        kept, sent = ordered(
-            (core == 1) & flag,
-            jnp.concatenate([blocks[0], inner[0]]),
-            jnp.concatenate([inner[1], blocks[3]]),
-        )
-        total = add(kept, trade(sent, (z, 0), (0, 2 * x)))
-        kept, sent = ordered((core == 0) & flag, total[:size], total[size:])
-        total = add(kept, trade(sent, (0, 2 * x), (z, 0)))
-    for mask in reversed(shared):
-        size = total.shape[0] // 2
-        total = add(total[:size], trade(total[size:], (mask, 0), (mask, 0)))
-    return total[None]
+    half = term.shape[0] // 2
+    kept, sent = ordered(core == 1, term[:half], term[half:])
+    outputs = []
+    for total in jnp.split(add(kept, trade(sent, (0, 1), (0, 1))), CHUNKS, axis=1):
+        for z, x in reversed(list(zip(paired, across))):
+            flag = (me // (2 * x)) % 2 == 1
+            size = total.shape[0] // 4
+            blocks = [total[i * size : (i + 1) * size] for i in range(4)]
+            inner = ordered(core == 1, blocks[1], blocks[2])
+            kept, sent = ordered(
+                (core == 1) & flag,
+                jnp.concatenate([blocks[0], inner[0]]),
+                jnp.concatenate([inner[1], blocks[3]]),
+            )
+            total = add(kept, trade(sent, (z, 0), (0, 2 * x)))
+            kept, sent = ordered((core == 0) & flag, total[:size], total[size:])
+            total = add(kept, trade(sent, (0, 2 * x), (z, 0)))
+        for mask in reversed(shared):
+            size = total.shape[0] // 2
+            total = add(total[:size], trade(total[size:], (mask, 0), (mask, 0)))
+        outputs.append(total)
+    return jnp.concatenate(outputs, axis=1)[None]
 
 
 def solution(mesh):

time: 55.3 us -> 56.4 us (1.020)
  matrix products: 7.52 us -> 2.12 us
  starting transfers between devices: 16.6 us -> 20 us
  local copies, waits for them, and re-layouts: 1.07 us -> 3.98 us
  other arithmetic: 2.12 us -> 3.22 us
  waiting for transfers between devices: 23.5 us -> 22.5 us
    dot_general x3 -> x2, matrix products: 6.66 us -> 1.25 us  [the longest x1 0.75 us: local(): term = jnp.dot(hidden_sum, base_down[0], preferred_element_type=jnp.float32)]
    ppermute x17 -> x19, starting transfers between devices: 16.6 us -> 20 us  [trade(): return lax.ppermute(value, ('expert', 'tensor'), pairs)]
    unnamed x10 -> x14, local copies, waits for them, and re-layouts: 0.43 us -> 3.43 us
    convert_element_type x2 -> x7, other arithmetic: 0.13 us -> 1.37 us  [add(): (kept.astype(jnp.float32) + received.astype(jnp.float32)).astype(jnp.bflo...]
    ppermute x17 -> x19, waiting for transfers between devices: 23.5 us -> 22.5 us  [trade(): return lax.ppermute(value, ('expert', 'tensor'), pairs)]
  transfers between devices with their start and end apart: 17 -> 19, of which waited for: 7 -> 12; matrix products, arithmetic and copies ran while one was open for 11% -> 3% of each run, Pallas kernels for 5% -> 5%
where the time goes in v14:
time: 56.4 us; the launch traced here: 56.2 us
  waiting for transfers between devices  22.5 us (40%)
  starting transfers between devices  20 us (35%)
  local copies, waits for them, and re-layouts  3.98 us (7%)
  Pallas kernels  3.93 us (7%)
  other arithmetic  3.22 us (6%)
  matrix products  2.12 us (4%)
    ppermute x19, waiting for transfers between devices, trade(): return lax.ppermute(value, ('expert', 'tensor'), pairs)  22.5 us
    ppermute x19, starting transfers between devices, trade(): return lax.ppermute(value, ('expert', 'tensor'), pairs)  20 us
    unnamed x14, local copies, waits for them, and re-layouts  3.43 us
    pallas_call x1, Pallas kernels, gate_up_product(): pl.pallas_call(gate_up_kernel, out_shape=jax.ShapeDtypeStruct((2 * x.shap...  2.95 us
    convert_element_type x7, other arithmetic, add(): (kept.astype(jnp.float32) + received.astype(jnp.float32)).astype(jnp.bflo...  1.37 us
  transfers between devices with their start and end apart: 19, of which 12 were waited for; matrix products, arithmetic and copies ran while one was open for 3% of the time, Pallas kernels for 5%

profile of v14, /device:TPU:0, one launch (start us, length us, event | category | flops | bytes accessed | tf_op | source)
XLA Modules:
  0.0 56.2 jit_solution(2225158824962231012)
XLA Ops:
  0.0 1.0 %shard_map.100 = bf16[4,7296]{1,0:T(4,128)(2,1)S(1)} custom-call(bf16[4,7168]{1,0:T(4,128)(2,1)} %bitcast.64, s32[4,8]{1,0:T(4,128)} %bitcast.69, s32[4,8]{1,0:T(4,128)} %bitcast.70), custom_call_target="tpu_custom_call" | custom-call | bytes 114688 | tf_op jit(solution)/shard_map/pallas_call | solution.py:68
  1.0 5.1 %collective-permute-start.3 = (bf16[4,7296]{1,0:T(4,128)(2,1)S(1)}, bf16[4,7296]{1,0:T(4,128)(2,1)S(1)}, u32[]{:S(2)}, u32[]{:S(2)}) collective-permute-start(bf16[4,7296]{1,0:T(4,128)(2,1)S(1)} %shard_map.100), channel_id=1, source_target_pairs={{0,12},{1,13},{2,14},{3,15},{4,8},{5,9},{6,10},{7,11},{8,4},{9,5},... | collective-permute-start | bytes 175112 | tf_op jit(solution)/shard_map/ppermute | solution.py:34
  6.1 0.6 %collective-permute-start.1 = (bf16[4,7296]{1,0:T(4,128)(2,1)S(1)}, bf16[4,7296]{1,0:T(4,128)(2,1)S(1)}, u32[]{:S(2)}, u32[]{:S(2)}) collective-permute-start(bf16[4,7296]{1,0:T(4,128)(2,1)S(1)} %shard_map.100), channel_id=1, source_target_pairs={{0,4},{1,5},{2,6},{3,7},{4,0},{5,1},{6,2},{7,3},{8,12},{9,13},{10,... | collective-permute-start | bytes 175112 | tf_op jit(solution)/shard_map/ppermute | solution.py:34
  6.7 1.6 %collective-permute-start = (bf16[4,7296]{1,0:T(4,128)(2,1)S(1)}, bf16[4,7296]{1,0:T(4,128)(2,1)S(1)}, u32[]{:S(2)}, u32[]{:S(2)}) collective-permute-start(bf16[4,7296]{1,0:T(4,128)(2,1)S(1)} %shard_map.100), channel_id=1, source_target_pairs={{0,2},{1,3},{2,0},{3,1},{4,6},{5,7},{6,4},{7,5},{8,10},{9,11},{10,... | collective-permute-start | bytes 175112 | tf_op jit(solution)/shard_map/ppermute | solution.py:34
  8.4 0.1 collective-permute-done.3
  8.5 2.7 %collective-permute-done.2 = bf16[4,7296]{1,0:T(4,128)(2,1)S(1)} collective-permute-done((bf16[4,7296]{1,0:T(4,128)(2,1)S(1)}, bf16[4,7296]{1,0:T(4,128)(2,1)S(1)}, u32[]{:S(2)}, u32[]{:S(2)}) %collective-permute-start.2) | collective-permute-done | bytes 58400 | tf_op jit(solution)/shard_map/ppermute | solution.py:34
  11.2 0.1 pad_maximum_fusion.1
  11.3 1.6 %collective-permute-start.4 = (bf16[12,7296]{1,0:T(8,128)(2,1)S(1)}, bf16[12,7296]{1,0:T(8,128)(2,1)S(1)}, u32[]{:S(2)}, u32[]{:S(2)}) collective-permute-start(bf16[12,7296]{1,0:T(8,128)(2,1)S(1)} %pad_maximum_fusion.1), channel_id=1, source_target_pairs={{0,2},{1,3},{2,0},{3,1},{4,6},{5,7},{6,4},{7,5},{8,10},{9,11},{10,... | collective-permute-start | bytes 525320 | tf_op jit(solution)/shard_map/ppermute | solution.py:34
  13.0 5.1 %collective-permute-done.4 = bf16[12,7296]{1,0:T(8,128)(2,1)S(1)} collective-permute-done((bf16[12,7296]{1,0:T(8,128)(2,1)S(1)}, bf16[12,7296]{1,0:T(8,128)(2,1)S(1)}, u32[]{:S(2)}, u32[]{:S(2)}) %collective-permute-start.4) | collective-permute-done | bytes 175136 | tf_op jit(solution)/shard_map/ppermute | solution.py:34
  18.2 0.2 broadcast_select_fusion.5
  18.3 0.3 concatenate.25
  18.8 1.8 %collective-permute-done.5 = bf16[32,7296]{1,0:T(8,128)(2,1)S(1)} collective-permute-done((bf16[32,7296]{1,0:T(8,128)(2,1)S(1)}, bf16[32,7296]{1,0:T(8,128)(2,1)S(1)}, u32[]{:S(2)}, u32[]{:S(2)}) %collective-permute-start.5) | collective-permute-done | bytes 466976 | tf_op jit(solution)/shard_map/ppermute | solution.py:34
  20.6 0.1 broadcast_select_fusion.1
  20.6 0.2 convert_reduce_fusion
  20.8 0.5 fusion.6
  21.3 1.4 %collective-permute-start.8 = (bf16[64,128]{1,0:T(8,128)(2,1)S(1)}, bf16[64,128]{1,0:T(8,128)(2,1)S(1)}, u32[]{:S(2)}, u32[]{:S(2)}) collective-permute-start(bf16[64,128]{1,0:T(8,128)(2,1)S(1)} %fusion.6), channel_id=1, source_target_pairs={{0,3},{1,2},{2,1},{3,0},{4,7},{5,6},{6,5},{7,4},{8,11},{9,10},{10,... | collective-permute-start | bytes 49160 | tf_op jit(solution)/shard_map/ppermute | solution.py:34
  22.7 0.5 collective-permute-start.7
  23.2 0.1 collective-permute-start.6
  23.3 0.1 fusion.33
  23.5 3.1 %copy-done.1 = bf16[1,7168,2,256]{3,2,1,0:T(2,128)(2,1)S(1)} copy-done((bf16[1,7168,2,256]{3,2,1,0:T(2,128)(2,1)S(1)}, bf16[1,7168,2,256]{3,2,1,0:T(2,128)(2,1)}, u32[]{:S(2)}) %copy-start.1) | copy-done | bytes 7340056
  26.6 3.0 %shard_map.101 = f32[128,256]{1,0:T(8,128)S(1)} custom-call(bf16[64,7296]{1,0:T(8,128)(2,1)S(1)} %pad_maximum_fusion.x, bf16[7168,2,256]{2,1,0:T(2,128)(2,1)S(1)} %bitcast.62), custom_call_target="tpu_custom_call" | custom-call | flops 469762048 | bytes 7340032 | tf_op jit(solution)/shard_map/pallas_call | solution.py:108
  29.6 0.1 select_reduce_fusion
  29.7 0.1 select_reduce_fusion.1
  29.9 0.2 fusion.11
  30.1 0.1 multiply_reduce_fusion
  30.2 0.3 copy-done.4
  30.5 0.2 convolution_convert_fusion
  30.8 0.5 collective-permute-start.9
  31.3 1.3 %collective-permute-start.11 = (bf16[64,128]{1,0:T(8,128)(2,1)S(1)}, bf16[64,128]{1,0:T(8,128)(2,1)S(1)}, u32[]{:S(2)}, u32[]{:S(2)}) collective-permute-start(bf16[64,128]{1,0:T(8,128)(2,1)S(1)} %get-tuple-element.34), channel_id=1, source_target_pairs={{0,3},{1,2},{2,1},{3,0},{4,7},{5,6},{6,5},{7,4},{8,11},{9,10},{10,... | collective-permute-start | bytes 49160 | tf_op jit(solution)/shard_map/ppermute | solution.py:34
  32.5 0.4 collective-permute-start.10
  33.0 0.8 %fusion.1 = f32[64,7168]{1,0:T(8,128)S(1)} fusion(bf16[1,256,7168]{2,1,0:T(8,128)(2,1)S(1)} %copy-done.2, bf16[64,256]{1,0:T(8,128)(2,1)S(1)} %get-tuple-element.5), kind=kOutput, calls=%fused_computation.2 | convolution fusion | flops 234881024 | bytes 5537792 | tf_op jit(solution)/shard_map/dot_general | solution.py:201
  33.7 0.7 %collective-permute-done.11 = bf16[64,128]{1,0:T(8,128)(2,1)S(1)} collective-permute-done((bf16[64,128]{1,0:T(8,128)(2,1)S(1)}, bf16[64,128]{1,0:T(8,128)(2,1)S(1)}, u32[]{:S(2)}, u32[]{:S(2)}) %collective-permute-start.11) | collective-permute-done | bytes 16416 | tf_op jit(solution)/shard_map/ppermute | solution.py:34
  34.4 1.8 %collective-permute-done.10 = bf16[64,128]{1,0:T(8,128)(2,1)S(1)} collective-permute-done((bf16[64,128]{1,0:T(8,128)(2,1)S(1)}, bf16[64,128]{1,0:T(8,128)(2,1)S(1)}, u32[]{:S(2)}, u32[]{:S(2)}) %collective-permute-start.10) | collective-permute-done | bytes 16416 | tf_op jit(solution)/shard_map/ppermute | solution.py:34
  36.3 0.5 fusion
  36.9 1.9 %collective-permute-done.12 = bf16[32,7168]{1,0:T(8,128)(2,1)} collective-permute-done((bf16[32,7168]{1,0:T(8,128)(2,1)S(1)}, bf16[32,7168]{1,0:T(8,128)(2,1)}, u32[]{:S(2)}, u32[]{:S(2)}) %collective-permute-start.12) | collective-permute-done | bytes 458784 | tf_op jit(solution)/shard_map/ppermute | solution.py:34
  38.8 1.2 %add_convert_fusion = bf16[32,7168]{1,0:T(8,128)(2,1)S(1)} fusion(bf16[32,7168]{1,0:T(8,128)(2,1)} %collective-permute-done.12, pred[]{:T(512)S(6)} %eq.28, bf16[64,7168]{1,0:T(8,128)(2,1)S(1)} %fusion), kind=kLoop, calls=%fused_computation.17 | loop fusion | flops 1146880 | bytes 1835009 | tf_op jit(solution)/shard_map/convert_element_type | solution.py:205
  40.1 0.6 %collective-permute-start.16 = (bf16[16,3584]{1,0:T(8,128)(2,1)S(1)}, bf16[16,3584]{1,0:T(8,128)(2,1)S(1)}, u32[]{:S(2)}, u32[]{:S(2)}) collective-permute-start(bf16[16,3584]{1,0:T(8,128)(2,1)S(1)} %broadcast_select_fusion.3), channel_id=1, source_target_pairs={{0,4},{1,3},{2,6},{3,1},{4,0},{5,7},{6,2},{7,5},{8,12},{9,11},{10,... | collective-permute-start | bytes 344072 | tf_op jit(solution)/shard_map/ppermute | solution.py:34
  40.8 1.5 %collective-permute-start.13 = (bf16[16,3584]{1,0:T(8,128)(2,1)S(1)}, bf16[16,3584]{1,0:T(8,128)(2,1)S(1)}, u32[]{:S(2)}, u32[]{:S(2)}) collective-permute-start(bf16[16,3584]{1,0:T(8,128)(2,1)S(1)} %broadcast_select_fusion.4), channel_id=1, source_target_pairs={{0,4},{1,3},{2,6},{3,1},{4,0},{5,7},{6,2},{7,5},{8,12},{9,11},{10,... | collective-permute-start | bytes 344072 | tf_op jit(solution)/shard_map/ppermute | solution.py:34
  42.3 2.7 %collective-permute-done.16 = bf16[16,3584]{1,0:T(8,128)(2,1)S(1)} collective-permute-done((bf16[16,3584]{1,0:T(8,128)(2,1)S(1)}, bf16[16,3584]{1,0:T(8,128)(2,1)S(1)}, u32[]{:S(2)}, u32[]{:S(2)}) %collective-permute-start.16) | collective-permute-done | bytes 114720 | tf_op jit(solution)/shard_map/ppermute | solution.py:34
  45.0 0.5 collective-permute-start.17
  45.5 0.7 %collective-permute-done.13 = bf16[16,3584]{1,0:T(8,128)(2,1)S(1)} collective-permute-done((bf16[16,3584]{1,0:T(8,128)(2,1)S(1)}, bf16[16,3584]{1,0:T(8,128)(2,1)S(1)}, u32[]{:S(2)}, u32[]{:S(2)}) %collective-permute-start.13) | collective-permute-done | bytes 114720 | tf_op jit(solution)/shard_map/ppermute | solution.py:34
  46.3 1.0 %collective-permute-start.14 = (bf16[8,3584]{1,0:T(8,128)(2,1)S(1)}, bf16[8,3584]{1,0:T(8,128)(2,1)S(1)}, u32[]{:S(2)}, u32[]{:S(2)}) collective-permute-start(bf16[8,3584]{1,0:T(8,128)(2,1)S(1)} %broadcast_select_fusion.18), channel_id=1, source_target_pairs={{0,2},{1,5},{2,0},{3,7},{4,6},{5,1},{6,4},{7,3},{8,10},{9,13},{10,... | collective-permute-start | bytes 172040 | tf_op jit(solution)/shard_map/ppermute | solution.py:34
  47.3 2.0 %collective-permute-done.17 = bf16[8,3584]{1,0:T(8,128)(2,1)S(1)} collective-permute-done((bf16[8,3584]{1,0:T(8,128)(2,1)S(1)}, bf16[8,3584]{1,0:T(8,128)(2,1)S(1)}, u32[]{:S(2)}, u32[]{:S(2)}) %collective-permute-start.17) | collective-permute-done | bytes 57376 | tf_op jit(solution)/shard_map/ppermute | solution.py:34
  49.3 1.3 %collective-permute-start.18 = (bf16[4,3584]{1,0:T(4,128)(2,1)S(1)}, bf16[4,3584]{1,0:T(4,128)(2,1)S(1)}, u32[]{:S(2)}, u32[]{:S(2)}) collective-permute-start(bf16[4,3584]{1,0:T(4,128)(2,1)S(1)} %slice.156), channel_id=1, source_target_pairs={{0,8},{1,9},{2,10},{3,11},{4,12},{5,13},{6,14},{7,15},{8,0},{9,1},... | collective-permute-start | bytes 86024 | tf_op jit(solution)/shard_map/ppermute | solution.py:34
  50.7 1.8 %collective-permute-start.15 = (bf16[4,3584]{1,0:T(4,128)(2,1)S(1)}, bf16[4,3584]{1,0:T(4,128)(2,1)S(1)}, u32[]{:S(2)}, u32[]{:S(2)}) collective-permute-start(bf16[4,3584]{1,0:T(4,128)(2,1)S(1)} %slice.148), channel_id=1, source_target_pairs={{0,8},{1,9},{2,10},{3,11},{4,12},{5,13},{6,14},{7,15},{8,0},{9,1},... | collective-permute-start | bytes 86024 | tf_op jit(solution)/shard_map/ppermute | solution.py:34
  52.5 2.0 %collective-permute-done.18 = bf16[4,3584]{1,0:T(4,128)(2,1)S(1)} collective-permute-done((bf16[4,3584]{1,0:T(4,128)(2,1)S(1)}, bf16[4,3584]{1,0:T(4,128)(2,1)S(1)}, u32[]{:S(2)}, u32[]{:S(2)}) %collective-permute-start.18) | collective-permute-done | bytes 28704 | tf_op jit(solution)/shard_map/ppermute | solution.py:34
  54.5 1.0 %collective-permute-done.15 = bf16[4,3584]{1,0:T(4,128)(2,1)S(1)} collective-permute-done((bf16[4,3584]{1,0:T(4,128)(2,1)S(1)}, bf16[4,3584]{1,0:T(4,128)(2,1)S(1)}, u32[]{:S(2)}, u32[]{:S(2)}) %collective-permute-start.15) | collective-permute-done | bytes 28704 | tf_op jit(solution)/shard_map/ppermute | solution.py:34
  55.5 0.7 %maximum_bitcast_fusion.2 = bf16[1,4,7168]{2,1,0:T(4,128)(2,1)} fusion(bf16[4,3584]{1,0:T(4,128)(2,1)S(1)} %add_convert_fusion.5, bf16[4,3584]{1,0:T(4,128)(2,1)S(1)} %add_convert_fusion.6), kind=kLoop, calls=%fused_computation.60 | loop fusion | flops 114688 | bytes 114688 | tf_op jit(solution)/shard_map/broadcast_in_dim | solution.py:228
  (47 shorter events, 0.9 us)
Async XLA Ops:
  0.0 36.3 %copy-start = (bf16[1,128,7168]{2,1,0:T(8,128)(2,1)S(1)}, bf16[1,128,7168]{2,1,0:T(8,128)(2,1)}, u32[]{:S(2)}) copy-start(bf16[1,128,7168]{2,1,0:T(8,128)(2,1)} %param.19) | copy-start | bytes 5505028
  1.0 7.5 %collective-permute-start.3 = (bf16[4,7296]{1,0:T(4,128)(2,1)S(1)}, bf16[4,7296]{1,0:T(4,128)(2,1)S(1)}, u32[]{:S(2)}, u32[]{:S(2)}) collective-permute-start(bf16[4,7296]{1,0:T(4,128)(2,1)S(1)} %shard_map.100), channel_id=1, source_target_pairs={{0,12},{1,13},{2,14},{3,15},{4,8},{5,9},{6,10},{7,11},{8,4},{9,5},... | collective-permute-start | bytes 175112 | tf_op jit(solution)/shard_map/ppermute | solution.py:34
  6.1 5.1 %collective-permute-start.2 = (bf16[4,7296]{1,0:T(4,128)(2,1)S(1)}, bf16[4,7296]{1,0:T(4,128)(2,1)S(1)}, u32[]{:S(2)}, u32[]{:S(2)}) collective-permute-start(bf16[4,7296]{1,0:T(4,128)(2,1)S(1)} %shard_map.100), channel_id=1, source_target_pairs={{0,8},{1,9},{2,10},{3,11},{4,12},{5,13},{6,14},{7,15},{8,0},{9,1},... | collective-permute-start | bytes 175112 | tf_op jit(solution)/shard_map/ppermute | solution.py:34
  6.1 5.1 %collective-permute-start.1 = (bf16[4,7296]{1,0:T(4,128)(2,1)S(1)}, bf16[4,7296]{1,0:T(4,128)(2,1)S(1)}, u32[]{:S(2)}, u32[]{:S(2)}) collective-permute-start(bf16[4,7296]{1,0:T(4,128)(2,1)S(1)} %shard_map.100), channel_id=1, source_target_pairs={{0,4},{1,5},{2,6},{3,7},{4,0},{5,1},{6,2},{7,3},{8,12},{9,13},{10,... | collective-permute-start | bytes 175112 | tf_op jit(solution)/shard_map/ppermute | solution.py:34
  6.7 6.2 %collective-permute-start = (bf16[4,7296]{1,0:T(4,128)(2,1)S(1)}, bf16[4,7296]{1,0:T(4,128)(2,1)S(1)}, u32[]{:S(2)}, u32[]{:S(2)}) collective-permute-start(bf16[4,7296]{1,0:T(4,128)(2,1)S(1)} %shard_map.100), channel_id=1, source_target_pairs={{0,2},{1,3},{2,0},{3,1},{4,6},{5,7},{6,4},{7,5},{8,10},{9,11},{10,... | collective-permute-start | bytes 175112 | tf_op jit(solution)/shard_map/ppermute | solution.py:34
  11.3 6.8 %collective-permute-start.4 = (bf16[12,7296]{1,0:T(8,128)(2,1)S(1)}, bf16[12,7296]{1,0:T(8,128)(2,1)S(1)}, u32[]{:S(2)}, u32[]{:S(2)}) collective-permute-start(bf16[12,7296]{1,0:T(8,128)(2,1)S(1)} %pad_maximum_fusion.1), channel_id=1, source_target_pairs={{0,2},{1,3},{2,0},{3,1},{4,6},{5,7},{6,4},{7,5},{8,10},{9,11},{10,... | collective-permute-start | bytes 525320 | tf_op jit(solution)/shard_map/ppermute | solution.py:34
  18.7 1.9 %collective-permute-start.5 = (bf16[32,7296]{1,0:T(8,128)(2,1)S(1)}, bf16[32,7296]{1,0:T(8,128)(2,1)S(1)}, u32[]{:S(2)}, u32[]{:S(2)}) collective-permute-start(bf16[32,7296]{1,0:T(8,128)(2,1)S(1)} %concatenate.25), channel_id=1, source_target_pairs={{0,1},{1,0},{2,3},{3,2},{4,5},{5,4},{6,7},{7,6},{8,9},{9,8},{10,11... | collective-permute-start | bytes 1400840 | tf_op jit(solution)/shard_map/ppermute | solution.py:34
  18.8 2.0 %copy-start.6 = (bf16[1,7168,128]{2,1,0:T(8,128)(2,1)S(1)}, bf16[1,7168,128]{2,1,0:T(8,128)(2,1)}, u32[]{:S(2)}) copy-start(bf16[1,7168,128]{2,1,0:T(8,128)(2,1)} %param.16) | copy-start | bytes 5505028
  21.3 8.5 %collective-permute-start.8 = (bf16[64,128]{1,0:T(8,128)(2,1)S(1)}, bf16[64,128]{1,0:T(8,128)(2,1)S(1)}, u32[]{:S(2)}, u32[]{:S(2)}) collective-permute-start(bf16[64,128]{1,0:T(8,128)(2,1)S(1)} %fusion.6), channel_id=1, source_target_pairs={{0,3},{1,2},{2,1},{3,0},{4,7},{5,6},{6,5},{7,4},{8,11},{9,10},{10,... | collective-permute-start | bytes 49160 | tf_op jit(solution)/shard_map/ppermute | solution.py:34
  22.7 7.1 %collective-permute-start.7 = (bf16[64,128]{1,0:T(8,128)(2,1)S(1)}, bf16[64,128]{1,0:T(8,128)(2,1)S(1)}, u32[]{:S(2)}, u32[]{:S(2)}) collective-permute-start(bf16[64,128]{1,0:T(8,128)(2,1)S(1)} %fusion.6), channel_id=1, source_target_pairs={{0,2},{1,3},{2,0},{3,1},{4,6},{5,7},{6,4},{7,5},{8,10},{9,11},{10,... | collective-permute-start | bytes 49160 | tf_op jit(solution)/shard_map/ppermute | solution.py:34
  23.2 6.7 %collective-permute-start.6 = (bf16[64,128]{1,0:T(8,128)(2,1)S(1)}, bf16[64,128]{1,0:T(8,128)(2,1)S(1)}, u32[]{:S(2)}, u32[]{:S(2)}) collective-permute-start(bf16[64,128]{1,0:T(8,128)(2,1)S(1)} %fusion.6), channel_id=1, source_target_pairs={{0,1},{1,0},{2,3},{3,2},{4,5},{5,4},{6,7},{7,6},{8,9},{9,8},{10,11... | collective-permute-start | bytes 49160 | tf_op jit(solution)/shard_map/ppermute | solution.py:34
  23.5 3.1 %copy-start.1 = (bf16[1,7168,2,256]{3,2,1,0:T(2,128)(2,1)S(1)}, bf16[1,7168,2,256]{3,2,1,0:T(2,128)(2,1)}, u32[]{:S(2)}) copy-start(bf16[1,7168,2,256]{3,2,1,0:T(2,128)(2,1)} %param.14) | copy-start | bytes 22020100
  26.6 3.0 %copy-start.5 = (s32[16]{0:T(128)S(1)}, s32[16]{0:T(128)}, u32[]{:S(2)}) copy-start(s32[16]{0:T(128)} %param.13) | copy-start | bytes 196
  26.6 3.3 %copy-start.3 = (bf16[1,4,128,2,256]{4,3,2,1,0:T(2,128)(2,1)S(1)}, bf16[1,4,128,2,256]{4,3,2,1,0:T(2,128)(2,1)}, u32[]{:S(2)}) copy-start(bf16[1,4,128,2,256]{4,3,2,1,0:T(2,128)(2,1)} %param.17) | copy-start | bytes 1572868
  26.6 6.3 %copy-start.2 = (bf16[1,256,7168]{2,1,0:T(8,128)(2,1)S(1)}, bf16[1,256,7168]{2,1,0:T(8,128)(2,1)}, u32[]{:S(2)}) copy-start(bf16[1,256,7168]{2,1,0:T(8,128)(2,1)} %param.15) | copy-start | bytes 11010052
  29.6 1.0 %copy-start.4 = (bf16[1,4,256,128]{3,2,1,0:T(8,128)(2,1)S(1)}, bf16[1,4,256,128]{3,2,1,0:T(8,128)(2,1)}, u32[]{:S(2)}) copy-start(bf16[1,4,256,128]{3,2,1,0:T(8,128)(2,1)} %param.18) | copy-start | bytes 786436
  30.8 3.0 %collective-permute-start.9 = (bf16[64,128]{1,0:T(8,128)(2,1)S(1)}, bf16[64,128]{1,0:T(8,128)(2,1)S(1)}, u32[]{:S(2)}, u32[]{:S(2)}) collective-permute-start(bf16[64,128]{1,0:T(8,128)(2,1)S(1)} %get-tuple-element.33), channel_id=1, source_target_pairs={{0,1},{1,0},{2,3},{3,2},{4,5},{5,4},{6,7},{7,6},{8,9},{9,8},{10,11... | collective-permute-start | bytes 49160 | tf_op jit(solution)/shard_map/ppermute | solution.py:34
  31.3 3.2 %collective-permute-start.11 = (bf16[64,128]{1,0:T(8,128)(2,1)S(1)}, bf16[64,128]{1,0:T(8,128)(2,1)S(1)}, u32[]{:S(2)}, u32[]{:S(2)}) collective-permute-start(bf16[64,128]{1,0:T(8,128)(2,1)S(1)} %get-tuple-element.34), channel_id=1, source_target_pairs={{0,3},{1,2},{2,1},{3,0},{4,7},{5,6},{6,5},{7,4},{8,11},{9,10},{10,... | collective-permute-start | bytes 49160 | tf_op jit(solution)/shard_map/ppermute | solution.py:34
  32.5 3.7 %collective-permute-start.10 = (bf16[64,128]{1,0:T(8,128)(2,1)S(1)}, bf16[64,128]{1,0:T(8,128)(2,1)S(1)}, u32[]{:S(2)}, u32[]{:S(2)}) collective-permute-start(bf16[64,128]{1,0:T(8,128)(2,1)S(1)} %get-tuple-element.35), channel_id=1, source_target_pairs={{0,2},{1,3},{2,0},{3,1},{4,6},{5,7},{6,4},{7,5},{8,10},{9,11},{10,... | collective-permute-start | bytes 49160 | tf_op jit(solution)/shard_map/ppermute | solution.py:34
  36.8 2.0 %collective-permute-start.12 = (bf16[32,7168]{1,0:T(8,128)(2,1)S(1)}, bf16[32,7168]{1,0:T(8,128)(2,1)}, u32[]{:S(2)}, u32[]{:S(2)}) collective-permute-start(bf16[32,7168]{1,0:T(8,128)(2,1)S(1)} %broadcast_select_fusion.2), channel_id=1, source_target_pairs={{0,1},{1,0},{2,3},{3,2},{4,5},{5,4},{6,7},{7,6},{8,9},{9,8},{10,11... | collective-permute-start | bytes 1376264 | tf_op jit(solution)/shard_map/ppermute | solution.py:34
  40.1 4.9 %collective-permute-start.16 = (bf16[16,3584]{1,0:T(8,128)(2,1)S(1)}, bf16[16,3584]{1,0:T(8,128)(2,1)S(1)}, u32[]{:S(2)}, u32[]{:S(2)}) collective-permute-start(bf16[16,3584]{1,0:T(8,128)(2,1)S(1)} %broadcast_select_fusion.3), channel_id=1, source_target_pairs={{0,4},{1,3},{2,6},{3,1},{4,0},{5,7},{6,2},{7,5},{8,12},{9,11},{10,... | collective-permute-start | bytes 344072 | tf_op jit(solution)/shard_map/ppermute | solution.py:34
  40.8 5.4 %collective-permute-start.13 = (bf16[16,3584]{1,0:T(8,128)(2,1)S(1)}, bf16[16,3584]{1,0:T(8,128)(2,1)S(1)}, u32[]{:S(2)}, u32[]{:S(2)}) collective-permute-start(bf16[16,3584]{1,0:T(8,128)(2,1)S(1)} %broadcast_select_fusion.4), channel_id=1, source_target_pairs={{0,4},{1,3},{2,6},{3,1},{4,0},{5,7},{6,2},{7,5},{8,12},{9,11},{10,... | collective-permute-start | bytes 344072 | tf_op jit(solution)/shard_map/ppermute | solution.py:34
  45.0 4.2 %collective-permute-start.17 = (bf16[8,3584]{1,0:T(8,128)(2,1)S(1)}, bf16[8,3584]{1,0:T(8,128)(2,1)S(1)}, u32[]{:S(2)}, u32[]{:S(2)}) collective-permute-start(bf16[8,3584]{1,0:T(8,128)(2,1)S(1)} %broadcast_select_fusion.17), channel_id=1, source_target_pairs={{0,2},{1,5},{2,0},{3,7},{4,6},{5,1},{6,4},{7,3},{8,10},{9,13},{10,... | collective-permute-start | bytes 172040 | tf_op jit(solution)/shard_map/ppermute | solution.py:34
  46.3 4.3 %collective-permute-start.14 = (bf16[8,3584]{1,0:T(8,128)(2,1)S(1)}, bf16[8,3584]{1,0:T(8,128)(2,1)S(1)}, u32[]{:S(2)}, u32[]{:S(2)}) collective-permute-start(bf16[8,3584]{1,0:T(8,128)(2,1)S(1)} %broadcast_select_fusion.18), channel_id=1, source_target_pairs={{0,2},{1,5},{2,0},{3,7},{4,6},{5,1},{6,4},{7,3},{8,10},{9,13},{10,... | collective-permute-start | bytes 172040 | tf_op jit(solution)/shard_map/ppermute | solution.py:34
  49.3 5.1 %collective-permute-start.18 = (bf16[4,3584]{1,0:T(4,128)(2,1)S(1)}, bf16[4,3584]{1,0:T(4,128)(2,1)S(1)}, u32[]{:S(2)}, u32[]{:S(2)}) collective-permute-start(bf16[4,3584]{1,0:T(4,128)(2,1)S(1)} %slice.156), channel_id=1, source_target_pairs={{0,8},{1,9},{2,10},{3,11},{4,12},{5,13},{6,14},{7,15},{8,0},{9,1},... | collective-permute-start | bytes 86024 | tf_op jit(solution)/shard_map/ppermute | solution.py:34
  50.7 4.8 %collective-permute-start.15 = (bf16[4,3584]{1,0:T(4,128)(2,1)S(1)}, bf16[4,3584]{1,0:T(4,128)(2,1)S(1)}, u32[]{:S(2)}, u32[]{:S(2)}) collective-permute-start(bf16[4,3584]{1,0:T(4,128)(2,1)S(1)} %slice.148), channel_id=1, source_target_pairs={{0,8},{1,9},{2,10},{3,11},{4,12},{5,13},{6,14},{7,15},{8,0},{9,1},... | collective-permute-start | bytes 86024 | tf_op jit(solution)/shard_map/ppermute | solution.py:34

commit v15 on v14

--- a/solution.py
+++ b/solution.py
@@ -1,3 +1,5 @@
+import functools
+
 import jax
 import jax.numpy as jnp
 from jax import lax
@@ -76,7 +78,7 @@
             pltpu.SemaphoreType.DMA((3,)),
         ],
         compiler_params=pltpu.CompilerParams(vmem_limit_bytes=4 << 20),
-        cost_estimate=pl.CostEstimate(flops=0, bytes_accessed=4 * tokens.size, transcendentals=0),
+        cost_estimate=pl.CostEstimate(flops=20 * 10**9, bytes_accessed=4 * tokens.size, transcendentals=0),
     )(in_hbm(tokens), in_hbm(routes), in_hbm(numerators))
 
 
@@ -117,6 +119,58 @@
     )(x, base)
 
 
+def join_kernel(own, received, joined):
+    half = own.shape[0]
+    core = lax.axis_index("tensor") % 2
+    joined[pl.ds(pl.multiple_of(core * half, half), half), :] = own[...]
+    joined[pl.ds(pl.multiple_of((1 - core) * half, half), half), :] = received[...]
+
+
+def join(own, received):
+    rows, width = own.shape
+    return pl.pallas_call(
+        join_kernel,
+        out_shape=jax.ShapeDtypeStruct((2 * rows, width), own.dtype),
+        in_specs=[VMEM, VMEM],
+        out_specs=VMEM,
+        compiler_params=pltpu.CompilerParams(vmem_limit_bytes=16 << 20),
+        cost_estimate=pl.CostEstimate(flops=0, bytes_accessed=6 * own.size, transcendentals=0),
+    )(own, received)
+
+
+def part_kernel(bit, term, received, *refs):
+    *outs, total = refs
+    half, width = total.shape
+    size, step = half // 4, width // (len(outs) // 2)
+    me = lax.axis_index("tensor")
+    core, flag = me % 2, (me // (2 * bit)) % 2
+    total[...] = term[pl.ds(pl.multiple_of(core * half, half), half), :].astype(jnp.float32) + received[
+        ...
+    ].astype(jnp.float32)
+    sent = (2 - core * (1 + flag), 3 - core * flag)
+    kept = (core * flag, 1 + core * (1 + flag))
+    for i, out in enumerate(outs):
+        columns = pl.ds((i // 2) * step, step)
+        rows = [
+            total[pl.ds(pl.multiple_of(block * size, size), size), columns] for block in (sent, kept)[i % 2]
+        ]
+        out[...] = jnp.concatenate(rows).astype(out.dtype)
+
+
+def add_and_part(term, received, bit):
+    half, width = received.shape
+    outs = pl.pallas_call(
+        functools.partial(part_kernel, bit),
+        out_shape=[jax.ShapeDtypeStruct((half // 2, width // CHUNKS), term.dtype)] * (2 * CHUNKS),
+        in_specs=[VMEM, VMEM],
+        out_specs=[VMEM] * (2 * CHUNKS),
+        scratch_shapes=[pltpu.VMEM((half, width), jnp.float32)],
+        compiler_params=pltpu.CompilerParams(vmem_limit_bytes=16 << 20),
+        cost_estimate=pl.CostEstimate(flops=0, bytes_accessed=6 * received.size, transcendentals=0),
+    )(term, received)
+    return list(zip(outs[::2], outs[1::2]))
+
+
 def local(
     tokens,
     routes,
@@ -166,7 +220,7 @@
         places += [(x | xbit, z) for x, z in places]
         places += [(x, z | zbit) for x, z in places]
     held = by_rows(jnp.concatenate([pieces[place] for place in places]))
-    held = by_rows(jnp.concatenate(ordered(core == 1, held, trade(held, (0, 1), (0, 1)))))
+    held = join(held, trade(held, (0, 1), (0, 1)))
 
     codes = jnp.dot(held[:, :width], delta_in[0], preferred_element_type=jnp.float32).astype(jnp.bfloat16)
     projected = gate_up_product(held, base_in[0])
@@ -205,20 +259,22 @@
         return (kept.astype(jnp.float32) + received.astype(jnp.float32)).astype(jnp.bfloat16)
 
     half = term.shape[0] // 2
-    kept, sent = ordered(core == 1, term[:half], term[half:])
+    sent = ordered(core == 1, term[half:], term[:half])[0]
     outputs = []
-    for total in jnp.split(add(kept, trade(sent, (0, 1), (0, 1))), CHUNKS, axis=1):
-        for z, x in reversed(list(zip(paired, across))):
+    for sent, kept in add_and_part(term, trade(sent, (0, 1), (0, 1)), across[-1]):
+        for i, (z, x) in enumerate(reversed(list(zip(paired, across)))):
             flag = (me // (2 * x)) % 2 == 1
-            size = total.shape[0] // 4
-            blocks = [total[i * size : (i + 1) * size] for i in range(4)]
-            inner = ordered(core == 1, blocks[1], blocks[2])
-            kept, sent = ordered(
-                (core == 1) & flag,
-                jnp.concatenate([blocks[0], inner[0]]),
-                jnp.concatenate([inner[1], blocks[3]]),
-            )
+            if i:
+                size = total.shape[0] // 4
+                blocks = [total[j * size : (j + 1) * size] for j in range(4)]
+                inner = ordered(core == 1, blocks[1], blocks[2])
+                kept, sent = ordered(
+                    (core == 1) & flag,
+                    jnp.concatenate([blocks[0], inner[0]]),
+                    jnp.concatenate([inner[1], blocks[3]]),
+                )
             total = add(kept, trade(sent, (z, 0), (0, 2 * x)))
+            size = total.shape[0] // 2
             kept, sent = ordered((core == 0) & flag, total[:size], total[size:])
             total = add(kept, trade(sent, (0, 2 * x), (z, 0)))
         for mask in reversed(shared):

time: 56.4 us -> 58.1 us (1.030)
  local copies, waits for them, and re-layouts: 3.98 us -> 6.94 us
  waiting for transfers between devices: 22.5 us -> 19.6 us
  matrix products: 2.12 us -> 4.11 us
  other arithmetic: 3.22 us -> 1.75 us
  starting transfers between devices: 20 us -> 20.8 us
    unnamed x14 -> x16, local copies, waits for them, and re-layouts: 3.43 us -> 6.38 us
    ppermute x19, waiting for transfers between devices: 22.5 us -> 19.6 us  [trade(): return lax.ppermute(value, ('expert', 'tensor'), pairs)]
    dot_general x1, matrix products: 0.75 us -> 2.79 us  [local(): term = jnp.dot(hidden_sum, base_down[0], preferred_element_type=jnp.float32)]
    convert_element_type x7 -> x6, other arithmetic: 1.37 us -> 0.15 us  [add(): (kept.astype(jnp.float32) + received.astype(jnp.float32)).astype(jnp.bflo...]
    ppermute x19, starting transfers between devices: 20 us -> 20.8 us  [trade(): return lax.ppermute(value, ('expert', 'tensor'), pairs)]
  transfers between devices with their start and end apart: 19 -> 19, of which waited for: 12 -> 10; matrix products, arithmetic and copies ran while one was open for 3% -> 6% of each run, Pallas kernels for 5% -> 5%
where the time goes in v15:
time: 58.1 us; the launch traced here: 57.8 us
  starting transfers between devices  20.8 us (36%)
  waiting for transfers between devices  19.6 us (34%)
  local copies, waits for them, and re-layouts  6.94 us (12%)
  Pallas kernels  4.2 us (7%)
  matrix products  4.11 us (7%)
  other arithmetic  1.75 us (3%)
    ppermute x19, starting transfers between devices, trade(): return lax.ppermute(value, ('expert', 'tensor'), pairs)  20.8 us
    ppermute x19, waiting for transfers between devices, trade(): return lax.ppermute(value, ('expert', 'tensor'), pairs)  19.6 us
    unnamed x16, local copies, waits for them, and re-layouts  6.38 us
    pallas_call x1, Pallas kernels, gate_up_product(): pl.pallas_call(gate_up_kernel, out_shape=jax.ShapeDtypeStruct((2 * x.shap...  2.95 us
    dot_general x1, matrix products, local(): term = jnp.dot(hidden_sum, base_down[0], preferred_element_type=jnp.float32)  2.79 us
  transfers between devices with their start and end apart: 19, of which 10 were waited for; matrix products, arithmetic and copies ran while one was open for 6% of the time, Pallas kernels for 5%

profile of v15, /device:TPU:0, one launch (start us, length us, event | category | flops | bytes accessed | tf_op | source)
XLA Modules:
  0.0 57.8 jit_solution(14781827366429968888)
XLA Ops:
  0.0 1.0 %shard_map.100 = bf16[4,7296]{1,0:T(4,128)(2,1)S(1)} custom-call(bf16[4,7168]{1,0:T(4,128)(2,1)} %bitcast.68, s32[4,8]{1,0:T(4,128)} %bitcast.69, s32[4,8]{1,0:T(4,128)} %bitcast.70), custom_call_target="tpu_custom_call" | custom-call | flops 20000000000 | bytes 114688 | tf_op jit(solution)/shard_map/pallas_call | solution.py:70
  1.0 5.1 %collective-permute-start.3 = (bf16[4,7296]{1,0:T(4,128)(2,1)S(1)}, bf16[4,7296]{1,0:T(4,128)(2,1)S(1)}, u32[]{:S(2)}, u32[]{:S(2)}) collective-permute-start(bf16[4,7296]{1,0:T(4,128)(2,1)S(1)} %shard_map.100), channel_id=1, source_target_pairs={{0,12},{1,13},{2,14},{3,15},{4,8},{5,9},{6,10},{7,11},{8,4},{9,5},... | collective-permute-start | bytes 175112 | tf_op jit(solution)/shard_map/ppermute | solution.py:36
  6.1 0.6 %collective-permute-start.1 = (bf16[4,7296]{1,0:T(4,128)(2,1)S(1)}, bf16[4,7296]{1,0:T(4,128)(2,1)S(1)}, u32[]{:S(2)}, u32[]{:S(2)}) collective-permute-start(bf16[4,7296]{1,0:T(4,128)(2,1)S(1)} %shard_map.100), channel_id=1, source_target_pairs={{0,4},{1,5},{2,6},{3,7},{4,0},{5,1},{6,2},{7,3},{8,12},{9,13},{10,... | collective-permute-start | bytes 175112 | tf_op jit(solution)/shard_map/ppermute | solution.py:36
  6.7 1.6 %collective-permute-start = (bf16[4,7296]{1,0:T(4,128)(2,1)S(1)}, bf16[4,7296]{1,0:T(4,128)(2,1)S(1)}, u32[]{:S(2)}, u32[]{:S(2)}) collective-permute-start(bf16[4,7296]{1,0:T(4,128)(2,1)S(1)} %shard_map.100), channel_id=1, source_target_pairs={{0,2},{1,3},{2,0},{3,1},{4,6},{5,7},{6,4},{7,5},{8,10},{9,11},{10,... | collective-permute-start | bytes 175112 | tf_op jit(solution)/shard_map/ppermute | solution.py:36
  8.4 0.1 collective-permute-done.3
  8.5 2.7 %collective-permute-done.2 = bf16[4,7296]{1,0:T(4,128)(2,1)S(1)} collective-permute-done((bf16[4,7296]{1,0:T(4,128)(2,1)S(1)}, bf16[4,7296]{1,0:T(4,128)(2,1)S(1)}, u32[]{:S(2)}, u32[]{:S(2)}) %collective-permute-start.2) | collective-permute-done | bytes 58400 | tf_op jit(solution)/shard_map/ppermute | solution.py:36
  11.2 0.1 pad_maximum_fusion
  11.3 1.6 %collective-permute-start.4 = (bf16[12,7296]{1,0:T(8,128)(2,1)S(1)}, bf16[12,7296]{1,0:T(8,128)(2,1)S(1)}, u32[]{:S(2)}, u32[]{:S(2)}) collective-permute-start(bf16[12,7296]{1,0:T(8,128)(2,1)S(1)} %pad_maximum_fusion), channel_id=1, source_target_pairs={{0,2},{1,3},{2,0},{3,1},{4,6},{5,7},{6,4},{7,5},{8,10},{9,11},{10,... | collective-permute-start | bytes 525320 | tf_op jit(solution)/shard_map/ppermute | solution.py:36
  13.0 5.1 %collective-permute-done.4 = bf16[12,7296]{1,0:T(8,128)(2,1)S(1)} collective-permute-done((bf16[12,7296]{1,0:T(8,128)(2,1)S(1)}, bf16[12,7296]{1,0:T(8,128)(2,1)S(1)}, u32[]{:S(2)}, u32[]{:S(2)}) %collective-permute-start.4) | collective-permute-done | bytes 175136 | tf_op jit(solution)/shard_map/ppermute | solution.py:36
  18.2 0.2 broadcast_select_fusion
  18.3 0.3 concatenate.10.own
  18.8 1.8 %collective-permute-done.5.received = bf16[32,7296]{1,0:T(8,128)(2,1)S(1)} collective-permute-done((bf16[32,7296]{1,0:T(8,128)(2,1)S(1)}, bf16[32,7296]{1,0:T(8,128)(2,1)S(1)}, u32[]{:S(2)}, u32[]{:S(2)}) %collective-permute-start.5) | collective-permute-done | bytes 466976 | tf_op jit(solution)/shard_map/ppermute | solution.py:36
  20.6 0.8 %copy-done.2 = bf16[32,7296]{1,0:T(8,128)(2,1)} copy-done((bf16[32,7296]{1,0:T(8,128)(2,1)}, bf16[32,7296]{1,0:T(8,128)(2,1)S(1)}, u32[]{:S(2)}) %copy-start.2) | copy-done | bytes 466968
  21.3 1.0 %copy-done.3 = bf16[32,7296]{1,0:T(8,128)(2,1)S(1)} copy-done((bf16[32,7296]{1,0:T(8,128)(2,1)S(1)}, bf16[32,7296]{1,0:T(8,128)(2,1)}, u32[]{:S(2)}) %copy-start.3) | copy-done | bytes 466968
  22.4 0.2 convert_reduce_fusion
  22.6 1.2 %copy-done.4 = bf16[1,7168,128]{2,1,0:T(8,128)(2,1)S(1)} copy-done((bf16[1,7168,128]{2,1,0:T(8,128)(2,1)S(1)}, bf16[1,7168,128]{2,1,0:T(8,128)(2,1)}, u32[]{:S(2)}) %copy-start.4) | copy-done | bytes 1835032
  23.9 0.5 fusion.6
  24.3 1.4 %collective-permute-start.8 = (bf16[64,128]{1,0:T(8,128)(2,1)S(1)}, bf16[64,128]{1,0:T(8,128)(2,1)S(1)}, u32[]{:S(2)}, u32[]{:S(2)}) collective-permute-start(bf16[64,128]{1,0:T(8,128)(2,1)S(1)} %fusion.6), channel_id=1, source_target_pairs={{0,3},{1,2},{2,1},{3,0},{4,7},{5,6},{6,5},{7,4},{8,11},{9,10},{10,... | collective-permute-start | bytes 49160 | tf_op jit(solution)/shard_map/ppermute | solution.py:36
  25.7 0.5 collective-permute-start.7
  26.2 0.1 collective-permute-start.6
  26.3 0.1 fusion.30
  26.4 3.1 %copy-done.1 = bf16[1,7168,2,256]{3,2,1,0:T(2,128)(2,1)S(1)} copy-done((bf16[1,7168,2,256]{3,2,1,0:T(2,128)(2,1)S(1)}, bf16[1,7168,2,256]{3,2,1,0:T(2,128)(2,1)}, u32[]{:S(2)}) %copy-start.1) | copy-done | bytes 7340056
  29.5 3.0 %shard_map.102 = f32[128,256]{1,0:T(8,128)S(1)} custom-call(bf16[64,7296]{1,0:T(8,128)(2,1)S(1)} %shard_map.101.x, bf16[7168,2,256]{2,1,0:T(2,128)(2,1)S(1)} %bitcast.62), custom_call_target="tpu_custom_call" | custom-call | flops 469762048 | bytes 7340032 | tf_op jit(solution)/shard_map/pallas_call | solution.py:110
  32.6 0.1 select_reduce_fusion
  32.7 0.1 select_reduce_fusion.1
  32.8 0.2 fusion.10
  33.1 0.1 multiply_reduce_fusion
  33.2 0.2 copy-done.6
  33.4 0.2 convolution_convert_fusion
  33.6 0.5 collective-permute-start.9
  34.1 1.3 %collective-permute-start.11 = (bf16[64,128]{1,0:T(8,128)(2,1)S(1)}, bf16[64,128]{1,0:T(8,128)(2,1)S(1)}, u32[]{:S(2)}, u32[]{:S(2)}) collective-permute-start(bf16[64,128]{1,0:T(8,128)(2,1)S(1)} %get-tuple-element.30), channel_id=1, source_target_pairs={{0,3},{1,2},{2,1},{3,0},{4,7},{5,6},{6,5},{7,4},{8,11},{9,10},{10,... | collective-permute-start | bytes 49160 | tf_op jit(solution)/shard_map/ppermute | solution.py:36
  35.4 0.4 collective-permute-start.10
  35.8 2.8 %fusion.1 = f32[64,7168]{1,0:T(8,128)S(1)} fusion(bf16[1,256,7168]{2,1,0:T(8,128)(2,1)} %param.15, bf16[64,256]{1,0:T(8,128)(2,1)S(1)} %get-tuple-element.13), kind=kOutput, calls=%fused_computation.2 | convolution fusion | flops 234881024 | bytes 5537792 | tf_op jit(solution)/shard_map/dot_general | solution.py:255
  38.7 0.5 collective-permute-done.10
  39.1 0.5 fusion.term
  39.7 1.8 %collective-permute-done.12.received = bf16[32,7168]{1,0:T(8,128)(2,1)S(1)} collective-permute-done((bf16[32,7168]{1,0:T(8,128)(2,1)S(1)}, bf16[32,7168]{1,0:T(8,128)(2,1)S(1)}, u32[]{:S(2)}, u32[]{:S(2)}) %collective-permute-start.12) | collective-permute-done | bytes 458784 | tf_op jit(solution)/shard_map/ppermute | solution.py:36
  41.5 0.2 shard_map.103
  41.7 0.6 %collective-permute-start.13 = (bf16[16,3584]{1,0:T(8,128)(2,1)S(1)}, bf16[16,3584]{1,0:T(8,128)(2,1)S(1)}, u32[]{:S(2)}, u32[]{:S(2)}) collective-permute-start(bf16[16,3584]{1,0:T(8,128)(2,1)S(1)} %get-tuple-element.10), channel_id=1, source_target_pairs={{0,4},{1,3},{2,6},{3,1},{4,0},{5,7},{6,2},{7,5},{8,12},{9,11},{10,... | collective-permute-start | bytes 344072 | tf_op jit(solution)/shard_map/ppermute | solution.py:36
  42.4 1.5 %collective-permute-start.16 = (bf16[16,3584]{1,0:T(8,128)(2,1)S(1)}, bf16[16,3584]{1,0:T(8,128)(2,1)S(1)}, u32[]{:S(2)}, u32[]{:S(2)}) collective-permute-start(bf16[16,3584]{1,0:T(8,128)(2,1)S(1)} %get-tuple-element.12), channel_id=1, source_target_pairs={{0,4},{1,3},{2,6},{3,1},{4,0},{5,7},{6,2},{7,5},{8,12},{9,11},{10,... | collective-permute-start | bytes 344072 | tf_op jit(solution)/shard_map/ppermute | solution.py:36
  43.8 2.8 %collective-permute-done.13 = bf16[16,3584]{1,0:T(8,128)(2,1)S(1)} collective-permute-done((bf16[16,3584]{1,0:T(8,128)(2,1)S(1)}, bf16[16,3584]{1,0:T(8,128)(2,1)S(1)}, u32[]{:S(2)}, u32[]{:S(2)}) %collective-permute-start.13) | collective-permute-done | bytes 114720 | tf_op jit(solution)/shard_map/ppermute | solution.py:36
  46.6 1.2 %collective-permute-start.14 = (bf16[8,3584]{1,0:T(8,128)(2,1)S(1)}, bf16[8,3584]{1,0:T(8,128)(2,1)S(1)}, u32[]{:S(2)}, u32[]{:S(2)}) collective-permute-start(bf16[8,3584]{1,0:T(8,128)(2,1)S(1)} %broadcast_select_fusion.9), channel_id=1, source_target_pairs={{0,2},{1,5},{2,0},{3,7},{4,6},{5,1},{6,4},{7,3},{8,10},{9,13},{10,... | collective-permute-start | bytes 172040 | tf_op jit(solution)/shard_map/ppermute | solution.py:36
  47.9 1.2 %collective-permute-start.17 = (bf16[8,3584]{1,0:T(8,128)(2,1)S(1)}, bf16[8,3584]{1,0:T(8,128)(2,1)S(1)}, u32[]{:S(2)}, u32[]{:S(2)}) collective-permute-start(bf16[8,3584]{1,0:T(8,128)(2,1)S(1)} %broadcast_select_fusion.8), channel_id=1, source_target_pairs={{0,2},{1,5},{2,0},{3,7},{4,6},{5,1},{6,4},{7,3},{8,10},{9,13},{10,... | collective-permute-start | bytes 172040 | tf_op jit(solution)/shard_map/ppermute | solution.py:36
  49.1 1.8 %collective-permute-done.14 = bf16[8,3584]{1,0:T(8,128)(2,1)S(1)} collective-permute-done((bf16[8,3584]{1,0:T(8,128)(2,1)S(1)}, bf16[8,3584]{1,0:T(8,128)(2,1)S(1)}, u32[]{:S(2)}, u32[]{:S(2)}) %collective-permute-start.14) | collective-permute-done | bytes 57376 | tf_op jit(solution)/shard_map/ppermute | solution.py:36
  50.9 1.3 %collective-permute-start.15 = (bf16[4,3584]{1,0:T(4,128)(2,1)S(1)}, bf16[4,3584]{1,0:T(4,128)(2,1)S(1)}, u32[]{:S(2)}, u32[]{:S(2)}) collective-permute-start(bf16[4,3584]{1,0:T(4,128)(2,1)S(1)} %slice.101), channel_id=1, source_target_pairs={{0,8},{1,9},{2,10},{3,11},{4,12},{5,13},{6,14},{7,15},{8,0},{9,1},... | collective-permute-start | bytes 86024 | tf_op jit(solution)/shard_map/ppermute | solution.py:36
  52.3 1.8 %collective-permute-start.18 = (bf16[4,3584]{1,0:T(4,128)(2,1)S(1)}, bf16[4,3584]{1,0:T(4,128)(2,1)S(1)}, u32[]{:S(2)}, u32[]{:S(2)}) collective-permute-start(bf16[4,3584]{1,0:T(4,128)(2,1)S(1)} %slice.105), channel_id=1, source_target_pairs={{0,8},{1,9},{2,10},{3,11},{4,12},{5,13},{6,14},{7,15},{8,0},{9,1},... | collective-permute-start | bytes 86024 | tf_op jit(solution)/shard_map/ppermute | solution.py:36
  54.1 2.0 %collective-permute-done.15 = bf16[4,3584]{1,0:T(4,128)(2,1)S(1)} collective-permute-done((bf16[4,3584]{1,0:T(4,128)(2,1)S(1)}, bf16[4,3584]{1,0:T(4,128)(2,1)S(1)}, u32[]{:S(2)}, u32[]{:S(2)}) %collective-permute-start.15) | collective-permute-done | bytes 28704 | tf_op jit(solution)/shard_map/ppermute | solution.py:36
  56.1 1.0 %collective-permute-done.18 = bf16[4,3584]{1,0:T(4,128)(2,1)S(1)} collective-permute-done((bf16[4,3584]{1,0:T(4,128)(2,1)S(1)}, bf16[4,3584]{1,0:T(4,128)(2,1)S(1)}, u32[]{:S(2)}, u32[]{:S(2)}) %collective-permute-start.18) | collective-permute-done | bytes 28704 | tf_op jit(solution)/shard_map/ppermute | solution.py:36
  57.1 0.7 %maximum_bitcast_fusion.2 = bf16[1,4,7168]{2,1,0:T(4,128)(2,1)} fusion(bf16[4,3584]{1,0:T(4,128)(2,1)S(1)} %add_convert_fusion.4, bf16[4,3584]{1,0:T(4,128)(2,1)S(1)} %add_convert_fusion.5), kind=kLoop, calls=%fused_computation.44 | loop fusion | flops 114688 | bytes 114688 | tf_op jit(solution)/shard_map/broadcast_in_dim | solution.py:284
  (45 shorter events, 0.8 us)
Async XLA Ops:
  0.0 39.1 %copy-start = (bf16[1,128,7168]{2,1,0:T(8,128)(2,1)S(1)}, bf16[1,128,7168]{2,1,0:T(8,128)(2,1)}, u32[]{:S(2)}) copy-start(bf16[1,128,7168]{2,1,0:T(8,128)(2,1)} %param.19) | copy-start | bytes 5505028
  1.0 7.5 %collective-permute-start.3 = (bf16[4,7296]{1,0:T(4,128)(2,1)S(1)}, bf16[4,7296]{1,0:T(4,128)(2,1)S(1)}, u32[]{:S(2)}, u32[]{:S(2)}) collective-permute-start(bf16[4,7296]{1,0:T(4,128)(2,1)S(1)} %shard_map.100), channel_id=1, source_target_pairs={{0,12},{1,13},{2,14},{3,15},{4,8},{5,9},{6,10},{7,11},{8,4},{9,5},... | collective-permute-start | bytes 175112 | tf_op jit(solution)/shard_map/ppermute | solution.py:36
  6.1 5.1 %collective-permute-start.2 = (bf16[4,7296]{1,0:T(4,128)(2,1)S(1)}, bf16[4,7296]{1,0:T(4,128)(2,1)S(1)}, u32[]{:S(2)}, u32[]{:S(2)}) collective-permute-start(bf16[4,7296]{1,0:T(4,128)(2,1)S(1)} %shard_map.100), channel_id=1, source_target_pairs={{0,8},{1,9},{2,10},{3,11},{4,12},{5,13},{6,14},{7,15},{8,0},{9,1},... | collective-permute-start | bytes 175112 | tf_op jit(solution)/shard_map/ppermute | solution.py:36
  6.1 5.1 %collective-permute-start.1 = (bf16[4,7296]{1,0:T(4,128)(2,1)S(1)}, bf16[4,7296]{1,0:T(4,128)(2,1)S(1)}, u32[]{:S(2)}, u32[]{:S(2)}) collective-permute-start(bf16[4,7296]{1,0:T(4,128)(2,1)S(1)} %shard_map.100), channel_id=1, source_target_pairs={{0,4},{1,5},{2,6},{3,7},{4,0},{5,1},{6,2},{7,3},{8,12},{9,13},{10,... | collective-permute-start | bytes 175112 | tf_op jit(solution)/shard_map/ppermute | solution.py:36
  6.7 6.2 %collective-permute-start = (bf16[4,7296]{1,0:T(4,128)(2,1)S(1)}, bf16[4,7296]{1,0:T(4,128)(2,1)S(1)}, u32[]{:S(2)}, u32[]{:S(2)}) collective-permute-start(bf16[4,7296]{1,0:T(4,128)(2,1)S(1)} %shard_map.100), channel_id=1, source_target_pairs={{0,2},{1,3},{2,0},{3,1},{4,6},{5,7},{6,4},{7,5},{8,10},{9,11},{10,... | collective-permute-start | bytes 175112 | tf_op jit(solution)/shard_map/ppermute | solution.py:36
  11.3 6.8 %collective-permute-start.4 = (bf16[12,7296]{1,0:T(8,128)(2,1)S(1)}, bf16[12,7296]{1,0:T(8,128)(2,1)S(1)}, u32[]{:S(2)}, u32[]{:S(2)}) collective-permute-start(bf16[12,7296]{1,0:T(8,128)(2,1)S(1)} %pad_maximum_fusion), channel_id=1, source_target_pairs={{0,2},{1,3},{2,0},{3,1},{4,6},{5,7},{6,4},{7,5},{8,10},{9,11},{10,... | collective-permute-start | bytes 525320 | tf_op jit(solution)/shard_map/ppermute | solution.py:36
  18.7 1.9 %collective-permute-start.5 = (bf16[32,7296]{1,0:T(8,128)(2,1)S(1)}, bf16[32,7296]{1,0:T(8,128)(2,1)S(1)}, u32[]{:S(2)}, u32[]{:S(2)}) collective-permute-start(bf16[32,7296]{1,0:T(8,128)(2,1)S(1)} %concatenate.10.own), channel_id=1, source_target_pairs={{0,1},{1,0},{2,3},{3,2},{4,5},{5,4},{6,7},{7,6},{8,9},{9,8},{10,11... | collective-permute-start | bytes 1400840 | tf_op jit(solution)/shard_map/ppermute | solution.py:36
  20.6 0.8 %copy-start.2 = (bf16[32,7296]{1,0:T(8,128)(2,1)}, bf16[32,7296]{1,0:T(8,128)(2,1)S(1)}, u32[]{:S(2)}) copy-start(bf16[32,7296]{1,0:T(8,128)(2,1)S(1)} %collective-permute-done.5.received) | copy-start | bytes 1400836
  21.3 1.0 %copy-start.3 = (bf16[32,7296]{1,0:T(8,128)(2,1)S(1)}, bf16[32,7296]{1,0:T(8,128)(2,1)}, u32[]{:S(2)}) copy-start(bf16[32,7296]{1,0:T(8,128)(2,1)} %copy-done.2) | copy-start | bytes 1400836
  22.4 1.5 %copy-start.4 = (bf16[1,7168,128]{2,1,0:T(8,128)(2,1)S(1)}, bf16[1,7168,128]{2,1,0:T(8,128)(2,1)}, u32[]{:S(2)}) copy-start(bf16[1,7168,128]{2,1,0:T(8,128)(2,1)} %param.16) | copy-start | bytes 5505028
  24.3 8.4 %collective-permute-start.8 = (bf16[64,128]{1,0:T(8,128)(2,1)S(1)}, bf16[64,128]{1,0:T(8,128)(2,1)S(1)}, u32[]{:S(2)}, u32[]{:S(2)}) collective-permute-start(bf16[64,128]{1,0:T(8,128)(2,1)S(1)} %fusion.6), channel_id=1, source_target_pairs={{0,3},{1,2},{2,1},{3,0},{4,7},{5,6},{6,5},{7,4},{8,11},{9,10},{10,... | collective-permute-start | bytes 49160 | tf_op jit(solution)/shard_map/ppermute | solution.py:36
  25.7 7.1 %collective-permute-start.7 = (bf16[64,128]{1,0:T(8,128)(2,1)S(1)}, bf16[64,128]{1,0:T(8,128)(2,1)S(1)}, u32[]{:S(2)}, u32[]{:S(2)}) collective-permute-start(bf16[64,128]{1,0:T(8,128)(2,1)S(1)} %fusion.6), channel_id=1, source_target_pairs={{0,2},{1,3},{2,0},{3,1},{4,6},{5,7},{6,4},{7,5},{8,10},{9,11},{10,... | collective-permute-start | bytes 49160 | tf_op jit(solution)/shard_map/ppermute | solution.py:36
  26.2 6.6 %collective-permute-start.6 = (bf16[64,128]{1,0:T(8,128)(2,1)S(1)}, bf16[64,128]{1,0:T(8,128)(2,1)S(1)}, u32[]{:S(2)}, u32[]{:S(2)}) collective-permute-start(bf16[64,128]{1,0:T(8,128)(2,1)S(1)} %fusion.6), channel_id=1, source_target_pairs={{0,1},{1,0},{2,3},{3,2},{4,5},{5,4},{6,7},{7,6},{8,9},{9,8},{10,11... | collective-permute-start | bytes 49160 | tf_op jit(solution)/shard_map/ppermute | solution.py:36
  26.4 3.1 %copy-start.1 = (bf16[1,7168,2,256]{3,2,1,0:T(2,128)(2,1)S(1)}, bf16[1,7168,2,256]{3,2,1,0:T(2,128)(2,1)}, u32[]{:S(2)}) copy-start(bf16[1,7168,2,256]{3,2,1,0:T(2,128)(2,1)} %param.14) | copy-start | bytes 22020100
  29.5 3.1 %copy-start.7 = (s32[16]{0:T(128)S(1)}, s32[16]{0:T(128)}, u32[]{:S(2)}) copy-start(s32[16]{0:T(128)} %param.13) | copy-start | bytes 196
  29.5 3.3 %copy-start.5 = (bf16[1,4,128,2,256]{4,3,2,1,0:T(2,128)(2,1)S(1)}, bf16[1,4,128,2,256]{4,3,2,1,0:T(2,128)(2,1)}, u32[]{:S(2)}) copy-start(bf16[1,4,128,2,256]{4,3,2,1,0:T(2,128)(2,1)} %param.17) | copy-start | bytes 1572868
  32.5 1.0 %copy-start.6 = (bf16[1,4,256,128]{3,2,1,0:T(8,128)(2,1)S(1)}, bf16[1,4,256,128]{3,2,1,0:T(8,128)(2,1)}, u32[]{:S(2)}) copy-start(bf16[1,4,256,128]{3,2,1,0:T(8,128)(2,1)} %param.18) | copy-start | bytes 786436
  33.6 5.0 %collective-permute-start.9 = (bf16[64,128]{1,0:T(8,128)(2,1)S(1)}, bf16[64,128]{1,0:T(8,128)(2,1)S(1)}, u32[]{:S(2)}, u32[]{:S(2)}) collective-permute-start(bf16[64,128]{1,0:T(8,128)(2,1)S(1)} %get-tuple-element.29), channel_id=1, source_target_pairs={{0,1},{1,0},{2,3},{3,2},{4,5},{5,4},{6,7},{7,6},{8,9},{9,8},{10,11... | collective-permute-start | bytes 49160 | tf_op jit(solution)/shard_map/ppermute | solution.py:36
  34.1 4.5 %collective-permute-start.11 = (bf16[64,128]{1,0:T(8,128)(2,1)S(1)}, bf16[64,128]{1,0:T(8,128)(2,1)S(1)}, u32[]{:S(2)}, u32[]{:S(2)}) collective-permute-start(bf16[64,128]{1,0:T(8,128)(2,1)S(1)} %get-tuple-element.30), channel_id=1, source_target_pairs={{0,3},{1,2},{2,1},{3,0},{4,7},{5,6},{6,5},{7,4},{8,11},{9,10},{10,... | collective-permute-start | bytes 49160 | tf_op jit(solution)/shard_map/ppermute | solution.py:36
  35.4 3.7 %collective-permute-start.10 = (bf16[64,128]{1,0:T(8,128)(2,1)S(1)}, bf16[64,128]{1,0:T(8,128)(2,1)S(1)}, u32[]{:S(2)}, u32[]{:S(2)}) collective-permute-start(bf16[64,128]{1,0:T(8,128)(2,1)S(1)} %get-tuple-element.31), channel_id=1, source_target_pairs={{0,2},{1,3},{2,0},{3,1},{4,6},{5,7},{6,4},{7,5},{8,10},{9,11},{10,... | collective-permute-start | bytes 49160 | tf_op jit(solution)/shard_map/ppermute | solution.py:36
  39.7 1.9 %collective-permute-start.12 = (bf16[32,7168]{1,0:T(8,128)(2,1)S(1)}, bf16[32,7168]{1,0:T(8,128)(2,1)S(1)}, u32[]{:S(2)}, u32[]{:S(2)}) collective-permute-start(bf16[32,7168]{1,0:T(8,128)(2,1)S(1)} %slice_select_fusion), channel_id=1, source_target_pairs={{0,1},{1,0},{2,3},{3,2},{4,5},{5,4},{6,7},{7,6},{8,9},{9,8},{10,11... | collective-permute-start | bytes 1376264 | tf_op jit(solution)/shard_map/ppermute | solution.py:36
  41.7 4.9 %collective-permute-start.13 = (bf16[16,3584]{1,0:T(8,128)(2,1)S(1)}, bf16[16,3584]{1,0:T(8,128)(2,1)S(1)}, u32[]{:S(2)}, u32[]{:S(2)}) collective-permute-start(bf16[16,3584]{1,0:T(8,128)(2,1)S(1)} %get-tuple-element.10), channel_id=1, source_target_pairs={{0,4},{1,3},{2,6},{3,1},{4,0},{5,7},{6,2},{7,5},{8,12},{9,11},{10,... | collective-permute-start | bytes 344072 | tf_op jit(solution)/shard_map/ppermute | solution.py:36
  42.4 5.5 %collective-permute-start.16 = (bf16[16,3584]{1,0:T(8,128)(2,1)S(1)}, bf16[16,3584]{1,0:T(8,128)(2,1)S(1)}, u32[]{:S(2)}, u32[]{:S(2)}) collective-permute-start(bf16[16,3584]{1,0:T(8,128)(2,1)S(1)} %get-tuple-element.12), channel_id=1, source_target_pairs={{0,4},{1,3},{2,6},{3,1},{4,0},{5,7},{6,2},{7,5},{8,12},{9,11},{10,... | collective-permute-start | bytes 344072 | tf_op jit(solution)/shard_map/ppermute | solution.py:36
  46.6 4.2 %collective-permute-start.14 = (bf16[8,3584]{1,0:T(8,128)(2,1)S(1)}, bf16[8,3584]{1,0:T(8,128)(2,1)S(1)}, u32[]{:S(2)}, u32[]{:S(2)}) collective-permute-start(bf16[8,3584]{1,0:T(8,128)(2,1)S(1)} %broadcast_select_fusion.9), channel_id=1, source_target_pairs={{0,2},{1,5},{2,0},{3,7},{4,6},{5,1},{6,4},{7,3},{8,10},{9,13},{10,... | collective-permute-start | bytes 172040 | tf_op jit(solution)/shard_map/ppermute | solution.py:36
  47.9 4.3 %collective-permute-start.17 = (bf16[8,3584]{1,0:T(8,128)(2,1)S(1)}, bf16[8,3584]{1,0:T(8,128)(2,1)S(1)}, u32[]{:S(2)}, u32[]{:S(2)}) collective-permute-start(bf16[8,3584]{1,0:T(8,128)(2,1)S(1)} %broadcast_select_fusion.8), channel_id=1, source_target_pairs={{0,2},{1,5},{2,0},{3,7},{4,6},{5,1},{6,4},{7,3},{8,10},{9,13},{10,... | collective-permute-start | bytes 172040 | tf_op jit(solution)/shard_map/ppermute | solution.py:36
  50.9 5.1 %collective-permute-start.15 = (bf16[4,3584]{1,0:T(4,128)(2,1)S(1)}, bf16[4,3584]{1,0:T(4,128)(2,1)S(1)}, u32[]{:S(2)}, u32[]{:S(2)}) collective-permute-start(bf16[4,3584]{1,0:T(4,128)(2,1)S(1)} %slice.101), channel_id=1, source_target_pairs={{0,8},{1,9},{2,10},{3,11},{4,12},{5,13},{6,14},{7,15},{8,0},{9,1},... | collective-permute-start | bytes 86024 | tf_op jit(solution)/shard_map/ppermute | solution.py:36
  52.3 4.8 %collective-permute-start.18 = (bf16[4,3584]{1,0:T(4,128)(2,1)S(1)}, bf16[4,3584]{1,0:T(4,128)(2,1)S(1)}, u32[]{:S(2)}, u32[]{:S(2)}) collective-permute-start(bf16[4,3584]{1,0:T(4,128)(2,1)S(1)} %slice.105), channel_id=1, source_target_pairs={{0,8},{1,9},{2,10},{3,11},{4,12},{5,13},{6,14},{7,15},{8,0},{9,1},... | collective-permute-start | bytes 86024 | tf_op jit(solution)/shard_map/ppermute | solution.py:36

commit v16 on v15

--- a/solution.py
+++ b/solution.py
@@ -119,25 +119,6 @@
     )(x, base)
 
 
-def join_kernel(own, received, joined):
-    half = own.shape[0]
-    core = lax.axis_index("tensor") % 2
-    joined[pl.ds(pl.multiple_of(core * half, half), half), :] = own[...]
-    joined[pl.ds(pl.multiple_of((1 - core) * half, half), half), :] = received[...]
-
-
-def join(own, received):
-    rows, width = own.shape
-    return pl.pallas_call(
-        join_kernel,
-        out_shape=jax.ShapeDtypeStruct((2 * rows, width), own.dtype),
-        in_specs=[VMEM, VMEM],
-        out_specs=VMEM,
-        compiler_params=pltpu.CompilerParams(vmem_limit_bytes=16 << 20),
-        cost_estimate=pl.CostEstimate(flops=0, bytes_accessed=6 * own.size, transcendentals=0),
-    )(own, received)
-
-
 def part_kernel(bit, term, received, *refs):
     *outs, total = refs
     half, width = total.shape
@@ -220,12 +201,13 @@
         places += [(x | xbit, z) for x, z in places]
         places += [(x, z | zbit) for x, z in places]
     held = by_rows(jnp.concatenate([pieces[place] for place in places]))
-    held = join(held, trade(held, (0, 1), (0, 1)))
-
-    codes = jnp.dot(held[:, :width], delta_in[0], preferred_element_type=jnp.float32).astype(jnp.bfloat16)
+    held = by_rows(jnp.concatenate(ordered(core == 1, held, trade(held, (0, 1), (0, 1)))))
+    rows, code_table = lax.optimization_barrier((held, delta_in[0]))
+
+    codes = jnp.dot(rows[:, :width], code_table, preferred_element_type=jnp.float32).astype(jnp.bfloat16)
     projected = gate_up_product(held, base_in[0])
 
-    side = by_rows(held[:, width:])
+    side = by_rows(rows[:, width:])
     all_routes = side[:, :top].astype(jnp.int32)
     numerator = side[:, top : 2 * top].astype(jnp.float32)
     position = lookup(place, all_routes)

time: 58.1 us -> 55.1 us (0.948)
  waiting for transfers between devices: 19.6 us -> 22.6 us
  local copies, waits for them, and re-layouts: 6.94 us -> 3.97 us
  matrix products: 4.11 us -> 2.08 us
  starting transfers between devices: 20.8 us -> 20 us
    unnamed x16 -> x14, local copies, waits for them, and re-layouts: 6.38 us -> 3.43 us
    ppermute x19, waiting for transfers between devices: 19.6 us -> 22.6 us  [trade(): return lax.ppermute(value, ('expert', 'tensor'), pairs)]
    dot_general x1, matrix products: 2.79 us -> 0.75 us  [local(): term = jnp.dot(hidden_sum, base_down[0], preferred_element_type=jnp.float32)]
    ppermute x19, starting transfers between devices: 20.8 us -> 20 us  [trade(): return lax.ppermute(value, ('expert', 'tensor'), pairs)]
  transfers between devices with their start and end apart: 19 -> 19, of which waited for: 10 -> 12; matrix products, arithmetic and copies ran while one was open for 6% -> 3% of each run, Pallas kernels for 5% -> 5%
where the time goes in v16:
time: 55.1 us; the launch traced here: 54.9 us
  waiting for transfers between devices  22.6 us (41%)
  starting transfers between devices  20 us (36%)
  Pallas kernels  4.12 us (7%)
  local copies, waits for them, and re-layouts  3.97 us (7%)
  matrix products  2.08 us (4%)
  other arithmetic  1.91 us (3%)
    ppermute x19, waiting for transfers between devices, trade(): return lax.ppermute(value, ('expert', 'tensor'), pairs)  22.6 us
    ppermute x19, starting transfers between devices, trade(): return lax.ppermute(value, ('expert', 'tensor'), pairs)  20 us
    unnamed x14, local copies, waits for them, and re-layouts  3.43 us
    pallas_call x1, Pallas kernels, gate_up_product(): pl.pallas_call(gate_up_kernel, out_shape=jax.ShapeDtypeStruct((2 * x.shap...  2.96 us
  transfers between devices with their start and end apart: 19, of which 12 were waited for; matrix products, arithmetic and copies ran while one was open for 3% of the time, Pallas kernels for 5%

profile of v16, /device:TPU:0, one launch (start us, length us, event | category | flops | bytes accessed | tf_op | source)
XLA Modules:
  0.0 54.9 jit_solution(3159825499887392813)
XLA Ops:
  0.0 1.0 %shard_map.100 = bf16[4,7296]{1,0:T(4,128)(2,1)S(1)} custom-call(bf16[4,7168]{1,0:T(4,128)(2,1)} %bitcast.66, s32[4,8]{1,0:T(4,128)} %bitcast.67, s32[4,8]{1,0:T(4,128)} %bitcast.68), custom_call_target="tpu_custom_call" | custom-call | flops 20000000000 | bytes 114688 | tf_op jit(solution)/shard_map/pallas_call | solution.py:70
  1.0 5.1 %collective-permute-start.3 = (bf16[4,7296]{1,0:T(4,128)(2,1)S(1)}, bf16[4,7296]{1,0:T(4,128)(2,1)S(1)}, u32[]{:S(2)}, u32[]{:S(2)}) collective-permute-start(bf16[4,7296]{1,0:T(4,128)(2,1)S(1)} %shard_map.100), channel_id=1, source_target_pairs={{0,12},{1,13},{2,14},{3,15},{4,8},{5,9},{6,10},{7,11},{8,4},{9,5},... | collective-permute-start | bytes 175112 | tf_op jit(solution)/shard_map/ppermute | solution.py:36
  6.1 0.6 %collective-permute-start.1 = (bf16[4,7296]{1,0:T(4,128)(2,1)S(1)}, bf16[4,7296]{1,0:T(4,128)(2,1)S(1)}, u32[]{:S(2)}, u32[]{:S(2)}) collective-permute-start(bf16[4,7296]{1,0:T(4,128)(2,1)S(1)} %shard_map.100), channel_id=1, source_target_pairs={{0,4},{1,5},{2,6},{3,7},{4,0},{5,1},{6,2},{7,3},{8,12},{9,13},{10,... | collective-permute-start | bytes 175112 | tf_op jit(solution)/shard_map/ppermute | solution.py:36
  6.7 1.6 %collective-permute-start = (bf16[4,7296]{1,0:T(4,128)(2,1)S(1)}, bf16[4,7296]{1,0:T(4,128)(2,1)S(1)}, u32[]{:S(2)}, u32[]{:S(2)}) collective-permute-start(bf16[4,7296]{1,0:T(4,128)(2,1)S(1)} %shard_map.100), channel_id=1, source_target_pairs={{0,2},{1,3},{2,0},{3,1},{4,6},{5,7},{6,4},{7,5},{8,10},{9,11},{10,... | collective-permute-start | bytes 175112 | tf_op jit(solution)/shard_map/ppermute | solution.py:36
  8.4 0.1 collective-permute-done.3
  8.5 2.7 %collective-permute-done.2 = bf16[4,7296]{1,0:T(4,128)(2,1)S(1)} collective-permute-done((bf16[4,7296]{1,0:T(4,128)(2,1)S(1)}, bf16[4,7296]{1,0:T(4,128)(2,1)S(1)}, u32[]{:S(2)}, u32[]{:S(2)}) %collective-permute-start.2) | collective-permute-done | bytes 58400 | tf_op jit(solution)/shard_map/ppermute | solution.py:36
  11.2 0.1 pad_maximum_fusion.1
  11.3 1.6 %collective-permute-start.4 = (bf16[12,7296]{1,0:T(8,128)(2,1)S(1)}, bf16[12,7296]{1,0:T(8,128)(2,1)S(1)}, u32[]{:S(2)}, u32[]{:S(2)}) collective-permute-start(bf16[12,7296]{1,0:T(8,128)(2,1)S(1)} %pad_maximum_fusion.1), channel_id=1, source_target_pairs={{0,2},{1,3},{2,0},{3,1},{4,6},{5,7},{6,4},{7,5},{8,10},{9,11},{10,... | collective-permute-start | bytes 525320 | tf_op jit(solution)/shard_map/ppermute | solution.py:36
  13.0 5.1 %collective-permute-done.4 = bf16[12,7296]{1,0:T(8,128)(2,1)S(1)} collective-permute-done((bf16[12,7296]{1,0:T(8,128)(2,1)S(1)}, bf16[12,7296]{1,0:T(8,128)(2,1)S(1)}, u32[]{:S(2)}, u32[]{:S(2)}) %collective-permute-start.4) | collective-permute-done | bytes 175136 | tf_op jit(solution)/shard_map/ppermute | solution.py:36
  18.2 0.2 broadcast_select_fusion.2
  18.3 0.3 concatenate.13
  18.8 1.8 %collective-permute-done.5 = bf16[32,7296]{1,0:T(8,128)(2,1)S(1)} collective-permute-done((bf16[32,7296]{1,0:T(8,128)(2,1)S(1)}, bf16[32,7296]{1,0:T(8,128)(2,1)S(1)}, u32[]{:S(2)}, u32[]{:S(2)}) %collective-permute-start.5) | collective-permute-done | bytes 466976 | tf_op jit(solution)/shard_map/ppermute | solution.py:36
  20.6 0.1 broadcast_select_fusion.1
  20.7 0.2 convert_reduce_fusion
  20.9 0.5 convolution_convert_fusion.1
  21.4 1.4 %collective-permute-start.8 = (bf16[64,128]{1,0:T(8,128)(2,1)S(1)}, bf16[64,128]{1,0:T(8,128)(2,1)S(1)}, u32[]{:S(2)}, u32[]{:S(2)}) collective-permute-start(bf16[64,128]{1,0:T(8,128)(2,1)S(1)} %convolution_convert_fusion.1), channel_id=1, source_target_pairs={{0,3},{1,2},{2,1},{3,0},{4,7},{5,6},{6,5},{7,4},{8,11},{9,10},{10,... | collective-permute-start | bytes 49160 | tf_op jit(solution)/shard_map/ppermute | solution.py:36
  22.8 0.5 collective-permute-start.7
  23.2 0.1 collective-permute-start.6
  23.3 0.1 fusion.25
  23.5 3.1 %copy-done.1 = bf16[1,7168,2,256]{3,2,1,0:T(2,128)(2,1)S(1)} copy-done((bf16[1,7168,2,256]{3,2,1,0:T(2,128)(2,1)S(1)}, bf16[1,7168,2,256]{3,2,1,0:T(2,128)(2,1)}, u32[]{:S(2)}) %copy-start.1) | copy-done | bytes 7340056
  26.6 3.0 %shard_map.101 = f32[128,256]{1,0:T(8,128)S(1)} custom-call(bf16[64,7296]{1,0:T(8,128)(2,1)S(1)} %pad_maximum_fusion.x, bf16[7168,2,256]{2,1,0:T(2,128)(2,1)S(1)} %bitcast.60), custom_call_target="tpu_custom_call" | custom-call | flops 469762048 | bytes 7340032 | tf_op jit(solution)/shard_map/pallas_call | solution.py:110
  29.6 0.1 select_reduce_fusion
  29.7 0.1 select_reduce_fusion.1
  29.9 0.2 fusion.5
  30.1 0.1 multiply_reduce_fusion
  30.3 0.3 copy-done.5
  30.6 0.2 convolution_convert_fusion
  30.8 0.5 collective-permute-start.9
  31.3 1.3 %collective-permute-start.11 = (bf16[64,128]{1,0:T(8,128)(2,1)S(1)}, bf16[64,128]{1,0:T(8,128)(2,1)S(1)}, u32[]{:S(2)}, u32[]{:S(2)}) collective-permute-start(bf16[64,128]{1,0:T(8,128)(2,1)S(1)} %get-tuple-element.36), channel_id=1, source_target_pairs={{0,3},{1,2},{2,1},{3,0},{4,7},{5,6},{6,5},{7,4},{8,11},{9,10},{10,... | collective-permute-start | bytes 49160 | tf_op jit(solution)/shard_map/ppermute | solution.py:36
  32.5 0.4 collective-permute-start.10
  33.0 0.8 %fusion.1 = f32[64,7168]{1,0:T(8,128)S(1)} fusion(bf16[1,256,7168]{2,1,0:T(8,128)(2,1)S(1)} %copy-done.2, bf16[64,256]{1,0:T(8,128)(2,1)S(1)} %get-tuple-element.17), kind=kOutput, calls=%fused_computation.2 | convolution fusion | flops 234881024 | bytes 5537792 | tf_op jit(solution)/shard_map/dot_general | solution.py:237
  33.7 0.7 %collective-permute-done.11 = bf16[64,128]{1,0:T(8,128)(2,1)S(1)} collective-permute-done((bf16[64,128]{1,0:T(8,128)(2,1)S(1)}, bf16[64,128]{1,0:T(8,128)(2,1)S(1)}, u32[]{:S(2)}, u32[]{:S(2)}) %collective-permute-start.11) | collective-permute-done | bytes 16416 | tf_op jit(solution)/shard_map/ppermute | solution.py:36
  34.4 1.8 %collective-permute-done.10 = bf16[64,128]{1,0:T(8,128)(2,1)S(1)} collective-permute-done((bf16[64,128]{1,0:T(8,128)(2,1)S(1)}, bf16[64,128]{1,0:T(8,128)(2,1)S(1)}, u32[]{:S(2)}, u32[]{:S(2)}) %collective-permute-start.10) | collective-permute-done | bytes 16416 | tf_op jit(solution)/shard_map/ppermute | solution.py:36
  36.3 0.5 fusion.term
  36.9 1.8 %collective-permute-done.12.received = bf16[32,7168]{1,0:T(8,128)(2,1)S(1)} collective-permute-done((bf16[32,7168]{1,0:T(8,128)(2,1)S(1)}, bf16[32,7168]{1,0:T(8,128)(2,1)S(1)}, u32[]{:S(2)}, u32[]{:S(2)}) %collective-permute-start.12) | collective-permute-done | bytes 458784 | tf_op jit(solution)/shard_map/ppermute | solution.py:36
  38.7 0.2 shard_map.102
  38.9 0.6 %collective-permute-start.13 = (bf16[16,3584]{1,0:T(8,128)(2,1)S(1)}, bf16[16,3584]{1,0:T(8,128)(2,1)S(1)}, u32[]{:S(2)}, u32[]{:S(2)}) collective-permute-start(bf16[16,3584]{1,0:T(8,128)(2,1)S(1)} %get-tuple-element.14), channel_id=1, source_target_pairs={{0,4},{1,3},{2,6},{3,1},{4,0},{5,7},{6,2},{7,5},{8,12},{9,11},{10,... | collective-permute-start | bytes 344072 | tf_op jit(solution)/shard_map/ppermute | solution.py:36
  39.5 1.5 %collective-permute-start.16 = (bf16[16,3584]{1,0:T(8,128)(2,1)S(1)}, bf16[16,3584]{1,0:T(8,128)(2,1)S(1)}, u32[]{:S(2)}, u32[]{:S(2)}) collective-permute-start(bf16[16,3584]{1,0:T(8,128)(2,1)S(1)} %get-tuple-element.16), channel_id=1, source_target_pairs={{0,4},{1,3},{2,6},{3,1},{4,0},{5,7},{6,2},{7,5},{8,12},{9,11},{10,... | collective-permute-start | bytes 344072 | tf_op jit(solution)/shard_map/ppermute | solution.py:36
  41.0 2.8 %collective-permute-done.13 = bf16[16,3584]{1,0:T(8,128)(2,1)S(1)} collective-permute-done((bf16[16,3584]{1,0:T(8,128)(2,1)S(1)}, bf16[16,3584]{1,0:T(8,128)(2,1)S(1)}, u32[]{:S(2)}, u32[]{:S(2)}) %collective-permute-start.13) | collective-permute-done | bytes 114720 | tf_op jit(solution)/shard_map/ppermute | solution.py:36
  43.8 0.5 collective-permute-start.14
  44.3 0.7 %collective-permute-done.16 = bf16[16,3584]{1,0:T(8,128)(2,1)S(1)} collective-permute-done((bf16[16,3584]{1,0:T(8,128)(2,1)S(1)}, bf16[16,3584]{1,0:T(8,128)(2,1)S(1)}, u32[]{:S(2)}, u32[]{:S(2)}) %collective-permute-start.16) | collective-permute-done | bytes 114720 | tf_op jit(solution)/shard_map/ppermute | solution.py:36
  45.0 1.0 %collective-permute-start.17 = (bf16[8,3584]{1,0:T(8,128)(2,1)S(1)}, bf16[8,3584]{1,0:T(8,128)(2,1)S(1)}, u32[]{:S(2)}, u32[]{:S(2)}) collective-permute-start(bf16[8,3584]{1,0:T(8,128)(2,1)S(1)} %broadcast_select_fusion.10), channel_id=1, source_target_pairs={{0,2},{1,5},{2,0},{3,7},{4,6},{5,1},{6,4},{7,3},{8,10},{9,13},{10,... | collective-permute-start | bytes 172040 | tf_op jit(solution)/shard_map/ppermute | solution.py:36
  46.0 2.0 %collective-permute-done.14 = bf16[8,3584]{1,0:T(8,128)(2,1)S(1)} collective-permute-done((bf16[8,3584]{1,0:T(8,128)(2,1)S(1)}, bf16[8,3584]{1,0:T(8,128)(2,1)S(1)}, u32[]{:S(2)}, u32[]{:S(2)}) %collective-permute-start.14) | collective-permute-done | bytes 57376 | tf_op jit(solution)/shard_map/ppermute | solution.py:36
  48.1 1.3 %collective-permute-start.15 = (bf16[4,3584]{1,0:T(4,128)(2,1)S(1)}, bf16[4,3584]{1,0:T(4,128)(2,1)S(1)}, u32[]{:S(2)}, u32[]{:S(2)}) collective-permute-start(bf16[4,3584]{1,0:T(4,128)(2,1)S(1)} %slice.98), channel_id=1, source_target_pairs={{0,8},{1,9},{2,10},{3,11},{4,12},{5,13},{6,14},{7,15},{8,0},{9,1},... | collective-permute-start | bytes 86024 | tf_op jit(solution)/shard_map/ppermute | solution.py:36
  49.4 1.8 %collective-permute-start.18 = (bf16[4,3584]{1,0:T(4,128)(2,1)S(1)}, bf16[4,3584]{1,0:T(4,128)(2,1)S(1)}, u32[]{:S(2)}, u32[]{:S(2)}) collective-permute-start(bf16[4,3584]{1,0:T(4,128)(2,1)S(1)} %slice.102), channel_id=1, source_target_pairs={{0,8},{1,9},{2,10},{3,11},{4,12},{5,13},{6,14},{7,15},{8,0},{9,1},... | collective-permute-start | bytes 86024 | tf_op jit(solution)/shard_map/ppermute | solution.py:36
  51.2 2.0 %collective-permute-done.15 = bf16[4,3584]{1,0:T(4,128)(2,1)S(1)} collective-permute-done((bf16[4,3584]{1,0:T(4,128)(2,1)S(1)}, bf16[4,3584]{1,0:T(4,128)(2,1)S(1)}, u32[]{:S(2)}, u32[]{:S(2)}) %collective-permute-start.15) | collective-permute-done | bytes 28704 | tf_op jit(solution)/shard_map/ppermute | solution.py:36
  53.2 1.0 %collective-permute-done.18 = bf16[4,3584]{1,0:T(4,128)(2,1)S(1)} collective-permute-done((bf16[4,3584]{1,0:T(4,128)(2,1)S(1)}, bf16[4,3584]{1,0:T(4,128)(2,1)S(1)}, u32[]{:S(2)}, u32[]{:S(2)}) %collective-permute-start.18) | collective-permute-done | bytes 28704 | tf_op jit(solution)/shard_map/ppermute | solution.py:36
  54.3 0.7 %maximum_bitcast_fusion.2 = bf16[1,4,7168]{2,1,0:T(4,128)(2,1)} fusion(bf16[4,3584]{1,0:T(4,128)(2,1)S(1)} %add_convert_fusion.4, bf16[4,3584]{1,0:T(4,128)(2,1)S(1)} %add_convert_fusion.5), kind=kLoop, calls=%fused_computation.45 | loop fusion | flops 114688 | bytes 114688 | tf_op jit(solution)/shard_map/broadcast_in_dim | solution.py:266
  (44 shorter events, 0.8 us)
Async XLA Ops:
  0.0 20.7 %copy-start = (bf16[1,7168,128]{2,1,0:T(8,128)(2,1)S(1)}, bf16[1,7168,128]{2,1,0:T(8,128)(2,1)}, u32[]{:S(2)}) copy-start(bf16[1,7168,128]{2,1,0:T(8,128)(2,1)} %param.16) | copy-start | bytes 5505028
  1.0 7.5 %collective-permute-start.3 = (bf16[4,7296]{1,0:T(4,128)(2,1)S(1)}, bf16[4,7296]{1,0:T(4,128)(2,1)S(1)}, u32[]{:S(2)}, u32[]{:S(2)}) collective-permute-start(bf16[4,7296]{1,0:T(4,128)(2,1)S(1)} %shard_map.100), channel_id=1, source_target_pairs={{0,12},{1,13},{2,14},{3,15},{4,8},{5,9},{6,10},{7,11},{8,4},{9,5},... | collective-permute-start | bytes 175112 | tf_op jit(solution)/shard_map/ppermute | solution.py:36
  6.1 5.1 %collective-permute-start.2 = (bf16[4,7296]{1,0:T(4,128)(2,1)S(1)}, bf16[4,7296]{1,0:T(4,128)(2,1)S(1)}, u32[]{:S(2)}, u32[]{:S(2)}) collective-permute-start(bf16[4,7296]{1,0:T(4,128)(2,1)S(1)} %shard_map.100), channel_id=1, source_target_pairs={{0,8},{1,9},{2,10},{3,11},{4,12},{5,13},{6,14},{7,15},{8,0},{9,1},... | collective-permute-start | bytes 175112 | tf_op jit(solution)/shard_map/ppermute | solution.py:36
  6.1 5.1 %collective-permute-start.1 = (bf16[4,7296]{1,0:T(4,128)(2,1)S(1)}, bf16[4,7296]{1,0:T(4,128)(2,1)S(1)}, u32[]{:S(2)}, u32[]{:S(2)}) collective-permute-start(bf16[4,7296]{1,0:T(4,128)(2,1)S(1)} %shard_map.100), channel_id=1, source_target_pairs={{0,4},{1,5},{2,6},{3,7},{4,0},{5,1},{6,2},{7,3},{8,12},{9,13},{10,... | collective-permute-start | bytes 175112 | tf_op jit(solution)/shard_map/ppermute | solution.py:36
  6.7 6.2 %collective-permute-start = (bf16[4,7296]{1,0:T(4,128)(2,1)S(1)}, bf16[4,7296]{1,0:T(4,128)(2,1)S(1)}, u32[]{:S(2)}, u32[]{:S(2)}) collective-permute-start(bf16[4,7296]{1,0:T(4,128)(2,1)S(1)} %shard_map.100), channel_id=1, source_target_pairs={{0,2},{1,3},{2,0},{3,1},{4,6},{5,7},{6,4},{7,5},{8,10},{9,11},{10,... | collective-permute-start | bytes 175112 | tf_op jit(solution)/shard_map/ppermute | solution.py:36
  11.3 6.8 %collective-permute-start.4 = (bf16[12,7296]{1,0:T(8,128)(2,1)S(1)}, bf16[12,7296]{1,0:T(8,128)(2,1)S(1)}, u32[]{:S(2)}, u32[]{:S(2)}) collective-permute-start(bf16[12,7296]{1,0:T(8,128)(2,1)S(1)} %pad_maximum_fusion.1), channel_id=1, source_target_pairs={{0,2},{1,3},{2,0},{3,1},{4,6},{5,7},{6,4},{7,5},{8,10},{9,11},{10,... | collective-permute-start | bytes 525320 | tf_op jit(solution)/shard_map/ppermute | solution.py:36
  18.7 1.9 %collective-permute-start.5 = (bf16[32,7296]{1,0:T(8,128)(2,1)S(1)}, bf16[32,7296]{1,0:T(8,128)(2,1)S(1)}, u32[]{:S(2)}, u32[]{:S(2)}) collective-permute-start(bf16[32,7296]{1,0:T(8,128)(2,1)S(1)} %concatenate.13), channel_id=1, source_target_pairs={{0,1},{1,0},{2,3},{3,2},{4,5},{5,4},{6,7},{7,6},{8,9},{9,8},{10,11... | collective-permute-start | bytes 1400840 | tf_op jit(solution)/shard_map/ppermute | solution.py:36
  21.4 8.4 %collective-permute-start.8 = (bf16[64,128]{1,0:T(8,128)(2,1)S(1)}, bf16[64,128]{1,0:T(8,128)(2,1)S(1)}, u32[]{:S(2)}, u32[]{:S(2)}) collective-permute-start(bf16[64,128]{1,0:T(8,128)(2,1)S(1)} %convolution_convert_fusion.1), channel_id=1, source_target_pairs={{0,3},{1,2},{2,1},{3,0},{4,7},{5,6},{6,5},{7,4},{8,11},{9,10},{10,... | collective-permute-start | bytes 49160 | tf_op jit(solution)/shard_map/ppermute | solution.py:36
  22.8 7.1 %collective-permute-start.7 = (bf16[64,128]{1,0:T(8,128)(2,1)S(1)}, bf16[64,128]{1,0:T(8,128)(2,1)S(1)}, u32[]{:S(2)}, u32[]{:S(2)}) collective-permute-start(bf16[64,128]{1,0:T(8,128)(2,1)S(1)} %convolution_convert_fusion.1), channel_id=1, source_target_pairs={{0,2},{1,3},{2,0},{3,1},{4,6},{5,7},{6,4},{7,5},{8,10},{9,11},{10,... | collective-permute-start | bytes 49160 | tf_op jit(solution)/shard_map/ppermute | solution.py:36
  23.2 6.6 %collective-permute-start.6 = (bf16[64,128]{1,0:T(8,128)(2,1)S(1)}, bf16[64,128]{1,0:T(8,128)(2,1)S(1)}, u32[]{:S(2)}, u32[]{:S(2)}) collective-permute-start(bf16[64,128]{1,0:T(8,128)(2,1)S(1)} %convolution_convert_fusion.1), channel_id=1, source_target_pairs={{0,1},{1,0},{2,3},{3,2},{4,5},{5,4},{6,7},{7,6},{8,9},{9,8},{10,11... | collective-permute-start | bytes 49160 | tf_op jit(solution)/shard_map/ppermute | solution.py:36
  23.5 3.1 %copy-start.1 = (bf16[1,7168,2,256]{3,2,1,0:T(2,128)(2,1)S(1)}, bf16[1,7168,2,256]{3,2,1,0:T(2,128)(2,1)}, u32[]{:S(2)}) copy-start(bf16[1,7168,2,256]{3,2,1,0:T(2,128)(2,1)} %param.14) | copy-start | bytes 22020100
  26.6 3.0 %copy-start.6 = (s32[16]{0:T(128)S(1)}, s32[16]{0:T(128)}, u32[]{:S(2)}) copy-start(s32[16]{0:T(128)} %param.13) | copy-start | bytes 196
  26.6 3.3 %copy-start.4 = (bf16[1,4,128,2,256]{4,3,2,1,0:T(2,128)(2,1)S(1)}, bf16[1,4,128,2,256]{4,3,2,1,0:T(2,128)(2,1)}, u32[]{:S(2)}) copy-start(bf16[1,4,128,2,256]{4,3,2,1,0:T(2,128)(2,1)} %param.17) | copy-start | bytes 1572868
  26.6 6.3 %copy-start.2 = (bf16[1,256,7168]{2,1,0:T(8,128)(2,1)S(1)}, bf16[1,256,7168]{2,1,0:T(8,128)(2,1)}, u32[]{:S(2)}) copy-start(bf16[1,256,7168]{2,1,0:T(8,128)(2,1)} %param.15) | copy-start | bytes 11010052
  29.6 1.0 %copy-start.5 = (bf16[1,4,256,128]{3,2,1,0:T(8,128)(2,1)S(1)}, bf16[1,4,256,128]{3,2,1,0:T(8,128)(2,1)}, u32[]{:S(2)}) copy-start(bf16[1,4,256,128]{3,2,1,0:T(8,128)(2,1)} %param.18) | copy-start | bytes 786436
  30.8 3.0 %collective-permute-start.9 = (bf16[64,128]{1,0:T(8,128)(2,1)S(1)}, bf16[64,128]{1,0:T(8,128)(2,1)S(1)}, u32[]{:S(2)}, u32[]{:S(2)}) collective-permute-start(bf16[64,128]{1,0:T(8,128)(2,1)S(1)} %get-tuple-element.35), channel_id=1, source_target_pairs={{0,1},{1,0},{2,3},{3,2},{4,5},{5,4},{6,7},{7,6},{8,9},{9,8},{10,11... | collective-permute-start | bytes 49160 | tf_op jit(solution)/shard_map/ppermute | solution.py:36
  31.3 3.2 %collective-permute-start.11 = (bf16[64,128]{1,0:T(8,128)(2,1)S(1)}, bf16[64,128]{1,0:T(8,128)(2,1)S(1)}, u32[]{:S(2)}, u32[]{:S(2)}) collective-permute-start(bf16[64,128]{1,0:T(8,128)(2,1)S(1)} %get-tuple-element.36), channel_id=1, source_target_pairs={{0,3},{1,2},{2,1},{3,0},{4,7},{5,6},{6,5},{7,4},{8,11},{9,10},{10,... | collective-permute-start | bytes 49160 | tf_op jit(solution)/shard_map/ppermute | solution.py:36
  32.5 3.7 %collective-permute-start.10 = (bf16[64,128]{1,0:T(8,128)(2,1)S(1)}, bf16[64,128]{1,0:T(8,128)(2,1)S(1)}, u32[]{:S(2)}, u32[]{:S(2)}) collective-permute-start(bf16[64,128]{1,0:T(8,128)(2,1)S(1)} %get-tuple-element.37), channel_id=1, source_target_pairs={{0,2},{1,3},{2,0},{3,1},{4,6},{5,7},{6,4},{7,5},{8,10},{9,11},{10,... | collective-permute-start | bytes 49160 | tf_op jit(solution)/shard_map/ppermute | solution.py:36
  33.0 3.3 %copy-start.3 = (bf16[1,128,7168]{2,1,0:T(8,128)(2,1)S(1)}, bf16[1,128,7168]{2,1,0:T(8,128)(2,1)}, u32[]{:S(2)}) copy-start(bf16[1,128,7168]{2,1,0:T(8,128)(2,1)} %param.19) | copy-start | bytes 5505028
  36.8 1.9 %collective-permute-start.12 = (bf16[32,7168]{1,0:T(8,128)(2,1)S(1)}, bf16[32,7168]{1,0:T(8,128)(2,1)S(1)}, u32[]{:S(2)}, u32[]{:S(2)}) collective-permute-start(bf16[32,7168]{1,0:T(8,128)(2,1)S(1)} %slice_select_fusion), channel_id=1, source_target_pairs={{0,1},{1,0},{2,3},{3,2},{4,5},{5,4},{6,7},{7,6},{8,9},{9,8},{10,11... | collective-permute-start | bytes 1376264 | tf_op jit(solution)/shard_map/ppermute | solution.py:36
  38.9 4.9 %collective-permute-start.13 = (bf16[16,3584]{1,0:T(8,128)(2,1)S(1)}, bf16[16,3584]{1,0:T(8,128)(2,1)S(1)}, u32[]{:S(2)}, u32[]{:S(2)}) collective-permute-start(bf16[16,3584]{1,0:T(8,128)(2,1)S(1)} %get-tuple-element.14), channel_id=1, source_target_pairs={{0,4},{1,3},{2,6},{3,1},{4,0},{5,7},{6,2},{7,5},{8,12},{9,11},{10,... | collective-permute-start | bytes 344072 | tf_op jit(solution)/shard_map/ppermute | solution.py:36
  39.5 5.5 %collective-permute-start.16 = (bf16[16,3584]{1,0:T(8,128)(2,1)S(1)}, bf16[16,3584]{1,0:T(8,128)(2,1)S(1)}, u32[]{:S(2)}, u32[]{:S(2)}) collective-permute-start(bf16[16,3584]{1,0:T(8,128)(2,1)S(1)} %get-tuple-element.16), channel_id=1, source_target_pairs={{0,4},{1,3},{2,6},{3,1},{4,0},{5,7},{6,2},{7,5},{8,12},{9,11},{10,... | collective-permute-start | bytes 344072 | tf_op jit(solution)/shard_map/ppermute | solution.py:36
  43.8 4.2 %collective-permute-start.14 = (bf16[8,3584]{1,0:T(8,128)(2,1)S(1)}, bf16[8,3584]{1,0:T(8,128)(2,1)S(1)}, u32[]{:S(2)}, u32[]{:S(2)}) collective-permute-start(bf16[8,3584]{1,0:T(8,128)(2,1)S(1)} %broadcast_select_fusion.11), channel_id=1, source_target_pairs={{0,2},{1,5},{2,0},{3,7},{4,6},{5,1},{6,4},{7,3},{8,10},{9,13},{10,... | collective-permute-start | bytes 172040 | tf_op jit(solution)/shard_map/ppermute | solution.py:36
  45.0 4.3 %collective-permute-start.17 = (bf16[8,3584]{1,0:T(8,128)(2,1)S(1)}, bf16[8,3584]{1,0:T(8,128)(2,1)S(1)}, u32[]{:S(2)}, u32[]{:S(2)}) collective-permute-start(bf16[8,3584]{1,0:T(8,128)(2,1)S(1)} %broadcast_select_fusion.10), channel_id=1, source_target_pairs={{0,2},{1,5},{2,0},{3,7},{4,6},{5,1},{6,4},{7,3},{8,10},{9,13},{10,... | collective-permute-start | bytes 172040 | tf_op jit(solution)/shard_map/ppermute | solution.py:36
  48.1 5.1 %collective-permute-start.15 = (bf16[4,3584]{1,0:T(4,128)(2,1)S(1)}, bf16[4,3584]{1,0:T(4,128)(2,1)S(1)}, u32[]{:S(2)}, u32[]{:S(2)}) collective-permute-start(bf16[4,3584]{1,0:T(4,128)(2,1)S(1)} %slice.98), channel_id=1, source_target_pairs={{0,8},{1,9},{2,10},{3,11},{4,12},{5,13},{6,14},{7,15},{8,0},{9,1},... | collective-permute-start | bytes 86024 | tf_op jit(solution)/shard_map/ppermute | solution.py:36
  49.4 4.8 %collective-permute-start.18 = (bf16[4,3584]{1,0:T(4,128)(2,1)S(1)}, bf16[4,3584]{1,0:T(4,128)(2,1)S(1)}, u32[]{:S(2)}, u32[]{:S(2)}) collective-permute-start(bf16[4,3584]{1,0:T(4,128)(2,1)S(1)} %slice.102), channel_id=1, source_target_pairs={{0,8},{1,9},{2,10},{3,11},{4,12},{5,13},{6,14},{7,15},{8,0},{9,1},... | collective-permute-start | bytes 86024 | tf_op jit(solution)/shard_map/ppermute | solution.py:36

commit v17 on v16

--- a/solution.py
+++ b/solution.py
@@ -119,6 +119,30 @@
     )(x, base)
 
 
+def down_kernel(hidden, base, out, weights, sems):
+    step = base.shape[1] // sems.shape[0]
+    parts = [pl.ds(k * step, step) for k in range(sems.shape[0])]
+    copies = [pltpu.make_async_copy(base.at[:, part], weights.at[:, part], sems.at[k]) for k, part in enumerate(parts)]
+    for copy in copies:
+        copy.start()
+    for copy, part in zip(copies, parts):
+        copy.wait()
+        out[:, part] = jnp.dot(hidden[...], weights[:, part], preferred_element_type=jnp.float32)
+
+
+def down_product(hidden, base):
+    rows, width = hidden.shape[0], base.shape[1]
+    return pl.pallas_call(
+        down_kernel,
+        out_shape=jax.ShapeDtypeStruct((rows, width), jnp.float32),
+        in_specs=[VMEM, HBM],
+        out_specs=VMEM,
+        scratch_shapes=[pltpu.VMEM(base.shape, base.dtype), pltpu.SemaphoreType.DMA((width // 1024,))],
+        compiler_params=pltpu.CompilerParams(vmem_limit_bytes=16 << 20),
+        cost_estimate=pl.CostEstimate(flops=2 * rows * base.size, bytes_accessed=2 * base.size, transcendentals=0),
+    )(hidden, in_hbm(base))
+
+
 def part_kernel(bit, term, received, *refs):
     *outs, total = refs
     half, width = total.shape
@@ -234,7 +258,7 @@
     own_scale = lax.dynamic_index_in_dim(scale, me, 0, keepdims=False)
     scaled = (own_scale[:, None] * lowrank).astype(jnp.bfloat16)
 
-    term = jnp.dot(hidden_sum, base_down[0], preferred_element_type=jnp.float32)
+    term = down_product(hidden_sum, base_down[0])
     term = (term + jnp.dot(scaled, delta_back[0], preferred_element_type=jnp.float32)).astype(jnp.bfloat16)
 
     def add(kept, received):

time: 55.1 us -> 55.1 us (level)
  Pallas kernels: 4.12 us -> 6.83 us
  waiting for transfers between devices: 22.6 us -> 19.9 us
  matrix products: 2.08 us -> 1.33 us
  starting transfers between devices: 20 us -> 20.7 us
    pallas_call x0 -> x1, Pallas kernels: none -> 2.71 us  [down_product(): pl.pallas_call(down_kernel, out_shape=jax.ShapeDtypeStruct((rows, width),...]
    ppermute x19, waiting for transfers between devices: 22.6 us -> 19.9 us  [trade(): return lax.ppermute(value, ('expert', 'tensor'), pairs)]
    dot_general x1 -> x0, matrix products: 0.75 us -> none  [local(): term = jnp.dot(hidden_sum, base_down[0], preferred_element_type=jnp.float32)]
    ppermute x19, starting transfers between devices: 20 us -> 20.7 us  [trade(): return lax.ppermute(value, ('expert', 'tensor'), pairs)]
    unnamed x14 -> x12, local copies, waits for them, and re-layouts: 3.43 us -> 3.43 us
  transfers between devices with their start and end apart: 19 -> 19, of which waited for: 12 -> 11; matrix products, arithmetic and copies ran while one was open for 3% -> 1% of each run, Pallas kernels for 5% -> 10%
where the time goes in v17:
time: 55.1 us; the launch traced here: 54.9 us
  starting transfers between devices  20.7 us (38%)
  waiting for transfers between devices  19.9 us (36%)
  Pallas kernels  6.83 us (12%)
  local copies, waits for them, and re-layouts  3.98 us (7%)
  other arithmetic  1.9 us (3%)
  matrix products  1.33 us (2%)
    ppermute x19, starting transfers between devices, trade(): return lax.ppermute(value, ('expert', 'tensor'), pairs)  20.7 us
    ppermute x19, waiting for transfers between devices, trade(): return lax.ppermute(value, ('expert', 'tensor'), pairs)  19.9 us
    unnamed x12, local copies, waits for them, and re-layouts  3.43 us
    pallas_call x1, Pallas kernels, gate_up_product(): pl.pallas_call(gate_up_kernel, out_shape=jax.ShapeDtypeStruct((2 * x.shap...  2.96 us
    pallas_call x1, Pallas kernels, down_product(): pl.pallas_call(down_kernel, out_shape=jax.ShapeDtypeStruct((rows, width),...  2.71 us
  transfers between devices with their start and end apart: 19, of which 11 were waited for; matrix products, arithmetic and copies ran while one was open for 1% of the time, Pallas kernels for 10%

profile of v17, /device:TPU:0, one launch (start us, length us, event | category | flops | bytes accessed | tf_op | source)
XLA Modules:
  0.0 54.9 jit_solution(6255202164937670796)
XLA Ops:
  0.0 1.0 %shard_map.100 = bf16[4,7296]{1,0:T(4,128)(2,1)S(1)} custom-call(bf16[4,7168]{1,0:T(4,128)(2,1)} %bitcast.64, s32[4,8]{1,0:T(4,128)} %bitcast.65, s32[4,8]{1,0:T(4,128)} %bitcast.66), custom_call_target="tpu_custom_call" | custom-call | flops 20000000000 | bytes 114688 | tf_op jit(solution)/shard_map/pallas_call | solution.py:70
  1.0 5.1 %collective-permute-start.3 = (bf16[4,7296]{1,0:T(4,128)(2,1)S(1)}, bf16[4,7296]{1,0:T(4,128)(2,1)S(1)}, u32[]{:S(2)}, u32[]{:S(2)}) collective-permute-start(bf16[4,7296]{1,0:T(4,128)(2,1)S(1)} %shard_map.100), channel_id=1, source_target_pairs={{0,12},{1,13},{2,14},{3,15},{4,8},{5,9},{6,10},{7,11},{8,4},{9,5},... | collective-permute-start | bytes 175112 | tf_op jit(solution)/shard_map/ppermute | solution.py:36
  6.1 0.6 %collective-permute-start.1 = (bf16[4,7296]{1,0:T(4,128)(2,1)S(1)}, bf16[4,7296]{1,0:T(4,128)(2,1)S(1)}, u32[]{:S(2)}, u32[]{:S(2)}) collective-permute-start(bf16[4,7296]{1,0:T(4,128)(2,1)S(1)} %shard_map.100), channel_id=1, source_target_pairs={{0,4},{1,5},{2,6},{3,7},{4,0},{5,1},{6,2},{7,3},{8,12},{9,13},{10,... | collective-permute-start | bytes 175112 | tf_op jit(solution)/shard_map/ppermute | solution.py:36
  6.7 1.6 %collective-permute-start = (bf16[4,7296]{1,0:T(4,128)(2,1)S(1)}, bf16[4,7296]{1,0:T(4,128)(2,1)S(1)}, u32[]{:S(2)}, u32[]{:S(2)}) collective-permute-start(bf16[4,7296]{1,0:T(4,128)(2,1)S(1)} %shard_map.100), channel_id=1, source_target_pairs={{0,2},{1,3},{2,0},{3,1},{4,6},{5,7},{6,4},{7,5},{8,10},{9,11},{10,... | collective-permute-start | bytes 175112 | tf_op jit(solution)/shard_map/ppermute | solution.py:36
  8.4 0.1 collective-permute-done.3
  8.5 2.7 %collective-permute-done.2 = bf16[4,7296]{1,0:T(4,128)(2,1)S(1)} collective-permute-done((bf16[4,7296]{1,0:T(4,128)(2,1)S(1)}, bf16[4,7296]{1,0:T(4,128)(2,1)S(1)}, u32[]{:S(2)}, u32[]{:S(2)}) %collective-permute-start.2) | collective-permute-done | bytes 58400 | tf_op jit(solution)/shard_map/ppermute | solution.py:36
  11.2 0.1 pad_maximum_fusion.1
  11.3 1.6 %collective-permute-start.4 = (bf16[12,7296]{1,0:T(8,128)(2,1)S(1)}, bf16[12,7296]{1,0:T(8,128)(2,1)S(1)}, u32[]{:S(2)}, u32[]{:S(2)}) collective-permute-start(bf16[12,7296]{1,0:T(8,128)(2,1)S(1)} %pad_maximum_fusion.1), channel_id=1, source_target_pairs={{0,2},{1,3},{2,0},{3,1},{4,6},{5,7},{6,4},{7,5},{8,10},{9,11},{10,... | collective-permute-start | bytes 525320 | tf_op jit(solution)/shard_map/ppermute | solution.py:36
  13.0 5.1 %collective-permute-done.4 = bf16[12,7296]{1,0:T(8,128)(2,1)S(1)} collective-permute-done((bf16[12,7296]{1,0:T(8,128)(2,1)S(1)}, bf16[12,7296]{1,0:T(8,128)(2,1)S(1)}, u32[]{:S(2)}, u32[]{:S(2)}) %collective-permute-start.4) | collective-permute-done | bytes 175136 | tf_op jit(solution)/shard_map/ppermute | solution.py:36
  18.2 0.2 broadcast_select_fusion.2
  18.3 0.3 concatenate.13
  18.7 0.1 collective-permute-start.5
  18.8 1.8 %collective-permute-done.5 = bf16[32,7296]{1,0:T(8,128)(2,1)S(1)} collective-permute-done((bf16[32,7296]{1,0:T(8,128)(2,1)S(1)}, bf16[32,7296]{1,0:T(8,128)(2,1)S(1)}, u32[]{:S(2)}, u32[]{:S(2)}) %collective-permute-start.5) | collective-permute-done | bytes 466976 | tf_op jit(solution)/shard_map/ppermute | solution.py:36
  20.6 0.1 broadcast_select_fusion.1
  20.7 0.2 convert_reduce_fusion
  20.9 0.5 convolution_convert_fusion.1
  21.4 1.4 %collective-permute-start.8 = (bf16[64,128]{1,0:T(8,128)(2,1)S(1)}, bf16[64,128]{1,0:T(8,128)(2,1)S(1)}, u32[]{:S(2)}, u32[]{:S(2)}) collective-permute-start(bf16[64,128]{1,0:T(8,128)(2,1)S(1)} %convolution_convert_fusion.1), channel_id=1, source_target_pairs={{0,3},{1,2},{2,1},{3,0},{4,7},{5,6},{6,5},{7,4},{8,11},{9,10},{10,... | collective-permute-start | bytes 49160 | tf_op jit(solution)/shard_map/ppermute | solution.py:36
  22.8 0.5 collective-permute-start.7
  23.2 0.1 collective-permute-start.6
  23.3 0.1 fusion.22
  23.5 3.1 %copy-done.1 = bf16[1,7168,2,256]{3,2,1,0:T(2,128)(2,1)S(1)} copy-done((bf16[1,7168,2,256]{3,2,1,0:T(2,128)(2,1)S(1)}, bf16[1,7168,2,256]{3,2,1,0:T(2,128)(2,1)}, u32[]{:S(2)}) %copy-start.1) | copy-done | bytes 7340056
  26.6 3.0 %shard_map.101 = f32[128,256]{1,0:T(8,128)S(1)} custom-call(bf16[64,7296]{1,0:T(8,128)(2,1)S(1)} %pad_maximum_fusion.x, bf16[7168,2,256]{2,1,0:T(2,128)(2,1)S(1)} %bitcast.57), custom_call_target="tpu_custom_call" | custom-call | flops 469762048 | bytes 7340032 | tf_op jit(solution)/shard_map/pallas_call | solution.py:110
  29.6 0.1 select_reduce_fusion
  29.7 0.1 select_reduce_fusion.1
  29.9 0.2 fusion.3
  30.1 0.1 multiply_reduce_fusion
  30.2 0.3 copy-done.4
  30.5 0.2 convolution_convert_fusion
  30.8 0.5 collective-permute-start.9
  31.3 1.3 %collective-permute-start.11 = (bf16[64,128]{1,0:T(8,128)(2,1)S(1)}, bf16[64,128]{1,0:T(8,128)(2,1)S(1)}, u32[]{:S(2)}, u32[]{:S(2)}) collective-permute-start(bf16[64,128]{1,0:T(8,128)(2,1)S(1)} %get-tuple-element.36), channel_id=1, source_target_pairs={{0,3},{1,2},{2,1},{3,0},{4,7},{5,6},{6,5},{7,4},{8,11},{9,10},{10,... | collective-permute-start | bytes 49160 | tf_op jit(solution)/shard_map/ppermute | solution.py:36
  32.5 0.4 collective-permute-start.10
  33.0 2.7 %shard_map.102 = f32[64,7168]{1,0:T(8,128)S(1)} custom-call(bf16[64,256]{1,0:T(8,128)(2,1)S(1)} %get-tuple-element.17.hidden, bf16[256,7168]{1,0:T(8,128)(2,1)} %bitcast.58), custom_call_target="tpu_custom_call" | custom-call | flops 234881024 | bytes 3670016 | tf_op jit(solution)/shard_map/pallas_call | solution.py:135
  35.7 0.6 %collective-permute-done.10 = bf16[64,128]{1,0:T(8,128)(2,1)S(1)} collective-permute-done((bf16[64,128]{1,0:T(8,128)(2,1)S(1)}, bf16[64,128]{1,0:T(8,128)(2,1)S(1)}, u32[]{:S(2)}, u32[]{:S(2)}) %collective-permute-start.10) | collective-permute-done | bytes 16416 | tf_op jit(solution)/shard_map/ppermute | solution.py:36
  36.3 0.5 fusion.term
  36.8 0.1 collective-permute-start.12
  36.9 1.8 %collective-permute-done.12.received = bf16[32,7168]{1,0:T(8,128)(2,1)S(1)} collective-permute-done((bf16[32,7168]{1,0:T(8,128)(2,1)S(1)}, bf16[32,7168]{1,0:T(8,128)(2,1)S(1)}, u32[]{:S(2)}, u32[]{:S(2)}) %collective-permute-start.12) | collective-permute-done | bytes 458784 | tf_op jit(solution)/shard_map/ppermute | solution.py:36
  38.7 0.2 shard_map.103
  38.9 0.6 %collective-permute-start.13 = (bf16[16,3584]{1,0:T(8,128)(2,1)S(1)}, bf16[16,3584]{1,0:T(8,128)(2,1)S(1)}, u32[]{:S(2)}, u32[]{:S(2)}) collective-permute-start(bf16[16,3584]{1,0:T(8,128)(2,1)S(1)} %get-tuple-element.14), channel_id=1, source_target_pairs={{0,4},{1,3},{2,6},{3,1},{4,0},{5,7},{6,2},{7,5},{8,12},{9,11},{10,... | collective-permute-start | bytes 344072 | tf_op jit(solution)/shard_map/ppermute | solution.py:36
  39.5 1.5 %collective-permute-start.16 = (bf16[16,3584]{1,0:T(8,128)(2,1)S(1)}, bf16[16,3584]{1,0:T(8,128)(2,1)S(1)}, u32[]{:S(2)}, u32[]{:S(2)}) collective-permute-start(bf16[16,3584]{1,0:T(8,128)(2,1)S(1)} %get-tuple-element.16), channel_id=1, source_target_pairs={{0,4},{1,3},{2,6},{3,1},{4,0},{5,7},{6,2},{7,5},{8,12},{9,11},{10,... | collective-permute-start | bytes 344072 | tf_op jit(solution)/shard_map/ppermute | solution.py:36
  41.0 2.8 %collective-permute-done.13 = bf16[16,3584]{1,0:T(8,128)(2,1)S(1)} collective-permute-done((bf16[16,3584]{1,0:T(8,128)(2,1)S(1)}, bf16[16,3584]{1,0:T(8,128)(2,1)S(1)}, u32[]{:S(2)}, u32[]{:S(2)}) %collective-permute-start.13) | collective-permute-done | bytes 114720 | tf_op jit(solution)/shard_map/ppermute | solution.py:36
  43.8 1.1 %collective-permute-start.14 = (bf16[8,3584]{1,0:T(8,128)(2,1)S(1)}, bf16[8,3584]{1,0:T(8,128)(2,1)S(1)}, u32[]{:S(2)}, u32[]{:S(2)}) collective-permute-start(bf16[8,3584]{1,0:T(8,128)(2,1)S(1)} %broadcast_select_fusion.11), channel_id=1, source_target_pairs={{0,2},{1,5},{2,0},{3,7},{4,6},{5,1},{6,4},{7,3},{8,10},{9,13},{10,... | collective-permute-start | bytes 172040 | tf_op jit(solution)/shard_map/ppermute | solution.py:36
  45.0 1.1 %collective-permute-start.17 = (bf16[8,3584]{1,0:T(8,128)(2,1)S(1)}, bf16[8,3584]{1,0:T(8,128)(2,1)S(1)}, u32[]{:S(2)}, u32[]{:S(2)}) collective-permute-start(bf16[8,3584]{1,0:T(8,128)(2,1)S(1)} %broadcast_select_fusion.10), channel_id=1, source_target_pairs={{0,2},{1,5},{2,0},{3,7},{4,6},{5,1},{6,4},{7,3},{8,10},{9,13},{10,... | collective-permute-start | bytes 172040 | tf_op jit(solution)/shard_map/ppermute | solution.py:36
  46.1 1.9 %collective-permute-done.14 = bf16[8,3584]{1,0:T(8,128)(2,1)S(1)} collective-permute-done((bf16[8,3584]{1,0:T(8,128)(2,1)S(1)}, bf16[8,3584]{1,0:T(8,128)(2,1)S(1)}, u32[]{:S(2)}, u32[]{:S(2)}) %collective-permute-start.14) | collective-permute-done | bytes 57376 | tf_op jit(solution)/shard_map/ppermute | solution.py:36
  48.1 1.3 %collective-permute-start.15 = (bf16[4,3584]{1,0:T(4,128)(2,1)S(1)}, bf16[4,3584]{1,0:T(4,128)(2,1)S(1)}, u32[]{:S(2)}, u32[]{:S(2)}) collective-permute-start(bf16[4,3584]{1,0:T(4,128)(2,1)S(1)} %slice.98), channel_id=1, source_target_pairs={{0,8},{1,9},{2,10},{3,11},{4,12},{5,13},{6,14},{7,15},{8,0},{9,1},... | collective-permute-start | bytes 86024 | tf_op jit(solution)/shard_map/ppermute | solution.py:36
  49.4 1.8 %collective-permute-start.18 = (bf16[4,3584]{1,0:T(4,128)(2,1)S(1)}, bf16[4,3584]{1,0:T(4,128)(2,1)S(1)}, u32[]{:S(2)}, u32[]{:S(2)}) collective-permute-start(bf16[4,3584]{1,0:T(4,128)(2,1)S(1)} %slice.102), channel_id=1, source_target_pairs={{0,8},{1,9},{2,10},{3,11},{4,12},{5,13},{6,14},{7,15},{8,0},{9,1},... | collective-permute-start | bytes 86024 | tf_op jit(solution)/shard_map/ppermute | solution.py:36
  51.2 2.0 %collective-permute-done.15 = bf16[4,3584]{1,0:T(4,128)(2,1)S(1)} collective-permute-done((bf16[4,3584]{1,0:T(4,128)(2,1)S(1)}, bf16[4,3584]{1,0:T(4,128)(2,1)S(1)}, u32[]{:S(2)}, u32[]{:S(2)}) %collective-permute-start.15) | collective-permute-done | bytes 28704 | tf_op jit(solution)/shard_map/ppermute | solution.py:36
  53.2 1.0 %collective-permute-done.18 = bf16[4,3584]{1,0:T(4,128)(2,1)S(1)} collective-permute-done((bf16[4,3584]{1,0:T(4,128)(2,1)S(1)}, bf16[4,3584]{1,0:T(4,128)(2,1)S(1)}, u32[]{:S(2)}, u32[]{:S(2)}) %collective-permute-start.18) | collective-permute-done | bytes 28704 | tf_op jit(solution)/shard_map/ppermute | solution.py:36
  54.3 0.7 %maximum_bitcast_fusion.2 = bf16[1,4,7168]{2,1,0:T(4,128)(2,1)} fusion(bf16[4,3584]{1,0:T(4,128)(2,1)S(1)} %add_convert_fusion.4, bf16[4,3584]{1,0:T(4,128)(2,1)S(1)} %add_convert_fusion.5), kind=kLoop, calls=%fused_computation.43 | loop fusion | flops 114688 | bytes 114688 | tf_op jit(solution)/shard_map/broadcast_in_dim | solution.py:290
  (42 shorter events, 0.7 us)
Async XLA Ops:
  0.0 20.7 %copy-start = (bf16[1,7168,128]{2,1,0:T(8,128)(2,1)S(1)}, bf16[1,7168,128]{2,1,0:T(8,128)(2,1)}, u32[]{:S(2)}) copy-start(bf16[1,7168,128]{2,1,0:T(8,128)(2,1)} %param.16) | copy-start | bytes 5505028
  1.0 7.5 %collective-permute-start.3 = (bf16[4,7296]{1,0:T(4,128)(2,1)S(1)}, bf16[4,7296]{1,0:T(4,128)(2,1)S(1)}, u32[]{:S(2)}, u32[]{:S(2)}) collective-permute-start(bf16[4,7296]{1,0:T(4,128)(2,1)S(1)} %shard_map.100), channel_id=1, source_target_pairs={{0,12},{1,13},{2,14},{3,15},{4,8},{5,9},{6,10},{7,11},{8,4},{9,5},... | collective-permute-start | bytes 175112 | tf_op jit(solution)/shard_map/ppermute | solution.py:36
  6.1 5.1 %collective-permute-start.2 = (bf16[4,7296]{1,0:T(4,128)(2,1)S(1)}, bf16[4,7296]{1,0:T(4,128)(2,1)S(1)}, u32[]{:S(2)}, u32[]{:S(2)}) collective-permute-start(bf16[4,7296]{1,0:T(4,128)(2,1)S(1)} %shard_map.100), channel_id=1, source_target_pairs={{0,8},{1,9},{2,10},{3,11},{4,12},{5,13},{6,14},{7,15},{8,0},{9,1},... | collective-permute-start | bytes 175112 | tf_op jit(solution)/shard_map/ppermute | solution.py:36
  6.1 5.1 %collective-permute-start.1 = (bf16[4,7296]{1,0:T(4,128)(2,1)S(1)}, bf16[4,7296]{1,0:T(4,128)(2,1)S(1)}, u32[]{:S(2)}, u32[]{:S(2)}) collective-permute-start(bf16[4,7296]{1,0:T(4,128)(2,1)S(1)} %shard_map.100), channel_id=1, source_target_pairs={{0,4},{1,5},{2,6},{3,7},{4,0},{5,1},{6,2},{7,3},{8,12},{9,13},{10,... | collective-permute-start | bytes 175112 | tf_op jit(solution)/shard_map/ppermute | solution.py:36
  6.7 6.2 %collective-permute-start = (bf16[4,7296]{1,0:T(4,128)(2,1)S(1)}, bf16[4,7296]{1,0:T(4,128)(2,1)S(1)}, u32[]{:S(2)}, u32[]{:S(2)}) collective-permute-start(bf16[4,7296]{1,0:T(4,128)(2,1)S(1)} %shard_map.100), channel_id=1, source_target_pairs={{0,2},{1,3},{2,0},{3,1},{4,6},{5,7},{6,4},{7,5},{8,10},{9,11},{10,... | collective-permute-start | bytes 175112 | tf_op jit(solution)/shard_map/ppermute | solution.py:36
  11.3 6.8 %collective-permute-start.4 = (bf16[12,7296]{1,0:T(8,128)(2,1)S(1)}, bf16[12,7296]{1,0:T(8,128)(2,1)S(1)}, u32[]{:S(2)}, u32[]{:S(2)}) collective-permute-start(bf16[12,7296]{1,0:T(8,128)(2,1)S(1)} %pad_maximum_fusion.1), channel_id=1, source_target_pairs={{0,2},{1,3},{2,0},{3,1},{4,6},{5,7},{6,4},{7,5},{8,10},{9,11},{10,... | collective-permute-start | bytes 525320 | tf_op jit(solution)/shard_map/ppermute | solution.py:36
  18.7 1.9 %collective-permute-start.5 = (bf16[32,7296]{1,0:T(8,128)(2,1)S(1)}, bf16[32,7296]{1,0:T(8,128)(2,1)S(1)}, u32[]{:S(2)}, u32[]{:S(2)}) collective-permute-start(bf16[32,7296]{1,0:T(8,128)(2,1)S(1)} %concatenate.13), channel_id=1, source_target_pairs={{0,1},{1,0},{2,3},{3,2},{4,5},{5,4},{6,7},{7,6},{8,9},{9,8},{10,11... | collective-permute-start | bytes 1400840 | tf_op jit(solution)/shard_map/ppermute | solution.py:36
  21.4 8.4 %collective-permute-start.8 = (bf16[64,128]{1,0:T(8,128)(2,1)S(1)}, bf16[64,128]{1,0:T(8,128)(2,1)S(1)}, u32[]{:S(2)}, u32[]{:S(2)}) collective-permute-start(bf16[64,128]{1,0:T(8,128)(2,1)S(1)} %convolution_convert_fusion.1), channel_id=1, source_target_pairs={{0,3},{1,2},{2,1},{3,0},{4,7},{5,6},{6,5},{7,4},{8,11},{9,10},{10,... | collective-permute-start | bytes 49160 | tf_op jit(solution)/shard_map/ppermute | solution.py:36
  22.8 7.1 %collective-permute-start.7 = (bf16[64,128]{1,0:T(8,128)(2,1)S(1)}, bf16[64,128]{1,0:T(8,128)(2,1)S(1)}, u32[]{:S(2)}, u32[]{:S(2)}) collective-permute-start(bf16[64,128]{1,0:T(8,128)(2,1)S(1)} %convolution_convert_fusion.1), channel_id=1, source_target_pairs={{0,2},{1,3},{2,0},{3,1},{4,6},{5,7},{6,4},{7,5},{8,10},{9,11},{10,... | collective-permute-start | bytes 49160 | tf_op jit(solution)/shard_map/ppermute | solution.py:36
  23.2 6.6 %collective-permute-start.6 = (bf16[64,128]{1,0:T(8,128)(2,1)S(1)}, bf16[64,128]{1,0:T(8,128)(2,1)S(1)}, u32[]{:S(2)}, u32[]{:S(2)}) collective-permute-start(bf16[64,128]{1,0:T(8,128)(2,1)S(1)} %convolution_convert_fusion.1), channel_id=1, source_target_pairs={{0,1},{1,0},{2,3},{3,2},{4,5},{5,4},{6,7},{7,6},{8,9},{9,8},{10,11... | collective-permute-start | bytes 49160 | tf_op jit(solution)/shard_map/ppermute | solution.py:36
  23.5 3.1 %copy-start.1 = (bf16[1,7168,2,256]{3,2,1,0:T(2,128)(2,1)S(1)}, bf16[1,7168,2,256]{3,2,1,0:T(2,128)(2,1)}, u32[]{:S(2)}) copy-start(bf16[1,7168,2,256]{3,2,1,0:T(2,128)(2,1)} %param.14) | copy-start | bytes 22020100
  26.6 3.0 %copy-start.5 = (s32[16]{0:T(128)S(1)}, s32[16]{0:T(128)}, u32[]{:S(2)}) copy-start(s32[16]{0:T(128)} %param.13) | copy-start | bytes 196
  26.6 3.3 %copy-start.3 = (bf16[1,4,128,2,256]{4,3,2,1,0:T(2,128)(2,1)S(1)}, bf16[1,4,128,2,256]{4,3,2,1,0:T(2,128)(2,1)}, u32[]{:S(2)}) copy-start(bf16[1,4,128,2,256]{4,3,2,1,0:T(2,128)(2,1)} %param.17) | copy-start | bytes 1572868
  29.6 1.0 %copy-start.4 = (bf16[1,4,256,128]{3,2,1,0:T(8,128)(2,1)S(1)}, bf16[1,4,256,128]{3,2,1,0:T(8,128)(2,1)}, u32[]{:S(2)}) copy-start(bf16[1,4,256,128]{3,2,1,0:T(8,128)(2,1)} %param.18) | copy-start | bytes 786436
  30.8 4.9 %collective-permute-start.9 = (bf16[64,128]{1,0:T(8,128)(2,1)S(1)}, bf16[64,128]{1,0:T(8,128)(2,1)S(1)}, u32[]{:S(2)}, u32[]{:S(2)}) collective-permute-start(bf16[64,128]{1,0:T(8,128)(2,1)S(1)} %get-tuple-element.35), channel_id=1, source_target_pairs={{0,1},{1,0},{2,3},{3,2},{4,5},{5,4},{6,7},{7,6},{8,9},{9,8},{10,11... | collective-permute-start | bytes 49160 | tf_op jit(solution)/shard_map/ppermute | solution.py:36
  31.3 4.4 %collective-permute-start.11 = (bf16[64,128]{1,0:T(8,128)(2,1)S(1)}, bf16[64,128]{1,0:T(8,128)(2,1)S(1)}, u32[]{:S(2)}, u32[]{:S(2)}) collective-permute-start(bf16[64,128]{1,0:T(8,128)(2,1)S(1)} %get-tuple-element.36), channel_id=1, source_target_pairs={{0,3},{1,2},{2,1},{3,0},{4,7},{5,6},{6,5},{7,4},{8,11},{9,10},{10,... | collective-permute-start | bytes 49160 | tf_op jit(solution)/shard_map/ppermute | solution.py:36
  32.5 3.7 %collective-permute-start.10 = (bf16[64,128]{1,0:T(8,128)(2,1)S(1)}, bf16[64,128]{1,0:T(8,128)(2,1)S(1)}, u32[]{:S(2)}, u32[]{:S(2)}) collective-permute-start(bf16[64,128]{1,0:T(8,128)(2,1)S(1)} %get-tuple-element.37), channel_id=1, source_target_pairs={{0,2},{1,3},{2,0},{3,1},{4,6},{5,7},{6,4},{7,5},{8,10},{9,11},{10,... | collective-permute-start | bytes 49160 | tf_op jit(solution)/shard_map/ppermute | solution.py:36
  33.0 3.3 %copy-start.2 = (bf16[1,128,7168]{2,1,0:T(8,128)(2,1)S(1)}, bf16[1,128,7168]{2,1,0:T(8,128)(2,1)}, u32[]{:S(2)}) copy-start(bf16[1,128,7168]{2,1,0:T(8,128)(2,1)} %param.19) | copy-start | bytes 5505028
  36.8 1.9 %collective-permute-start.12 = (bf16[32,7168]{1,0:T(8,128)(2,1)S(1)}, bf16[32,7168]{1,0:T(8,128)(2,1)S(1)}, u32[]{:S(2)}, u32[]{:S(2)}) collective-permute-start(bf16[32,7168]{1,0:T(8,128)(2,1)S(1)} %slice_select_fusion), channel_id=1, source_target_pairs={{0,1},{1,0},{2,3},{3,2},{4,5},{5,4},{6,7},{7,6},{8,9},{9,8},{10,11... | collective-permute-start | bytes 1376264 | tf_op jit(solution)/shard_map/ppermute | solution.py:36
  38.9 4.9 %collective-permute-start.13 = (bf16[16,3584]{1,0:T(8,128)(2,1)S(1)}, bf16[16,3584]{1,0:T(8,128)(2,1)S(1)}, u32[]{:S(2)}, u32[]{:S(2)}) collective-permute-start(bf16[16,3584]{1,0:T(8,128)(2,1)S(1)} %get-tuple-element.14), channel_id=1, source_target_pairs={{0,4},{1,3},{2,6},{3,1},{4,0},{5,7},{6,2},{7,5},{8,12},{9,11},{10,... | collective-permute-start | bytes 344072 | tf_op jit(solution)/shard_map/ppermute | solution.py:36
  39.5 5.5 %collective-permute-start.16 = (bf16[16,3584]{1,0:T(8,128)(2,1)S(1)}, bf16[16,3584]{1,0:T(8,128)(2,1)S(1)}, u32[]{:S(2)}, u32[]{:S(2)}) collective-permute-start(bf16[16,3584]{1,0:T(8,128)(2,1)S(1)} %get-tuple-element.16), channel_id=1, source_target_pairs={{0,4},{1,3},{2,6},{3,1},{4,0},{5,7},{6,2},{7,5},{8,12},{9,11},{10,... | collective-permute-start | bytes 344072 | tf_op jit(solution)/shard_map/ppermute | solution.py:36
  43.8 4.2 %collective-permute-start.14 = (bf16[8,3584]{1,0:T(8,128)(2,1)S(1)}, bf16[8,3584]{1,0:T(8,128)(2,1)S(1)}, u32[]{:S(2)}, u32[]{:S(2)}) collective-permute-start(bf16[8,3584]{1,0:T(8,128)(2,1)S(1)} %broadcast_select_fusion.11), channel_id=1, source_target_pairs={{0,2},{1,5},{2,0},{3,7},{4,6},{5,1},{6,4},{7,3},{8,10},{9,13},{10,... | collective-permute-start | bytes 172040 | tf_op jit(solution)/shard_map/ppermute | solution.py:36
  45.0 4.4 %collective-permute-start.17 = (bf16[8,3584]{1,0:T(8,128)(2,1)S(1)}, bf16[8,3584]{1,0:T(8,128)(2,1)S(1)}, u32[]{:S(2)}, u32[]{:S(2)}) collective-permute-start(bf16[8,3584]{1,0:T(8,128)(2,1)S(1)} %broadcast_select_fusion.10), channel_id=1, source_target_pairs={{0,2},{1,5},{2,0},{3,7},{4,6},{5,1},{6,4},{7,3},{8,10},{9,13},{10,... | collective-permute-start | bytes 172040 | tf_op jit(solution)/shard_map/ppermute | solution.py:36
  48.1 5.1 %collective-permute-start.15 = (bf16[4,3584]{1,0:T(4,128)(2,1)S(1)}, bf16[4,3584]{1,0:T(4,128)(2,1)S(1)}, u32[]{:S(2)}, u32[]{:S(2)}) collective-permute-start(bf16[4,3584]{1,0:T(4,128)(2,1)S(1)} %slice.98), channel_id=1, source_target_pairs={{0,8},{1,9},{2,10},{3,11},{4,12},{5,13},{6,14},{7,15},{8,0},{9,1},... | collective-permute-start | bytes 86024 | tf_op jit(solution)/shard_map/ppermute | solution.py:36
  49.4 4.8 %collective-permute-start.18 = (bf16[4,3584]{1,0:T(4,128)(2,1)S(1)}, bf16[4,3584]{1,0:T(4,128)(2,1)S(1)}, u32[]{:S(2)}, u32[]{:S(2)}) collective-permute-start(bf16[4,3584]{1,0:T(4,128)(2,1)S(1)} %slice.102), channel_id=1, source_target_pairs={{0,8},{1,9},{2,10},{3,11},{4,12},{5,13},{6,14},{7,15},{8,0},{9,1},... | collective-permute-start | bytes 86024 | tf_op jit(solution)/shard_map/ppermute | solution.py:36

commit v18 on v16

--- a/solution.py
+++ b/solution.py
@@ -46,6 +46,10 @@
 
 def ordered(flip, first, second):
     return jnp.where(flip, second, first), jnp.where(flip, first, second)
+
+
+def add(kept, received):
+    return (kept.astype(jnp.float32) + received.astype(jnp.float32)).astype(jnp.bfloat16)
 
 
 def pack_kernel(tokens, routes, numerators, packed, routes_in, numerators_in, sems):
@@ -82,25 +86,30 @@
     )(in_hbm(tokens), in_hbm(routes), in_hbm(numerators))
 
 
-def gate_up_kernel(x, base, out):
-    depth, _, columns = base.shape
-    step = 512
+def gate_up_kernel(x, base, out, weights, sems):
+    depth, _, columns = weights.shape
+    step = depth // sems.shape[0]
+    copies = [
+        pltpu.make_async_copy(base.at[pl.ds(k, step)], weights.at[pl.ds(k, step)], sems.at[k // step])
+        for k in range(0, depth, step)
+    ]
+    for copy in copies:
+        copy.start()
     row = lax.broadcasted_iota(jnp.int32, (128, 256), 0)
     column = lax.broadcasted_iota(jnp.int32, (128, 256), 1)
     spread = jnp.where(column // 2 == row, 1.0, 0.0).astype(jnp.bfloat16)
     is_odd = (lax.broadcasted_iota(jnp.int32, (1, 2 * step), 1) % 2).astype(jnp.float32)
     odd_mask, even_mask = is_odd.astype(jnp.bfloat16), (1.0 - is_odd).astype(jnp.bfloat16)
     count = x.shape[0]
-    flat = base.reshape(2 * depth, columns)
+    flat = weights.reshape(2 * depth, columns)
     total = jnp.zeros(out.shape, jnp.float32)
     for k in range(0, depth, step):
         stacked = jnp.concatenate([x[:, i : i + 128] for i in range(k, k + step, 128)])
         wide = jnp.dot(stacked, spread, preferred_element_type=jnp.float32).astype(jnp.bfloat16)
         wide = jnp.concatenate([wide[i : i + count] for i in range(0, stacked.shape[0], count)], axis=1)
+        copies[k // step].wait()
         total += jnp.dot(
-            jnp.concatenate([wide * even_mask, wide * odd_mask]),
-            flat[2 * k : 2 * (k + step), :],
-            preferred_element_type=jnp.float32,
+            jnp.concatenate([wide * even_mask, wide * odd_mask]), flat[2 * k : 2 * (k + step), :], preferred_element_type=jnp.float32
         )
     out[...] = total
 
@@ -110,13 +119,14 @@
     return pl.pallas_call(
         gate_up_kernel,
         out_shape=jax.ShapeDtypeStruct((2 * x.shape[0], columns), jnp.float32),
-        in_specs=[VMEM, VMEM],
+        in_specs=[VMEM, HBM],
         out_specs=VMEM,
-        compiler_params=pltpu.CompilerParams(vmem_limit_bytes=16 << 20),
+        scratch_shapes=[pltpu.VMEM(base.shape, base.dtype), pltpu.SemaphoreType.DMA((depth // 512,))],
+        compiler_params=pltpu.CompilerParams(vmem_limit_bytes=32 << 20),
         cost_estimate=pl.CostEstimate(
             flops=4 * x.shape[0] * depth * columns, bytes_accessed=2 * base.size, transcendentals=0
         ),
-    )(x, base)
+    )(x, in_hbm(base))
 
 
 def part_kernel(bit, term, received, *refs):
@@ -227,18 +237,19 @@
     partial_codes = jnp.einsum(
         "srf,sfk->srk", hidden.astype(jnp.bfloat16), delta_down[0], preferred_element_type=jnp.float32
     ).astype(jnp.bfloat16)
-    lowrank = lax.dynamic_index_in_dim(partial_codes, me, 0, keepdims=False).astype(jnp.float32)
-    for m in range(1, members):
-        sent = lax.dynamic_index_in_dim(partial_codes, me ^ m, 0, keepdims=False)
-        lowrank = lowrank + trade(sent, (0, m), (0, m)).astype(jnp.float32)
+    by_core = partial_codes.reshape(chips, 2, *partial_codes.shape[1:])
+    kept, sent = (lax.dynamic_index_in_dim(by_core, c, 1, keepdims=False) for c in (core, 1 - core))
+    by_chip = add(kept, trade(sent, (0, 1), (0, 1)))
+    chip = me // 2
+    lowrank = lax.dynamic_index_in_dim(by_chip, chip, 0, keepdims=False).astype(jnp.float32)
+    for m in range(1, chips):
+        sent = lax.dynamic_index_in_dim(by_chip, chip ^ m, 0, keepdims=False)
+        lowrank = lowrank + trade(sent, (0, 2 * m), (0, 2 * m)).astype(jnp.float32)
     own_scale = lax.dynamic_index_in_dim(scale, me, 0, keepdims=False)
     scaled = (own_scale[:, None] * lowrank).astype(jnp.bfloat16)
 
     term = jnp.dot(hidden_sum, base_down[0], preferred_element_type=jnp.float32)
     term = (term + jnp.dot(scaled, delta_back[0], preferred_element_type=jnp.float32)).astype(jnp.bfloat16)
-
-    def add(kept, received):
-        return (kept.astype(jnp.float32) + received.astype(jnp.float32)).astype(jnp.bfloat16)
 
     half = term.shape[0] // 2
     sent = ordered(core == 1, term[half:], term[:half])[0]

time: 55.1 us -> 54.2 us (0.984)
  local copies, waits for them, and re-layouts: 3.97 us -> 0.9 us
  Pallas kernels: 4.12 us -> 6.26 us
  waiting for transfers between devices: 22.6 us -> 21.6 us
  starting transfers between devices: 20 us -> 20.9 us
    unnamed x14 -> x12, local copies, waits for them, and re-layouts: 3.43 us -> 0.35 us
    pallas_call x1, Pallas kernels: 2.96 us -> 5.1 us  [gate_up_product(): pl.pallas_call(gate_up_kernel, out_shape=jax.ShapeDtypeStruct((2 * x.shap...]
    ppermute x19 -> x18, waiting for transfers between devices: 22.6 us -> 21.6 us  [trade(): return lax.ppermute(value, ('expert', 'tensor'), pairs)]
    ppermute x19 -> x18, starting transfers between devices: 20 us -> 20.9 us  [trade(): return lax.ppermute(value, ('expert', 'tensor'), pairs)]
  transfers between devices with their start and end apart: 19 -> 18, of which waited for: 12 -> 12; matrix products, arithmetic and copies ran while one was open for 3% -> 3% of each run, Pallas kernels for 5% -> 9%
where the time goes in v18:
time: 54.2 us; the launch traced here: 54 us
  waiting for transfers between devices  21.6 us (40%)
  starting transfers between devices  20.9 us (39%)
  Pallas kernels  6.26 us (12%)
  matrix products  2.07 us (4%)
  other arithmetic  1.91 us (4%)
  local copies, waits for them, and re-layouts  0.9 us (2%)
    ppermute x18, waiting for transfers between devices, trade(): return lax.ppermute(value, ('expert', 'tensor'), pairs)  21.6 us
    ppermute x18, starting transfers between devices, trade(): return lax.ppermute(value, ('expert', 'tensor'), pairs)  20.9 us
    pallas_call x1, Pallas kernels, gate_up_product(): pl.pallas_call(gate_up_kernel, out_shape=jax.ShapeDtypeStruct((2 * x.shap...  5.1 us
  transfers between devices with their start and end apart: 18, of which 12 were waited for; matrix products, arithmetic and copies ran while one was open for 3% of the time, Pallas kernels for 9%

profile of v18, /device:TPU:0, one launch (start us, length us, event | category | flops | bytes accessed | tf_op | source)
XLA Modules:
  0.0 54.0 jit_solution(9239116334560801982)
XLA Ops:
  0.0 1.0 %shard_map.100 = bf16[4,7296]{1,0:T(4,128)(2,1)S(1)} custom-call(bf16[4,7168]{1,0:T(4,128)(2,1)} %bitcast.70, s32[4,8]{1,0:T(4,128)} %bitcast.71, s32[4,8]{1,0:T(4,128)} %bitcast.72), custom_call_target="tpu_custom_call" | custom-call | flops 20000000000 | bytes 114688 | tf_op jit(solution)/shard_map/pallas_call | solution.py:74
  1.0 5.1 %collective-permute-start.3 = (bf16[4,7296]{1,0:T(4,128)(2,1)S(1)}, bf16[4,7296]{1,0:T(4,128)(2,1)S(1)}, u32[]{:S(2)}, u32[]{:S(2)}) collective-permute-start(bf16[4,7296]{1,0:T(4,128)(2,1)S(1)} %shard_map.100), channel_id=1, source_target_pairs={{0,12},{1,13},{2,14},{3,15},{4,8},{5,9},{6,10},{7,11},{8,4},{9,5},... | collective-permute-start | bytes 175112 | tf_op jit(solution)/shard_map/ppermute | solution.py:36
  6.1 0.6 %collective-permute-start.1 = (bf16[4,7296]{1,0:T(4,128)(2,1)S(1)}, bf16[4,7296]{1,0:T(4,128)(2,1)S(1)}, u32[]{:S(2)}, u32[]{:S(2)}) collective-permute-start(bf16[4,7296]{1,0:T(4,128)(2,1)S(1)} %shard_map.100), channel_id=1, source_target_pairs={{0,4},{1,5},{2,6},{3,7},{4,0},{5,1},{6,2},{7,3},{8,12},{9,13},{10,... | collective-permute-start | bytes 175112 | tf_op jit(solution)/shard_map/ppermute | solution.py:36
  6.7 1.6 %collective-permute-start = (bf16[4,7296]{1,0:T(4,128)(2,1)S(1)}, bf16[4,7296]{1,0:T(4,128)(2,1)S(1)}, u32[]{:S(2)}, u32[]{:S(2)}) collective-permute-start(bf16[4,7296]{1,0:T(4,128)(2,1)S(1)} %shard_map.100), channel_id=1, source_target_pairs={{0,2},{1,3},{2,0},{3,1},{4,6},{5,7},{6,4},{7,5},{8,10},{9,11},{10,... | collective-permute-start | bytes 175112 | tf_op jit(solution)/shard_map/ppermute | solution.py:36
  8.4 0.1 collective-permute-done.3
  8.5 2.7 %collective-permute-done.2 = bf16[4,7296]{1,0:T(4,128)(2,1)S(1)} collective-permute-done((bf16[4,7296]{1,0:T(4,128)(2,1)S(1)}, bf16[4,7296]{1,0:T(4,128)(2,1)S(1)}, u32[]{:S(2)}, u32[]{:S(2)}) %collective-permute-start.2) | collective-permute-done | bytes 58400 | tf_op jit(solution)/shard_map/ppermute | solution.py:36
  11.2 0.1 pad_maximum_fusion.1
  11.3 1.6 %collective-permute-start.4 = (bf16[12,7296]{1,0:T(8,128)(2,1)S(1)}, bf16[12,7296]{1,0:T(8,128)(2,1)S(1)}, u32[]{:S(2)}, u32[]{:S(2)}) collective-permute-start(bf16[12,7296]{1,0:T(8,128)(2,1)S(1)} %pad_maximum_fusion.1), channel_id=1, source_target_pairs={{0,2},{1,3},{2,0},{3,1},{4,6},{5,7},{6,4},{7,5},{8,10},{9,11},{10,... | collective-permute-start | bytes 525320 | tf_op jit(solution)/shard_map/ppermute | solution.py:36
  13.0 5.1 %collective-permute-done.4 = bf16[12,7296]{1,0:T(8,128)(2,1)S(1)} collective-permute-done((bf16[12,7296]{1,0:T(8,128)(2,1)S(1)}, bf16[12,7296]{1,0:T(8,128)(2,1)S(1)}, u32[]{:S(2)}, u32[]{:S(2)}) %collective-permute-start.4) | collective-permute-done | bytes 175136 | tf_op jit(solution)/shard_map/ppermute | solution.py:36
  18.2 0.2 broadcast_select_fusion.2
  18.3 0.3 concatenate.13
  18.7 0.1 collective-permute-start.5
  18.8 1.7 %collective-permute-done.5 = bf16[32,7296]{1,0:T(8,128)(2,1)S(1)} collective-permute-done((bf16[32,7296]{1,0:T(8,128)(2,1)S(1)}, bf16[32,7296]{1,0:T(8,128)(2,1)S(1)}, u32[]{:S(2)}, u32[]{:S(2)}) %collective-permute-start.5) | collective-permute-done | bytes 466976 | tf_op jit(solution)/shard_map/ppermute | solution.py:36
  20.6 0.1 broadcast_select_fusion.1
  20.6 0.1 pad_maximum_fusion.x
  20.7 0.2 convert_reduce_fusion
  20.9 0.5 convolution_convert_fusion.1
  21.4 1.4 %collective-permute-start.8 = (bf16[64,128]{1,0:T(8,128)(2,1)S(1)}, bf16[64,128]{1,0:T(8,128)(2,1)S(1)}, u32[]{:S(2)}, u32[]{:S(2)}) collective-permute-start(bf16[64,128]{1,0:T(8,128)(2,1)S(1)} %convolution_convert_fusion.1), channel_id=1, source_target_pairs={{0,3},{1,2},{2,1},{3,0},{4,7},{5,6},{6,5},{7,4},{8,11},{9,10},{10,... | collective-permute-start | bytes 49160 | tf_op jit(solution)/shard_map/ppermute | solution.py:36
  22.8 0.5 collective-permute-start.7
  23.2 0.1 collective-permute-start.6
  23.3 0.1 fusion.24
  23.5 5.1 %shard_map.101 = f32[128,256]{1,0:T(8,128)S(1)} custom-call(bf16[64,7296]{1,0:T(8,128)(2,1)S(1)} %pad_maximum_fusion.x, bf16[7168,2,256]{2,1,0:T(2,128)(2,1)} %bitcast.62), custom_call_target="tpu_custom_call" | custom-call | flops 469762048 | bytes 7340032 | tf_op jit(solution)/shard_map/pallas_call | solution.py:119
  28.7 0.1 select_reduce_fusion
  28.8 0.1 select_reduce_fusion.1
  28.9 0.2 fusion.5
  29.1 0.1 multiply_reduce_fusion
  29.3 0.3 copy-done.4
  29.6 0.2 convolution_convert_fusion
  29.8 0.5 collective-permute-start.9
  30.3 0.9 %collective-permute-done.9 = bf16[2,64,128]{2,1,0:T(8,128)(2,1)S(1)} collective-permute-done((bf16[2,64,128]{2,1,0:T(8,128)(2,1)S(1)}, bf16[2,64,128]{2,1,0:T(8,128)(2,1)S(1)}, u32[]{:S(2)}, u32[]{:S(2)}) %collective-permute-start.9) | collective-permute-done | bytes 32800 | tf_op jit(solution)/shard_map/ppermute | solution.py:36
  31.2 1.6 %collective-permute-start.10 = (bf16[64,128]{1,0:T(8,128)(2,1)S(1)}, bf16[64,128]{1,0:T(8,128)(2,1)S(1)}, u32[]{:S(2)}, u32[]{:S(2)}) collective-permute-start(bf16[64,128]{1,0:T(8,128)(2,1)S(1)} %dynamic-slice_bitcast_fusion.1), channel_id=1, source_target_pairs={{0,2},{1,3},{2,0},{3,1},{4,6},{5,7},{6,4},{7,5},{8,10},{9,11},{10,... | collective-permute-start | bytes 49160 | tf_op jit(solution)/shard_map/ppermute | solution.py:36
  32.8 0.8 %fusion.1 = f32[64,7168]{1,0:T(8,128)S(1)} fusion(bf16[1,256,7168]{2,1,0:T(8,128)(2,1)S(1)} %copy-done.1, bf16[64,256]{1,0:T(8,128)(2,1)S(1)} %get-tuple-element.17), kind=kOutput, calls=%fused_computation.2 | convolution fusion | flops 234881024 | bytes 5537792 | tf_op jit(solution)/shard_map/dot_general | solution.py:251
  33.6 1.4 %collective-permute-done.10 = bf16[64,128]{1,0:T(8,128)(2,1)S(1)} collective-permute-done((bf16[64,128]{1,0:T(8,128)(2,1)S(1)}, bf16[64,128]{1,0:T(8,128)(2,1)S(1)}, u32[]{:S(2)}, u32[]{:S(2)}) %collective-permute-start.10) | collective-permute-done | bytes 16416 | tf_op jit(solution)/shard_map/ppermute | solution.py:36
  35.0 0.5 fusion.term
  35.6 1.8 %collective-permute-done.11.received = bf16[32,7168]{1,0:T(8,128)(2,1)S(1)} collective-permute-done((bf16[32,7168]{1,0:T(8,128)(2,1)S(1)}, bf16[32,7168]{1,0:T(8,128)(2,1)S(1)}, u32[]{:S(2)}, u32[]{:S(2)}) %collective-permute-start.11) | collective-permute-done | bytes 458784 | tf_op jit(solution)/shard_map/ppermute | solution.py:36
  37.4 0.2 shard_map.102
  37.6 0.7 %collective-permute-start.12 = (bf16[16,3584]{1,0:T(8,128)(2,1)S(1)}, bf16[16,3584]{1,0:T(8,128)(2,1)S(1)}, u32[]{:S(2)}, u32[]{:S(2)}) collective-permute-start(bf16[16,3584]{1,0:T(8,128)(2,1)S(1)} %get-tuple-element.14), channel_id=1, source_target_pairs={{0,4},{1,3},{2,6},{3,1},{4,0},{5,7},{6,2},{7,5},{8,12},{9,11},{10,... | collective-permute-start | bytes 344072 | tf_op jit(solution)/shard_map/ppermute | solution.py:36
  38.3 1.4 %collective-permute-start.15 = (bf16[16,3584]{1,0:T(8,128)(2,1)S(1)}, bf16[16,3584]{1,0:T(8,128)(2,1)S(1)}, u32[]{:S(2)}, u32[]{:S(2)}) collective-permute-start(bf16[16,3584]{1,0:T(8,128)(2,1)S(1)} %get-tuple-element.16), channel_id=1, source_target_pairs={{0,4},{1,3},{2,6},{3,1},{4,0},{5,7},{6,2},{7,5},{8,12},{9,11},{10,... | collective-permute-start | bytes 344072 | tf_op jit(solution)/shard_map/ppermute | solution.py:36
  39.7 2.8 %collective-permute-done.12 = bf16[16,3584]{1,0:T(8,128)(2,1)S(1)} collective-permute-done((bf16[16,3584]{1,0:T(8,128)(2,1)S(1)}, bf16[16,3584]{1,0:T(8,128)(2,1)S(1)}, u32[]{:S(2)}, u32[]{:S(2)}) %collective-permute-start.12) | collective-permute-done | bytes 114720 | tf_op jit(solution)/shard_map/ppermute | solution.py:36
  42.5 1.6 %collective-permute-start.13 = (bf16[8,3584]{1,0:T(8,128)(2,1)S(1)}, bf16[8,3584]{1,0:T(8,128)(2,1)S(1)}, u32[]{:S(2)}, u32[]{:S(2)}) collective-permute-start(bf16[8,3584]{1,0:T(8,128)(2,1)S(1)} %broadcast_select_fusion.11), channel_id=1, source_target_pairs={{0,2},{1,5},{2,0},{3,7},{4,6},{5,1},{6,4},{7,3},{8,10},{9,13},{10,... | collective-permute-start | bytes 172040 | tf_op jit(solution)/shard_map/ppermute | solution.py:36
  44.2 1.2 %collective-permute-start.16 = (bf16[8,3584]{1,0:T(8,128)(2,1)S(1)}, bf16[8,3584]{1,0:T(8,128)(2,1)S(1)}, u32[]{:S(2)}, u32[]{:S(2)}) collective-permute-start(bf16[8,3584]{1,0:T(8,128)(2,1)S(1)} %broadcast_select_fusion.10), channel_id=1, source_target_pairs={{0,2},{1,5},{2,0},{3,7},{4,6},{5,1},{6,4},{7,3},{8,10},{9,13},{10,... | collective-permute-start | bytes 172040 | tf_op jit(solution)/shard_map/ppermute | solution.py:36
  45.4 1.4 %collective-permute-done.13 = bf16[8,3584]{1,0:T(8,128)(2,1)S(1)} collective-permute-done((bf16[8,3584]{1,0:T(8,128)(2,1)S(1)}, bf16[8,3584]{1,0:T(8,128)(2,1)S(1)}, u32[]{:S(2)}, u32[]{:S(2)}) %collective-permute-start.13) | collective-permute-done | bytes 57376 | tf_op jit(solution)/shard_map/ppermute | solution.py:36
  46.8 1.4 %collective-permute-start.14 = (bf16[4,3584]{1,0:T(4,128)(2,1)S(1)}, bf16[4,3584]{1,0:T(4,128)(2,1)S(1)}, u32[]{:S(2)}, u32[]{:S(2)}) collective-permute-start(bf16[4,3584]{1,0:T(4,128)(2,1)S(1)} %slice.98), channel_id=1, source_target_pairs={{0,8},{1,9},{2,10},{3,11},{4,12},{5,13},{6,14},{7,15},{8,0},{9,1},... | collective-permute-start | bytes 86024 | tf_op jit(solution)/shard_map/ppermute | solution.py:36
  48.2 0.3 collective-permute-done.16
  48.5 1.4 %collective-permute-start.17 = (bf16[4,3584]{1,0:T(4,128)(2,1)S(1)}, bf16[4,3584]{1,0:T(4,128)(2,1)S(1)}, u32[]{:S(2)}, u32[]{:S(2)}) collective-permute-start(bf16[4,3584]{1,0:T(4,128)(2,1)S(1)} %slice.102), channel_id=1, source_target_pairs={{0,8},{1,9},{2,10},{3,11},{4,12},{5,13},{6,14},{7,15},{8,0},{9,1},... | collective-permute-start | bytes 86024 | tf_op jit(solution)/shard_map/ppermute | solution.py:36
  49.9 2.0 %collective-permute-done.14 = bf16[4,3584]{1,0:T(4,128)(2,1)S(1)} collective-permute-done((bf16[4,3584]{1,0:T(4,128)(2,1)S(1)}, bf16[4,3584]{1,0:T(4,128)(2,1)S(1)}, u32[]{:S(2)}, u32[]{:S(2)}) %collective-permute-start.14) | collective-permute-done | bytes 28704 | tf_op jit(solution)/shard_map/ppermute | solution.py:36
  52.0 1.4 %collective-permute-done.17 = bf16[4,3584]{1,0:T(4,128)(2,1)S(1)} collective-permute-done((bf16[4,3584]{1,0:T(4,128)(2,1)S(1)}, bf16[4,3584]{1,0:T(4,128)(2,1)S(1)}, u32[]{:S(2)}, u32[]{:S(2)}) %collective-permute-start.17) | collective-permute-done | bytes 28704 | tf_op jit(solution)/shard_map/ppermute | solution.py:36
  53.3 0.7 %maximum_bitcast_fusion.2 = bf16[1,4,7168]{2,1,0:T(4,128)(2,1)} fusion(bf16[4,3584]{1,0:T(4,128)(2,1)S(1)} %add_convert_fusion.4, bf16[4,3584]{1,0:T(4,128)(2,1)S(1)} %add_convert_fusion.5), kind=kLoop, calls=%fused_computation.47 | loop fusion | flops 114688 | bytes 114688 | tf_op jit(solution)/shard_map/broadcast_in_dim | solution.py:277
  (42 shorter events, 0.6 us)
Async XLA Ops:
  0.0 20.7 %copy-start = (bf16[1,7168,128]{2,1,0:T(8,128)(2,1)S(1)}, bf16[1,7168,128]{2,1,0:T(8,128)(2,1)}, u32[]{:S(2)}) copy-start(bf16[1,7168,128]{2,1,0:T(8,128)(2,1)} %param.16) | copy-start | bytes 5505028
  1.0 7.5 %collective-permute-start.3 = (bf16[4,7296]{1,0:T(4,128)(2,1)S(1)}, bf16[4,7296]{1,0:T(4,128)(2,1)S(1)}, u32[]{:S(2)}, u32[]{:S(2)}) collective-permute-start(bf16[4,7296]{1,0:T(4,128)(2,1)S(1)} %shard_map.100), channel_id=1, source_target_pairs={{0,12},{1,13},{2,14},{3,15},{4,8},{5,9},{6,10},{7,11},{8,4},{9,5},... | collective-permute-start | bytes 175112 | tf_op jit(solution)/shard_map/ppermute | solution.py:36
  6.1 5.1 %collective-permute-start.2 = (bf16[4,7296]{1,0:T(4,128)(2,1)S(1)}, bf16[4,7296]{1,0:T(4,128)(2,1)S(1)}, u32[]{:S(2)}, u32[]{:S(2)}) collective-permute-start(bf16[4,7296]{1,0:T(4,128)(2,1)S(1)} %shard_map.100), channel_id=1, source_target_pairs={{0,8},{1,9},{2,10},{3,11},{4,12},{5,13},{6,14},{7,15},{8,0},{9,1},... | collective-permute-start | bytes 175112 | tf_op jit(solution)/shard_map/ppermute | solution.py:36
  6.1 5.1 %collective-permute-start.1 = (bf16[4,7296]{1,0:T(4,128)(2,1)S(1)}, bf16[4,7296]{1,0:T(4,128)(2,1)S(1)}, u32[]{:S(2)}, u32[]{:S(2)}) collective-permute-start(bf16[4,7296]{1,0:T(4,128)(2,1)S(1)} %shard_map.100), channel_id=1, source_target_pairs={{0,4},{1,5},{2,6},{3,7},{4,0},{5,1},{6,2},{7,3},{8,12},{9,13},{10,... | collective-permute-start | bytes 175112 | tf_op jit(solution)/shard_map/ppermute | solution.py:36
  6.7 6.2 %collective-permute-start = (bf16[4,7296]{1,0:T(4,128)(2,1)S(1)}, bf16[4,7296]{1,0:T(4,128)(2,1)S(1)}, u32[]{:S(2)}, u32[]{:S(2)}) collective-permute-start(bf16[4,7296]{1,0:T(4,128)(2,1)S(1)} %shard_map.100), channel_id=1, source_target_pairs={{0,2},{1,3},{2,0},{3,1},{4,6},{5,7},{6,4},{7,5},{8,10},{9,11},{10,... | collective-permute-start | bytes 175112 | tf_op jit(solution)/shard_map/ppermute | solution.py:36
  11.3 6.8 %collective-permute-start.4 = (bf16[12,7296]{1,0:T(8,128)(2,1)S(1)}, bf16[12,7296]{1,0:T(8,128)(2,1)S(1)}, u32[]{:S(2)}, u32[]{:S(2)}) collective-permute-start(bf16[12,7296]{1,0:T(8,128)(2,1)S(1)} %pad_maximum_fusion.1), channel_id=1, source_target_pairs={{0,2},{1,3},{2,0},{3,1},{4,6},{5,7},{6,4},{7,5},{8,10},{9,11},{10,... | collective-permute-start | bytes 525320 | tf_op jit(solution)/shard_map/ppermute | solution.py:36
  18.7 1.9 %collective-permute-start.5 = (bf16[32,7296]{1,0:T(8,128)(2,1)S(1)}, bf16[32,7296]{1,0:T(8,128)(2,1)S(1)}, u32[]{:S(2)}, u32[]{:S(2)}) collective-permute-start(bf16[32,7296]{1,0:T(8,128)(2,1)S(1)} %concatenate.13), channel_id=1, source_target_pairs={{0,1},{1,0},{2,3},{3,2},{4,5},{5,4},{6,7},{7,6},{8,9},{9,8},{10,11... | collective-permute-start | bytes 1400840 | tf_op jit(solution)/shard_map/ppermute | solution.py:36
  21.4 7.5 %collective-permute-start.8 = (bf16[64,128]{1,0:T(8,128)(2,1)S(1)}, bf16[64,128]{1,0:T(8,128)(2,1)S(1)}, u32[]{:S(2)}, u32[]{:S(2)}) collective-permute-start(bf16[64,128]{1,0:T(8,128)(2,1)S(1)} %convolution_convert_fusion.1), channel_id=1, source_target_pairs={{0,3},{1,2},{2,1},{3,0},{4,7},{5,6},{6,5},{7,4},{8,11},{9,10},{10,... | collective-permute-start | bytes 49160 | tf_op jit(solution)/shard_map/ppermute | solution.py:36
  22.8 6.1 %collective-permute-start.7 = (bf16[64,128]{1,0:T(8,128)(2,1)S(1)}, bf16[64,128]{1,0:T(8,128)(2,1)S(1)}, u32[]{:S(2)}, u32[]{:S(2)}) collective-permute-start(bf16[64,128]{1,0:T(8,128)(2,1)S(1)} %convolution_convert_fusion.1), channel_id=1, source_target_pairs={{0,2},{1,3},{2,0},{3,1},{4,6},{5,7},{6,4},{7,5},{8,10},{9,11},{10,... | collective-permute-start | bytes 49160 | tf_op jit(solution)/shard_map/ppermute | solution.py:36
  23.2 5.6 %collective-permute-start.6 = (bf16[64,128]{1,0:T(8,128)(2,1)S(1)}, bf16[64,128]{1,0:T(8,128)(2,1)S(1)}, u32[]{:S(2)}, u32[]{:S(2)}) collective-permute-start(bf16[64,128]{1,0:T(8,128)(2,1)S(1)} %convolution_convert_fusion.1), channel_id=1, source_target_pairs={{0,1},{1,0},{2,3},{3,2},{4,5},{5,4},{6,7},{7,6},{8,9},{9,8},{10,11... | collective-permute-start | bytes 49160 | tf_op jit(solution)/shard_map/ppermute | solution.py:36
  23.5 5.1 %copy-start.5 = (s32[16]{0:T(128)S(1)}, s32[16]{0:T(128)}, u32[]{:S(2)}) copy-start(s32[16]{0:T(128)} %param.13) | copy-start | bytes 196
  23.5 5.4 %copy-start.3 = (bf16[1,4,128,2,256]{4,3,2,1,0:T(2,128)(2,1)S(1)}, bf16[1,4,128,2,256]{4,3,2,1,0:T(2,128)(2,1)}, u32[]{:S(2)}) copy-start(bf16[1,4,128,2,256]{4,3,2,1,0:T(2,128)(2,1)} %param.17) | copy-start | bytes 1572868
  23.5 9.3 %copy-start.1 = (bf16[1,256,7168]{2,1,0:T(8,128)(2,1)S(1)}, bf16[1,256,7168]{2,1,0:T(8,128)(2,1)}, u32[]{:S(2)}) copy-start(bf16[1,256,7168]{2,1,0:T(8,128)(2,1)} %param.15) | copy-start | bytes 11010052
  28.6 1.0 %copy-start.4 = (bf16[1,4,256,128]{3,2,1,0:T(8,128)(2,1)S(1)}, bf16[1,4,256,128]{3,2,1,0:T(8,128)(2,1)}, u32[]{:S(2)}) copy-start(bf16[1,4,256,128]{3,2,1,0:T(8,128)(2,1)} %param.18) | copy-start | bytes 786436
  29.8 1.4 %collective-permute-start.9 = (bf16[2,64,128]{2,1,0:T(8,128)(2,1)S(1)}, bf16[2,64,128]{2,1,0:T(8,128)(2,1)S(1)}, u32[]{:S(2)}, u32[]{:S(2)}) collective-permute-start(bf16[2,64,128]{2,1,0:T(8,128)(2,1)S(1)} %dynamic-slice_bitcast_fusion), channel_id=1, source_target_pairs={{0,1},{1,0},{2,3},{3,2},{4,5},{5,4},{6,7},{7,6},{8,9},{9,8},{10,11... | collective-permute-start | bytes 98312 | tf_op jit(solution)/shard_map/ppermute | solution.py:36
  31.2 3.8 %collective-permute-start.10 = (bf16[64,128]{1,0:T(8,128)(2,1)S(1)}, bf16[64,128]{1,0:T(8,128)(2,1)S(1)}, u32[]{:S(2)}, u32[]{:S(2)}) collective-permute-start(bf16[64,128]{1,0:T(8,128)(2,1)S(1)} %dynamic-slice_bitcast_fusion.1), channel_id=1, source_target_pairs={{0,2},{1,3},{2,0},{3,1},{4,6},{5,7},{6,4},{7,5},{8,10},{9,11},{10,... | collective-permute-start | bytes 49160 | tf_op jit(solution)/shard_map/ppermute | solution.py:36
  32.8 2.2 %copy-start.2 = (bf16[1,128,7168]{2,1,0:T(8,128)(2,1)S(1)}, bf16[1,128,7168]{2,1,0:T(8,128)(2,1)}, u32[]{:S(2)}) copy-start(bf16[1,128,7168]{2,1,0:T(8,128)(2,1)} %param.19) | copy-start | bytes 5505028
  35.5 1.9 %collective-permute-start.11 = (bf16[32,7168]{1,0:T(8,128)(2,1)S(1)}, bf16[32,7168]{1,0:T(8,128)(2,1)S(1)}, u32[]{:S(2)}, u32[]{:S(2)}) collective-permute-start(bf16[32,7168]{1,0:T(8,128)(2,1)S(1)} %slice_select_fusion), channel_id=1, source_target_pairs={{0,1},{1,0},{2,3},{3,2},{4,5},{5,4},{6,7},{7,6},{8,9},{9,8},{10,11... | collective-permute-start | bytes 1376264 | tf_op jit(solution)/shard_map/ppermute | solution.py:36
  37.6 4.9 %collective-permute-start.12 = (bf16[16,3584]{1,0:T(8,128)(2,1)S(1)}, bf16[16,3584]{1,0:T(8,128)(2,1)S(1)}, u32[]{:S(2)}, u32[]{:S(2)}) collective-permute-start(bf16[16,3584]{1,0:T(8,128)(2,1)S(1)} %get-tuple-element.14), channel_id=1, source_target_pairs={{0,4},{1,3},{2,6},{3,1},{4,0},{5,7},{6,2},{7,5},{8,12},{9,11},{10,... | collective-permute-start | bytes 344072 | tf_op jit(solution)/shard_map/ppermute | solution.py:36
  38.3 5.8 %collective-permute-start.15 = (bf16[16,3584]{1,0:T(8,128)(2,1)S(1)}, bf16[16,3584]{1,0:T(8,128)(2,1)S(1)}, u32[]{:S(2)}, u32[]{:S(2)}) collective-permute-start(bf16[16,3584]{1,0:T(8,128)(2,1)S(1)} %get-tuple-element.16), channel_id=1, source_target_pairs={{0,4},{1,3},{2,6},{3,1},{4,0},{5,7},{6,2},{7,5},{8,12},{9,11},{10,... | collective-permute-start | bytes 344072 | tf_op jit(solution)/shard_map/ppermute | solution.py:36
  42.5 4.2 %collective-permute-start.13 = (bf16[8,3584]{1,0:T(8,128)(2,1)S(1)}, bf16[8,3584]{1,0:T(8,128)(2,1)S(1)}, u32[]{:S(2)}, u32[]{:S(2)}) collective-permute-start(bf16[8,3584]{1,0:T(8,128)(2,1)S(1)} %broadcast_select_fusion.11), channel_id=1, source_target_pairs={{0,2},{1,5},{2,0},{3,7},{4,6},{5,1},{6,4},{7,3},{8,10},{9,13},{10,... | collective-permute-start | bytes 172040 | tf_op jit(solution)/shard_map/ppermute | solution.py:36
  44.2 4.2 %collective-permute-start.16 = (bf16[8,3584]{1,0:T(8,128)(2,1)S(1)}, bf16[8,3584]{1,0:T(8,128)(2,1)S(1)}, u32[]{:S(2)}, u32[]{:S(2)}) collective-permute-start(bf16[8,3584]{1,0:T(8,128)(2,1)S(1)} %broadcast_select_fusion.10), channel_id=1, source_target_pairs={{0,2},{1,5},{2,0},{3,7},{4,6},{5,1},{6,4},{7,3},{8,10},{9,13},{10,... | collective-permute-start | bytes 172040 | tf_op jit(solution)/shard_map/ppermute | solution.py:36
  46.8 5.1 %collective-permute-start.14 = (bf16[4,3584]{1,0:T(4,128)(2,1)S(1)}, bf16[4,3584]{1,0:T(4,128)(2,1)S(1)}, u32[]{:S(2)}, u32[]{:S(2)}) collective-permute-start(bf16[4,3584]{1,0:T(4,128)(2,1)S(1)} %slice.98), channel_id=1, source_target_pairs={{0,8},{1,9},{2,10},{3,11},{4,12},{5,13},{6,14},{7,15},{8,0},{9,1},... | collective-permute-start | bytes 86024 | tf_op jit(solution)/shard_map/ppermute | solution.py:36
  48.5 4.8 %collective-permute-start.17 = (bf16[4,3584]{1,0:T(4,128)(2,1)S(1)}, bf16[4,3584]{1,0:T(4,128)(2,1)S(1)}, u32[]{:S(2)}, u32[]{:S(2)}) collective-permute-start(bf16[4,3584]{1,0:T(4,128)(2,1)S(1)} %slice.102), channel_id=1, source_target_pairs={{0,8},{1,9},{2,10},{3,11},{4,12},{5,13},{6,14},{7,15},{8,0},{9,1},... | collective-permute-start | bytes 86024 | tf_op jit(solution)/shard_map/ppermute | solution.py:36

commit v19 on v18

--- a/solution.py
+++ b/solution.py
@@ -138,8 +138,9 @@
     total[...] = term[pl.ds(pl.multiple_of(core * half, half), half), :].astype(jnp.float32) + received[
         ...
     ].astype(jnp.float32)
-    sent = (2 - core * (1 + flag), 3 - core * flag)
-    kept = (core * flag, 1 + core * (1 + flag))
+    by_x = 1 - core
+    sent = (2 - by_x * (1 + flag), 3 - by_x * flag)
+    kept = (by_x * flag, 1 + by_x * (1 + flag))
     for i, out in enumerate(outs):
         columns = pl.ds((i // 2) * step, step)
         rows = [
@@ -248,7 +249,8 @@
     own_scale = lax.dynamic_index_in_dim(scale, me, 0, keepdims=False)
     scaled = (own_scale[:, None] * lowrank).astype(jnp.bfloat16)
 
-    term = jnp.dot(hidden_sum, base_down[0], preferred_element_type=jnp.float32)
+    hidden_sum, down_table = lax.optimization_barrier((hidden_sum, base_down[0]))
+    term = jnp.dot(hidden_sum, down_table, preferred_element_type=jnp.float32)
     term = (term + jnp.dot(scaled, delta_back[0], preferred_element_type=jnp.float32)).astype(jnp.bfloat16)
 
     half = term.shape[0] // 2
@@ -260,16 +262,16 @@
             if i:
                 size = total.shape[0] // 4
                 blocks = [total[j * size : (j + 1) * size] for j in range(4)]
-                inner = ordered(core == 1, blocks[1], blocks[2])
+                inner = ordered(core == 0, blocks[1], blocks[2])
                 kept, sent = ordered(
-                    (core == 1) & flag,
+                    (core == 0) & flag,
                     jnp.concatenate([blocks[0], inner[0]]),
                     jnp.concatenate([inner[1], blocks[3]]),
                 )
+            total = add(kept, trade(sent, (0, 2 * x), (z, 0)))
+            size = total.shape[0] // 2
+            kept, sent = ordered((core == 1) & flag, total[:size], total[size:])
             total = add(kept, trade(sent, (z, 0), (0, 2 * x)))
-            size = total.shape[0] // 2
-            kept, sent = ordered((core == 0) & flag, total[:size], total[size:])
-            total = add(kept, trade(sent, (0, 2 * x), (z, 0)))
         for mask in reversed(shared):
             size = total.shape[0] // 2
             total = add(total[:size], trade(total[size:], (mask, 0), (mask, 0)))

time: 54.2 us -> 54 us (level)
  starting transfers between devices: 20.9 us -> 19.7 us
  waiting for transfers between devices: 21.6 us -> 22.7 us
    ppermute x18, starting transfers between devices: 20.9 us -> 19.7 us  [trade(): return lax.ppermute(value, ('expert', 'tensor'), pairs)]
    ppermute x18, waiting for transfers between devices: 21.6 us -> 22.7 us  [trade(): return lax.ppermute(value, ('expert', 'tensor'), pairs)]
  transfers between devices with their start and end apart: 18 -> 18, of which waited for: 12 -> 13; matrix products, arithmetic and copies ran while one was open for 3% -> 3% of each run, Pallas kernels for 9% -> 9%
where the time goes in v19:
time: 54 us; the launch traced here: 53.9 us
  waiting for transfers between devices  22.7 us (42%)
  starting transfers between devices  19.7 us (36%)
  Pallas kernels  6.26 us (12%)
  matrix products  2.07 us (4%)
  other arithmetic  1.91 us (4%)
  local copies, waits for them, and re-layouts  0.9 us (2%)
    ppermute x18, waiting for transfers between devices, trade(): return lax.ppermute(value, ('expert', 'tensor'), pairs)  22.7 us
    ppermute x18, starting transfers between devices, trade(): return lax.ppermute(value, ('expert', 'tensor'), pairs)  19.7 us
    pallas_call x1, Pallas kernels, gate_up_product(): pl.pallas_call(gate_up_kernel, out_shape=jax.ShapeDtypeStruct((2 * x.shap...  5.1 us
  transfers between devices with their start and end apart: 18, of which 13 were waited for; matrix products, arithmetic and copies ran while one was open for 3% of the time, Pallas kernels for 9%

profile of v19, /device:TPU:0, one launch (start us, length us, event | category | flops | bytes accessed | tf_op | source)
XLA Modules:
  0.0 53.9 jit_solution(7777025001604532654)
XLA Ops:
  0.0 1.0 %shard_map.100 = bf16[4,7296]{1,0:T(4,128)(2,1)S(1)} custom-call(bf16[4,7168]{1,0:T(4,128)(2,1)} %bitcast.70, s32[4,8]{1,0:T(4,128)} %bitcast.71, s32[4,8]{1,0:T(4,128)} %bitcast.72), custom_call_target="tpu_custom_call" | custom-call | flops 20000000000 | bytes 114688 | tf_op jit(solution)/shard_map/pallas_call | solution.py:74
  1.0 5.1 %collective-permute-start.3 = (bf16[4,7296]{1,0:T(4,128)(2,1)S(1)}, bf16[4,7296]{1,0:T(4,128)(2,1)S(1)}, u32[]{:S(2)}, u32[]{:S(2)}) collective-permute-start(bf16[4,7296]{1,0:T(4,128)(2,1)S(1)} %shard_map.100), channel_id=1, source_target_pairs={{0,12},{1,13},{2,14},{3,15},{4,8},{5,9},{6,10},{7,11},{8,4},{9,5},... | collective-permute-start | bytes 175112 | tf_op jit(solution)/shard_map/ppermute | solution.py:36
  6.1 0.6 %collective-permute-start.1 = (bf16[4,7296]{1,0:T(4,128)(2,1)S(1)}, bf16[4,7296]{1,0:T(4,128)(2,1)S(1)}, u32[]{:S(2)}, u32[]{:S(2)}) collective-permute-start(bf16[4,7296]{1,0:T(4,128)(2,1)S(1)} %shard_map.100), channel_id=1, source_target_pairs={{0,4},{1,5},{2,6},{3,7},{4,0},{5,1},{6,2},{7,3},{8,12},{9,13},{10,... | collective-permute-start | bytes 175112 | tf_op jit(solution)/shard_map/ppermute | solution.py:36
  6.7 1.6 %collective-permute-start = (bf16[4,7296]{1,0:T(4,128)(2,1)S(1)}, bf16[4,7296]{1,0:T(4,128)(2,1)S(1)}, u32[]{:S(2)}, u32[]{:S(2)}) collective-permute-start(bf16[4,7296]{1,0:T(4,128)(2,1)S(1)} %shard_map.100), channel_id=1, source_target_pairs={{0,2},{1,3},{2,0},{3,1},{4,6},{5,7},{6,4},{7,5},{8,10},{9,11},{10,... | collective-permute-start | bytes 175112 | tf_op jit(solution)/shard_map/ppermute | solution.py:36
  8.4 0.1 collective-permute-done.3
  8.5 2.7 %collective-permute-done.2 = bf16[4,7296]{1,0:T(4,128)(2,1)S(1)} collective-permute-done((bf16[4,7296]{1,0:T(4,128)(2,1)S(1)}, bf16[4,7296]{1,0:T(4,128)(2,1)S(1)}, u32[]{:S(2)}, u32[]{:S(2)}) %collective-permute-start.2) | collective-permute-done | bytes 58400 | tf_op jit(solution)/shard_map/ppermute | solution.py:36
  11.2 0.1 pad_maximum_fusion.1
  11.3 1.6 %collective-permute-start.4 = (bf16[12,7296]{1,0:T(8,128)(2,1)S(1)}, bf16[12,7296]{1,0:T(8,128)(2,1)S(1)}, u32[]{:S(2)}, u32[]{:S(2)}) collective-permute-start(bf16[12,7296]{1,0:T(8,128)(2,1)S(1)} %pad_maximum_fusion.1), channel_id=1, source_target_pairs={{0,2},{1,3},{2,0},{3,1},{4,6},{5,7},{6,4},{7,5},{8,10},{9,11},{10,... | collective-permute-start | bytes 525320 | tf_op jit(solution)/shard_map/ppermute | solution.py:36
  13.0 5.1 %collective-permute-done.4 = bf16[12,7296]{1,0:T(8,128)(2,1)S(1)} collective-permute-done((bf16[12,7296]{1,0:T(8,128)(2,1)S(1)}, bf16[12,7296]{1,0:T(8,128)(2,1)S(1)}, u32[]{:S(2)}, u32[]{:S(2)}) %collective-permute-start.4) | collective-permute-done | bytes 175136 | tf_op jit(solution)/shard_map/ppermute | solution.py:36
  18.2 0.2 broadcast_select_fusion.2
  18.3 0.3 concatenate.13
  18.7 0.1 collective-permute-start.5
  18.8 1.7 %collective-permute-done.5 = bf16[32,7296]{1,0:T(8,128)(2,1)S(1)} collective-permute-done((bf16[32,7296]{1,0:T(8,128)(2,1)S(1)}, bf16[32,7296]{1,0:T(8,128)(2,1)S(1)}, u32[]{:S(2)}, u32[]{:S(2)}) %collective-permute-start.5) | collective-permute-done | bytes 466976 | tf_op jit(solution)/shard_map/ppermute | solution.py:36
  20.6 0.1 broadcast_select_fusion.1
  20.7 0.2 convert_reduce_fusion
  20.9 0.5 convolution_convert_fusion.1
  21.4 1.4 %collective-permute-start.8 = (bf16[64,128]{1,0:T(8,128)(2,1)S(1)}, bf16[64,128]{1,0:T(8,128)(2,1)S(1)}, u32[]{:S(2)}, u32[]{:S(2)}) collective-permute-start(bf16[64,128]{1,0:T(8,128)(2,1)S(1)} %convolution_convert_fusion.1), channel_id=1, source_target_pairs={{0,3},{1,2},{2,1},{3,0},{4,7},{5,6},{6,5},{7,4},{8,11},{9,10},{10,... | collective-permute-start | bytes 49160 | tf_op jit(solution)/shard_map/ppermute | solution.py:36
  22.8 0.5 collective-permute-start.7
  23.2 0.1 collective-permute-start.6
  23.3 0.1 fusion.21
  23.5 5.1 %shard_map.101 = f32[128,256]{1,0:T(8,128)S(1)} custom-call(bf16[64,7296]{1,0:T(8,128)(2,1)S(1)} %pad_maximum_fusion.x, bf16[7168,2,256]{2,1,0:T(2,128)(2,1)} %bitcast.61), custom_call_target="tpu_custom_call" | custom-call | flops 469762048 | bytes 7340032 | tf_op jit(solution)/shard_map/pallas_call | solution.py:119
  28.7 0.1 select_reduce_fusion
  28.8 0.1 select_reduce_fusion.1
  28.9 0.2 fusion.3
  29.1 0.1 multiply_reduce_fusion
  29.3 0.3 copy-done.4
  29.6 0.2 convolution_convert_fusion
  29.8 0.5 collective-permute-start.9
  30.3 0.9 %collective-permute-done.9 = bf16[2,64,128]{2,1,0:T(8,128)(2,1)S(1)} collective-permute-done((bf16[2,64,128]{2,1,0:T(8,128)(2,1)S(1)}, bf16[2,64,128]{2,1,0:T(8,128)(2,1)S(1)}, u32[]{:S(2)}, u32[]{:S(2)}) %collective-permute-start.9) | collective-permute-done | bytes 32800 | tf_op jit(solution)/shard_map/ppermute | solution.py:36
  31.2 1.6 %collective-permute-start.10 = (bf16[64,128]{1,0:T(8,128)(2,1)S(1)}, bf16[64,128]{1,0:T(8,128)(2,1)S(1)}, u32[]{:S(2)}, u32[]{:S(2)}) collective-permute-start(bf16[64,128]{1,0:T(8,128)(2,1)S(1)} %dynamic-slice_bitcast_fusion.1), channel_id=1, source_target_pairs={{0,2},{1,3},{2,0},{3,1},{4,6},{5,7},{6,4},{7,5},{8,10},{9,11},{10,... | collective-permute-start | bytes 49160 | tf_op jit(solution)/shard_map/ppermute | solution.py:36
  32.8 0.8 %fusion.31 = f32[64,7168]{1,0:T(8,128)S(1)} fusion(bf16[64,256]{1,0:T(8,128)(2,1)S(1)} %get-tuple-element.15, bf16[256,7168]{1,0:T(8,128)(2,1)S(1)} %bitcast.62), kind=kOutput, calls=%fused_computation.75 | convolution fusion | flops 234881024 | bytes 5537792 | tf_op jit(solution)/shard_map/dot_general | solution.py:253
  33.6 1.4 %collective-permute-done.10 = bf16[64,128]{1,0:T(8,128)(2,1)S(1)} collective-permute-done((bf16[64,128]{1,0:T(8,128)(2,1)S(1)}, bf16[64,128]{1,0:T(8,128)(2,1)S(1)}, u32[]{:S(2)}, u32[]{:S(2)}) %collective-permute-start.10) | collective-permute-done | bytes 16416 | tf_op jit(solution)/shard_map/ppermute | solution.py:36
  35.0 0.5 fusion.term
  35.6 1.8 %collective-permute-done.11.received = bf16[32,7168]{1,0:T(8,128)(2,1)S(1)} collective-permute-done((bf16[32,7168]{1,0:T(8,128)(2,1)S(1)}, bf16[32,7168]{1,0:T(8,128)(2,1)S(1)}, u32[]{:S(2)}, u32[]{:S(2)}) %collective-permute-start.11) | collective-permute-done | bytes 458784 | tf_op jit(solution)/shard_map/ppermute | solution.py:36
  37.4 0.2 shard_map.102
  37.6 1.6 %collective-permute-start.12 = (bf16[16,3584]{1,0:T(8,128)(2,1)S(1)}, bf16[16,3584]{1,0:T(8,128)(2,1)S(1)}, u32[]{:S(2)}, u32[]{:S(2)}) collective-permute-start(bf16[16,3584]{1,0:T(8,128)(2,1)S(1)} %get-tuple-element.18), channel_id=1, source_target_pairs={{0,2},{1,5},{2,0},{3,7},{4,6},{5,1},{6,4},{7,3},{8,10},{9,13},{10,... | collective-permute-start | bytes 344072 | tf_op jit(solution)/shard_map/ppermute | solution.py:36
  39.2 0.4 collective-permute-start.15
  39.7 2.8 %collective-permute-done.12 = bf16[16,3584]{1,0:T(8,128)(2,1)S(1)} collective-permute-done((bf16[16,3584]{1,0:T(8,128)(2,1)S(1)}, bf16[16,3584]{1,0:T(8,128)(2,1)S(1)}, u32[]{:S(2)}, u32[]{:S(2)}) %collective-permute-start.12) | collective-permute-done | bytes 114720 | tf_op jit(solution)/shard_map/ppermute | solution.py:36
  42.5 0.7 %collective-permute-start.13 = (bf16[8,3584]{1,0:T(8,128)(2,1)S(1)}, bf16[8,3584]{1,0:T(8,128)(2,1)S(1)}, u32[]{:S(2)}, u32[]{:S(2)}) collective-permute-start(bf16[8,3584]{1,0:T(8,128)(2,1)S(1)} %broadcast_select_fusion.11), channel_id=1, source_target_pairs={{0,4},{1,3},{2,6},{3,1},{4,0},{5,7},{6,2},{7,5},{8,12},{9,11},{10,... | collective-permute-start | bytes 172040 | tf_op jit(solution)/shard_map/ppermute | solution.py:36
  43.2 0.8 %collective-permute-done.15 = bf16[16,3584]{1,0:T(8,128)(2,1)S(1)} collective-permute-done((bf16[16,3584]{1,0:T(8,128)(2,1)S(1)}, bf16[16,3584]{1,0:T(8,128)(2,1)S(1)}, u32[]{:S(2)}, u32[]{:S(2)}) %collective-permute-start.15) | collective-permute-done | bytes 114720 | tf_op jit(solution)/shard_map/ppermute | solution.py:36
  44.1 0.6 %collective-permute-start.16 = (bf16[8,3584]{1,0:T(8,128)(2,1)S(1)}, bf16[8,3584]{1,0:T(8,128)(2,1)S(1)}, u32[]{:S(2)}, u32[]{:S(2)}) collective-permute-start(bf16[8,3584]{1,0:T(8,128)(2,1)S(1)} %broadcast_select_fusion.10), channel_id=1, source_target_pairs={{0,4},{1,3},{2,6},{3,1},{4,0},{5,7},{6,2},{7,5},{8,12},{9,11},{10,... | collective-permute-start | bytes 172040 | tf_op jit(solution)/shard_map/ppermute | solution.py:36
  44.7 2.0 %collective-permute-done.13 = bf16[8,3584]{1,0:T(8,128)(2,1)S(1)} collective-permute-done((bf16[8,3584]{1,0:T(8,128)(2,1)S(1)}, bf16[8,3584]{1,0:T(8,128)(2,1)S(1)}, u32[]{:S(2)}, u32[]{:S(2)}) %collective-permute-start.13) | collective-permute-done | bytes 57376 | tf_op jit(solution)/shard_map/ppermute | solution.py:36
  46.8 1.4 %collective-permute-start.14 = (bf16[4,3584]{1,0:T(4,128)(2,1)S(1)}, bf16[4,3584]{1,0:T(4,128)(2,1)S(1)}, u32[]{:S(2)}, u32[]{:S(2)}) collective-permute-start(bf16[4,3584]{1,0:T(4,128)(2,1)S(1)} %slice.98), channel_id=1, source_target_pairs={{0,8},{1,9},{2,10},{3,11},{4,12},{5,13},{6,14},{7,15},{8,0},{9,1},... | collective-permute-start | bytes 86024 | tf_op jit(solution)/shard_map/ppermute | solution.py:36
  48.2 0.2 collective-permute-done.16
  48.4 1.7 %collective-permute-start.17 = (bf16[4,3584]{1,0:T(4,128)(2,1)S(1)}, bf16[4,3584]{1,0:T(4,128)(2,1)S(1)}, u32[]{:S(2)}, u32[]{:S(2)}) collective-permute-start(bf16[4,3584]{1,0:T(4,128)(2,1)S(1)} %slice.102), channel_id=1, source_target_pairs={{0,8},{1,9},{2,10},{3,11},{4,12},{5,13},{6,14},{7,15},{8,0},{9,1},... | collective-permute-start | bytes 86024 | tf_op jit(solution)/shard_map/ppermute | solution.py:36
  50.0 1.9 %collective-permute-done.14 = bf16[4,3584]{1,0:T(4,128)(2,1)S(1)} collective-permute-done((bf16[4,3584]{1,0:T(4,128)(2,1)S(1)}, bf16[4,3584]{1,0:T(4,128)(2,1)S(1)}, u32[]{:S(2)}, u32[]{:S(2)}) %collective-permute-start.14) | collective-permute-done | bytes 28704 | tf_op jit(solution)/shard_map/ppermute | solution.py:36
  52.0 1.3 %collective-permute-done.17 = bf16[4,3584]{1,0:T(4,128)(2,1)S(1)} collective-permute-done((bf16[4,3584]{1,0:T(4,128)(2,1)S(1)}, bf16[4,3584]{1,0:T(4,128)(2,1)S(1)}, u32[]{:S(2)}, u32[]{:S(2)}) %collective-permute-start.17) | collective-permute-done | bytes 28704 | tf_op jit(solution)/shard_map/ppermute | solution.py:36
  53.2 0.7 %maximum_bitcast_fusion.2 = bf16[1,4,7168]{2,1,0:T(4,128)(2,1)} fusion(bf16[4,3584]{1,0:T(4,128)(2,1)S(1)} %add_convert_fusion.4, bf16[4,3584]{1,0:T(4,128)(2,1)S(1)} %add_convert_fusion.5), kind=kLoop, calls=%fused_computation.45 | loop fusion | flops 114688 | bytes 114688 | tf_op jit(solution)/shard_map/broadcast_in_dim | solution.py:279
  (42 shorter events, 0.7 us)
Async XLA Ops:
  0.0 20.7 %copy-start = (bf16[1,7168,128]{2,1,0:T(8,128)(2,1)S(1)}, bf16[1,7168,128]{2,1,0:T(8,128)(2,1)}, u32[]{:S(2)}) copy-start(bf16[1,7168,128]{2,1,0:T(8,128)(2,1)} %param.16) | copy-start | bytes 5505028
  1.0 7.5 %collective-permute-start.3 = (bf16[4,7296]{1,0:T(4,128)(2,1)S(1)}, bf16[4,7296]{1,0:T(4,128)(2,1)S(1)}, u32[]{:S(2)}, u32[]{:S(2)}) collective-permute-start(bf16[4,7296]{1,0:T(4,128)(2,1)S(1)} %shard_map.100), channel_id=1, source_target_pairs={{0,12},{1,13},{2,14},{3,15},{4,8},{5,9},{6,10},{7,11},{8,4},{9,5},... | collective-permute-start | bytes 175112 | tf_op jit(solution)/shard_map/ppermute | solution.py:36
  6.1 5.1 %collective-permute-start.2 = (bf16[4,7296]{1,0:T(4,128)(2,1)S(1)}, bf16[4,7296]{1,0:T(4,128)(2,1)S(1)}, u32[]{:S(2)}, u32[]{:S(2)}) collective-permute-start(bf16[4,7296]{1,0:T(4,128)(2,1)S(1)} %shard_map.100), channel_id=1, source_target_pairs={{0,8},{1,9},{2,10},{3,11},{4,12},{5,13},{6,14},{7,15},{8,0},{9,1},... | collective-permute-start | bytes 175112 | tf_op jit(solution)/shard_map/ppermute | solution.py:36
  6.1 5.1 %collective-permute-start.1 = (bf16[4,7296]{1,0:T(4,128)(2,1)S(1)}, bf16[4,7296]{1,0:T(4,128)(2,1)S(1)}, u32[]{:S(2)}, u32[]{:S(2)}) collective-permute-start(bf16[4,7296]{1,0:T(4,128)(2,1)S(1)} %shard_map.100), channel_id=1, source_target_pairs={{0,4},{1,5},{2,6},{3,7},{4,0},{5,1},{6,2},{7,3},{8,12},{9,13},{10,... | collective-permute-start | bytes 175112 | tf_op jit(solution)/shard_map/ppermute | solution.py:36
  6.7 6.2 %collective-permute-start = (bf16[4,7296]{1,0:T(4,128)(2,1)S(1)}, bf16[4,7296]{1,0:T(4,128)(2,1)S(1)}, u32[]{:S(2)}, u32[]{:S(2)}) collective-permute-start(bf16[4,7296]{1,0:T(4,128)(2,1)S(1)} %shard_map.100), channel_id=1, source_target_pairs={{0,2},{1,3},{2,0},{3,1},{4,6},{5,7},{6,4},{7,5},{8,10},{9,11},{10,... | collective-permute-start | bytes 175112 | tf_op jit(solution)/shard_map/ppermute | solution.py:36
  11.3 6.8 %collective-permute-start.4 = (bf16[12,7296]{1,0:T(8,128)(2,1)S(1)}, bf16[12,7296]{1,0:T(8,128)(2,1)S(1)}, u32[]{:S(2)}, u32[]{:S(2)}) collective-permute-start(bf16[12,7296]{1,0:T(8,128)(2,1)S(1)} %pad_maximum_fusion.1), channel_id=1, source_target_pairs={{0,2},{1,3},{2,0},{3,1},{4,6},{5,7},{6,4},{7,5},{8,10},{9,11},{10,... | collective-permute-start | bytes 525320 | tf_op jit(solution)/shard_map/ppermute | solution.py:36
  18.7 1.9 %collective-permute-start.5 = (bf16[32,7296]{1,0:T(8,128)(2,1)S(1)}, bf16[32,7296]{1,0:T(8,128)(2,1)S(1)}, u32[]{:S(2)}, u32[]{:S(2)}) collective-permute-start(bf16[32,7296]{1,0:T(8,128)(2,1)S(1)} %concatenate.13), channel_id=1, source_target_pairs={{0,1},{1,0},{2,3},{3,2},{4,5},{5,4},{6,7},{7,6},{8,9},{9,8},{10,11... | collective-permute-start | bytes 1400840 | tf_op jit(solution)/shard_map/ppermute | solution.py:36
  21.4 7.5 %collective-permute-start.8 = (bf16[64,128]{1,0:T(8,128)(2,1)S(1)}, bf16[64,128]{1,0:T(8,128)(2,1)S(1)}, u32[]{:S(2)}, u32[]{:S(2)}) collective-permute-start(bf16[64,128]{1,0:T(8,128)(2,1)S(1)} %convolution_convert_fusion.1), channel_id=1, source_target_pairs={{0,3},{1,2},{2,1},{3,0},{4,7},{5,6},{6,5},{7,4},{8,11},{9,10},{10,... | collective-permute-start | bytes 49160 | tf_op jit(solution)/shard_map/ppermute | solution.py:36
  22.8 6.1 %collective-permute-start.7 = (bf16[64,128]{1,0:T(8,128)(2,1)S(1)}, bf16[64,128]{1,0:T(8,128)(2,1)S(1)}, u32[]{:S(2)}, u32[]{:S(2)}) collective-permute-start(bf16[64,128]{1,0:T(8,128)(2,1)S(1)} %convolution_convert_fusion.1), channel_id=1, source_target_pairs={{0,2},{1,3},{2,0},{3,1},{4,6},{5,7},{6,4},{7,5},{8,10},{9,11},{10,... | collective-permute-start | bytes 49160 | tf_op jit(solution)/shard_map/ppermute | solution.py:36
  23.2 5.6 %collective-permute-start.6 = (bf16[64,128]{1,0:T(8,128)(2,1)S(1)}, bf16[64,128]{1,0:T(8,128)(2,1)S(1)}, u32[]{:S(2)}, u32[]{:S(2)}) collective-permute-start(bf16[64,128]{1,0:T(8,128)(2,1)S(1)} %convolution_convert_fusion.1), channel_id=1, source_target_pairs={{0,1},{1,0},{2,3},{3,2},{4,5},{5,4},{6,7},{7,6},{8,9},{9,8},{10,11... | collective-permute-start | bytes 49160 | tf_op jit(solution)/shard_map/ppermute | solution.py:36
  23.5 5.1 %copy-start.5 = (s32[16]{0:T(128)S(1)}, s32[16]{0:T(128)}, u32[]{:S(2)}) copy-start(s32[16]{0:T(128)} %param.13) | copy-start | bytes 196
  23.5 5.4 %copy-start.3 = (bf16[1,4,128,2,256]{4,3,2,1,0:T(2,128)(2,1)S(1)}, bf16[1,4,128,2,256]{4,3,2,1,0:T(2,128)(2,1)}, u32[]{:S(2)}) copy-start(bf16[1,4,128,2,256]{4,3,2,1,0:T(2,128)(2,1)} %param.17) | copy-start | bytes 1572868
  23.5 9.3 %copy-start.1 = (bf16[1,256,7168]{2,1,0:T(8,128)(2,1)S(1)}, bf16[1,256,7168]{2,1,0:T(8,128)(2,1)}, u32[]{:S(2)}) copy-start(bf16[1,256,7168]{2,1,0:T(8,128)(2,1)} %param.15) | copy-start | bytes 11010052
  28.6 1.0 %copy-start.4 = (bf16[1,4,256,128]{3,2,1,0:T(8,128)(2,1)S(1)}, bf16[1,4,256,128]{3,2,1,0:T(8,128)(2,1)}, u32[]{:S(2)}) copy-start(bf16[1,4,256,128]{3,2,1,0:T(8,128)(2,1)} %param.18) | copy-start | bytes 786436
  29.8 1.4 %collective-permute-start.9 = (bf16[2,64,128]{2,1,0:T(8,128)(2,1)S(1)}, bf16[2,64,128]{2,1,0:T(8,128)(2,1)S(1)}, u32[]{:S(2)}, u32[]{:S(2)}) collective-permute-start(bf16[2,64,128]{2,1,0:T(8,128)(2,1)S(1)} %dynamic-slice_bitcast_fusion), channel_id=1, source_target_pairs={{0,1},{1,0},{2,3},{3,2},{4,5},{5,4},{6,7},{7,6},{8,9},{9,8},{10,11... | collective-permute-start | bytes 98312 | tf_op jit(solution)/shard_map/ppermute | solution.py:36
  31.2 3.8 %copy-start.2 = (bf16[1,128,7168]{2,1,0:T(8,128)(2,1)S(1)}, bf16[1,128,7168]{2,1,0:T(8,128)(2,1)}, u32[]{:S(2)}) copy-start(bf16[1,128,7168]{2,1,0:T(8,128)(2,1)} %param.19) | copy-start | bytes 5505028
  31.2 3.8 %collective-permute-start.10 = (bf16[64,128]{1,0:T(8,128)(2,1)S(1)}, bf16[64,128]{1,0:T(8,128)(2,1)S(1)}, u32[]{:S(2)}, u32[]{:S(2)}) collective-permute-start(bf16[64,128]{1,0:T(8,128)(2,1)S(1)} %dynamic-slice_bitcast_fusion.1), channel_id=1, source_target_pairs={{0,2},{1,3},{2,0},{3,1},{4,6},{5,7},{6,4},{7,5},{8,10},{9,11},{10,... | collective-permute-start | bytes 49160 | tf_op jit(solution)/shard_map/ppermute | solution.py:36
  35.5 1.9 %collective-permute-start.11 = (bf16[32,7168]{1,0:T(8,128)(2,1)S(1)}, bf16[32,7168]{1,0:T(8,128)(2,1)S(1)}, u32[]{:S(2)}, u32[]{:S(2)}) collective-permute-start(bf16[32,7168]{1,0:T(8,128)(2,1)S(1)} %slice_select_fusion), channel_id=1, source_target_pairs={{0,1},{1,0},{2,3},{3,2},{4,5},{5,4},{6,7},{7,6},{8,9},{9,8},{10,11... | collective-permute-start | bytes 1376264 | tf_op jit(solution)/shard_map/ppermute | solution.py:36
  37.6 4.9 %collective-permute-start.12 = (bf16[16,3584]{1,0:T(8,128)(2,1)S(1)}, bf16[16,3584]{1,0:T(8,128)(2,1)S(1)}, u32[]{:S(2)}, u32[]{:S(2)}) collective-permute-start(bf16[16,3584]{1,0:T(8,128)(2,1)S(1)} %get-tuple-element.18), channel_id=1, source_target_pairs={{0,2},{1,5},{2,0},{3,7},{4,6},{5,1},{6,4},{7,3},{8,10},{9,13},{10,... | collective-permute-start | bytes 344072 | tf_op jit(solution)/shard_map/ppermute | solution.py:36
  39.2 4.8 %collective-permute-start.15 = (bf16[16,3584]{1,0:T(8,128)(2,1)S(1)}, bf16[16,3584]{1,0:T(8,128)(2,1)S(1)}, u32[]{:S(2)}, u32[]{:S(2)}) collective-permute-start(bf16[16,3584]{1,0:T(8,128)(2,1)S(1)} %get-tuple-element.20), channel_id=1, source_target_pairs={{0,2},{1,5},{2,0},{3,7},{4,6},{5,1},{6,4},{7,3},{8,10},{9,13},{10,... | collective-permute-start | bytes 344072 | tf_op jit(solution)/shard_map/ppermute | solution.py:36
  42.5 4.2 %collective-permute-start.13 = (bf16[8,3584]{1,0:T(8,128)(2,1)S(1)}, bf16[8,3584]{1,0:T(8,128)(2,1)S(1)}, u32[]{:S(2)}, u32[]{:S(2)}) collective-permute-start(bf16[8,3584]{1,0:T(8,128)(2,1)S(1)} %broadcast_select_fusion.11), channel_id=1, source_target_pairs={{0,4},{1,3},{2,6},{3,1},{4,0},{5,7},{6,2},{7,5},{8,12},{9,11},{10,... | collective-permute-start | bytes 172040 | tf_op jit(solution)/shard_map/ppermute | solution.py:36
  44.1 4.2 %collective-permute-start.16 = (bf16[8,3584]{1,0:T(8,128)(2,1)S(1)}, bf16[8,3584]{1,0:T(8,128)(2,1)S(1)}, u32[]{:S(2)}, u32[]{:S(2)}) collective-permute-start(bf16[8,3584]{1,0:T(8,128)(2,1)S(1)} %broadcast_select_fusion.10), channel_id=1, source_target_pairs={{0,4},{1,3},{2,6},{3,1},{4,0},{5,7},{6,2},{7,5},{8,12},{9,11},{10,... | collective-permute-start | bytes 172040 | tf_op jit(solution)/shard_map/ppermute | solution.py:36
  46.8 5.1 %collective-permute-start.14 = (bf16[4,3584]{1,0:T(4,128)(2,1)S(1)}, bf16[4,3584]{1,0:T(4,128)(2,1)S(1)}, u32[]{:S(2)}, u32[]{:S(2)}) collective-permute-start(bf16[4,3584]{1,0:T(4,128)(2,1)S(1)} %slice.98), channel_id=1, source_target_pairs={{0,8},{1,9},{2,10},{3,11},{4,12},{5,13},{6,14},{7,15},{8,0},{9,1},... | collective-permute-start | bytes 86024 | tf_op jit(solution)/shard_map/ppermute | solution.py:36
  48.4 4.8 %collective-permute-start.17 = (bf16[4,3584]{1,0:T(4,128)(2,1)S(1)}, bf16[4,3584]{1,0:T(4,128)(2,1)S(1)}, u32[]{:S(2)}, u32[]{:S(2)}) collective-permute-start(bf16[4,3584]{1,0:T(4,128)(2,1)S(1)} %slice.102), channel_id=1, source_target_pairs={{0,8},{1,9},{2,10},{3,11},{4,12},{5,13},{6,14},{7,15},{8,0},{9,1},... | collective-permute-start | bytes 86024 | tf_op jit(solution)/shard_map/ppermute | solution.py:36

commit v20 on v17

--- a/solution.py
+++ b/solution.py
@@ -1,4 +1,5 @@
 import functools
+import itertools
 
 import jax
 import jax.numpy as jnp
@@ -46,6 +47,10 @@
 
 def ordered(flip, first, second):
     return jnp.where(flip, second, first), jnp.where(flip, first, second)
+
+
+def add(kept, received):
+    return (kept.astype(jnp.float32) + received.astype(jnp.float32)).astype(jnp.bfloat16)
 
 
 def pack_kernel(tokens, routes, numerators, packed, routes_in, numerators_in, sems):
@@ -152,8 +157,9 @@
     total[...] = term[pl.ds(pl.multiple_of(core * half, half), half), :].astype(jnp.float32) + received[
         ...
     ].astype(jnp.float32)
-    sent = (2 - core * (1 + flag), 3 - core * flag)
-    kept = (core * flag, 1 + core * (1 + flag))
+    by_x = 1 - core
+    sent = (core + by_x * 2 * (1 - flag), 3 - by_x * 2 * flag)
+    kept = (by_x * 2 * flag, 2 * core + by_x * (2 * flag + 1))
     for i, out in enumerate(outs):
         columns = pl.ds((i // 2) * step, step)
         rows = [
@@ -206,32 +212,34 @@
         pieces[0, z] = trade(packed, (z, 0), (z, 0))
     for x in range(1, chips):
         pieces[x, 0] = trade(packed, (0, 2 * x), (0, 2 * x))
-    rest = jnp.concatenate([pieces[0, z] for z in range(1, clusters)])
-    for x in range(1, chips):
-        received = trade(rest, (0, 2 * x), (0, 2 * x))
-        for z in range(1, clusters):
-            pieces[x, z] = received[(z - 1) * count : z * count]
-
-    for bit in across:
-        for x in range(chips):
-            if not x & bit:
-                for z in range(clusters):
-                    flag = (me // (2 * bit)) % 2 == 1
-                    pieces[x, z], pieces[x | bit, z] = ordered(flag, pieces[x, z], pieces[x | bit, z])
     places = [(0, 0)]
     for mask in shared:
         places += [(x, z | mask) for x, z in places]
     for zbit, xbit in zip(paired, across):
+        places += [(x, z | zbit) for x, z in places]
         places += [(x | xbit, z) for x, z in places]
-        places += [(x, z | zbit) for x, z in places]
-    held = by_rows(jnp.concatenate([pieces[place] for place in places]))
+    later = [z for x, z in places if x == 0 and z]
+    rest = jnp.concatenate([pieces[0, z] for z in later])
+    rest, *firsts = lax.optimization_barrier((rest, *(pieces[x, 0] for x in range(1, chips))))
+    pieces.update({(x, 0): first for x, first in enumerate(firsts, 1)})
+    for x in range(chips):
+        received = trade(rest, (0, 2 * x), (0, 2 * x)) if x else rest
+        for i, z in enumerate(later):
+            pieces[x, z] = received[i * count : (i + 1) * count]
+    segments = [(x, tuple(z for _, z in run)) for x, run in itertools.groupby(places, lambda place: place[0])]
+    runs = {(x, zs): jnp.concatenate([pieces[x, z] for z in zs]) for x, zs in segments}
+    for bit in across:
+        flag = (me // (2 * bit)) % 2 == 1
+        for x, zs in runs:
+            if not x & bit:
+                runs[x, zs], runs[x | bit, zs] = ordered(flag, runs[x, zs], runs[x | bit, zs])
+    held = by_rows(jnp.concatenate([runs[segment] for segment in segments]))
     held = by_rows(jnp.concatenate(ordered(core == 1, held, trade(held, (0, 1), (0, 1)))))
-    rows, code_table = lax.optimization_barrier((held, delta_in[0]))
-
-    codes = jnp.dot(rows[:, :width], code_table, preferred_element_type=jnp.float32).astype(jnp.bfloat16)
+
+    codes = jnp.dot(held[:, :width], delta_in[0], preferred_element_type=jnp.float32).astype(jnp.bfloat16)
     projected = gate_up_product(held, base_in[0])
 
-    side = by_rows(rows[:, width:])
+    side = by_rows(held[:, width:])
     all_routes = side[:, :top].astype(jnp.int32)
     numerator = side[:, top : 2 * top].astype(jnp.float32)
     position = lookup(place, all_routes)
@@ -251,18 +259,19 @@
     partial_codes = jnp.einsum(
         "srf,sfk->srk", hidden.astype(jnp.bfloat16), delta_down[0], preferred_element_type=jnp.float32
     ).astype(jnp.bfloat16)
-    lowrank = lax.dynamic_index_in_dim(partial_codes, me, 0, keepdims=False).astype(jnp.float32)
-    for m in range(1, members):
-        sent = lax.dynamic_index_in_dim(partial_codes, me ^ m, 0, keepdims=False)
-        lowrank = lowrank + trade(sent, (0, m), (0, m)).astype(jnp.float32)
+    by_core = partial_codes.reshape(chips, 2, *partial_codes.shape[1:])
+    kept, sent = (lax.dynamic_index_in_dim(by_core, c, 1, keepdims=False) for c in (core, 1 - core))
+    by_chip = add(kept, trade(sent, (0, 1), (0, 1)))
+    chip = me // 2
+    lowrank = lax.dynamic_index_in_dim(by_chip, chip, 0, keepdims=False).astype(jnp.float32)
+    for m in range(1, chips):
+        sent = lax.dynamic_index_in_dim(by_chip, chip ^ m, 0, keepdims=False)
+        lowrank = lowrank + trade(sent, (0, 2 * m), (0, 2 * m)).astype(jnp.float32)
     own_scale = lax.dynamic_index_in_dim(scale, me, 0, keepdims=False)
     scaled = (own_scale[:, None] * lowrank).astype(jnp.bfloat16)
 
     term = down_product(hidden_sum, base_down[0])
     term = (term + jnp.dot(scaled, delta_back[0], preferred_element_type=jnp.float32)).astype(jnp.bfloat16)
-
-    def add(kept, received):
-        return (kept.astype(jnp.float32) + received.astype(jnp.float32)).astype(jnp.bfloat16)
 
     half = term.shape[0] // 2
     sent = ordered(core == 1, term[half:], term[:half])[0]
@@ -275,14 +284,14 @@
                 blocks = [total[j * size : (j + 1) * size] for j in range(4)]
                 inner = ordered(core == 1, blocks[1], blocks[2])
                 kept, sent = ordered(
-                    (core == 1) & flag,
+                    (core == 0) & flag,
                     jnp.concatenate([blocks[0], inner[0]]),
                     jnp.concatenate([inner[1], blocks[3]]),
                 )
+            total = add(kept, trade(sent, (0, 2 * x), (z, 0)))
+            size = total.shape[0] // 2
+            kept, sent = ordered((core == 1) & flag, total[:size], total[size:])
             total = add(kept, trade(sent, (z, 0), (0, 2 * x)))
-            size = total.shape[0] // 2
-            kept, sent = ordered((core == 0) & flag, total[:size], total[size:])
-            total = add(kept, trade(sent, (0, 2 * x), (z, 0)))
         for mask in reversed(shared):
             size = total.shape[0] // 2
             total = add(total[:size], trade(total[size:], (mask, 0), (mask, 0)))

time: 55.1 us -> 55.2 us (level)
  starting transfers between devices: 20.7 us -> 22 us
  waiting for transfers between devices: 19.9 us -> 19 us
    ppermute x19 -> x18, starting transfers between devices: 20.7 us -> 22 us  [trade(): return lax.ppermute(value, ('expert', 'tensor'), pairs)]
    ppermute x19 -> x18, waiting for transfers between devices: 19.9 us -> 19 us  [trade(): return lax.ppermute(value, ('expert', 'tensor'), pairs)]
  transfers between devices with their start and end apart: 19 -> 18, of which waited for: 11 -> 11; matrix products, arithmetic and copies ran while one was open for 1% -> 1% of each run, Pallas kernels for 10% -> 10%
where the time goes in v20:
time: 55.2 us; the launch traced here: 55 us
  starting transfers between devices  22 us (40%)
  waiting for transfers between devices  19 us (34%)
  Pallas kernels  6.69 us (12%)
  local copies, waits for them, and re-layouts  3.66 us (7%)
  other arithmetic  2.03 us (4%)
  matrix products  1.31 us (2%)
    ppermute x18, starting transfers between devices, trade(): return lax.ppermute(value, ('expert', 'tensor'), pairs)  22 us
    ppermute x18, waiting for transfers between devices, trade(): return lax.ppermute(value, ('expert', 'tensor'), pairs)  19 us
    unnamed x12, local copies, waits for them, and re-layouts  3.45 us
    pallas_call x1, Pallas kernels, gate_up_product(): pl.pallas_call(gate_up_kernel, out_shape=jax.ShapeDtypeStruct((2 * x.shap...  2.95 us
    pallas_call x1, Pallas kernels, down_product(): pl.pallas_call(down_kernel, out_shape=jax.ShapeDtypeStruct((rows, width),...  2.57 us
  transfers between devices with their start and end apart: 18, of which 11 were waited for; matrix products, arithmetic and copies ran while one was open for 1% of the time, Pallas kernels for 10%

profile of v20, /device:TPU:0, one launch (start us, length us, event | category | flops | bytes accessed | tf_op | source)
XLA Modules:
  0.0 55.0 jit_solution(13964772023940955644)
XLA Ops:
  0.0 1.0 %shard_map.100 = bf16[4,7296]{1,0:T(4,128)(2,1)S(1)} custom-call(bf16[4,7168]{1,0:T(4,128)(2,1)} %bitcast.70, s32[4,8]{1,0:T(4,128)} %bitcast.71, s32[4,8]{1,0:T(4,128)} %bitcast.72), custom_call_target="tpu_custom_call" | custom-call | flops 20000000000 | bytes 114688 | tf_op jit(solution)/shard_map/pallas_call | solution.py:75
  1.0 5.1 %collective-permute-start.2 = (bf16[4,7296]{1,0:T(4,128)(2,1)S(1)}, bf16[4,7296]{1,0:T(4,128)(2,1)S(1)}, u32[]{:S(2)}, u32[]{:S(2)}) collective-permute-start(bf16[4,7296]{1,0:T(4,128)(2,1)S(1)} %shard_map.100), channel_id=1, source_target_pairs={{0,12},{1,13},{2,14},{3,15},{4,8},{5,9},{6,10},{7,11},{8,4},{9,5},... | collective-permute-start | bytes 175112 | tf_op jit(solution)/shard_map/ppermute | solution.py:37
  6.1 0.6 %collective-permute-start = (bf16[4,7296]{1,0:T(4,128)(2,1)S(1)}, bf16[4,7296]{1,0:T(4,128)(2,1)S(1)}, u32[]{:S(2)}, u32[]{:S(2)}) collective-permute-start(bf16[4,7296]{1,0:T(4,128)(2,1)S(1)} %shard_map.100), channel_id=1, source_target_pairs={{0,8},{1,9},{2,10},{3,11},{4,12},{5,13},{6,14},{7,15},{8,0},{9,1},... | collective-permute-start | bytes 175112 | tf_op jit(solution)/shard_map/ppermute | solution.py:37
  6.7 1.6 %collective-permute-start.3 = (bf16[4,7296]{1,0:T(4,128)(2,1)S(1)}, bf16[4,7296]{1,0:T(4,128)(2,1)S(1)}, u32[]{:S(2)}, u32[]{:S(2)}) collective-permute-start(bf16[4,7296]{1,0:T(4,128)(2,1)S(1)} %shard_map.100), channel_id=1, source_target_pairs={{0,2},{1,3},{2,0},{3,1},{4,6},{5,7},{6,4},{7,5},{8,10},{9,11},{10,... | collective-permute-start | bytes 175112 | tf_op jit(solution)/shard_map/ppermute | solution.py:37
  8.4 0.4 collective-permute-done.2
  8.8 1.7 %collective-permute-done.1 = bf16[4,7296]{1,0:T(4,128)(2,1)S(1)} collective-permute-done((bf16[4,7296]{1,0:T(4,128)(2,1)S(1)}, bf16[4,7296]{1,0:T(4,128)(2,1)S(1)}, u32[]{:S(2)}, u32[]{:S(2)}) %collective-permute-start.1) | collective-permute-done | bytes 58400 | tf_op jit(solution)/shard_map/ppermute | solution.py:37
  10.4 1.1 %collective-permute-done = bf16[4,7296]{1,0:T(4,128)(2,1)S(1)} collective-permute-done((bf16[4,7296]{1,0:T(4,128)(2,1)S(1)}, bf16[4,7296]{1,0:T(4,128)(2,1)S(1)}, u32[]{:S(2)}, u32[]{:S(2)}) %collective-permute-start) | collective-permute-done | bytes 58400 | tf_op jit(solution)/shard_map/ppermute | solution.py:37
  11.6 0.1 pad_maximum_fusion.2
  11.7 1.6 %collective-permute-start.4 = (bf16[12,7296]{1,0:T(8,128)(2,1)S(1)}, bf16[12,7296]{1,0:T(8,128)(2,1)S(1)}, u32[]{:S(2)}, u32[]{:S(2)}) collective-permute-start(bf16[12,7296]{1,0:T(8,128)(2,1)S(1)} %pad_maximum_fusion.2), channel_id=1, source_target_pairs={{0,2},{1,3},{2,0},{3,1},{4,6},{5,7},{6,4},{7,5},{8,10},{9,11},{10,... | collective-permute-start | bytes 525320 | tf_op jit(solution)/shard_map/ppermute | solution.py:37
  13.3 4.6 %collective-permute-done.4 = bf16[12,7296]{1,0:T(8,128)(2,1)S(1)} collective-permute-done((bf16[12,7296]{1,0:T(8,128)(2,1)S(1)}, bf16[12,7296]{1,0:T(8,128)(2,1)S(1)}, u32[]{:S(2)}, u32[]{:S(2)}) %collective-permute-start.4) | collective-permute-done | bytes 175136 | tf_op jit(solution)/shard_map/ppermute | solution.py:37
  17.8 0.2 broadcast_select_fusion.3
  18.1 0.1 collective-permute-start.5
  18.3 1.7 %collective-permute-done.5 = bf16[32,7296]{1,0:T(8,128)(2,1)S(1)} collective-permute-done((bf16[32,7296]{1,0:T(8,128)(2,1)S(1)}, bf16[32,7296]{1,0:T(8,128)(2,1)S(1)}, u32[]{:S(2)}, u32[]{:S(2)}) %collective-permute-start.5) | collective-permute-done | bytes 466976 | tf_op jit(solution)/shard_map/ppermute | solution.py:37
  20.0 0.2 broadcast_select_fusion.1
  20.1 0.2 convert_reduce_fusion
  20.3 0.5 fusion.4
  20.8 1.3 %collective-permute-start.8 = (bf16[64,128]{1,0:T(8,128)(2,1)S(1)}, bf16[64,128]{1,0:T(8,128)(2,1)S(1)}, u32[]{:S(2)}, u32[]{:S(2)}) collective-permute-start(bf16[64,128]{1,0:T(8,128)(2,1)S(1)} %fusion.4), channel_id=1, source_target_pairs={{0,3},{1,2},{2,1},{3,0},{4,7},{5,6},{6,5},{7,4},{8,11},{9,10},{10,... | collective-permute-start | bytes 49160 | tf_op jit(solution)/shard_map/ppermute | solution.py:37
  22.1 0.5 collective-permute-start.7
  22.6 0.1 collective-permute-start.6
  22.7 0.1 pad_maximum_fusion.x
  22.8 0.1 fusion.29
  23.0 3.1 %copy-done.1 = bf16[1,7168,2,256]{3,2,1,0:T(2,128)(2,1)S(1)} copy-done((bf16[1,7168,2,256]{3,2,1,0:T(2,128)(2,1)S(1)}, bf16[1,7168,2,256]{3,2,1,0:T(2,128)(2,1)}, u32[]{:S(2)}) %copy-start.1) | copy-done | bytes 7340056
  26.1 3.0 %shard_map.101 = f32[128,256]{1,0:T(8,128)S(1)} custom-call(bf16[64,7296]{1,0:T(8,128)(2,1)S(1)} %pad_maximum_fusion.x, bf16[7168,2,256]{2,1,0:T(2,128)(2,1)S(1)} %bitcast.61), custom_call_target="tpu_custom_call" | custom-call | flops 469762048 | bytes 7340032 | tf_op jit(solution)/shard_map/pallas_call | solution.py:115
  29.1 0.1 select_reduce_fusion
  29.2 0.1 select_reduce_fusion.1
  29.4 0.2 fusion.9
  29.6 0.1 multiply_reduce_fusion
  29.7 0.3 copy-done.3
  30.0 0.2 convolution_convert_fusion
  30.2 0.5 collective-permute-start.9
  30.7 0.9 %collective-permute-done.9 = bf16[2,64,128]{2,1,0:T(8,128)(2,1)S(1)} collective-permute-done((bf16[2,64,128]{2,1,0:T(8,128)(2,1)S(1)}, bf16[2,64,128]{2,1,0:T(8,128)(2,1)S(1)}, u32[]{:S(2)}, u32[]{:S(2)}) %collective-permute-start.9) | collective-permute-done | bytes 32800 | tf_op jit(solution)/shard_map/ppermute | solution.py:37
  31.6 1.6 %collective-permute-start.10 = (bf16[64,128]{1,0:T(8,128)(2,1)S(1)}, bf16[64,128]{1,0:T(8,128)(2,1)S(1)}, u32[]{:S(2)}, u32[]{:S(2)}) collective-permute-start(bf16[64,128]{1,0:T(8,128)(2,1)S(1)} %dynamic-slice_bitcast_fusion.1), channel_id=1, source_target_pairs={{0,2},{1,3},{2,0},{3,1},{4,6},{5,7},{6,4},{7,5},{8,10},{9,11},{10,... | collective-permute-start | bytes 49160 | tf_op jit(solution)/shard_map/ppermute | solution.py:37
  33.2 2.6 %shard_map.102 = f32[64,7168]{1,0:T(8,128)S(1)} custom-call(bf16[64,256]{1,0:T(8,128)(2,1)S(1)} %get-tuple-element.17.hidden, bf16[256,7168]{1,0:T(8,128)(2,1)} %bitcast.62), custom_call_target="tpu_custom_call" | custom-call | flops 234881024 | bytes 3670016 | tf_op jit(solution)/shard_map/pallas_call | solution.py:140
  35.8 0.5 fusion.term
  36.3 0.1 collective-permute-start.11
  36.5 1.7 %collective-permute-done.11.received = bf16[32,7168]{1,0:T(8,128)(2,1)S(1)} collective-permute-done((bf16[32,7168]{1,0:T(8,128)(2,1)S(1)}, bf16[32,7168]{1,0:T(8,128)(2,1)S(1)}, u32[]{:S(2)}, u32[]{:S(2)}) %collective-permute-start.11) | collective-permute-done | bytes 458784 | tf_op jit(solution)/shard_map/ppermute | solution.py:37
  38.2 0.2 shard_map.103
  38.4 1.2 %collective-permute-start.12 = (bf16[16,3584]{1,0:T(8,128)(2,1)S(1)}, bf16[16,3584]{1,0:T(8,128)(2,1)S(1)}, u32[]{:S(2)}, u32[]{:S(2)}) collective-permute-start(bf16[16,3584]{1,0:T(8,128)(2,1)S(1)} %get-tuple-element.14), channel_id=1, source_target_pairs={{0,2},{1,5},{2,0},{3,7},{4,6},{5,1},{6,4},{7,3},{8,10},{9,13},{10,... | collective-permute-start | bytes 344072 | tf_op jit(solution)/shard_map/ppermute | solution.py:37
  39.6 0.9 %collective-permute-start.15 = (bf16[16,3584]{1,0:T(8,128)(2,1)S(1)}, bf16[16,3584]{1,0:T(8,128)(2,1)S(1)}, u32[]{:S(2)}, u32[]{:S(2)}) collective-permute-start(bf16[16,3584]{1,0:T(8,128)(2,1)S(1)} %get-tuple-element.16), channel_id=1, source_target_pairs={{0,2},{1,5},{2,0},{3,7},{4,6},{5,1},{6,4},{7,3},{8,10},{9,13},{10,... | collective-permute-start | bytes 344072 | tf_op jit(solution)/shard_map/ppermute | solution.py:37
  40.5 2.8 %collective-permute-done.12 = bf16[16,3584]{1,0:T(8,128)(2,1)S(1)} collective-permute-done((bf16[16,3584]{1,0:T(8,128)(2,1)S(1)}, bf16[16,3584]{1,0:T(8,128)(2,1)S(1)}, u32[]{:S(2)}, u32[]{:S(2)}) %collective-permute-start.12) | collective-permute-done | bytes 114720 | tf_op jit(solution)/shard_map/ppermute | solution.py:37
  43.3 1.7 %collective-permute-start.13 = (bf16[8,3584]{1,0:T(8,128)(2,1)S(1)}, bf16[8,3584]{1,0:T(8,128)(2,1)S(1)}, u32[]{:S(2)}, u32[]{:S(2)}) collective-permute-start(bf16[8,3584]{1,0:T(8,128)(2,1)S(1)} %broadcast_select_fusion.5), channel_id=1, source_target_pairs={{0,4},{1,3},{2,6},{3,1},{4,0},{5,7},{6,2},{7,5},{8,12},{9,11},{10,... | collective-permute-start | bytes 172040 | tf_op jit(solution)/shard_map/ppermute | solution.py:37
  45.1 1.2 %collective-permute-start.16 = (bf16[8,3584]{1,0:T(8,128)(2,1)S(1)}, bf16[8,3584]{1,0:T(8,128)(2,1)S(1)}, u32[]{:S(2)}, u32[]{:S(2)}) collective-permute-start(bf16[8,3584]{1,0:T(8,128)(2,1)S(1)} %broadcast_select_fusion.4), channel_id=1, source_target_pairs={{0,4},{1,3},{2,6},{3,1},{4,0},{5,7},{6,2},{7,5},{8,12},{9,11},{10,... | collective-permute-start | bytes 172040 | tf_op jit(solution)/shard_map/ppermute | solution.py:37
  46.2 1.3 %collective-permute-done.13 = bf16[8,3584]{1,0:T(8,128)(2,1)S(1)} collective-permute-done((bf16[8,3584]{1,0:T(8,128)(2,1)S(1)}, bf16[8,3584]{1,0:T(8,128)(2,1)S(1)}, u32[]{:S(2)}, u32[]{:S(2)}) %collective-permute-start.13) | collective-permute-done | bytes 57376 | tf_op jit(solution)/shard_map/ppermute | solution.py:37
  47.6 1.9 %collective-permute-start.14 = (bf16[4,3584]{1,0:T(4,128)(2,1)S(1)}, bf16[4,3584]{1,0:T(4,128)(2,1)S(1)}, u32[]{:S(2)}, u32[]{:S(2)}) collective-permute-start(bf16[4,3584]{1,0:T(4,128)(2,1)S(1)} %slice.97), channel_id=1, source_target_pairs={{0,8},{1,9},{2,10},{3,11},{4,12},{5,13},{6,14},{7,15},{8,0},{9,1},... | collective-permute-start | bytes 86024 | tf_op jit(solution)/shard_map/ppermute | solution.py:37
  49.5 2.0 %collective-permute-start.17 = (bf16[4,3584]{1,0:T(4,128)(2,1)S(1)}, bf16[4,3584]{1,0:T(4,128)(2,1)S(1)}, u32[]{:S(2)}, u32[]{:S(2)}) collective-permute-start(bf16[4,3584]{1,0:T(4,128)(2,1)S(1)} %slice.101), channel_id=1, source_target_pairs={{0,8},{1,9},{2,10},{3,11},{4,12},{5,13},{6,14},{7,15},{8,0},{9,1},... | collective-permute-start | bytes 86024 | tf_op jit(solution)/shard_map/ppermute | solution.py:37
  51.6 1.1 %collective-permute-done.14 = bf16[4,3584]{1,0:T(4,128)(2,1)S(1)} collective-permute-done((bf16[4,3584]{1,0:T(4,128)(2,1)S(1)}, bf16[4,3584]{1,0:T(4,128)(2,1)S(1)}, u32[]{:S(2)}, u32[]{:S(2)}) %collective-permute-start.14) | collective-permute-done | bytes 28704 | tf_op jit(solution)/shard_map/ppermute | solution.py:37
  52.7 1.7 %collective-permute-done.17 = bf16[4,3584]{1,0:T(4,128)(2,1)S(1)} collective-permute-done((bf16[4,3584]{1,0:T(4,128)(2,1)S(1)}, bf16[4,3584]{1,0:T(4,128)(2,1)S(1)}, u32[]{:S(2)}, u32[]{:S(2)}) %collective-permute-start.17) | collective-permute-done | bytes 28704 | tf_op jit(solution)/shard_map/ppermute | solution.py:37
  54.4 0.7 %maximum_bitcast_fusion.2 = bf16[1,4,7168]{2,1,0:T(4,128)(2,1)} fusion(bf16[4,3584]{1,0:T(4,128)(2,1)S(1)} %add_convert_fusion.4, bf16[4,3584]{1,0:T(4,128)(2,1)S(1)} %add_convert_fusion.5), kind=kLoop, calls=%fused_computation.50 | loop fusion | flops 114688 | bytes 114688 | tf_op jit(solution)/shard_map/broadcast_in_dim | solution.py:299
  (41 shorter events, 0.6 us)
Async XLA Ops:
  0.0 35.8 %copy-start = (bf16[1,128,7168]{2,1,0:T(8,128)(2,1)S(1)}, bf16[1,128,7168]{2,1,0:T(8,128)(2,1)}, u32[]{:S(2)}) copy-start(bf16[1,128,7168]{2,1,0:T(8,128)(2,1)} %param.19) | copy-start | bytes 5505028
  1.0 7.8 %collective-permute-start.2 = (bf16[4,7296]{1,0:T(4,128)(2,1)S(1)}, bf16[4,7296]{1,0:T(4,128)(2,1)S(1)}, u32[]{:S(2)}, u32[]{:S(2)}) collective-permute-start(bf16[4,7296]{1,0:T(4,128)(2,1)S(1)} %shard_map.100), channel_id=1, source_target_pairs={{0,12},{1,13},{2,14},{3,15},{4,8},{5,9},{6,10},{7,11},{8,4},{9,5},... | collective-permute-start | bytes 175112 | tf_op jit(solution)/shard_map/ppermute | solution.py:37
  6.1 4.3 %collective-permute-start.1 = (bf16[4,7296]{1,0:T(4,128)(2,1)S(1)}, bf16[4,7296]{1,0:T(4,128)(2,1)S(1)}, u32[]{:S(2)}, u32[]{:S(2)}) collective-permute-start(bf16[4,7296]{1,0:T(4,128)(2,1)S(1)} %shard_map.100), channel_id=1, source_target_pairs={{0,4},{1,5},{2,6},{3,7},{4,0},{5,1},{6,2},{7,3},{8,12},{9,13},{10,... | collective-permute-start | bytes 175112 | tf_op jit(solution)/shard_map/ppermute | solution.py:37
  6.1 5.5 %collective-permute-start = (bf16[4,7296]{1,0:T(4,128)(2,1)S(1)}, bf16[4,7296]{1,0:T(4,128)(2,1)S(1)}, u32[]{:S(2)}, u32[]{:S(2)}) collective-permute-start(bf16[4,7296]{1,0:T(4,128)(2,1)S(1)} %shard_map.100), channel_id=1, source_target_pairs={{0,8},{1,9},{2,10},{3,11},{4,12},{5,13},{6,14},{7,15},{8,0},{9,1},... | collective-permute-start | bytes 175112 | tf_op jit(solution)/shard_map/ppermute | solution.py:37
  6.7 4.9 %collective-permute-start.3 = (bf16[4,7296]{1,0:T(4,128)(2,1)S(1)}, bf16[4,7296]{1,0:T(4,128)(2,1)S(1)}, u32[]{:S(2)}, u32[]{:S(2)}) collective-permute-start(bf16[4,7296]{1,0:T(4,128)(2,1)S(1)} %shard_map.100), channel_id=1, source_target_pairs={{0,2},{1,3},{2,0},{3,1},{4,6},{5,7},{6,4},{7,5},{8,10},{9,11},{10,... | collective-permute-start | bytes 175112 | tf_op jit(solution)/shard_map/ppermute | solution.py:37
  11.7 6.1 %collective-permute-start.4 = (bf16[12,7296]{1,0:T(8,128)(2,1)S(1)}, bf16[12,7296]{1,0:T(8,128)(2,1)S(1)}, u32[]{:S(2)}, u32[]{:S(2)}) collective-permute-start(bf16[12,7296]{1,0:T(8,128)(2,1)S(1)} %pad_maximum_fusion.2), channel_id=1, source_target_pairs={{0,2},{1,3},{2,0},{3,1},{4,6},{5,7},{6,4},{7,5},{8,10},{9,11},{10,... | collective-permute-start | bytes 525320 | tf_op jit(solution)/shard_map/ppermute | solution.py:37
  18.1 1.9 %collective-permute-start.5 = (bf16[32,7296]{1,0:T(8,128)(2,1)S(1)}, bf16[32,7296]{1,0:T(8,128)(2,1)S(1)}, u32[]{:S(2)}, u32[]{:S(2)}) collective-permute-start(bf16[32,7296]{1,0:T(8,128)(2,1)S(1)} %pad_maximum_fusion.1), channel_id=1, source_target_pairs={{0,1},{1,0},{2,3},{3,2},{4,5},{5,4},{6,7},{7,6},{8,9},{9,8},{10,11... | collective-permute-start | bytes 1400840 | tf_op jit(solution)/shard_map/ppermute | solution.py:37
  18.2 2.1 %copy-start.5 = (bf16[1,7168,128]{2,1,0:T(8,128)(2,1)S(1)}, bf16[1,7168,128]{2,1,0:T(8,128)(2,1)}, u32[]{:S(2)}) copy-start(bf16[1,7168,128]{2,1,0:T(8,128)(2,1)} %param.16) | copy-start | bytes 5505028
  20.8 8.5 %collective-permute-start.8 = (bf16[64,128]{1,0:T(8,128)(2,1)S(1)}, bf16[64,128]{1,0:T(8,128)(2,1)S(1)}, u32[]{:S(2)}, u32[]{:S(2)}) collective-permute-start(bf16[64,128]{1,0:T(8,128)(2,1)S(1)} %fusion.4), channel_id=1, source_target_pairs={{0,3},{1,2},{2,1},{3,0},{4,7},{5,6},{6,5},{7,4},{8,11},{9,10},{10,... | collective-permute-start | bytes 49160 | tf_op jit(solution)/shard_map/ppermute | solution.py:37
  22.1 7.2 %collective-permute-start.7 = (bf16[64,128]{1,0:T(8,128)(2,1)S(1)}, bf16[64,128]{1,0:T(8,128)(2,1)S(1)}, u32[]{:S(2)}, u32[]{:S(2)}) collective-permute-start(bf16[64,128]{1,0:T(8,128)(2,1)S(1)} %fusion.4), channel_id=1, source_target_pairs={{0,2},{1,3},{2,0},{3,1},{4,6},{5,7},{6,4},{7,5},{8,10},{9,11},{10,... | collective-permute-start | bytes 49160 | tf_op jit(solution)/shard_map/ppermute | solution.py:37
  22.6 6.7 %collective-permute-start.6 = (bf16[64,128]{1,0:T(8,128)(2,1)S(1)}, bf16[64,128]{1,0:T(8,128)(2,1)S(1)}, u32[]{:S(2)}, u32[]{:S(2)}) collective-permute-start(bf16[64,128]{1,0:T(8,128)(2,1)S(1)} %fusion.4), channel_id=1, source_target_pairs={{0,1},{1,0},{2,3},{3,2},{4,5},{5,4},{6,7},{7,6},{8,9},{9,8},{10,11... | collective-permute-start | bytes 49160 | tf_op jit(solution)/shard_map/ppermute | solution.py:37
  23.0 3.1 %copy-start.1 = (bf16[1,7168,2,256]{3,2,1,0:T(2,128)(2,1)S(1)}, bf16[1,7168,2,256]{3,2,1,0:T(2,128)(2,1)}, u32[]{:S(2)}) copy-start(bf16[1,7168,2,256]{3,2,1,0:T(2,128)(2,1)} %param.14) | copy-start | bytes 22020100
  26.1 3.0 %copy-start.4 = (s32[16]{0:T(128)S(1)}, s32[16]{0:T(128)}, u32[]{:S(2)}) copy-start(s32[16]{0:T(128)} %param.13) | copy-start | bytes 196
  26.1 3.2 %copy-start.2 = (bf16[1,4,128,2,256]{4,3,2,1,0:T(2,128)(2,1)S(1)}, bf16[1,4,128,2,256]{4,3,2,1,0:T(2,128)(2,1)}, u32[]{:S(2)}) copy-start(bf16[1,4,128,2,256]{4,3,2,1,0:T(2,128)(2,1)} %param.17) | copy-start | bytes 1572868
  29.1 1.0 %copy-start.3 = (bf16[1,4,256,128]{3,2,1,0:T(8,128)(2,1)S(1)}, bf16[1,4,256,128]{3,2,1,0:T(8,128)(2,1)}, u32[]{:S(2)}) copy-start(bf16[1,4,256,128]{3,2,1,0:T(8,128)(2,1)} %param.18) | copy-start | bytes 786436
  30.2 1.4 %collective-permute-start.9 = (bf16[2,64,128]{2,1,0:T(8,128)(2,1)S(1)}, bf16[2,64,128]{2,1,0:T(8,128)(2,1)S(1)}, u32[]{:S(2)}, u32[]{:S(2)}) collective-permute-start(bf16[2,64,128]{2,1,0:T(8,128)(2,1)S(1)} %dynamic-slice_bitcast_fusion), channel_id=1, source_target_pairs={{0,1},{1,0},{2,3},{3,2},{4,5},{5,4},{6,7},{7,6},{8,9},{9,8},{10,11... | collective-permute-start | bytes 98312 | tf_op jit(solution)/shard_map/ppermute | solution.py:37
  31.6 4.2 %collective-permute-start.10 = (bf16[64,128]{1,0:T(8,128)(2,1)S(1)}, bf16[64,128]{1,0:T(8,128)(2,1)S(1)}, u32[]{:S(2)}, u32[]{:S(2)}) collective-permute-start(bf16[64,128]{1,0:T(8,128)(2,1)S(1)} %dynamic-slice_bitcast_fusion.1), channel_id=1, source_target_pairs={{0,2},{1,3},{2,0},{3,1},{4,6},{5,7},{6,4},{7,5},{8,10},{9,11},{10,... | collective-permute-start | bytes 49160 | tf_op jit(solution)/shard_map/ppermute | solution.py:37
  36.3 1.9 %collective-permute-start.11 = (bf16[32,7168]{1,0:T(8,128)(2,1)S(1)}, bf16[32,7168]{1,0:T(8,128)(2,1)S(1)}, u32[]{:S(2)}, u32[]{:S(2)}) collective-permute-start(bf16[32,7168]{1,0:T(8,128)(2,1)S(1)} %slice_select_fusion), channel_id=1, source_target_pairs={{0,1},{1,0},{2,3},{3,2},{4,5},{5,4},{6,7},{7,6},{8,9},{9,8},{10,11... | collective-permute-start | bytes 1376264 | tf_op jit(solution)/shard_map/ppermute | solution.py:37
  38.4 4.9 %collective-permute-start.12 = (bf16[16,3584]{1,0:T(8,128)(2,1)S(1)}, bf16[16,3584]{1,0:T(8,128)(2,1)S(1)}, u32[]{:S(2)}, u32[]{:S(2)}) collective-permute-start(bf16[16,3584]{1,0:T(8,128)(2,1)S(1)} %get-tuple-element.14), channel_id=1, source_target_pairs={{0,2},{1,5},{2,0},{3,7},{4,6},{5,1},{6,4},{7,3},{8,10},{9,13},{10,... | collective-permute-start | bytes 344072 | tf_op jit(solution)/shard_map/ppermute | solution.py:37
  39.6 5.4 %collective-permute-start.15 = (bf16[16,3584]{1,0:T(8,128)(2,1)S(1)}, bf16[16,3584]{1,0:T(8,128)(2,1)S(1)}, u32[]{:S(2)}, u32[]{:S(2)}) collective-permute-start(bf16[16,3584]{1,0:T(8,128)(2,1)S(1)} %get-tuple-element.16), channel_id=1, source_target_pairs={{0,2},{1,5},{2,0},{3,7},{4,6},{5,1},{6,4},{7,3},{8,10},{9,13},{10,... | collective-permute-start | bytes 344072 | tf_op jit(solution)/shard_map/ppermute | solution.py:37
  43.3 4.2 %collective-permute-start.13 = (bf16[8,3584]{1,0:T(8,128)(2,1)S(1)}, bf16[8,3584]{1,0:T(8,128)(2,1)S(1)}, u32[]{:S(2)}, u32[]{:S(2)}) collective-permute-start(bf16[8,3584]{1,0:T(8,128)(2,1)S(1)} %broadcast_select_fusion.5), channel_id=1, source_target_pairs={{0,4},{1,3},{2,6},{3,1},{4,0},{5,7},{6,2},{7,5},{8,12},{9,11},{10,... | collective-permute-start | bytes 172040 | tf_op jit(solution)/shard_map/ppermute | solution.py:37
  45.1 4.4 %collective-permute-start.16 = (bf16[8,3584]{1,0:T(8,128)(2,1)S(1)}, bf16[8,3584]{1,0:T(8,128)(2,1)S(1)}, u32[]{:S(2)}, u32[]{:S(2)}) collective-permute-start(bf16[8,3584]{1,0:T(8,128)(2,1)S(1)} %broadcast_select_fusion.4), channel_id=1, source_target_pairs={{0,4},{1,3},{2,6},{3,1},{4,0},{5,7},{6,2},{7,5},{8,12},{9,11},{10,... | collective-permute-start | bytes 172040 | tf_op jit(solution)/shard_map/ppermute | solution.py:37
  47.6 5.0 %collective-permute-start.14 = (bf16[4,3584]{1,0:T(4,128)(2,1)S(1)}, bf16[4,3584]{1,0:T(4,128)(2,1)S(1)}, u32[]{:S(2)}, u32[]{:S(2)}) collective-permute-start(bf16[4,3584]{1,0:T(4,128)(2,1)S(1)} %slice.97), channel_id=1, source_target_pairs={{0,8},{1,9},{2,10},{3,11},{4,12},{5,13},{6,14},{7,15},{8,0},{9,1},... | collective-permute-start | bytes 86024 | tf_op jit(solution)/shard_map/ppermute | solution.py:37
  49.5 4.8 %collective-permute-start.17 = (bf16[4,3584]{1,0:T(4,128)(2,1)S(1)}, bf16[4,3584]{1,0:T(4,128)(2,1)S(1)}, u32[]{:S(2)}, u32[]{:S(2)}) collective-permute-start(bf16[4,3584]{1,0:T(4,128)(2,1)S(1)} %slice.101), channel_id=1, source_target_pairs={{0,8},{1,9},{2,10},{3,11},{4,12},{5,13},{6,14},{7,15},{8,0},{9,1},... | collective-permute-start | bytes 86024 | tf_op jit(solution)/shard_map/ppermute | solution.py:37

commit v21 on v19

--- a/solution.py
+++ b/solution.py
@@ -1,4 +1,5 @@
 import functools
+import itertools
 
 import jax
 import jax.numpy as jnp
@@ -139,8 +140,8 @@
         ...
     ].astype(jnp.float32)
     by_x = 1 - core
-    sent = (2 - by_x * (1 + flag), 3 - by_x * flag)
-    kept = (by_x * flag, 1 + by_x * (1 + flag))
+    sent = (core + by_x * 2 * (1 - flag), 3 - by_x * 2 * flag)
+    kept = (by_x * 2 * flag, 2 * core + by_x * (2 * flag + 1))
     for i, out in enumerate(outs):
         columns = pl.ds((i // 2) * step, step)
         rows = [
@@ -193,25 +194,28 @@
         pieces[0, z] = trade(packed, (z, 0), (z, 0))
     for x in range(1, chips):
         pieces[x, 0] = trade(packed, (0, 2 * x), (0, 2 * x))
-    rest = jnp.concatenate([pieces[0, z] for z in range(1, clusters)])
-    for x in range(1, chips):
-        received = trade(rest, (0, 2 * x), (0, 2 * x))
-        for z in range(1, clusters):
-            pieces[x, z] = received[(z - 1) * count : z * count]
-
-    for bit in across:
-        for x in range(chips):
-            if not x & bit:
-                for z in range(clusters):
-                    flag = (me // (2 * bit)) % 2 == 1
-                    pieces[x, z], pieces[x | bit, z] = ordered(flag, pieces[x, z], pieces[x | bit, z])
     places = [(0, 0)]
     for mask in shared:
         places += [(x, z | mask) for x, z in places]
     for zbit, xbit in zip(paired, across):
+        places += [(x, z | zbit) for x, z in places]
         places += [(x | xbit, z) for x, z in places]
-        places += [(x, z | zbit) for x, z in places]
-    held = by_rows(jnp.concatenate([pieces[place] for place in places]))
+    later = [z for x, z in places if x == 0 and z]
+    rest = jnp.concatenate([pieces[0, z] for z in later])
+    rest, *firsts = lax.optimization_barrier((rest, *(pieces[x, 0] for x in range(1, chips))))
+    pieces.update({(x, 0): first for x, first in enumerate(firsts, 1)})
+    for x in range(chips):
+        received = trade(rest, (0, 2 * x), (0, 2 * x)) if x else rest
+        for i, z in enumerate(later):
+            pieces[x, z] = received[i * count : (i + 1) * count]
+    segments = [(x, tuple(z for _, z in run)) for x, run in itertools.groupby(places, lambda place: place[0])]
+    runs = {(x, zs): jnp.concatenate([pieces[x, z] for z in zs]) for x, zs in segments}
+    for bit in across:
+        flag = (me // (2 * bit)) % 2 == 1
+        for x, zs in runs:
+            if not x & bit:
+                runs[x, zs], runs[x | bit, zs] = ordered(flag, runs[x, zs], runs[x | bit, zs])
+    held = by_rows(jnp.concatenate([runs[segment] for segment in segments]))
     held = by_rows(jnp.concatenate(ordered(core == 1, held, trade(held, (0, 1), (0, 1)))))
     rows, code_table = lax.optimization_barrier((held, delta_in[0]))
 
@@ -249,8 +253,7 @@
     own_scale = lax.dynamic_index_in_dim(scale, me, 0, keepdims=False)
     scaled = (own_scale[:, None] * lowrank).astype(jnp.bfloat16)
 
-    hidden_sum, down_table = lax.optimization_barrier((hidden_sum, base_down[0]))
-    term = jnp.dot(hidden_sum, down_table, preferred_element_type=jnp.float32)
+    term = jnp.dot(hidden_sum, base_down[0], preferred_element_type=jnp.float32)
     term = (term + jnp.dot(scaled, delta_back[0], preferred_element_type=jnp.float32)).astype(jnp.bfloat16)
 
     half = term.shape[0] // 2
@@ -262,7 +265,7 @@
             if i:
                 size = total.shape[0] // 4
                 blocks = [total[j * size : (j + 1) * size] for j in range(4)]
-                inner = ordered(core == 0, blocks[1], blocks[2])
+                inner = ordered(core == 1, blocks[1], blocks[2])
                 kept, sent = ordered(
                     (core == 0) & flag,
                     jnp.concatenate([blocks[0], inner[0]]),

time: 54 us -> 53.9 us (level)
  starting transfers between devices: 19.7 us -> 22.2 us
  waiting for transfers between devices: 22.7 us -> 20.2 us
    ppermute x18, starting transfers between devices: 19.7 us -> 22.2 us  [trade(): return lax.ppermute(value, ('expert', 'tensor'), pairs)]
    ppermute x18, waiting for transfers between devices: 22.7 us -> 20.2 us  [trade(): return lax.ppermute(value, ('expert', 'tensor'), pairs)]
  transfers between devices with their start and end apart: 18 -> 18, of which waited for: 13 -> 12; matrix products, arithmetic and copies ran while one was open for 3% -> 3% of each run, Pallas kernels for 9% -> 9%
where the time goes in v21:
time: 53.9 us; the launch traced here: 53.7 us
  starting transfers between devices  22.2 us (41%)
  waiting for transfers between devices  20.2 us (37%)
  Pallas kernels  6.26 us (12%)
  matrix products  2.07 us (4%)
  other arithmetic  2.03 us (4%)
  local copies, waits for them, and re-layouts  0.56 us (1%)
    ppermute x18, starting transfers between devices, trade(): return lax.ppermute(value, ('expert', 'tensor'), pairs)  22.2 us
    ppermute x18, waiting for transfers between devices, trade(): return lax.ppermute(value, ('expert', 'tensor'), pairs)  20.2 us
    pallas_call x1, Pallas kernels, gate_up_product(): pl.pallas_call(gate_up_kernel, out_shape=jax.ShapeDtypeStruct((2 * x.shap...  5.09 us
  transfers between devices with their start and end apart: 18, of which 12 were waited for; matrix products, arithmetic and copies ran while one was open for 3% of the time, Pallas kernels for 9%

profile of v21, /device:TPU:0, one launch (start us, length us, event | category | flops | bytes accessed | tf_op | source)
XLA Modules:
  0.0 53.7 jit_solution(12954490906660268745)
XLA Ops:
  0.0 1.0 %shard_map.100 = bf16[4,7296]{1,0:T(4,128)(2,1)S(1)} custom-call(bf16[4,7168]{1,0:T(4,128)(2,1)} %bitcast.70, s32[4,8]{1,0:T(4,128)} %bitcast.71, s32[4,8]{1,0:T(4,128)} %bitcast.72), custom_call_target="tpu_custom_call" | custom-call | flops 20000000000 | bytes 114688 | tf_op jit(solution)/shard_map/pallas_call | solution.py:75
  1.0 5.1 %collective-permute-start.2 = (bf16[4,7296]{1,0:T(4,128)(2,1)S(1)}, bf16[4,7296]{1,0:T(4,128)(2,1)S(1)}, u32[]{:S(2)}, u32[]{:S(2)}) collective-permute-start(bf16[4,7296]{1,0:T(4,128)(2,1)S(1)} %shard_map.100), channel_id=1, source_target_pairs={{0,12},{1,13},{2,14},{3,15},{4,8},{5,9},{6,10},{7,11},{8,4},{9,5},... | collective-permute-start | bytes 175112 | tf_op jit(solution)/shard_map/ppermute | solution.py:37
  6.1 0.6 %collective-permute-start = (bf16[4,7296]{1,0:T(4,128)(2,1)S(1)}, bf16[4,7296]{1,0:T(4,128)(2,1)S(1)}, u32[]{:S(2)}, u32[]{:S(2)}) collective-permute-start(bf16[4,7296]{1,0:T(4,128)(2,1)S(1)} %shard_map.100), channel_id=1, source_target_pairs={{0,8},{1,9},{2,10},{3,11},{4,12},{5,13},{6,14},{7,15},{8,0},{9,1},... | collective-permute-start | bytes 175112 | tf_op jit(solution)/shard_map/ppermute | solution.py:37
  6.7 1.6 %collective-permute-start.3 = (bf16[4,7296]{1,0:T(4,128)(2,1)S(1)}, bf16[4,7296]{1,0:T(4,128)(2,1)S(1)}, u32[]{:S(2)}, u32[]{:S(2)}) collective-permute-start(bf16[4,7296]{1,0:T(4,128)(2,1)S(1)} %shard_map.100), channel_id=1, source_target_pairs={{0,2},{1,3},{2,0},{3,1},{4,6},{5,7},{6,4},{7,5},{8,10},{9,11},{10,... | collective-permute-start | bytes 175112 | tf_op jit(solution)/shard_map/ppermute | solution.py:37
  8.4 0.4 collective-permute-done.2
  8.8 1.7 %collective-permute-done.1 = bf16[4,7296]{1,0:T(4,128)(2,1)S(1)} collective-permute-done((bf16[4,7296]{1,0:T(4,128)(2,1)S(1)}, bf16[4,7296]{1,0:T(4,128)(2,1)S(1)}, u32[]{:S(2)}, u32[]{:S(2)}) %collective-permute-start.1) | collective-permute-done | bytes 58400 | tf_op jit(solution)/shard_map/ppermute | solution.py:37
  10.4 1.1 %collective-permute-done = bf16[4,7296]{1,0:T(4,128)(2,1)S(1)} collective-permute-done((bf16[4,7296]{1,0:T(4,128)(2,1)S(1)}, bf16[4,7296]{1,0:T(4,128)(2,1)S(1)}, u32[]{:S(2)}, u32[]{:S(2)}) %collective-permute-start) | collective-permute-done | bytes 58400 | tf_op jit(solution)/shard_map/ppermute | solution.py:37
  11.6 0.1 pad_maximum_fusion.2
  11.7 1.6 %collective-permute-start.4 = (bf16[12,7296]{1,0:T(8,128)(2,1)S(1)}, bf16[12,7296]{1,0:T(8,128)(2,1)S(1)}, u32[]{:S(2)}, u32[]{:S(2)}) collective-permute-start(bf16[12,7296]{1,0:T(8,128)(2,1)S(1)} %pad_maximum_fusion.2), channel_id=1, source_target_pairs={{0,2},{1,3},{2,0},{3,1},{4,6},{5,7},{6,4},{7,5},{8,10},{9,11},{10,... | collective-permute-start | bytes 525320 | tf_op jit(solution)/shard_map/ppermute | solution.py:37
  13.3 4.6 %collective-permute-done.4 = bf16[12,7296]{1,0:T(8,128)(2,1)S(1)} collective-permute-done((bf16[12,7296]{1,0:T(8,128)(2,1)S(1)}, bf16[12,7296]{1,0:T(8,128)(2,1)S(1)}, u32[]{:S(2)}, u32[]{:S(2)}) %collective-permute-start.4) | collective-permute-done | bytes 175136 | tf_op jit(solution)/shard_map/ppermute | solution.py:37
  17.8 0.2 broadcast_select_fusion.3
  18.1 0.1 collective-permute-start.5
  18.2 1.7 %collective-permute-done.5 = bf16[32,7296]{1,0:T(8,128)(2,1)S(1)} collective-permute-done((bf16[32,7296]{1,0:T(8,128)(2,1)S(1)}, bf16[32,7296]{1,0:T(8,128)(2,1)S(1)}, u32[]{:S(2)}, u32[]{:S(2)}) %collective-permute-start.5) | collective-permute-done | bytes 466976 | tf_op jit(solution)/shard_map/ppermute | solution.py:37
  20.0 0.2 broadcast_select_fusion.1
  20.1 0.1 pad_maximum_fusion.x
  20.2 0.2 convert_reduce_fusion
  20.4 0.5 convolution_convert_fusion.1
  20.9 1.3 %collective-permute-start.8 = (bf16[64,128]{1,0:T(8,128)(2,1)S(1)}, bf16[64,128]{1,0:T(8,128)(2,1)S(1)}, u32[]{:S(2)}, u32[]{:S(2)}) collective-permute-start(bf16[64,128]{1,0:T(8,128)(2,1)S(1)} %convolution_convert_fusion.1), channel_id=1, source_target_pairs={{0,3},{1,2},{2,1},{3,0},{4,7},{5,6},{6,5},{7,4},{8,11},{9,10},{10,... | collective-permute-start | bytes 49160 | tf_op jit(solution)/shard_map/ppermute | solution.py:37
  22.2 0.5 collective-permute-start.7
  22.7 0.1 collective-permute-start.6
  22.8 0.1 fusion.24
  23.0 5.1 %shard_map.101 = f32[128,256]{1,0:T(8,128)S(1)} custom-call(bf16[64,7296]{1,0:T(8,128)(2,1)S(1)} %pad_maximum_fusion.x, bf16[7168,2,256]{2,1,0:T(2,128)(2,1)} %bitcast.62), custom_call_target="tpu_custom_call" | custom-call | flops 469762048 | bytes 7340032 | tf_op jit(solution)/shard_map/pallas_call | solution.py:120
  28.2 0.1 select_reduce_fusion
  28.3 0.1 select_reduce_fusion.1
  28.4 0.2 fusion.5
  28.6 0.1 multiply_reduce_fusion
  28.8 0.3 copy-done.4
  29.1 0.2 convolution_convert_fusion
  29.3 0.5 collective-permute-start.9
  29.8 0.9 %collective-permute-done.9 = bf16[2,64,128]{2,1,0:T(8,128)(2,1)S(1)} collective-permute-done((bf16[2,64,128]{2,1,0:T(8,128)(2,1)S(1)}, bf16[2,64,128]{2,1,0:T(8,128)(2,1)S(1)}, u32[]{:S(2)}, u32[]{:S(2)}) %collective-permute-start.9) | collective-permute-done | bytes 32800 | tf_op jit(solution)/shard_map/ppermute | solution.py:37
  30.7 1.6 %collective-permute-start.10 = (bf16[64,128]{1,0:T(8,128)(2,1)S(1)}, bf16[64,128]{1,0:T(8,128)(2,1)S(1)}, u32[]{:S(2)}, u32[]{:S(2)}) collective-permute-start(bf16[64,128]{1,0:T(8,128)(2,1)S(1)} %dynamic-slice_bitcast_fusion.1), channel_id=1, source_target_pairs={{0,2},{1,3},{2,0},{3,1},{4,6},{5,7},{6,4},{7,5},{8,10},{9,11},{10,... | collective-permute-start | bytes 49160 | tf_op jit(solution)/shard_map/ppermute | solution.py:37
  32.3 0.8 %fusion.1 = f32[64,7168]{1,0:T(8,128)S(1)} fusion(bf16[1,256,7168]{2,1,0:T(8,128)(2,1)S(1)} %copy-done.1, bf16[64,256]{1,0:T(8,128)(2,1)S(1)} %get-tuple-element.21), kind=kOutput, calls=%fused_computation.2 | convolution fusion | flops 234881024 | bytes 5537792 | tf_op jit(solution)/shard_map/dot_general | solution.py:256
  33.0 1.5 %collective-permute-done.10 = bf16[64,128]{1,0:T(8,128)(2,1)S(1)} collective-permute-done((bf16[64,128]{1,0:T(8,128)(2,1)S(1)}, bf16[64,128]{1,0:T(8,128)(2,1)S(1)}, u32[]{:S(2)}, u32[]{:S(2)}) %collective-permute-start.10) | collective-permute-done | bytes 16416 | tf_op jit(solution)/shard_map/ppermute | solution.py:37
  34.5 0.5 fusion.term
  35.0 0.1 collective-permute-start.11
  35.1 1.8 %collective-permute-done.11.received = bf16[32,7168]{1,0:T(8,128)(2,1)S(1)} collective-permute-done((bf16[32,7168]{1,0:T(8,128)(2,1)S(1)}, bf16[32,7168]{1,0:T(8,128)(2,1)S(1)}, u32[]{:S(2)}, u32[]{:S(2)}) %collective-permute-start.11) | collective-permute-done | bytes 458784 | tf_op jit(solution)/shard_map/ppermute | solution.py:37
  36.9 0.2 shard_map.102
  37.1 1.6 %collective-permute-start.12 = (bf16[16,3584]{1,0:T(8,128)(2,1)S(1)}, bf16[16,3584]{1,0:T(8,128)(2,1)S(1)}, u32[]{:S(2)}, u32[]{:S(2)}) collective-permute-start(bf16[16,3584]{1,0:T(8,128)(2,1)S(1)} %get-tuple-element.18), channel_id=1, source_target_pairs={{0,2},{1,5},{2,0},{3,7},{4,6},{5,1},{6,4},{7,3},{8,10},{9,13},{10,... | collective-permute-start | bytes 344072 | tf_op jit(solution)/shard_map/ppermute | solution.py:37
  38.6 0.5 collective-permute-start.15
  39.2 2.8 %collective-permute-done.12 = bf16[16,3584]{1,0:T(8,128)(2,1)S(1)} collective-permute-done((bf16[16,3584]{1,0:T(8,128)(2,1)S(1)}, bf16[16,3584]{1,0:T(8,128)(2,1)S(1)}, u32[]{:S(2)}, u32[]{:S(2)}) %collective-permute-start.12) | collective-permute-done | bytes 114720 | tf_op jit(solution)/shard_map/ppermute | solution.py:37
  42.0 1.7 %collective-permute-start.13 = (bf16[8,3584]{1,0:T(8,128)(2,1)S(1)}, bf16[8,3584]{1,0:T(8,128)(2,1)S(1)}, u32[]{:S(2)}, u32[]{:S(2)}) collective-permute-start(bf16[8,3584]{1,0:T(8,128)(2,1)S(1)} %broadcast_select_fusion.5), channel_id=1, source_target_pairs={{0,4},{1,3},{2,6},{3,1},{4,0},{5,7},{6,2},{7,5},{8,12},{9,11},{10,... | collective-permute-start | bytes 172040 | tf_op jit(solution)/shard_map/ppermute | solution.py:37
  43.7 1.4 %collective-permute-start.16 = (bf16[8,3584]{1,0:T(8,128)(2,1)S(1)}, bf16[8,3584]{1,0:T(8,128)(2,1)S(1)}, u32[]{:S(2)}, u32[]{:S(2)}) collective-permute-start(bf16[8,3584]{1,0:T(8,128)(2,1)S(1)} %broadcast_select_fusion.4), channel_id=1, source_target_pairs={{0,4},{1,3},{2,6},{3,1},{4,0},{5,7},{6,2},{7,5},{8,12},{9,11},{10,... | collective-permute-start | bytes 172040 | tf_op jit(solution)/shard_map/ppermute | solution.py:37
  45.2 1.1 %collective-permute-done.13 = bf16[8,3584]{1,0:T(8,128)(2,1)S(1)} collective-permute-done((bf16[8,3584]{1,0:T(8,128)(2,1)S(1)}, bf16[8,3584]{1,0:T(8,128)(2,1)S(1)}, u32[]{:S(2)}, u32[]{:S(2)}) %collective-permute-start.13) | collective-permute-done | bytes 57376 | tf_op jit(solution)/shard_map/ppermute | solution.py:37
  46.3 1.9 %collective-permute-start.14 = (bf16[4,3584]{1,0:T(4,128)(2,1)S(1)}, bf16[4,3584]{1,0:T(4,128)(2,1)S(1)}, u32[]{:S(2)}, u32[]{:S(2)}) collective-permute-start(bf16[4,3584]{1,0:T(4,128)(2,1)S(1)} %slice.91), channel_id=1, source_target_pairs={{0,8},{1,9},{2,10},{3,11},{4,12},{5,13},{6,14},{7,15},{8,0},{9,1},... | collective-permute-start | bytes 86024 | tf_op jit(solution)/shard_map/ppermute | solution.py:37
  48.2 2.1 %collective-permute-start.17 = (bf16[4,3584]{1,0:T(4,128)(2,1)S(1)}, bf16[4,3584]{1,0:T(4,128)(2,1)S(1)}, u32[]{:S(2)}, u32[]{:S(2)}) collective-permute-start(bf16[4,3584]{1,0:T(4,128)(2,1)S(1)} %slice.95), channel_id=1, source_target_pairs={{0,8},{1,9},{2,10},{3,11},{4,12},{5,13},{6,14},{7,15},{8,0},{9,1},... | collective-permute-start | bytes 86024 | tf_op jit(solution)/shard_map/ppermute | solution.py:37
  50.3 1.1 %collective-permute-done.14 = bf16[4,3584]{1,0:T(4,128)(2,1)S(1)} collective-permute-done((bf16[4,3584]{1,0:T(4,128)(2,1)S(1)}, bf16[4,3584]{1,0:T(4,128)(2,1)S(1)}, u32[]{:S(2)}, u32[]{:S(2)}) %collective-permute-start.14) | collective-permute-done | bytes 28704 | tf_op jit(solution)/shard_map/ppermute | solution.py:37
  51.4 1.7 %collective-permute-done.17 = bf16[4,3584]{1,0:T(4,128)(2,1)S(1)} collective-permute-done((bf16[4,3584]{1,0:T(4,128)(2,1)S(1)}, bf16[4,3584]{1,0:T(4,128)(2,1)S(1)}, u32[]{:S(2)}, u32[]{:S(2)}) %collective-permute-start.17) | collective-permute-done | bytes 28704 | tf_op jit(solution)/shard_map/ppermute | solution.py:37
  53.1 0.7 %maximum_bitcast_fusion.2 = bf16[1,4,7168]{2,1,0:T(4,128)(2,1)} fusion(bf16[4,3584]{1,0:T(4,128)(2,1)S(1)} %add_convert_fusion.4, bf16[4,3584]{1,0:T(4,128)(2,1)S(1)} %add_convert_fusion.5), kind=kLoop, calls=%fused_computation.44 | loop fusion | flops 114688 | bytes 114688 | tf_op jit(solution)/shard_map/broadcast_in_dim | solution.py:282
  (41 shorter events, 0.6 us)
Async XLA Ops:
  0.0 20.2 %copy-start = (bf16[1,7168,128]{2,1,0:T(8,128)(2,1)S(1)}, bf16[1,7168,128]{2,1,0:T(8,128)(2,1)}, u32[]{:S(2)}) copy-start(bf16[1,7168,128]{2,1,0:T(8,128)(2,1)} %param.16) | copy-start | bytes 5505028
  1.0 7.8 %collective-permute-start.2 = (bf16[4,7296]{1,0:T(4,128)(2,1)S(1)}, bf16[4,7296]{1,0:T(4,128)(2,1)S(1)}, u32[]{:S(2)}, u32[]{:S(2)}) collective-permute-start(bf16[4,7296]{1,0:T(4,128)(2,1)S(1)} %shard_map.100), channel_id=1, source_target_pairs={{0,12},{1,13},{2,14},{3,15},{4,8},{5,9},{6,10},{7,11},{8,4},{9,5},... | collective-permute-start | bytes 175112 | tf_op jit(solution)/shard_map/ppermute | solution.py:37
  6.1 4.3 %collective-permute-start.1 = (bf16[4,7296]{1,0:T(4,128)(2,1)S(1)}, bf16[4,7296]{1,0:T(4,128)(2,1)S(1)}, u32[]{:S(2)}, u32[]{:S(2)}) collective-permute-start(bf16[4,7296]{1,0:T(4,128)(2,1)S(1)} %shard_map.100), channel_id=1, source_target_pairs={{0,4},{1,5},{2,6},{3,7},{4,0},{5,1},{6,2},{7,3},{8,12},{9,13},{10,... | collective-permute-start | bytes 175112 | tf_op jit(solution)/shard_map/ppermute | solution.py:37
  6.1 5.5 %collective-permute-start = (bf16[4,7296]{1,0:T(4,128)(2,1)S(1)}, bf16[4,7296]{1,0:T(4,128)(2,1)S(1)}, u32[]{:S(2)}, u32[]{:S(2)}) collective-permute-start(bf16[4,7296]{1,0:T(4,128)(2,1)S(1)} %shard_map.100), channel_id=1, source_target_pairs={{0,8},{1,9},{2,10},{3,11},{4,12},{5,13},{6,14},{7,15},{8,0},{9,1},... | collective-permute-start | bytes 175112 | tf_op jit(solution)/shard_map/ppermute | solution.py:37
  6.7 4.9 %collective-permute-start.3 = (bf16[4,7296]{1,0:T(4,128)(2,1)S(1)}, bf16[4,7296]{1,0:T(4,128)(2,1)S(1)}, u32[]{:S(2)}, u32[]{:S(2)}) collective-permute-start(bf16[4,7296]{1,0:T(4,128)(2,1)S(1)} %shard_map.100), channel_id=1, source_target_pairs={{0,2},{1,3},{2,0},{3,1},{4,6},{5,7},{6,4},{7,5},{8,10},{9,11},{10,... | collective-permute-start | bytes 175112 | tf_op jit(solution)/shard_map/ppermute | solution.py:37
  11.7 6.1 %collective-permute-start.4 = (bf16[12,7296]{1,0:T(8,128)(2,1)S(1)}, bf16[12,7296]{1,0:T(8,128)(2,1)S(1)}, u32[]{:S(2)}, u32[]{:S(2)}) collective-permute-start(bf16[12,7296]{1,0:T(8,128)(2,1)S(1)} %pad_maximum_fusion.2), channel_id=1, source_target_pairs={{0,2},{1,3},{2,0},{3,1},{4,6},{5,7},{6,4},{7,5},{8,10},{9,11},{10,... | collective-permute-start | bytes 525320 | tf_op jit(solution)/shard_map/ppermute | solution.py:37
  18.1 1.9 %collective-permute-start.5 = (bf16[32,7296]{1,0:T(8,128)(2,1)S(1)}, bf16[32,7296]{1,0:T(8,128)(2,1)S(1)}, u32[]{:S(2)}, u32[]{:S(2)}) collective-permute-start(bf16[32,7296]{1,0:T(8,128)(2,1)S(1)} %pad_maximum_fusion.1), channel_id=1, source_target_pairs={{0,1},{1,0},{2,3},{3,2},{4,5},{5,4},{6,7},{7,6},{8,9},{9,8},{10,11... | collective-permute-start | bytes 1400840 | tf_op jit(solution)/shard_map/ppermute | solution.py:37
  20.9 7.5 %collective-permute-start.8 = (bf16[64,128]{1,0:T(8,128)(2,1)S(1)}, bf16[64,128]{1,0:T(8,128)(2,1)S(1)}, u32[]{:S(2)}, u32[]{:S(2)}) collective-permute-start(bf16[64,128]{1,0:T(8,128)(2,1)S(1)} %convolution_convert_fusion.1), channel_id=1, source_target_pairs={{0,3},{1,2},{2,1},{3,0},{4,7},{5,6},{6,5},{7,4},{8,11},{9,10},{10,... | collective-permute-start | bytes 49160 | tf_op jit(solution)/shard_map/ppermute | solution.py:37
  22.2 6.2 %collective-permute-start.7 = (bf16[64,128]{1,0:T(8,128)(2,1)S(1)}, bf16[64,128]{1,0:T(8,128)(2,1)S(1)}, u32[]{:S(2)}, u32[]{:S(2)}) collective-permute-start(bf16[64,128]{1,0:T(8,128)(2,1)S(1)} %convolution_convert_fusion.1), channel_id=1, source_target_pairs={{0,2},{1,3},{2,0},{3,1},{4,6},{5,7},{6,4},{7,5},{8,10},{9,11},{10,... | collective-permute-start | bytes 49160 | tf_op jit(solution)/shard_map/ppermute | solution.py:37
  22.7 5.6 %collective-permute-start.6 = (bf16[64,128]{1,0:T(8,128)(2,1)S(1)}, bf16[64,128]{1,0:T(8,128)(2,1)S(1)}, u32[]{:S(2)}, u32[]{:S(2)}) collective-permute-start(bf16[64,128]{1,0:T(8,128)(2,1)S(1)} %convolution_convert_fusion.1), channel_id=1, source_target_pairs={{0,1},{1,0},{2,3},{3,2},{4,5},{5,4},{6,7},{7,6},{8,9},{9,8},{10,11... | collective-permute-start | bytes 49160 | tf_op jit(solution)/shard_map/ppermute | solution.py:37
  23.0 5.1 %copy-start.5 = (s32[16]{0:T(128)S(1)}, s32[16]{0:T(128)}, u32[]{:S(2)}) copy-start(s32[16]{0:T(128)} %param.13) | copy-start | bytes 196
  23.0 5.4 %copy-start.3 = (bf16[1,4,128,2,256]{4,3,2,1,0:T(2,128)(2,1)S(1)}, bf16[1,4,128,2,256]{4,3,2,1,0:T(2,128)(2,1)}, u32[]{:S(2)}) copy-start(bf16[1,4,128,2,256]{4,3,2,1,0:T(2,128)(2,1)} %param.17) | copy-start | bytes 1572868
  23.0 9.2 %copy-start.1 = (bf16[1,256,7168]{2,1,0:T(8,128)(2,1)S(1)}, bf16[1,256,7168]{2,1,0:T(8,128)(2,1)}, u32[]{:S(2)}) copy-start(bf16[1,256,7168]{2,1,0:T(8,128)(2,1)} %param.15) | copy-start | bytes 11010052
  28.1 1.0 %copy-start.4 = (bf16[1,4,256,128]{3,2,1,0:T(8,128)(2,1)S(1)}, bf16[1,4,256,128]{3,2,1,0:T(8,128)(2,1)}, u32[]{:S(2)}) copy-start(bf16[1,4,256,128]{3,2,1,0:T(8,128)(2,1)} %param.18) | copy-start | bytes 786436
  29.3 1.4 %collective-permute-start.9 = (bf16[2,64,128]{2,1,0:T(8,128)(2,1)S(1)}, bf16[2,64,128]{2,1,0:T(8,128)(2,1)S(1)}, u32[]{:S(2)}, u32[]{:S(2)}) collective-permute-start(bf16[2,64,128]{2,1,0:T(8,128)(2,1)S(1)} %dynamic-slice_bitcast_fusion), channel_id=1, source_target_pairs={{0,1},{1,0},{2,3},{3,2},{4,5},{5,4},{6,7},{7,6},{8,9},{9,8},{10,11... | collective-permute-start | bytes 98312 | tf_op jit(solution)/shard_map/ppermute | solution.py:37
  30.7 3.8 %collective-permute-start.10 = (bf16[64,128]{1,0:T(8,128)(2,1)S(1)}, bf16[64,128]{1,0:T(8,128)(2,1)S(1)}, u32[]{:S(2)}, u32[]{:S(2)}) collective-permute-start(bf16[64,128]{1,0:T(8,128)(2,1)S(1)} %dynamic-slice_bitcast_fusion.1), channel_id=1, source_target_pairs={{0,2},{1,3},{2,0},{3,1},{4,6},{5,7},{6,4},{7,5},{8,10},{9,11},{10,... | collective-permute-start | bytes 49160 | tf_op jit(solution)/shard_map/ppermute | solution.py:37
  32.2 2.2 %copy-start.2 = (bf16[1,128,7168]{2,1,0:T(8,128)(2,1)S(1)}, bf16[1,128,7168]{2,1,0:T(8,128)(2,1)}, u32[]{:S(2)}) copy-start(bf16[1,128,7168]{2,1,0:T(8,128)(2,1)} %param.19) | copy-start | bytes 5505028
  35.0 1.9 %collective-permute-start.11 = (bf16[32,7168]{1,0:T(8,128)(2,1)S(1)}, bf16[32,7168]{1,0:T(8,128)(2,1)S(1)}, u32[]{:S(2)}, u32[]{:S(2)}) collective-permute-start(bf16[32,7168]{1,0:T(8,128)(2,1)S(1)} %slice_select_fusion), channel_id=1, source_target_pairs={{0,1},{1,0},{2,3},{3,2},{4,5},{5,4},{6,7},{7,6},{8,9},{9,8},{10,11... | collective-permute-start | bytes 1376264 | tf_op jit(solution)/shard_map/ppermute | solution.py:37
  37.1 4.9 %collective-permute-start.12 = (bf16[16,3584]{1,0:T(8,128)(2,1)S(1)}, bf16[16,3584]{1,0:T(8,128)(2,1)S(1)}, u32[]{:S(2)}, u32[]{:S(2)}) collective-permute-start(bf16[16,3584]{1,0:T(8,128)(2,1)S(1)} %get-tuple-element.18), channel_id=1, source_target_pairs={{0,2},{1,5},{2,0},{3,7},{4,6},{5,1},{6,4},{7,3},{8,10},{9,13},{10,... | collective-permute-start | bytes 344072 | tf_op jit(solution)/shard_map/ppermute | solution.py:37
  38.6 5.0 %collective-permute-start.15 = (bf16[16,3584]{1,0:T(8,128)(2,1)S(1)}, bf16[16,3584]{1,0:T(8,128)(2,1)S(1)}, u32[]{:S(2)}, u32[]{:S(2)}) collective-permute-start(bf16[16,3584]{1,0:T(8,128)(2,1)S(1)} %get-tuple-element.20), channel_id=1, source_target_pairs={{0,2},{1,5},{2,0},{3,7},{4,6},{5,1},{6,4},{7,3},{8,10},{9,13},{10,... | collective-permute-start | bytes 344072 | tf_op jit(solution)/shard_map/ppermute | solution.py:37
  42.0 4.2 %collective-permute-start.13 = (bf16[8,3584]{1,0:T(8,128)(2,1)S(1)}, bf16[8,3584]{1,0:T(8,128)(2,1)S(1)}, u32[]{:S(2)}, u32[]{:S(2)}) collective-permute-start(bf16[8,3584]{1,0:T(8,128)(2,1)S(1)} %broadcast_select_fusion.5), channel_id=1, source_target_pairs={{0,4},{1,3},{2,6},{3,1},{4,0},{5,7},{6,2},{7,5},{8,12},{9,11},{10,... | collective-permute-start | bytes 172040 | tf_op jit(solution)/shard_map/ppermute | solution.py:37
  43.7 4.4 %collective-permute-start.16 = (bf16[8,3584]{1,0:T(8,128)(2,1)S(1)}, bf16[8,3584]{1,0:T(8,128)(2,1)S(1)}, u32[]{:S(2)}, u32[]{:S(2)}) collective-permute-start(bf16[8,3584]{1,0:T(8,128)(2,1)S(1)} %broadcast_select_fusion.4), channel_id=1, source_target_pairs={{0,4},{1,3},{2,6},{3,1},{4,0},{5,7},{6,2},{7,5},{8,12},{9,11},{10,... | collective-permute-start | bytes 172040 | tf_op jit(solution)/shard_map/ppermute | solution.py:37
  46.3 5.1 %collective-permute-start.14 = (bf16[4,3584]{1,0:T(4,128)(2,1)S(1)}, bf16[4,3584]{1,0:T(4,128)(2,1)S(1)}, u32[]{:S(2)}, u32[]{:S(2)}) collective-permute-start(bf16[4,3584]{1,0:T(4,128)(2,1)S(1)} %slice.91), channel_id=1, source_target_pairs={{0,8},{1,9},{2,10},{3,11},{4,12},{5,13},{6,14},{7,15},{8,0},{9,1},... | collective-permute-start | bytes 86024 | tf_op jit(solution)/shard_map/ppermute | solution.py:37
  48.2 4.8 %collective-permute-start.17 = (bf16[4,3584]{1,0:T(4,128)(2,1)S(1)}, bf16[4,3584]{1,0:T(4,128)(2,1)S(1)}, u32[]{:S(2)}, u32[]{:S(2)}) collective-permute-start(bf16[4,3584]{1,0:T(4,128)(2,1)S(1)} %slice.95), channel_id=1, source_target_pairs={{0,8},{1,9},{2,10},{3,11},{4,12},{5,13},{6,14},{7,15},{8,0},{9,1},... | collective-permute-start | bytes 86024 | tf_op jit(solution)/shard_map/ppermute | solution.py:37

commit v22 on v20

--- a/solution.py
+++ b/solution.py
@@ -122,30 +122,6 @@
             flops=4 * x.shape[0] * depth * columns, bytes_accessed=2 * base.size, transcendentals=0
         ),
     )(x, base)
-
-
-def down_kernel(hidden, base, out, weights, sems):
-    step = base.shape[1] // sems.shape[0]
-    parts = [pl.ds(k * step, step) for k in range(sems.shape[0])]
-    copies = [pltpu.make_async_copy(base.at[:, part], weights.at[:, part], sems.at[k]) for k, part in enumerate(parts)]
-    for copy in copies:
-        copy.start()
-    for copy, part in zip(copies, parts):
-        copy.wait()
-        out[:, part] = jnp.dot(hidden[...], weights[:, part], preferred_element_type=jnp.float32)
-
-
-def down_product(hidden, base):
-    rows, width = hidden.shape[0], base.shape[1]
-    return pl.pallas_call(
-        down_kernel,
-        out_shape=jax.ShapeDtypeStruct((rows, width), jnp.float32),
-        in_specs=[VMEM, HBM],
-        out_specs=VMEM,
-        scratch_shapes=[pltpu.VMEM(base.shape, base.dtype), pltpu.SemaphoreType.DMA((width // 1024,))],
-        compiler_params=pltpu.CompilerParams(vmem_limit_bytes=16 << 20),
-        cost_estimate=pl.CostEstimate(flops=2 * rows * base.size, bytes_accessed=2 * base.size, transcendentals=0),
-    )(hidden, in_hbm(base))
 
 
 def part_kernel(bit, term, received, *refs):
@@ -235,8 +211,9 @@
                 runs[x, zs], runs[x | bit, zs] = ordered(flag, runs[x, zs], runs[x | bit, zs])
     held = by_rows(jnp.concatenate([runs[segment] for segment in segments]))
     held = by_rows(jnp.concatenate(ordered(core == 1, held, trade(held, (0, 1), (0, 1)))))
-
-    codes = jnp.dot(held[:, :width], delta_in[0], preferred_element_type=jnp.float32).astype(jnp.bfloat16)
+    _, code_table = lax.optimization_barrier((held, delta_in[0]))
+
+    codes = jnp.dot(held[:, :width], code_table, preferred_element_type=jnp.float32).astype(jnp.bfloat16)
     projected = gate_up_product(held, base_in[0])
 
     side = by_rows(held[:, width:])
@@ -270,7 +247,7 @@
     own_scale = lax.dynamic_index_in_dim(scale, me, 0, keepdims=False)
     scaled = (own_scale[:, None] * lowrank).astype(jnp.bfloat16)
 
-    term = down_product(hidden_sum, base_down[0])
+    term = jnp.dot(hidden_sum, base_down[0], preferred_element_type=jnp.float32)
     term = (term + jnp.dot(scaled, delta_back[0], preferred_element_type=jnp.float32)).astype(jnp.bfloat16)
 
     half = term.shape[0] // 2

time: 55.2 us -> 54.9 us (level)
  Pallas kernels: 6.69 us -> 4.12 us
  waiting for transfers between devices: 19 us -> 20.2 us
  matrix products: 1.31 us -> 2.06 us
    pallas_call x1 -> x0, Pallas kernels: 2.57 us -> none  [down_product(): pl.pallas_call(down_kernel, out_shape=jax.ShapeDtypeStruct((rows, width),...]
    ppermute x18, waiting for transfers between devices: 19 us -> 20.2 us  [trade(): return lax.ppermute(value, ('expert', 'tensor'), pairs)]
    dot_general x1 -> x2, matrix products: 0.46 us -> 1.22 us  [the longest x1 0.75 us: local(): term = jnp.dot(hidden_sum, base_down[0], preferred_element_type=jnp.float32)]
    unnamed x12 -> x14, local copies, waits for them, and re-layouts: 3.45 us -> 3.45 us
  transfers between devices with their start and end apart: 18 -> 18, of which waited for: 11 -> 12; matrix products, arithmetic and copies ran while one was open for 1% -> 3% of each run, Pallas kernels for 10% -> 5%
where the time goes in v22:
time: 54.9 us; the launch traced here: 54.7 us
  starting transfers between devices  22.2 us (40%)
  waiting for transfers between devices  20.2 us (37%)
  Pallas kernels  4.12 us (8%)
  local copies, waits for them, and re-layouts  3.66 us (7%)
  matrix products  2.06 us (4%)
  other arithmetic  2.03 us (4%)
    ppermute x18, starting transfers between devices, trade(): return lax.ppermute(value, ('expert', 'tensor'), pairs)  22.2 us
    ppermute x18, waiting for transfers between devices, trade(): return lax.ppermute(value, ('expert', 'tensor'), pairs)  20.2 us
    unnamed x14, local copies, waits for them, and re-layouts  3.45 us
    pallas_call x1, Pallas kernels, gate_up_product(): pl.pallas_call(gate_up_kernel, out_shape=jax.ShapeDtypeStruct((2 * x.shap...  2.96 us
  transfers between devices with their start and end apart: 18, of which 12 were waited for; matrix products, arithmetic and copies ran while one was open for 3% of the time, Pallas kernels for 5%

profile of v22, /device:TPU:0, one launch (start us, length us, event | category | flops | bytes accessed | tf_op | source)
XLA Modules:
  0.0 54.7 jit_solution(18161543502800395138)
XLA Ops:
  0.0 1.0 %shard_map.100 = bf16[4,7296]{1,0:T(4,128)(2,1)S(1)} custom-call(bf16[4,7168]{1,0:T(4,128)(2,1)} %bitcast.70, s32[4,8]{1,0:T(4,128)} %bitcast.71, s32[4,8]{1,0:T(4,128)} %bitcast.72), custom_call_target="tpu_custom_call" | custom-call | flops 20000000000 | bytes 114688 | tf_op jit(solution)/shard_map/pallas_call | solution.py:75
  1.0 5.1 %collective-permute-start.2 = (bf16[4,7296]{1,0:T(4,128)(2,1)S(1)}, bf16[4,7296]{1,0:T(4,128)(2,1)S(1)}, u32[]{:S(2)}, u32[]{:S(2)}) collective-permute-start(bf16[4,7296]{1,0:T(4,128)(2,1)S(1)} %shard_map.100), channel_id=1, source_target_pairs={{0,12},{1,13},{2,14},{3,15},{4,8},{5,9},{6,10},{7,11},{8,4},{9,5},... | collective-permute-start | bytes 175112 | tf_op jit(solution)/shard_map/ppermute | solution.py:37
  6.1 0.6 %collective-permute-start = (bf16[4,7296]{1,0:T(4,128)(2,1)S(1)}, bf16[4,7296]{1,0:T(4,128)(2,1)S(1)}, u32[]{:S(2)}, u32[]{:S(2)}) collective-permute-start(bf16[4,7296]{1,0:T(4,128)(2,1)S(1)} %shard_map.100), channel_id=1, source_target_pairs={{0,8},{1,9},{2,10},{3,11},{4,12},{5,13},{6,14},{7,15},{8,0},{9,1},... | collective-permute-start | bytes 175112 | tf_op jit(solution)/shard_map/ppermute | solution.py:37
  6.7 1.6 %collective-permute-start.3 = (bf16[4,7296]{1,0:T(4,128)(2,1)S(1)}, bf16[4,7296]{1,0:T(4,128)(2,1)S(1)}, u32[]{:S(2)}, u32[]{:S(2)}) collective-permute-start(bf16[4,7296]{1,0:T(4,128)(2,1)S(1)} %shard_map.100), channel_id=1, source_target_pairs={{0,2},{1,3},{2,0},{3,1},{4,6},{5,7},{6,4},{7,5},{8,10},{9,11},{10,... | collective-permute-start | bytes 175112 | tf_op jit(solution)/shard_map/ppermute | solution.py:37
  8.4 0.4 collective-permute-done.2
  8.8 1.7 %collective-permute-done.1 = bf16[4,7296]{1,0:T(4,128)(2,1)S(1)} collective-permute-done((bf16[4,7296]{1,0:T(4,128)(2,1)S(1)}, bf16[4,7296]{1,0:T(4,128)(2,1)S(1)}, u32[]{:S(2)}, u32[]{:S(2)}) %collective-permute-start.1) | collective-permute-done | bytes 58400 | tf_op jit(solution)/shard_map/ppermute | solution.py:37
  10.4 1.1 %collective-permute-done = bf16[4,7296]{1,0:T(4,128)(2,1)S(1)} collective-permute-done((bf16[4,7296]{1,0:T(4,128)(2,1)S(1)}, bf16[4,7296]{1,0:T(4,128)(2,1)S(1)}, u32[]{:S(2)}, u32[]{:S(2)}) %collective-permute-start) | collective-permute-done | bytes 58400 | tf_op jit(solution)/shard_map/ppermute | solution.py:37
  11.6 0.1 pad_maximum_fusion.2
  11.7 1.6 %collective-permute-start.4 = (bf16[12,7296]{1,0:T(8,128)(2,1)S(1)}, bf16[12,7296]{1,0:T(8,128)(2,1)S(1)}, u32[]{:S(2)}, u32[]{:S(2)}) collective-permute-start(bf16[12,7296]{1,0:T(8,128)(2,1)S(1)} %pad_maximum_fusion.2), channel_id=1, source_target_pairs={{0,2},{1,3},{2,0},{3,1},{4,6},{5,7},{6,4},{7,5},{8,10},{9,11},{10,... | collective-permute-start | bytes 525320 | tf_op jit(solution)/shard_map/ppermute | solution.py:37
  13.3 4.6 %collective-permute-done.4 = bf16[12,7296]{1,0:T(8,128)(2,1)S(1)} collective-permute-done((bf16[12,7296]{1,0:T(8,128)(2,1)S(1)}, bf16[12,7296]{1,0:T(8,128)(2,1)S(1)}, u32[]{:S(2)}, u32[]{:S(2)}) %collective-permute-start.4) | collective-permute-done | bytes 175136 | tf_op jit(solution)/shard_map/ppermute | solution.py:37
  17.8 0.2 broadcast_select_fusion.3
  18.2 1.7 %collective-permute-done.5 = bf16[32,7296]{1,0:T(8,128)(2,1)S(1)} collective-permute-done((bf16[32,7296]{1,0:T(8,128)(2,1)S(1)}, bf16[32,7296]{1,0:T(8,128)(2,1)S(1)}, u32[]{:S(2)}, u32[]{:S(2)}) %collective-permute-start.5) | collective-permute-done | bytes 466976 | tf_op jit(solution)/shard_map/ppermute | solution.py:37
  20.0 0.2 broadcast_select_fusion.1
  20.1 0.2 convert_reduce_fusion
  20.3 0.1 pad_maximum_fusion.x
  20.4 0.5 convolution_convert_fusion.1
  20.9 1.3 %collective-permute-start.8 = (bf16[64,128]{1,0:T(8,128)(2,1)S(1)}, bf16[64,128]{1,0:T(8,128)(2,1)S(1)}, u32[]{:S(2)}, u32[]{:S(2)}) collective-permute-start(bf16[64,128]{1,0:T(8,128)(2,1)S(1)} %convolution_convert_fusion.1), channel_id=1, source_target_pairs={{0,3},{1,2},{2,1},{3,0},{4,7},{5,6},{6,5},{7,4},{8,11},{9,10},{10,... | collective-permute-start | bytes 49160 | tf_op jit(solution)/shard_map/ppermute | solution.py:37
  22.2 0.5 collective-permute-start.7
  22.7 0.1 collective-permute-start.6
  22.8 0.1 fusion.27
  23.0 3.1 %copy-done.1 = bf16[1,7168,2,256]{3,2,1,0:T(2,128)(2,1)S(1)} copy-done((bf16[1,7168,2,256]{3,2,1,0:T(2,128)(2,1)S(1)}, bf16[1,7168,2,256]{3,2,1,0:T(2,128)(2,1)}, u32[]{:S(2)}) %copy-start.1) | copy-done | bytes 7340056
  26.1 3.0 %shard_map.101 = f32[128,256]{1,0:T(8,128)S(1)} custom-call(bf16[64,7296]{1,0:T(8,128)(2,1)S(1)} %pad_maximum_fusion.x, bf16[7168,2,256]{2,1,0:T(2,128)(2,1)S(1)} %bitcast.62), custom_call_target="tpu_custom_call" | custom-call | flops 469762048 | bytes 7340032 | tf_op jit(solution)/shard_map/pallas_call | solution.py:115
  29.1 0.1 select_reduce_fusion
  29.2 0.1 select_reduce_fusion.1
  29.4 0.2 fusion.6
  29.6 0.1 multiply_reduce_fusion
  29.7 0.3 copy-done.5
  30.1 0.2 convolution_convert_fusion
  30.3 0.5 collective-permute-start.9
  30.8 0.9 %collective-permute-done.9 = bf16[2,64,128]{2,1,0:T(8,128)(2,1)S(1)} collective-permute-done((bf16[2,64,128]{2,1,0:T(8,128)(2,1)S(1)}, bf16[2,64,128]{2,1,0:T(8,128)(2,1)S(1)}, u32[]{:S(2)}, u32[]{:S(2)}) %collective-permute-start.9) | collective-permute-done | bytes 32800 | tf_op jit(solution)/shard_map/ppermute | solution.py:37
  31.6 1.6 %collective-permute-start.10 = (bf16[64,128]{1,0:T(8,128)(2,1)S(1)}, bf16[64,128]{1,0:T(8,128)(2,1)S(1)}, u32[]{:S(2)}, u32[]{:S(2)}) collective-permute-start(bf16[64,128]{1,0:T(8,128)(2,1)S(1)} %dynamic-slice_bitcast_fusion.1), channel_id=1, source_target_pairs={{0,2},{1,3},{2,0},{3,1},{4,6},{5,7},{6,4},{7,5},{8,10},{9,11},{10,... | collective-permute-start | bytes 49160 | tf_op jit(solution)/shard_map/ppermute | solution.py:37
  33.2 0.8 %fusion.1 = f32[64,7168]{1,0:T(8,128)S(1)} fusion(bf16[1,256,7168]{2,1,0:T(8,128)(2,1)S(1)} %copy-done.2, bf16[64,256]{1,0:T(8,128)(2,1)S(1)} %get-tuple-element.19), kind=kOutput, calls=%fused_computation.2 | convolution fusion | flops 234881024 | bytes 5537792 | tf_op jit(solution)/shard_map/dot_general | solution.py:250
  34.0 1.5 %collective-permute-done.10 = bf16[64,128]{1,0:T(8,128)(2,1)S(1)} collective-permute-done((bf16[64,128]{1,0:T(8,128)(2,1)S(1)}, bf16[64,128]{1,0:T(8,128)(2,1)S(1)}, u32[]{:S(2)}, u32[]{:S(2)}) %collective-permute-start.10) | collective-permute-done | bytes 16416 | tf_op jit(solution)/shard_map/ppermute | solution.py:37
  35.4 0.5 fusion.term
  36.0 0.1 collective-permute-start.11
  36.0 1.8 %collective-permute-done.11.received = bf16[32,7168]{1,0:T(8,128)(2,1)S(1)} collective-permute-done((bf16[32,7168]{1,0:T(8,128)(2,1)S(1)}, bf16[32,7168]{1,0:T(8,128)(2,1)S(1)}, u32[]{:S(2)}, u32[]{:S(2)}) %collective-permute-start.11) | collective-permute-done | bytes 458784 | tf_op jit(solution)/shard_map/ppermute | solution.py:37
  37.9 0.2 shard_map.102
  38.0 1.6 %collective-permute-start.12 = (bf16[16,3584]{1,0:T(8,128)(2,1)S(1)}, bf16[16,3584]{1,0:T(8,128)(2,1)S(1)}, u32[]{:S(2)}, u32[]{:S(2)}) collective-permute-start(bf16[16,3584]{1,0:T(8,128)(2,1)S(1)} %get-tuple-element.16), channel_id=1, source_target_pairs={{0,2},{1,5},{2,0},{3,7},{4,6},{5,1},{6,4},{7,3},{8,10},{9,13},{10,... | collective-permute-start | bytes 344072 | tf_op jit(solution)/shard_map/ppermute | solution.py:37
  39.6 0.5 collective-permute-start.15
  40.1 2.8 %collective-permute-done.12 = bf16[16,3584]{1,0:T(8,128)(2,1)S(1)} collective-permute-done((bf16[16,3584]{1,0:T(8,128)(2,1)S(1)}, bf16[16,3584]{1,0:T(8,128)(2,1)S(1)}, u32[]{:S(2)}, u32[]{:S(2)}) %collective-permute-start.12) | collective-permute-done | bytes 114720 | tf_op jit(solution)/shard_map/ppermute | solution.py:37
  43.0 1.7 %collective-permute-start.13 = (bf16[8,3584]{1,0:T(8,128)(2,1)S(1)}, bf16[8,3584]{1,0:T(8,128)(2,1)S(1)}, u32[]{:S(2)}, u32[]{:S(2)}) collective-permute-start(bf16[8,3584]{1,0:T(8,128)(2,1)S(1)} %broadcast_select_fusion.5), channel_id=1, source_target_pairs={{0,4},{1,3},{2,6},{3,1},{4,0},{5,7},{6,2},{7,5},{8,12},{9,11},{10,... | collective-permute-start | bytes 172040 | tf_op jit(solution)/shard_map/ppermute | solution.py:37
  44.7 1.4 %collective-permute-start.16 = (bf16[8,3584]{1,0:T(8,128)(2,1)S(1)}, bf16[8,3584]{1,0:T(8,128)(2,1)S(1)}, u32[]{:S(2)}, u32[]{:S(2)}) collective-permute-start(bf16[8,3584]{1,0:T(8,128)(2,1)S(1)} %broadcast_select_fusion.4), channel_id=1, source_target_pairs={{0,4},{1,3},{2,6},{3,1},{4,0},{5,7},{6,2},{7,5},{8,12},{9,11},{10,... | collective-permute-start | bytes 172040 | tf_op jit(solution)/shard_map/ppermute | solution.py:37
  46.1 1.1 %collective-permute-done.13 = bf16[8,3584]{1,0:T(8,128)(2,1)S(1)} collective-permute-done((bf16[8,3584]{1,0:T(8,128)(2,1)S(1)}, bf16[8,3584]{1,0:T(8,128)(2,1)S(1)}, u32[]{:S(2)}, u32[]{:S(2)}) %collective-permute-start.13) | collective-permute-done | bytes 57376 | tf_op jit(solution)/shard_map/ppermute | solution.py:37
  47.3 1.9 %collective-permute-start.14 = (bf16[4,3584]{1,0:T(4,128)(2,1)S(1)}, bf16[4,3584]{1,0:T(4,128)(2,1)S(1)}, u32[]{:S(2)}, u32[]{:S(2)}) collective-permute-start(bf16[4,3584]{1,0:T(4,128)(2,1)S(1)} %slice.97), channel_id=1, source_target_pairs={{0,8},{1,9},{2,10},{3,11},{4,12},{5,13},{6,14},{7,15},{8,0},{9,1},... | collective-permute-start | bytes 86024 | tf_op jit(solution)/shard_map/ppermute | solution.py:37
  49.2 2.0 %collective-permute-start.17 = (bf16[4,3584]{1,0:T(4,128)(2,1)S(1)}, bf16[4,3584]{1,0:T(4,128)(2,1)S(1)}, u32[]{:S(2)}, u32[]{:S(2)}) collective-permute-start(bf16[4,3584]{1,0:T(4,128)(2,1)S(1)} %slice.101), channel_id=1, source_target_pairs={{0,8},{1,9},{2,10},{3,11},{4,12},{5,13},{6,14},{7,15},{8,0},{9,1},... | collective-permute-start | bytes 86024 | tf_op jit(solution)/shard_map/ppermute | solution.py:37
  51.2 1.1 %collective-permute-done.14 = bf16[4,3584]{1,0:T(4,128)(2,1)S(1)} collective-permute-done((bf16[4,3584]{1,0:T(4,128)(2,1)S(1)}, bf16[4,3584]{1,0:T(4,128)(2,1)S(1)}, u32[]{:S(2)}, u32[]{:S(2)}) %collective-permute-start.14) | collective-permute-done | bytes 28704 | tf_op jit(solution)/shard_map/ppermute | solution.py:37
  52.3 1.7 %collective-permute-done.17 = bf16[4,3584]{1,0:T(4,128)(2,1)S(1)} collective-permute-done((bf16[4,3584]{1,0:T(4,128)(2,1)S(1)}, bf16[4,3584]{1,0:T(4,128)(2,1)S(1)}, u32[]{:S(2)}, u32[]{:S(2)}) %collective-permute-start.17) | collective-permute-done | bytes 28704 | tf_op jit(solution)/shard_map/ppermute | solution.py:37
  54.0 0.7 %maximum_bitcast_fusion.2 = bf16[1,4,7168]{2,1,0:T(4,128)(2,1)} fusion(bf16[4,3584]{1,0:T(4,128)(2,1)S(1)} %add_convert_fusion.4, bf16[4,3584]{1,0:T(4,128)(2,1)S(1)} %add_convert_fusion.5), kind=kLoop, calls=%fused_computation.50 | loop fusion | flops 114688 | bytes 114688 | tf_op jit(solution)/shard_map/broadcast_in_dim | solution.py:276
  (43 shorter events, 0.6 us)
Async XLA Ops:
  0.0 20.4 %copy-start = (bf16[1,7168,128]{2,1,0:T(8,128)(2,1)S(1)}, bf16[1,7168,128]{2,1,0:T(8,128)(2,1)}, u32[]{:S(2)}) copy-start(bf16[1,7168,128]{2,1,0:T(8,128)(2,1)} %param.16) | copy-start | bytes 5505028
  1.0 7.8 %collective-permute-start.2 = (bf16[4,7296]{1,0:T(4,128)(2,1)S(1)}, bf16[4,7296]{1,0:T(4,128)(2,1)S(1)}, u32[]{:S(2)}, u32[]{:S(2)}) collective-permute-start(bf16[4,7296]{1,0:T(4,128)(2,1)S(1)} %shard_map.100), channel_id=1, source_target_pairs={{0,12},{1,13},{2,14},{3,15},{4,8},{5,9},{6,10},{7,11},{8,4},{9,5},... | collective-permute-start | bytes 175112 | tf_op jit(solution)/shard_map/ppermute | solution.py:37
  6.1 4.3 %collective-permute-start.1 = (bf16[4,7296]{1,0:T(4,128)(2,1)S(1)}, bf16[4,7296]{1,0:T(4,128)(2,1)S(1)}, u32[]{:S(2)}, u32[]{:S(2)}) collective-permute-start(bf16[4,7296]{1,0:T(4,128)(2,1)S(1)} %shard_map.100), channel_id=1, source_target_pairs={{0,4},{1,5},{2,6},{3,7},{4,0},{5,1},{6,2},{7,3},{8,12},{9,13},{10,... | collective-permute-start | bytes 175112 | tf_op jit(solution)/shard_map/ppermute | solution.py:37
  6.1 5.5 %collective-permute-start = (bf16[4,7296]{1,0:T(4,128)(2,1)S(1)}, bf16[4,7296]{1,0:T(4,128)(2,1)S(1)}, u32[]{:S(2)}, u32[]{:S(2)}) collective-permute-start(bf16[4,7296]{1,0:T(4,128)(2,1)S(1)} %shard_map.100), channel_id=1, source_target_pairs={{0,8},{1,9},{2,10},{3,11},{4,12},{5,13},{6,14},{7,15},{8,0},{9,1},... | collective-permute-start | bytes 175112 | tf_op jit(solution)/shard_map/ppermute | solution.py:37
  6.7 4.9 %collective-permute-start.3 = (bf16[4,7296]{1,0:T(4,128)(2,1)S(1)}, bf16[4,7296]{1,0:T(4,128)(2,1)S(1)}, u32[]{:S(2)}, u32[]{:S(2)}) collective-permute-start(bf16[4,7296]{1,0:T(4,128)(2,1)S(1)} %shard_map.100), channel_id=1, source_target_pairs={{0,2},{1,3},{2,0},{3,1},{4,6},{5,7},{6,4},{7,5},{8,10},{9,11},{10,... | collective-permute-start | bytes 175112 | tf_op jit(solution)/shard_map/ppermute | solution.py:37
  11.7 6.1 %collective-permute-start.4 = (bf16[12,7296]{1,0:T(8,128)(2,1)S(1)}, bf16[12,7296]{1,0:T(8,128)(2,1)S(1)}, u32[]{:S(2)}, u32[]{:S(2)}) collective-permute-start(bf16[12,7296]{1,0:T(8,128)(2,1)S(1)} %pad_maximum_fusion.2), channel_id=1, source_target_pairs={{0,2},{1,3},{2,0},{3,1},{4,6},{5,7},{6,4},{7,5},{8,10},{9,11},{10,... | collective-permute-start | bytes 525320 | tf_op jit(solution)/shard_map/ppermute | solution.py:37
  18.1 1.9 %collective-permute-start.5 = (bf16[32,7296]{1,0:T(8,128)(2,1)S(1)}, bf16[32,7296]{1,0:T(8,128)(2,1)S(1)}, u32[]{:S(2)}, u32[]{:S(2)}) collective-permute-start(bf16[32,7296]{1,0:T(8,128)(2,1)S(1)} %pad_maximum_fusion.1), channel_id=1, source_target_pairs={{0,1},{1,0},{2,3},{3,2},{4,5},{5,4},{6,7},{7,6},{8,9},{9,8},{10,11... | collective-permute-start | bytes 1400840 | tf_op jit(solution)/shard_map/ppermute | solution.py:37
  20.9 8.4 %collective-permute-start.8 = (bf16[64,128]{1,0:T(8,128)(2,1)S(1)}, bf16[64,128]{1,0:T(8,128)(2,1)S(1)}, u32[]{:S(2)}, u32[]{:S(2)}) collective-permute-start(bf16[64,128]{1,0:T(8,128)(2,1)S(1)} %convolution_convert_fusion.1), channel_id=1, source_target_pairs={{0,3},{1,2},{2,1},{3,0},{4,7},{5,6},{6,5},{7,4},{8,11},{9,10},{10,... | collective-permute-start | bytes 49160 | tf_op jit(solution)/shard_map/ppermute | solution.py:37
  22.2 7.1 %collective-permute-start.7 = (bf16[64,128]{1,0:T(8,128)(2,1)S(1)}, bf16[64,128]{1,0:T(8,128)(2,1)S(1)}, u32[]{:S(2)}, u32[]{:S(2)}) collective-permute-start(bf16[64,128]{1,0:T(8,128)(2,1)S(1)} %convolution_convert_fusion.1), channel_id=1, source_target_pairs={{0,2},{1,3},{2,0},{3,1},{4,6},{5,7},{6,4},{7,5},{8,10},{9,11},{10,... | collective-permute-start | bytes 49160 | tf_op jit(solution)/shard_map/ppermute | solution.py:37
  22.7 6.6 %collective-permute-start.6 = (bf16[64,128]{1,0:T(8,128)(2,1)S(1)}, bf16[64,128]{1,0:T(8,128)(2,1)S(1)}, u32[]{:S(2)}, u32[]{:S(2)}) collective-permute-start(bf16[64,128]{1,0:T(8,128)(2,1)S(1)} %convolution_convert_fusion.1), channel_id=1, source_target_pairs={{0,1},{1,0},{2,3},{3,2},{4,5},{5,4},{6,7},{7,6},{8,9},{9,8},{10,11... | collective-permute-start | bytes 49160 | tf_op jit(solution)/shard_map/ppermute | solution.py:37
  23.0 3.1 %copy-start.1 = (bf16[1,7168,2,256]{3,2,1,0:T(2,128)(2,1)S(1)}, bf16[1,7168,2,256]{3,2,1,0:T(2,128)(2,1)}, u32[]{:S(2)}) copy-start(bf16[1,7168,2,256]{3,2,1,0:T(2,128)(2,1)} %param.14) | copy-start | bytes 22020100
  26.1 3.0 %copy-start.6 = (s32[16]{0:T(128)S(1)}, s32[16]{0:T(128)}, u32[]{:S(2)}) copy-start(s32[16]{0:T(128)} %param.13) | copy-start | bytes 196
  26.1 3.3 %copy-start.4 = (bf16[1,4,128,2,256]{4,3,2,1,0:T(2,128)(2,1)S(1)}, bf16[1,4,128,2,256]{4,3,2,1,0:T(2,128)(2,1)}, u32[]{:S(2)}) copy-start(bf16[1,4,128,2,256]{4,3,2,1,0:T(2,128)(2,1)} %param.17) | copy-start | bytes 1572868
  26.1 7.1 %copy-start.2 = (bf16[1,256,7168]{2,1,0:T(8,128)(2,1)S(1)}, bf16[1,256,7168]{2,1,0:T(8,128)(2,1)}, u32[]{:S(2)}) copy-start(bf16[1,256,7168]{2,1,0:T(8,128)(2,1)} %param.15) | copy-start | bytes 11010052
  29.1 1.0 %copy-start.5 = (bf16[1,4,256,128]{3,2,1,0:T(8,128)(2,1)S(1)}, bf16[1,4,256,128]{3,2,1,0:T(8,128)(2,1)}, u32[]{:S(2)}) copy-start(bf16[1,4,256,128]{3,2,1,0:T(8,128)(2,1)} %param.18) | copy-start | bytes 786436
  30.3 1.4 %collective-permute-start.9 = (bf16[2,64,128]{2,1,0:T(8,128)(2,1)S(1)}, bf16[2,64,128]{2,1,0:T(8,128)(2,1)S(1)}, u32[]{:S(2)}, u32[]{:S(2)}) collective-permute-start(bf16[2,64,128]{2,1,0:T(8,128)(2,1)S(1)} %dynamic-slice_bitcast_fusion), channel_id=1, source_target_pairs={{0,1},{1,0},{2,3},{3,2},{4,5},{5,4},{6,7},{7,6},{8,9},{9,8},{10,11... | collective-permute-start | bytes 98312 | tf_op jit(solution)/shard_map/ppermute | solution.py:37
  31.6 3.8 %collective-permute-start.10 = (bf16[64,128]{1,0:T(8,128)(2,1)S(1)}, bf16[64,128]{1,0:T(8,128)(2,1)S(1)}, u32[]{:S(2)}, u32[]{:S(2)}) collective-permute-start(bf16[64,128]{1,0:T(8,128)(2,1)S(1)} %dynamic-slice_bitcast_fusion.1), channel_id=1, source_target_pairs={{0,2},{1,3},{2,0},{3,1},{4,6},{5,7},{6,4},{7,5},{8,10},{9,11},{10,... | collective-permute-start | bytes 49160 | tf_op jit(solution)/shard_map/ppermute | solution.py:37
  33.2 2.2 %copy-start.3 = (bf16[1,128,7168]{2,1,0:T(8,128)(2,1)S(1)}, bf16[1,128,7168]{2,1,0:T(8,128)(2,1)}, u32[]{:S(2)}) copy-start(bf16[1,128,7168]{2,1,0:T(8,128)(2,1)} %param.19) | copy-start | bytes 5505028
  36.0 1.9 %collective-permute-start.11 = (bf16[32,7168]{1,0:T(8,128)(2,1)S(1)}, bf16[32,7168]{1,0:T(8,128)(2,1)S(1)}, u32[]{:S(2)}, u32[]{:S(2)}) collective-permute-start(bf16[32,7168]{1,0:T(8,128)(2,1)S(1)} %slice_select_fusion), channel_id=1, source_target_pairs={{0,1},{1,0},{2,3},{3,2},{4,5},{5,4},{6,7},{7,6},{8,9},{9,8},{10,11... | collective-permute-start | bytes 1376264 | tf_op jit(solution)/shard_map/ppermute | solution.py:37
  38.0 4.9 %collective-permute-start.12 = (bf16[16,3584]{1,0:T(8,128)(2,1)S(1)}, bf16[16,3584]{1,0:T(8,128)(2,1)S(1)}, u32[]{:S(2)}, u32[]{:S(2)}) collective-permute-start(bf16[16,3584]{1,0:T(8,128)(2,1)S(1)} %get-tuple-element.16), channel_id=1, source_target_pairs={{0,2},{1,5},{2,0},{3,7},{4,6},{5,1},{6,4},{7,3},{8,10},{9,13},{10,... | collective-permute-start | bytes 344072 | tf_op jit(solution)/shard_map/ppermute | solution.py:37
  39.6 5.0 %collective-permute-start.15 = (bf16[16,3584]{1,0:T(8,128)(2,1)S(1)}, bf16[16,3584]{1,0:T(8,128)(2,1)S(1)}, u32[]{:S(2)}, u32[]{:S(2)}) collective-permute-start(bf16[16,3584]{1,0:T(8,128)(2,1)S(1)} %get-tuple-element.18), channel_id=1, source_target_pairs={{0,2},{1,5},{2,0},{3,7},{4,6},{5,1},{6,4},{7,3},{8,10},{9,13},{10,... | collective-permute-start | bytes 344072 | tf_op jit(solution)/shard_map/ppermute | solution.py:37
  43.0 4.2 %collective-permute-start.13 = (bf16[8,3584]{1,0:T(8,128)(2,1)S(1)}, bf16[8,3584]{1,0:T(8,128)(2,1)S(1)}, u32[]{:S(2)}, u32[]{:S(2)}) collective-permute-start(bf16[8,3584]{1,0:T(8,128)(2,1)S(1)} %broadcast_select_fusion.5), channel_id=1, source_target_pairs={{0,4},{1,3},{2,6},{3,1},{4,0},{5,7},{6,2},{7,5},{8,12},{9,11},{10,... | collective-permute-start | bytes 172040 | tf_op jit(solution)/shard_map/ppermute | solution.py:37
  44.7 4.4 %collective-permute-start.16 = (bf16[8,3584]{1,0:T(8,128)(2,1)S(1)}, bf16[8,3584]{1,0:T(8,128)(2,1)S(1)}, u32[]{:S(2)}, u32[]{:S(2)}) collective-permute-start(bf16[8,3584]{1,0:T(8,128)(2,1)S(1)} %broadcast_select_fusion.4), channel_id=1, source_target_pairs={{0,4},{1,3},{2,6},{3,1},{4,0},{5,7},{6,2},{7,5},{8,12},{9,11},{10,... | collective-permute-start | bytes 172040 | tf_op jit(solution)/shard_map/ppermute | solution.py:37
  47.3 5.1 %collective-permute-start.14 = (bf16[4,3584]{1,0:T(4,128)(2,1)S(1)}, bf16[4,3584]{1,0:T(4,128)(2,1)S(1)}, u32[]{:S(2)}, u32[]{:S(2)}) collective-permute-start(bf16[4,3584]{1,0:T(4,128)(2,1)S(1)} %slice.97), channel_id=1, source_target_pairs={{0,8},{1,9},{2,10},{3,11},{4,12},{5,13},{6,14},{7,15},{8,0},{9,1},... | collective-permute-start | bytes 86024 | tf_op jit(solution)/shard_map/ppermute | solution.py:37
  49.2 4.8 %collective-permute-start.17 = (bf16[4,3584]{1,0:T(4,128)(2,1)S(1)}, bf16[4,3584]{1,0:T(4,128)(2,1)S(1)}, u32[]{:S(2)}, u32[]{:S(2)}) collective-permute-start(bf16[4,3584]{1,0:T(4,128)(2,1)S(1)} %slice.101), channel_id=1, source_target_pairs={{0,8},{1,9},{2,10},{3,11},{4,12},{5,13},{6,14},{7,15},{8,0},{9,1},... | collective-permute-start | bytes 86024 | tf_op jit(solution)/shard_map/ppermute | solution.py:37

commit v23 on v21

--- a/solution.py
+++ b/solution.py
@@ -130,10 +130,34 @@
     )(x, in_hbm(base))
 
 
+def down_kernel(hidden, base, out, weights, sems):
+    step = base.shape[1] // sems.shape[0]
+    parts = [pl.ds(k * step, step) for k in range(sems.shape[0])]
+    copies = [pltpu.make_async_copy(base.at[:, part], weights.at[:, part], sems.at[k]) for k, part in enumerate(parts)]
+    for copy in copies:
+        copy.start()
+    for copy, part in zip(copies, parts):
+        copy.wait()
+        out[:, part] = jnp.dot(hidden[...], weights[:, part], preferred_element_type=jnp.float32)
+
+
+def down_product(hidden, base):
+    rows, width = hidden.shape[0], base.shape[1]
+    return pl.pallas_call(
+        down_kernel,
+        out_shape=jax.ShapeDtypeStruct((rows, width), jnp.float32),
+        in_specs=[VMEM, HBM],
+        out_specs=VMEM,
+        scratch_shapes=[pltpu.VMEM(base.shape, base.dtype), pltpu.SemaphoreType.DMA((width // 1024,))],
+        compiler_params=pltpu.CompilerParams(vmem_limit_bytes=16 << 20),
+        cost_estimate=pl.CostEstimate(flops=2 * rows * base.size, bytes_accessed=2 * base.size, transcendentals=0),
+    )(hidden, in_hbm(base))
+
+
 def part_kernel(bit, term, received, *refs):
     *outs, total = refs
-    half, width = total.shape
-    size, step = half // 4, width // (len(outs) // 2)
+    half = total.shape[0]
+    size = half // 4
     me = lax.axis_index("tensor")
     core, flag = me % 2, (me // (2 * bit)) % 2
     total[...] = term[pl.ds(pl.multiple_of(core * half, half), half), :].astype(jnp.float32) + received[
@@ -142,26 +166,22 @@
     by_x = 1 - core
     sent = (core + by_x * 2 * (1 - flag), 3 - by_x * 2 * flag)
     kept = (by_x * 2 * flag, 2 * core + by_x * (2 * flag + 1))
-    for i, out in enumerate(outs):
-        columns = pl.ds((i // 2) * step, step)
-        rows = [
-            total[pl.ds(pl.multiple_of(block * size, size), size), columns] for block in (sent, kept)[i % 2]
-        ]
+    for blocks, out in zip((sent, kept), outs):
+        rows = [total[pl.ds(pl.multiple_of(block * size, size), size), :] for block in blocks]
         out[...] = jnp.concatenate(rows).astype(out.dtype)
 
 
 def add_and_part(term, received, bit):
     half, width = received.shape
-    outs = pl.pallas_call(
+    return pl.pallas_call(
         functools.partial(part_kernel, bit),
-        out_shape=[jax.ShapeDtypeStruct((half // 2, width // CHUNKS), term.dtype)] * (2 * CHUNKS),
+        out_shape=[jax.ShapeDtypeStruct((half // 2, width), term.dtype)] * 2,
         in_specs=[VMEM, VMEM],
-        out_specs=[VMEM] * (2 * CHUNKS),
+        out_specs=[VMEM] * 2,
         scratch_shapes=[pltpu.VMEM((half, width), jnp.float32)],
         compiler_params=pltpu.CompilerParams(vmem_limit_bytes=16 << 20),
         cost_estimate=pl.CostEstimate(flops=0, bytes_accessed=6 * received.size, transcendentals=0),
     )(term, received)
-    return list(zip(outs[::2], outs[1::2]))
 
 
 def local(
@@ -253,13 +273,16 @@
     own_scale = lax.dynamic_index_in_dim(scale, me, 0, keepdims=False)
     scaled = (own_scale[:, None] * lowrank).astype(jnp.bfloat16)
 
-    term = jnp.dot(hidden_sum, base_down[0], preferred_element_type=jnp.float32)
-    term = (term + jnp.dot(scaled, delta_back[0], preferred_element_type=jnp.float32)).astype(jnp.bfloat16)
-
-    half = term.shape[0] // 2
-    sent = ordered(core == 1, term[half:], term[:half])[0]
+    base = down_product(hidden_sum, base_down[0])
+
+    half, step = base.shape[0] // 2, width // CHUNKS
     outputs = []
-    for sent, kept in add_and_part(term, trade(sent, (0, 1), (0, 1)), across[-1]):
+    for c in range(CHUNKS):
+        columns = slice(c * step, (c + 1) * step)
+        term = jnp.dot(scaled, delta_back[0, :, columns], preferred_element_type=jnp.float32)
+        term = (base[:, columns] + term).astype(jnp.bfloat16)
+        sent = ordered(core == 1, term[half:], term[:half])[0]
+        sent, kept = add_and_part(term, trade(sent, (0, 1), (0, 1)), across[-1])
         for i, (z, x) in enumerate(reversed(list(zip(paired, across)))):
             flag = (me // (2 * x)) % 2 == 1
             if i:

time: 53.9 us -> 53.7 us (level)
  Pallas kernels: 6.26 us -> 8.88 us
  waiting for transfers between devices: 20.2 us -> 17.6 us
  matrix products: 2.07 us -> 1.52 us
    pallas_call x0 -> x1, Pallas kernels: none -> 2.71 us  [down_product(): pl.pallas_call(down_kernel, out_shape=jax.ShapeDtypeStruct((rows, width),...]
    ppermute x18 -> x19, waiting for transfers between devices: 20.2 us -> 17.6 us  [trade(): return lax.ppermute(value, ('expert', 'tensor'), pairs)]
    dot_general x2, matrix products: 1.21 us -> 0.66 us  [local(): jnp.dot(scaled, delta_back[0, :, columns], preferred_element_type=jnp.flo...]
    ppermute x18 -> x19, starting transfers between devices: 22.2 us -> 22.6 us  [trade(): return lax.ppermute(value, ('expert', 'tensor'), pairs)]
  transfers between devices with their start and end apart: 18 -> 19, of which waited for: 12 -> 11; matrix products, arithmetic and copies ran while one was open for 3% -> 2% of each run, Pallas kernels for 9% -> 15%
where the time goes in v23:
time: 53.7 us; the launch traced here: 53.5 us
  starting transfers between devices  22.6 us (42%)
  waiting for transfers between devices  17.6 us (33%)
  Pallas kernels  8.88 us (17%)
  other arithmetic  2.02 us (4%)
  matrix products  1.52 us (3%)
  local copies, waits for them, and re-layouts  0.55 us (1%)
    ppermute x19, starting transfers between devices, trade(): return lax.ppermute(value, ('expert', 'tensor'), pairs)  22.6 us
    ppermute x19, waiting for transfers between devices, trade(): return lax.ppermute(value, ('expert', 'tensor'), pairs)  17.6 us
    pallas_call x1, Pallas kernels, gate_up_product(): pl.pallas_call(gate_up_kernel, out_shape=jax.ShapeDtypeStruct((2 * x.shap...  5 us
    pallas_call x1, Pallas kernels, down_product(): pl.pallas_call(down_kernel, out_shape=jax.ShapeDtypeStruct((rows, width),...  2.71 us
  transfers between devices with their start and end apart: 19, of which 11 were waited for; matrix products, arithmetic and copies ran while one was open for 2% of the time, Pallas kernels for 15%

profile of v23, /device:TPU:0, one launch (start us, length us, event | category | flops | bytes accessed | tf_op | source)
XLA Modules:
  0.0 53.5 jit_solution(1306640197920213176)
XLA Ops:
  0.0 1.0 %shard_map.100 = bf16[4,7296]{1,0:T(4,128)(2,1)S(1)} custom-call(bf16[4,7168]{1,0:T(4,128)(2,1)} %bitcast.70, s32[4,8]{1,0:T(4,128)} %bitcast.71, s32[4,8]{1,0:T(4,128)} %bitcast.72), custom_call_target="tpu_custom_call" | custom-call | flops 20000000000 | bytes 114688 | tf_op jit(solution)/shard_map/pallas_call | solution.py:75
  1.0 5.1 %collective-permute-start.2 = (bf16[4,7296]{1,0:T(4,128)(2,1)S(1)}, bf16[4,7296]{1,0:T(4,128)(2,1)S(1)}, u32[]{:S(2)}, u32[]{:S(2)}) collective-permute-start(bf16[4,7296]{1,0:T(4,128)(2,1)S(1)} %shard_map.100), channel_id=1, source_target_pairs={{0,12},{1,13},{2,14},{3,15},{4,8},{5,9},{6,10},{7,11},{8,4},{9,5},... | collective-permute-start | bytes 175112 | tf_op jit(solution)/shard_map/ppermute | solution.py:37
  6.1 0.6 %collective-permute-start = (bf16[4,7296]{1,0:T(4,128)(2,1)S(1)}, bf16[4,7296]{1,0:T(4,128)(2,1)S(1)}, u32[]{:S(2)}, u32[]{:S(2)}) collective-permute-start(bf16[4,7296]{1,0:T(4,128)(2,1)S(1)} %shard_map.100), channel_id=1, source_target_pairs={{0,8},{1,9},{2,10},{3,11},{4,12},{5,13},{6,14},{7,15},{8,0},{9,1},... | collective-permute-start | bytes 175112 | tf_op jit(solution)/shard_map/ppermute | solution.py:37
  6.7 1.6 %collective-permute-start.3 = (bf16[4,7296]{1,0:T(4,128)(2,1)S(1)}, bf16[4,7296]{1,0:T(4,128)(2,1)S(1)}, u32[]{:S(2)}, u32[]{:S(2)}) collective-permute-start(bf16[4,7296]{1,0:T(4,128)(2,1)S(1)} %shard_map.100), channel_id=1, source_target_pairs={{0,2},{1,3},{2,0},{3,1},{4,6},{5,7},{6,4},{7,5},{8,10},{9,11},{10,... | collective-permute-start | bytes 175112 | tf_op jit(solution)/shard_map/ppermute | solution.py:37
  8.4 0.4 collective-permute-done.2
  8.8 1.7 %collective-permute-done.1 = bf16[4,7296]{1,0:T(4,128)(2,1)S(1)} collective-permute-done((bf16[4,7296]{1,0:T(4,128)(2,1)S(1)}, bf16[4,7296]{1,0:T(4,128)(2,1)S(1)}, u32[]{:S(2)}, u32[]{:S(2)}) %collective-permute-start.1) | collective-permute-done | bytes 58400 | tf_op jit(solution)/shard_map/ppermute | solution.py:37
  10.4 1.1 %collective-permute-done = bf16[4,7296]{1,0:T(4,128)(2,1)S(1)} collective-permute-done((bf16[4,7296]{1,0:T(4,128)(2,1)S(1)}, bf16[4,7296]{1,0:T(4,128)(2,1)S(1)}, u32[]{:S(2)}, u32[]{:S(2)}) %collective-permute-start) | collective-permute-done | bytes 58400 | tf_op jit(solution)/shard_map/ppermute | solution.py:37
  11.6 0.1 pad_maximum_fusion.2
  11.7 1.6 %collective-permute-start.4 = (bf16[12,7296]{1,0:T(8,128)(2,1)S(1)}, bf16[12,7296]{1,0:T(8,128)(2,1)S(1)}, u32[]{:S(2)}, u32[]{:S(2)}) collective-permute-start(bf16[12,7296]{1,0:T(8,128)(2,1)S(1)} %pad_maximum_fusion.2), channel_id=1, source_target_pairs={{0,2},{1,3},{2,0},{3,1},{4,6},{5,7},{6,4},{7,5},{8,10},{9,11},{10,... | collective-permute-start | bytes 525320 | tf_op jit(solution)/shard_map/ppermute | solution.py:37
  13.3 4.6 %collective-permute-done.4 = bf16[12,7296]{1,0:T(8,128)(2,1)S(1)} collective-permute-done((bf16[12,7296]{1,0:T(8,128)(2,1)S(1)}, bf16[12,7296]{1,0:T(8,128)(2,1)S(1)}, u32[]{:S(2)}, u32[]{:S(2)}) %collective-permute-start.4) | collective-permute-done | bytes 175136 | tf_op jit(solution)/shard_map/ppermute | solution.py:37
  17.8 0.2 broadcast_select_fusion.3
  18.2 1.7 %collective-permute-done.5 = bf16[32,7296]{1,0:T(8,128)(2,1)S(1)} collective-permute-done((bf16[32,7296]{1,0:T(8,128)(2,1)S(1)}, bf16[32,7296]{1,0:T(8,128)(2,1)S(1)}, u32[]{:S(2)}, u32[]{:S(2)}) %collective-permute-start.5) | collective-permute-done | bytes 466976 | tf_op jit(solution)/shard_map/ppermute | solution.py:37
  20.0 0.2 broadcast_select_fusion.1
  20.2 0.2 convert_reduce_fusion
  20.4 0.5 convolution_convert_fusion.1
  20.9 1.3 %collective-permute-start.8 = (bf16[64,128]{1,0:T(8,128)(2,1)S(1)}, bf16[64,128]{1,0:T(8,128)(2,1)S(1)}, u32[]{:S(2)}, u32[]{:S(2)}) collective-permute-start(bf16[64,128]{1,0:T(8,128)(2,1)S(1)} %convolution_convert_fusion.1), channel_id=1, source_target_pairs={{0,3},{1,2},{2,1},{3,0},{4,7},{5,6},{6,5},{7,4},{8,11},{9,10},{10,... | collective-permute-start | bytes 49160 | tf_op jit(solution)/shard_map/ppermute | solution.py:37
  22.2 0.5 collective-permute-start.7
  22.7 0.1 collective-permute-start.6
  22.8 0.1 fusion.25
  23.0 5.0 %shard_map.101 = f32[128,256]{1,0:T(8,128)S(1)} custom-call(bf16[64,7296]{1,0:T(8,128)(2,1)S(1)} %pad_maximum_fusion.x, bf16[7168,2,256]{2,1,0:T(2,128)(2,1)} %bitcast.61), custom_call_target="tpu_custom_call" | custom-call | flops 469762048 | bytes 7340032 | tf_op jit(solution)/shard_map/pallas_call | solution.py:120
  28.1 0.1 select_reduce_fusion
  28.2 0.1 select_reduce_fusion.1
  28.3 0.2 fusion.7
  28.5 0.1 multiply_reduce_fusion
  28.7 0.3 copy-done.3
  29.0 0.2 convolution_convert_fusion
  29.2 0.5 collective-permute-start.9
  29.7 0.9 %collective-permute-done.9 = bf16[2,64,128]{2,1,0:T(8,128)(2,1)S(1)} collective-permute-done((bf16[2,64,128]{2,1,0:T(8,128)(2,1)S(1)}, bf16[2,64,128]{2,1,0:T(8,128)(2,1)S(1)}, u32[]{:S(2)}, u32[]{:S(2)}) %collective-permute-start.9) | collective-permute-done | bytes 32800 | tf_op jit(solution)/shard_map/ppermute | solution.py:37
  30.6 1.6 %collective-permute-start.10 = (bf16[64,128]{1,0:T(8,128)(2,1)S(1)}, bf16[64,128]{1,0:T(8,128)(2,1)S(1)}, u32[]{:S(2)}, u32[]{:S(2)}) collective-permute-start(bf16[64,128]{1,0:T(8,128)(2,1)S(1)} %dynamic-slice_bitcast_fusion.1), channel_id=1, source_target_pairs={{0,2},{1,3},{2,0},{3,1},{4,6},{5,7},{6,4},{7,5},{8,10},{9,11},{10,... | collective-permute-start | bytes 49160 | tf_op jit(solution)/shard_map/ppermute | solution.py:37
  32.2 2.7 %shard_map.102 = f32[64,7168]{1,0:T(8,128)S(1)} custom-call(bf16[64,256]{1,0:T(8,128)(2,1)S(1)} %get-tuple-element.21.hidden, bf16[256,7168]{1,0:T(8,128)(2,1)} %bitcast.62), custom_call_target="tpu_custom_call" | custom-call | flops 234881024 | bytes 3670016 | tf_op jit(solution)/shard_map/pallas_call | solution.py:146
  34.9 0.3 fusion.1.term
  35.3 0.1 collective-permute-start.15
  35.4 0.3 fusion.term
  35.8 0.5 collective-permute-start.11
  36.3 0.5 %collective-permute-done.15.received = bf16[32,3584]{1,0:T(8,128)(2,1)S(1)} collective-permute-done((bf16[32,3584]{1,0:T(8,128)(2,1)S(1)}, bf16[32,3584]{1,0:T(8,128)(2,1)S(1)}, u32[]{:S(2)}, u32[]{:S(2)}) %collective-permute-start.15) | collective-permute-done | bytes 229408 | tf_op jit(solution)/shard_map/ppermute | solution.py:37
  36.8 0.1 shard_map.104
  36.9 1.1 %collective-permute-start.16 = (bf16[16,3584]{1,0:T(8,128)(2,1)S(1)}, bf16[16,3584]{1,0:T(8,128)(2,1)S(1)}, u32[]{:S(2)}, u32[]{:S(2)}) collective-permute-start(bf16[16,3584]{1,0:T(8,128)(2,1)S(1)} %get-tuple-element.20), channel_id=1, source_target_pairs={{0,2},{1,5},{2,0},{3,7},{4,6},{5,1},{6,4},{7,3},{8,10},{9,13},{10,... | collective-permute-start | bytes 344072 | tf_op jit(solution)/shard_map/ppermute | solution.py:37
  38.0 0.1 shard_map.103
  38.1 1.1 %collective-permute-start.12 = (bf16[16,3584]{1,0:T(8,128)(2,1)S(1)}, bf16[16,3584]{1,0:T(8,128)(2,1)S(1)}, u32[]{:S(2)}, u32[]{:S(2)}) collective-permute-start(bf16[16,3584]{1,0:T(8,128)(2,1)S(1)} %get-tuple-element.18), channel_id=1, source_target_pairs={{0,2},{1,5},{2,0},{3,7},{4,6},{5,1},{6,4},{7,3},{8,10},{9,13},{10,... | collective-permute-start | bytes 344072 | tf_op jit(solution)/shard_map/ppermute | solution.py:37
  39.2 2.6 %collective-permute-done.16 = bf16[16,3584]{1,0:T(8,128)(2,1)S(1)} collective-permute-done((bf16[16,3584]{1,0:T(8,128)(2,1)S(1)}, bf16[16,3584]{1,0:T(8,128)(2,1)S(1)}, u32[]{:S(2)}, u32[]{:S(2)}) %collective-permute-start.16) | collective-permute-done | bytes 114720 | tf_op jit(solution)/shard_map/ppermute | solution.py:37
  41.8 1.7 %collective-permute-start.17 = (bf16[8,3584]{1,0:T(8,128)(2,1)S(1)}, bf16[8,3584]{1,0:T(8,128)(2,1)S(1)}, u32[]{:S(2)}, u32[]{:S(2)}) collective-permute-start(bf16[8,3584]{1,0:T(8,128)(2,1)S(1)} %broadcast_select_fusion.4), channel_id=1, source_target_pairs={{0,4},{1,3},{2,6},{3,1},{4,0},{5,7},{6,2},{7,5},{8,12},{9,11},{10,... | collective-permute-start | bytes 172040 | tf_op jit(solution)/shard_map/ppermute | solution.py:37
  43.6 1.2 %collective-permute-start.13 = (bf16[8,3584]{1,0:T(8,128)(2,1)S(1)}, bf16[8,3584]{1,0:T(8,128)(2,1)S(1)}, u32[]{:S(2)}, u32[]{:S(2)}) collective-permute-start(bf16[8,3584]{1,0:T(8,128)(2,1)S(1)} %broadcast_select_fusion.5), channel_id=1, source_target_pairs={{0,4},{1,3},{2,6},{3,1},{4,0},{5,7},{6,2},{7,5},{8,12},{9,11},{10,... | collective-permute-start | bytes 172040 | tf_op jit(solution)/shard_map/ppermute | solution.py:37
  44.7 1.3 %collective-permute-done.17 = bf16[8,3584]{1,0:T(8,128)(2,1)S(1)} collective-permute-done((bf16[8,3584]{1,0:T(8,128)(2,1)S(1)}, bf16[8,3584]{1,0:T(8,128)(2,1)S(1)}, u32[]{:S(2)}, u32[]{:S(2)}) %collective-permute-start.17) | collective-permute-done | bytes 57376 | tf_op jit(solution)/shard_map/ppermute | solution.py:37
  46.1 1.8 %collective-permute-start.18 = (bf16[4,3584]{1,0:T(4,128)(2,1)S(1)}, bf16[4,3584]{1,0:T(4,128)(2,1)S(1)}, u32[]{:S(2)}, u32[]{:S(2)}) collective-permute-start(bf16[4,3584]{1,0:T(4,128)(2,1)S(1)} %slice.123), channel_id=1, source_target_pairs={{0,8},{1,9},{2,10},{3,11},{4,12},{5,13},{6,14},{7,15},{8,0},{9,1},... | collective-permute-start | bytes 86024 | tf_op jit(solution)/shard_map/ppermute | solution.py:37
  48.0 2.1 %collective-permute-start.14 = (bf16[4,3584]{1,0:T(4,128)(2,1)S(1)}, bf16[4,3584]{1,0:T(4,128)(2,1)S(1)}, u32[]{:S(2)}, u32[]{:S(2)}) collective-permute-start(bf16[4,3584]{1,0:T(4,128)(2,1)S(1)} %slice.116), channel_id=1, source_target_pairs={{0,8},{1,9},{2,10},{3,11},{4,12},{5,13},{6,14},{7,15},{8,0},{9,1},... | collective-permute-start | bytes 86024 | tf_op jit(solution)/shard_map/ppermute | solution.py:37
  50.1 1.1 %collective-permute-done.18 = bf16[4,3584]{1,0:T(4,128)(2,1)S(1)} collective-permute-done((bf16[4,3584]{1,0:T(4,128)(2,1)S(1)}, bf16[4,3584]{1,0:T(4,128)(2,1)S(1)}, u32[]{:S(2)}, u32[]{:S(2)}) %collective-permute-start.18) | collective-permute-done | bytes 28704 | tf_op jit(solution)/shard_map/ppermute | solution.py:37
  51.2 1.7 %collective-permute-done.14 = bf16[4,3584]{1,0:T(4,128)(2,1)S(1)} collective-permute-done((bf16[4,3584]{1,0:T(4,128)(2,1)S(1)}, bf16[4,3584]{1,0:T(4,128)(2,1)S(1)}, u32[]{:S(2)}, u32[]{:S(2)}) %collective-permute-start.14) | collective-permute-done | bytes 28704 | tf_op jit(solution)/shard_map/ppermute | solution.py:37
  52.9 0.7 %maximum_bitcast_fusion.2 = bf16[1,4,7168]{2,1,0:T(4,128)(2,1)} fusion(bf16[4,3584]{1,0:T(4,128)(2,1)S(1)} %add_convert_fusion.4, bf16[4,3584]{1,0:T(4,128)(2,1)S(1)} %add_convert_fusion.5), kind=kLoop, calls=%fused_computation.48 | loop fusion | flops 114688 | bytes 114688 | tf_op jit(solution)/shard_map/broadcast_in_dim | solution.py:305
  (44 shorter events, 0.7 us)
Async XLA Ops:
  0.0 20.2 %copy-start = (bf16[1,7168,128]{2,1,0:T(8,128)(2,1)S(1)}, bf16[1,7168,128]{2,1,0:T(8,128)(2,1)}, u32[]{:S(2)}) copy-start(bf16[1,7168,128]{2,1,0:T(8,128)(2,1)} %param.16) | copy-start | bytes 5505028
  1.0 7.8 %collective-permute-start.2 = (bf16[4,7296]{1,0:T(4,128)(2,1)S(1)}, bf16[4,7296]{1,0:T(4,128)(2,1)S(1)}, u32[]{:S(2)}, u32[]{:S(2)}) collective-permute-start(bf16[4,7296]{1,0:T(4,128)(2,1)S(1)} %shard_map.100), channel_id=1, source_target_pairs={{0,12},{1,13},{2,14},{3,15},{4,8},{5,9},{6,10},{7,11},{8,4},{9,5},... | collective-permute-start | bytes 175112 | tf_op jit(solution)/shard_map/ppermute | solution.py:37
  6.1 4.3 %collective-permute-start.1 = (bf16[4,7296]{1,0:T(4,128)(2,1)S(1)}, bf16[4,7296]{1,0:T(4,128)(2,1)S(1)}, u32[]{:S(2)}, u32[]{:S(2)}) collective-permute-start(bf16[4,7296]{1,0:T(4,128)(2,1)S(1)} %shard_map.100), channel_id=1, source_target_pairs={{0,4},{1,5},{2,6},{3,7},{4,0},{5,1},{6,2},{7,3},{8,12},{9,13},{10,... | collective-permute-start | bytes 175112 | tf_op jit(solution)/shard_map/ppermute | solution.py:37
  6.1 5.5 %collective-permute-start = (bf16[4,7296]{1,0:T(4,128)(2,1)S(1)}, bf16[4,7296]{1,0:T(4,128)(2,1)S(1)}, u32[]{:S(2)}, u32[]{:S(2)}) collective-permute-start(bf16[4,7296]{1,0:T(4,128)(2,1)S(1)} %shard_map.100), channel_id=1, source_target_pairs={{0,8},{1,9},{2,10},{3,11},{4,12},{5,13},{6,14},{7,15},{8,0},{9,1},... | collective-permute-start | bytes 175112 | tf_op jit(solution)/shard_map/ppermute | solution.py:37
  6.7 4.9 %collective-permute-start.3 = (bf16[4,7296]{1,0:T(4,128)(2,1)S(1)}, bf16[4,7296]{1,0:T(4,128)(2,1)S(1)}, u32[]{:S(2)}, u32[]{:S(2)}) collective-permute-start(bf16[4,7296]{1,0:T(4,128)(2,1)S(1)} %shard_map.100), channel_id=1, source_target_pairs={{0,2},{1,3},{2,0},{3,1},{4,6},{5,7},{6,4},{7,5},{8,10},{9,11},{10,... | collective-permute-start | bytes 175112 | tf_op jit(solution)/shard_map/ppermute | solution.py:37
  11.7 6.1 %collective-permute-start.4 = (bf16[12,7296]{1,0:T(8,128)(2,1)S(1)}, bf16[12,7296]{1,0:T(8,128)(2,1)S(1)}, u32[]{:S(2)}, u32[]{:S(2)}) collective-permute-start(bf16[12,7296]{1,0:T(8,128)(2,1)S(1)} %pad_maximum_fusion.2), channel_id=1, source_target_pairs={{0,2},{1,3},{2,0},{3,1},{4,6},{5,7},{6,4},{7,5},{8,10},{9,11},{10,... | collective-permute-start | bytes 525320 | tf_op jit(solution)/shard_map/ppermute | solution.py:37
  18.1 1.9 %collective-permute-start.5 = (bf16[32,7296]{1,0:T(8,128)(2,1)S(1)}, bf16[32,7296]{1,0:T(8,128)(2,1)S(1)}, u32[]{:S(2)}, u32[]{:S(2)}) collective-permute-start(bf16[32,7296]{1,0:T(8,128)(2,1)S(1)} %pad_maximum_fusion.1), channel_id=1, source_target_pairs={{0,1},{1,0},{2,3},{3,2},{4,5},{5,4},{6,7},{7,6},{8,9},{9,8},{10,11... | collective-permute-start | bytes 1400840 | tf_op jit(solution)/shard_map/ppermute | solution.py:37
  20.9 7.4 %collective-permute-start.8 = (bf16[64,128]{1,0:T(8,128)(2,1)S(1)}, bf16[64,128]{1,0:T(8,128)(2,1)S(1)}, u32[]{:S(2)}, u32[]{:S(2)}) collective-permute-start(bf16[64,128]{1,0:T(8,128)(2,1)S(1)} %convolution_convert_fusion.1), channel_id=1, source_target_pairs={{0,3},{1,2},{2,1},{3,0},{4,7},{5,6},{6,5},{7,4},{8,11},{9,10},{10,... | collective-permute-start | bytes 49160 | tf_op jit(solution)/shard_map/ppermute | solution.py:37
  22.2 6.1 %collective-permute-start.7 = (bf16[64,128]{1,0:T(8,128)(2,1)S(1)}, bf16[64,128]{1,0:T(8,128)(2,1)S(1)}, u32[]{:S(2)}, u32[]{:S(2)}) collective-permute-start(bf16[64,128]{1,0:T(8,128)(2,1)S(1)} %convolution_convert_fusion.1), channel_id=1, source_target_pairs={{0,2},{1,3},{2,0},{3,1},{4,6},{5,7},{6,4},{7,5},{8,10},{9,11},{10,... | collective-permute-start | bytes 49160 | tf_op jit(solution)/shard_map/ppermute | solution.py:37
  22.7 5.5 %collective-permute-start.6 = (bf16[64,128]{1,0:T(8,128)(2,1)S(1)}, bf16[64,128]{1,0:T(8,128)(2,1)S(1)}, u32[]{:S(2)}, u32[]{:S(2)}) collective-permute-start(bf16[64,128]{1,0:T(8,128)(2,1)S(1)} %convolution_convert_fusion.1), channel_id=1, source_target_pairs={{0,1},{1,0},{2,3},{3,2},{4,5},{5,4},{6,7},{7,6},{8,9},{9,8},{10,11... | collective-permute-start | bytes 49160 | tf_op jit(solution)/shard_map/ppermute | solution.py:37
  23.0 5.0 %copy-start.4 = (s32[16]{0:T(128)S(1)}, s32[16]{0:T(128)}, u32[]{:S(2)}) copy-start(s32[16]{0:T(128)} %param.13) | copy-start | bytes 196
  23.0 5.3 %copy-start.2 = (bf16[1,4,128,2,256]{4,3,2,1,0:T(2,128)(2,1)S(1)}, bf16[1,4,128,2,256]{4,3,2,1,0:T(2,128)(2,1)}, u32[]{:S(2)}) copy-start(bf16[1,4,128,2,256]{4,3,2,1,0:T(2,128)(2,1)} %param.17) | copy-start | bytes 1572868
  28.0 1.0 %copy-start.3 = (bf16[1,4,256,128]{3,2,1,0:T(8,128)(2,1)S(1)}, bf16[1,4,256,128]{3,2,1,0:T(8,128)(2,1)}, u32[]{:S(2)}) copy-start(bf16[1,4,256,128]{3,2,1,0:T(8,128)(2,1)} %param.18) | copy-start | bytes 786436
  29.2 1.4 %collective-permute-start.9 = (bf16[2,64,128]{2,1,0:T(8,128)(2,1)S(1)}, bf16[2,64,128]{2,1,0:T(8,128)(2,1)S(1)}, u32[]{:S(2)}, u32[]{:S(2)}) collective-permute-start(bf16[2,64,128]{2,1,0:T(8,128)(2,1)S(1)} %dynamic-slice_bitcast_fusion), channel_id=1, source_target_pairs={{0,1},{1,0},{2,3},{3,2},{4,5},{5,4},{6,7},{7,6},{8,9},{9,8},{10,11... | collective-permute-start | bytes 98312 | tf_op jit(solution)/shard_map/ppermute | solution.py:37
  30.6 4.3 %collective-permute-start.10 = (bf16[64,128]{1,0:T(8,128)(2,1)S(1)}, bf16[64,128]{1,0:T(8,128)(2,1)S(1)}, u32[]{:S(2)}, u32[]{:S(2)}) collective-permute-start(bf16[64,128]{1,0:T(8,128)(2,1)S(1)} %dynamic-slice_bitcast_fusion.1), channel_id=1, source_target_pairs={{0,2},{1,3},{2,0},{3,1},{4,6},{5,7},{6,4},{7,5},{8,10},{9,11},{10,... | collective-permute-start | bytes 49160 | tf_op jit(solution)/shard_map/ppermute | solution.py:37
  32.2 2.7 %copy-start.1 = (bf16[1,128,7168]{2,1,0:T(8,128)(2,1)S(1)}, bf16[1,128,7168]{2,1,0:T(8,128)(2,1)}, u32[]{:S(2)}) copy-start(bf16[1,128,7168]{2,1,0:T(8,128)(2,1)} %param.19) | copy-start | bytes 5505028
  35.3 1.6 %collective-permute-start.15 = (bf16[32,3584]{1,0:T(8,128)(2,1)S(1)}, bf16[32,3584]{1,0:T(8,128)(2,1)S(1)}, u32[]{:S(2)}, u32[]{:S(2)}) collective-permute-start(bf16[32,3584]{1,0:T(8,128)(2,1)S(1)} %slice_select_fusion), channel_id=1, source_target_pairs={{0,1},{1,0},{2,3},{3,2},{4,5},{5,4},{6,7},{7,6},{8,9},{9,8},{10,11... | collective-permute-start | bytes 688136 | tf_op jit(solution)/shard_map/ppermute | solution.py:37
  35.8 2.2 %collective-permute-start.11 = (bf16[32,3584]{1,0:T(8,128)(2,1)S(1)}, bf16[32,3584]{1,0:T(8,128)(2,1)S(1)}, u32[]{:S(2)}, u32[]{:S(2)}) collective-permute-start(bf16[32,3584]{1,0:T(8,128)(2,1)S(1)} %slice_select_fusion.1), channel_id=1, source_target_pairs={{0,1},{1,0},{2,3},{3,2},{4,5},{5,4},{6,7},{7,6},{8,9},{9,8},{10,11... | collective-permute-start | bytes 688136 | tf_op jit(solution)/shard_map/ppermute | solution.py:37
  36.9 4.9 %collective-permute-start.16 = (bf16[16,3584]{1,0:T(8,128)(2,1)S(1)}, bf16[16,3584]{1,0:T(8,128)(2,1)S(1)}, u32[]{:S(2)}, u32[]{:S(2)}) collective-permute-start(bf16[16,3584]{1,0:T(8,128)(2,1)S(1)} %get-tuple-element.20), channel_id=1, source_target_pairs={{0,2},{1,5},{2,0},{3,7},{4,6},{5,1},{6,4},{7,3},{8,10},{9,13},{10,... | collective-permute-start | bytes 344072 | tf_op jit(solution)/shard_map/ppermute | solution.py:37
  38.1 5.4 %collective-permute-start.12 = (bf16[16,3584]{1,0:T(8,128)(2,1)S(1)}, bf16[16,3584]{1,0:T(8,128)(2,1)S(1)}, u32[]{:S(2)}, u32[]{:S(2)}) collective-permute-start(bf16[16,3584]{1,0:T(8,128)(2,1)S(1)} %get-tuple-element.18), channel_id=1, source_target_pairs={{0,2},{1,5},{2,0},{3,7},{4,6},{5,1},{6,4},{7,3},{8,10},{9,13},{10,... | collective-permute-start | bytes 344072 | tf_op jit(solution)/shard_map/ppermute | solution.py:37
  41.8 4.2 %collective-permute-start.17 = (bf16[8,3584]{1,0:T(8,128)(2,1)S(1)}, bf16[8,3584]{1,0:T(8,128)(2,1)S(1)}, u32[]{:S(2)}, u32[]{:S(2)}) collective-permute-start(bf16[8,3584]{1,0:T(8,128)(2,1)S(1)} %broadcast_select_fusion.4), channel_id=1, source_target_pairs={{0,4},{1,3},{2,6},{3,1},{4,0},{5,7},{6,2},{7,5},{8,12},{9,11},{10,... | collective-permute-start | bytes 172040 | tf_op jit(solution)/shard_map/ppermute | solution.py:37
  43.6 4.4 %collective-permute-start.13 = (bf16[8,3584]{1,0:T(8,128)(2,1)S(1)}, bf16[8,3584]{1,0:T(8,128)(2,1)S(1)}, u32[]{:S(2)}, u32[]{:S(2)}) collective-permute-start(bf16[8,3584]{1,0:T(8,128)(2,1)S(1)} %broadcast_select_fusion.5), channel_id=1, source_target_pairs={{0,4},{1,3},{2,6},{3,1},{4,0},{5,7},{6,2},{7,5},{8,12},{9,11},{10,... | collective-permute-start | bytes 172040 | tf_op jit(solution)/shard_map/ppermute | solution.py:37
  46.1 5.0 %collective-permute-start.18 = (bf16[4,3584]{1,0:T(4,128)(2,1)S(1)}, bf16[4,3584]{1,0:T(4,128)(2,1)S(1)}, u32[]{:S(2)}, u32[]{:S(2)}) collective-permute-start(bf16[4,3584]{1,0:T(4,128)(2,1)S(1)} %slice.123), channel_id=1, source_target_pairs={{0,8},{1,9},{2,10},{3,11},{4,12},{5,13},{6,14},{7,15},{8,0},{9,1},... | collective-permute-start | bytes 86024 | tf_op jit(solution)/shard_map/ppermute | solution.py:37
  48.0 4.8 %collective-permute-start.14 = (bf16[4,3584]{1,0:T(4,128)(2,1)S(1)}, bf16[4,3584]{1,0:T(4,128)(2,1)S(1)}, u32[]{:S(2)}, u32[]{:S(2)}) collective-permute-start(bf16[4,3584]{1,0:T(4,128)(2,1)S(1)} %slice.116), channel_id=1, source_target_pairs={{0,8},{1,9},{2,10},{3,11},{4,12},{5,13},{6,14},{7,15},{8,0},{9,1},... | collective-permute-start | bytes 86024 | tf_op jit(solution)/shard_map/ppermute | solution.py:37

commit v24 on v23

--- a/solution.py
+++ b/solution.py
@@ -10,6 +10,8 @@
 from jax.sharding import PartitionSpec as P
 
 CHUNKS = 2
+PIECES = (1, 2, 4, 4)
+DOWN_PIECES = (1, 3)
 VMEM = pl.BlockSpec(memory_space=pltpu.VMEM)
 HBM = pl.BlockSpec(memory_space=pltpu.HBM)
 
@@ -87,14 +89,22 @@
     )(in_hbm(tokens), in_hbm(routes), in_hbm(numerators))
 
 
+def piece_bounds(size, step, pieces):
+    ends = [0]
+    for piece in pieces:
+        ends.append(ends[-1] + piece * step)
+    return list(zip(ends, [*ends[1:], size]))
+
+
 def gate_up_kernel(x, base, out, weights, sems):
     depth, _, columns = weights.shape
-    step = depth // sems.shape[0]
-    copies = [
-        pltpu.make_async_copy(base.at[pl.ds(k, step)], weights.at[pl.ds(k, step)], sems.at[k // step])
-        for k in range(0, depth, step)
-    ]
-    for copy in copies:
+    step = 512
+    bounds = piece_bounds(depth, step, PIECES)
+    copies = {
+        low: pltpu.make_async_copy(base.at[pl.ds(low, high - low)], weights.at[pl.ds(low, high - low)], sems.at[i])
+        for i, (low, high) in enumerate(bounds)
+    }
+    for copy in copies.values():
         copy.start()
     row = lax.broadcasted_iota(jnp.int32, (128, 256), 0)
     column = lax.broadcasted_iota(jnp.int32, (128, 256), 1)
@@ -108,7 +118,8 @@
         stacked = jnp.concatenate([x[:, i : i + 128] for i in range(k, k + step, 128)])
         wide = jnp.dot(stacked, spread, preferred_element_type=jnp.float32).astype(jnp.bfloat16)
         wide = jnp.concatenate([wide[i : i + count] for i in range(0, stacked.shape[0], count)], axis=1)
-        copies[k // step].wait()
+        if k in copies:
+            copies[k].wait()
         total += jnp.dot(
             jnp.concatenate([wide * even_mask, wide * odd_mask]), flat[2 * k : 2 * (k + step), :], preferred_element_type=jnp.float32
         )
@@ -122,7 +133,7 @@
         out_shape=jax.ShapeDtypeStruct((2 * x.shape[0], columns), jnp.float32),
         in_specs=[VMEM, HBM],
         out_specs=VMEM,
-        scratch_shapes=[pltpu.VMEM(base.shape, base.dtype), pltpu.SemaphoreType.DMA((depth // 512,))],
+        scratch_shapes=[pltpu.VMEM(base.shape, base.dtype), pltpu.SemaphoreType.DMA((len(PIECES) + 1,))],
         compiler_params=pltpu.CompilerParams(vmem_limit_bytes=32 << 20),
         cost_estimate=pl.CostEstimate(
             flops=4 * x.shape[0] * depth * columns, bytes_accessed=2 * base.size, transcendentals=0
@@ -131,13 +142,19 @@
 
 
 def down_kernel(hidden, base, out, weights, sems):
-    step = base.shape[1] // sems.shape[0]
-    parts = [pl.ds(k * step, step) for k in range(sems.shape[0])]
-    copies = [pltpu.make_async_copy(base.at[:, part], weights.at[:, part], sems.at[k]) for k, part in enumerate(parts)]
-    for copy in copies:
+    step = 1024
+    copies = {
+        low: pltpu.make_async_copy(
+            base.at[:, pl.ds(low, high - low)], weights.at[:, pl.ds(low, high - low)], sems.at[i]
+        )
+        for i, (low, high) in enumerate(piece_bounds(base.shape[1], step, DOWN_PIECES))
+    }
+    for copy in copies.values():
         copy.start()
-    for copy, part in zip(copies, parts):
-        copy.wait()
+    for k in range(0, base.shape[1], step):
+        if k in copies:
+            copies[k].wait()
+        part = pl.ds(k, step)
         out[:, part] = jnp.dot(hidden[...], weights[:, part], preferred_element_type=jnp.float32)
 
 
@@ -148,7 +165,7 @@
         out_shape=jax.ShapeDtypeStruct((rows, width), jnp.float32),
         in_specs=[VMEM, HBM],
         out_specs=VMEM,
-        scratch_shapes=[pltpu.VMEM(base.shape, base.dtype), pltpu.SemaphoreType.DMA((width // 1024,))],
+        scratch_shapes=[pltpu.VMEM(base.shape, base.dtype), pltpu.SemaphoreType.DMA((len(DOWN_PIECES) + 1,))],
         compiler_params=pltpu.CompilerParams(vmem_limit_bytes=16 << 20),
         cost_estimate=pl.CostEstimate(flops=2 * rows * base.size, bytes_accessed=2 * base.size, transcendentals=0),
     )(hidden, in_hbm(base))

time: 53.7 us -> 53 us (0.987)
  Pallas kernels: 8.88 us -> 8.22 us
    pallas_call x1, Pallas kernels: 5 us -> 4.46 us  [gate_up_product(): pl.pallas_call(gate_up_kernel, out_shape=jax.ShapeDtypeStruct((2 * x.shap...]
  transfers between devices with their start and end apart: 19 -> 19, of which waited for: 11 -> 11; matrix products, arithmetic and copies ran while one was open for 2% -> 2% of each run, Pallas kernels for 15% -> 14%
where the time goes in v24:
time: 53 us; the launch traced here: 52.9 us
  starting transfers between devices  22.6 us (43%)
  waiting for transfers between devices  17.6 us (33%)
  Pallas kernels  8.22 us (16%)
  other arithmetic  2.02 us (4%)
  matrix products  1.52 us (3%)
  local copies, waits for them, and re-layouts  0.55 us (1%)
    ppermute x19, starting transfers between devices, trade(): return lax.ppermute(value, ('expert', 'tensor'), pairs)  22.6 us
    ppermute x19, waiting for transfers between devices, trade(): return lax.ppermute(value, ('expert', 'tensor'), pairs)  17.6 us
    pallas_call x1, Pallas kernels, gate_up_product(): pl.pallas_call(gate_up_kernel, out_shape=jax.ShapeDtypeStruct((2 * x.shap...  4.46 us
    pallas_call x1, Pallas kernels, down_product(): pl.pallas_call(down_kernel, out_shape=jax.ShapeDtypeStruct((rows, width),...  2.59 us
  transfers between devices with their start and end apart: 19, of which 11 were waited for; matrix products, arithmetic and copies ran while one was open for 2% of the time, Pallas kernels for 14%

profile of v24, /device:TPU:0, one launch (start us, length us, event | category | flops | bytes accessed | tf_op | source)
XLA Modules:
  0.0 52.9 jit_solution(12810046633745007943)
XLA Ops:
  0.0 1.0 %shard_map.100 = bf16[4,7296]{1,0:T(4,128)(2,1)S(1)} custom-call(bf16[4,7168]{1,0:T(4,128)(2,1)} %bitcast.70, s32[4,8]{1,0:T(4,128)} %bitcast.71, s32[4,8]{1,0:T(4,128)} %bitcast.72), custom_call_target="tpu_custom_call" | custom-call | flops 20000000000 | bytes 114688 | tf_op jit(solution)/shard_map/pallas_call | solution.py:77
  1.0 5.1 %collective-permute-start.2 = (bf16[4,7296]{1,0:T(4,128)(2,1)S(1)}, bf16[4,7296]{1,0:T(4,128)(2,1)S(1)}, u32[]{:S(2)}, u32[]{:S(2)}) collective-permute-start(bf16[4,7296]{1,0:T(4,128)(2,1)S(1)} %shard_map.100), channel_id=1, source_target_pairs={{0,12},{1,13},{2,14},{3,15},{4,8},{5,9},{6,10},{7,11},{8,4},{9,5},... | collective-permute-start | bytes 175112 | tf_op jit(solution)/shard_map/ppermute | solution.py:39
  6.1 0.6 %collective-permute-start = (bf16[4,7296]{1,0:T(4,128)(2,1)S(1)}, bf16[4,7296]{1,0:T(4,128)(2,1)S(1)}, u32[]{:S(2)}, u32[]{:S(2)}) collective-permute-start(bf16[4,7296]{1,0:T(4,128)(2,1)S(1)} %shard_map.100), channel_id=1, source_target_pairs={{0,8},{1,9},{2,10},{3,11},{4,12},{5,13},{6,14},{7,15},{8,0},{9,1},... | collective-permute-start | bytes 175112 | tf_op jit(solution)/shard_map/ppermute | solution.py:39
  6.7 1.6 %collective-permute-start.3 = (bf16[4,7296]{1,0:T(4,128)(2,1)S(1)}, bf16[4,7296]{1,0:T(4,128)(2,1)S(1)}, u32[]{:S(2)}, u32[]{:S(2)}) collective-permute-start(bf16[4,7296]{1,0:T(4,128)(2,1)S(1)} %shard_map.100), channel_id=1, source_target_pairs={{0,2},{1,3},{2,0},{3,1},{4,6},{5,7},{6,4},{7,5},{8,10},{9,11},{10,... | collective-permute-start | bytes 175112 | tf_op jit(solution)/shard_map/ppermute | solution.py:39
  8.4 0.4 collective-permute-done.2
  8.8 1.7 %collective-permute-done.1 = bf16[4,7296]{1,0:T(4,128)(2,1)S(1)} collective-permute-done((bf16[4,7296]{1,0:T(4,128)(2,1)S(1)}, bf16[4,7296]{1,0:T(4,128)(2,1)S(1)}, u32[]{:S(2)}, u32[]{:S(2)}) %collective-permute-start.1) | collective-permute-done | bytes 58400 | tf_op jit(solution)/shard_map/ppermute | solution.py:39
  10.4 1.1 %collective-permute-done = bf16[4,7296]{1,0:T(4,128)(2,1)S(1)} collective-permute-done((bf16[4,7296]{1,0:T(4,128)(2,1)S(1)}, bf16[4,7296]{1,0:T(4,128)(2,1)S(1)}, u32[]{:S(2)}, u32[]{:S(2)}) %collective-permute-start) | collective-permute-done | bytes 58400 | tf_op jit(solution)/shard_map/ppermute | solution.py:39
  11.6 0.1 pad_maximum_fusion.2
  11.7 1.6 %collective-permute-start.4 = (bf16[12,7296]{1,0:T(8,128)(2,1)S(1)}, bf16[12,7296]{1,0:T(8,128)(2,1)S(1)}, u32[]{:S(2)}, u32[]{:S(2)}) collective-permute-start(bf16[12,7296]{1,0:T(8,128)(2,1)S(1)} %pad_maximum_fusion.2), channel_id=1, source_target_pairs={{0,2},{1,3},{2,0},{3,1},{4,6},{5,7},{6,4},{7,5},{8,10},{9,11},{10,... | collective-permute-start | bytes 525320 | tf_op jit(solution)/shard_map/ppermute | solution.py:39
  13.3 4.6 %collective-permute-done.4 = bf16[12,7296]{1,0:T(8,128)(2,1)S(1)} collective-permute-done((bf16[12,7296]{1,0:T(8,128)(2,1)S(1)}, bf16[12,7296]{1,0:T(8,128)(2,1)S(1)}, u32[]{:S(2)}, u32[]{:S(2)}) %collective-permute-start.4) | collective-permute-done | bytes 175136 | tf_op jit(solution)/shard_map/ppermute | solution.py:39
  17.8 0.2 broadcast_select_fusion.3
  18.2 1.7 %collective-permute-done.5 = bf16[32,7296]{1,0:T(8,128)(2,1)S(1)} collective-permute-done((bf16[32,7296]{1,0:T(8,128)(2,1)S(1)}, bf16[32,7296]{1,0:T(8,128)(2,1)S(1)}, u32[]{:S(2)}, u32[]{:S(2)}) %collective-permute-start.5) | collective-permute-done | bytes 466976 | tf_op jit(solution)/shard_map/ppermute | solution.py:39
  20.0 0.2 broadcast_select_fusion.1
  20.2 0.2 convert_reduce_fusion
  20.4 0.5 convolution_convert_fusion.1
  20.9 1.3 %collective-permute-start.8 = (bf16[64,128]{1,0:T(8,128)(2,1)S(1)}, bf16[64,128]{1,0:T(8,128)(2,1)S(1)}, u32[]{:S(2)}, u32[]{:S(2)}) collective-permute-start(bf16[64,128]{1,0:T(8,128)(2,1)S(1)} %convolution_convert_fusion.1), channel_id=1, source_target_pairs={{0,3},{1,2},{2,1},{3,0},{4,7},{5,6},{6,5},{7,4},{8,11},{9,10},{10,... | collective-permute-start | bytes 49160 | tf_op jit(solution)/shard_map/ppermute | solution.py:39
  22.2 0.5 %collective-permute-start.7 = (bf16[64,128]{1,0:T(8,128)(2,1)S(1)}, bf16[64,128]{1,0:T(8,128)(2,1)S(1)}, u32[]{:S(2)}, u32[]{:S(2)}) collective-permute-start(bf16[64,128]{1,0:T(8,128)(2,1)S(1)} %convolution_convert_fusion.1), channel_id=1, source_target_pairs={{0,2},{1,3},{2,0},{3,1},{4,6},{5,7},{6,4},{7,5},{8,10},{9,11},{10,... | collective-permute-start | bytes 49160 | tf_op jit(solution)/shard_map/ppermute | solution.py:39
  22.7 0.1 collective-permute-start.6
  22.8 0.1 fusion.25
  23.0 4.5 %shard_map.101 = f32[128,256]{1,0:T(8,128)S(1)} custom-call(bf16[64,7296]{1,0:T(8,128)(2,1)S(1)} %pad_maximum_fusion.x, bf16[7168,2,256]{2,1,0:T(2,128)(2,1)} %bitcast.61), custom_call_target="tpu_custom_call" | custom-call | flops 469762048 | bytes 7340032 | tf_op jit(solution)/shard_map/pallas_call | solution.py:131
  27.5 0.1 select_reduce_fusion
  27.6 0.1 select_reduce_fusion.1
  27.8 0.2 fusion.7
  28.0 0.1 multiply_reduce_fusion
  28.1 0.3 copy-done.3
  28.4 0.2 convolution_convert_fusion
  28.6 0.5 collective-permute-start.9
  29.2 0.9 %collective-permute-done.9 = bf16[2,64,128]{2,1,0:T(8,128)(2,1)S(1)} collective-permute-done((bf16[2,64,128]{2,1,0:T(8,128)(2,1)S(1)}, bf16[2,64,128]{2,1,0:T(8,128)(2,1)S(1)}, u32[]{:S(2)}, u32[]{:S(2)}) %collective-permute-start.9) | collective-permute-done | bytes 32800 | tf_op jit(solution)/shard_map/ppermute | solution.py:39
  30.0 1.6 %collective-permute-start.10 = (bf16[64,128]{1,0:T(8,128)(2,1)S(1)}, bf16[64,128]{1,0:T(8,128)(2,1)S(1)}, u32[]{:S(2)}, u32[]{:S(2)}) collective-permute-start(bf16[64,128]{1,0:T(8,128)(2,1)S(1)} %dynamic-slice_bitcast_fusion.1), channel_id=1, source_target_pairs={{0,2},{1,3},{2,0},{3,1},{4,6},{5,7},{6,4},{7,5},{8,10},{9,11},{10,... | collective-permute-start | bytes 49160 | tf_op jit(solution)/shard_map/ppermute | solution.py:39
  31.6 2.6 %shard_map.102 = f32[64,7168]{1,0:T(8,128)S(1)} custom-call(bf16[64,256]{1,0:T(8,128)(2,1)S(1)} %get-tuple-element.21.hidden, bf16[256,7168]{1,0:T(8,128)(2,1)} %bitcast.62), custom_call_target="tpu_custom_call" | custom-call | flops 234881024 | bytes 3670016 | tf_op jit(solution)/shard_map/pallas_call | solution.py:163
  34.2 0.3 fusion.1.term
  34.6 0.1 collective-permute-start.15
  34.7 0.3 fusion.term
  35.1 0.5 collective-permute-start.11
  35.6 0.5 %collective-permute-done.15.received = bf16[32,3584]{1,0:T(8,128)(2,1)S(1)} collective-permute-done((bf16[32,3584]{1,0:T(8,128)(2,1)S(1)}, bf16[32,3584]{1,0:T(8,128)(2,1)S(1)}, u32[]{:S(2)}, u32[]{:S(2)}) %collective-permute-start.15) | collective-permute-done | bytes 229408 | tf_op jit(solution)/shard_map/ppermute | solution.py:39
  36.2 0.1 shard_map.104
  36.3 1.2 %collective-permute-start.16 = (bf16[16,3584]{1,0:T(8,128)(2,1)S(1)}, bf16[16,3584]{1,0:T(8,128)(2,1)S(1)}, u32[]{:S(2)}, u32[]{:S(2)}) collective-permute-start(bf16[16,3584]{1,0:T(8,128)(2,1)S(1)} %get-tuple-element.20), channel_id=1, source_target_pairs={{0,2},{1,5},{2,0},{3,7},{4,6},{5,1},{6,4},{7,3},{8,10},{9,13},{10,... | collective-permute-start | bytes 344072 | tf_op jit(solution)/shard_map/ppermute | solution.py:39
  37.4 0.1 shard_map.103
  37.5 1.0 %collective-permute-start.12 = (bf16[16,3584]{1,0:T(8,128)(2,1)S(1)}, bf16[16,3584]{1,0:T(8,128)(2,1)S(1)}, u32[]{:S(2)}, u32[]{:S(2)}) collective-permute-start(bf16[16,3584]{1,0:T(8,128)(2,1)S(1)} %get-tuple-element.18), channel_id=1, source_target_pairs={{0,2},{1,5},{2,0},{3,7},{4,6},{5,1},{6,4},{7,3},{8,10},{9,13},{10,... | collective-permute-start | bytes 344072 | tf_op jit(solution)/shard_map/ppermute | solution.py:39
  38.5 2.6 %collective-permute-done.16 = bf16[16,3584]{1,0:T(8,128)(2,1)S(1)} collective-permute-done((bf16[16,3584]{1,0:T(8,128)(2,1)S(1)}, bf16[16,3584]{1,0:T(8,128)(2,1)S(1)}, u32[]{:S(2)}, u32[]{:S(2)}) %collective-permute-start.16) | collective-permute-done | bytes 114720 | tf_op jit(solution)/shard_map/ppermute | solution.py:39
  41.2 1.7 %collective-permute-start.17 = (bf16[8,3584]{1,0:T(8,128)(2,1)S(1)}, bf16[8,3584]{1,0:T(8,128)(2,1)S(1)}, u32[]{:S(2)}, u32[]{:S(2)}) collective-permute-start(bf16[8,3584]{1,0:T(8,128)(2,1)S(1)} %broadcast_select_fusion.4), channel_id=1, source_target_pairs={{0,4},{1,3},{2,6},{3,1},{4,0},{5,7},{6,2},{7,5},{8,12},{9,11},{10,... | collective-permute-start | bytes 172040 | tf_op jit(solution)/shard_map/ppermute | solution.py:39
  42.9 1.2 %collective-permute-start.13 = (bf16[8,3584]{1,0:T(8,128)(2,1)S(1)}, bf16[8,3584]{1,0:T(8,128)(2,1)S(1)}, u32[]{:S(2)}, u32[]{:S(2)}) collective-permute-start(bf16[8,3584]{1,0:T(8,128)(2,1)S(1)} %broadcast_select_fusion.5), channel_id=1, source_target_pairs={{0,4},{1,3},{2,6},{3,1},{4,0},{5,7},{6,2},{7,5},{8,12},{9,11},{10,... | collective-permute-start | bytes 172040 | tf_op jit(solution)/shard_map/ppermute | solution.py:39
  44.1 1.3 %collective-permute-done.17 = bf16[8,3584]{1,0:T(8,128)(2,1)S(1)} collective-permute-done((bf16[8,3584]{1,0:T(8,128)(2,1)S(1)}, bf16[8,3584]{1,0:T(8,128)(2,1)S(1)}, u32[]{:S(2)}, u32[]{:S(2)}) %collective-permute-start.17) | collective-permute-done | bytes 57376 | tf_op jit(solution)/shard_map/ppermute | solution.py:39
  45.5 1.8 %collective-permute-start.18 = (bf16[4,3584]{1,0:T(4,128)(2,1)S(1)}, bf16[4,3584]{1,0:T(4,128)(2,1)S(1)}, u32[]{:S(2)}, u32[]{:S(2)}) collective-permute-start(bf16[4,3584]{1,0:T(4,128)(2,1)S(1)} %slice.123), channel_id=1, source_target_pairs={{0,8},{1,9},{2,10},{3,11},{4,12},{5,13},{6,14},{7,15},{8,0},{9,1},... | collective-permute-start | bytes 86024 | tf_op jit(solution)/shard_map/ppermute | solution.py:39
  47.4 2.0 %collective-permute-start.14 = (bf16[4,3584]{1,0:T(4,128)(2,1)S(1)}, bf16[4,3584]{1,0:T(4,128)(2,1)S(1)}, u32[]{:S(2)}, u32[]{:S(2)}) collective-permute-start(bf16[4,3584]{1,0:T(4,128)(2,1)S(1)} %slice.116), channel_id=1, source_target_pairs={{0,8},{1,9},{2,10},{3,11},{4,12},{5,13},{6,14},{7,15},{8,0},{9,1},... | collective-permute-start | bytes 86024 | tf_op jit(solution)/shard_map/ppermute | solution.py:39
  49.4 1.1 %collective-permute-done.18 = bf16[4,3584]{1,0:T(4,128)(2,1)S(1)} collective-permute-done((bf16[4,3584]{1,0:T(4,128)(2,1)S(1)}, bf16[4,3584]{1,0:T(4,128)(2,1)S(1)}, u32[]{:S(2)}, u32[]{:S(2)}) %collective-permute-start.18) | collective-permute-done | bytes 28704 | tf_op jit(solution)/shard_map/ppermute | solution.py:39
  50.5 1.7 %collective-permute-done.14 = bf16[4,3584]{1,0:T(4,128)(2,1)S(1)} collective-permute-done((bf16[4,3584]{1,0:T(4,128)(2,1)S(1)}, bf16[4,3584]{1,0:T(4,128)(2,1)S(1)}, u32[]{:S(2)}, u32[]{:S(2)}) %collective-permute-start.14) | collective-permute-done | bytes 28704 | tf_op jit(solution)/shard_map/ppermute | solution.py:39
  52.2 0.7 %maximum_bitcast_fusion.2 = bf16[1,4,7168]{2,1,0:T(4,128)(2,1)} fusion(bf16[4,3584]{1,0:T(4,128)(2,1)S(1)} %add_convert_fusion.4, bf16[4,3584]{1,0:T(4,128)(2,1)S(1)} %add_convert_fusion.5), kind=kLoop, calls=%fused_computation.48 | loop fusion | flops 114688 | bytes 114688 | tf_op jit(solution)/shard_map/broadcast_in_dim | solution.py:322
  (44 shorter events, 0.7 us)
Async XLA Ops:
  0.0 20.2 %copy-start = (bf16[1,7168,128]{2,1,0:T(8,128)(2,1)S(1)}, bf16[1,7168,128]{2,1,0:T(8,128)(2,1)}, u32[]{:S(2)}) copy-start(bf16[1,7168,128]{2,1,0:T(8,128)(2,1)} %param.16) | copy-start | bytes 5505028
  1.0 7.8 %collective-permute-start.2 = (bf16[4,7296]{1,0:T(4,128)(2,1)S(1)}, bf16[4,7296]{1,0:T(4,128)(2,1)S(1)}, u32[]{:S(2)}, u32[]{:S(2)}) collective-permute-start(bf16[4,7296]{1,0:T(4,128)(2,1)S(1)} %shard_map.100), channel_id=1, source_target_pairs={{0,12},{1,13},{2,14},{3,15},{4,8},{5,9},{6,10},{7,11},{8,4},{9,5},... | collective-permute-start | bytes 175112 | tf_op jit(solution)/shard_map/ppermute | solution.py:39
  6.1 4.3 %collective-permute-start.1 = (bf16[4,7296]{1,0:T(4,128)(2,1)S(1)}, bf16[4,7296]{1,0:T(4,128)(2,1)S(1)}, u32[]{:S(2)}, u32[]{:S(2)}) collective-permute-start(bf16[4,7296]{1,0:T(4,128)(2,1)S(1)} %shard_map.100), channel_id=1, source_target_pairs={{0,4},{1,5},{2,6},{3,7},{4,0},{5,1},{6,2},{7,3},{8,12},{9,13},{10,... | collective-permute-start | bytes 175112 | tf_op jit(solution)/shard_map/ppermute | solution.py:39
  6.1 5.5 %collective-permute-start = (bf16[4,7296]{1,0:T(4,128)(2,1)S(1)}, bf16[4,7296]{1,0:T(4,128)(2,1)S(1)}, u32[]{:S(2)}, u32[]{:S(2)}) collective-permute-start(bf16[4,7296]{1,0:T(4,128)(2,1)S(1)} %shard_map.100), channel_id=1, source_target_pairs={{0,8},{1,9},{2,10},{3,11},{4,12},{5,13},{6,14},{7,15},{8,0},{9,1},... | collective-permute-start | bytes 175112 | tf_op jit(solution)/shard_map/ppermute | solution.py:39
  6.7 4.9 %collective-permute-start.3 = (bf16[4,7296]{1,0:T(4,128)(2,1)S(1)}, bf16[4,7296]{1,0:T(4,128)(2,1)S(1)}, u32[]{:S(2)}, u32[]{:S(2)}) collective-permute-start(bf16[4,7296]{1,0:T(4,128)(2,1)S(1)} %shard_map.100), channel_id=1, source_target_pairs={{0,2},{1,3},{2,0},{3,1},{4,6},{5,7},{6,4},{7,5},{8,10},{9,11},{10,... | collective-permute-start | bytes 175112 | tf_op jit(solution)/shard_map/ppermute | solution.py:39
  11.7 6.1 %collective-permute-start.4 = (bf16[12,7296]{1,0:T(8,128)(2,1)S(1)}, bf16[12,7296]{1,0:T(8,128)(2,1)S(1)}, u32[]{:S(2)}, u32[]{:S(2)}) collective-permute-start(bf16[12,7296]{1,0:T(8,128)(2,1)S(1)} %pad_maximum_fusion.2), channel_id=1, source_target_pairs={{0,2},{1,3},{2,0},{3,1},{4,6},{5,7},{6,4},{7,5},{8,10},{9,11},{10,... | collective-permute-start | bytes 525320 | tf_op jit(solution)/shard_map/ppermute | solution.py:39
  18.1 1.9 %collective-permute-start.5 = (bf16[32,7296]{1,0:T(8,128)(2,1)S(1)}, bf16[32,7296]{1,0:T(8,128)(2,1)S(1)}, u32[]{:S(2)}, u32[]{:S(2)}) collective-permute-start(bf16[32,7296]{1,0:T(8,128)(2,1)S(1)} %pad_maximum_fusion.1), channel_id=1, source_target_pairs={{0,1},{1,0},{2,3},{3,2},{4,5},{5,4},{6,7},{7,6},{8,9},{9,8},{10,11... | collective-permute-start | bytes 1400840 | tf_op jit(solution)/shard_map/ppermute | solution.py:39
  20.9 6.8 %collective-permute-start.8 = (bf16[64,128]{1,0:T(8,128)(2,1)S(1)}, bf16[64,128]{1,0:T(8,128)(2,1)S(1)}, u32[]{:S(2)}, u32[]{:S(2)}) collective-permute-start(bf16[64,128]{1,0:T(8,128)(2,1)S(1)} %convolution_convert_fusion.1), channel_id=1, source_target_pairs={{0,3},{1,2},{2,1},{3,0},{4,7},{5,6},{6,5},{7,4},{8,11},{9,10},{10,... | collective-permute-start | bytes 49160 | tf_op jit(solution)/shard_map/ppermute | solution.py:39
  22.2 5.5 %collective-permute-start.7 = (bf16[64,128]{1,0:T(8,128)(2,1)S(1)}, bf16[64,128]{1,0:T(8,128)(2,1)S(1)}, u32[]{:S(2)}, u32[]{:S(2)}) collective-permute-start(bf16[64,128]{1,0:T(8,128)(2,1)S(1)} %convolution_convert_fusion.1), channel_id=1, source_target_pairs={{0,2},{1,3},{2,0},{3,1},{4,6},{5,7},{6,4},{7,5},{8,10},{9,11},{10,... | collective-permute-start | bytes 49160 | tf_op jit(solution)/shard_map/ppermute | solution.py:39
  22.7 5.0 %collective-permute-start.6 = (bf16[64,128]{1,0:T(8,128)(2,1)S(1)}, bf16[64,128]{1,0:T(8,128)(2,1)S(1)}, u32[]{:S(2)}, u32[]{:S(2)}) collective-permute-start(bf16[64,128]{1,0:T(8,128)(2,1)S(1)} %convolution_convert_fusion.1), channel_id=1, source_target_pairs={{0,1},{1,0},{2,3},{3,2},{4,5},{5,4},{6,7},{7,6},{8,9},{9,8},{10,11... | collective-permute-start | bytes 49160 | tf_op jit(solution)/shard_map/ppermute | solution.py:39
  23.0 4.5 %copy-start.4 = (s32[16]{0:T(128)S(1)}, s32[16]{0:T(128)}, u32[]{:S(2)}) copy-start(s32[16]{0:T(128)} %param.13) | copy-start | bytes 196
  23.0 4.8 %copy-start.2 = (bf16[1,4,128,2,256]{4,3,2,1,0:T(2,128)(2,1)S(1)}, bf16[1,4,128,2,256]{4,3,2,1,0:T(2,128)(2,1)}, u32[]{:S(2)}) copy-start(bf16[1,4,128,2,256]{4,3,2,1,0:T(2,128)(2,1)} %param.17) | copy-start | bytes 1572868
  27.5 1.0 %copy-start.3 = (bf16[1,4,256,128]{3,2,1,0:T(8,128)(2,1)S(1)}, bf16[1,4,256,128]{3,2,1,0:T(8,128)(2,1)}, u32[]{:S(2)}) copy-start(bf16[1,4,256,128]{3,2,1,0:T(8,128)(2,1)} %param.18) | copy-start | bytes 786436
  28.6 1.4 %collective-permute-start.9 = (bf16[2,64,128]{2,1,0:T(8,128)(2,1)S(1)}, bf16[2,64,128]{2,1,0:T(8,128)(2,1)S(1)}, u32[]{:S(2)}, u32[]{:S(2)}) collective-permute-start(bf16[2,64,128]{2,1,0:T(8,128)(2,1)S(1)} %dynamic-slice_bitcast_fusion), channel_id=1, source_target_pairs={{0,1},{1,0},{2,3},{3,2},{4,5},{5,4},{6,7},{7,6},{8,9},{9,8},{10,11... | collective-permute-start | bytes 98312 | tf_op jit(solution)/shard_map/ppermute | solution.py:39
  30.0 4.2 %collective-permute-start.10 = (bf16[64,128]{1,0:T(8,128)(2,1)S(1)}, bf16[64,128]{1,0:T(8,128)(2,1)S(1)}, u32[]{:S(2)}, u32[]{:S(2)}) collective-permute-start(bf16[64,128]{1,0:T(8,128)(2,1)S(1)} %dynamic-slice_bitcast_fusion.1), channel_id=1, source_target_pairs={{0,2},{1,3},{2,0},{3,1},{4,6},{5,7},{6,4},{7,5},{8,10},{9,11},{10,... | collective-permute-start | bytes 49160 | tf_op jit(solution)/shard_map/ppermute | solution.py:39
  31.6 2.6 %copy-start.1 = (bf16[1,128,7168]{2,1,0:T(8,128)(2,1)S(1)}, bf16[1,128,7168]{2,1,0:T(8,128)(2,1)}, u32[]{:S(2)}) copy-start(bf16[1,128,7168]{2,1,0:T(8,128)(2,1)} %param.19) | copy-start | bytes 5505028
  34.6 1.6 %collective-permute-start.15 = (bf16[32,3584]{1,0:T(8,128)(2,1)S(1)}, bf16[32,3584]{1,0:T(8,128)(2,1)S(1)}, u32[]{:S(2)}, u32[]{:S(2)}) collective-permute-start(bf16[32,3584]{1,0:T(8,128)(2,1)S(1)} %slice_select_fusion), channel_id=1, source_target_pairs={{0,1},{1,0},{2,3},{3,2},{4,5},{5,4},{6,7},{7,6},{8,9},{9,8},{10,11... | collective-permute-start | bytes 688136 | tf_op jit(solution)/shard_map/ppermute | solution.py:39
  35.1 2.3 %collective-permute-start.11 = (bf16[32,3584]{1,0:T(8,128)(2,1)S(1)}, bf16[32,3584]{1,0:T(8,128)(2,1)S(1)}, u32[]{:S(2)}, u32[]{:S(2)}) collective-permute-start(bf16[32,3584]{1,0:T(8,128)(2,1)S(1)} %slice_select_fusion.1), channel_id=1, source_target_pairs={{0,1},{1,0},{2,3},{3,2},{4,5},{5,4},{6,7},{7,6},{8,9},{9,8},{10,11... | collective-permute-start | bytes 688136 | tf_op jit(solution)/shard_map/ppermute | solution.py:39
  36.3 4.9 %collective-permute-start.16 = (bf16[16,3584]{1,0:T(8,128)(2,1)S(1)}, bf16[16,3584]{1,0:T(8,128)(2,1)S(1)}, u32[]{:S(2)}, u32[]{:S(2)}) collective-permute-start(bf16[16,3584]{1,0:T(8,128)(2,1)S(1)} %get-tuple-element.20), channel_id=1, source_target_pairs={{0,2},{1,5},{2,0},{3,7},{4,6},{5,1},{6,4},{7,3},{8,10},{9,13},{10,... | collective-permute-start | bytes 344072 | tf_op jit(solution)/shard_map/ppermute | solution.py:39
  37.5 5.3 %collective-permute-start.12 = (bf16[16,3584]{1,0:T(8,128)(2,1)S(1)}, bf16[16,3584]{1,0:T(8,128)(2,1)S(1)}, u32[]{:S(2)}, u32[]{:S(2)}) collective-permute-start(bf16[16,3584]{1,0:T(8,128)(2,1)S(1)} %get-tuple-element.18), channel_id=1, source_target_pairs={{0,2},{1,5},{2,0},{3,7},{4,6},{5,1},{6,4},{7,3},{8,10},{9,13},{10,... | collective-permute-start | bytes 344072 | tf_op jit(solution)/shard_map/ppermute | solution.py:39
  41.2 4.2 %collective-permute-start.17 = (bf16[8,3584]{1,0:T(8,128)(2,1)S(1)}, bf16[8,3584]{1,0:T(8,128)(2,1)S(1)}, u32[]{:S(2)}, u32[]{:S(2)}) collective-permute-start(bf16[8,3584]{1,0:T(8,128)(2,1)S(1)} %broadcast_select_fusion.4), channel_id=1, source_target_pairs={{0,4},{1,3},{2,6},{3,1},{4,0},{5,7},{6,2},{7,5},{8,12},{9,11},{10,... | collective-permute-start | bytes 172040 | tf_op jit(solution)/shard_map/ppermute | solution.py:39
  42.9 4.4 %collective-permute-start.13 = (bf16[8,3584]{1,0:T(8,128)(2,1)S(1)}, bf16[8,3584]{1,0:T(8,128)(2,1)S(1)}, u32[]{:S(2)}, u32[]{:S(2)}) collective-permute-start(bf16[8,3584]{1,0:T(8,128)(2,1)S(1)} %broadcast_select_fusion.5), channel_id=1, source_target_pairs={{0,4},{1,3},{2,6},{3,1},{4,0},{5,7},{6,2},{7,5},{8,12},{9,11},{10,... | collective-permute-start | bytes 172040 | tf_op jit(solution)/shard_map/ppermute | solution.py:39
  45.5 5.0 %collective-permute-start.18 = (bf16[4,3584]{1,0:T(4,128)(2,1)S(1)}, bf16[4,3584]{1,0:T(4,128)(2,1)S(1)}, u32[]{:S(2)}, u32[]{:S(2)}) collective-permute-start(bf16[4,3584]{1,0:T(4,128)(2,1)S(1)} %slice.123), channel_id=1, source_target_pairs={{0,8},{1,9},{2,10},{3,11},{4,12},{5,13},{6,14},{7,15},{8,0},{9,1},... | collective-permute-start | bytes 86024 | tf_op jit(solution)/shard_map/ppermute | solution.py:39
  47.4 4.8 %collective-permute-start.14 = (bf16[4,3584]{1,0:T(4,128)(2,1)S(1)}, bf16[4,3584]{1,0:T(4,128)(2,1)S(1)}, u32[]{:S(2)}, u32[]{:S(2)}) collective-permute-start(bf16[4,3584]{1,0:T(4,128)(2,1)S(1)} %slice.116), channel_id=1, source_target_pairs={{0,8},{1,9},{2,10},{3,11},{4,12},{5,13},{6,14},{7,15},{8,0},{9,1},... | collective-permute-start | bytes 86024 | tf_op jit(solution)/shard_map/ppermute | solution.py:39

commit v25 on v24

--- a/solution.py
+++ b/solution.py
@@ -11,7 +11,6 @@
 
 CHUNKS = 2
 PIECES = (1, 2, 4, 4)
-DOWN_PIECES = (1, 3)
 VMEM = pl.BlockSpec(memory_space=pltpu.VMEM)
 HBM = pl.BlockSpec(memory_space=pltpu.HBM)
 
@@ -139,36 +138,6 @@
             flops=4 * x.shape[0] * depth * columns, bytes_accessed=2 * base.size, transcendentals=0
         ),
     )(x, in_hbm(base))
-
-
-def down_kernel(hidden, base, out, weights, sems):
-    step = 1024
-    copies = {
-        low: pltpu.make_async_copy(
-            base.at[:, pl.ds(low, high - low)], weights.at[:, pl.ds(low, high - low)], sems.at[i]
-        )
-        for i, (low, high) in enumerate(piece_bounds(base.shape[1], step, DOWN_PIECES))
-    }
-    for copy in copies.values():
-        copy.start()
-    for k in range(0, base.shape[1], step):
-        if k in copies:
-            copies[k].wait()
-        part = pl.ds(k, step)
-        out[:, part] = jnp.dot(hidden[...], weights[:, part], preferred_element_type=jnp.float32)
-
-
-def down_product(hidden, base):
-    rows, width = hidden.shape[0], base.shape[1]
-    return pl.pallas_call(
-        down_kernel,
-        out_shape=jax.ShapeDtypeStruct((rows, width), jnp.float32),
-        in_specs=[VMEM, HBM],
-        out_specs=VMEM,
-        scratch_shapes=[pltpu.VMEM(base.shape, base.dtype), pltpu.SemaphoreType.DMA((len(DOWN_PIECES) + 1,))],
-        compiler_params=pltpu.CompilerParams(vmem_limit_bytes=16 << 20),
-        cost_estimate=pl.CostEstimate(flops=2 * rows * base.size, bytes_accessed=2 * base.size, transcendentals=0),
-    )(hidden, in_hbm(base))
 
 
 def part_kernel(bit, term, received, *refs):
@@ -259,6 +228,16 @@
     codes = jnp.dot(rows[:, :width], code_table, preferred_element_type=jnp.float32).astype(jnp.bfloat16)
     projected = gate_up_product(held, base_in[0])
 
+    codes = jnp.stack([codes if m == 0 else trade(codes, (0, m), (0, m)) for m in range(members)])
+    by_slot = jnp.stack([lax.dynamic_index_in_dim(codes, s ^ me, 0, keepdims=False) for s in range(members)])
+
+    lifted = jnp.einsum("srk,skgf->srgf", by_slot, delta_mid[0], preferred_element_type=jnp.float32)
+    total = held.shape[0]
+    hidden = jax.nn.silu(projected[None, :total] + lifted[:, :, 0]) * (projected[None, total:] + lifted[:, :, 1])
+    partial_codes = jnp.einsum(
+        "srf,sfk->srk", hidden.astype(jnp.bfloat16), delta_down[0], preferred_element_type=jnp.float32
+    ).astype(jnp.bfloat16)
+    hidden, rows, partial_codes = lax.optimization_barrier((hidden, rows, partial_codes))
     side = by_rows(rows[:, width:])
     all_routes = side[:, :top].astype(jnp.int32)
     numerator = side[:, top : 2 * top].astype(jnp.float32)
@@ -268,17 +247,8 @@
     scale = jnp.sum(
         jnp.where(position[None] == target[:, None, None], weight[None].astype(jnp.float32), 0.0), axis=-1
     )
-
-    codes = jnp.stack([codes if m == 0 else trade(codes, (0, m), (0, m)) for m in range(members)])
-    by_slot = jnp.stack([lax.dynamic_index_in_dim(codes, s ^ me, 0, keepdims=False) for s in range(members)])
-
-    lifted = jnp.einsum("srk,skgf->srgf", by_slot, delta_mid[0], preferred_element_type=jnp.float32)
-    total = held.shape[0]
-    hidden = jax.nn.silu(projected[None, :total] + lifted[:, :, 0]) * (projected[None, total:] + lifted[:, :, 1])
     hidden_sum = jnp.sum(scale[:, :, None] * hidden, axis=0).astype(jnp.bfloat16)
-    partial_codes = jnp.einsum(
-        "srf,sfk->srk", hidden.astype(jnp.bfloat16), delta_down[0], preferred_element_type=jnp.float32
-    ).astype(jnp.bfloat16)
+
     by_core = partial_codes.reshape(chips, 2, *partial_codes.shape[1:])
     kept, sent = (lax.dynamic_index_in_dim(by_core, c, 1, keepdims=False) for c in (core, 1 - core))
     by_chip = add(kept, trade(sent, (0, 1), (0, 1)))
@@ -290,7 +260,7 @@
     own_scale = lax.dynamic_index_in_dim(scale, me, 0, keepdims=False)
     scaled = (own_scale[:, None] * lowrank).astype(jnp.bfloat16)
 
-    base = down_product(hidden_sum, base_down[0])
+    base = jnp.dot(hidden_sum, base_down[0], preferred_element_type=jnp.float32)
 
     half, step = base.shape[0] // 2, width // CHUNKS
     outputs = []

time: 53 us -> 55 us (1.038)
  matrix products: 1.52 us -> 4.44 us
  Pallas kernels: 8.22 us -> 5.61 us
  waiting for transfers between devices: 17.6 us -> 18.6 us
    dot_general x0 -> x1, matrix products: none -> 2.93 us  [local(): base = jnp.dot(hidden_sum, base_down[0], preferred_element_type=jnp.float32)]
    pallas_call x1 -> x0, Pallas kernels: 2.59 us -> none  [down_product(): pl.pallas_call(down_kernel, out_shape=jax.ShapeDtypeStruct((rows, width),...]
    ppermute x19, waiting for transfers between devices: 17.6 us -> 18.6 us  [trade(): return lax.ppermute(value, ('expert', 'tensor'), pairs)]
  transfers between devices with their start and end apart: 19 -> 19, of which waited for: 11 -> 11; matrix products, arithmetic and copies ran while one was open for 2% -> 7% of each run, Pallas kernels for 14% -> 8%
where the time goes in v25:
time: 55 us; the launch traced here: 54.8 us
  starting transfers between devices  23 us (42%)
  waiting for transfers between devices  18.6 us (34%)
  Pallas kernels  5.61 us (10%)
  matrix products  4.44 us (8%)
  other arithmetic  2.11 us (4%)
  local copies, waits for them, and re-layouts  0.74 us (1%)
    ppermute x19, starting transfers between devices, trade(): return lax.ppermute(value, ('expert', 'tensor'), pairs)  23 us
    ppermute x19, waiting for transfers between devices, trade(): return lax.ppermute(value, ('expert', 'tensor'), pairs)  18.6 us
    pallas_call x1, Pallas kernels, gate_up_product(): pl.pallas_call(gate_up_kernel, out_shape=jax.ShapeDtypeStruct((2 * x.shap...  4.44 us
    dot_general x1, matrix products, local(): base = jnp.dot(hidden_sum, base_down[0], preferred_element_type=jnp.float32)  2.93 us
  transfers between devices with their start and end apart: 19, of which 11 were waited for; matrix products, arithmetic and copies ran while one was open for 7% of the time, Pallas kernels for 8%

profile of v25, /device:TPU:0, one launch (start us, length us, event | category | flops | bytes accessed | tf_op | source)
XLA Modules:
  0.0 54.8 jit_solution(3723715425008066439)
XLA Ops:
  0.0 1.0 %shard_map.100 = bf16[4,7296]{1,0:T(4,128)(2,1)S(1)} custom-call(bf16[4,7168]{1,0:T(4,128)(2,1)} %bitcast.69, s32[4,8]{1,0:T(4,128)} %bitcast.70, s32[4,8]{1,0:T(4,128)} %bitcast.71), custom_call_target="tpu_custom_call" | custom-call | flops 20000000000 | bytes 114688 | tf_op jit(solution)/shard_map/pallas_call | solution.py:76
  1.0 5.1 %collective-permute-start.2 = (bf16[4,7296]{1,0:T(4,128)(2,1)S(1)}, bf16[4,7296]{1,0:T(4,128)(2,1)S(1)}, u32[]{:S(2)}, u32[]{:S(2)}) collective-permute-start(bf16[4,7296]{1,0:T(4,128)(2,1)S(1)} %shard_map.100), channel_id=1, source_target_pairs={{0,12},{1,13},{2,14},{3,15},{4,8},{5,9},{6,10},{7,11},{8,4},{9,5},... | collective-permute-start | bytes 175112 | tf_op jit(solution)/shard_map/ppermute | solution.py:38
  6.1 0.6 %collective-permute-start = (bf16[4,7296]{1,0:T(4,128)(2,1)S(1)}, bf16[4,7296]{1,0:T(4,128)(2,1)S(1)}, u32[]{:S(2)}, u32[]{:S(2)}) collective-permute-start(bf16[4,7296]{1,0:T(4,128)(2,1)S(1)} %shard_map.100), channel_id=1, source_target_pairs={{0,8},{1,9},{2,10},{3,11},{4,12},{5,13},{6,14},{7,15},{8,0},{9,1},... | collective-permute-start | bytes 175112 | tf_op jit(solution)/shard_map/ppermute | solution.py:38
  6.7 1.6 %collective-permute-start.3 = (bf16[4,7296]{1,0:T(4,128)(2,1)S(1)}, bf16[4,7296]{1,0:T(4,128)(2,1)S(1)}, u32[]{:S(2)}, u32[]{:S(2)}) collective-permute-start(bf16[4,7296]{1,0:T(4,128)(2,1)S(1)} %shard_map.100), channel_id=1, source_target_pairs={{0,2},{1,3},{2,0},{3,1},{4,6},{5,7},{6,4},{7,5},{8,10},{9,11},{10,... | collective-permute-start | bytes 175112 | tf_op jit(solution)/shard_map/ppermute | solution.py:38
  8.4 0.4 collective-permute-done.2
  8.8 1.7 %collective-permute-done.1 = bf16[4,7296]{1,0:T(4,128)(2,1)S(1)} collective-permute-done((bf16[4,7296]{1,0:T(4,128)(2,1)S(1)}, bf16[4,7296]{1,0:T(4,128)(2,1)S(1)}, u32[]{:S(2)}, u32[]{:S(2)}) %collective-permute-start.1) | collective-permute-done | bytes 58400 | tf_op jit(solution)/shard_map/ppermute | solution.py:38
  10.4 1.1 %collective-permute-done = bf16[4,7296]{1,0:T(4,128)(2,1)S(1)} collective-permute-done((bf16[4,7296]{1,0:T(4,128)(2,1)S(1)}, bf16[4,7296]{1,0:T(4,128)(2,1)S(1)}, u32[]{:S(2)}, u32[]{:S(2)}) %collective-permute-start) | collective-permute-done | bytes 58400 | tf_op jit(solution)/shard_map/ppermute | solution.py:38
  11.6 0.1 pad_maximum_fusion.2
  11.7 1.6 %collective-permute-start.4 = (bf16[12,7296]{1,0:T(8,128)(2,1)S(1)}, bf16[12,7296]{1,0:T(8,128)(2,1)S(1)}, u32[]{:S(2)}, u32[]{:S(2)}) collective-permute-start(bf16[12,7296]{1,0:T(8,128)(2,1)S(1)} %pad_maximum_fusion.2), channel_id=1, source_target_pairs={{0,2},{1,3},{2,0},{3,1},{4,6},{5,7},{6,4},{7,5},{8,10},{9,11},{10,... | collective-permute-start | bytes 525320 | tf_op jit(solution)/shard_map/ppermute | solution.py:38
  13.3 4.6 %collective-permute-done.4 = bf16[12,7296]{1,0:T(8,128)(2,1)S(1)} collective-permute-done((bf16[12,7296]{1,0:T(8,128)(2,1)S(1)}, bf16[12,7296]{1,0:T(8,128)(2,1)S(1)}, u32[]{:S(2)}, u32[]{:S(2)}) %collective-permute-start.4) | collective-permute-done | bytes 175136 | tf_op jit(solution)/shard_map/ppermute | solution.py:38
  17.8 0.2 broadcast_select_fusion.3
  18.2 1.7 %collective-permute-done.5 = bf16[32,7296]{1,0:T(8,128)(2,1)S(1)} collective-permute-done((bf16[32,7296]{1,0:T(8,128)(2,1)S(1)}, bf16[32,7296]{1,0:T(8,128)(2,1)S(1)}, u32[]{:S(2)}, u32[]{:S(2)}) %collective-permute-start.5) | collective-permute-done | bytes 466976 | tf_op jit(solution)/shard_map/ppermute | solution.py:38
  20.0 0.2 broadcast_select_fusion.1
  20.2 0.5 convolution_convert_fusion.1
  20.7 1.3 %collective-permute-start.8 = (bf16[64,128]{1,0:T(8,128)(2,1)S(1)}, bf16[64,128]{1,0:T(8,128)(2,1)S(1)}, u32[]{:S(2)}, u32[]{:S(2)}) collective-permute-start(bf16[64,128]{1,0:T(8,128)(2,1)S(1)} %convolution_convert_fusion.1), channel_id=1, source_target_pairs={{0,3},{1,2},{2,1},{3,0},{4,7},{5,6},{6,5},{7,4},{8,11},{9,10},{10,... | collective-permute-start | bytes 49160 | tf_op jit(solution)/shard_map/ppermute | solution.py:38
  22.0 0.5 collective-permute-start.7
  22.5 0.1 collective-permute-start.6
  22.6 4.4 %shard_map.101 = f32[128,256]{1,0:T(8,128)S(1)} custom-call(bf16[64,7296]{1,0:T(8,128)(2,1)S(1)} %pad_maximum_fusion.x, bf16[7168,2,256]{2,1,0:T(2,128)(2,1)} %bitcast.61), custom_call_target="tpu_custom_call" | custom-call | flops 469762048 | bytes 7340032 | tf_op jit(solution)/shard_map/pallas_call | solution.py:130
  27.2 0.2 fusion.9
  27.4 0.1 fusion.12
  27.5 0.5 copy-done.3
  28.0 0.2 convolution_convert_fusion
  28.2 0.2 convert_reduce_fusion
  28.4 0.1 fusion.28
  28.6 0.5 collective-permute-start.9
  29.1 0.1 select_reduce_fusion
  29.2 0.1 select_reduce_fusion.1
  29.3 0.1 multiply_reduce_fusion
  29.4 2.9 %fusion.2 = f32[64,7168]{1,0:T(8,128)S(1)} fusion(bf16[1,256,7168]{2,1,0:T(8,128)(2,1)} %param.15, bf16[64,256]{1,0:T(8,128)(2,1)S(1)} %multiply_reduce_fusion), kind=kOutput, calls=%fused_computation.4 | convolution fusion | flops 234881024 | bytes 5537792 | tf_op jit(solution)/shard_map/dot_general | solution.py:263
  32.4 1.6 %collective-permute-start.10 = (bf16[64,128]{1,0:T(8,128)(2,1)S(1)}, bf16[64,128]{1,0:T(8,128)(2,1)S(1)}, u32[]{:S(2)}, u32[]{:S(2)}) collective-permute-start(bf16[64,128]{1,0:T(8,128)(2,1)S(1)} %dynamic-slice_bitcast_fusion.1), channel_id=1, source_target_pairs={{0,2},{1,3},{2,0},{3,1},{4,6},{5,7},{6,4},{7,5},{8,10},{9,11},{10,... | collective-permute-start | bytes 49160 | tf_op jit(solution)/shard_map/ppermute | solution.py:38
  33.9 2.2 %collective-permute-done.10 = bf16[64,128]{1,0:T(8,128)(2,1)S(1)} collective-permute-done((bf16[64,128]{1,0:T(8,128)(2,1)S(1)}, bf16[64,128]{1,0:T(8,128)(2,1)S(1)}, u32[]{:S(2)}, u32[]{:S(2)}) %collective-permute-start.10) | collective-permute-done | bytes 16416 | tf_op jit(solution)/shard_map/ppermute | solution.py:38
  36.2 0.3 fusion.1.term
  36.6 0.3 fusion.term
  37.0 0.6 %collective-permute-start.11 = (bf16[32,3584]{1,0:T(8,128)(2,1)S(1)}, bf16[32,3584]{1,0:T(8,128)(2,1)S(1)}, u32[]{:S(2)}, u32[]{:S(2)}) collective-permute-start(bf16[32,3584]{1,0:T(8,128)(2,1)S(1)} %slice_select_fusion.1), channel_id=1, source_target_pairs={{0,1},{1,0},{2,3},{3,2},{4,5},{5,4},{6,7},{7,6},{8,9},{9,8},{10,11... | collective-permute-start | bytes 688136 | tf_op jit(solution)/shard_map/ppermute | solution.py:38
  37.6 0.5 collective-permute-done.15.received
  38.1 0.1 shard_map.103
  38.2 1.6 %collective-permute-start.16 = (bf16[16,3584]{1,0:T(8,128)(2,1)S(1)}, bf16[16,3584]{1,0:T(8,128)(2,1)S(1)}, u32[]{:S(2)}, u32[]{:S(2)}) collective-permute-start(bf16[16,3584]{1,0:T(8,128)(2,1)S(1)} %get-tuple-element.26), channel_id=1, source_target_pairs={{0,2},{1,5},{2,0},{3,7},{4,6},{5,1},{6,4},{7,3},{8,10},{9,13},{10,... | collective-permute-start | bytes 344072 | tf_op jit(solution)/shard_map/ppermute | solution.py:38
  39.8 0.1 shard_map.102
  39.9 0.6 %collective-permute-start.12 = (bf16[16,3584]{1,0:T(8,128)(2,1)S(1)}, bf16[16,3584]{1,0:T(8,128)(2,1)S(1)}, u32[]{:S(2)}, u32[]{:S(2)}) collective-permute-start(bf16[16,3584]{1,0:T(8,128)(2,1)S(1)} %get-tuple-element.24), channel_id=1, source_target_pairs={{0,2},{1,5},{2,0},{3,7},{4,6},{5,1},{6,4},{7,3},{8,10},{9,13},{10,... | collective-permute-start | bytes 344072 | tf_op jit(solution)/shard_map/ppermute | solution.py:38
  40.5 2.6 %collective-permute-done.16 = bf16[16,3584]{1,0:T(8,128)(2,1)S(1)} collective-permute-done((bf16[16,3584]{1,0:T(8,128)(2,1)S(1)}, bf16[16,3584]{1,0:T(8,128)(2,1)S(1)}, u32[]{:S(2)}, u32[]{:S(2)}) %collective-permute-start.16) | collective-permute-done | bytes 114720 | tf_op jit(solution)/shard_map/ppermute | solution.py:38
  43.1 1.7 %collective-permute-start.17 = (bf16[8,3584]{1,0:T(8,128)(2,1)S(1)}, bf16[8,3584]{1,0:T(8,128)(2,1)S(1)}, u32[]{:S(2)}, u32[]{:S(2)}) collective-permute-start(bf16[8,3584]{1,0:T(8,128)(2,1)S(1)} %broadcast_select_fusion.4), channel_id=1, source_target_pairs={{0,4},{1,3},{2,6},{3,1},{4,0},{5,7},{6,2},{7,5},{8,12},{9,11},{10,... | collective-permute-start | bytes 172040 | tf_op jit(solution)/shard_map/ppermute | solution.py:38
  44.9 1.6 %collective-permute-start.13 = (bf16[8,3584]{1,0:T(8,128)(2,1)S(1)}, bf16[8,3584]{1,0:T(8,128)(2,1)S(1)}, u32[]{:S(2)}, u32[]{:S(2)}) collective-permute-start(bf16[8,3584]{1,0:T(8,128)(2,1)S(1)} %broadcast_select_fusion.5), channel_id=1, source_target_pairs={{0,4},{1,3},{2,6},{3,1},{4,0},{5,7},{6,2},{7,5},{8,12},{9,11},{10,... | collective-permute-start | bytes 172040 | tf_op jit(solution)/shard_map/ppermute | solution.py:38
  46.5 0.9 %collective-permute-done.17 = bf16[8,3584]{1,0:T(8,128)(2,1)S(1)} collective-permute-done((bf16[8,3584]{1,0:T(8,128)(2,1)S(1)}, bf16[8,3584]{1,0:T(8,128)(2,1)S(1)}, u32[]{:S(2)}, u32[]{:S(2)}) %collective-permute-start.17) | collective-permute-done | bytes 57376 | tf_op jit(solution)/shard_map/ppermute | solution.py:38
  47.4 1.9 %collective-permute-start.18 = (bf16[4,3584]{1,0:T(4,128)(2,1)S(1)}, bf16[4,3584]{1,0:T(4,128)(2,1)S(1)}, u32[]{:S(2)}, u32[]{:S(2)}) collective-permute-start(bf16[4,3584]{1,0:T(4,128)(2,1)S(1)} %slice.123), channel_id=1, source_target_pairs={{0,8},{1,9},{2,10},{3,11},{4,12},{5,13},{6,14},{7,15},{8,0},{9,1},... | collective-permute-start | bytes 86024 | tf_op jit(solution)/shard_map/ppermute | solution.py:38
  49.3 2.0 %collective-permute-start.14 = (bf16[4,3584]{1,0:T(4,128)(2,1)S(1)}, bf16[4,3584]{1,0:T(4,128)(2,1)S(1)}, u32[]{:S(2)}, u32[]{:S(2)}) collective-permute-start(bf16[4,3584]{1,0:T(4,128)(2,1)S(1)} %slice.116), channel_id=1, source_target_pairs={{0,8},{1,9},{2,10},{3,11},{4,12},{5,13},{6,14},{7,15},{8,0},{9,1},... | collective-permute-start | bytes 86024 | tf_op jit(solution)/shard_map/ppermute | solution.py:38
  51.4 1.1 %collective-permute-done.18 = bf16[4,3584]{1,0:T(4,128)(2,1)S(1)} collective-permute-done((bf16[4,3584]{1,0:T(4,128)(2,1)S(1)}, bf16[4,3584]{1,0:T(4,128)(2,1)S(1)}, u32[]{:S(2)}, u32[]{:S(2)}) %collective-permute-start.18) | collective-permute-done | bytes 28704 | tf_op jit(solution)/shard_map/ppermute | solution.py:38
  52.5 1.7 %collective-permute-done.14 = bf16[4,3584]{1,0:T(4,128)(2,1)S(1)} collective-permute-done((bf16[4,3584]{1,0:T(4,128)(2,1)S(1)}, bf16[4,3584]{1,0:T(4,128)(2,1)S(1)}, u32[]{:S(2)}, u32[]{:S(2)}) %collective-permute-start.14) | collective-permute-done | bytes 28704 | tf_op jit(solution)/shard_map/ppermute | solution.py:38
  54.2 0.7 %maximum_bitcast_fusion.2 = bf16[1,4,7168]{2,1,0:T(4,128)(2,1)} fusion(bf16[4,3584]{1,0:T(4,128)(2,1)S(1)} %add_convert_fusion.4, bf16[4,3584]{1,0:T(4,128)(2,1)S(1)} %add_convert_fusion.5), kind=kLoop, calls=%fused_computation.50 | loop fusion | flops 114688 | bytes 114688 | tf_op jit(solution)/shard_map/broadcast_in_dim | solution.py:292
  (45 shorter events, 0.8 us)
Async XLA Ops:
  0.0 20.2 %copy-start = (bf16[1,7168,128]{2,1,0:T(8,128)(2,1)S(1)}, bf16[1,7168,128]{2,1,0:T(8,128)(2,1)}, u32[]{:S(2)}) copy-start(bf16[1,7168,128]{2,1,0:T(8,128)(2,1)} %param.16) | copy-start | bytes 5505028
  1.0 7.8 %collective-permute-start.2 = (bf16[4,7296]{1,0:T(4,128)(2,1)S(1)}, bf16[4,7296]{1,0:T(4,128)(2,1)S(1)}, u32[]{:S(2)}, u32[]{:S(2)}) collective-permute-start(bf16[4,7296]{1,0:T(4,128)(2,1)S(1)} %shard_map.100), channel_id=1, source_target_pairs={{0,12},{1,13},{2,14},{3,15},{4,8},{5,9},{6,10},{7,11},{8,4},{9,5},... | collective-permute-start | bytes 175112 | tf_op jit(solution)/shard_map/ppermute | solution.py:38
  6.1 4.3 %collective-permute-start.1 = (bf16[4,7296]{1,0:T(4,128)(2,1)S(1)}, bf16[4,7296]{1,0:T(4,128)(2,1)S(1)}, u32[]{:S(2)}, u32[]{:S(2)}) collective-permute-start(bf16[4,7296]{1,0:T(4,128)(2,1)S(1)} %shard_map.100), channel_id=1, source_target_pairs={{0,4},{1,5},{2,6},{3,7},{4,0},{5,1},{6,2},{7,3},{8,12},{9,13},{10,... | collective-permute-start | bytes 175112 | tf_op jit(solution)/shard_map/ppermute | solution.py:38
  6.1 5.5 %collective-permute-start = (bf16[4,7296]{1,0:T(4,128)(2,1)S(1)}, bf16[4,7296]{1,0:T(4,128)(2,1)S(1)}, u32[]{:S(2)}, u32[]{:S(2)}) collective-permute-start(bf16[4,7296]{1,0:T(4,128)(2,1)S(1)} %shard_map.100), channel_id=1, source_target_pairs={{0,8},{1,9},{2,10},{3,11},{4,12},{5,13},{6,14},{7,15},{8,0},{9,1},... | collective-permute-start | bytes 175112 | tf_op jit(solution)/shard_map/ppermute | solution.py:38
  6.7 4.9 %collective-permute-start.3 = (bf16[4,7296]{1,0:T(4,128)(2,1)S(1)}, bf16[4,7296]{1,0:T(4,128)(2,1)S(1)}, u32[]{:S(2)}, u32[]{:S(2)}) collective-permute-start(bf16[4,7296]{1,0:T(4,128)(2,1)S(1)} %shard_map.100), channel_id=1, source_target_pairs={{0,2},{1,3},{2,0},{3,1},{4,6},{5,7},{6,4},{7,5},{8,10},{9,11},{10,... | collective-permute-start | bytes 175112 | tf_op jit(solution)/shard_map/ppermute | solution.py:38
  11.7 6.1 %collective-permute-start.4 = (bf16[12,7296]{1,0:T(8,128)(2,1)S(1)}, bf16[12,7296]{1,0:T(8,128)(2,1)S(1)}, u32[]{:S(2)}, u32[]{:S(2)}) collective-permute-start(bf16[12,7296]{1,0:T(8,128)(2,1)S(1)} %pad_maximum_fusion.2), channel_id=1, source_target_pairs={{0,2},{1,3},{2,0},{3,1},{4,6},{5,7},{6,4},{7,5},{8,10},{9,11},{10,... | collective-permute-start | bytes 525320 | tf_op jit(solution)/shard_map/ppermute | solution.py:38
  18.1 1.9 %collective-permute-start.5 = (bf16[32,7296]{1,0:T(8,128)(2,1)S(1)}, bf16[32,7296]{1,0:T(8,128)(2,1)S(1)}, u32[]{:S(2)}, u32[]{:S(2)}) collective-permute-start(bf16[32,7296]{1,0:T(8,128)(2,1)S(1)} %pad_maximum_fusion.1), channel_id=1, source_target_pairs={{0,1},{1,0},{2,3},{3,2},{4,5},{5,4},{6,7},{7,6},{8,9},{9,8},{10,11... | collective-permute-start | bytes 1400840 | tf_op jit(solution)/shard_map/ppermute | solution.py:38
  20.7 6.4 %collective-permute-start.8 = (bf16[64,128]{1,0:T(8,128)(2,1)S(1)}, bf16[64,128]{1,0:T(8,128)(2,1)S(1)}, u32[]{:S(2)}, u32[]{:S(2)}) collective-permute-start(bf16[64,128]{1,0:T(8,128)(2,1)S(1)} %convolution_convert_fusion.1), channel_id=1, source_target_pairs={{0,3},{1,2},{2,1},{3,0},{4,7},{5,6},{6,5},{7,4},{8,11},{9,10},{10,... | collective-permute-start | bytes 49160 | tf_op jit(solution)/shard_map/ppermute | solution.py:38
  22.0 5.1 %collective-permute-start.7 = (bf16[64,128]{1,0:T(8,128)(2,1)S(1)}, bf16[64,128]{1,0:T(8,128)(2,1)S(1)}, u32[]{:S(2)}, u32[]{:S(2)}) collective-permute-start(bf16[64,128]{1,0:T(8,128)(2,1)S(1)} %convolution_convert_fusion.1), channel_id=1, source_target_pairs={{0,2},{1,3},{2,0},{3,1},{4,6},{5,7},{6,4},{7,5},{8,10},{9,11},{10,... | collective-permute-start | bytes 49160 | tf_op jit(solution)/shard_map/ppermute | solution.py:38
  22.5 4.6 %collective-permute-start.6 = (bf16[64,128]{1,0:T(8,128)(2,1)S(1)}, bf16[64,128]{1,0:T(8,128)(2,1)S(1)}, u32[]{:S(2)}, u32[]{:S(2)}) collective-permute-start(bf16[64,128]{1,0:T(8,128)(2,1)S(1)} %convolution_convert_fusion.1), channel_id=1, source_target_pairs={{0,1},{1,0},{2,3},{3,2},{4,5},{5,4},{6,7},{7,6},{8,9},{9,8},{10,11... | collective-permute-start | bytes 49160 | tf_op jit(solution)/shard_map/ppermute | solution.py:38
  22.6 4.6 %copy-start.2 = (bf16[1,4,128,2,256]{4,3,2,1,0:T(2,128)(2,1)S(1)}, bf16[1,4,128,2,256]{4,3,2,1,0:T(2,128)(2,1)}, u32[]{:S(2)}) copy-start(bf16[1,4,128,2,256]{4,3,2,1,0:T(2,128)(2,1)} %param.17) | copy-start | bytes 1572868
  27.1 1.0 %copy-start.3 = (bf16[1,4,256,128]{3,2,1,0:T(8,128)(2,1)S(1)}, bf16[1,4,256,128]{3,2,1,0:T(8,128)(2,1)}, u32[]{:S(2)}) copy-start(bf16[1,4,256,128]{3,2,1,0:T(8,128)(2,1)} %param.18) | copy-start | bytes 786436
  27.1 2.0 %copy-start.4 = (s32[16]{0:T(128)S(1)}, s32[16]{0:T(128)}, u32[]{:S(2)}) copy-start(s32[16]{0:T(128)} %param.13) | copy-start | bytes 196
  28.6 3.7 %collective-permute-start.9 = (bf16[2,64,128]{2,1,0:T(8,128)(2,1)S(1)}, bf16[2,64,128]{2,1,0:T(8,128)(2,1)S(1)}, u32[]{:S(2)}, u32[]{:S(2)}) collective-permute-start(bf16[2,64,128]{2,1,0:T(8,128)(2,1)S(1)} %dynamic-slice_bitcast_fusion), channel_id=1, source_target_pairs={{0,1},{1,0},{2,3},{3,2},{4,5},{5,4},{6,7},{7,6},{8,9},{9,8},{10,11... | collective-permute-start | bytes 98312 | tf_op jit(solution)/shard_map/ppermute | solution.py:38
  29.4 6.8 %copy-start.1 = (bf16[1,128,7168]{2,1,0:T(8,128)(2,1)S(1)}, bf16[1,128,7168]{2,1,0:T(8,128)(2,1)}, u32[]{:S(2)}) copy-start(bf16[1,128,7168]{2,1,0:T(8,128)(2,1)} %param.19) | copy-start | bytes 5505028
  32.4 3.8 %collective-permute-start.10 = (bf16[64,128]{1,0:T(8,128)(2,1)S(1)}, bf16[64,128]{1,0:T(8,128)(2,1)S(1)}, u32[]{:S(2)}, u32[]{:S(2)}) collective-permute-start(bf16[64,128]{1,0:T(8,128)(2,1)S(1)} %dynamic-slice_bitcast_fusion.1), channel_id=1, source_target_pairs={{0,2},{1,3},{2,0},{3,1},{4,6},{5,7},{6,4},{7,5},{8,10},{9,11},{10,... | collective-permute-start | bytes 49160 | tf_op jit(solution)/shard_map/ppermute | solution.py:38
  36.5 1.6 %collective-permute-start.15 = (bf16[32,3584]{1,0:T(8,128)(2,1)S(1)}, bf16[32,3584]{1,0:T(8,128)(2,1)S(1)}, u32[]{:S(2)}, u32[]{:S(2)}) collective-permute-start(bf16[32,3584]{1,0:T(8,128)(2,1)S(1)} %slice_select_fusion), channel_id=1, source_target_pairs={{0,1},{1,0},{2,3},{3,2},{4,5},{5,4},{6,7},{7,6},{8,9},{9,8},{10,11... | collective-permute-start | bytes 688136 | tf_op jit(solution)/shard_map/ppermute | solution.py:38
  37.0 2.8 %collective-permute-start.11 = (bf16[32,3584]{1,0:T(8,128)(2,1)S(1)}, bf16[32,3584]{1,0:T(8,128)(2,1)S(1)}, u32[]{:S(2)}, u32[]{:S(2)}) collective-permute-start(bf16[32,3584]{1,0:T(8,128)(2,1)S(1)} %slice_select_fusion.1), channel_id=1, source_target_pairs={{0,1},{1,0},{2,3},{3,2},{4,5},{5,4},{6,7},{7,6},{8,9},{9,8},{10,11... | collective-permute-start | bytes 688136 | tf_op jit(solution)/shard_map/ppermute | solution.py:38
  38.2 4.9 %collective-permute-start.16 = (bf16[16,3584]{1,0:T(8,128)(2,1)S(1)}, bf16[16,3584]{1,0:T(8,128)(2,1)S(1)}, u32[]{:S(2)}, u32[]{:S(2)}) collective-permute-start(bf16[16,3584]{1,0:T(8,128)(2,1)S(1)} %get-tuple-element.26), channel_id=1, source_target_pairs={{0,2},{1,5},{2,0},{3,7},{4,6},{5,1},{6,4},{7,3},{8,10},{9,13},{10,... | collective-permute-start | bytes 344072 | tf_op jit(solution)/shard_map/ppermute | solution.py:38
  39.9 4.9 %collective-permute-start.12 = (bf16[16,3584]{1,0:T(8,128)(2,1)S(1)}, bf16[16,3584]{1,0:T(8,128)(2,1)S(1)}, u32[]{:S(2)}, u32[]{:S(2)}) collective-permute-start(bf16[16,3584]{1,0:T(8,128)(2,1)S(1)} %get-tuple-element.24), channel_id=1, source_target_pairs={{0,2},{1,5},{2,0},{3,7},{4,6},{5,1},{6,4},{7,3},{8,10},{9,13},{10,... | collective-permute-start | bytes 344072 | tf_op jit(solution)/shard_map/ppermute | solution.py:38
  43.1 4.2 %collective-permute-start.17 = (bf16[8,3584]{1,0:T(8,128)(2,1)S(1)}, bf16[8,3584]{1,0:T(8,128)(2,1)S(1)}, u32[]{:S(2)}, u32[]{:S(2)}) collective-permute-start(bf16[8,3584]{1,0:T(8,128)(2,1)S(1)} %broadcast_select_fusion.4), channel_id=1, source_target_pairs={{0,4},{1,3},{2,6},{3,1},{4,0},{5,7},{6,2},{7,5},{8,12},{9,11},{10,... | collective-permute-start | bytes 172040 | tf_op jit(solution)/shard_map/ppermute | solution.py:38
  44.9 4.4 %collective-permute-start.13 = (bf16[8,3584]{1,0:T(8,128)(2,1)S(1)}, bf16[8,3584]{1,0:T(8,128)(2,1)S(1)}, u32[]{:S(2)}, u32[]{:S(2)}) collective-permute-start(bf16[8,3584]{1,0:T(8,128)(2,1)S(1)} %broadcast_select_fusion.5), channel_id=1, source_target_pairs={{0,4},{1,3},{2,6},{3,1},{4,0},{5,7},{6,2},{7,5},{8,12},{9,11},{10,... | collective-permute-start | bytes 172040 | tf_op jit(solution)/shard_map/ppermute | solution.py:38
  47.4 5.1 %collective-permute-start.18 = (bf16[4,3584]{1,0:T(4,128)(2,1)S(1)}, bf16[4,3584]{1,0:T(4,128)(2,1)S(1)}, u32[]{:S(2)}, u32[]{:S(2)}) collective-permute-start(bf16[4,3584]{1,0:T(4,128)(2,1)S(1)} %slice.123), channel_id=1, source_target_pairs={{0,8},{1,9},{2,10},{3,11},{4,12},{5,13},{6,14},{7,15},{8,0},{9,1},... | collective-permute-start | bytes 86024 | tf_op jit(solution)/shard_map/ppermute | solution.py:38
  49.3 4.8 %collective-permute-start.14 = (bf16[4,3584]{1,0:T(4,128)(2,1)S(1)}, bf16[4,3584]{1,0:T(4,128)(2,1)S(1)}, u32[]{:S(2)}, u32[]{:S(2)}) collective-permute-start(bf16[4,3584]{1,0:T(4,128)(2,1)S(1)} %slice.116), channel_id=1, source_target_pairs={{0,8},{1,9},{2,10},{3,11},{4,12},{5,13},{6,14},{7,15},{8,0},{9,1},... | collective-permute-start | bytes 86024 | tf_op jit(solution)/shard_map/ppermute | solution.py:38

commit v26 on v25

--- a/solution.py
+++ b/solution.py
@@ -228,16 +228,6 @@
     codes = jnp.dot(rows[:, :width], code_table, preferred_element_type=jnp.float32).astype(jnp.bfloat16)
     projected = gate_up_product(held, base_in[0])
 
-    codes = jnp.stack([codes if m == 0 else trade(codes, (0, m), (0, m)) for m in range(members)])
-    by_slot = jnp.stack([lax.dynamic_index_in_dim(codes, s ^ me, 0, keepdims=False) for s in range(members)])
-
-    lifted = jnp.einsum("srk,skgf->srgf", by_slot, delta_mid[0], preferred_element_type=jnp.float32)
-    total = held.shape[0]
-    hidden = jax.nn.silu(projected[None, :total] + lifted[:, :, 0]) * (projected[None, total:] + lifted[:, :, 1])
-    partial_codes = jnp.einsum(
-        "srf,sfk->srk", hidden.astype(jnp.bfloat16), delta_down[0], preferred_element_type=jnp.float32
-    ).astype(jnp.bfloat16)
-    hidden, rows, partial_codes = lax.optimization_barrier((hidden, rows, partial_codes))
     side = by_rows(rows[:, width:])
     all_routes = side[:, :top].astype(jnp.int32)
     numerator = side[:, top : 2 * top].astype(jnp.float32)
@@ -247,8 +237,17 @@
     scale = jnp.sum(
         jnp.where(position[None] == target[:, None, None], weight[None].astype(jnp.float32), 0.0), axis=-1
     )
+
+    codes = jnp.stack([codes if m == 0 else trade(codes, (0, m), (0, m)) for m in range(members)])
+    by_slot = jnp.stack([lax.dynamic_index_in_dim(codes, s ^ me, 0, keepdims=False) for s in range(members)])
+
+    lifted = jnp.einsum("srk,skgf->srgf", by_slot, delta_mid[0], preferred_element_type=jnp.float32)
+    total = held.shape[0]
+    hidden = jax.nn.silu(projected[None, :total] + lifted[:, :, 0]) * (projected[None, total:] + lifted[:, :, 1])
     hidden_sum = jnp.sum(scale[:, :, None] * hidden, axis=0).astype(jnp.bfloat16)
-
+    partial_codes = jnp.einsum(
+        "srf,sfk->srk", hidden.astype(jnp.bfloat16), delta_down[0], preferred_element_type=jnp.float32
+    ).astype(jnp.bfloat16)
     by_core = partial_codes.reshape(chips, 2, *partial_codes.shape[1:])
     kept, sent = (lax.dynamic_index_in_dim(by_core, c, 1, keepdims=False) for c in (core, 1 - core))
     by_chip = add(kept, trade(sent, (0, 1), (0, 1)))

time: 55 us -> 52.8 us (0.960)
  matrix products: 4.44 us -> 2.27 us
    dot_general x1, matrix products: 2.93 us -> 0.75 us  [local(): base = jnp.dot(hidden_sum, base_down[0], preferred_element_type=jnp.float32)]
  transfers between devices with their start and end apart: 19 -> 19, of which waited for: 11 -> 12; matrix products, arithmetic and copies ran while one was open for 7% -> 3% of each run, Pallas kernels for 8% -> 9%
where the time goes in v26:
time: 52.8 us; the launch traced here: 52.6 us
  starting transfers between devices  23 us (44%)
  waiting for transfers between devices  18.7 us (35%)
  Pallas kernels  5.72 us (11%)
  matrix products  2.27 us (4%)
  other arithmetic  2.02 us (4%)
  local copies, waits for them, and re-layouts  0.56 us (1%)
    ppermute x19, starting transfers between devices, trade(): return lax.ppermute(value, ('expert', 'tensor'), pairs)  23 us
    ppermute x19, waiting for transfers between devices, trade(): return lax.ppermute(value, ('expert', 'tensor'), pairs)  18.7 us
    pallas_call x1, Pallas kernels, gate_up_product(): pl.pallas_call(gate_up_kernel, out_shape=jax.ShapeDtypeStruct((2 * x.shap...  4.56 us
  transfers between devices with their start and end apart: 19, of which 12 were waited for; matrix products, arithmetic and copies ran while one was open for 3% of the time, Pallas kernels for 9%

profile of v26, /device:TPU:0, one launch (start us, length us, event | category | flops | bytes accessed | tf_op | source)
XLA Modules:
  0.0 52.6 jit_solution(9190775149491543055)
XLA Ops:
  0.0 1.0 %shard_map.100 = bf16[4,7296]{1,0:T(4,128)(2,1)S(1)} custom-call(bf16[4,7168]{1,0:T(4,128)(2,1)} %bitcast.72, s32[4,8]{1,0:T(4,128)} %bitcast.73, s32[4,8]{1,0:T(4,128)} %bitcast.74), custom_call_target="tpu_custom_call" | custom-call | flops 20000000000 | bytes 114688 | tf_op jit(solution)/shard_map/pallas_call | solution.py:76
  1.0 5.1 %collective-permute-start.2 = (bf16[4,7296]{1,0:T(4,128)(2,1)S(1)}, bf16[4,7296]{1,0:T(4,128)(2,1)S(1)}, u32[]{:S(2)}, u32[]{:S(2)}) collective-permute-start(bf16[4,7296]{1,0:T(4,128)(2,1)S(1)} %shard_map.100), channel_id=1, source_target_pairs={{0,12},{1,13},{2,14},{3,15},{4,8},{5,9},{6,10},{7,11},{8,4},{9,5},... | collective-permute-start | bytes 175112 | tf_op jit(solution)/shard_map/ppermute | solution.py:38
  6.1 0.6 %collective-permute-start = (bf16[4,7296]{1,0:T(4,128)(2,1)S(1)}, bf16[4,7296]{1,0:T(4,128)(2,1)S(1)}, u32[]{:S(2)}, u32[]{:S(2)}) collective-permute-start(bf16[4,7296]{1,0:T(4,128)(2,1)S(1)} %shard_map.100), channel_id=1, source_target_pairs={{0,8},{1,9},{2,10},{3,11},{4,12},{5,13},{6,14},{7,15},{8,0},{9,1},... | collective-permute-start | bytes 175112 | tf_op jit(solution)/shard_map/ppermute | solution.py:38
  6.7 1.6 %collective-permute-start.3 = (bf16[4,7296]{1,0:T(4,128)(2,1)S(1)}, bf16[4,7296]{1,0:T(4,128)(2,1)S(1)}, u32[]{:S(2)}, u32[]{:S(2)}) collective-permute-start(bf16[4,7296]{1,0:T(4,128)(2,1)S(1)} %shard_map.100), channel_id=1, source_target_pairs={{0,2},{1,3},{2,0},{3,1},{4,6},{5,7},{6,4},{7,5},{8,10},{9,11},{10,... | collective-permute-start | bytes 175112 | tf_op jit(solution)/shard_map/ppermute | solution.py:38
  8.4 0.4 collective-permute-done.2
  8.8 1.7 %collective-permute-done.1 = bf16[4,7296]{1,0:T(4,128)(2,1)S(1)} collective-permute-done((bf16[4,7296]{1,0:T(4,128)(2,1)S(1)}, bf16[4,7296]{1,0:T(4,128)(2,1)S(1)}, u32[]{:S(2)}, u32[]{:S(2)}) %collective-permute-start.1) | collective-permute-done | bytes 58400 | tf_op jit(solution)/shard_map/ppermute | solution.py:38
  10.4 1.1 %collective-permute-done = bf16[4,7296]{1,0:T(4,128)(2,1)S(1)} collective-permute-done((bf16[4,7296]{1,0:T(4,128)(2,1)S(1)}, bf16[4,7296]{1,0:T(4,128)(2,1)S(1)}, u32[]{:S(2)}, u32[]{:S(2)}) %collective-permute-start) | collective-permute-done | bytes 58400 | tf_op jit(solution)/shard_map/ppermute | solution.py:38
  11.6 0.1 pad_maximum_fusion.2
  11.7 1.6 %collective-permute-start.4 = (bf16[12,7296]{1,0:T(8,128)(2,1)S(1)}, bf16[12,7296]{1,0:T(8,128)(2,1)S(1)}, u32[]{:S(2)}, u32[]{:S(2)}) collective-permute-start(bf16[12,7296]{1,0:T(8,128)(2,1)S(1)} %pad_maximum_fusion.2), channel_id=1, source_target_pairs={{0,2},{1,3},{2,0},{3,1},{4,6},{5,7},{6,4},{7,5},{8,10},{9,11},{10,... | collective-permute-start | bytes 525320 | tf_op jit(solution)/shard_map/ppermute | solution.py:38
  13.3 4.6 %collective-permute-done.4 = bf16[12,7296]{1,0:T(8,128)(2,1)S(1)} collective-permute-done((bf16[12,7296]{1,0:T(8,128)(2,1)S(1)}, bf16[12,7296]{1,0:T(8,128)(2,1)S(1)}, u32[]{:S(2)}, u32[]{:S(2)}) %collective-permute-start.4) | collective-permute-done | bytes 175136 | tf_op jit(solution)/shard_map/ppermute | solution.py:38
  17.8 0.2 broadcast_select_fusion.3
  18.2 1.7 %collective-permute-done.5 = bf16[32,7296]{1,0:T(8,128)(2,1)S(1)} collective-permute-done((bf16[32,7296]{1,0:T(8,128)(2,1)S(1)}, bf16[32,7296]{1,0:T(8,128)(2,1)S(1)}, u32[]{:S(2)}, u32[]{:S(2)}) %collective-permute-start.5) | collective-permute-done | bytes 466976 | tf_op jit(solution)/shard_map/ppermute | solution.py:38
  20.0 0.2 broadcast_select_fusion.1
  20.2 0.2 convert_reduce_fusion
  20.4 0.5 convolution_convert_fusion.1
  20.9 1.3 %collective-permute-start.8 = (bf16[64,128]{1,0:T(8,128)(2,1)S(1)}, bf16[64,128]{1,0:T(8,128)(2,1)S(1)}, u32[]{:S(2)}, u32[]{:S(2)}) collective-permute-start(bf16[64,128]{1,0:T(8,128)(2,1)S(1)} %convolution_convert_fusion.1), channel_id=1, source_target_pairs={{0,3},{1,2},{2,1},{3,0},{4,7},{5,6},{6,5},{7,4},{8,11},{9,10},{10,... | collective-permute-start | bytes 49160 | tf_op jit(solution)/shard_map/ppermute | solution.py:38
  22.2 0.5 %collective-permute-start.7 = (bf16[64,128]{1,0:T(8,128)(2,1)S(1)}, bf16[64,128]{1,0:T(8,128)(2,1)S(1)}, u32[]{:S(2)}, u32[]{:S(2)}) collective-permute-start(bf16[64,128]{1,0:T(8,128)(2,1)S(1)} %convolution_convert_fusion.1), channel_id=1, source_target_pairs={{0,2},{1,3},{2,0},{3,1},{4,6},{5,7},{6,4},{7,5},{8,10},{9,11},{10,... | collective-permute-start | bytes 49160 | tf_op jit(solution)/shard_map/ppermute | solution.py:38
  22.7 0.1 collective-permute-start.6
  22.8 0.1 fusion.28
  23.0 4.6 %shard_map.101 = f32[128,256]{1,0:T(8,128)S(1)} custom-call(bf16[64,7296]{1,0:T(8,128)(2,1)S(1)} %pad_maximum_fusion.x, bf16[7168,2,256]{2,1,0:T(2,128)(2,1)} %bitcast.64), custom_call_target="tpu_custom_call" | custom-call | flops 469762048 | bytes 7340032 | tf_op jit(solution)/shard_map/pallas_call | solution.py:130
  27.6 0.1 select_reduce_fusion
  27.7 0.1 select_reduce_fusion.1
  27.9 0.2 fusion.9
  28.1 0.1 multiply_reduce_fusion
  28.2 0.3 copy-done.4
  28.5 0.2 convolution_convert_fusion
  28.7 0.5 collective-permute-start.9
  29.2 0.9 %collective-permute-done.9 = bf16[2,64,128]{2,1,0:T(8,128)(2,1)S(1)} collective-permute-done((bf16[2,64,128]{2,1,0:T(8,128)(2,1)S(1)}, bf16[2,64,128]{2,1,0:T(8,128)(2,1)S(1)}, u32[]{:S(2)}, u32[]{:S(2)}) %collective-permute-start.9) | collective-permute-done | bytes 32800 | tf_op jit(solution)/shard_map/ppermute | solution.py:38
  30.1 1.6 %collective-permute-start.10 = (bf16[64,128]{1,0:T(8,128)(2,1)S(1)}, bf16[64,128]{1,0:T(8,128)(2,1)S(1)}, u32[]{:S(2)}, u32[]{:S(2)}) collective-permute-start(bf16[64,128]{1,0:T(8,128)(2,1)S(1)} %dynamic-slice_bitcast_fusion.1), channel_id=1, source_target_pairs={{0,2},{1,3},{2,0},{3,1},{4,6},{5,7},{6,4},{7,5},{8,10},{9,11},{10,... | collective-permute-start | bytes 49160 | tf_op jit(solution)/shard_map/ppermute | solution.py:38
  31.7 0.8 %fusion.2 = f32[64,7168]{1,0:T(8,128)S(1)} fusion(bf16[1,256,7168]{2,1,0:T(8,128)(2,1)S(1)} %copy-done.1, bf16[64,256]{1,0:T(8,128)(2,1)S(1)} %get-tuple-element.21), kind=kOutput, calls=%fused_computation.4 | convolution fusion | flops 234881024 | bytes 5537792 | tf_op jit(solution)/shard_map/dot_general | solution.py:262
  32.5 1.5 %collective-permute-done.10 = bf16[64,128]{1,0:T(8,128)(2,1)S(1)} collective-permute-done((bf16[64,128]{1,0:T(8,128)(2,1)S(1)}, bf16[64,128]{1,0:T(8,128)(2,1)S(1)}, u32[]{:S(2)}, u32[]{:S(2)}) %collective-permute-start.10) | collective-permute-done | bytes 16416 | tf_op jit(solution)/shard_map/ppermute | solution.py:38
  33.9 0.3 fusion.1.term
  34.4 0.3 fusion.term
  34.8 0.6 %collective-permute-start.11 = (bf16[32,3584]{1,0:T(8,128)(2,1)S(1)}, bf16[32,3584]{1,0:T(8,128)(2,1)S(1)}, u32[]{:S(2)}, u32[]{:S(2)}) collective-permute-start(bf16[32,3584]{1,0:T(8,128)(2,1)S(1)} %slice_select_fusion.1), channel_id=1, source_target_pairs={{0,1},{1,0},{2,3},{3,2},{4,5},{5,4},{6,7},{7,6},{8,9},{9,8},{10,11... | collective-permute-start | bytes 688136 | tf_op jit(solution)/shard_map/ppermute | solution.py:38
  35.3 0.5 %collective-permute-done.15.received = bf16[32,3584]{1,0:T(8,128)(2,1)S(1)} collective-permute-done((bf16[32,3584]{1,0:T(8,128)(2,1)S(1)}, bf16[32,3584]{1,0:T(8,128)(2,1)S(1)}, u32[]{:S(2)}, u32[]{:S(2)}) %collective-permute-start.15) | collective-permute-done | bytes 229408 | tf_op jit(solution)/shard_map/ppermute | solution.py:38
  35.9 0.1 shard_map.103
  36.0 1.6 %collective-permute-start.16 = (bf16[16,3584]{1,0:T(8,128)(2,1)S(1)}, bf16[16,3584]{1,0:T(8,128)(2,1)S(1)}, u32[]{:S(2)}, u32[]{:S(2)}) collective-permute-start(bf16[16,3584]{1,0:T(8,128)(2,1)S(1)} %get-tuple-element.20), channel_id=1, source_target_pairs={{0,2},{1,5},{2,0},{3,7},{4,6},{5,1},{6,4},{7,3},{8,10},{9,13},{10,... | collective-permute-start | bytes 344072 | tf_op jit(solution)/shard_map/ppermute | solution.py:38
  37.5 0.1 shard_map.102
  37.6 0.6 %collective-permute-start.12 = (bf16[16,3584]{1,0:T(8,128)(2,1)S(1)}, bf16[16,3584]{1,0:T(8,128)(2,1)S(1)}, u32[]{:S(2)}, u32[]{:S(2)}) collective-permute-start(bf16[16,3584]{1,0:T(8,128)(2,1)S(1)} %get-tuple-element.18), channel_id=1, source_target_pairs={{0,2},{1,5},{2,0},{3,7},{4,6},{5,1},{6,4},{7,3},{8,10},{9,13},{10,... | collective-permute-start | bytes 344072 | tf_op jit(solution)/shard_map/ppermute | solution.py:38
  38.2 2.6 %collective-permute-done.16 = bf16[16,3584]{1,0:T(8,128)(2,1)S(1)} collective-permute-done((bf16[16,3584]{1,0:T(8,128)(2,1)S(1)}, bf16[16,3584]{1,0:T(8,128)(2,1)S(1)}, u32[]{:S(2)}, u32[]{:S(2)}) %collective-permute-start.16) | collective-permute-done | bytes 114720 | tf_op jit(solution)/shard_map/ppermute | solution.py:38
  40.9 1.7 %collective-permute-start.17 = (bf16[8,3584]{1,0:T(8,128)(2,1)S(1)}, bf16[8,3584]{1,0:T(8,128)(2,1)S(1)}, u32[]{:S(2)}, u32[]{:S(2)}) collective-permute-start(bf16[8,3584]{1,0:T(8,128)(2,1)S(1)} %broadcast_select_fusion.4), channel_id=1, source_target_pairs={{0,4},{1,3},{2,6},{3,1},{4,0},{5,7},{6,2},{7,5},{8,12},{9,11},{10,... | collective-permute-start | bytes 172040 | tf_op jit(solution)/shard_map/ppermute | solution.py:38
  42.6 1.6 %collective-permute-start.13 = (bf16[8,3584]{1,0:T(8,128)(2,1)S(1)}, bf16[8,3584]{1,0:T(8,128)(2,1)S(1)}, u32[]{:S(2)}, u32[]{:S(2)}) collective-permute-start(bf16[8,3584]{1,0:T(8,128)(2,1)S(1)} %broadcast_select_fusion.5), channel_id=1, source_target_pairs={{0,4},{1,3},{2,6},{3,1},{4,0},{5,7},{6,2},{7,5},{8,12},{9,11},{10,... | collective-permute-start | bytes 172040 | tf_op jit(solution)/shard_map/ppermute | solution.py:38
  44.2 0.9 %collective-permute-done.17 = bf16[8,3584]{1,0:T(8,128)(2,1)S(1)} collective-permute-done((bf16[8,3584]{1,0:T(8,128)(2,1)S(1)}, bf16[8,3584]{1,0:T(8,128)(2,1)S(1)}, u32[]{:S(2)}, u32[]{:S(2)}) %collective-permute-start.17) | collective-permute-done | bytes 57376 | tf_op jit(solution)/shard_map/ppermute | solution.py:38
  45.2 1.9 %collective-permute-start.18 = (bf16[4,3584]{1,0:T(4,128)(2,1)S(1)}, bf16[4,3584]{1,0:T(4,128)(2,1)S(1)}, u32[]{:S(2)}, u32[]{:S(2)}) collective-permute-start(bf16[4,3584]{1,0:T(4,128)(2,1)S(1)} %slice.123), channel_id=1, source_target_pairs={{0,8},{1,9},{2,10},{3,11},{4,12},{5,13},{6,14},{7,15},{8,0},{9,1},... | collective-permute-start | bytes 86024 | tf_op jit(solution)/shard_map/ppermute | solution.py:38
  47.1 2.0 %collective-permute-start.14 = (bf16[4,3584]{1,0:T(4,128)(2,1)S(1)}, bf16[4,3584]{1,0:T(4,128)(2,1)S(1)}, u32[]{:S(2)}, u32[]{:S(2)}) collective-permute-start(bf16[4,3584]{1,0:T(4,128)(2,1)S(1)} %slice.116), channel_id=1, source_target_pairs={{0,8},{1,9},{2,10},{3,11},{4,12},{5,13},{6,14},{7,15},{8,0},{9,1},... | collective-permute-start | bytes 86024 | tf_op jit(solution)/shard_map/ppermute | solution.py:38
  49.1 1.1 %collective-permute-done.18 = bf16[4,3584]{1,0:T(4,128)(2,1)S(1)} collective-permute-done((bf16[4,3584]{1,0:T(4,128)(2,1)S(1)}, bf16[4,3584]{1,0:T(4,128)(2,1)S(1)}, u32[]{:S(2)}, u32[]{:S(2)}) %collective-permute-start.18) | collective-permute-done | bytes 28704 | tf_op jit(solution)/shard_map/ppermute | solution.py:38
  50.3 1.7 %collective-permute-done.14 = bf16[4,3584]{1,0:T(4,128)(2,1)S(1)} collective-permute-done((bf16[4,3584]{1,0:T(4,128)(2,1)S(1)}, bf16[4,3584]{1,0:T(4,128)(2,1)S(1)}, u32[]{:S(2)}, u32[]{:S(2)}) %collective-permute-start.14) | collective-permute-done | bytes 28704 | tf_op jit(solution)/shard_map/ppermute | solution.py:38
  52.0 0.7 %maximum_bitcast_fusion.2 = bf16[1,4,7168]{2,1,0:T(4,128)(2,1)} fusion(bf16[4,3584]{1,0:T(4,128)(2,1)S(1)} %add_convert_fusion.4, bf16[4,3584]{1,0:T(4,128)(2,1)S(1)} %add_convert_fusion.5), kind=kLoop, calls=%fused_computation.50 | loop fusion | flops 114688 | bytes 114688 | tf_op jit(solution)/shard_map/broadcast_in_dim | solution.py:291
  (46 shorter events, 0.8 us)
Async XLA Ops:
  0.0 20.2 %copy-start = (bf16[1,7168,128]{2,1,0:T(8,128)(2,1)S(1)}, bf16[1,7168,128]{2,1,0:T(8,128)(2,1)}, u32[]{:S(2)}) copy-start(bf16[1,7168,128]{2,1,0:T(8,128)(2,1)} %param.16) | copy-start | bytes 5505028
  1.0 7.8 %collective-permute-start.2 = (bf16[4,7296]{1,0:T(4,128)(2,1)S(1)}, bf16[4,7296]{1,0:T(4,128)(2,1)S(1)}, u32[]{:S(2)}, u32[]{:S(2)}) collective-permute-start(bf16[4,7296]{1,0:T(4,128)(2,1)S(1)} %shard_map.100), channel_id=1, source_target_pairs={{0,12},{1,13},{2,14},{3,15},{4,8},{5,9},{6,10},{7,11},{8,4},{9,5},... | collective-permute-start | bytes 175112 | tf_op jit(solution)/shard_map/ppermute | solution.py:38
  6.1 4.3 %collective-permute-start.1 = (bf16[4,7296]{1,0:T(4,128)(2,1)S(1)}, bf16[4,7296]{1,0:T(4,128)(2,1)S(1)}, u32[]{:S(2)}, u32[]{:S(2)}) collective-permute-start(bf16[4,7296]{1,0:T(4,128)(2,1)S(1)} %shard_map.100), channel_id=1, source_target_pairs={{0,4},{1,5},{2,6},{3,7},{4,0},{5,1},{6,2},{7,3},{8,12},{9,13},{10,... | collective-permute-start | bytes 175112 | tf_op jit(solution)/shard_map/ppermute | solution.py:38
  6.1 5.5 %collective-permute-start = (bf16[4,7296]{1,0:T(4,128)(2,1)S(1)}, bf16[4,7296]{1,0:T(4,128)(2,1)S(1)}, u32[]{:S(2)}, u32[]{:S(2)}) collective-permute-start(bf16[4,7296]{1,0:T(4,128)(2,1)S(1)} %shard_map.100), channel_id=1, source_target_pairs={{0,8},{1,9},{2,10},{3,11},{4,12},{5,13},{6,14},{7,15},{8,0},{9,1},... | collective-permute-start | bytes 175112 | tf_op jit(solution)/shard_map/ppermute | solution.py:38
  6.7 4.9 %collective-permute-start.3 = (bf16[4,7296]{1,0:T(4,128)(2,1)S(1)}, bf16[4,7296]{1,0:T(4,128)(2,1)S(1)}, u32[]{:S(2)}, u32[]{:S(2)}) collective-permute-start(bf16[4,7296]{1,0:T(4,128)(2,1)S(1)} %shard_map.100), channel_id=1, source_target_pairs={{0,2},{1,3},{2,0},{3,1},{4,6},{5,7},{6,4},{7,5},{8,10},{9,11},{10,... | collective-permute-start | bytes 175112 | tf_op jit(solution)/shard_map/ppermute | solution.py:38
  11.7 6.1 %collective-permute-start.4 = (bf16[12,7296]{1,0:T(8,128)(2,1)S(1)}, bf16[12,7296]{1,0:T(8,128)(2,1)S(1)}, u32[]{:S(2)}, u32[]{:S(2)}) collective-permute-start(bf16[12,7296]{1,0:T(8,128)(2,1)S(1)} %pad_maximum_fusion.2), channel_id=1, source_target_pairs={{0,2},{1,3},{2,0},{3,1},{4,6},{5,7},{6,4},{7,5},{8,10},{9,11},{10,... | collective-permute-start | bytes 525320 | tf_op jit(solution)/shard_map/ppermute | solution.py:38
  18.1 1.9 %collective-permute-start.5 = (bf16[32,7296]{1,0:T(8,128)(2,1)S(1)}, bf16[32,7296]{1,0:T(8,128)(2,1)S(1)}, u32[]{:S(2)}, u32[]{:S(2)}) collective-permute-start(bf16[32,7296]{1,0:T(8,128)(2,1)S(1)} %pad_maximum_fusion.1), channel_id=1, source_target_pairs={{0,1},{1,0},{2,3},{3,2},{4,5},{5,4},{6,7},{7,6},{8,9},{9,8},{10,11... | collective-permute-start | bytes 1400840 | tf_op jit(solution)/shard_map/ppermute | solution.py:38
  20.9 6.9 %collective-permute-start.8 = (bf16[64,128]{1,0:T(8,128)(2,1)S(1)}, bf16[64,128]{1,0:T(8,128)(2,1)S(1)}, u32[]{:S(2)}, u32[]{:S(2)}) collective-permute-start(bf16[64,128]{1,0:T(8,128)(2,1)S(1)} %convolution_convert_fusion.1), channel_id=1, source_target_pairs={{0,3},{1,2},{2,1},{3,0},{4,7},{5,6},{6,5},{7,4},{8,11},{9,10},{10,... | collective-permute-start | bytes 49160 | tf_op jit(solution)/shard_map/ppermute | solution.py:38
  22.2 5.6 %collective-permute-start.7 = (bf16[64,128]{1,0:T(8,128)(2,1)S(1)}, bf16[64,128]{1,0:T(8,128)(2,1)S(1)}, u32[]{:S(2)}, u32[]{:S(2)}) collective-permute-start(bf16[64,128]{1,0:T(8,128)(2,1)S(1)} %convolution_convert_fusion.1), channel_id=1, source_target_pairs={{0,2},{1,3},{2,0},{3,1},{4,6},{5,7},{6,4},{7,5},{8,10},{9,11},{10,... | collective-permute-start | bytes 49160 | tf_op jit(solution)/shard_map/ppermute | solution.py:38
  22.7 5.1 %collective-permute-start.6 = (bf16[64,128]{1,0:T(8,128)(2,1)S(1)}, bf16[64,128]{1,0:T(8,128)(2,1)S(1)}, u32[]{:S(2)}, u32[]{:S(2)}) collective-permute-start(bf16[64,128]{1,0:T(8,128)(2,1)S(1)} %convolution_convert_fusion.1), channel_id=1, source_target_pairs={{0,1},{1,0},{2,3},{3,2},{4,5},{5,4},{6,7},{7,6},{8,9},{9,8},{10,11... | collective-permute-start | bytes 49160 | tf_op jit(solution)/shard_map/ppermute | solution.py:38
  23.0 4.6 %copy-start.5 = (s32[16]{0:T(128)S(1)}, s32[16]{0:T(128)}, u32[]{:S(2)}) copy-start(s32[16]{0:T(128)} %param.13) | copy-start | bytes 196
  23.0 4.9 %copy-start.3 = (bf16[1,4,128,2,256]{4,3,2,1,0:T(2,128)(2,1)S(1)}, bf16[1,4,128,2,256]{4,3,2,1,0:T(2,128)(2,1)}, u32[]{:S(2)}) copy-start(bf16[1,4,128,2,256]{4,3,2,1,0:T(2,128)(2,1)} %param.17) | copy-start | bytes 1572868
  23.0 8.7 %copy-start.1 = (bf16[1,256,7168]{2,1,0:T(8,128)(2,1)S(1)}, bf16[1,256,7168]{2,1,0:T(8,128)(2,1)}, u32[]{:S(2)}) copy-start(bf16[1,256,7168]{2,1,0:T(8,128)(2,1)} %param.15) | copy-start | bytes 11010052
  27.6 1.0 %copy-start.4 = (bf16[1,4,256,128]{3,2,1,0:T(8,128)(2,1)S(1)}, bf16[1,4,256,128]{3,2,1,0:T(8,128)(2,1)}, u32[]{:S(2)}) copy-start(bf16[1,4,256,128]{3,2,1,0:T(8,128)(2,1)} %param.18) | copy-start | bytes 786436
  28.7 1.4 %collective-permute-start.9 = (bf16[2,64,128]{2,1,0:T(8,128)(2,1)S(1)}, bf16[2,64,128]{2,1,0:T(8,128)(2,1)S(1)}, u32[]{:S(2)}, u32[]{:S(2)}) collective-permute-start(bf16[2,64,128]{2,1,0:T(8,128)(2,1)S(1)} %dynamic-slice_bitcast_fusion), channel_id=1, source_target_pairs={{0,1},{1,0},{2,3},{3,2},{4,5},{5,4},{6,7},{7,6},{8,9},{9,8},{10,11... | collective-permute-start | bytes 98312 | tf_op jit(solution)/shard_map/ppermute | solution.py:38
  30.1 3.8 %collective-permute-start.10 = (bf16[64,128]{1,0:T(8,128)(2,1)S(1)}, bf16[64,128]{1,0:T(8,128)(2,1)S(1)}, u32[]{:S(2)}, u32[]{:S(2)}) collective-permute-start(bf16[64,128]{1,0:T(8,128)(2,1)S(1)} %dynamic-slice_bitcast_fusion.1), channel_id=1, source_target_pairs={{0,2},{1,3},{2,0},{3,1},{4,6},{5,7},{6,4},{7,5},{8,10},{9,11},{10,... | collective-permute-start | bytes 49160 | tf_op jit(solution)/shard_map/ppermute | solution.py:38
  31.7 2.2 %copy-start.2 = (bf16[1,128,7168]{2,1,0:T(8,128)(2,1)S(1)}, bf16[1,128,7168]{2,1,0:T(8,128)(2,1)}, u32[]{:S(2)}) copy-start(bf16[1,128,7168]{2,1,0:T(8,128)(2,1)} %param.19) | copy-start | bytes 5505028
  34.3 1.6 %collective-permute-start.15 = (bf16[32,3584]{1,0:T(8,128)(2,1)S(1)}, bf16[32,3584]{1,0:T(8,128)(2,1)S(1)}, u32[]{:S(2)}, u32[]{:S(2)}) collective-permute-start(bf16[32,3584]{1,0:T(8,128)(2,1)S(1)} %slice_select_fusion), channel_id=1, source_target_pairs={{0,1},{1,0},{2,3},{3,2},{4,5},{5,4},{6,7},{7,6},{8,9},{9,8},{10,11... | collective-permute-start | bytes 688136 | tf_op jit(solution)/shard_map/ppermute | solution.py:38
  34.8 2.8 %collective-permute-start.11 = (bf16[32,3584]{1,0:T(8,128)(2,1)S(1)}, bf16[32,3584]{1,0:T(8,128)(2,1)S(1)}, u32[]{:S(2)}, u32[]{:S(2)}) collective-permute-start(bf16[32,3584]{1,0:T(8,128)(2,1)S(1)} %slice_select_fusion.1), channel_id=1, source_target_pairs={{0,1},{1,0},{2,3},{3,2},{4,5},{5,4},{6,7},{7,6},{8,9},{9,8},{10,11... | collective-permute-start | bytes 688136 | tf_op jit(solution)/shard_map/ppermute | solution.py:38
  36.0 4.9 %collective-permute-start.16 = (bf16[16,3584]{1,0:T(8,128)(2,1)S(1)}, bf16[16,3584]{1,0:T(8,128)(2,1)S(1)}, u32[]{:S(2)}, u32[]{:S(2)}) collective-permute-start(bf16[16,3584]{1,0:T(8,128)(2,1)S(1)} %get-tuple-element.20), channel_id=1, source_target_pairs={{0,2},{1,5},{2,0},{3,7},{4,6},{5,1},{6,4},{7,3},{8,10},{9,13},{10,... | collective-permute-start | bytes 344072 | tf_op jit(solution)/shard_map/ppermute | solution.py:38
  37.6 4.9 %collective-permute-start.12 = (bf16[16,3584]{1,0:T(8,128)(2,1)S(1)}, bf16[16,3584]{1,0:T(8,128)(2,1)S(1)}, u32[]{:S(2)}, u32[]{:S(2)}) collective-permute-start(bf16[16,3584]{1,0:T(8,128)(2,1)S(1)} %get-tuple-element.18), channel_id=1, source_target_pairs={{0,2},{1,5},{2,0},{3,7},{4,6},{5,1},{6,4},{7,3},{8,10},{9,13},{10,... | collective-permute-start | bytes 344072 | tf_op jit(solution)/shard_map/ppermute | solution.py:38
  40.9 4.2 %collective-permute-start.17 = (bf16[8,3584]{1,0:T(8,128)(2,1)S(1)}, bf16[8,3584]{1,0:T(8,128)(2,1)S(1)}, u32[]{:S(2)}, u32[]{:S(2)}) collective-permute-start(bf16[8,3584]{1,0:T(8,128)(2,1)S(1)} %broadcast_select_fusion.4), channel_id=1, source_target_pairs={{0,4},{1,3},{2,6},{3,1},{4,0},{5,7},{6,2},{7,5},{8,12},{9,11},{10,... | collective-permute-start | bytes 172040 | tf_op jit(solution)/shard_map/ppermute | solution.py:38
  42.6 4.4 %collective-permute-start.13 = (bf16[8,3584]{1,0:T(8,128)(2,1)S(1)}, bf16[8,3584]{1,0:T(8,128)(2,1)S(1)}, u32[]{:S(2)}, u32[]{:S(2)}) collective-permute-start(bf16[8,3584]{1,0:T(8,128)(2,1)S(1)} %broadcast_select_fusion.5), channel_id=1, source_target_pairs={{0,4},{1,3},{2,6},{3,1},{4,0},{5,7},{6,2},{7,5},{8,12},{9,11},{10,... | collective-permute-start | bytes 172040 | tf_op jit(solution)/shard_map/ppermute | solution.py:38
  45.2 5.1 %collective-permute-start.18 = (bf16[4,3584]{1,0:T(4,128)(2,1)S(1)}, bf16[4,3584]{1,0:T(4,128)(2,1)S(1)}, u32[]{:S(2)}, u32[]{:S(2)}) collective-permute-start(bf16[4,3584]{1,0:T(4,128)(2,1)S(1)} %slice.123), channel_id=1, source_target_pairs={{0,8},{1,9},{2,10},{3,11},{4,12},{5,13},{6,14},{7,15},{8,0},{9,1},... | collective-permute-start | bytes 86024 | tf_op jit(solution)/shard_map/ppermute | solution.py:38
  47.1 4.8 %collective-permute-start.14 = (bf16[4,3584]{1,0:T(4,128)(2,1)S(1)}, bf16[4,3584]{1,0:T(4,128)(2,1)S(1)}, u32[]{:S(2)}, u32[]{:S(2)}) collective-permute-start(bf16[4,3584]{1,0:T(4,128)(2,1)S(1)} %slice.116), channel_id=1, source_target_pairs={{0,8},{1,9},{2,10},{3,11},{4,12},{5,13},{6,14},{7,15},{8,0},{9,1},... | collective-permute-start | bytes 86024 | tf_op jit(solution)/shard_map/ppermute | solution.py:38

commit v27 on v26

--- a/solution.py
+++ b/solution.py
@@ -21,11 +21,6 @@
 
 def by_rows(value):
     return with_layout_constraint(value, Layout((0, 1)))
-
-
-def lookup(table, index):
-    keys = jnp.arange(table.shape[0], dtype=jnp.int32)
-    return jnp.sum(jnp.where(index[..., None] == keys, table, 0), axis=-1)
 
 
 def trade(value, even, odd):
@@ -54,38 +49,48 @@
     return (kept.astype(jnp.float32) + received.astype(jnp.float32)).astype(jnp.bfloat16)
 
 
-def pack_kernel(tokens, routes, numerators, packed, routes_in, numerators_in, sems):
+def pack_kernel(tokens, routes, numerators, place, packed, routes_in, numerators_in, place_in, sems):
     width, top = tokens.shape[1], routes.shape[1]
     copies = [
         pltpu.make_async_copy(tokens, packed.at[:, pl.ds(0, width)], sems.at[0]),
         pltpu.make_async_copy(routes, routes_in, sems.at[1]),
         pltpu.make_async_copy(numerators, numerators_in, sems.at[2]),
+        pltpu.make_async_copy(place, place_in, sems.at[3]),
     ]
     for copy in copies:
         copy.start()
-    packed[:, width:] = jnp.zeros((packed.shape[0], packed.shape[1] - width), packed.dtype)
     for copy in copies[1:]:
         copy.wait()
-    packed[:, width : width + top] = routes_in[...].astype(jnp.float32).astype(packed.dtype)
-    packed[:, width + top : width + 2 * top] = numerators_in[...].astype(jnp.float32).astype(packed.dtype)
+    named = routes_in[...]
+    position = jnp.zeros(named.shape, jnp.int32)
+    for expert in range(place.shape[0]):
+        position = jnp.where(named == expert, place_in[expert], position)
+    numerator = numerators_in[...].astype(jnp.float32)
+    weight = 2.5 * numerator / jnp.sum(numerator, axis=1, keepdims=True)
+    column = lax.broadcasted_iota(jnp.int32, (packed.shape[0], packed.shape[1] - width), 1)
+    table = jnp.zeros(column.shape, jnp.float32)
+    for k in range(top):
+        table += jnp.where(column == position[:, k : k + 1], weight[:, k : k + 1], 0.0)
+    packed[:, width:] = table.astype(packed.dtype)
     copies[0].wait()
 
 
-def pack(tokens, routes, numerators):
+def pack(tokens, routes, numerators, place):
     count, width = tokens.shape
     return pl.pallas_call(
         pack_kernel,
         out_shape=jax.ShapeDtypeStruct((count, width + 128), tokens.dtype),
-        in_specs=[HBM] * 3,
+        in_specs=[HBM] * 4,
         out_specs=VMEM,
         scratch_shapes=[
             pltpu.VMEM(routes.shape, routes.dtype),
             pltpu.VMEM(numerators.shape, numerators.dtype),
-            pltpu.SemaphoreType.DMA((3,)),
+            pltpu.SMEM(place.shape, place.dtype),
+            pltpu.SemaphoreType.DMA((4,)),
         ],
         compiler_params=pltpu.CompilerParams(vmem_limit_bytes=4 << 20),
         cost_estimate=pl.CostEstimate(flops=20 * 10**9, bytes_accessed=4 * tokens.size, transcendentals=0),
-    )(in_hbm(tokens), in_hbm(routes), in_hbm(numerators))
+    )(in_hbm(tokens), in_hbm(routes), in_hbm(numerators), in_hbm(place))
 
 
 def piece_bounds(size, step, pieces):
@@ -188,12 +193,11 @@
     cluster = lax.axis_index("expert")
     core = me % 2
     count, width = tokens.shape[1:]
-    top = routes.shape[2]
 
     along, across = halves(clusters), halves(members // 2)
     shared, paired = along[: len(along) - len(across)], along[len(along) - len(across) :]
 
-    packed = pack(tokens[0], routes[0], numerators[0])
+    packed = pack(tokens[0], routes[0], numerators[0], place)
     chips = members // 2
     pieces = {(0, 0): packed}
     for z in range(clusters - 1, 0, -1):
@@ -228,15 +232,8 @@
     codes = jnp.dot(rows[:, :width], code_table, preferred_element_type=jnp.float32).astype(jnp.bfloat16)
     projected = gate_up_product(held, base_in[0])
 
-    side = by_rows(rows[:, width:])
-    all_routes = side[:, :top].astype(jnp.int32)
-    numerator = side[:, top : 2 * top].astype(jnp.float32)
-    position = lookup(place, all_routes)
-    weight = (2.5 * numerator / jnp.sum(numerator, axis=-1, keepdims=True)).astype(jnp.bfloat16)
-    target = cluster * members + jnp.arange(members, dtype=jnp.int32)
-    scale = jnp.sum(
-        jnp.where(position[None] == target[:, None, None], weight[None].astype(jnp.float32), 0.0), axis=-1
-    )
+    scale = lax.dynamic_slice_in_dim(rows[:, width:], cluster * members, members, axis=1)
+    scale = scale.astype(jnp.float32).T
 
     codes = jnp.stack([codes if m == 0 else trade(codes, (0, m), (0, m)) for m in range(members)])
     by_slot = jnp.stack([lax.dynamic_index_in_dim(codes, s ^ me, 0, keepdims=False) for s in range(members)])

time: 52.8 us -> 53.1 us (level)
  matrix products: 2.27 us -> 4.44 us
  waiting for transfers between devices: 18.7 us -> 17.5 us
    dot_general x1, matrix products: 0.75 us -> 2.92 us  [local(): base = jnp.dot(hidden_sum, base_down[0], preferred_element_type=jnp.float32)]
    ppermute x19, waiting for transfers between devices: 18.7 us -> 17.5 us  [trade(): return lax.ppermute(value, ('expert', 'tensor'), pairs)]
  transfers between devices with their start and end apart: 19 -> 19, of which waited for: 12 -> 11; matrix products, arithmetic and copies ran while one was open for 3% -> 7% of each run, Pallas kernels for 9% -> 9%
where the time goes in v27:
time: 53.1 us; the launch traced here: 52.9 us
  starting transfers between devices  22.6 us (43%)
  waiting for transfers between devices  17.5 us (33%)
  Pallas kernels  5.72 us (11%)
  matrix products  4.44 us (8%)
  other arithmetic  1.68 us (3%)
  local copies, waits for them, and re-layouts  0.69 us (1%)
    ppermute x19, starting transfers between devices, trade(): return lax.ppermute(value, ('expert', 'tensor'), pairs)  22.6 us
    ppermute x19, waiting for transfers between devices, trade(): return lax.ppermute(value, ('expert', 'tensor'), pairs)  17.5 us
    pallas_call x1, Pallas kernels, gate_up_product(): pl.pallas_call(gate_up_kernel, out_shape=jax.ShapeDtypeStruct((2 * x.shap...  4.44 us
    dot_general x1, matrix products, local(): base = jnp.dot(hidden_sum, base_down[0], preferred_element_type=jnp.float32)  2.92 us
    pallas_call x1, Pallas kernels, pack(): pl.pallas_call(pack_kernel, out_shape=jax.ShapeDtypeStruct((count, width...  1.09 us
  transfers between devices with their start and end apart: 19, of which 11 were waited for; matrix products, arithmetic and copies ran while one was open for 7% of the time, Pallas kernels for 9%

profile of v27, /device:TPU:0, one launch (start us, length us, event | category | flops | bytes accessed | tf_op | source)
XLA Modules:
  0.0 52.9 jit_solution(2460427301252019546)
XLA Ops:
  0.0 1.1 %shard_map.100 = bf16[4,7296]{1,0:T(4,128)(2,1)S(1)} custom-call(bf16[4,7168]{1,0:T(4,128)(2,1)} %bitcast.72, s32[4,8]{1,0:T(4,128)} %bitcast.73, s32[4,8]{1,0:T(4,128)} %bitcast.74, s32[16]{0:T(128)} %place.1), custom_call_target="tpu_custom_call" | custom-call | flops 20000000000 | bytes 114688 | tf_op jit(solution)/shard_map/pallas_call | solution.py:80
  1.1 5.1 %collective-permute-start.2 = (bf16[4,7296]{1,0:T(4,128)(2,1)S(1)}, bf16[4,7296]{1,0:T(4,128)(2,1)S(1)}, u32[]{:S(2)}, u32[]{:S(2)}) collective-permute-start(bf16[4,7296]{1,0:T(4,128)(2,1)S(1)} %shard_map.100), channel_id=1, source_target_pairs={{0,12},{1,13},{2,14},{3,15},{4,8},{5,9},{6,10},{7,11},{8,4},{9,5},... | collective-permute-start | bytes 175112 | tf_op jit(solution)/shard_map/ppermute | solution.py:33
  6.2 0.6 %collective-permute-start = (bf16[4,7296]{1,0:T(4,128)(2,1)S(1)}, bf16[4,7296]{1,0:T(4,128)(2,1)S(1)}, u32[]{:S(2)}, u32[]{:S(2)}) collective-permute-start(bf16[4,7296]{1,0:T(4,128)(2,1)S(1)} %shard_map.100), channel_id=1, source_target_pairs={{0,8},{1,9},{2,10},{3,11},{4,12},{5,13},{6,14},{7,15},{8,0},{9,1},... | collective-permute-start | bytes 175112 | tf_op jit(solution)/shard_map/ppermute | solution.py:33
  6.9 1.6 %collective-permute-start.3 = (bf16[4,7296]{1,0:T(4,128)(2,1)S(1)}, bf16[4,7296]{1,0:T(4,128)(2,1)S(1)}, u32[]{:S(2)}, u32[]{:S(2)}) collective-permute-start(bf16[4,7296]{1,0:T(4,128)(2,1)S(1)} %shard_map.100), channel_id=1, source_target_pairs={{0,2},{1,3},{2,0},{3,1},{4,6},{5,7},{6,4},{7,5},{8,10},{9,11},{10,... | collective-permute-start | bytes 175112 | tf_op jit(solution)/shard_map/ppermute | solution.py:33
  8.5 0.4 collective-permute-done.2
  8.9 1.7 %collective-permute-done.1 = bf16[4,7296]{1,0:T(4,128)(2,1)S(1)} collective-permute-done((bf16[4,7296]{1,0:T(4,128)(2,1)S(1)}, bf16[4,7296]{1,0:T(4,128)(2,1)S(1)}, u32[]{:S(2)}, u32[]{:S(2)}) %collective-permute-start.1) | collective-permute-done | bytes 58400 | tf_op jit(solution)/shard_map/ppermute | solution.py:33
  10.6 1.1 %collective-permute-done = bf16[4,7296]{1,0:T(4,128)(2,1)S(1)} collective-permute-done((bf16[4,7296]{1,0:T(4,128)(2,1)S(1)}, bf16[4,7296]{1,0:T(4,128)(2,1)S(1)}, u32[]{:S(2)}, u32[]{:S(2)}) %collective-permute-start) | collective-permute-done | bytes 58400 | tf_op jit(solution)/shard_map/ppermute | solution.py:33
  11.7 0.1 pad_maximum_fusion.2
  11.8 1.6 %collective-permute-start.4 = (bf16[12,7296]{1,0:T(8,128)(2,1)S(1)}, bf16[12,7296]{1,0:T(8,128)(2,1)S(1)}, u32[]{:S(2)}, u32[]{:S(2)}) collective-permute-start(bf16[12,7296]{1,0:T(8,128)(2,1)S(1)} %pad_maximum_fusion.2), channel_id=1, source_target_pairs={{0,2},{1,3},{2,0},{3,1},{4,6},{5,7},{6,4},{7,5},{8,10},{9,11},{10,... | collective-permute-start | bytes 525320 | tf_op jit(solution)/shard_map/ppermute | solution.py:33
  13.4 4.6 %collective-permute-done.4 = bf16[12,7296]{1,0:T(8,128)(2,1)S(1)} collective-permute-done((bf16[12,7296]{1,0:T(8,128)(2,1)S(1)}, bf16[12,7296]{1,0:T(8,128)(2,1)S(1)}, u32[]{:S(2)}, u32[]{:S(2)}) %collective-permute-start.4) | collective-permute-done | bytes 175136 | tf_op jit(solution)/shard_map/ppermute | solution.py:33
  17.9 0.2 broadcast_select_fusion.3
  18.3 1.8 %collective-permute-done.5 = bf16[32,7296]{1,0:T(8,128)(2,1)S(1)} collective-permute-done((bf16[32,7296]{1,0:T(8,128)(2,1)S(1)}, bf16[32,7296]{1,0:T(8,128)(2,1)S(1)}, u32[]{:S(2)}, u32[]{:S(2)}) %collective-permute-start.5) | collective-permute-done | bytes 466976 | tf_op jit(solution)/shard_map/ppermute | solution.py:33
  20.1 0.2 broadcast_select_fusion.1
  20.3 0.1 pad_maximum_fusion.x
  20.3 0.5 convolution_convert_fusion.1
  20.8 1.3 %collective-permute-start.8 = (bf16[64,128]{1,0:T(8,128)(2,1)S(1)}, bf16[64,128]{1,0:T(8,128)(2,1)S(1)}, u32[]{:S(2)}, u32[]{:S(2)}) collective-permute-start(bf16[64,128]{1,0:T(8,128)(2,1)S(1)} %convolution_convert_fusion.1), channel_id=1, source_target_pairs={{0,3},{1,2},{2,1},{3,0},{4,7},{5,6},{6,5},{7,4},{8,11},{9,10},{10,... | collective-permute-start | bytes 49160 | tf_op jit(solution)/shard_map/ppermute | solution.py:33
  22.1 0.5 %collective-permute-start.7 = (bf16[64,128]{1,0:T(8,128)(2,1)S(1)}, bf16[64,128]{1,0:T(8,128)(2,1)S(1)}, u32[]{:S(2)}, u32[]{:S(2)}) collective-permute-start(bf16[64,128]{1,0:T(8,128)(2,1)S(1)} %convolution_convert_fusion.1), channel_id=1, source_target_pairs={{0,2},{1,3},{2,0},{3,1},{4,6},{5,7},{6,4},{7,5},{8,10},{9,11},{10,... | collective-permute-start | bytes 49160 | tf_op jit(solution)/shard_map/ppermute | solution.py:33
  22.7 0.1 collective-permute-start.6
  22.8 4.4 %shard_map.101 = f32[128,256]{1,0:T(8,128)S(1)} custom-call(bf16[64,7296]{1,0:T(8,128)(2,1)S(1)} %pad_maximum_fusion.x, bf16[7168,2,256]{2,1,0:T(2,128)(2,1)} %bitcast.64), custom_call_target="tpu_custom_call" | custom-call | flops 469762048 | bytes 7340032 | tf_op jit(solution)/shard_map/pallas_call | solution.py:135
  27.2 0.1 dynamic-slice_convert_fusion
  27.3 0.1 copy.14
  27.5 0.2 fusion.9
  27.7 0.1 multiply_reduce_fusion
  27.8 0.3 copy-done.3
  28.2 0.2 convolution_convert_fusion
  28.4 0.5 collective-permute-start.9
  28.9 0.2 dynamic-slice_reduce_fusion
  29.0 0.7 %collective-permute-done.9 = bf16[2,64,128]{2,1,0:T(8,128)(2,1)S(1)} collective-permute-done((bf16[2,64,128]{2,1,0:T(8,128)(2,1)S(1)}, bf16[2,64,128]{2,1,0:T(8,128)(2,1)S(1)}, u32[]{:S(2)}, u32[]{:S(2)}) %collective-permute-start.9) | collective-permute-done | bytes 32800 | tf_op jit(solution)/shard_map/ppermute | solution.py:33
  29.8 1.6 %collective-permute-start.10 = (bf16[64,128]{1,0:T(8,128)(2,1)S(1)}, bf16[64,128]{1,0:T(8,128)(2,1)S(1)}, u32[]{:S(2)}, u32[]{:S(2)}) collective-permute-start(bf16[64,128]{1,0:T(8,128)(2,1)S(1)} %dynamic-slice_bitcast_fusion.1), channel_id=1, source_target_pairs={{0,2},{1,3},{2,0},{3,1},{4,6},{5,7},{6,4},{7,5},{8,10},{9,11},{10,... | collective-permute-start | bytes 49160 | tf_op jit(solution)/shard_map/ppermute | solution.py:33
  31.3 2.9 %fusion.2 = f32[64,7168]{1,0:T(8,128)S(1)} fusion(bf16[1,256,7168]{2,1,0:T(8,128)(2,1)} %param.15, bf16[64,256]{1,0:T(8,128)(2,1)S(1)} %get-tuple-element.21), kind=kOutput, calls=%fused_computation.4 | convolution fusion | flops 234881024 | bytes 5537792 | tf_op jit(solution)/shard_map/dot_general | solution.py:259
  34.3 0.3 fusion.1.term
  34.7 0.1 collective-permute-start.15
  34.8 0.3 fusion.term
  35.2 0.5 collective-permute-start.11
  35.7 0.5 %collective-permute-done.15.received = bf16[32,3584]{1,0:T(8,128)(2,1)S(1)} collective-permute-done((bf16[32,3584]{1,0:T(8,128)(2,1)S(1)}, bf16[32,3584]{1,0:T(8,128)(2,1)S(1)}, u32[]{:S(2)}, u32[]{:S(2)}) %collective-permute-start.15) | collective-permute-done | bytes 229408 | tf_op jit(solution)/shard_map/ppermute | solution.py:33
  36.2 0.1 shard_map.103
  36.3 0.9 %collective-permute-start.16 = (bf16[16,3584]{1,0:T(8,128)(2,1)S(1)}, bf16[16,3584]{1,0:T(8,128)(2,1)S(1)}, u32[]{:S(2)}, u32[]{:S(2)}) collective-permute-start(bf16[16,3584]{1,0:T(8,128)(2,1)S(1)} %get-tuple-element.20), channel_id=1, source_target_pairs={{0,2},{1,5},{2,0},{3,7},{4,6},{5,1},{6,4},{7,3},{8,10},{9,13},{10,... | collective-permute-start | bytes 344072 | tf_op jit(solution)/shard_map/ppermute | solution.py:33
  37.2 0.1 shard_map.102
  37.3 1.3 %collective-permute-start.12 = (bf16[16,3584]{1,0:T(8,128)(2,1)S(1)}, bf16[16,3584]{1,0:T(8,128)(2,1)S(1)}, u32[]{:S(2)}, u32[]{:S(2)}) collective-permute-start(bf16[16,3584]{1,0:T(8,128)(2,1)S(1)} %get-tuple-element.18), channel_id=1, source_target_pairs={{0,2},{1,5},{2,0},{3,7},{4,6},{5,1},{6,4},{7,3},{8,10},{9,13},{10,... | collective-permute-start | bytes 344072 | tf_op jit(solution)/shard_map/ppermute | solution.py:33
  38.6 2.6 %collective-permute-done.16 = bf16[16,3584]{1,0:T(8,128)(2,1)S(1)} collective-permute-done((bf16[16,3584]{1,0:T(8,128)(2,1)S(1)}, bf16[16,3584]{1,0:T(8,128)(2,1)S(1)}, u32[]{:S(2)}, u32[]{:S(2)}) %collective-permute-start.16) | collective-permute-done | bytes 114720 | tf_op jit(solution)/shard_map/ppermute | solution.py:33
  41.2 1.7 %collective-permute-start.17 = (bf16[8,3584]{1,0:T(8,128)(2,1)S(1)}, bf16[8,3584]{1,0:T(8,128)(2,1)S(1)}, u32[]{:S(2)}, u32[]{:S(2)}) collective-permute-start(bf16[8,3584]{1,0:T(8,128)(2,1)S(1)} %broadcast_select_fusion.4), channel_id=1, source_target_pairs={{0,4},{1,3},{2,6},{3,1},{4,0},{5,7},{6,2},{7,5},{8,12},{9,11},{10,... | collective-permute-start | bytes 172040 | tf_op jit(solution)/shard_map/ppermute | solution.py:33
  42.9 1.2 %collective-permute-start.13 = (bf16[8,3584]{1,0:T(8,128)(2,1)S(1)}, bf16[8,3584]{1,0:T(8,128)(2,1)S(1)}, u32[]{:S(2)}, u32[]{:S(2)}) collective-permute-start(bf16[8,3584]{1,0:T(8,128)(2,1)S(1)} %broadcast_select_fusion.5), channel_id=1, source_target_pairs={{0,4},{1,3},{2,6},{3,1},{4,0},{5,7},{6,2},{7,5},{8,12},{9,11},{10,... | collective-permute-start | bytes 172040 | tf_op jit(solution)/shard_map/ppermute | solution.py:33
  44.1 1.3 %collective-permute-done.17 = bf16[8,3584]{1,0:T(8,128)(2,1)S(1)} collective-permute-done((bf16[8,3584]{1,0:T(8,128)(2,1)S(1)}, bf16[8,3584]{1,0:T(8,128)(2,1)S(1)}, u32[]{:S(2)}, u32[]{:S(2)}) %collective-permute-start.17) | collective-permute-done | bytes 57376 | tf_op jit(solution)/shard_map/ppermute | solution.py:33
  45.5 1.8 %collective-permute-start.18 = (bf16[4,3584]{1,0:T(4,128)(2,1)S(1)}, bf16[4,3584]{1,0:T(4,128)(2,1)S(1)}, u32[]{:S(2)}, u32[]{:S(2)}) collective-permute-start(bf16[4,3584]{1,0:T(4,128)(2,1)S(1)} %slice.113), channel_id=1, source_target_pairs={{0,8},{1,9},{2,10},{3,11},{4,12},{5,13},{6,14},{7,15},{8,0},{9,1},... | collective-permute-start | bytes 86024 | tf_op jit(solution)/shard_map/ppermute | solution.py:33
  47.4 2.0 %collective-permute-start.14 = (bf16[4,3584]{1,0:T(4,128)(2,1)S(1)}, bf16[4,3584]{1,0:T(4,128)(2,1)S(1)}, u32[]{:S(2)}, u32[]{:S(2)}) collective-permute-start(bf16[4,3584]{1,0:T(4,128)(2,1)S(1)} %slice.106), channel_id=1, source_target_pairs={{0,8},{1,9},{2,10},{3,11},{4,12},{5,13},{6,14},{7,15},{8,0},{9,1},... | collective-permute-start | bytes 86024 | tf_op jit(solution)/shard_map/ppermute | solution.py:33
  49.5 1.1 %collective-permute-done.18 = bf16[4,3584]{1,0:T(4,128)(2,1)S(1)} collective-permute-done((bf16[4,3584]{1,0:T(4,128)(2,1)S(1)}, bf16[4,3584]{1,0:T(4,128)(2,1)S(1)}, u32[]{:S(2)}, u32[]{:S(2)}) %collective-permute-start.18) | collective-permute-done | bytes 28704 | tf_op jit(solution)/shard_map/ppermute | solution.py:33
  50.6 1.7 %collective-permute-done.14 = bf16[4,3584]{1,0:T(4,128)(2,1)S(1)} collective-permute-done((bf16[4,3584]{1,0:T(4,128)(2,1)S(1)}, bf16[4,3584]{1,0:T(4,128)(2,1)S(1)}, u32[]{:S(2)}, u32[]{:S(2)}) %collective-permute-start.14) | collective-permute-done | bytes 28704 | tf_op jit(solution)/shard_map/ppermute | solution.py:33
  52.3 0.7 %maximum_bitcast_fusion.2 = bf16[1,4,7168]{2,1,0:T(4,128)(2,1)} fusion(bf16[4,3584]{1,0:T(4,128)(2,1)S(1)} %add_convert_fusion.4, bf16[4,3584]{1,0:T(4,128)(2,1)S(1)} %add_convert_fusion.5), kind=kLoop, calls=%fused_computation.48 | loop fusion | flops 114688 | bytes 114688 | tf_op jit(solution)/shard_map/broadcast_in_dim | solution.py:288
  (37 shorter events, 0.5 us)
Async XLA Ops:
  0.0 20.3 %copy-start = (bf16[1,7168,128]{2,1,0:T(8,128)(2,1)S(1)}, bf16[1,7168,128]{2,1,0:T(8,128)(2,1)}, u32[]{:S(2)}) copy-start(bf16[1,7168,128]{2,1,0:T(8,128)(2,1)} %param.16) | copy-start | bytes 5505028
  1.1 7.8 %collective-permute-start.2 = (bf16[4,7296]{1,0:T(4,128)(2,1)S(1)}, bf16[4,7296]{1,0:T(4,128)(2,1)S(1)}, u32[]{:S(2)}, u32[]{:S(2)}) collective-permute-start(bf16[4,7296]{1,0:T(4,128)(2,1)S(1)} %shard_map.100), channel_id=1, source_target_pairs={{0,12},{1,13},{2,14},{3,15},{4,8},{5,9},{6,10},{7,11},{8,4},{9,5},... | collective-permute-start | bytes 175112 | tf_op jit(solution)/shard_map/ppermute | solution.py:33
  6.2 4.3 %collective-permute-start.1 = (bf16[4,7296]{1,0:T(4,128)(2,1)S(1)}, bf16[4,7296]{1,0:T(4,128)(2,1)S(1)}, u32[]{:S(2)}, u32[]{:S(2)}) collective-permute-start(bf16[4,7296]{1,0:T(4,128)(2,1)S(1)} %shard_map.100), channel_id=1, source_target_pairs={{0,4},{1,5},{2,6},{3,7},{4,0},{5,1},{6,2},{7,3},{8,12},{9,13},{10,... | collective-permute-start | bytes 175112 | tf_op jit(solution)/shard_map/ppermute | solution.py:33
  6.2 5.5 %collective-permute-start = (bf16[4,7296]{1,0:T(4,128)(2,1)S(1)}, bf16[4,7296]{1,0:T(4,128)(2,1)S(1)}, u32[]{:S(2)}, u32[]{:S(2)}) collective-permute-start(bf16[4,7296]{1,0:T(4,128)(2,1)S(1)} %shard_map.100), channel_id=1, source_target_pairs={{0,8},{1,9},{2,10},{3,11},{4,12},{5,13},{6,14},{7,15},{8,0},{9,1},... | collective-permute-start | bytes 175112 | tf_op jit(solution)/shard_map/ppermute | solution.py:33
  6.9 4.9 %collective-permute-start.3 = (bf16[4,7296]{1,0:T(4,128)(2,1)S(1)}, bf16[4,7296]{1,0:T(4,128)(2,1)S(1)}, u32[]{:S(2)}, u32[]{:S(2)}) collective-permute-start(bf16[4,7296]{1,0:T(4,128)(2,1)S(1)} %shard_map.100), channel_id=1, source_target_pairs={{0,2},{1,3},{2,0},{3,1},{4,6},{5,7},{6,4},{7,5},{8,10},{9,11},{10,... | collective-permute-start | bytes 175112 | tf_op jit(solution)/shard_map/ppermute | solution.py:33
  11.8 6.1 %collective-permute-start.4 = (bf16[12,7296]{1,0:T(8,128)(2,1)S(1)}, bf16[12,7296]{1,0:T(8,128)(2,1)S(1)}, u32[]{:S(2)}, u32[]{:S(2)}) collective-permute-start(bf16[12,7296]{1,0:T(8,128)(2,1)S(1)} %pad_maximum_fusion.2), channel_id=1, source_target_pairs={{0,2},{1,3},{2,0},{3,1},{4,6},{5,7},{6,4},{7,5},{8,10},{9,11},{10,... | collective-permute-start | bytes 525320 | tf_op jit(solution)/shard_map/ppermute | solution.py:33
  18.2 1.9 %collective-permute-start.5 = (bf16[32,7296]{1,0:T(8,128)(2,1)S(1)}, bf16[32,7296]{1,0:T(8,128)(2,1)S(1)}, u32[]{:S(2)}, u32[]{:S(2)}) collective-permute-start(bf16[32,7296]{1,0:T(8,128)(2,1)S(1)} %pad_maximum_fusion.1), channel_id=1, source_target_pairs={{0,1},{1,0},{2,3},{3,2},{4,5},{5,4},{6,7},{7,6},{8,9},{9,8},{10,11... | collective-permute-start | bytes 1400840 | tf_op jit(solution)/shard_map/ppermute | solution.py:33
  20.8 6.6 %collective-permute-start.8 = (bf16[64,128]{1,0:T(8,128)(2,1)S(1)}, bf16[64,128]{1,0:T(8,128)(2,1)S(1)}, u32[]{:S(2)}, u32[]{:S(2)}) collective-permute-start(bf16[64,128]{1,0:T(8,128)(2,1)S(1)} %convolution_convert_fusion.1), channel_id=1, source_target_pairs={{0,3},{1,2},{2,1},{3,0},{4,7},{5,6},{6,5},{7,4},{8,11},{9,10},{10,... | collective-permute-start | bytes 49160 | tf_op jit(solution)/shard_map/ppermute | solution.py:33
  22.1 5.3 %collective-permute-start.7 = (bf16[64,128]{1,0:T(8,128)(2,1)S(1)}, bf16[64,128]{1,0:T(8,128)(2,1)S(1)}, u32[]{:S(2)}, u32[]{:S(2)}) collective-permute-start(bf16[64,128]{1,0:T(8,128)(2,1)S(1)} %convolution_convert_fusion.1), channel_id=1, source_target_pairs={{0,2},{1,3},{2,0},{3,1},{4,6},{5,7},{6,4},{7,5},{8,10},{9,11},{10,... | collective-permute-start | bytes 49160 | tf_op jit(solution)/shard_map/ppermute | solution.py:33
  22.7 4.7 %collective-permute-start.6 = (bf16[64,128]{1,0:T(8,128)(2,1)S(1)}, bf16[64,128]{1,0:T(8,128)(2,1)S(1)}, u32[]{:S(2)}, u32[]{:S(2)}) collective-permute-start(bf16[64,128]{1,0:T(8,128)(2,1)S(1)} %convolution_convert_fusion.1), channel_id=1, source_target_pairs={{0,1},{1,0},{2,3},{3,2},{4,5},{5,4},{6,7},{7,6},{8,9},{9,8},{10,11... | collective-permute-start | bytes 49160 | tf_op jit(solution)/shard_map/ppermute | solution.py:33
  22.7 4.7 %copy-start.2 = (bf16[1,4,128,2,256]{4,3,2,1,0:T(2,128)(2,1)S(1)}, bf16[1,4,128,2,256]{4,3,2,1,0:T(2,128)(2,1)}, u32[]{:S(2)}) copy-start(bf16[1,4,128,2,256]{4,3,2,1,0:T(2,128)(2,1)} %param.17) | copy-start | bytes 1572868
  27.2 1.0 %copy-start.3 = (bf16[1,4,256,128]{3,2,1,0:T(8,128)(2,1)S(1)}, bf16[1,4,256,128]{3,2,1,0:T(8,128)(2,1)}, u32[]{:S(2)}) copy-start(bf16[1,4,256,128]{3,2,1,0:T(8,128)(2,1)} %param.18) | copy-start | bytes 786436
  28.4 1.4 %collective-permute-start.9 = (bf16[2,64,128]{2,1,0:T(8,128)(2,1)S(1)}, bf16[2,64,128]{2,1,0:T(8,128)(2,1)S(1)}, u32[]{:S(2)}, u32[]{:S(2)}) collective-permute-start(bf16[2,64,128]{2,1,0:T(8,128)(2,1)S(1)} %dynamic-slice_bitcast_fusion), channel_id=1, source_target_pairs={{0,1},{1,0},{2,3},{3,2},{4,5},{5,4},{6,7},{7,6},{8,9},{9,8},{10,11... | collective-permute-start | bytes 98312 | tf_op jit(solution)/shard_map/ppermute | solution.py:33
  29.8 4.5 %collective-permute-start.10 = (bf16[64,128]{1,0:T(8,128)(2,1)S(1)}, bf16[64,128]{1,0:T(8,128)(2,1)S(1)}, u32[]{:S(2)}, u32[]{:S(2)}) collective-permute-start(bf16[64,128]{1,0:T(8,128)(2,1)S(1)} %dynamic-slice_bitcast_fusion.1), channel_id=1, source_target_pairs={{0,2},{1,3},{2,0},{3,1},{4,6},{5,7},{6,4},{7,5},{8,10},{9,11},{10,... | collective-permute-start | bytes 49160 | tf_op jit(solution)/shard_map/ppermute | solution.py:33
  31.3 2.9 %copy-start.1 = (bf16[1,128,7168]{2,1,0:T(8,128)(2,1)S(1)}, bf16[1,128,7168]{2,1,0:T(8,128)(2,1)}, u32[]{:S(2)}) copy-start(bf16[1,128,7168]{2,1,0:T(8,128)(2,1)} %param.19) | copy-start | bytes 5505028
  34.7 1.6 %collective-permute-start.15 = (bf16[32,3584]{1,0:T(8,128)(2,1)S(1)}, bf16[32,3584]{1,0:T(8,128)(2,1)S(1)}, u32[]{:S(2)}, u32[]{:S(2)}) collective-permute-start(bf16[32,3584]{1,0:T(8,128)(2,1)S(1)} %slice_select_fusion), channel_id=1, source_target_pairs={{0,1},{1,0},{2,3},{3,2},{4,5},{5,4},{6,7},{7,6},{8,9},{9,8},{10,11... | collective-permute-start | bytes 688136 | tf_op jit(solution)/shard_map/ppermute | solution.py:33
  35.2 2.0 %collective-permute-start.11 = (bf16[32,3584]{1,0:T(8,128)(2,1)S(1)}, bf16[32,3584]{1,0:T(8,128)(2,1)S(1)}, u32[]{:S(2)}, u32[]{:S(2)}) collective-permute-start(bf16[32,3584]{1,0:T(8,128)(2,1)S(1)} %slice_select_fusion.1), channel_id=1, source_target_pairs={{0,1},{1,0},{2,3},{3,2},{4,5},{5,4},{6,7},{7,6},{8,9},{9,8},{10,11... | collective-permute-start | bytes 688136 | tf_op jit(solution)/shard_map/ppermute | solution.py:33
  36.3 4.9 %collective-permute-start.16 = (bf16[16,3584]{1,0:T(8,128)(2,1)S(1)}, bf16[16,3584]{1,0:T(8,128)(2,1)S(1)}, u32[]{:S(2)}, u32[]{:S(2)}) collective-permute-start(bf16[16,3584]{1,0:T(8,128)(2,1)S(1)} %get-tuple-element.20), channel_id=1, source_target_pairs={{0,2},{1,5},{2,0},{3,7},{4,6},{5,1},{6,4},{7,3},{8,10},{9,13},{10,... | collective-permute-start | bytes 344072 | tf_op jit(solution)/shard_map/ppermute | solution.py:33
  37.3 5.6 %collective-permute-start.12 = (bf16[16,3584]{1,0:T(8,128)(2,1)S(1)}, bf16[16,3584]{1,0:T(8,128)(2,1)S(1)}, u32[]{:S(2)}, u32[]{:S(2)}) collective-permute-start(bf16[16,3584]{1,0:T(8,128)(2,1)S(1)} %get-tuple-element.18), channel_id=1, source_target_pairs={{0,2},{1,5},{2,0},{3,7},{4,6},{5,1},{6,4},{7,3},{8,10},{9,13},{10,... | collective-permute-start | bytes 344072 | tf_op jit(solution)/shard_map/ppermute | solution.py:33
  41.2 4.2 %collective-permute-start.17 = (bf16[8,3584]{1,0:T(8,128)(2,1)S(1)}, bf16[8,3584]{1,0:T(8,128)(2,1)S(1)}, u32[]{:S(2)}, u32[]{:S(2)}) collective-permute-start(bf16[8,3584]{1,0:T(8,128)(2,1)S(1)} %broadcast_select_fusion.4), channel_id=1, source_target_pairs={{0,4},{1,3},{2,6},{3,1},{4,0},{5,7},{6,2},{7,5},{8,12},{9,11},{10,... | collective-permute-start | bytes 172040 | tf_op jit(solution)/shard_map/ppermute | solution.py:33
  42.9 4.4 %collective-permute-start.13 = (bf16[8,3584]{1,0:T(8,128)(2,1)S(1)}, bf16[8,3584]{1,0:T(8,128)(2,1)S(1)}, u32[]{:S(2)}, u32[]{:S(2)}) collective-permute-start(bf16[8,3584]{1,0:T(8,128)(2,1)S(1)} %broadcast_select_fusion.5), channel_id=1, source_target_pairs={{0,4},{1,3},{2,6},{3,1},{4,0},{5,7},{6,2},{7,5},{8,12},{9,11},{10,... | collective-permute-start | bytes 172040 | tf_op jit(solution)/shard_map/ppermute | solution.py:33
  45.5 5.0 %collective-permute-start.18 = (bf16[4,3584]{1,0:T(4,128)(2,1)S(1)}, bf16[4,3584]{1,0:T(4,128)(2,1)S(1)}, u32[]{:S(2)}, u32[]{:S(2)}) collective-permute-start(bf16[4,3584]{1,0:T(4,128)(2,1)S(1)} %slice.113), channel_id=1, source_target_pairs={{0,8},{1,9},{2,10},{3,11},{4,12},{5,13},{6,14},{7,15},{8,0},{9,1},... | collective-permute-start | bytes 86024 | tf_op jit(solution)/shard_map/ppermute | solution.py:33
  47.4 4.8 %collective-permute-start.14 = (bf16[4,3584]{1,0:T(4,128)(2,1)S(1)}, bf16[4,3584]{1,0:T(4,128)(2,1)S(1)}, u32[]{:S(2)}, u32[]{:S(2)}) collective-permute-start(bf16[4,3584]{1,0:T(4,128)(2,1)S(1)} %slice.106), channel_id=1, source_target_pairs={{0,8},{1,9},{2,10},{3,11},{4,12},{5,13},{6,14},{7,15},{8,0},{9,1},... | collective-permute-start | bytes 86024 | tf_op jit(solution)/shard_map/ppermute | solution.py:33

commit v28 on v27

--- a/solution.py
+++ b/solution.py
@@ -11,6 +11,7 @@
 
 CHUNKS = 2
 PIECES = (1, 2, 4, 4)
+DOWN_PIECES = (1, 3)
 VMEM = pl.BlockSpec(memory_space=pltpu.VMEM)
 HBM = pl.BlockSpec(memory_space=pltpu.HBM)
 
@@ -143,6 +144,36 @@
             flops=4 * x.shape[0] * depth * columns, bytes_accessed=2 * base.size, transcendentals=0
         ),
     )(x, in_hbm(base))
+
+
+def down_kernel(hidden, base, out, weights, sems):
+    step = 1024
+    copies = {
+        low: pltpu.make_async_copy(
+            base.at[:, pl.ds(low, high - low)], weights.at[:, pl.ds(low, high - low)], sems.at[i]
+        )
+        for i, (low, high) in enumerate(piece_bounds(base.shape[1], step, DOWN_PIECES))
+    }
+    for copy in copies.values():
+        copy.start()
+    for k in range(0, base.shape[1], step):
+        if k in copies:
+            copies[k].wait()
+        part = pl.ds(k, step)
+        out[:, part] = jnp.dot(hidden[...], weights[:, part], preferred_element_type=jnp.float32)
+
+
+def down_product(hidden, base):
+    rows, width = hidden.shape[0], base.shape[1]
+    return pl.pallas_call(
+        down_kernel,
+        out_shape=jax.ShapeDtypeStruct((rows, width), jnp.float32),
+        in_specs=[VMEM, HBM],
+        out_specs=VMEM,
+        scratch_shapes=[pltpu.VMEM(base.shape, base.dtype), pltpu.SemaphoreType.DMA((len(DOWN_PIECES) + 1,))],
+        compiler_params=pltpu.CompilerParams(vmem_limit_bytes=16 << 20),
+        cost_estimate=pl.CostEstimate(flops=2 * rows * base.size, bytes_accessed=2 * base.size, transcendentals=0),
+    )(hidden, in_hbm(base))
 
 
 def part_kernel(bit, term, received, *refs):
@@ -256,7 +287,7 @@
     own_scale = lax.dynamic_index_in_dim(scale, me, 0, keepdims=False)
     scaled = (own_scale[:, None] * lowrank).astype(jnp.bfloat16)
 
-    base = jnp.dot(hidden_sum, base_down[0], preferred_element_type=jnp.float32)
+    base = down_product(hidden_sum, base_down[0])
 
     half, step = base.shape[0] // 2, width // CHUNKS
     outputs = []

time: 53.1 us -> 52.8 us (level)
  matrix products: 4.44 us -> 1.52 us
  Pallas kernels: 5.72 us -> 8.31 us
    dot_general x1 -> x0, matrix products: 2.92 us -> none  [local(): base = jnp.dot(hidden_sum, base_down[0], preferred_element_type=jnp.float32)]
    pallas_call x0 -> x1, Pallas kernels: none -> 2.59 us  [down_product(): pl.pallas_call(down_kernel, out_shape=jax.ShapeDtypeStruct((rows, width),...]
  transfers between devices with their start and end apart: 19 -> 19, of which waited for: 11 -> 11; matrix products, arithmetic and copies ran while one was open for 7% -> 2% of each run, Pallas kernels for 9% -> 14%
where the time goes in v28:
time: 52.8 us; the launch traced here: 52.6 us
  starting transfers between devices  22.6 us (43%)
  waiting for transfers between devices  17.4 us (33%)
  Pallas kernels  8.31 us (16%)
  other arithmetic  1.68 us (3%)
  matrix products  1.52 us (3%)
  local copies, waits for them, and re-layouts  0.69 us (1%)
    ppermute x19, starting transfers between devices, trade(): return lax.ppermute(value, ('expert', 'tensor'), pairs)  22.6 us
    ppermute x19, waiting for transfers between devices, trade(): return lax.ppermute(value, ('expert', 'tensor'), pairs)  17.4 us
    pallas_call x1, Pallas kernels, gate_up_product(): pl.pallas_call(gate_up_kernel, out_shape=jax.ShapeDtypeStruct((2 * x.shap...  4.44 us
    pallas_call x1, Pallas kernels, down_product(): pl.pallas_call(down_kernel, out_shape=jax.ShapeDtypeStruct((rows, width),...  2.59 us
    pallas_call x1, Pallas kernels, pack(): pl.pallas_call(pack_kernel, out_shape=jax.ShapeDtypeStruct((count, width...  1.09 us
  transfers between devices with their start and end apart: 19, of which 11 were waited for; matrix products, arithmetic and copies ran while one was open for 2% of the time, Pallas kernels for 14%

profile of v28, /device:TPU:0, one launch (start us, length us, event | category | flops | bytes accessed | tf_op | source)
XLA Modules:
  0.0 52.6 jit_solution(10927466472653024555)
XLA Ops:
  0.0 1.1 %shard_map.100 = bf16[4,7296]{1,0:T(4,128)(2,1)S(1)} custom-call(bf16[4,7168]{1,0:T(4,128)(2,1)} %bitcast.70, s32[4,8]{1,0:T(4,128)} %bitcast.71, s32[4,8]{1,0:T(4,128)} %bitcast.72, s32[16]{0:T(128)} %place.1), custom_call_target="tpu_custom_call" | custom-call | flops 20000000000 | bytes 114688 | tf_op jit(solution)/shard_map/pallas_call | solution.py:81
  1.1 5.1 %collective-permute-start.2 = (bf16[4,7296]{1,0:T(4,128)(2,1)S(1)}, bf16[4,7296]{1,0:T(4,128)(2,1)S(1)}, u32[]{:S(2)}, u32[]{:S(2)}) collective-permute-start(bf16[4,7296]{1,0:T(4,128)(2,1)S(1)} %shard_map.100), channel_id=1, source_target_pairs={{0,12},{1,13},{2,14},{3,15},{4,8},{5,9},{6,10},{7,11},{8,4},{9,5},... | collective-permute-start | bytes 175112 | tf_op jit(solution)/shard_map/ppermute | solution.py:34
  6.2 0.6 %collective-permute-start = (bf16[4,7296]{1,0:T(4,128)(2,1)S(1)}, bf16[4,7296]{1,0:T(4,128)(2,1)S(1)}, u32[]{:S(2)}, u32[]{:S(2)}) collective-permute-start(bf16[4,7296]{1,0:T(4,128)(2,1)S(1)} %shard_map.100), channel_id=1, source_target_pairs={{0,8},{1,9},{2,10},{3,11},{4,12},{5,13},{6,14},{7,15},{8,0},{9,1},... | collective-permute-start | bytes 175112 | tf_op jit(solution)/shard_map/ppermute | solution.py:34
  6.9 1.6 %collective-permute-start.3 = (bf16[4,7296]{1,0:T(4,128)(2,1)S(1)}, bf16[4,7296]{1,0:T(4,128)(2,1)S(1)}, u32[]{:S(2)}, u32[]{:S(2)}) collective-permute-start(bf16[4,7296]{1,0:T(4,128)(2,1)S(1)} %shard_map.100), channel_id=1, source_target_pairs={{0,2},{1,3},{2,0},{3,1},{4,6},{5,7},{6,4},{7,5},{8,10},{9,11},{10,... | collective-permute-start | bytes 175112 | tf_op jit(solution)/shard_map/ppermute | solution.py:34
  8.5 0.4 collective-permute-done.2
  8.9 1.7 %collective-permute-done.1 = bf16[4,7296]{1,0:T(4,128)(2,1)S(1)} collective-permute-done((bf16[4,7296]{1,0:T(4,128)(2,1)S(1)}, bf16[4,7296]{1,0:T(4,128)(2,1)S(1)}, u32[]{:S(2)}, u32[]{:S(2)}) %collective-permute-start.1) | collective-permute-done | bytes 58400 | tf_op jit(solution)/shard_map/ppermute | solution.py:34
  10.6 1.1 %collective-permute-done = bf16[4,7296]{1,0:T(4,128)(2,1)S(1)} collective-permute-done((bf16[4,7296]{1,0:T(4,128)(2,1)S(1)}, bf16[4,7296]{1,0:T(4,128)(2,1)S(1)}, u32[]{:S(2)}, u32[]{:S(2)}) %collective-permute-start) | collective-permute-done | bytes 58400 | tf_op jit(solution)/shard_map/ppermute | solution.py:34
  11.7 0.1 pad_maximum_fusion.2
  11.8 1.6 %collective-permute-start.4 = (bf16[12,7296]{1,0:T(8,128)(2,1)S(1)}, bf16[12,7296]{1,0:T(8,128)(2,1)S(1)}, u32[]{:S(2)}, u32[]{:S(2)}) collective-permute-start(bf16[12,7296]{1,0:T(8,128)(2,1)S(1)} %pad_maximum_fusion.2), channel_id=1, source_target_pairs={{0,2},{1,3},{2,0},{3,1},{4,6},{5,7},{6,4},{7,5},{8,10},{9,11},{10,... | collective-permute-start | bytes 525320 | tf_op jit(solution)/shard_map/ppermute | solution.py:34
  13.4 4.6 %collective-permute-done.4 = bf16[12,7296]{1,0:T(8,128)(2,1)S(1)} collective-permute-done((bf16[12,7296]{1,0:T(8,128)(2,1)S(1)}, bf16[12,7296]{1,0:T(8,128)(2,1)S(1)}, u32[]{:S(2)}, u32[]{:S(2)}) %collective-permute-start.4) | collective-permute-done | bytes 175136 | tf_op jit(solution)/shard_map/ppermute | solution.py:34
  17.9 0.2 broadcast_select_fusion.3
  18.3 1.8 %collective-permute-done.5 = bf16[32,7296]{1,0:T(8,128)(2,1)S(1)} collective-permute-done((bf16[32,7296]{1,0:T(8,128)(2,1)S(1)}, bf16[32,7296]{1,0:T(8,128)(2,1)S(1)}, u32[]{:S(2)}, u32[]{:S(2)}) %collective-permute-start.5) | collective-permute-done | bytes 466976 | tf_op jit(solution)/shard_map/ppermute | solution.py:34
  20.1 0.2 broadcast_select_fusion.1
  20.3 0.1 pad_maximum_fusion.x
  20.3 0.5 convolution_convert_fusion.1
  20.8 1.3 %collective-permute-start.8 = (bf16[64,128]{1,0:T(8,128)(2,1)S(1)}, bf16[64,128]{1,0:T(8,128)(2,1)S(1)}, u32[]{:S(2)}, u32[]{:S(2)}) collective-permute-start(bf16[64,128]{1,0:T(8,128)(2,1)S(1)} %convolution_convert_fusion.1), channel_id=1, source_target_pairs={{0,3},{1,2},{2,1},{3,0},{4,7},{5,6},{6,5},{7,4},{8,11},{9,10},{10,... | collective-permute-start | bytes 49160 | tf_op jit(solution)/shard_map/ppermute | solution.py:34
  22.1 0.5 %collective-permute-start.7 = (bf16[64,128]{1,0:T(8,128)(2,1)S(1)}, bf16[64,128]{1,0:T(8,128)(2,1)S(1)}, u32[]{:S(2)}, u32[]{:S(2)}) collective-permute-start(bf16[64,128]{1,0:T(8,128)(2,1)S(1)} %convolution_convert_fusion.1), channel_id=1, source_target_pairs={{0,2},{1,3},{2,0},{3,1},{4,6},{5,7},{6,4},{7,5},{8,10},{9,11},{10,... | collective-permute-start | bytes 49160 | tf_op jit(solution)/shard_map/ppermute | solution.py:34
  22.7 0.1 collective-permute-start.6
  22.8 4.4 %shard_map.101 = f32[128,256]{1,0:T(8,128)S(1)} custom-call(bf16[64,7296]{1,0:T(8,128)(2,1)S(1)} %pad_maximum_fusion.x, bf16[7168,2,256]{2,1,0:T(2,128)(2,1)} %bitcast.61), custom_call_target="tpu_custom_call" | custom-call | flops 469762048 | bytes 7340032 | tf_op jit(solution)/shard_map/pallas_call | solution.py:136
  27.2 0.1 dynamic-slice_convert_fusion
  27.3 0.1 copy.14
  27.5 0.2 fusion.7
  27.7 0.1 multiply_reduce_fusion
  27.8 0.3 copy-done.3
  28.2 0.2 convolution_convert_fusion
  28.4 0.5 collective-permute-start.9
  28.9 0.2 dynamic-slice_reduce_fusion
  29.0 0.7 %collective-permute-done.9 = bf16[2,64,128]{2,1,0:T(8,128)(2,1)S(1)} collective-permute-done((bf16[2,64,128]{2,1,0:T(8,128)(2,1)S(1)}, bf16[2,64,128]{2,1,0:T(8,128)(2,1)S(1)}, u32[]{:S(2)}, u32[]{:S(2)}) %collective-permute-start.9) | collective-permute-done | bytes 32800 | tf_op jit(solution)/shard_map/ppermute | solution.py:34
  29.8 1.6 %collective-permute-start.10 = (bf16[64,128]{1,0:T(8,128)(2,1)S(1)}, bf16[64,128]{1,0:T(8,128)(2,1)S(1)}, u32[]{:S(2)}, u32[]{:S(2)}) collective-permute-start(bf16[64,128]{1,0:T(8,128)(2,1)S(1)} %dynamic-slice_bitcast_fusion.1), channel_id=1, source_target_pairs={{0,2},{1,3},{2,0},{3,1},{4,6},{5,7},{6,4},{7,5},{8,10},{9,11},{10,... | collective-permute-start | bytes 49160 | tf_op jit(solution)/shard_map/ppermute | solution.py:34
  31.3 2.6 %shard_map.102 = f32[64,7168]{1,0:T(8,128)S(1)} custom-call(bf16[64,256]{1,0:T(8,128)(2,1)S(1)} %get-tuple-element.21.hidden, bf16[256,7168]{1,0:T(8,128)(2,1)} %bitcast.62), custom_call_target="tpu_custom_call" | custom-call | flops 234881024 | bytes 3670016 | tf_op jit(solution)/shard_map/pallas_call | solution.py:168
  34.0 0.3 fusion.1.term
  34.3 0.1 collective-permute-start.15
  34.5 0.3 fusion.term
  34.8 0.5 collective-permute-start.11
  35.3 0.5 %collective-permute-done.15.received = bf16[32,3584]{1,0:T(8,128)(2,1)S(1)} collective-permute-done((bf16[32,3584]{1,0:T(8,128)(2,1)S(1)}, bf16[32,3584]{1,0:T(8,128)(2,1)S(1)}, u32[]{:S(2)}, u32[]{:S(2)}) %collective-permute-start.15) | collective-permute-done | bytes 229408 | tf_op jit(solution)/shard_map/ppermute | solution.py:34
  35.9 0.1 shard_map.104
  36.0 1.2 %collective-permute-start.16 = (bf16[16,3584]{1,0:T(8,128)(2,1)S(1)}, bf16[16,3584]{1,0:T(8,128)(2,1)S(1)}, u32[]{:S(2)}, u32[]{:S(2)}) collective-permute-start(bf16[16,3584]{1,0:T(8,128)(2,1)S(1)} %get-tuple-element.20), channel_id=1, source_target_pairs={{0,2},{1,5},{2,0},{3,7},{4,6},{5,1},{6,4},{7,3},{8,10},{9,13},{10,... | collective-permute-start | bytes 344072 | tf_op jit(solution)/shard_map/ppermute | solution.py:34
  37.2 0.1 shard_map.103
  37.3 1.0 %collective-permute-start.12 = (bf16[16,3584]{1,0:T(8,128)(2,1)S(1)}, bf16[16,3584]{1,0:T(8,128)(2,1)S(1)}, u32[]{:S(2)}, u32[]{:S(2)}) collective-permute-start(bf16[16,3584]{1,0:T(8,128)(2,1)S(1)} %get-tuple-element.18), channel_id=1, source_target_pairs={{0,2},{1,5},{2,0},{3,7},{4,6},{5,1},{6,4},{7,3},{8,10},{9,13},{10,... | collective-permute-start | bytes 344072 | tf_op jit(solution)/shard_map/ppermute | solution.py:34
  38.2 2.6 %collective-permute-done.16 = bf16[16,3584]{1,0:T(8,128)(2,1)S(1)} collective-permute-done((bf16[16,3584]{1,0:T(8,128)(2,1)S(1)}, bf16[16,3584]{1,0:T(8,128)(2,1)S(1)}, u32[]{:S(2)}, u32[]{:S(2)}) %collective-permute-start.16) | collective-permute-done | bytes 114720 | tf_op jit(solution)/shard_map/ppermute | solution.py:34
  40.9 1.7 %collective-permute-start.17 = (bf16[8,3584]{1,0:T(8,128)(2,1)S(1)}, bf16[8,3584]{1,0:T(8,128)(2,1)S(1)}, u32[]{:S(2)}, u32[]{:S(2)}) collective-permute-start(bf16[8,3584]{1,0:T(8,128)(2,1)S(1)} %broadcast_select_fusion.4), channel_id=1, source_target_pairs={{0,4},{1,3},{2,6},{3,1},{4,0},{5,7},{6,2},{7,5},{8,12},{9,11},{10,... | collective-permute-start | bytes 172040 | tf_op jit(solution)/shard_map/ppermute | solution.py:34
  42.6 1.2 %collective-permute-start.13 = (bf16[8,3584]{1,0:T(8,128)(2,1)S(1)}, bf16[8,3584]{1,0:T(8,128)(2,1)S(1)}, u32[]{:S(2)}, u32[]{:S(2)}) collective-permute-start(bf16[8,3584]{1,0:T(8,128)(2,1)S(1)} %broadcast_select_fusion.5), channel_id=1, source_target_pairs={{0,4},{1,3},{2,6},{3,1},{4,0},{5,7},{6,2},{7,5},{8,12},{9,11},{10,... | collective-permute-start | bytes 172040 | tf_op jit(solution)/shard_map/ppermute | solution.py:34
  43.9 1.3 %collective-permute-done.17 = bf16[8,3584]{1,0:T(8,128)(2,1)S(1)} collective-permute-done((bf16[8,3584]{1,0:T(8,128)(2,1)S(1)}, bf16[8,3584]{1,0:T(8,128)(2,1)S(1)}, u32[]{:S(2)}, u32[]{:S(2)}) %collective-permute-start.17) | collective-permute-done | bytes 57376 | tf_op jit(solution)/shard_map/ppermute | solution.py:34
  45.2 1.8 %collective-permute-start.18 = (bf16[4,3584]{1,0:T(4,128)(2,1)S(1)}, bf16[4,3584]{1,0:T(4,128)(2,1)S(1)}, u32[]{:S(2)}, u32[]{:S(2)}) collective-permute-start(bf16[4,3584]{1,0:T(4,128)(2,1)S(1)} %slice.113), channel_id=1, source_target_pairs={{0,8},{1,9},{2,10},{3,11},{4,12},{5,13},{6,14},{7,15},{8,0},{9,1},... | collective-permute-start | bytes 86024 | tf_op jit(solution)/shard_map/ppermute | solution.py:34
  47.1 2.0 %collective-permute-start.14 = (bf16[4,3584]{1,0:T(4,128)(2,1)S(1)}, bf16[4,3584]{1,0:T(4,128)(2,1)S(1)}, u32[]{:S(2)}, u32[]{:S(2)}) collective-permute-start(bf16[4,3584]{1,0:T(4,128)(2,1)S(1)} %slice.106), channel_id=1, source_target_pairs={{0,8},{1,9},{2,10},{3,11},{4,12},{5,13},{6,14},{7,15},{8,0},{9,1},... | collective-permute-start | bytes 86024 | tf_op jit(solution)/shard_map/ppermute | solution.py:34
  49.1 1.1 %collective-permute-done.18 = bf16[4,3584]{1,0:T(4,128)(2,1)S(1)} collective-permute-done((bf16[4,3584]{1,0:T(4,128)(2,1)S(1)}, bf16[4,3584]{1,0:T(4,128)(2,1)S(1)}, u32[]{:S(2)}, u32[]{:S(2)}) %collective-permute-start.18) | collective-permute-done | bytes 28704 | tf_op jit(solution)/shard_map/ppermute | solution.py:34
  50.3 1.7 %collective-permute-done.14 = bf16[4,3584]{1,0:T(4,128)(2,1)S(1)} collective-permute-done((bf16[4,3584]{1,0:T(4,128)(2,1)S(1)}, bf16[4,3584]{1,0:T(4,128)(2,1)S(1)}, u32[]{:S(2)}, u32[]{:S(2)}) %collective-permute-start.14) | collective-permute-done | bytes 28704 | tf_op jit(solution)/shard_map/ppermute | solution.py:34
  51.9 0.7 %maximum_bitcast_fusion.2 = bf16[1,4,7168]{2,1,0:T(4,128)(2,1)} fusion(bf16[4,3584]{1,0:T(4,128)(2,1)S(1)} %add_convert_fusion.4, bf16[4,3584]{1,0:T(4,128)(2,1)S(1)} %add_convert_fusion.5), kind=kLoop, calls=%fused_computation.46 | loop fusion | flops 114688 | bytes 114688 | tf_op jit(solution)/shard_map/broadcast_in_dim | solution.py:319
  (37 shorter events, 0.5 us)
Async XLA Ops:
  0.0 20.3 %copy-start = (bf16[1,7168,128]{2,1,0:T(8,128)(2,1)S(1)}, bf16[1,7168,128]{2,1,0:T(8,128)(2,1)}, u32[]{:S(2)}) copy-start(bf16[1,7168,128]{2,1,0:T(8,128)(2,1)} %param.16) | copy-start | bytes 5505028
  1.1 7.8 %collective-permute-start.2 = (bf16[4,7296]{1,0:T(4,128)(2,1)S(1)}, bf16[4,7296]{1,0:T(4,128)(2,1)S(1)}, u32[]{:S(2)}, u32[]{:S(2)}) collective-permute-start(bf16[4,7296]{1,0:T(4,128)(2,1)S(1)} %shard_map.100), channel_id=1, source_target_pairs={{0,12},{1,13},{2,14},{3,15},{4,8},{5,9},{6,10},{7,11},{8,4},{9,5},... | collective-permute-start | bytes 175112 | tf_op jit(solution)/shard_map/ppermute | solution.py:34
  6.2 4.3 %collective-permute-start.1 = (bf16[4,7296]{1,0:T(4,128)(2,1)S(1)}, bf16[4,7296]{1,0:T(4,128)(2,1)S(1)}, u32[]{:S(2)}, u32[]{:S(2)}) collective-permute-start(bf16[4,7296]{1,0:T(4,128)(2,1)S(1)} %shard_map.100), channel_id=1, source_target_pairs={{0,4},{1,5},{2,6},{3,7},{4,0},{5,1},{6,2},{7,3},{8,12},{9,13},{10,... | collective-permute-start | bytes 175112 | tf_op jit(solution)/shard_map/ppermute | solution.py:34
  6.2 5.5 %collective-permute-start = (bf16[4,7296]{1,0:T(4,128)(2,1)S(1)}, bf16[4,7296]{1,0:T(4,128)(2,1)S(1)}, u32[]{:S(2)}, u32[]{:S(2)}) collective-permute-start(bf16[4,7296]{1,0:T(4,128)(2,1)S(1)} %shard_map.100), channel_id=1, source_target_pairs={{0,8},{1,9},{2,10},{3,11},{4,12},{5,13},{6,14},{7,15},{8,0},{9,1},... | collective-permute-start | bytes 175112 | tf_op jit(solution)/shard_map/ppermute | solution.py:34
  6.9 4.9 %collective-permute-start.3 = (bf16[4,7296]{1,0:T(4,128)(2,1)S(1)}, bf16[4,7296]{1,0:T(4,128)(2,1)S(1)}, u32[]{:S(2)}, u32[]{:S(2)}) collective-permute-start(bf16[4,7296]{1,0:T(4,128)(2,1)S(1)} %shard_map.100), channel_id=1, source_target_pairs={{0,2},{1,3},{2,0},{3,1},{4,6},{5,7},{6,4},{7,5},{8,10},{9,11},{10,... | collective-permute-start | bytes 175112 | tf_op jit(solution)/shard_map/ppermute | solution.py:34
  11.8 6.1 %collective-permute-start.4 = (bf16[12,7296]{1,0:T(8,128)(2,1)S(1)}, bf16[12,7296]{1,0:T(8,128)(2,1)S(1)}, u32[]{:S(2)}, u32[]{:S(2)}) collective-permute-start(bf16[12,7296]{1,0:T(8,128)(2,1)S(1)} %pad_maximum_fusion.2), channel_id=1, source_target_pairs={{0,2},{1,3},{2,0},{3,1},{4,6},{5,7},{6,4},{7,5},{8,10},{9,11},{10,... | collective-permute-start | bytes 525320 | tf_op jit(solution)/shard_map/ppermute | solution.py:34
  18.2 1.9 %collective-permute-start.5 = (bf16[32,7296]{1,0:T(8,128)(2,1)S(1)}, bf16[32,7296]{1,0:T(8,128)(2,1)S(1)}, u32[]{:S(2)}, u32[]{:S(2)}) collective-permute-start(bf16[32,7296]{1,0:T(8,128)(2,1)S(1)} %pad_maximum_fusion.1), channel_id=1, source_target_pairs={{0,1},{1,0},{2,3},{3,2},{4,5},{5,4},{6,7},{7,6},{8,9},{9,8},{10,11... | collective-permute-start | bytes 1400840 | tf_op jit(solution)/shard_map/ppermute | solution.py:34
  20.8 6.6 %collective-permute-start.8 = (bf16[64,128]{1,0:T(8,128)(2,1)S(1)}, bf16[64,128]{1,0:T(8,128)(2,1)S(1)}, u32[]{:S(2)}, u32[]{:S(2)}) collective-permute-start(bf16[64,128]{1,0:T(8,128)(2,1)S(1)} %convolution_convert_fusion.1), channel_id=1, source_target_pairs={{0,3},{1,2},{2,1},{3,0},{4,7},{5,6},{6,5},{7,4},{8,11},{9,10},{10,... | collective-permute-start | bytes 49160 | tf_op jit(solution)/shard_map/ppermute | solution.py:34
  22.1 5.3 %collective-permute-start.7 = (bf16[64,128]{1,0:T(8,128)(2,1)S(1)}, bf16[64,128]{1,0:T(8,128)(2,1)S(1)}, u32[]{:S(2)}, u32[]{:S(2)}) collective-permute-start(bf16[64,128]{1,0:T(8,128)(2,1)S(1)} %convolution_convert_fusion.1), channel_id=1, source_target_pairs={{0,2},{1,3},{2,0},{3,1},{4,6},{5,7},{6,4},{7,5},{8,10},{9,11},{10,... | collective-permute-start | bytes 49160 | tf_op jit(solution)/shard_map/ppermute | solution.py:34
  22.7 4.7 %collective-permute-start.6 = (bf16[64,128]{1,0:T(8,128)(2,1)S(1)}, bf16[64,128]{1,0:T(8,128)(2,1)S(1)}, u32[]{:S(2)}, u32[]{:S(2)}) collective-permute-start(bf16[64,128]{1,0:T(8,128)(2,1)S(1)} %convolution_convert_fusion.1), channel_id=1, source_target_pairs={{0,1},{1,0},{2,3},{3,2},{4,5},{5,4},{6,7},{7,6},{8,9},{9,8},{10,11... | collective-permute-start | bytes 49160 | tf_op jit(solution)/shard_map/ppermute | solution.py:34
  22.7 4.7 %copy-start.2 = (bf16[1,4,128,2,256]{4,3,2,1,0:T(2,128)(2,1)S(1)}, bf16[1,4,128,2,256]{4,3,2,1,0:T(2,128)(2,1)}, u32[]{:S(2)}) copy-start(bf16[1,4,128,2,256]{4,3,2,1,0:T(2,128)(2,1)} %param.17) | copy-start | bytes 1572868
  27.2 1.0 %copy-start.3 = (bf16[1,4,256,128]{3,2,1,0:T(8,128)(2,1)S(1)}, bf16[1,4,256,128]{3,2,1,0:T(8,128)(2,1)}, u32[]{:S(2)}) copy-start(bf16[1,4,256,128]{3,2,1,0:T(8,128)(2,1)} %param.18) | copy-start | bytes 786436
  28.4 1.4 %collective-permute-start.9 = (bf16[2,64,128]{2,1,0:T(8,128)(2,1)S(1)}, bf16[2,64,128]{2,1,0:T(8,128)(2,1)S(1)}, u32[]{:S(2)}, u32[]{:S(2)}) collective-permute-start(bf16[2,64,128]{2,1,0:T(8,128)(2,1)S(1)} %dynamic-slice_bitcast_fusion), channel_id=1, source_target_pairs={{0,1},{1,0},{2,3},{3,2},{4,5},{5,4},{6,7},{7,6},{8,9},{9,8},{10,11... | collective-permute-start | bytes 98312 | tf_op jit(solution)/shard_map/ppermute | solution.py:34
  29.8 4.2 %collective-permute-start.10 = (bf16[64,128]{1,0:T(8,128)(2,1)S(1)}, bf16[64,128]{1,0:T(8,128)(2,1)S(1)}, u32[]{:S(2)}, u32[]{:S(2)}) collective-permute-start(bf16[64,128]{1,0:T(8,128)(2,1)S(1)} %dynamic-slice_bitcast_fusion.1), channel_id=1, source_target_pairs={{0,2},{1,3},{2,0},{3,1},{4,6},{5,7},{6,4},{7,5},{8,10},{9,11},{10,... | collective-permute-start | bytes 49160 | tf_op jit(solution)/shard_map/ppermute | solution.py:34
  31.3 2.6 %copy-start.1 = (bf16[1,128,7168]{2,1,0:T(8,128)(2,1)S(1)}, bf16[1,128,7168]{2,1,0:T(8,128)(2,1)}, u32[]{:S(2)}) copy-start(bf16[1,128,7168]{2,1,0:T(8,128)(2,1)} %param.19) | copy-start | bytes 5505028
  34.3 1.6 %collective-permute-start.15 = (bf16[32,3584]{1,0:T(8,128)(2,1)S(1)}, bf16[32,3584]{1,0:T(8,128)(2,1)S(1)}, u32[]{:S(2)}, u32[]{:S(2)}) collective-permute-start(bf16[32,3584]{1,0:T(8,128)(2,1)S(1)} %slice_select_fusion), channel_id=1, source_target_pairs={{0,1},{1,0},{2,3},{3,2},{4,5},{5,4},{6,7},{7,6},{8,9},{9,8},{10,11... | collective-permute-start | bytes 688136 | tf_op jit(solution)/shard_map/ppermute | solution.py:34
  34.8 2.3 %collective-permute-start.11 = (bf16[32,3584]{1,0:T(8,128)(2,1)S(1)}, bf16[32,3584]{1,0:T(8,128)(2,1)S(1)}, u32[]{:S(2)}, u32[]{:S(2)}) collective-permute-start(bf16[32,3584]{1,0:T(8,128)(2,1)S(1)} %slice_select_fusion.1), channel_id=1, source_target_pairs={{0,1},{1,0},{2,3},{3,2},{4,5},{5,4},{6,7},{7,6},{8,9},{9,8},{10,11... | collective-permute-start | bytes 688136 | tf_op jit(solution)/shard_map/ppermute | solution.py:34
  36.0 4.9 %collective-permute-start.16 = (bf16[16,3584]{1,0:T(8,128)(2,1)S(1)}, bf16[16,3584]{1,0:T(8,128)(2,1)S(1)}, u32[]{:S(2)}, u32[]{:S(2)}) collective-permute-start(bf16[16,3584]{1,0:T(8,128)(2,1)S(1)} %get-tuple-element.20), channel_id=1, source_target_pairs={{0,2},{1,5},{2,0},{3,7},{4,6},{5,1},{6,4},{7,3},{8,10},{9,13},{10,... | collective-permute-start | bytes 344072 | tf_op jit(solution)/shard_map/ppermute | solution.py:34
  37.3 5.3 %collective-permute-start.12 = (bf16[16,3584]{1,0:T(8,128)(2,1)S(1)}, bf16[16,3584]{1,0:T(8,128)(2,1)S(1)}, u32[]{:S(2)}, u32[]{:S(2)}) collective-permute-start(bf16[16,3584]{1,0:T(8,128)(2,1)S(1)} %get-tuple-element.18), channel_id=1, source_target_pairs={{0,2},{1,5},{2,0},{3,7},{4,6},{5,1},{6,4},{7,3},{8,10},{9,13},{10,... | collective-permute-start | bytes 344072 | tf_op jit(solution)/shard_map/ppermute | solution.py:34
  40.9 4.2 %collective-permute-start.17 = (bf16[8,3584]{1,0:T(8,128)(2,1)S(1)}, bf16[8,3584]{1,0:T(8,128)(2,1)S(1)}, u32[]{:S(2)}, u32[]{:S(2)}) collective-permute-start(bf16[8,3584]{1,0:T(8,128)(2,1)S(1)} %broadcast_select_fusion.4), channel_id=1, source_target_pairs={{0,4},{1,3},{2,6},{3,1},{4,0},{5,7},{6,2},{7,5},{8,12},{9,11},{10,... | collective-permute-start | bytes 172040 | tf_op jit(solution)/shard_map/ppermute | solution.py:34
  42.6 4.4 %collective-permute-start.13 = (bf16[8,3584]{1,0:T(8,128)(2,1)S(1)}, bf16[8,3584]{1,0:T(8,128)(2,1)S(1)}, u32[]{:S(2)}, u32[]{:S(2)}) collective-permute-start(bf16[8,3584]{1,0:T(8,128)(2,1)S(1)} %broadcast_select_fusion.5), channel_id=1, source_target_pairs={{0,4},{1,3},{2,6},{3,1},{4,0},{5,7},{6,2},{7,5},{8,12},{9,11},{10,... | collective-permute-start | bytes 172040 | tf_op jit(solution)/shard_map/ppermute | solution.py:34
  45.2 5.0 %collective-permute-start.18 = (bf16[4,3584]{1,0:T(4,128)(2,1)S(1)}, bf16[4,3584]{1,0:T(4,128)(2,1)S(1)}, u32[]{:S(2)}, u32[]{:S(2)}) collective-permute-start(bf16[4,3584]{1,0:T(4,128)(2,1)S(1)} %slice.113), channel_id=1, source_target_pairs={{0,8},{1,9},{2,10},{3,11},{4,12},{5,13},{6,14},{7,15},{8,0},{9,1},... | collective-permute-start | bytes 86024 | tf_op jit(solution)/shard_map/ppermute | solution.py:34
  47.1 4.8 %collective-permute-start.14 = (bf16[4,3584]{1,0:T(4,128)(2,1)S(1)}, bf16[4,3584]{1,0:T(4,128)(2,1)S(1)}, u32[]{:S(2)}, u32[]{:S(2)}) collective-permute-start(bf16[4,3584]{1,0:T(4,128)(2,1)S(1)} %slice.106), channel_id=1, source_target_pairs={{0,8},{1,9},{2,10},{3,11},{4,12},{5,13},{6,14},{7,15},{8,0},{9,1},... | collective-permute-start | bytes 86024 | tf_op jit(solution)/shard_map/ppermute | solution.py:34

commit v29 on v28

--- a/solution.py
+++ b/solution.py
@@ -10,8 +10,8 @@
 from jax.sharding import PartitionSpec as P
 
 CHUNKS = 2
-PIECES = (1, 2, 4, 4)
-DOWN_PIECES = (1, 3)
+PIECES = (1, 3, 5)
+DOWN_PIECES = (2,)
 VMEM = pl.BlockSpec(memory_space=pltpu.VMEM)
 HBM = pl.BlockSpec(memory_space=pltpu.HBM)
 

time: 52.8 us -> 53.1 us (level)
  no operation moved by 1% of the time
where the time goes in v29:
time: 53.1 us; the launch traced here: 53 us
  starting transfers between devices  22.6 us (43%)
  waiting for transfers between devices  17.5 us (33%)
  Pallas kernels  8.69 us (16%)
  other arithmetic  1.68 us (3%)
  matrix products  1.53 us (3%)
  local copies, waits for them, and re-layouts  0.69 us (1%)
    ppermute x19, starting transfers between devices, trade(): return lax.ppermute(value, ('expert', 'tensor'), pairs)  22.6 us
    ppermute x19, waiting for transfers between devices, trade(): return lax.ppermute(value, ('expert', 'tensor'), pairs)  17.5 us
    pallas_call x1, Pallas kernels, gate_up_product(): pl.pallas_call(gate_up_kernel, out_shape=jax.ShapeDtypeStruct((2 * x.shap...  4.63 us
    pallas_call x1, Pallas kernels, down_product(): pl.pallas_call(down_kernel, out_shape=jax.ShapeDtypeStruct((rows, width),...  2.78 us
    pallas_call x1, Pallas kernels, pack(): pl.pallas_call(pack_kernel, out_shape=jax.ShapeDtypeStruct((count, width...  1.09 us
  transfers between devices with their start and end apart: 19, of which 11 were waited for; matrix products, arithmetic and copies ran while one was open for 2% of the time, Pallas kernels for 14%

profile of v29, /device:TPU:0, one launch (start us, length us, event | category | flops | bytes accessed | tf_op | source)
XLA Modules:
  0.0 53.0 jit_solution(13447920050348021922)
XLA Ops:
  0.0 1.1 %shard_map.100 = bf16[4,7296]{1,0:T(4,128)(2,1)S(1)} custom-call(bf16[4,7168]{1,0:T(4,128)(2,1)} %bitcast.70, s32[4,8]{1,0:T(4,128)} %bitcast.71, s32[4,8]{1,0:T(4,128)} %bitcast.72, s32[16]{0:T(128)} %place.1), custom_call_target="tpu_custom_call" | custom-call | flops 20000000000 | bytes 114688 | tf_op jit(solution)/shard_map/pallas_call | solution.py:81
  1.1 5.1 %collective-permute-start.2 = (bf16[4,7296]{1,0:T(4,128)(2,1)S(1)}, bf16[4,7296]{1,0:T(4,128)(2,1)S(1)}, u32[]{:S(2)}, u32[]{:S(2)}) collective-permute-start(bf16[4,7296]{1,0:T(4,128)(2,1)S(1)} %shard_map.100), channel_id=1, source_target_pairs={{0,12},{1,13},{2,14},{3,15},{4,8},{5,9},{6,10},{7,11},{8,4},{9,5},... | collective-permute-start | bytes 175112 | tf_op jit(solution)/shard_map/ppermute | solution.py:34
  6.2 0.6 %collective-permute-start = (bf16[4,7296]{1,0:T(4,128)(2,1)S(1)}, bf16[4,7296]{1,0:T(4,128)(2,1)S(1)}, u32[]{:S(2)}, u32[]{:S(2)}) collective-permute-start(bf16[4,7296]{1,0:T(4,128)(2,1)S(1)} %shard_map.100), channel_id=1, source_target_pairs={{0,8},{1,9},{2,10},{3,11},{4,12},{5,13},{6,14},{7,15},{8,0},{9,1},... | collective-permute-start | bytes 175112 | tf_op jit(solution)/shard_map/ppermute | solution.py:34
  6.9 1.6 %collective-permute-start.3 = (bf16[4,7296]{1,0:T(4,128)(2,1)S(1)}, bf16[4,7296]{1,0:T(4,128)(2,1)S(1)}, u32[]{:S(2)}, u32[]{:S(2)}) collective-permute-start(bf16[4,7296]{1,0:T(4,128)(2,1)S(1)} %shard_map.100), channel_id=1, source_target_pairs={{0,2},{1,3},{2,0},{3,1},{4,6},{5,7},{6,4},{7,5},{8,10},{9,11},{10,... | collective-permute-start | bytes 175112 | tf_op jit(solution)/shard_map/ppermute | solution.py:34
  8.5 0.4 collective-permute-done.2
  8.9 1.7 %collective-permute-done.1 = bf16[4,7296]{1,0:T(4,128)(2,1)S(1)} collective-permute-done((bf16[4,7296]{1,0:T(4,128)(2,1)S(1)}, bf16[4,7296]{1,0:T(4,128)(2,1)S(1)}, u32[]{:S(2)}, u32[]{:S(2)}) %collective-permute-start.1) | collective-permute-done | bytes 58400 | tf_op jit(solution)/shard_map/ppermute | solution.py:34
  10.6 1.1 %collective-permute-done = bf16[4,7296]{1,0:T(4,128)(2,1)S(1)} collective-permute-done((bf16[4,7296]{1,0:T(4,128)(2,1)S(1)}, bf16[4,7296]{1,0:T(4,128)(2,1)S(1)}, u32[]{:S(2)}, u32[]{:S(2)}) %collective-permute-start) | collective-permute-done | bytes 58400 | tf_op jit(solution)/shard_map/ppermute | solution.py:34
  11.7 0.1 pad_maximum_fusion.2
  11.8 1.6 %collective-permute-start.4 = (bf16[12,7296]{1,0:T(8,128)(2,1)S(1)}, bf16[12,7296]{1,0:T(8,128)(2,1)S(1)}, u32[]{:S(2)}, u32[]{:S(2)}) collective-permute-start(bf16[12,7296]{1,0:T(8,128)(2,1)S(1)} %pad_maximum_fusion.2), channel_id=1, source_target_pairs={{0,2},{1,3},{2,0},{3,1},{4,6},{5,7},{6,4},{7,5},{8,10},{9,11},{10,... | collective-permute-start | bytes 525320 | tf_op jit(solution)/shard_map/ppermute | solution.py:34
  13.4 4.6 %collective-permute-done.4 = bf16[12,7296]{1,0:T(8,128)(2,1)S(1)} collective-permute-done((bf16[12,7296]{1,0:T(8,128)(2,1)S(1)}, bf16[12,7296]{1,0:T(8,128)(2,1)S(1)}, u32[]{:S(2)}, u32[]{:S(2)}) %collective-permute-start.4) | collective-permute-done | bytes 175136 | tf_op jit(solution)/shard_map/ppermute | solution.py:34
  17.9 0.2 broadcast_select_fusion.3
  18.3 1.8 %collective-permute-done.5 = bf16[32,7296]{1,0:T(8,128)(2,1)S(1)} collective-permute-done((bf16[32,7296]{1,0:T(8,128)(2,1)S(1)}, bf16[32,7296]{1,0:T(8,128)(2,1)S(1)}, u32[]{:S(2)}, u32[]{:S(2)}) %collective-permute-start.5) | collective-permute-done | bytes 466976 | tf_op jit(solution)/shard_map/ppermute | solution.py:34
  20.1 0.2 broadcast_select_fusion.1
  20.3 0.1 pad_maximum_fusion.x
  20.3 0.5 convolution_convert_fusion.1
  20.8 1.3 %collective-permute-start.8 = (bf16[64,128]{1,0:T(8,128)(2,1)S(1)}, bf16[64,128]{1,0:T(8,128)(2,1)S(1)}, u32[]{:S(2)}, u32[]{:S(2)}) collective-permute-start(bf16[64,128]{1,0:T(8,128)(2,1)S(1)} %convolution_convert_fusion.1), channel_id=1, source_target_pairs={{0,3},{1,2},{2,1},{3,0},{4,7},{5,6},{6,5},{7,4},{8,11},{9,10},{10,... | collective-permute-start | bytes 49160 | tf_op jit(solution)/shard_map/ppermute | solution.py:34
  22.1 0.5 %collective-permute-start.7 = (bf16[64,128]{1,0:T(8,128)(2,1)S(1)}, bf16[64,128]{1,0:T(8,128)(2,1)S(1)}, u32[]{:S(2)}, u32[]{:S(2)}) collective-permute-start(bf16[64,128]{1,0:T(8,128)(2,1)S(1)} %convolution_convert_fusion.1), channel_id=1, source_target_pairs={{0,2},{1,3},{2,0},{3,1},{4,6},{5,7},{6,4},{7,5},{8,10},{9,11},{10,... | collective-permute-start | bytes 49160 | tf_op jit(solution)/shard_map/ppermute | solution.py:34
  22.7 0.1 collective-permute-start.6
  22.8 4.6 %shard_map.101 = f32[128,256]{1,0:T(8,128)S(1)} custom-call(bf16[64,7296]{1,0:T(8,128)(2,1)S(1)} %pad_maximum_fusion.x, bf16[7168,2,256]{2,1,0:T(2,128)(2,1)} %bitcast.61), custom_call_target="tpu_custom_call" | custom-call | flops 469762048 | bytes 7340032 | tf_op jit(solution)/shard_map/pallas_call | solution.py:136
  27.4 0.1 dynamic-slice_convert_fusion
  27.5 0.1 copy.14
  27.7 0.2 fusion.7
  27.9 0.1 multiply_reduce_fusion
  28.0 0.3 copy-done.3
  28.3 0.2 convolution_convert_fusion
  28.6 0.5 collective-permute-start.9
  29.0 0.2 dynamic-slice_reduce_fusion
  29.2 0.7 %collective-permute-done.9 = bf16[2,64,128]{2,1,0:T(8,128)(2,1)S(1)} collective-permute-done((bf16[2,64,128]{2,1,0:T(8,128)(2,1)S(1)}, bf16[2,64,128]{2,1,0:T(8,128)(2,1)S(1)}, u32[]{:S(2)}, u32[]{:S(2)}) %collective-permute-start.9) | collective-permute-done | bytes 32800 | tf_op jit(solution)/shard_map/ppermute | solution.py:34
  29.9 1.6 %collective-permute-start.10 = (bf16[64,128]{1,0:T(8,128)(2,1)S(1)}, bf16[64,128]{1,0:T(8,128)(2,1)S(1)}, u32[]{:S(2)}, u32[]{:S(2)}) collective-permute-start(bf16[64,128]{1,0:T(8,128)(2,1)S(1)} %dynamic-slice_bitcast_fusion.1), channel_id=1, source_target_pairs={{0,2},{1,3},{2,0},{3,1},{4,6},{5,7},{6,4},{7,5},{8,10},{9,11},{10,... | collective-permute-start | bytes 49160 | tf_op jit(solution)/shard_map/ppermute | solution.py:34
  31.5 2.8 %shard_map.102 = f32[64,7168]{1,0:T(8,128)S(1)} custom-call(bf16[64,256]{1,0:T(8,128)(2,1)S(1)} %get-tuple-element.21.hidden, bf16[256,7168]{1,0:T(8,128)(2,1)} %bitcast.62), custom_call_target="tpu_custom_call" | custom-call | flops 234881024 | bytes 3670016 | tf_op jit(solution)/shard_map/pallas_call | solution.py:168
  34.3 0.3 fusion.1.term
  34.7 0.1 collective-permute-start.15
  34.8 0.3 fusion.term
  35.2 0.5 collective-permute-start.11
  35.7 0.5 %collective-permute-done.15.received = bf16[32,3584]{1,0:T(8,128)(2,1)S(1)} collective-permute-done((bf16[32,3584]{1,0:T(8,128)(2,1)S(1)}, bf16[32,3584]{1,0:T(8,128)(2,1)S(1)}, u32[]{:S(2)}, u32[]{:S(2)}) %collective-permute-start.15) | collective-permute-done | bytes 229408 | tf_op jit(solution)/shard_map/ppermute | solution.py:34
  36.3 0.1 shard_map.104
  36.4 1.0 %collective-permute-start.16 = (bf16[16,3584]{1,0:T(8,128)(2,1)S(1)}, bf16[16,3584]{1,0:T(8,128)(2,1)S(1)}, u32[]{:S(2)}, u32[]{:S(2)}) collective-permute-start(bf16[16,3584]{1,0:T(8,128)(2,1)S(1)} %get-tuple-element.20), channel_id=1, source_target_pairs={{0,2},{1,5},{2,0},{3,7},{4,6},{5,1},{6,4},{7,3},{8,10},{9,13},{10,... | collective-permute-start | bytes 344072 | tf_op jit(solution)/shard_map/ppermute | solution.py:34
  37.3 0.1 shard_map.103
  37.4 1.2 %collective-permute-start.12 = (bf16[16,3584]{1,0:T(8,128)(2,1)S(1)}, bf16[16,3584]{1,0:T(8,128)(2,1)S(1)}, u32[]{:S(2)}, u32[]{:S(2)}) collective-permute-start(bf16[16,3584]{1,0:T(8,128)(2,1)S(1)} %get-tuple-element.18), channel_id=1, source_target_pairs={{0,2},{1,5},{2,0},{3,7},{4,6},{5,1},{6,4},{7,3},{8,10},{9,13},{10,... | collective-permute-start | bytes 344072 | tf_op jit(solution)/shard_map/ppermute | solution.py:34
  38.6 2.6 %collective-permute-done.16 = bf16[16,3584]{1,0:T(8,128)(2,1)S(1)} collective-permute-done((bf16[16,3584]{1,0:T(8,128)(2,1)S(1)}, bf16[16,3584]{1,0:T(8,128)(2,1)S(1)}, u32[]{:S(2)}, u32[]{:S(2)}) %collective-permute-start.16) | collective-permute-done | bytes 114720 | tf_op jit(solution)/shard_map/ppermute | solution.py:34
  41.3 1.7 %collective-permute-start.17 = (bf16[8,3584]{1,0:T(8,128)(2,1)S(1)}, bf16[8,3584]{1,0:T(8,128)(2,1)S(1)}, u32[]{:S(2)}, u32[]{:S(2)}) collective-permute-start(bf16[8,3584]{1,0:T(8,128)(2,1)S(1)} %broadcast_select_fusion.4), channel_id=1, source_target_pairs={{0,4},{1,3},{2,6},{3,1},{4,0},{5,7},{6,2},{7,5},{8,12},{9,11},{10,... | collective-permute-start | bytes 172040 | tf_op jit(solution)/shard_map/ppermute | solution.py:34
  43.0 1.2 %collective-permute-start.13 = (bf16[8,3584]{1,0:T(8,128)(2,1)S(1)}, bf16[8,3584]{1,0:T(8,128)(2,1)S(1)}, u32[]{:S(2)}, u32[]{:S(2)}) collective-permute-start(bf16[8,3584]{1,0:T(8,128)(2,1)S(1)} %broadcast_select_fusion.5), channel_id=1, source_target_pairs={{0,4},{1,3},{2,6},{3,1},{4,0},{5,7},{6,2},{7,5},{8,12},{9,11},{10,... | collective-permute-start | bytes 172040 | tf_op jit(solution)/shard_map/ppermute | solution.py:34
  44.2 1.3 %collective-permute-done.17 = bf16[8,3584]{1,0:T(8,128)(2,1)S(1)} collective-permute-done((bf16[8,3584]{1,0:T(8,128)(2,1)S(1)}, bf16[8,3584]{1,0:T(8,128)(2,1)S(1)}, u32[]{:S(2)}, u32[]{:S(2)}) %collective-permute-start.17) | collective-permute-done | bytes 57376 | tf_op jit(solution)/shard_map/ppermute | solution.py:34
  45.6 1.8 %collective-permute-start.18 = (bf16[4,3584]{1,0:T(4,128)(2,1)S(1)}, bf16[4,3584]{1,0:T(4,128)(2,1)S(1)}, u32[]{:S(2)}, u32[]{:S(2)}) collective-permute-start(bf16[4,3584]{1,0:T(4,128)(2,1)S(1)} %slice.113), channel_id=1, source_target_pairs={{0,8},{1,9},{2,10},{3,11},{4,12},{5,13},{6,14},{7,15},{8,0},{9,1},... | collective-permute-start | bytes 86024 | tf_op jit(solution)/shard_map/ppermute | solution.py:34
  47.5 2.0 %collective-permute-start.14 = (bf16[4,3584]{1,0:T(4,128)(2,1)S(1)}, bf16[4,3584]{1,0:T(4,128)(2,1)S(1)}, u32[]{:S(2)}, u32[]{:S(2)}) collective-permute-start(bf16[4,3584]{1,0:T(4,128)(2,1)S(1)} %slice.106), channel_id=1, source_target_pairs={{0,8},{1,9},{2,10},{3,11},{4,12},{5,13},{6,14},{7,15},{8,0},{9,1},... | collective-permute-start | bytes 86024 | tf_op jit(solution)/shard_map/ppermute | solution.py:34
  49.5 1.1 %collective-permute-done.18 = bf16[4,3584]{1,0:T(4,128)(2,1)S(1)} collective-permute-done((bf16[4,3584]{1,0:T(4,128)(2,1)S(1)}, bf16[4,3584]{1,0:T(4,128)(2,1)S(1)}, u32[]{:S(2)}, u32[]{:S(2)}) %collective-permute-start.18) | collective-permute-done | bytes 28704 | tf_op jit(solution)/shard_map/ppermute | solution.py:34
  50.6 1.7 %collective-permute-done.14 = bf16[4,3584]{1,0:T(4,128)(2,1)S(1)} collective-permute-done((bf16[4,3584]{1,0:T(4,128)(2,1)S(1)}, bf16[4,3584]{1,0:T(4,128)(2,1)S(1)}, u32[]{:S(2)}, u32[]{:S(2)}) %collective-permute-start.14) | collective-permute-done | bytes 28704 | tf_op jit(solution)/shard_map/ppermute | solution.py:34
  52.3 0.7 %maximum_bitcast_fusion.2 = bf16[1,4,7168]{2,1,0:T(4,128)(2,1)} fusion(bf16[4,3584]{1,0:T(4,128)(2,1)S(1)} %add_convert_fusion.4, bf16[4,3584]{1,0:T(4,128)(2,1)S(1)} %add_convert_fusion.5), kind=kLoop, calls=%fused_computation.46 | loop fusion | flops 114688 | bytes 114688 | tf_op jit(solution)/shard_map/broadcast_in_dim | solution.py:319
  (37 shorter events, 0.5 us)
Async XLA Ops:
  0.0 20.3 %copy-start = (bf16[1,7168,128]{2,1,0:T(8,128)(2,1)S(1)}, bf16[1,7168,128]{2,1,0:T(8,128)(2,1)}, u32[]{:S(2)}) copy-start(bf16[1,7168,128]{2,1,0:T(8,128)(2,1)} %param.16) | copy-start | bytes 5505028
  1.1 7.8 %collective-permute-start.2 = (bf16[4,7296]{1,0:T(4,128)(2,1)S(1)}, bf16[4,7296]{1,0:T(4,128)(2,1)S(1)}, u32[]{:S(2)}, u32[]{:S(2)}) collective-permute-start(bf16[4,7296]{1,0:T(4,128)(2,1)S(1)} %shard_map.100), channel_id=1, source_target_pairs={{0,12},{1,13},{2,14},{3,15},{4,8},{5,9},{6,10},{7,11},{8,4},{9,5},... | collective-permute-start | bytes 175112 | tf_op jit(solution)/shard_map/ppermute | solution.py:34
  6.2 4.3 %collective-permute-start.1 = (bf16[4,7296]{1,0:T(4,128)(2,1)S(1)}, bf16[4,7296]{1,0:T(4,128)(2,1)S(1)}, u32[]{:S(2)}, u32[]{:S(2)}) collective-permute-start(bf16[4,7296]{1,0:T(4,128)(2,1)S(1)} %shard_map.100), channel_id=1, source_target_pairs={{0,4},{1,5},{2,6},{3,7},{4,0},{5,1},{6,2},{7,3},{8,12},{9,13},{10,... | collective-permute-start | bytes 175112 | tf_op jit(solution)/shard_map/ppermute | solution.py:34
  6.2 5.5 %collective-permute-start = (bf16[4,7296]{1,0:T(4,128)(2,1)S(1)}, bf16[4,7296]{1,0:T(4,128)(2,1)S(1)}, u32[]{:S(2)}, u32[]{:S(2)}) collective-permute-start(bf16[4,7296]{1,0:T(4,128)(2,1)S(1)} %shard_map.100), channel_id=1, source_target_pairs={{0,8},{1,9},{2,10},{3,11},{4,12},{5,13},{6,14},{7,15},{8,0},{9,1},... | collective-permute-start | bytes 175112 | tf_op jit(solution)/shard_map/ppermute | solution.py:34
  6.9 4.9 %collective-permute-start.3 = (bf16[4,7296]{1,0:T(4,128)(2,1)S(1)}, bf16[4,7296]{1,0:T(4,128)(2,1)S(1)}, u32[]{:S(2)}, u32[]{:S(2)}) collective-permute-start(bf16[4,7296]{1,0:T(4,128)(2,1)S(1)} %shard_map.100), channel_id=1, source_target_pairs={{0,2},{1,3},{2,0},{3,1},{4,6},{5,7},{6,4},{7,5},{8,10},{9,11},{10,... | collective-permute-start | bytes 175112 | tf_op jit(solution)/shard_map/ppermute | solution.py:34
  11.8 6.1 %collective-permute-start.4 = (bf16[12,7296]{1,0:T(8,128)(2,1)S(1)}, bf16[12,7296]{1,0:T(8,128)(2,1)S(1)}, u32[]{:S(2)}, u32[]{:S(2)}) collective-permute-start(bf16[12,7296]{1,0:T(8,128)(2,1)S(1)} %pad_maximum_fusion.2), channel_id=1, source_target_pairs={{0,2},{1,3},{2,0},{3,1},{4,6},{5,7},{6,4},{7,5},{8,10},{9,11},{10,... | collective-permute-start | bytes 525320 | tf_op jit(solution)/shard_map/ppermute | solution.py:34
  18.2 1.9 %collective-permute-start.5 = (bf16[32,7296]{1,0:T(8,128)(2,1)S(1)}, bf16[32,7296]{1,0:T(8,128)(2,1)S(1)}, u32[]{:S(2)}, u32[]{:S(2)}) collective-permute-start(bf16[32,7296]{1,0:T(8,128)(2,1)S(1)} %pad_maximum_fusion.1), channel_id=1, source_target_pairs={{0,1},{1,0},{2,3},{3,2},{4,5},{5,4},{6,7},{7,6},{8,9},{9,8},{10,11... | collective-permute-start | bytes 1400840 | tf_op jit(solution)/shard_map/ppermute | solution.py:34
  20.8 6.8 %collective-permute-start.8 = (bf16[64,128]{1,0:T(8,128)(2,1)S(1)}, bf16[64,128]{1,0:T(8,128)(2,1)S(1)}, u32[]{:S(2)}, u32[]{:S(2)}) collective-permute-start(bf16[64,128]{1,0:T(8,128)(2,1)S(1)} %convolution_convert_fusion.1), channel_id=1, source_target_pairs={{0,3},{1,2},{2,1},{3,0},{4,7},{5,6},{6,5},{7,4},{8,11},{9,10},{10,... | collective-permute-start | bytes 49160 | tf_op jit(solution)/shard_map/ppermute | solution.py:34
  22.1 5.4 %collective-permute-start.7 = (bf16[64,128]{1,0:T(8,128)(2,1)S(1)}, bf16[64,128]{1,0:T(8,128)(2,1)S(1)}, u32[]{:S(2)}, u32[]{:S(2)}) collective-permute-start(bf16[64,128]{1,0:T(8,128)(2,1)S(1)} %convolution_convert_fusion.1), channel_id=1, source_target_pairs={{0,2},{1,3},{2,0},{3,1},{4,6},{5,7},{6,4},{7,5},{8,10},{9,11},{10,... | collective-permute-start | bytes 49160 | tf_op jit(solution)/shard_map/ppermute | solution.py:34
  22.7 4.9 %collective-permute-start.6 = (bf16[64,128]{1,0:T(8,128)(2,1)S(1)}, bf16[64,128]{1,0:T(8,128)(2,1)S(1)}, u32[]{:S(2)}, u32[]{:S(2)}) collective-permute-start(bf16[64,128]{1,0:T(8,128)(2,1)S(1)} %convolution_convert_fusion.1), channel_id=1, source_target_pairs={{0,1},{1,0},{2,3},{3,2},{4,5},{5,4},{6,7},{7,6},{8,9},{9,8},{10,11... | collective-permute-start | bytes 49160 | tf_op jit(solution)/shard_map/ppermute | solution.py:34
  22.7 4.9 %copy-start.2 = (bf16[1,4,128,2,256]{4,3,2,1,0:T(2,128)(2,1)S(1)}, bf16[1,4,128,2,256]{4,3,2,1,0:T(2,128)(2,1)}, u32[]{:S(2)}) copy-start(bf16[1,4,128,2,256]{4,3,2,1,0:T(2,128)(2,1)} %param.17) | copy-start | bytes 1572868
  27.4 1.0 %copy-start.3 = (bf16[1,4,256,128]{3,2,1,0:T(8,128)(2,1)S(1)}, bf16[1,4,256,128]{3,2,1,0:T(8,128)(2,1)}, u32[]{:S(2)}) copy-start(bf16[1,4,256,128]{3,2,1,0:T(8,128)(2,1)} %param.18) | copy-start | bytes 786436
  28.6 1.4 %collective-permute-start.9 = (bf16[2,64,128]{2,1,0:T(8,128)(2,1)S(1)}, bf16[2,64,128]{2,1,0:T(8,128)(2,1)S(1)}, u32[]{:S(2)}, u32[]{:S(2)}) collective-permute-start(bf16[2,64,128]{2,1,0:T(8,128)(2,1)S(1)} %dynamic-slice_bitcast_fusion), channel_id=1, source_target_pairs={{0,1},{1,0},{2,3},{3,2},{4,5},{5,4},{6,7},{7,6},{8,9},{9,8},{10,11... | collective-permute-start | bytes 98312 | tf_op jit(solution)/shard_map/ppermute | solution.py:34
  29.9 4.4 %collective-permute-start.10 = (bf16[64,128]{1,0:T(8,128)(2,1)S(1)}, bf16[64,128]{1,0:T(8,128)(2,1)S(1)}, u32[]{:S(2)}, u32[]{:S(2)}) collective-permute-start(bf16[64,128]{1,0:T(8,128)(2,1)S(1)} %dynamic-slice_bitcast_fusion.1), channel_id=1, source_target_pairs={{0,2},{1,3},{2,0},{3,1},{4,6},{5,7},{6,4},{7,5},{8,10},{9,11},{10,... | collective-permute-start | bytes 49160 | tf_op jit(solution)/shard_map/ppermute | solution.py:34
  31.5 2.8 %copy-start.1 = (bf16[1,128,7168]{2,1,0:T(8,128)(2,1)S(1)}, bf16[1,128,7168]{2,1,0:T(8,128)(2,1)}, u32[]{:S(2)}) copy-start(bf16[1,128,7168]{2,1,0:T(8,128)(2,1)} %param.19) | copy-start | bytes 5505028
  34.7 1.6 %collective-permute-start.15 = (bf16[32,3584]{1,0:T(8,128)(2,1)S(1)}, bf16[32,3584]{1,0:T(8,128)(2,1)S(1)}, u32[]{:S(2)}, u32[]{:S(2)}) collective-permute-start(bf16[32,3584]{1,0:T(8,128)(2,1)S(1)} %slice_select_fusion), channel_id=1, source_target_pairs={{0,1},{1,0},{2,3},{3,2},{4,5},{5,4},{6,7},{7,6},{8,9},{9,8},{10,11... | collective-permute-start | bytes 688136 | tf_op jit(solution)/shard_map/ppermute | solution.py:34
  35.2 2.1 %collective-permute-start.11 = (bf16[32,3584]{1,0:T(8,128)(2,1)S(1)}, bf16[32,3584]{1,0:T(8,128)(2,1)S(1)}, u32[]{:S(2)}, u32[]{:S(2)}) collective-permute-start(bf16[32,3584]{1,0:T(8,128)(2,1)S(1)} %slice_select_fusion.1), channel_id=1, source_target_pairs={{0,1},{1,0},{2,3},{3,2},{4,5},{5,4},{6,7},{7,6},{8,9},{9,8},{10,11... | collective-permute-start | bytes 688136 | tf_op jit(solution)/shard_map/ppermute | solution.py:34
  36.4 4.9 %collective-permute-start.16 = (bf16[16,3584]{1,0:T(8,128)(2,1)S(1)}, bf16[16,3584]{1,0:T(8,128)(2,1)S(1)}, u32[]{:S(2)}, u32[]{:S(2)}) collective-permute-start(bf16[16,3584]{1,0:T(8,128)(2,1)S(1)} %get-tuple-element.20), channel_id=1, source_target_pairs={{0,2},{1,5},{2,0},{3,7},{4,6},{5,1},{6,4},{7,3},{8,10},{9,13},{10,... | collective-permute-start | bytes 344072 | tf_op jit(solution)/shard_map/ppermute | solution.py:34
  37.4 5.5 %collective-permute-start.12 = (bf16[16,3584]{1,0:T(8,128)(2,1)S(1)}, bf16[16,3584]{1,0:T(8,128)(2,1)S(1)}, u32[]{:S(2)}, u32[]{:S(2)}) collective-permute-start(bf16[16,3584]{1,0:T(8,128)(2,1)S(1)} %get-tuple-element.18), channel_id=1, source_target_pairs={{0,2},{1,5},{2,0},{3,7},{4,6},{5,1},{6,4},{7,3},{8,10},{9,13},{10,... | collective-permute-start | bytes 344072 | tf_op jit(solution)/shard_map/ppermute | solution.py:34
  41.3 4.2 %collective-permute-start.17 = (bf16[8,3584]{1,0:T(8,128)(2,1)S(1)}, bf16[8,3584]{1,0:T(8,128)(2,1)S(1)}, u32[]{:S(2)}, u32[]{:S(2)}) collective-permute-start(bf16[8,3584]{1,0:T(8,128)(2,1)S(1)} %broadcast_select_fusion.4), channel_id=1, source_target_pairs={{0,4},{1,3},{2,6},{3,1},{4,0},{5,7},{6,2},{7,5},{8,12},{9,11},{10,... | collective-permute-start | bytes 172040 | tf_op jit(solution)/shard_map/ppermute | solution.py:34
  43.0 4.4 %collective-permute-start.13 = (bf16[8,3584]{1,0:T(8,128)(2,1)S(1)}, bf16[8,3584]{1,0:T(8,128)(2,1)S(1)}, u32[]{:S(2)}, u32[]{:S(2)}) collective-permute-start(bf16[8,3584]{1,0:T(8,128)(2,1)S(1)} %broadcast_select_fusion.5), channel_id=1, source_target_pairs={{0,4},{1,3},{2,6},{3,1},{4,0},{5,7},{6,2},{7,5},{8,12},{9,11},{10,... | collective-permute-start | bytes 172040 | tf_op jit(solution)/shard_map/ppermute | solution.py:34
  45.6 5.0 %collective-permute-start.18 = (bf16[4,3584]{1,0:T(4,128)(2,1)S(1)}, bf16[4,3584]{1,0:T(4,128)(2,1)S(1)}, u32[]{:S(2)}, u32[]{:S(2)}) collective-permute-start(bf16[4,3584]{1,0:T(4,128)(2,1)S(1)} %slice.113), channel_id=1, source_target_pairs={{0,8},{1,9},{2,10},{3,11},{4,12},{5,13},{6,14},{7,15},{8,0},{9,1},... | collective-permute-start | bytes 86024 | tf_op jit(solution)/shard_map/ppermute | solution.py:34
  47.5 4.8 %collective-permute-start.14 = (bf16[4,3584]{1,0:T(4,128)(2,1)S(1)}, bf16[4,3584]{1,0:T(4,128)(2,1)S(1)}, u32[]{:S(2)}, u32[]{:S(2)}) collective-permute-start(bf16[4,3584]{1,0:T(4,128)(2,1)S(1)} %slice.106), channel_id=1, source_target_pairs={{0,8},{1,9},{2,10},{3,11},{4,12},{5,13},{6,14},{7,15},{8,0},{9,1},... | collective-permute-start | bytes 86024 | tf_op jit(solution)/shard_map/ppermute | solution.py:34
